TPU v7x, 32 devices: a whole 2x2x4 slice. The times are simulated.
32 devices in a mesh: grp: 2 (over y), lon: 4 (over z), lat: 4 (over x, core).
Axes of the slice: x: 2, y: 2, z: 4, core: 2. Of those that a mesh axis runs over, the one named last changes fastest.
Arguments:
- grid_in: bfloat16 [64, 1024, 474], P(('grp', 'lat'), 'lon'), parts along dimension 0, may hold values from -6 to 6
- mesh_lat: bfloat16 [8192, 512], P(('grp', 'lon', 'lat')), parts along dimension 0, may hold values from -6 to 6
- edge_w: bfloat16 [1024, 128, 128], P(('grp', 'lon', 'lat')), parts along dimension 0, may hold values from -0.23925781 to 0.23925781
- edge_src: int32 [1024], P(('grp', 'lon', 'lat')), parts along dimension 0, may hold values from 0 to 39
- edge_dst: int32 [1024], P(('grp', 'lon', 'lat')), parts along dimension 0, may hold values from 0 to 1
- block_count: int32 [32], P(('grp', 'lon', 'lat')), parts along dimension 0, may hold values from 16 to 32, as said below
- embed_w: bfloat16 [474, 512], replicated, may hold values from -0.25 to 0.25
- message_w: bfloat16 [512, 512], replicated, may hold values from -0.25 to 0.25
- up_w: bfloat16 [512, 512], replicated, may hold values from -0.25 to 0.25
- out_w: bfloat16 [512, 512], replicated, may hold values from -0.25 to 0.25
- gain: float32 [512], replicated, may hold values from 0.1 to 1.9
- cot: bfloat16 [8192, 512], P(('grp', 'lon', 'lat')), parts along dimension 0, may hold values from -6 to 6
Outputs:
- mesh_new: bfloat16 [8192, 512], P(('grp', 'lon', 'lat')), parts along dimension 0
- mesh_latent_gradient: float32 [8192, 512], P(('grp', 'lon', 'lat')), parts along dimension 0
- grad_embed: float32 [948, 512], P('grp'), parts along dimension 0
- grad_message: float32 [1024, 512], P('grp'), parts along dimension 0
- grad_up: float32 [1024, 512], P('grp'), parts along dimension 0
- grad_out: float32 [1024, 512], P('grp'), parts along dimension 0
- grad_gain: float32 [1024], P('grp'), parts along dimension 0
There are 2 independent parts, one for each index of `grp`. A program takes and returns all parts, laid end to end along the dimension named above; an argument that names none is the same for every part. Nothing has to cross between parts.
Inputs may be any that keep to these rules, and one draw needn't show every extreme that they name: `block_count`: each tile uses between 16 and 32 slots; some tile uses all 32.
All inputs are finite; a program needn't handle non-finite values.
Results may differ from a plain program's by a relative error of at most 0.013.
Values may be sent and summed in bfloat16 or wider, within the bound.
No kernel may reach another device: no remote copies, remote signals or barrier semaphores. Data moves between devices by JAX's collectives and lax.ppermute only.
A program may use at most 128 MiB of HBM per device.

v0:
```python
import jax
import jax.numpy as jnp
from jax import lax
from jax.sharding import PartitionSpec as P

epsilon = 1e-05


def extended_2(cells, sides, width):
    for axis, dim in sides:
        count = lax.axis_size(axis)
        head = lax.slice_in_dim(cells, 0, width, axis=dim)
        tail = lax.slice_in_dim(cells, cells.shape[dim] - width, cells.shape[dim], axis=dim)
        cells = jnp.concatenate(
            [
                lax.ppermute(tail, axis, [(i, (i + 1) % count) for i in range(count)]),
                cells,
                lax.ppermute(head, axis, [((i + 1) % count, i) for i in range(count)]),
            ],
            axis=dim,
        )
    return cells


def passed_along(value, axis, by):
    length = lax.axis_size(axis)
    return lax.ppermute(value, axis, [(i, (i + by) % length) for i in range(length)])


def silu_slope(value_entries):
    sigma = jax.nn.sigmoid(value_entries)
    return sigma * (1.0 + value_entries * (1.0 - sigma))


def embed_rows(inputs, embed_w, message_w):
    features = inputs.shape[-1]
    pre = jnp.dot(inputs.reshape(-1, features), embed_w, preferred_element_type=jnp.float32)
    hidden = jax.nn.silu(pre).astype(jnp.bfloat16)
    message = jnp.dot(hidden, message_w, preferred_element_type=jnp.float32).astype(jnp.bfloat16)
    return (pre, hidden, message)


def on_device(
    grid_in,
    mesh_lat,
    edge_w,
    edge_src,
    edge_dst,
    block_count,
    embed_w,
    message_w,
    up_w,
    out_w,
    gain,
    cot,
):
    tile_rows, tile_cols, features = grid_in.shape
    latent = message_w.shape[0]
    block = edge_w.shape[1]
    half_block = block // 2
    slot_total = edge_w.shape[0]
    mesh_blocks = mesh_lat.shape[0] // block
    pieces = (tile_cols + block) // half_block
    windows = pieces - 1
    pre_own, hidden_own, message_own = embed_rows(grid_in, embed_w, message_w)
    extended = extended_2(
        message_own.reshape(tile_rows, tile_cols, latent), (("lon", 1),), half_block
    )
    halves = extended.reshape(tile_rows * pieces, half_block, latent)
    first = edge_src // windows * pieces + edge_src % windows
    block_groups = jnp.concatenate((halves[first], halves[first + 1]), axis=1)
    active = (lax.iota(jnp.int32, slot_total) < block_count[0]).astype(jnp.bfloat16)
    weight_entries = edge_w * active[:, None, None]
    product_terms = jnp.einsum(
        "yjc,ycz->yjz", weight_entries, block_groups, preferred_element_type=jnp.float32
    )
    onehot = (edge_dst[None, :] == lax.iota(jnp.int32, mesh_blocks)[:, None]).astype(jnp.float32)
    aggregate = jnp.einsum(
        "gb,bmd->gmd", onehot, product_terms, precision=lax.Precision.HIGHEST
    ).reshape(-1, latent)
    mesh_rows = mesh_lat.astype(jnp.float32)
    summed = mesh_rows + aggregate
    rinv = lax.rsqrt(jnp.mean(summed * summed, axis=1, keepdims=True) + epsilon)
    qhat = summed * rinv
    normed = (qhat * gain).astype(jnp.bfloat16)
    pre_up = jnp.dot(normed, up_w, preferred_element_type=jnp.float32)
    update = jax.nn.silu(pre_up).astype(jnp.bfloat16)
    mesh_new = (mesh_rows + jnp.dot(update, out_w, preferred_element_type=jnp.float32)).astype(
        jnp.bfloat16
    )
    grad_out = jnp.dot(update.T, cot, preferred_element_type=jnp.float32)
    grad_update = jnp.dot(cot, out_w.T, preferred_element_type=jnp.float32)
    grad_pre_up = (grad_update * silu_slope(pre_up)).astype(jnp.bfloat16)
    grad_up = jnp.dot(normed.T, grad_pre_up, preferred_element_type=jnp.float32)
    grad_normed = jnp.dot(grad_pre_up, up_w.T, preferred_element_type=jnp.float32)
    grad_gain = jnp.sum(grad_normed * qhat, axis=0)
    grad_qhat = grad_normed * gain
    grad_q = rinv * (grad_qhat - qhat * jnp.mean(grad_qhat * qhat, axis=1, keepdims=True))
    mesh_latent_gradient = cot.astype(jnp.float32) + grad_q
    grad_aggregate = grad_q.astype(jnp.bfloat16).reshape(mesh_blocks, block, latent)
    selected_entries = grad_aggregate[edge_dst]
    backward_result = jnp.einsum(
        "woi,won->win", weight_entries, selected_entries, preferred_element_type=jnp.float32
    )
    spread = jnp.zeros((tile_rows * pieces, half_block, latent), jnp.float32)
    spread = (
        spread.at[first]
        .add(backward_result[:, :half_block])
        .at[first + 1]
        .add(backward_result[:, half_block:])
    )
    spread = spread.reshape(tile_rows, tile_cols + block, latent)
    west_rim = spread[:, :half_block]
    east_rim = spread[:, half_block + tile_cols :]
    middle = spread[:, half_block : half_block + tile_cols]
    from_east = passed_along(west_rim.astype(jnp.bfloat16), "lon", -1).astype(west_rim.dtype)
    from_west = passed_along(east_rim.astype(jnp.bfloat16), "lon", 1).astype(east_rim.dtype)
    middle = middle.at[:, tile_cols - half_block :].add(from_east).at[:, :half_block].add(from_west)
    grad_message_b = middle.reshape(-1, latent).astype(jnp.bfloat16)
    grad_message = jnp.dot(hidden_own.T, grad_message_b, preferred_element_type=jnp.float32)
    grad_hidden = jnp.dot(grad_message_b, message_w.T, preferred_element_type=jnp.float32)
    grad_pre = (grad_hidden * silu_slope(pre_own)).astype(jnp.bfloat16)
    grad_embed = jnp.dot(
        grid_in.reshape(-1, features).T, grad_pre, preferred_element_type=jnp.float32
    )
    totals = lax.psum((grad_embed, grad_message, grad_up, grad_out, grad_gain), ("lon", "lat"))
    return (mesh_new, mesh_latent_gradient, totals[0], totals[1], totals[2], totals[3], totals[4])


def solution(mesh):
    return jax.shard_map(
        on_device,
        mesh=mesh,
        in_specs=(
            P(("grp", "lat"), "lon", None),
            P(("grp", "lon", "lat"), None),
            P(("grp", "lon", "lat"), None, None),
            P(("grp", "lon", "lat")),
            P(("grp", "lon", "lat")),
            P(("grp", "lon", "lat")),
            P(),
            P(),
            P(),
            P(),
            P(),
            P(("grp", "lon", "lat"), None),
        ),
        out_specs=(
            P(("grp", "lon", "lat"), None),
            P(("grp", "lon", "lat"), None),
            P("grp", None),
            P("grp", None),
            P("grp", None),
            P("grp", None),
            P("grp"),
        ),
        check_vma=False,
    )
```

profile of v0, /device:TPU:0, one launch (start us, length us, event | category | flops | bytes accessed | tf_op | source)
XLA Modules:
  0.0 262.6 jit_solution(3447000385697528091)
XLA Ops:
  9.7 3.9 %multiply_convert_fusion.1 = (bf16[2048,512]{1,0:T(8,128)(2,1)S(1)}, f32[2048,512]{1,0:T(8,128)}) fusion(bf16[2048,474]{0,1:T(8,128)(2,1)S(1)} %bitcast.53, bf16[474,512]{1,0:T(8,128)(2,1)S(1)} %copy-done.13), kind=kOutput, calls=%fused_computation.12 | convolution fusion | flops 999292928 | bytes 8718336 | tf_op jit(solution)/shard_map/dot_general | solution.py:37
  14.9 3.1 %collective-permute-start = (bf16[8,64,512]{2,1,0:T(8,128)(2,1)S(1)}, bf16[8,64,512]{2,1,0:T(8,128)(2,1)S(1)}, u32[]{:S(2)}, u32[]{:S(2)}) collective-permute-start(bf16[8,64,512]{2,1,0:T(8,128)(2,1)S(1)} %get-tuple-element.45), channel_id=1, source_target_pairs={{0,4},{4,8},{8,12},{12,0},{1,5},{5,9},{9,13},{13,1},{2,6},{6,10},{... | collective-permute-start | bytes 1572872 | tf_op jit(solution)/shard_map/ppermute | solution.py:16
  20.9 12.0 %collective-permute-done = bf16[8,64,512]{2,1,0:T(8,128)(2,1)S(1)} collective-permute-done((bf16[8,64,512]{2,1,0:T(8,128)(2,1)S(1)}, bf16[8,64,512]{2,1,0:T(8,128)(2,1)S(1)}, u32[]{:S(2)}, u32[]{:S(2)}) %collective-permute-start) | collective-permute-done | bytes 524320 | tf_op jit(solution)/shard_map/ppermute | solution.py:16
  32.9 9.8 %collective-permute-done.1 = bf16[8,64,512]{2,1,0:T(8,128)(2,1)S(1)} collective-permute-done((bf16[8,64,512]{2,1,0:T(8,128)(2,1)S(1)}, bf16[8,64,512]{2,1,0:T(8,128)(2,1)S(1)}, u32[]{:S(2)}, u32[]{:S(2)}) %collective-permute-start.1) | collective-permute-done | bytes 524320 | tf_op jit(solution)/shard_map/ppermute | solution.py:18
  44.4 2.6 gather_fusion.1
  47.0 3.9 %gather_fusion = bf16[32,64,512]{2,1,0:T(8,128)(2,1)} fusion(bf16[48,64,512]{2,1,0:T(8,128)(2,1)} %bitcast.47, s32[1024]{0:T(1024)S(1)} %pad_clamp_fusion.2), kind=kCustom, calls=%fused_computation | custom fusion | bytes 4194432 | tf_op jit(solution)/shard_map/gather | solution.py:71
  50.9 3.2 %fusion.2 = f32[32,128,512]{2,1,0:T(8,128)S(1)} fusion(bf16[32,64,512]{2,1,0:T(8,128)(2,1)S(1)} %gather_fusion.1, bf16[32,64,512]{2,1,0:T(8,128)(2,1)} %gather_fusion, bf16[32,128,128]{2,1,0:T(8,128)(2,1)} %param.18, bf16[32]{0:T(256)(128)(2,1)S(1)} %compare_convert_fusion), kind=kOutput, calls=%fused_computation.7 | convolution fusion | flops 545783808 | bytes 13631552 | tf_op jit(solution)/shard_map/yjc,ycz->yjz/dot_general | solution.py:74
  54.2 7.5 %fusion = f32[2,128,512]{2,0,1:T(2,128)S(1)} fusion(f32[32,128,512]{2,1,0:T(8,128)S(1)} %fusion.2, s32[32]{0:T(128)S(1)} %copy-done.10), kind=kOutput, calls=%fused_computation.5 | convolution fusion | flops 50331712 | bytes 8913024 | tf_op jit(solution)/shard_map/gb,bmd->gmd/dot_general | solution.py:78
  64.2 2.8 %gather_fusion.2 = bf16[32,128,512]{2,1,0:T(8,128)(2,1)} fusion(bf16[2,128,512]{2,1,0:T(8,128)(2,1)S(1)} %bitcast.45, s32[1024]{0:T(1024)S(1)} %pad_clamp_fusion), kind=kCustom, calls=%fused_computation.2 | custom fusion | bytes 8388736 | tf_op jit(solution)/shard_map/gather | solution.py:101
  67.0 3.8 %fusion.10 = f32[32,128,512]{2,1,0:T(8,128)S(1)} fusion(bf16[32,128,512]{2,1,0:T(8,128)(2,1)} %gather_fusion.2, bf16[32,128,128]{2,1,0:T(8,128)(2,1)S(1)} %copy-done.1, bf16[32]{0:T(256)(128)(2,1)S(1)} %compare_convert_fusion), kind=kOutput, calls=%fused_computation.25 | convolution fusion | flops 537395200 | bytes 13631552 | tf_op jit(solution)/shard_map/woi,won->win/dot_general | solution.py:102
  70.8 4.4 %fusion.27 = (f32[32,64,512]{2,1,0:T(8,128)}, f32[32,64,512]{2,1,0:T(8,128)}) fusion(f32[32,128,512]{2,1,0:T(8,128)S(1)} %fusion.10), kind=kLoop, calls=%fused_computation.62 | loop fusion | bytes 16777216 | tf_op jit(solution)/shard_map/slice | solution.py:110
  75.2 3.5 %broadcast_in_dim.10 = f32[48,64,512]{2,1,0:T(8,128)} broadcast(f32[]{:T(128)} %constant.95.clone.1), dimensions={} | broadcast | bytes 6291460 | tf_op jit(solution)/shard_map/broadcast_in_dim | solution.py:105
  78.7 9.9 %scatter_fusion = f32[48,64,512]{2,1,0:T(8,128)} fusion(f32[48,64,512]{2,1,0:T(8,128)} %broadcast_in_dim.10, s32[32]{0:T(128)S(1)} %get-tuple-element.39, f32[32,64,512]{2,1,0:T(8,128)} %get-tuple-element.42), kind=kCustom, calls=%fused_computation.3 | custom fusion | flops 1048576 | bytes 12583040 | tf_op jit(solution)/shard_map/scatter-add | solution.py:108
  88.6 10.0 %scatter_fusion.1 = f32[48,64,512]{2,1,0:T(8,128)} fusion(f32[48,64,512]{2,1,0:T(8,128)} %scatter_fusion, s32[32]{0:T(128)S(1)} %compare_select_fusion.1, f32[32,64,512]{2,1,0:T(8,128)} %get-tuple-element.41), kind=kCustom, calls=%fused_computation.4 | custom fusion | flops 1048576 | bytes 12583040 | tf_op jit(solution)/shard_map/scatter-add | solution.py:110
  98.5 3.4 %bitcast_convert_fusion = bf16[8,384,512]{2,1,0:T(8,128)(2,1)S(1)} fusion(f32[8,384,512]{2,1,0:T(8,128)} %bitcast.40), kind=kLoop, calls=%fused_computation.56 | loop fusion | flops 1572864 | bytes 9437184 | tf_op jit(solution)/shard_map/convert.1
  102.0 2.2 collective-permute-start.2
  107.8 8.8 %collective-permute-done.2 = bf16[8,64,512]{2,1,0:T(8,128)(2,1)S(1)} collective-permute-done((bf16[8,64,512]{2,1,0:T(8,128)(2,1)S(1)}, bf16[8,64,512]{2,1,0:T(8,128)(2,1)S(1)}, u32[]{:S(2)}, u32[]{:S(2)}) %collective-permute-start.2) | collective-permute-done | bytes 524320 | tf_op jit(solution)/shard_map/ppermute | solution.py:27
  116.8 10.7 %collective-permute-done.3 = bf16[8,64,512]{2,1,0:T(8,128)(2,1)S(1)} collective-permute-done((bf16[8,64,512]{2,1,0:T(8,128)(2,1)S(1)}, bf16[8,64,512]{2,1,0:T(8,128)(2,1)S(1)}, u32[]{:S(2)}, u32[]{:S(2)}) %collective-permute-start.3) | collective-permute-done | bytes 524320 | tf_op jit(solution)/shard_map/ppermute | solution.py:27
  128.1 2.2 fusion.30
  130.3 6.7 %convolution_bitcast_fusion = f32[474,512]{1,0:T(8,128)} fusion(bf16[2048,474]{0,1:T(8,128)(2,1)} %bitcast.54, f32[2048,512]{1,0:T(8,128)} %get-tuple-element.50, bf16[2048,512]{1,0:T(8,128)(2,1)S(1)} %bitcast.52, bf16[512,512]{1,0:T(8,128)(2,1)S(1)} %copy-done), kind=kOutput, calls=%fused_computation.16 | convolution fusion | flops 2077229056 | bytes 9728000 | tf_op jit(solution)/shard_map/dot_general | solution.py:123
  137.0 34.1 %psum.39 = f32[512]{0:T(512)} all-reduce(f32[512]{0:T(512)S(1)} %get-tuple-element.31), channel_id=1, replica_groups=mesh['grp'=2,'lon'=4,'lat'=4] {'lon','lat'}, use_global_device_ids=true, to_apply=%region_9.10 | all-reduce | flops 512 | bytes 4096 | tf_op jit(solution)/shard_map/psum | solution.py:126
  173.2 76.1 %all-reduce.3.cloned.1.call-done = (f32[474,512]{1,0:T(8,128)}, f32[512,512]{1,0:T(8,128)}, f32[512,512]{1,0:T(8,128)}, f32[512,512]{1,0:T(8,128)}) async-done(((f32[474,512]{1,0:T(8,128)}, f32[512,512]{1,0:T(8,128)}, f32[512,512]{1,0:T(8,128)}, f32[512,512]{1,0:T(8,128)}), (f32[474,512]{1,0:T(8,128)}, f32[512,512]{1,0:T(8,128)}, f32[512,512]{1,0:T(8,128)}, ...) | async-done | bytes 4116496 | tf_op jit(solution)/shard_map/psum | solution.py:126
  249.2 2.4 copy.36
  251.6 2.3 copy.37
  (70 shorter events, 18.7 us)
Async XLA Ops:
  7.2 6.3 %copy-start = (bf16[512,512]{1,0:T(8,128)(2,1)S(1)}, bf16[512,512]{1,0:T(8,128)(2,1)}, u32[]{:S(2)}) copy-start(bf16[512,512]{1,0:T(8,128)(2,1)} %param.23) | copy-start | bytes 1572868
  7.2 2.5 copy-start.13
  7.2 242.0 %all-reduce.3.cloned.1.call-start = ((), (), s32[]{:S(2)}) async-start(), calls=%async_computation | async-start | bytes 8257536 | tf_op jit(solution)/shard_map/psum | solution.py:126
  9.6 3.9 %copy-start.3 = (bf16[60,8,8,256]{3,1,2,0:T(8,128)(2,1)}, bf16[60,8,8,256]{3,1,2,0:T(8,128)(2,1)S(1)}, u32[]{:S(2)}) copy-start(bf16[60,8,8,256]{3,1,2,0:T(8,128)(2,1)S(1)} %copy.24) | copy-start | bytes 5898244
  13.5 1.3 copy-start.14
  13.5 7.3 %copy-start.10 = (s32[32]{0:T(128)S(1)}, s32[32]{0:T(128)}, u32[]{:S(2)}) copy-start(s32[32]{0:T(128)} %param.20) | copy-start | bytes 388
  13.5 7.3 %copy-start.11 = (s32[32]{0:T(128)S(1)}, s32[32]{0:T(128)}, u32[]{:S(2)}) copy-start(s32[32]{0:T(128)} %param.19) | copy-start | bytes 388
  14.9 17.9 %collective-permute-start = (bf16[8,64,512]{2,1,0:T(8,128)(2,1)S(1)}, bf16[8,64,512]{2,1,0:T(8,128)(2,1)S(1)}, u32[]{:S(2)}, u32[]{:S(2)}) collective-permute-start(bf16[8,64,512]{2,1,0:T(8,128)(2,1)S(1)} %get-tuple-element.45), channel_id=1, source_target_pairs={{0,4},{4,8},{8,12},{12,0},{1,5},{5,9},{9,13},{13,1},{2,6},{6,10},{... | collective-permute-start | bytes 1572872 | tf_op jit(solution)/shard_map/ppermute | solution.py:16
  18.0 24.6 %collective-permute-start.1 = (bf16[8,64,512]{2,1,0:T(8,128)(2,1)S(1)}, bf16[8,64,512]{2,1,0:T(8,128)(2,1)S(1)}, u32[]{:S(2)}, u32[]{:S(2)}) collective-permute-start(bf16[8,64,512]{2,1,0:T(8,128)(2,1)S(1)} %get-tuple-element.46), channel_id=1, source_target_pairs={{4,0},{8,4},{12,8},{0,12},{5,1},{9,5},{13,9},{1,13},{6,2},{10,6},{... | collective-permute-start | bytes 1572872 | tf_op jit(solution)/shard_map/ppermute | solution.py:18
  54.1 7.7 %copy-start.6 = (bf16[256,512]{1,0:T(8,128)(2,1)S(1)}, bf16[256,512]{1,0:T(8,128)(2,1)}, u32[]{:S(2)}) copy-start(bf16[256,512]{1,0:T(8,128)(2,1)} %param.17) | copy-start | bytes 786436
  54.1 7.9 %copy-start.2 = (bf16[512,512]{1,0:T(8,128)(2,1)S(1)}, bf16[512,512]{1,0:T(8,128)(2,1)}, u32[]{:S(2)}) copy-start(bf16[512,512]{1,0:T(8,128)(2,1)} %param.24) | copy-start | bytes 1572868
  54.1 7.9 %copy-start.9 = (f32[512]{0:T(512)S(1)}, f32[512]{0:T(512)}, u32[]{:S(2)}) copy-start(f32[512]{0:T(512)} %param.26) | copy-start | bytes 6148
  54.2 8.2 %copy-start.7 = (bf16[256,512]{1,0:T(8,128)(2,1)S(1)}, bf16[256,512]{1,0:T(8,128)(2,1)}, u32[]{:S(2)}) copy-start(bf16[256,512]{1,0:T(8,128)(2,1)} %param.27) | copy-start | bytes 786436
  54.2 8.2 %copy-start.12 = (bf16[512,512]{1,0:T(8,128)(2,1)S(1)}, bf16[512,512]{1,0:T(8,128)(2,1)}, u32[]{:S(2)}) copy-start(bf16[512,512]{1,0:T(8,128)(2,1)} %param.25) | copy-start | bytes 1572868
  64.2 2.8 %copy-start.1 = (bf16[32,128,128]{2,1,0:T(8,128)(2,1)S(1)}, bf16[32,128,128]{2,1,0:T(8,128)(2,1)}, u32[]{:S(2)}) copy-start(bf16[32,128,128]{2,1,0:T(8,128)(2,1)} %param.18) | copy-start | bytes 3145732
  98.5 5.7 %slice-start = ((s8[6291456]{0:T(1024)(128)(4,1)}), s8[4194304]{0:T(1024)(128)(4,1)S(1)}, s32[]{:S(2)}) async-start(s8[6291456]{0:T(1024)(128)(4,1)} %bitcast.41), calls=%async_computation.1 | async-start | bytes 8388608
  98.5 5.7 %slice-start.1 = ((s8[6291456]{0:T(1024)(128)(4,1)}), s8[2097152]{0:T(1024)(128)(4,1)S(1)}, s32[]{:S(2)}) async-start(s8[6291456]{0:T(1024)(128)(4,1)} %bitcast.41), calls=%async_computation.2 | async-start | bytes 4194304
  102.0 14.6 %collective-permute-start.2 = (bf16[8,64,512]{2,1,0:T(8,128)(2,1)S(1)}, bf16[8,64,512]{2,1,0:T(8,128)(2,1)S(1)}, u32[]{:S(2)}, u32[]{:S(2)}) collective-permute-start(bf16[8,64,512]{2,1,0:T(8,128)(2,1)S(1)} %get-tuple-element.44), channel_id=1, source_target_pairs={{0,12},{4,0},{8,4},{12,8},{1,13},{5,1},{9,5},{13,9},{2,14},{6,2},{... | collective-permute-start | bytes 1572872 | tf_op jit(solution)/shard_map/ppermute | solution.py:27
  104.2 2.3 copy-start.8
  104.7 22.8 %collective-permute-start.3 = (bf16[8,64,512]{2,1,0:T(8,128)(2,1)S(1)}, bf16[8,64,512]{2,1,0:T(8,128)(2,1)S(1)}, u32[]{:S(2)}, u32[]{:S(2)}) collective-permute-start(bf16[8,64,512]{2,1,0:T(8,128)(2,1)S(1)} %get-tuple-element.43), channel_id=1, source_target_pairs={{0,4},{4,8},{8,12},{12,0},{1,5},{5,9},{9,13},{13,1},{2,6},{6,10},{... | collective-permute-start | bytes 1572872 | tf_op jit(solution)/shard_map/ppermute | solution.py:27
  116.8 11.2 %copy-start.15 = (bf16[2048,512]{1,0:T(8,128)(2,1)S(1)}, bf16[2048,512]{1,0:T(8,128)(2,1)}, u32[]{:S(2)}) copy-start(bf16[2048,512]{1,0:T(8,128)(2,1)} %copy-done.14) | copy-start | bytes 6291460
  249.2 4.6 %copy-start.5 = (f32[512,512]{1,0:T(8,128)S(1)}, f32[512,512]{1,0:T(8,128)}, u32[]{:S(2)}) copy-start(f32[512,512]{1,0:T(8,128)} %get-tuple-element.57) | copy-start | bytes 3145732
  249.2 5.6 %copy-start.4 = (f32[512,512]{1,0:T(8,128)S(1)}, f32[512,512]{1,0:T(8,128)}, u32[]{:S(2)}) copy-start(f32[512,512]{1,0:T(8,128)} %get-tuple-element.58) | copy-start | bytes 3145732
Sparse Core Ops, SparseCore 0:
  137.1 112.0 all-reduce.2
where the time goes:
time: 263 us
  waiting for transfers between devices  117 us (44%)
  matrix products  34.5 us (13%)
  blocking collectives  34.1 us (13%)
  local copies, waits for them, and re-layouts  26.9 us (10%)
  other arithmetic  26.9 us (10%)
  between operations  15 us (6%)
  starting transfers between devices  7.84 us (3%)
    psum x1, waiting for transfers between devices, on_device(): lax.psum((grad_embed, grad_message, grad_up, grad_out, grad_gain), ('lon'...  76.1 us
    psum x1, blocking collectives, on_device(): lax.psum((grad_embed, grad_message, grad_up, grad_out, grad_gain), ('lon'...  34.1 us
    scatter-add x2, other arithmetic, on_device(): spread = spread.at[first].add(backward_result[:, :half_block]).at[first +...  19.9 us
    ppermute x2, waiting for transfers between devices, passed_along(): lax.ppermute(value, axis, [(i, (i + by) % length) for i in range(length)])  19.5 us
    ppermute x1, waiting for transfers between devices, extended_2(): lax.ppermute(tail, axis, [(i, (i + 1) % count) for i in range(count)])  12 us
    ppermute x1, waiting for transfers between devices, extended_2(): lax.ppermute(head, axis, [((i + 1) % count, i) for i in range(count)])  9.79 us
    unnamed x42, local copies, waits for them, and re-layouts  9.08 us
    dot_general x1, matrix products, on_device(): jnp.einsum('gb,bmd->gmd', onehot, product_terms, precision=lax.Precision....  7.52 us
  transfers between devices with their start and end apart: 5, of which 5 were waited for; matrix products, arithmetic and copies ran while one was open for 2% of the time, Pallas kernels for 0%

commit v1 on v0

v1 whole, which is shorter than its diff:
```python
import jax
import jax.numpy as jnp
from jax import lax
from jax.experimental import pallas as pl
from jax.experimental.pallas import tpu as pltpu
from jax.sharding import PartitionSpec as P

epsilon = 1e-05
BF = jnp.bfloat16
F32 = jnp.float32
VMEM_BYTES = 48 * 1024 * 1024


def contract(a, b, dim_a, dim_b):
    return lax.dot_general(a, b, (((dim_a,), (dim_b,)), ((), ())), preferred_element_type=F32)


def silu_pair(pre):
    sigma = jax.nn.sigmoid(pre)
    return pre * sigma, sigma * (1.0 + pre * (1.0 - sigma))


def own_kernel(src, dst, count, grid, embed_w, edge_w, cot, out_w, a_halo, a_t, h_own, slope, x_t, grad_update, acc):
    rows, cols, features = grid.shape
    block = edge_w.shape[1]
    half = block // 2
    own_blocks = cols // block
    windows = 2 * own_blocks + 1
    nodes = acc.shape[1]
    acc[...] = jnp.zeros(acc.shape, F32)
    lane = lax.broadcasted_iota(jnp.int32, (block, block), 1)

    def slot(b, carry):
        source = src[b]
        row = source // windows
        window = source - row * windows
        at = window // 2
        target = pl.ds(pl.multiple_of(dst[b] * block, block), block)
        weights = edge_w[b].astype(F32)

        @pl.when(window % 2 == 1)
        def _():
            acc[row * own_blocks + at, target, :] += weights

        @pl.when(window % 2 == 0)
        def _():
            halo_block = rows * own_blocks + row
            turned = pltpu.roll(weights, half, 1)
            first = jnp.where(at == 0, halo_block, row * own_blocks + at - 1)
            second = jnp.where(at == own_blocks, halo_block, row * own_blocks + at)
            acc[first, target, :] += jnp.where(lane >= half, turned, 0.0)
            acc[second, target, :] += jnp.where(lane < half, turned, 0.0)

        return carry

    lax.fori_loop(0, count[0], slot, 0)
    total = jnp.zeros(h_own.shape, F32)
    for r in range(rows):
        part = jnp.concatenate([acc[r * own_blocks + k] for k in range(own_blocks)], axis=1)
        a_t[r * cols : (r + 1) * cols, :] = part.T.astype(BF)
        inputs = grid[r]
        pre = contract(inputs, embed_w[...], 1, 0)
        hidden, hidden_slope = silu_pair(pre)
        slope[r * cols : (r + 1) * cols, :] = hidden_slope.astype(BF)
        total += contract(part.astype(BF), hidden.astype(BF), 1, 0)
        x_t[:, r * cols : (r + 1) * cols] = inputs.T
    h_own[...] = total
    base = rows * own_blocks
    for r in range(rows):
        part = acc[base + r]
        a_halo[:, r * block : (r + 1) * block] = part.astype(BF)
        a_t[(base + r) * block : (base + r + 1) * block, :] = part.T.astype(BF)
    grad_update[...] = contract(cot[...], out_w[...], 1, 1)


def mesh_kernel(
    me, east, west, a_halo, h_own, embed_w, message_w, up_w, out_w, gain, mesh_lat, cot, grad_update,
    mesh_new, mesh_grad, grads, grad_gain, back, slope, x_t, stack,
):
    rows, half, features = east.shape
    latent = message_w.shape[0]
    total = h_own[...]
    for r in range(rows):
        at = slice(r * 2 * half, (r + 1) * 2 * half)
        inputs = jnp.concatenate([east[r], west[r]], axis=0)
        x_t[:, at] = inputs.T
        hidden, hidden_slope = silu_pair(contract(inputs, embed_w[...], 1, 0))
        slope[at, :] = hidden_slope.astype(BF)
        total += contract(a_halo[:, at], hidden.astype(BF), 1, 0)
    gathered = total.astype(BF)
    mesh_rows = mesh_lat[...].astype(F32)
    summed = mesh_rows + contract(gathered, message_w[...], 1, 0)
    rinv = lax.rsqrt(jnp.mean(summed * summed, axis=1, keepdims=True) + epsilon)
    qhat = summed * rinv
    gains = gain[...]
    normed = (qhat * gains).astype(BF)
    pre_up = contract(normed, up_w[...], 1, 0)
    silu_up, up_slope = silu_pair(pre_up)
    update = silu_up.astype(BF)
    grad_pre_up = (grad_update[...] * up_slope).astype(BF)
    grad_normed = contract(grad_pre_up, up_w[...], 1, 1)
    grad_gain[...] = jnp.sum(grad_normed * qhat, axis=0, keepdims=True)
    grad_qhat = grad_normed * gains
    grad_q = rinv * (grad_qhat - qhat * jnp.mean(grad_qhat * qhat, axis=1, keepdims=True))
    grad_aggregate = grad_q.astype(BF)
    back[...] = contract(grad_aggregate, message_w[...], 1, 1).astype(BF)
    mesh_grad[...] = cot[...].astype(F32) + grad_q
    mesh_new[...] = (mesh_rows + contract(update, out_w[...], 1, 0)).astype(BF)
    stack[:latent, :] = contract(gathered, grad_aggregate, 0, 0).astype(BF)
    stack[latent : 2 * latent, :] = contract(normed, grad_pre_up, 0, 0).astype(BF)
    stack[2 * latent :, :] = contract(update, cot[...], 0, 0).astype(BF)
    parts, count, size, _ = grads.shape
    for p in range(parts):
        for j in range(count):
            at = pl.multiple_of((p * count + (me[p] ^ j)) * size, 16)
            grads[p, j] = stack[pl.ds(at, size), :]


def grid_kernel(me, back, a_t, slope_own, slope_halo, x_t_own, x_t_halo, grad_gain, grads, total):
    step = pl.program_id(0)
    steps = pl.num_programs(0)
    features = x_t_own.shape[0]

    def term(slope, x_t):
        hidden = contract(a_t[...], back[...], 1, 0)
        grad_pre = (hidden * slope[...].astype(F32)).astype(BF)
        return contract(x_t[...], grad_pre, 1, 0)

    @pl.when(step == 0)
    def _():
        total[...] = jnp.zeros(total.shape, F32)
        total[features : features + 1, :] = grad_gain[...]

    @pl.when(step < steps - 2)
    def _():
        total[:features, :] += term(slope_own, x_t_own)

    @pl.when(step >= steps - 2)
    def _():
        total[:features, :] += term(slope_halo, x_t_halo)

    @pl.when(step == steps - 1)
    def _():
        parts, count, size, _ = grads.shape
        for p in range(parts):
            for j in range(count):
                at = pl.multiple_of((p * count + (me[p] ^ j)) * size, 8)
                grads[p, j] = total[pl.ds(at, size), :].astype(BF)


def order_kernel(me, kept, got, *outs):
    parts, half, size, latent = kept.shape
    count = 2 * half
    rows = outs[0].shape[0]
    pieces = []
    for p in range(parts):
        top = (me[p] >= half).astype(jnp.int32)
        low = me[p] & (half - 1)
        for a in range(count):
            mine = kept[p, (a & (half - 1)) ^ low]
            theirs = got[p, (a & (half - 1)) ^ low]
            chunk = jnp.where(top == a // half, mine, theirs).astype(F32)
            first = (p * count + a) * size
            pieces.append((first, chunk))
    for first, chunk in pieces:
        start = 0
        for out in outs:
            low = max(first, start)
            high = min(first + size, start + out.shape[0])
            if low < high:
                out[low - start : high - start, :] = chunk[low - first : high - first]
            start += out.shape[0]


SMEM = pl.BlockSpec(memory_space=pltpu.SMEM)
VMEM = pl.BlockSpec(memory_space=pltpu.VMEM)


def bits(axis):
    return [(axis, 1 << k) for k in range(lax.axis_size(axis).bit_length() - 1)]


def swapped(value, axis, bit):
    return lax.ppermute(value, axis, [(i, i ^ bit) for i in range(lax.axis_size(axis))])


def chunk_count(steps, rows):
    count = 1
    while count < 2 ** len(steps) and rows % (32 * count) == 0:
        count *= 2
    return count


def place(steps, count):
    used = steps[: count.bit_length() - 1]
    me = jnp.int32(0)
    for axis, bit in used:
        me = 2 * me + ((lax.axis_index(axis) & bit) != 0).astype(jnp.int32)
    return me


def summed_over(chunks, steps):
    acc = chunks
    halved = []
    for axis, bit in steps:
        if acc.shape[0] > 1:
            half = acc.shape[0] // 2
            got = swapped(acc[half:], axis, bit)
            acc = (acc[:half].astype(F32) + got.astype(F32)).astype(BF)
            halved.append((axis, bit))
        else:
            acc = (acc.astype(F32) + swapped(acc, axis, bit).astype(F32)).astype(BF)
    for axis, bit in halved[:0:-1]:
        acc = jnp.concatenate([acc, swapped(acc, axis, bit)], axis=0)
    return acc, swapped(acc, *halved[0])


def on_device(grid_in, mesh_lat, edge_w, edge_src, edge_dst, block_count, embed_w, message_w, up_w, out_w, gain, cot):
    rows, cols, features = grid_in.shape
    latent = message_w.shape[0]
    slots, block, _ = edge_w.shape
    half = block // 2
    nodes = mesh_lat.shape[0]
    own = rows * cols
    halo = rows * block
    blocks = (own + halo) // block
    params = pltpu.CompilerParams(vmem_limit_bytes=VMEM_BYTES)

    count = lax.axis_size("lon")
    east = lax.ppermute(grid_in[:, :half], "lon", [((i + 1) % count, i) for i in range(count)])
    west = lax.ppermute(grid_in[:, cols - half :], "lon", [(i, (i + 1) % count) for i in range(count)])

    shape = jax.ShapeDtypeStruct
    a_halo, a_t, h_own, slope_own, x_t_own, grad_update = pl.pallas_call(
        own_kernel,
        name="own_points",
        in_specs=[SMEM] * 3 + [VMEM] * 5,
        out_specs=[VMEM] * 6,
        out_shape=[
            shape((nodes, halo), BF),
            shape((own + halo, nodes), BF),
            shape((nodes, latent), F32),
            shape((own, latent), BF),
            shape((features, own), BF),
            shape((nodes, latent), F32),
        ],
        scratch_shapes=[pltpu.VMEM((blocks, nodes, block), F32)],
        compiler_params=params,
        cost_estimate=pl.CostEstimate(flops=4_000_000_000, bytes_accessed=14_000_000, transcendentals=2_000_000),
    )(edge_src, edge_dst, block_count, grid_in, embed_w, edge_w, cot, out_w)

    lat_bits, lon_bits = bits("lat"), bits("lon")
    x_first = lat_bits + lon_bits
    z_first = lat_bits[:1] + lon_bits + lat_bits[1:]
    orders = (x_first, z_first)
    mesh_count = chunk_count(x_first, 3 * latent // 2)
    mesh_me = jnp.stack([place(order, mesh_count) for order in orders])
    mesh_new, mesh_grad, mesh_terms, gain_term, back, slope_halo, x_t_halo = pl.pallas_call(
        mesh_kernel,
        name="mesh_nodes",
        in_specs=[SMEM] + [VMEM] * 12,
        out_specs=[VMEM] * 7,
        out_shape=[
            shape((nodes, latent), BF),
            shape((nodes, latent), F32),
            shape((2, mesh_count, 3 * latent // 2 // mesh_count, latent), BF),
            shape((1, latent), F32),
            shape((nodes, latent), BF),
            shape((halo, latent), BF),
            shape((features, halo), BF),
        ],
        scratch_shapes=[pltpu.VMEM((3 * latent, latent), BF)],
        compiler_params=params,
        cost_estimate=pl.CostEstimate(flops=2_500_000_000, bytes_accessed=10_000_000, transcendentals=1_000_000),
    )(
        mesh_me, east, west, a_halo, h_own, embed_w, message_w, up_w, out_w, gain.reshape(1, latent),
        mesh_lat, cot, grad_update,
    )

    padded = -(-(features + 1) // 128) * 128
    embed_count = chunk_count(x_first, padded)
    embed_me = jnp.stack([place(x_first, embed_count)])
    tile = halo // 2
    own_steps = own // tile
    steps = own_steps + 2
    embed_terms = pl.pallas_call(
        grid_kernel,
        name="grid_points",
        grid_spec=pltpu.PrefetchScalarGridSpec(
            num_scalar_prefetch=1,
            grid=(steps,),
            in_specs=[
                pl.BlockSpec((nodes, latent), lambda i, me: (0, 0)),
                pl.BlockSpec((tile, nodes), lambda i, me: (i, 0)),
                pl.BlockSpec((tile, latent), lambda i, me: (jnp.minimum(i, own_steps - 1), 0)),
                pl.BlockSpec((tile, latent), lambda i, me: (jnp.maximum(i - own_steps, 0), 0)),
                pl.BlockSpec((features, tile), lambda i, me: (0, jnp.minimum(i, own_steps - 1))),
                pl.BlockSpec((features, tile), lambda i, me: (0, jnp.maximum(i - own_steps, 0))),
                pl.BlockSpec((1, latent), lambda i, me: (0, 0)),
            ],
            out_specs=pl.BlockSpec((1, embed_count, padded // embed_count, latent), lambda i, me: (0, 0, 0, 0)),
            scratch_shapes=[pltpu.VMEM((padded, latent), F32)],
        ),
        out_shape=shape((1, embed_count, padded // embed_count, latent), BF),
        compiler_params=params,
        cost_estimate=pl.CostEstimate(flops=2_400_000_000, bytes_accessed=9_000_000, transcendentals=0),
    )(embed_me, back, a_t, slope_own, slope_halo, x_t_own, x_t_halo, gain_term)

    pairs = [summed_over(mesh_terms[k], order) for k, order in enumerate(orders)]
    embed_pair = summed_over(embed_terms[0], x_first)

    def ordered(me, pairs, row_counts):
        kept = jnp.stack([pair[0] for pair in pairs])
        got = jnp.stack([pair[1] for pair in pairs])
        return pl.pallas_call(
            order_kernel,
            name="ordered",
            in_specs=[SMEM, VMEM, VMEM],
            out_specs=[VMEM] * len(row_counts),
            out_shape=[shape((n, latent), F32) for n in row_counts],
            compiler_params=params,
            cost_estimate=pl.CostEstimate(flops=0, bytes_accessed=4_000_000, transcendentals=0),
        )(me, kept, got)

    grad_message, grad_up, grad_out = ordered(mesh_me, pairs, [latent] * 3)
    grad_embed, rest = ordered(embed_me, [embed_pair], [features, padded - features])
    return (mesh_new, mesh_grad, grad_embed, grad_message, grad_up, grad_out, rest[0])


def solution(mesh):
    tiles = ("grp", "lon", "lat")
    return jax.shard_map(
        on_device,
        mesh=mesh,
        in_specs=(
            P(("grp", "lat"), "lon", None),
            P(tiles, None),
            P(tiles, None, None),
            P(tiles),
            P(tiles),
            P(tiles),
            P(),
            P(),
            P(),
            P(),
            P(),
            P(tiles, None),
        ),
        out_specs=(
            P(tiles, None),
            P(tiles, None),
            P("grp", None),
            P("grp", None),
            P("grp", None),
            P("grp", None),
            P("grp"),
        ),
        check_vma=False,
    )
```

time: 263 us -> 109 us (0.41)
  waiting for transfers between devices: 117 us -> 40.6 us
  matrix products: 34.5 us -> 0 us
  blocking collectives: 34.1 us -> 0 us
  other arithmetic: 26.9 us -> 1.04 us
  Pallas kernels: 0 us -> 25.7 us
  starting transfers between devices: 7.84 us -> 29.9 us
  local copies, waits for them, and re-layouts: 26.9 us -> 9.96 us
  between operations: 15 us -> 1.65 us
    psum x1 -> x0, waiting for transfers between devices: 76.1 us -> none  [on_device(): lax.psum((grad_embed, grad_message, grad_up, grad_out, grad_gain), ('lon'...]
    dot_general x13 -> x0, matrix products: 34.5 us -> none  [the longest x1 7.52 us: on_device(): jnp.einsum('gb,bmd->gmd', onehot, product_terms, precision=lax.Precision....]
    psum x1 -> x0, blocking collectives: 34.1 us -> none  [on_device(): lax.psum((grad_embed, grad_message, grad_up, grad_out, grad_gain), ('lon'...]
    pallas_call x0 -> x5, Pallas kernels: none -> 25.7 us  [the longest x1 9.26 us: on_device(): pl.pallas_call(own_kernel, name='own_points', in_specs=[SMEM] * 3 + [VMEM...]
    ppermute x4 -> x26, starting transfers between devices: 7.8 us -> 29.9 us  [the longest x24 24.8 us: swapped(): lax.ppermute(value, axis, [(i, i ^ bit) for i in range(lax.axis_size(axis...]
    scatter-add x4 -> x0, other arithmetic: 20.3 us -> none  [the longest x2 19.9 us: on_device(): spread = spread.at[first].add(backward_result[:, :half_block]).at[first +...]
    gather x3 -> x0, local copies, waits for them, and re-layouts: 9.28 us -> none  [the longest x2 6.5 us: on_device(): block_groups = jnp.concatenate((halves[first], halves[first + 1]), axis=1)]
    broadcast_in_dim x1 -> x0, local copies, waits for them, and re-layouts: 3.47 us -> none  [on_device(): spread = jnp.zeros((tile_rows * pieces, half_block, latent), jnp.float32)]
  transfers between devices with their start and end apart: 5 -> 26, of which waited for: 5 -> 16; matrix products, arithmetic and copies ran while one was open for 2% -> 1% of each run, Pallas kernels for 0% -> 9%
where the time goes in v1:
time: 109 us
  waiting for transfers between devices  40.6 us (37%)
  starting transfers between devices  29.9 us (27%)
  Pallas kernels  25.7 us (24%)
  local copies, waits for them, and re-layouts  9.96 us (9%)
  between operations  1.65 us (2%)
    ppermute x24, waiting for transfers between devices, swapped(): lax.ppermute(value, axis, [(i, i ^ bit) for i in range(lax.axis_size(axis...  27.9 us
    ppermute x24, starting transfers between devices, swapped(): lax.ppermute(value, axis, [(i, i ^ bit) for i in range(lax.axis_size(axis...  24.8 us
    ppermute x1, waiting for transfers between devices, on_device(): lax.ppermute(grid_in[:, :half], 'lon', [((i + 1) % count, i) for i in ran...  9.8 us
    pallas_call x1, Pallas kernels, on_device(): pl.pallas_call(own_kernel, name='own_points', in_specs=[SMEM] * 3 + [VMEM...  9.26 us
    pallas_call x1, Pallas kernels, on_device(): pl.pallas_call(mesh_kernel, name='mesh_nodes', in_specs=[SMEM] + [VMEM] *...  7.11 us
    unnamed x27, local copies, waits for them, and re-layouts  6.83 us
    pallas_call x1, Pallas kernels, on_device(): pl.pallas_call(grid_kernel, name='grid_points', grid_spec=pltpu.PrefetchS...  5.96 us
    pallas_call x2, Pallas kernels, ordered(): pl.pallas_call(order_kernel, name='ordered', in_specs=[SMEM, VMEM, VMEM],...  3.36 us
  transfers between devices with their start and end apart: 26, of which 16 were waited for; matrix products, arithmetic and copies ran while one was open for 1% of the time, Pallas kernels for 9%

profile of v1, /device:TPU:0, one launch (start us, length us, event | category | flops | bytes accessed | tf_op | source)
XLA Modules:
  0.0 108.8 jit_solution(7709126306139847177)
XLA Ops:
  0.6 4.4 %copy.19.grid = bf16[8,256,474]{2,1,0:T(8,128)(2,1)} copy(bf16[8,256,474]{1,0,2:T(8,128)(2,1)} %param.12) | data formatting | bytes 3883008 | tf_op args[0]
  5.0 2.4 %fusion.6 = (bf16[8,64,474]{2,1,0:T(8,128)(2,1)}, bf16[8,64,474]{2,1,0:T(8,128)(2,1)}) fusion(bf16[8,256,474]{2,1,0:T(8,128)(2,1)} %copy.19.grid), kind=kLoop, calls=%fused_computation.34 | loop fusion | bytes 1941504 | tf_op jit(solution)/shard_map/slice | solution.py:231
  7.4 3.0 %collective-permute-start.1 = (bf16[8,64,474]{2,1,0:T(8,128)(2,1)}, bf16[8,64,474]{2,1,0:T(8,128)(2,1)S(1)}, u32[]{:S(2)}, u32[]{:S(2)}) collective-permute-start(bf16[8,64,474]{2,1,0:T(8,128)(2,1)} %get-tuple-element.43), channel_id=1, source_target_pairs={{0,4},{4,8},{8,12},{12,0},{1,5},{5,9},{9,13},{13,1},{2,6},{6,10},{... | collective-permute-start | bytes 1456136 | tf_op jit(solution)/shard_map/ppermute | solution.py:231
  10.5 2.0 %collective-permute-start = (bf16[8,64,474]{2,1,0:T(8,128)(2,1)}, bf16[8,64,474]{2,1,0:T(8,128)(2,1)S(1)}, u32[]{:S(2)}, u32[]{:S(2)}) collective-permute-start(bf16[8,64,474]{2,1,0:T(8,128)(2,1)} %get-tuple-element.44), channel_id=1, source_target_pairs={{4,0},{8,4},{12,8},{0,12},{5,1},{9,5},{13,9},{1,13},{6,2},{10,6},{... | collective-permute-start | bytes 1456136 | tf_op jit(solution)/shard_map/ppermute | solution.py:230
  13.3 9.3 %own_points.1 = (bf16[256,1024]{1,0:T(8,128)(2,1)S(1)}, bf16[3072,256]{1,0:T(8,128)(2,1)S(1)}, f32[256,512]{1,0:T(8,128)S(1)}, bf16[2048,512]{1,0:T(8,128)(2,1)}...) custom-call(s32[32]{0:T(128)S(1)} %copy-done.8, s32[32]{0:T(128)S(1)} %copy-done.9, s32[1]{0:T(128)S(6)} %copy.22.count, ...), custom_call_target="tpu_custom_call" | custom-call | flops 4000000000 | bytes 14000000 | tf_op jit(solution)/shard_map/own_points/pallas_call | solution.py:234
  22.6 2.9 %collective-permute-done.1.west = bf16[8,64,474]{2,1,0:T(8,128)(2,1)S(1)} collective-permute-done((bf16[8,64,474]{2,1,0:T(8,128)(2,1)}, bf16[8,64,474]{2,1,0:T(8,128)(2,1)S(1)}, u32[]{:S(2)}, u32[]{:S(2)}) %collective-permute-start.1) | collective-permute-done | bytes 485408 | tf_op jit(solution)/shard_map/ppermute | solution.py:231
  25.5 9.8 %collective-permute-done.east = bf16[8,64,474]{2,1,0:T(8,128)(2,1)S(1)} collective-permute-done((bf16[8,64,474]{2,1,0:T(8,128)(2,1)}, bf16[8,64,474]{2,1,0:T(8,128)(2,1)S(1)}, u32[]{:S(2)}, u32[]{:S(2)}) %collective-permute-start) | collective-permute-done | bytes 485408 | tf_op jit(solution)/shard_map/ppermute | solution.py:230
  35.3 7.1 %mesh_nodes.1 = (bf16[256,512]{1,0:T(8,128)(2,1)}, f32[256,512]{1,0:T(8,128)}, bf16[2,16,48,512]{3,2,1,0:T(8,128)(2,1)}, f32[1,512]{1,0:T(1,128)S(1)}, bf16[256,...) custom-call(s32[2]{0:T(128)S(1)} %pad_add_fusion.me, ...), custom_call_target="tpu_custom_call" | custom-call | flops 2500000000 | bytes 10000000 | tf_op jit(solution)/shard_map/mesh_nodes/pallas_call | solution.py:258
  44.8 6.0 %grid_points.1 = bf16[1,16,32,512]{3,2,1,0:T(8,128)(2,1)S(1)} custom-call(s32[1]{0:T(128)} %bitcast.me, bf16[256,512]{1,0:T(8,128)(2,1)S(1)} %get-tuple-element.30.back, bf16[3072,256]{1,0:T(8,128)(2,1)S(1)} %get-tuple-element.31.a_t, bf16[2048,512]{1,0:T(8,128)(2,1)} %get-tuple-element.32.slope_own, bf16[1024,512]{1,0:T(8,128)(2,1)S(1)} %copy-done.10, ...), custom_call_target="tpu_custom_call" | custom-call | flops 2400000000 | bytes 9000000 | tf_op jit(solution)/shard_map/grid_points/pallas_call | solution.py:286
  54.7 3.4 %collective-permute-done.3 = bf16[4,32,512]{2,1,0:T(8,128)(2,1)S(1)} collective-permute-done((bf16[4,32,512]{2,1,0:T(8,128)(2,1)S(1)}, bf16[4,32,512]{2,1,0:T(8,128)(2,1)S(1)}, u32[]{:S(2)}, u32[]{:S(2)}) %collective-permute-start.3) | collective-permute-done | bytes 131104 | tf_op jit(solution)/shard_map/ppermute | solution.py:184
  59.4 3.1 %collective-permute-done.4 = bf16[2,32,512]{2,1,0:T(8,128)(2,1)S(1)} collective-permute-done((bf16[2,32,512]{2,1,0:T(8,128)(2,1)S(1)}, bf16[2,32,512]{2,1,0:T(8,128)(2,1)S(1)}, u32[]{:S(2)}, u32[]{:S(2)}) %collective-permute-start.4) | collective-permute-done | bytes 65568 | tf_op jit(solution)/shard_map/ppermute | solution.py:184
  64.2 1.6 %collective-permute-start.18 = (bf16[4,48,512]{2,1,0:T(8,128)(2,1)S(1)}, bf16[4,48,512]{2,1,0:T(8,128)(2,1)S(1)}, u32[]{:S(2)}, u32[]{:S(2)}) collective-permute-start(bf16[4,48,512]{2,1,0:T(8,128)(2,1)S(1)} %slice.146), channel_id=1, source_target_pairs={{0,4},{4,0},{8,12},{12,8},{1,5},{5,1},{9,13},{13,9},{2,6},{6,2},{1... | collective-permute-start | bytes 589832 | tf_op jit(solution)/shard_map/ppermute | solution.py:184
  65.9 1.6 %collective-permute-done.5 = bf16[1,32,512]{2,1,0:T(8,128)(2,1)S(1)} collective-permute-done((bf16[1,32,512]{2,1,0:T(8,128)(2,1)S(1)}, bf16[1,32,512]{2,1,0:T(8,128)(2,1)S(1)}, u32[]{:S(2)}, u32[]{:S(2)}) %collective-permute-start.5) | collective-permute-done | bytes 32800 | tf_op jit(solution)/shard_map/ppermute | solution.py:184
  67.5 1.7 %collective-permute-start.6 = (bf16[1,32,512]{2,1,0:T(8,128)(2,1)S(1)}, bf16[1,32,512]{2,1,0:T(8,128)(2,1)S(1)}, u32[]{:S(2)}, u32[]{:S(2)}) collective-permute-start(bf16[1,32,512]{2,1,0:T(8,128)(2,1)S(1)} %add_convert_fusion.8), channel_id=1, source_target_pairs={{0,8},{4,12},{8,0},{12,4},{1,9},{5,13},{9,1},{13,5},{2,10},{6,14},... | collective-permute-start | bytes 98312 | tf_op jit(solution)/shard_map/ppermute | solution.py:184
  70.8 1.6 %collective-permute-done.6 = bf16[1,32,512]{2,1,0:T(8,128)(2,1)S(1)} collective-permute-done((bf16[1,32,512]{2,1,0:T(8,128)(2,1)S(1)}, bf16[1,32,512]{2,1,0:T(8,128)(2,1)S(1)}, u32[]{:S(2)}, u32[]{:S(2)}) %collective-permute-start.6) | collective-permute-done | bytes 32800 | tf_op jit(solution)/shard_map/ppermute | solution.py:184
  72.3 1.7 %collective-permute-start.7 = (bf16[2,32,512]{2,1,0:T(8,128)(2,1)S(1)}, bf16[2,32,512]{2,1,0:T(8,128)(2,1)S(1)}, u32[]{:S(2)}, u32[]{:S(2)}) collective-permute-start(bf16[2,32,512]{2,1,0:T(8,128)(2,1)S(1)} %pad_maximum_fusion.10), channel_id=1, source_target_pairs={{0,4},{4,0},{8,12},{12,8},{1,5},{5,1},{9,13},{13,9},{2,6},{6,2},{1... | collective-permute-start | bytes 196616 | tf_op jit(solution)/shard_map/ppermute | solution.py:184
  74.1 2.3 %collective-permute-start.19 = (bf16[2,48,512]{2,1,0:T(8,128)(2,1)S(1)}, bf16[2,48,512]{2,1,0:T(8,128)(2,1)S(1)}, u32[]{:S(2)}, u32[]{:S(2)}) collective-permute-start(bf16[2,48,512]{2,1,0:T(8,128)(2,1)S(1)} %slice.148), channel_id=1, source_target_pairs={{0,8},{4,12},{8,0},{12,4},{1,9},{5,13},{9,1},{13,5},{2,10},{6,14},... | collective-permute-start | bytes 294920 | tf_op jit(solution)/shard_map/ppermute | solution.py:184
  78.6 3.2 %collective-permute-done.19 = bf16[2,48,512]{2,1,0:T(8,128)(2,1)S(1)} collective-permute-done((bf16[2,48,512]{2,1,0:T(8,128)(2,1)S(1)}, bf16[2,48,512]{2,1,0:T(8,128)(2,1)S(1)}, u32[]{:S(2)}, u32[]{:S(2)}) %collective-permute-start.19) | collective-permute-done | bytes 98336 | tf_op jit(solution)/shard_map/ppermute | solution.py:184
  83.6 2.3 %collective-permute-done.20 = bf16[1,48,512]{2,1,0:T(8,128)(2,1)S(1)} collective-permute-done((bf16[1,48,512]{2,1,0:T(8,128)(2,1)S(1)}, bf16[1,48,512]{2,1,0:T(8,128)(2,1)S(1)}, u32[]{:S(2)}, u32[]{:S(2)}) %collective-permute-start.20) | collective-permute-done | bytes 49184 | tf_op jit(solution)/shard_map/ppermute | solution.py:184
  90.1 1.9 %collective-permute-start.22 = (bf16[2,48,512]{2,1,0:T(8,128)(2,1)S(1)}, bf16[2,48,512]{2,1,0:T(8,128)(2,1)S(1)}, u32[]{:S(2)}, u32[]{:S(2)}) collective-permute-start(bf16[2,48,512]{2,1,0:T(8,128)(2,1)S(1)} %pad_maximum_fusion.9), channel_id=1, source_target_pairs={{0,8},{4,12},{8,0},{12,4},{1,9},{5,13},{9,1},{13,5},{2,10},{6,14},... | collective-permute-start | bytes 294920 | tf_op jit(solution)/shard_map/ppermute | solution.py:184
  92.0 2.1 %collective-permute-done.14 = bf16[1,48,512]{2,1,0:T(8,128)(2,1)S(1)} collective-permute-done((bf16[1,48,512]{2,1,0:T(8,128)(2,1)S(1)}, bf16[1,48,512]{2,1,0:T(8,128)(2,1)S(1)}, u32[]{:S(2)}, u32[]{:S(2)}) %collective-permute-start.14) | collective-permute-done | bytes 49184 | tf_op jit(solution)/shard_map/ppermute | solution.py:184
  95.7 1.7 %collective-permute-start.23 = (bf16[4,48,512]{2,1,0:T(8,128)(2,1)S(1)}, bf16[4,48,512]{2,1,0:T(8,128)(2,1)S(1)}, u32[]{:S(2)}, u32[]{:S(2)}) collective-permute-start(bf16[4,48,512]{2,1,0:T(8,128)(2,1)S(1)} %pad_maximum_fusion.6), channel_id=1, source_target_pairs={{0,4},{4,0},{8,12},{12,8},{1,5},{5,1},{9,13},{13,9},{2,6},{6,2},{1... | collective-permute-start | bytes 589832 | tf_op jit(solution)/shard_map/ppermute | solution.py:184
  101.6 2.9 %collective-permute-done.16 = bf16[4,48,512]{2,1,0:T(8,128)(2,1)S(1)} collective-permute-done((bf16[4,48,512]{2,1,0:T(8,128)(2,1)S(1)}, bf16[4,48,512]{2,1,0:T(8,128)(2,1)S(1)}, u32[]{:S(2)}, u32[]{:S(2)}) %collective-permute-start.16) | collective-permute-done | bytes 196640 | tf_op jit(solution)/shard_map/ppermute | solution.py:184
  106.5 2.3 %ordered.3 = (f32[512,512]{1,0:T(8,128)}, f32[512,512]{1,0:T(8,128)}, f32[512,512]{1,0:T(8,128)}) custom-call(s32[2]{0:T(128)S(1)} %pad_add_fusion.me, bf16[2,8,48,512]{3,2,1,0:T(8,128)(2,1)S(1)} %pad_maximum_fusion.kept, bf16[2,8,48,512]{3,2,1,0:T(8,128)(2,1)S(1)} %pad_maximum_fusion.1.got), custom_call_target="tpu_custom_call" | custom-call | bytes 4000000 | tf_op jit(solution)/shard_map/ordered/pallas_call | solution.py:315
  (96 shorter events, 26.9 us)
Async XLA Ops:
  7.4 18.1 %collective-permute-start.1 = (bf16[8,64,474]{2,1,0:T(8,128)(2,1)}, bf16[8,64,474]{2,1,0:T(8,128)(2,1)S(1)}, u32[]{:S(2)}, u32[]{:S(2)}) collective-permute-start(bf16[8,64,474]{2,1,0:T(8,128)(2,1)} %get-tuple-element.43), channel_id=1, source_target_pairs={{0,4},{4,8},{8,12},{12,0},{1,5},{5,9},{9,13},{13,1},{2,6},{6,10},{... | collective-permute-start | bytes 1456136 | tf_op jit(solution)/shard_map/ppermute | solution.py:231
  10.5 24.8 %collective-permute-start = (bf16[8,64,474]{2,1,0:T(8,128)(2,1)}, bf16[8,64,474]{2,1,0:T(8,128)(2,1)S(1)}, u32[]{:S(2)}, u32[]{:S(2)}) collective-permute-start(bf16[8,64,474]{2,1,0:T(8,128)(2,1)} %get-tuple-element.44), channel_id=1, source_target_pairs={{4,0},{8,4},{12,8},{0,12},{5,1},{9,5},{13,9},{1,13},{6,2},{10,6},{... | collective-permute-start | bytes 1456136 | tf_op jit(solution)/shard_map/ppermute | solution.py:230
  52.5 5.6 %collective-permute-start.3 = (bf16[4,32,512]{2,1,0:T(8,128)(2,1)S(1)}, bf16[4,32,512]{2,1,0:T(8,128)(2,1)S(1)}, u32[]{:S(2)}, u32[]{:S(2)}) collective-permute-start(bf16[4,32,512]{2,1,0:T(8,128)(2,1)S(1)} %slice.134), channel_id=1, source_target_pairs={{0,2},{1,3},{2,0},{3,1},{4,6},{5,7},{6,4},{7,5},{8,10},{9,11},{10,... | collective-permute-start | bytes 393224 | tf_op jit(solution)/shard_map/ppermute | solution.py:184
  54.2 9.8 %collective-permute-start.10 = (bf16[8,48,512]{2,1,0:T(8,128)(2,1)S(1)}, bf16[8,48,512]{2,1,0:T(8,128)(2,1)S(1)}, u32[]{:S(2)}, u32[]{:S(2)}) collective-permute-start(bf16[8,48,512]{2,1,0:T(8,128)(2,1)S(1)} %get-tuple-element.47), channel_id=1, source_target_pairs={{0,1},{1,0},{2,3},{3,2},{4,5},{5,4},{6,7},{7,6},{8,9},{9,8},{10,11... | collective-permute-start | bytes 1179656 | tf_op jit(solution)/shard_map/ppermute | solution.py:184
  54.2 9.7 %collective-permute-start.17 = (bf16[8,48,512]{2,1,0:T(8,128)(2,1)S(1)}, bf16[8,48,512]{2,1,0:T(8,128)(2,1)S(1)}, u32[]{:S(2)}, u32[]{:S(2)}) collective-permute-start(bf16[8,48,512]{2,1,0:T(8,128)(2,1)S(1)} %get-tuple-element.48), channel_id=1, source_target_pairs={{0,1},{1,0},{2,3},{3,2},{4,5},{5,4},{6,7},{7,6},{8,9},{9,8},{10,11... | collective-permute-start | bytes 1179656 | tf_op jit(solution)/shard_map/ppermute | solution.py:184
  58.2 4.3 %collective-permute-start.4 = (bf16[2,32,512]{2,1,0:T(8,128)(2,1)S(1)}, bf16[2,32,512]{2,1,0:T(8,128)(2,1)S(1)}, u32[]{:S(2)}, u32[]{:S(2)}) collective-permute-start(bf16[2,32,512]{2,1,0:T(8,128)(2,1)S(1)} %slice.136), channel_id=1, source_target_pairs={{0,4},{4,0},{8,12},{12,8},{1,5},{5,1},{9,13},{13,9},{2,6},{6,2},{1... | collective-permute-start | bytes 196616 | tf_op jit(solution)/shard_map/ppermute | solution.py:184
  62.6 4.9 %collective-permute-start.5 = (bf16[1,32,512]{2,1,0:T(8,128)(2,1)S(1)}, bf16[1,32,512]{2,1,0:T(8,128)(2,1)S(1)}, u32[]{:S(2)}, u32[]{:S(2)}) collective-permute-start(bf16[1,32,512]{2,1,0:T(8,128)(2,1)S(1)} %slice.138), channel_id=1, source_target_pairs={{0,8},{4,12},{8,0},{12,4},{1,9},{5,13},{9,1},{13,5},{2,10},{6,14},... | collective-permute-start | bytes 98312 | tf_op jit(solution)/shard_map/ppermute | solution.py:184
  64.2 9.8 %collective-permute-start.18 = (bf16[4,48,512]{2,1,0:T(8,128)(2,1)S(1)}, bf16[4,48,512]{2,1,0:T(8,128)(2,1)S(1)}, u32[]{:S(2)}, u32[]{:S(2)}) collective-permute-start(bf16[4,48,512]{2,1,0:T(8,128)(2,1)S(1)} %slice.146), channel_id=1, source_target_pairs={{0,4},{4,0},{8,12},{12,8},{1,5},{5,1},{9,13},{13,9},{2,6},{6,2},{1... | collective-permute-start | bytes 589832 | tf_op jit(solution)/shard_map/ppermute | solution.py:184
  67.5 4.9 %collective-permute-start.6 = (bf16[1,32,512]{2,1,0:T(8,128)(2,1)S(1)}, bf16[1,32,512]{2,1,0:T(8,128)(2,1)S(1)}, u32[]{:S(2)}, u32[]{:S(2)}) collective-permute-start(bf16[1,32,512]{2,1,0:T(8,128)(2,1)S(1)} %add_convert_fusion.8), channel_id=1, source_target_pairs={{0,8},{4,12},{8,0},{12,4},{1,9},{5,13},{9,1},{13,5},{2,10},{6,14},... | collective-permute-start | bytes 98312 | tf_op jit(solution)/shard_map/ppermute | solution.py:184
  69.2 7.1 %collective-permute-start.11 = (bf16[4,48,512]{2,1,0:T(8,128)(2,1)S(1)}, bf16[4,48,512]{2,1,0:T(8,128)(2,1)S(1)}, u32[]{:S(2)}, u32[]{:S(2)}) collective-permute-start(bf16[4,48,512]{2,1,0:T(8,128)(2,1)S(1)} %slice.140), channel_id=1, source_target_pairs={{0,2},{1,3},{2,0},{3,1},{4,6},{5,7},{6,4},{7,5},{8,10},{9,11},{10,... | collective-permute-start | bytes 589832 | tf_op jit(solution)/shard_map/ppermute | solution.py:184
  72.3 4.6 %collective-permute-start.7 = (bf16[2,32,512]{2,1,0:T(8,128)(2,1)S(1)}, bf16[2,32,512]{2,1,0:T(8,128)(2,1)S(1)}, u32[]{:S(2)}, u32[]{:S(2)}) collective-permute-start(bf16[2,32,512]{2,1,0:T(8,128)(2,1)S(1)} %pad_maximum_fusion.10), channel_id=1, source_target_pairs={{0,4},{4,0},{8,12},{12,8},{1,5},{5,1},{9,13},{13,9},{2,6},{6,2},{1... | collective-permute-start | bytes 196616 | tf_op jit(solution)/shard_map/ppermute | solution.py:184
  74.1 7.7 %collective-permute-start.19 = (bf16[2,48,512]{2,1,0:T(8,128)(2,1)S(1)}, bf16[2,48,512]{2,1,0:T(8,128)(2,1)S(1)}, u32[]{:S(2)}, u32[]{:S(2)}) collective-permute-start(bf16[2,48,512]{2,1,0:T(8,128)(2,1)S(1)} %slice.148), channel_id=1, source_target_pairs={{0,8},{4,12},{8,0},{12,4},{1,9},{5,13},{9,1},{13,5},{2,10},{6,14},... | collective-permute-start | bytes 294920 | tf_op jit(solution)/shard_map/ppermute | solution.py:184
  76.4 6.9 %collective-permute-start.12 = (bf16[2,48,512]{2,1,0:T(8,128)(2,1)S(1)}, bf16[2,48,512]{2,1,0:T(8,128)(2,1)S(1)}, u32[]{:S(2)}, u32[]{:S(2)}) collective-permute-start(bf16[2,48,512]{2,1,0:T(8,128)(2,1)S(1)} %slice.142), channel_id=1, source_target_pairs={{0,4},{4,0},{8,12},{12,8},{1,5},{5,1},{9,13},{13,9},{2,6},{6,2},{1... | collective-permute-start | bytes 294920 | tf_op jit(solution)/shard_map/ppermute | solution.py:184
  77.0 23.4 %collective-permute-start.8 = (bf16[4,32,512]{2,1,0:T(8,128)(2,1)S(1)}, bf16[4,32,512]{2,1,0:T(8,128)(2,1)S(1)}, u32[]{:S(2)}, u32[]{:S(2)}) collective-permute-start(bf16[4,32,512]{2,1,0:T(8,128)(2,1)S(1)} %pad_maximum_fusion.7), channel_id=1, source_target_pairs={{0,2},{1,3},{2,0},{3,1},{4,6},{5,7},{6,4},{7,5},{8,10},{9,11},{10,... | collective-permute-start | bytes 393224 | tf_op jit(solution)/shard_map/ppermute | solution.py:184
  81.8 4.2 %collective-permute-start.20 = (bf16[1,48,512]{2,1,0:T(8,128)(2,1)S(1)}, bf16[1,48,512]{2,1,0:T(8,128)(2,1)S(1)}, u32[]{:S(2)}, u32[]{:S(2)}) collective-permute-start(bf16[1,48,512]{2,1,0:T(8,128)(2,1)S(1)} %slice.150), channel_id=1, source_target_pairs={{0,2},{1,3},{2,0},{3,1},{4,6},{5,7},{6,4},{7,5},{8,10},{9,11},{10,... | collective-permute-start | bytes 147464 | tf_op jit(solution)/shard_map/ppermute | solution.py:184
  83.4 5.5 %collective-permute-start.13 = (bf16[1,48,512]{2,1,0:T(8,128)(2,1)S(1)}, bf16[1,48,512]{2,1,0:T(8,128)(2,1)S(1)}, u32[]{:S(2)}, u32[]{:S(2)}) collective-permute-start(bf16[1,48,512]{2,1,0:T(8,128)(2,1)S(1)} %slice.144), channel_id=1, source_target_pairs={{0,8},{4,12},{8,0},{12,4},{1,9},{5,13},{9,1},{13,5},{2,10},{6,14},... | collective-permute-start | bytes 147464 | tf_op jit(solution)/shard_map/ppermute | solution.py:184
  86.0 4.2 %collective-permute-start.21 = (bf16[1,48,512]{2,1,0:T(8,128)(2,1)S(1)}, bf16[1,48,512]{2,1,0:T(8,128)(2,1)S(1)}, u32[]{:S(2)}, u32[]{:S(2)}) collective-permute-start(bf16[1,48,512]{2,1,0:T(8,128)(2,1)S(1)} %add_convert_fusion.6), channel_id=1, source_target_pairs={{0,2},{1,3},{2,0},{3,1},{4,6},{5,7},{6,4},{7,5},{8,10},{9,11},{10,... | collective-permute-start | bytes 147464 | tf_op jit(solution)/shard_map/ppermute | solution.py:184
  88.9 5.2 %collective-permute-start.14 = (bf16[1,48,512]{2,1,0:T(8,128)(2,1)S(1)}, bf16[1,48,512]{2,1,0:T(8,128)(2,1)S(1)}, u32[]{:S(2)}, u32[]{:S(2)}) collective-permute-start(bf16[1,48,512]{2,1,0:T(8,128)(2,1)S(1)} %add_convert_fusion.7), channel_id=1, source_target_pairs={{0,8},{4,12},{8,0},{12,4},{1,9},{5,13},{9,1},{13,5},{2,10},{6,14},... | collective-permute-start | bytes 147464 | tf_op jit(solution)/shard_map/ppermute | solution.py:184
  90.1 5.6 %collective-permute-start.22 = (bf16[2,48,512]{2,1,0:T(8,128)(2,1)S(1)}, bf16[2,48,512]{2,1,0:T(8,128)(2,1)S(1)}, u32[]{:S(2)}, u32[]{:S(2)}) collective-permute-start(bf16[2,48,512]{2,1,0:T(8,128)(2,1)S(1)} %pad_maximum_fusion.9), channel_id=1, source_target_pairs={{0,8},{4,12},{8,0},{12,4},{1,9},{5,13},{9,1},{13,5},{2,10},{6,14},... | collective-permute-start | bytes 294920 | tf_op jit(solution)/shard_map/ppermute | solution.py:184
  94.1 4.7 %collective-permute-start.15 = (bf16[2,48,512]{2,1,0:T(8,128)(2,1)S(1)}, bf16[2,48,512]{2,1,0:T(8,128)(2,1)S(1)}, u32[]{:S(2)}, u32[]{:S(2)}) collective-permute-start(bf16[2,48,512]{2,1,0:T(8,128)(2,1)S(1)} %pad_maximum_fusion.8), channel_id=1, source_target_pairs={{0,4},{4,0},{8,12},{12,8},{1,5},{5,1},{9,13},{13,9},{2,6},{6,2},{1... | collective-permute-start | bytes 294920 | tf_op jit(solution)/shard_map/ppermute | solution.py:184
  95.7 5.7 %collective-permute-start.23 = (bf16[4,48,512]{2,1,0:T(8,128)(2,1)S(1)}, bf16[4,48,512]{2,1,0:T(8,128)(2,1)S(1)}, u32[]{:S(2)}, u32[]{:S(2)}) collective-permute-start(bf16[4,48,512]{2,1,0:T(8,128)(2,1)S(1)} %pad_maximum_fusion.6), channel_id=1, source_target_pairs={{0,4},{4,0},{8,12},{12,8},{1,5},{5,1},{9,13},{13,9},{2,6},{6,2},{1... | collective-permute-start | bytes 589832 | tf_op jit(solution)/shard_map/ppermute | solution.py:184
  98.8 5.7 %collective-permute-start.16 = (bf16[4,48,512]{2,1,0:T(8,128)(2,1)S(1)}, bf16[4,48,512]{2,1,0:T(8,128)(2,1)S(1)}, u32[]{:S(2)}, u32[]{:S(2)}) collective-permute-start(bf16[4,48,512]{2,1,0:T(8,128)(2,1)S(1)} %pad_maximum_fusion.5), channel_id=1, source_target_pairs={{0,2},{1,3},{2,0},{3,1},{4,6},{5,7},{6,4},{7,5},{8,10},{9,11},{10,... | collective-permute-start | bytes 589832 | tf_op jit(solution)/shard_map/ppermute | solution.py:184
  100.4 4.3 %collective-permute-start.9 = (bf16[8,32,512]{2,1,0:T(8,128)(2,1)S(1)}, bf16[8,32,512]{2,1,0:T(8,128)(2,1)S(1)}, u32[]{:S(2)}, u32[]{:S(2)}) collective-permute-start(bf16[8,32,512]{2,1,0:T(8,128)(2,1)S(1)} %get-tuple-element.53), channel_id=1, source_target_pairs={{0,1},{1,0},{2,3},{3,2},{4,5},{5,4},{6,7},{7,6},{8,9},{9,8},{10,11... | collective-permute-start | bytes 786440 | tf_op jit(solution)/shard_map/ppermute | solution.py:184
  101.5 4.9 %collective-permute-start.25 = (bf16[8,48,512]{2,1,0:T(8,128)(2,1)S(1)}, bf16[8,48,512]{2,1,0:T(8,128)(2,1)S(1)}, u32[]{:S(2)}, u32[]{:S(2)}) collective-permute-start(bf16[8,48,512]{2,1,0:T(8,128)(2,1)S(1)} %get-tuple-element.51), channel_id=1, source_target_pairs={{0,1},{1,0},{2,3},{3,2},{4,5},{5,4},{6,7},{7,6},{8,9},{9,8},{10,11... | collective-permute-start | bytes 1179656 | tf_op jit(solution)/shard_map/ppermute | solution.py:184
  (15 other events, 150.9 us)

commit v2 on v0

v2 whole, which is shorter than its diff:
```python
import jax
import jax.numpy as jnp
from jax import lax
from jax.experimental import pallas as pl
from jax.experimental.pallas import tpu as pltpu
from jax.sharding import PartitionSpec as P

epsilon = 1e-05
BF = jnp.bfloat16
F32 = jnp.float32
MIB = 1024 * 1024
SMEM = pl.BlockSpec(memory_space=pltpu.SMEM)
VMEM = pl.BlockSpec(memory_space=pltpu.VMEM)
shape = jax.ShapeDtypeStruct


def contract(a, b, dim_a, dim_b):
    return lax.dot_general(a, b, (((dim_a,), (dim_b,)), ((), ())), preferred_element_type=F32)


def silu_pair(pre):
    sigma = jax.nn.sigmoid(pre)
    return pre * sigma, sigma * (1.0 + pre * (1.0 - sigma))


def pack_kernel(grid, to_west, to_east, wide):
    features, rows, cols = grid.shape
    half = to_west.shape[1] // rows
    block = 2 * half
    last = cols // block - 1
    for k in (0, last):
        wide[k] = grid[:, :, k * block : (k + 1) * block].astype(F32).reshape(features * rows, block)
    lane = lax.broadcasted_iota(jnp.int32, (features, block), 1)
    for pair in range(rows // 2):
        even = pl.ds(2 * pair, features, stride=rows)
        odd = pl.ds(2 * pair + 1, features, stride=rows)
        at = slice(pair * block, (pair + 1) * block)
        head = jnp.where(lane < half, wide[0, even, :], pltpu.roll(wide[0, odd, :], half, 1))
        tail = jnp.where(lane < half, pltpu.roll(wide[last, even, :], half, 1), wide[last, odd, :])
        to_west[:, at] = head.astype(BF)
        to_east[:, at] = tail.astype(BF)


def own_kernel(
    src, dst, count, grid, embed_w, edge_w, cot, out_w,
    weights_all, x_t, embed_t, h_own, slope, grad_update, acc, wide,
):
    features, rows, cols = grid.shape
    block = edge_w.shape[1]
    half = block // 2
    own_blocks = cols // block
    windows = 2 * own_blocks + 1
    west_base = rows * own_blocks
    east_base = west_base + rows // 2
    acc[...] = jnp.zeros(acc.shape, F32)
    lane = lax.broadcasted_iota(jnp.int32, (block, block), 1)

    def slot(b, carry):
        source = src[b]
        row = source // windows
        window = source - row * windows
        at = window // 2
        target = pl.ds(pl.multiple_of(dst[b] * block, block), block)
        weights = edge_w[b].astype(F32)

        @pl.when(window % 2 == 1)
        def _():
            acc[row * own_blocks + at, target, :] += weights

        @pl.when(window % 2 == 0)
        def _():
            turned = pltpu.roll(weights, half, 1)
            odd_row = row % 2 == 1
            first = jnp.where(at == 0, west_base + row // 2, row * own_blocks + at - 1)
            first_high = (at > 0) | odd_row
            second = jnp.where(at == own_blocks, east_base + row // 2, row * own_blocks + at)
            second_high = (at == own_blocks) & odd_row
            acc[first, target, :] += jnp.where(
                first_high, jnp.where(lane >= half, turned, 0.0), jnp.where(lane < half, weights, 0.0)
            )
            acc[second, target, :] += jnp.where(
                second_high, jnp.where(lane >= half, weights, 0.0), jnp.where(lane < half, turned, 0.0)
            )

        return carry

    lax.fori_loop(0, count[0], slot, 0)
    for k in range(acc.shape[0]):
        weights_all[:, k * block : (k + 1) * block] = acc[k].astype(BF)
    for k in range(own_blocks):
        wide[k] = grid[:, :, k * block : (k + 1) * block].astype(F32).reshape(features * rows, block)
    embed_t[...] = embed_w[...].T
    total = jnp.zeros(h_own.shape, F32)
    for r in range(rows):
        at = slice(r * cols, (r + 1) * cols)
        for k in range(own_blocks):
            x_t[:, r * cols + k * block : r * cols + (k + 1) * block] = wide[
                k, pl.ds(r, features, stride=rows), :
            ].astype(BF)
        hidden, hidden_slope = silu_pair(contract(embed_t[...], x_t[:, at], 1, 0))
        slope[:, at] = hidden_slope.astype(BF)
        total += contract(weights_all[:, at], hidden.astype(BF), 1, 1)
    h_own[...] = total
    grad_update[...] = contract(cot[...], out_w[...], 1, 1)


def halo_part(x, embed_t, weights, slope):
    hidden, hidden_slope = silu_pair(contract(embed_t[...], x[...], 1, 0))
    slope[...] = hidden_slope.astype(BF)
    return contract(weights, hidden.astype(BF), 1, 1)


def west_kernel(first, x, embed_t, weights_all, h_own, h_sum, slope):
    points = x.shape[1]
    h_sum[...] = h_own[...] + halo_part(x, embed_t, weights_all[:, first : first + points], slope)


def mesh_kernel(
    perm, x, embed_t, weights_all, h_sum, message_w, up_w, out_w, gain, mesh_lat, cot, grad_update,
    mesh_new, mesh_grad, grads_0, grads_1, grad_gain, back, slope, stack,
):
    points = x.shape[1]
    first = weights_all.shape[1] - points
    total = h_sum[...] + halo_part(x, embed_t, weights_all[:, first:], slope)
    gathered = total.astype(BF)
    mesh_rows = mesh_lat[...].astype(F32)
    summed = mesh_rows + contract(gathered, message_w[...], 1, 0)
    rinv = lax.rsqrt(jnp.mean(summed * summed, axis=1, keepdims=True) + epsilon)
    qhat = summed * rinv
    gains = gain[...]
    normed = (qhat * gains).astype(BF)
    pre_up = contract(normed, up_w[...], 1, 0)
    silu_up, up_slope = silu_pair(pre_up)
    update = silu_up.astype(BF)
    grad_pre_up = (grad_update[...] * up_slope).astype(BF)
    grad_normed = contract(grad_pre_up, up_w[...], 1, 1)
    grad_gain[...] = jnp.sum(grad_normed * qhat, axis=0, keepdims=True)
    grad_qhat = grad_normed * gains
    grad_q = rinv * (grad_qhat - qhat * jnp.mean(grad_qhat * qhat, axis=1, keepdims=True))
    grad_aggregate = grad_q.astype(BF)
    back[...] = contract(message_w[...], grad_aggregate, 1, 1).astype(BF)
    mesh_grad[...] = cot[...].astype(F32) + grad_q
    mesh_new[...] = (mesh_rows + contract(update, out_w[...], 1, 0)).astype(BF)
    stack[0] = contract(gathered, grad_aggregate, 0, 0).astype(BF)
    stack[1] = contract(normed, grad_pre_up, 0, 0).astype(BF)
    stack[2] = contract(update, cot[...], 0, 0).astype(BF)
    _, matrices, size, _ = grads_0.shape
    for j in range(4):
        at = pl.multiple_of(perm[j] * (2 * size), 2 * size)
        for k in range(matrices):
            grads_0[j, k] = stack[k, pl.ds(at, size), :]
            grads_1[j, k] = stack[k, pl.ds(at + size, size), :]


def grid_kernel(perm, back, weights_all, slope_own, slope_west, slope_east, x_own, x_west, x_east, grad_gain, grads, total):
    features = x_own.shape[0]
    tile = x_west.shape[1]
    pieces = []
    for x, slope in ((x_own, slope_own), (x_west, slope_west), (x_east, slope_east)):
        pieces += [(x, slope, k) for k in range(x.shape[1] // tile)]
    sums = jnp.zeros((features, total.shape[1]), F32)
    for n, (x, slope, k) in enumerate(pieces):
        at = slice(k * tile, (k + 1) * tile)
        hidden = contract(back[...], weights_all[:, n * tile : (n + 1) * tile], 1, 0)
        grad_pre = (hidden * slope[:, at].astype(F32)).astype(BF)
        sums += contract(x[:, at], grad_pre, 1, 1)
    total[...] = jnp.zeros(total.shape, F32)
    total[:features, :] = sums
    total[features : features + 1, :] = grad_gain[...]
    size = grads.shape[2]
    for j in range(4):
        grads[j, 0] = total[pl.ds(pl.multiple_of(perm[j] * size, size), size), :].astype(BF)


def order_mesh_kernel(perm, *refs):
    chunks, outs = refs[:-3], refs[-3:]
    for part in range(2):
        for j, chunk in enumerate(chunks[4 * part : 4 * part + 4]):
            size = chunk.shape[1]
            at = pl.multiple_of(perm[j] * (2 * size), 2 * size) + part * size
            for k, out in enumerate(outs):
                out[pl.ds(at, size), :] = chunk[k].astype(F32)


def order_grid_kernel(perm, *refs):
    chunks, (grad_embed, grad_gain, total) = refs[:4], refs[4:]
    for j, chunk in enumerate(chunks):
        size = chunk.shape[1]
        total[pl.ds(pl.multiple_of(perm[j] * size, size), size), :] = chunk[0].astype(F32)
    features = grad_embed.shape[0]
    grad_embed[...] = total[:features, :]
    grad_gain[...] = total[features : features + 1, :]


def role_steps():
    lat = [("lat", 2 << k) for k in range(lax.axis_size("lat").bit_length() - 2)]
    lon = [("lon", 1 << k) for k in range(lax.axis_size("lon").bit_length() - 1)]
    return (lat + lon, lon + lat)


def core_swapped(value):
    return lax.ppermute(value, "lat", [(i, i ^ 1) for i in range(lax.axis_size("lat"))])


def swapped(value, step):
    lats = lax.axis_size("lat")
    pairs = []
    for lon in range(lax.axis_size("lon")):
        for lat in range(lats):
            axis, bit = role_steps()[lat & 1][step]
            other = (lon ^ bit) * lats + lat if axis == "lon" else lon * lats + (lat ^ bit)
            pairs.append((lon * lats + lat, other))
    return lax.ppermute(value, ("lon", "lat"), pairs)


def chunk_order():
    core = lax.axis_index("lat") & 1
    side = [((lax.axis_index(axis) & bit) != 0).astype(jnp.int32) for axis, bit in (s[0] for s in role_steps())]
    mine = jnp.where(core == 0, side[0], side[1])
    theirs = jnp.where(core == 0, side[1], side[0])
    return jnp.stack([2 * core + mine, 2 * core + 1 - mine, 2 - 2 * core + theirs, 3 - 2 * core - theirs])


def added(a, b):
    return (a.astype(F32) + b.astype(F32)).astype(BF)


def all_summed(grads):
    kept = added(grads[:2], core_swapped(grads[2:]))
    mine = added(kept[0], swapped(kept[1], 0))
    for step in range(1, len(role_steps()[0])):
        mine = added(mine, swapped(mine, step))
    partners = swapped(mine, 0)
    return mine, partners, core_swapped(mine), core_swapped(partners)


def on_device(grid_in, mesh_lat, edge_w, edge_src, edge_dst, block_count, embed_w, message_w, up_w, out_w, gain, cot):
    rows, cols, features = grid_in.shape
    latent = message_w.shape[0]
    block = edge_w.shape[1]
    half = block // 2
    nodes = mesh_lat.shape[0]
    own = rows * cols
    side = rows * half
    points = own + 2 * side
    grid = jnp.transpose(grid_in, (2, 0, 1))

    def call(kernel, name, in_specs, out_shape, flops, bytes_accessed, limit, scratch_shapes=()):
        return pl.pallas_call(
            kernel,
            name=name,
            in_specs=in_specs,
            out_specs=[VMEM] * len(out_shape),
            out_shape=out_shape,
            scratch_shapes=list(scratch_shapes),
            compiler_params=pltpu.CompilerParams(vmem_limit_bytes=limit * MIB),
            cost_estimate=pl.CostEstimate(flops=flops, bytes_accessed=bytes_accessed, transcendentals=0),
        )

    to_west, to_east = call(
        pack_kernel, "pack", [VMEM], [shape((features, side), BF)] * 2, 0, 3 * MIB, 20,
        [pltpu.VMEM((cols // block, features * rows, block), F32)],
    )(grid)
    count = lax.axis_size("lon")
    x_west = lax.ppermute(to_east, "lon", [(i, (i + 1) % count) for i in range(count)])
    x_east = lax.ppermute(to_west, "lon", [((i + 1) % count, i) for i in range(count)])

    weights_all, x_own, embed_t, h_own, slope_own, grad_update = call(
        own_kernel, "own_points", [SMEM] * 3 + [VMEM] * 5,
        [
            shape((nodes, points), BF),
            shape((features, own), BF),
            shape((latent, features), BF),
            shape((nodes, latent), F32),
            shape((latent, own), BF),
            shape((nodes, latent), F32),
        ],
        4_000_000_000, 12 * MIB, 32,
        [pltpu.VMEM((points // block, nodes, block), F32), pltpu.VMEM((cols // block, features * rows, block), F32)],
    )(edge_src, edge_dst, block_count, grid, embed_w, edge_w, cot, out_w)

    h_sum, slope_west = call(
        lambda *refs: west_kernel(own, *refs), "west_points", [VMEM] * 4,
        [shape((nodes, latent), F32), shape((latent, side), BF)],
        600_000_000, 3 * MIB, 16,
    )(x_west, embed_t, weights_all, h_own)

    perm = chunk_order()
    mesh_new, mesh_grad, grads_0, grads_1, gain_term, back, slope_east = call(
        mesh_kernel, "mesh_nodes", [SMEM] + [VMEM] * 11,
        [
            shape((nodes, latent), BF),
            shape((nodes, latent), F32),
            shape((4, 3, latent // 8, latent), BF),
            shape((4, 3, latent // 8, latent), BF),
            shape((1, latent), F32),
            shape((latent, nodes), BF),
            shape((latent, side), BF),
        ],
        2_000_000_000, 8 * MIB, 16, [pltpu.VMEM((3, latent, latent), BF)],
    )(
        perm, x_east, embed_t, weights_all, h_sum, message_w, up_w, out_w, gain.reshape(1, latent),
        mesh_lat, cot, grad_update,
    )

    padded = -(-(features + 1) // 128) * 128
    (grads_2,) = call(
        grid_kernel, "grid_points", [SMEM] + [VMEM] * 9, [shape((4, 1, padded // 4, latent), BF)],
        2_400_000_000, 9 * MIB, 16, [pltpu.VMEM((padded, latent), F32)],
    )(perm, back, weights_all, slope_own, slope_west, slope_east, x_own, x_west, x_east, gain_term)

    summed = [all_summed(grads) for grads in (grads_0, grads_1, grads_2)]
    grad_message, grad_up, grad_out = call(
        order_mesh_kernel, "order_mesh", [SMEM] + [VMEM] * 8, [shape((latent, latent), F32)] * 3, 0, 5 * MIB, 16
    )(perm, *summed[0], *summed[1])
    grad_embed, grad_gain = call(
        order_grid_kernel, "order_grid", [SMEM] + [VMEM] * 4,
        [shape((features, latent), F32), shape((1, latent), F32)], 0, 2 * MIB, 16,
        [pltpu.VMEM((padded, latent), F32)],
    )(perm, *summed[2])
    return (mesh_new, mesh_grad, grad_embed, grad_message, grad_up, grad_out, grad_gain[0])


def solution(mesh):
    tiles = ("grp", "lon", "lat")
    return jax.shard_map(
        on_device,
        mesh=mesh,
        in_specs=(
            P(("grp", "lat"), "lon", None),
            P(tiles, None),
            P(tiles, None, None),
            P(tiles),
            P(tiles),
            P(tiles),
            P(),
            P(),
            P(),
            P(),
            P(),
            P(tiles, None),
        ),
        out_specs=(
            P(tiles, None),
            P(tiles, None),
            P("grp", None),
            P("grp", None),
            P("grp", None),
            P("grp", None),
            P("grp"),
        ),
        check_vma=False,
    )
```

time: 263 us -> 91.3 us (0.35)
  waiting for transfers between devices: 117 us -> 31.9 us
  matrix products: 34.5 us -> 0 us
  blocking collectives: 34.1 us -> 0 us
  other arithmetic: 26.9 us -> 0.75 us
  Pallas kernels: 0 us -> 21.9 us
  starting transfers between devices: 7.84 us -> 28.9 us
  local copies, waits for them, and re-layouts: 26.9 us -> 5.93 us
  between operations: 15 us -> 1.59 us
    psum x1 -> x0, waiting for transfers between devices: 76.1 us -> none  [on_device(): lax.psum((grad_embed, grad_message, grad_up, grad_out, grad_gain), ('lon'...]
    dot_general x13 -> x0, matrix products: 34.5 us -> none  [the longest x1 7.52 us: on_device(): jnp.einsum('gb,bmd->gmd', onehot, product_terms, precision=lax.Precision....]
    psum x1 -> x0, blocking collectives: 34.1 us -> none  [on_device(): lax.psum((grad_embed, grad_message, grad_up, grad_out, grad_gain), ('lon'...]
    pallas_call x0 -> x7, Pallas kernels: none -> 21.9 us  [the longest x1 7.72 us: on_device(): call(own_kernel, 'own_points', [SMEM] * 3 + [VMEM] * 5, [shape((nodes, po...]
    ppermute x4 -> x23, starting transfers between devices: 7.8 us -> 28.9 us  [the longest x12 19.3 us: swapped(): return lax.ppermute(value, ('lon', 'lat'), pairs)]
    scatter-add x4 -> x0, other arithmetic: 20.3 us -> none  [the longest x2 19.9 us: on_device(): spread = spread.at[first].add(backward_result[:, :half_block]).at[first +...]
    ppermute x4 -> x23, waiting for transfers between devices: 41.2 us -> 31.9 us  [the longest x12 20.8 us: swapped(): return lax.ppermute(value, ('lon', 'lat'), pairs)]
    gather x3 -> x0, local copies, waits for them, and re-layouts: 9.28 us -> none  [the longest x2 6.5 us: on_device(): block_groups = jnp.concatenate((halves[first], halves[first + 1]), axis=1)]
  transfers between devices with their start and end apart: 5 -> 23, of which waited for: 5 -> 12; matrix products, arithmetic and copies ran while one was open for 2% -> 1% of each run, Pallas kernels for 0% -> 11%
where the time goes in v2:
time: 91.3 us; the launch traced here: 91 us
  waiting for transfers between devices  31.9 us (35%)
  starting transfers between devices  28.9 us (32%)
  Pallas kernels  21.9 us (24%)
  local copies, waits for them, and re-layouts  5.93 us (6%)
  between operations  1.59 us (2%)
    ppermute x12, waiting for transfers between devices, swapped(): return lax.ppermute(value, ('lon', 'lat'), pairs)  20.8 us
    ppermute x12, starting transfers between devices, swapped(): return lax.ppermute(value, ('lon', 'lat'), pairs)  19.3 us
    ppermute x1, waiting for transfers between devices, on_device(): lax.ppermute(to_east, 'lon', [(i, (i + 1) % count) for i in range(count)])  9.13 us
    pallas_call x1, Pallas kernels, on_device(): call(own_kernel, 'own_points', [SMEM] * 3 + [VMEM] * 5, [shape((nodes, po...  7.72 us
    unnamed x24, local copies, waits for them, and re-layouts  5.82 us
    ppermute x1, starting transfers between devices, on_device(): lax.ppermute(to_west, 'lon', [((i + 1) % count, i) for i in range(count)])  5.05 us
    ppermute x9, starting transfers between devices, core_swapped(): lax.ppermute(value, 'lat', [(i, i ^ 1) for i in range(lax.axis_size('lat'...  4.54 us
    pallas_call x1, Pallas kernels, on_device(): call(mesh_kernel, 'mesh_nodes', [SMEM] + [VMEM] * 11, [shape((nodes, late...  4.16 us
  transfers between devices with their start and end apart: 23, of which 12 were waited for; matrix products, arithmetic and copies ran while one was open for 1% of the time, Pallas kernels for 11%

profile of v2, /device:TPU:0, one launch (start us, length us, event | category | flops | bytes accessed | tf_op | source)
XLA Modules:
  0.0 91.0 jit_solution(8997918132374918537)
XLA Ops:
  0.7 1.5 %copy-done = bf16[8,256,474]{1,0,2:T(8,128)(2,1)S(1)} copy-done((bf16[8,256,474]{1,0,2:T(8,128)(2,1)S(1)}, bf16[8,256,474]{1,0,2:T(8,128)(2,1)}, u32[]{:S(2)}) %copy-start) | copy-done | bytes 1941528
  2.2 1.7 %pack.1 = (bf16[474,512]{1,0:T(8,128)(2,1)S(1)}, bf16[474,512]{1,0:T(8,128)(2,1)}) custom-call(bf16[474,8,256]{2,1,0:T(8,128)(2,1)S(1)} %bitcast.28), custom_call_target="tpu_custom_call" | custom-call | bytes 3145728 | tf_op jit(solution)/shard_map/pack/pallas_call | solution.py:260
  3.9 5.0 %collective-permute-start = (bf16[474,512]{1,0:T(8,128)(2,1)S(1)}, bf16[474,512]{1,0:T(8,128)(2,1)S(1)}, u32[]{:S(2)}, u32[]{:S(2)}) collective-permute-start(bf16[474,512]{1,0:T(8,128)(2,1)S(1)} %get-tuple-element.29), channel_id=1, source_target_pairs={{4,0},{8,4},{12,8},{0,12},{5,1},{9,5},{13,9},{1,13},{6,2},{10,6},{... | collective-permute-start | bytes 1456136 | tf_op jit(solution)/shard_map/ppermute | solution.py:266
  14.0 7.7 %own_points.1 = (bf16[256,3072]{1,0:T(8,128)(2,1)S(1)}, bf16[474,2048]{1,0:T(8,128)(2,1)S(1)}, bf16[512,474]{1,0:T(8,128)(2,1)S(1)}, f32[256,512]{1,0:T(8,128)S(...) custom-call(s32[32]{0:T(128)S(1)} %copy-done.10, s32[32]{0:T(128)S(1)} %copy-done.11, s32[1]{0:T(128)S(6)} %copy.19.count, ...), custom_call_target="tpu_custom_call" | custom-call | flops 4000000000 | bytes 12582912 | tf_op jit(solution)/shard_map/own_points/pallas_call | solution.py:268
  21.8 9.1 %collective-permute-done.1.refs_0_.x_west = bf16[474,512]{1,0:T(8,128)(2,1)S(1)} collective-permute-done((bf16[474,512]{1,0:T(8,128)(2,1)}, bf16[474,512]{1,0:T(8,128)(2,1)S(1)}, u32[]{:S(2)}, u32[]{:S(2)}) %collective-permute-start.1) | collective-permute-done | bytes 485408 | tf_op jit(solution)/shard_map/ppermute | solution.py:265
  31.8 4.2 %mesh_nodes.1 = (bf16[256,512]{1,0:T(8,128)(2,1)}, f32[256,512]{1,0:T(8,128)}, bf16[4,3,64,512]{3,2,1,0:T(8,128)(2,1)S(1)}, bf16[4,3,64,512]{3,2,1,0:T(8,128)(2,...) custom-call(s32[4]{0:T(128)S(1)} %pad_add_fusion.perm, ...), custom_call_target="tpu_custom_call" | custom-call | flops 2000000000 | bytes 8388608 | tf_op jit(solution)/shard_map/mesh_nodes/pallas_call | solution.py:289
  36.0 3.4 %grid_points.1 = bf16[4,1,128,512]{3,2,1,0:T(8,128)(2,1)S(1)} custom-call(s32[4]{0:T(128)S(1)} %pad_add_fusion.perm, bf16[512,256]{1,0:T(8,128)(2,1)S(1)} %get-tuple-element.38.back, bf16[256,3072]{1,0:T(8,128)(2,1)S(1)} %get-tuple-element.31.refs_2_.weights_all, bf16[512,2048]{1,0:T(8,128)(2,1)S(1)} %get-tuple-element.39.slope_own, ...), custom_call_target="tpu_custom_call" | custom-call | flops 2400000000 | bytes 9437184 | tf_op jit(solution)/shard_map/grid_points/pallas_call | solution.py:307
  41.1 1.5 %collective-permute-start.3 = (bf16[1,128,512]{2,1,0:T(8,128)(2,1)S(1)}, bf16[1,128,512]{2,1,0:T(8,128)(2,1)S(1)}, u32[]{:S(2)}, u32[]{:S(2)}) collective-permute-start(bf16[1,128,512]{2,1,0:T(8,128)(2,1)S(1)} %slice_bitcast_fusion.4), channel_id=1, source_target_pairs={{0,2},{1,5},{2,0},{3,7},{4,6},{5,1},{6,4},{7,3},{8,10},{9,13},{10,... | collective-permute-start | bytes 393224 | tf_op jit(solution)/shard_map/ppermute | solution.py:213
  42.8 3.4 %collective-permute-done.3 = bf16[1,128,512]{2,1,0:T(8,128)(2,1)S(1)} collective-permute-done((bf16[1,128,512]{2,1,0:T(8,128)(2,1)S(1)}, bf16[1,128,512]{2,1,0:T(8,128)(2,1)S(1)}, u32[]{:S(2)}, u32[]{:S(2)}) %collective-permute-start.3) | collective-permute-done | bytes 131104 | tf_op jit(solution)/shard_map/ppermute | solution.py:213
  46.2 1.7 %collective-permute-start.4 = (bf16[1,128,512]{2,1,0:T(8,128)(2,1)S(1)}, bf16[1,128,512]{2,1,0:T(8,128)(2,1)S(1)}, u32[]{:S(2)}, u32[]{:S(2)}) collective-permute-start(bf16[1,128,512]{2,1,0:T(8,128)(2,1)S(1)} %fusion.2), channel_id=1, source_target_pairs={{0,4},{1,9},{2,6},{3,11},{4,0},{5,13},{6,2},{7,15},{8,12},{9,1},{1... | collective-permute-start | bytes 393224 | tf_op jit(solution)/shard_map/ppermute | solution.py:213
  48.0 1.6 %collective-permute-start.17 = (bf16[3,64,512]{2,1,0:T(8,128)(2,1)S(1)}, bf16[3,64,512]{2,1,0:T(8,128)(2,1)S(1)}, u32[]{:S(2)}, u32[]{:S(2)}) collective-permute-start(bf16[3,64,512]{2,1,0:T(8,128)(2,1)S(1)} %slice_bitcast_fusion), channel_id=1, source_target_pairs={{0,2},{1,5},{2,0},{3,7},{4,6},{5,1},{6,4},{7,3},{8,10},{9,13},{10,... | collective-permute-start | bytes 589832 | tf_op jit(solution)/shard_map/ppermute | solution.py:213
  50.3 3.0 %collective-permute-done.4 = bf16[1,128,512]{2,1,0:T(8,128)(2,1)S(1)} collective-permute-done((bf16[1,128,512]{2,1,0:T(8,128)(2,1)S(1)}, bf16[1,128,512]{2,1,0:T(8,128)(2,1)S(1)}, u32[]{:S(2)}, u32[]{:S(2)}) %collective-permute-start.4) | collective-permute-done | bytes 131104 | tf_op jit(solution)/shard_map/ppermute | solution.py:213
  54.0 2.5 %collective-permute-start.18 = (bf16[3,64,512]{2,1,0:T(8,128)(2,1)S(1)}, bf16[3,64,512]{2,1,0:T(8,128)(2,1)S(1)}, u32[]{:S(2)}, u32[]{:S(2)}) collective-permute-start(bf16[3,64,512]{2,1,0:T(8,128)(2,1)S(1)} %fusion), channel_id=1, source_target_pairs={{0,4},{1,9},{2,6},{3,11},{4,0},{5,13},{6,2},{7,15},{8,12},{9,1},{1... | collective-permute-start | bytes 589832 | tf_op jit(solution)/shard_map/ppermute | solution.py:213
  57.4 4.4 %collective-permute-done.18 = bf16[3,64,512]{2,1,0:T(8,128)(2,1)S(1)} collective-permute-done((bf16[3,64,512]{2,1,0:T(8,128)(2,1)S(1)}, bf16[3,64,512]{2,1,0:T(8,128)(2,1)S(1)}, u32[]{:S(2)}, u32[]{:S(2)}) %collective-permute-start.18) | collective-permute-done | bytes 196640 | tf_op jit(solution)/shard_map/ppermute | solution.py:213
  61.9 4.0 %collective-permute-start.19 = (bf16[3,64,512]{2,1,0:T(8,128)(2,1)S(1)}, bf16[3,64,512]{2,1,0:T(8,128)(2,1)S(1)}, u32[]{:S(2)}, u32[]{:S(2)}) collective-permute-start(bf16[3,64,512]{2,1,0:T(8,128)(2,1)S(1)} %add_convert_fusion.4), channel_id=1, source_target_pairs={{0,8},{1,3},{2,10},{3,1},{4,12},{5,7},{6,14},{7,5},{8,0},{9,11},{1... | collective-permute-start | bytes 589832 | tf_op jit(solution)/shard_map/ppermute | solution.py:213
  66.0 2.3 %collective-permute-start.12 = (bf16[3,64,512]{2,1,0:T(8,128)(2,1)S(1)}, bf16[3,64,512]{2,1,0:T(8,128)(2,1)S(1)}, u32[]{:S(2)}, u32[]{:S(2)}) collective-permute-start(bf16[3,64,512]{2,1,0:T(8,128)(2,1)S(1)} %add_convert_fusion.6), channel_id=1, source_target_pairs={{0,8},{1,3},{2,10},{3,1},{4,12},{5,7},{6,14},{7,5},{8,0},{9,11},{1... | collective-permute-start | bytes 589832 | tf_op jit(solution)/shard_map/ppermute | solution.py:213
  68.3 6.9 %collective-permute-done.19 = bf16[3,64,512]{2,1,0:T(8,128)(2,1)S(1)} collective-permute-done((bf16[3,64,512]{2,1,0:T(8,128)(2,1)S(1)}, bf16[3,64,512]{2,1,0:T(8,128)(2,1)S(1)}, u32[]{:S(2)}, u32[]{:S(2)}) %collective-permute-start.19) | collective-permute-done | bytes 196640 | tf_op jit(solution)/shard_map/ppermute | solution.py:213
  75.2 1.6 %collective-permute-start.20 = (bf16[3,64,512]{2,1,0:T(8,128)(2,1)S(1)}, bf16[3,64,512]{2,1,0:T(8,128)(2,1)S(1)}, u32[]{:S(2)}, u32[]{:S(2)}) collective-permute-start(bf16[3,64,512]{2,1,0:T(8,128)(2,1)S(1)} %add_convert_fusion.3.refs_4_), channel_id=1, source_target_pairs={{0,2},{1,5},{2,0},{3,7},{4,6},{5,1},{6,4},{7,3},{8,10},{9,13},{10,... | collective-permute-start | bytes 589832 | tf_op jit(solution)/shard_map/ppermute | solution.py:213
  77.4 1.6 %collective-permute-start.13 = (bf16[3,64,512]{2,1,0:T(8,128)(2,1)S(1)}, bf16[3,64,512]{2,1,0:T(8,128)(2,1)S(1)}, u32[]{:S(2)}, u32[]{:S(2)}) collective-permute-start(bf16[3,64,512]{2,1,0:T(8,128)(2,1)S(1)} %add_convert_fusion.5.refs_0_), channel_id=1, source_target_pairs={{0,2},{1,5},{2,0},{3,7},{4,6},{5,1},{6,4},{7,3},{8,10},{9,13},{10,... | collective-permute-start | bytes 589832 | tf_op jit(solution)/shard_map/ppermute | solution.py:213
  80.1 1.5 %collective-permute-start.6 = (bf16[1,128,512]{2,1,0:T(8,128)(2,1)S(1)}, bf16[1,128,512]{2,1,0:T(8,128)(2,1)S(1)}, u32[]{:S(2)}, u32[]{:S(2)}) collective-permute-start(bf16[1,128,512]{2,1,0:T(8,128)(2,1)S(1)} %add_convert_fusion.7.refs_0_), channel_id=1, source_target_pairs={{0,2},{1,5},{2,0},{3,7},{4,6},{5,1},{6,4},{7,3},{8,10},{9,13},{10,... | collective-permute-start | bytes 393224 | tf_op jit(solution)/shard_map/ppermute | solution.py:213
  82.2 1.4 %collective-permute-done.13.refs_1_ = bf16[3,64,512]{2,1,0:T(8,128)(2,1)S(1)} collective-permute-done((bf16[3,64,512]{2,1,0:T(8,128)(2,1)S(1)}, bf16[3,64,512]{2,1,0:T(8,128)(2,1)S(1)}, u32[]{:S(2)}, u32[]{:S(2)}) %collective-permute-start.13) | collective-permute-done | bytes 196640 | tf_op jit(solution)/shard_map/ppermute | solution.py:213
  83.6 1.3 %collective-permute-start.15 = (bf16[3,64,512]{2,1,0:T(8,128)(2,1)S(1)}, bf16[3,64,512]{2,1,0:T(8,128)(2,1)S(1)}, u32[]{:S(2)}, u32[]{:S(2)}) collective-permute-start(bf16[3,64,512]{2,1,0:T(8,128)(2,1)S(1)} %collective-permute-done.13.refs_1_), channel_id=1, source_target_pairs={{0,1},{1,0},{2,3},{3,2},{4,5},{5,4},{6,7},{7,6},{8,9},{9,8},{10,11... | collective-permute-start | bytes 589832 | tf_op jit(solution)/shard_map/ppermute | solution.py:202
  86.9 1.6 %order_grid.1 = (f32[474,512]{1,0:T(8,128)}, f32[1,512]{1,0:T(1,128)}) custom-call(s32[4]{0:T(128)S(1)} %pad_add_fusion.perm, bf16[1,128,512]{2,1,0:T(8,128)(2,1)S(1)} %add_convert_fusion.7.refs_0_, bf16[1,128,512]{2,1,0:T(8,128)(2,1)S(1)} %collective-permute-done.6.refs_1_, bf16[1,128,512]{2,1,0:T(8,128)(2,1)S(1)} %collective-permute-done.7.refs_2_, ...), custom_call_target="tpu_custom_call" | custom-call | bytes 2097152 | tf_op jit(solution)/shard_map/order_grid/pallas_call | solution.py:316
  88.6 2.4 %order_mesh.1 = (f32[512,512]{1,0:T(8,128)}, f32[512,512]{1,0:T(8,128)}, f32[512,512]{1,0:T(8,128)}) custom-call(s32[4]{0:T(128)S(1)} %pad_add_fusion.perm, bf16[3,64,512]{2,1,0:T(8,128)(2,1)S(1)} %add_convert_fusion.5.refs_0_, bf16[3,64,512]{2,1,0:T(8,128)(2,1)S(1)} %collective-permute-done.13.refs_1_, ...), custom_call_target="tpu_custom_call" | custom-call | bytes 5242880 | tf_op jit(solution)/shard_map/order_mesh/pallas_call | solution.py:313
  (72 shorter events, 14.0 us)
Async XLA Ops:
  3.9 27.8 %collective-permute-start = (bf16[474,512]{1,0:T(8,128)(2,1)S(1)}, bf16[474,512]{1,0:T(8,128)(2,1)S(1)}, u32[]{:S(2)}, u32[]{:S(2)}) collective-permute-start(bf16[474,512]{1,0:T(8,128)(2,1)S(1)} %get-tuple-element.29), channel_id=1, source_target_pairs={{4,0},{8,4},{12,8},{0,12},{5,1},{9,5},{13,9},{1,13},{6,2},{10,6},{... | collective-permute-start | bytes 1456136 | tf_op jit(solution)/shard_map/ppermute | solution.py:266
  9.0 21.9 %collective-permute-start.1 = (bf16[474,512]{1,0:T(8,128)(2,1)}, bf16[474,512]{1,0:T(8,128)(2,1)S(1)}, u32[]{:S(2)}, u32[]{:S(2)}) collective-permute-start(bf16[474,512]{1,0:T(8,128)(2,1)} %get-tuple-element.32), channel_id=1, source_target_pairs={{0,4},{4,8},{8,12},{12,0},{1,5},{5,9},{9,13},{13,1},{2,6},{6,10},{... | collective-permute-start | bytes 1456136 | tf_op jit(solution)/shard_map/ppermute | solution.py:265
  21.7 10.1 %copy-start.4 = (bf16[512,512]{1,0:T(8,128)(2,1)S(1)}, bf16[512,512]{1,0:T(8,128)(2,1)}, u32[]{:S(2)}) copy-start(bf16[512,512]{1,0:T(8,128)(2,1)} %message_w.1) | copy-start | bytes 1572868
  39.4 1.6 %collective-permute-start.2 = (bf16[2,1,128,512]{3,2,1,0:T(8,128)(2,1)S(1)}, bf16[2,1,128,512]{3,2,1,0:T(8,128)(2,1)S(1)}, u32[]{:S(2)}, u32[]{:S(2)}) collective-permute-start(bf16[2,1,128,512]{3,2,1,0:T(8,128)(2,1)S(1)} %slice.49), channel_id=1, source_target_pairs={{0,1},{1,0},{2,3},{3,2},{4,5},{5,4},{6,7},{7,6},{8,9},{9,8},{10,11... | collective-permute-start | bytes 786440 | tf_op jit(solution)/shard_map/ppermute | solution.py:202
  39.6 8.3 %collective-permute-start.16 = (bf16[2,3,64,512]{3,2,1,0:T(8,128)(2,1)S(1)}, bf16[2,3,64,512]{3,2,1,0:T(8,128)(2,1)S(1)}, u32[]{:S(2)}, u32[]{:S(2)}) collective-permute-start(bf16[2,3,64,512]{3,2,1,0:T(8,128)(2,1)S(1)} %slice.45), channel_id=1, source_target_pairs={{0,1},{1,0},{2,3},{3,2},{4,5},{5,4},{6,7},{7,6},{8,9},{9,8},{10,11... | collective-permute-start | bytes 1179656 | tf_op jit(solution)/shard_map/ppermute | solution.py:202
  41.1 5.0 %collective-permute-start.3 = (bf16[1,128,512]{2,1,0:T(8,128)(2,1)S(1)}, bf16[1,128,512]{2,1,0:T(8,128)(2,1)S(1)}, u32[]{:S(2)}, u32[]{:S(2)}) collective-permute-start(bf16[1,128,512]{2,1,0:T(8,128)(2,1)S(1)} %slice_bitcast_fusion.4), channel_id=1, source_target_pairs={{0,2},{1,5},{2,0},{3,7},{4,6},{5,1},{6,4},{7,3},{8,10},{9,13},{10,... | collective-permute-start | bytes 393224 | tf_op jit(solution)/shard_map/ppermute | solution.py:213
  42.7 6.9 %collective-permute-start.9 = (bf16[2,3,64,512]{3,2,1,0:T(8,128)(2,1)S(1)}, bf16[2,3,64,512]{3,2,1,0:T(8,128)(2,1)S(1)}, u32[]{:S(2)}, u32[]{:S(2)}) collective-permute-start(bf16[2,3,64,512]{3,2,1,0:T(8,128)(2,1)S(1)} %slice.41), channel_id=1, source_target_pairs={{0,1},{1,0},{2,3},{3,2},{4,5},{5,4},{6,7},{7,6},{8,9},{9,8},{10,11... | collective-permute-start | bytes 1179656 | tf_op jit(solution)/shard_map/ppermute | solution.py:202
  46.2 7.1 %collective-permute-start.4 = (bf16[1,128,512]{2,1,0:T(8,128)(2,1)S(1)}, bf16[1,128,512]{2,1,0:T(8,128)(2,1)S(1)}, u32[]{:S(2)}, u32[]{:S(2)}) collective-permute-start(bf16[1,128,512]{2,1,0:T(8,128)(2,1)S(1)} %fusion.2), channel_id=1, source_target_pairs={{0,4},{1,9},{2,6},{3,11},{4,0},{5,13},{6,2},{7,15},{8,12},{9,1},{1... | collective-permute-start | bytes 393224 | tf_op jit(solution)/shard_map/ppermute | solution.py:213
  48.0 5.9 %collective-permute-start.17 = (bf16[3,64,512]{2,1,0:T(8,128)(2,1)S(1)}, bf16[3,64,512]{2,1,0:T(8,128)(2,1)S(1)}, u32[]{:S(2)}, u32[]{:S(2)}) collective-permute-start(bf16[3,64,512]{2,1,0:T(8,128)(2,1)S(1)} %slice_bitcast_fusion), channel_id=1, source_target_pairs={{0,2},{1,5},{2,0},{3,7},{4,6},{5,1},{6,4},{7,3},{8,10},{9,13},{10,... | collective-permute-start | bytes 589832 | tf_op jit(solution)/shard_map/ppermute | solution.py:213
  49.7 7.5 %collective-permute-start.10 = (bf16[3,64,512]{2,1,0:T(8,128)(2,1)S(1)}, bf16[3,64,512]{2,1,0:T(8,128)(2,1)S(1)}, u32[]{:S(2)}, u32[]{:S(2)}) collective-permute-start(bf16[3,64,512]{2,1,0:T(8,128)(2,1)S(1)} %slice_bitcast_fusion.2), channel_id=1, source_target_pairs={{0,2},{1,5},{2,0},{3,7},{4,6},{5,1},{6,4},{7,3},{8,10},{9,13},{10,... | collective-permute-start | bytes 589832 | tf_op jit(solution)/shard_map/ppermute | solution.py:213
  53.4 25.5 %collective-permute-start.5 = (bf16[1,128,512]{2,1,0:T(8,128)(2,1)S(1)}, bf16[1,128,512]{2,1,0:T(8,128)(2,1)S(1)}, u32[]{:S(2)}, u32[]{:S(2)}) collective-permute-start(bf16[1,128,512]{2,1,0:T(8,128)(2,1)S(1)} %add_convert_fusion.8), channel_id=1, source_target_pairs={{0,8},{1,3},{2,10},{3,1},{4,12},{5,7},{6,14},{7,5},{8,0},{9,11},{1... | collective-permute-start | bytes 393224 | tf_op jit(solution)/shard_map/ppermute | solution.py:213
  54.0 7.8 %collective-permute-start.18 = (bf16[3,64,512]{2,1,0:T(8,128)(2,1)S(1)}, bf16[3,64,512]{2,1,0:T(8,128)(2,1)S(1)}, u32[]{:S(2)}, u32[]{:S(2)}) collective-permute-start(bf16[3,64,512]{2,1,0:T(8,128)(2,1)S(1)} %fusion), channel_id=1, source_target_pairs={{0,4},{1,9},{2,6},{3,11},{4,0},{5,13},{6,2},{7,15},{8,12},{9,1},{1... | collective-permute-start | bytes 589832 | tf_op jit(solution)/shard_map/ppermute | solution.py:213
  57.3 8.6 %collective-permute-start.11 = (bf16[3,64,512]{2,1,0:T(8,128)(2,1)S(1)}, bf16[3,64,512]{2,1,0:T(8,128)(2,1)S(1)}, u32[]{:S(2)}, u32[]{:S(2)}) collective-permute-start(bf16[3,64,512]{2,1,0:T(8,128)(2,1)S(1)} %fusion.1), channel_id=1, source_target_pairs={{0,4},{1,9},{2,6},{3,11},{4,0},{5,13},{6,2},{7,15},{8,12},{9,1},{1... | collective-permute-start | bytes 589832 | tf_op jit(solution)/shard_map/ppermute | solution.py:213
  61.9 13.3 %collective-permute-start.19 = (bf16[3,64,512]{2,1,0:T(8,128)(2,1)S(1)}, bf16[3,64,512]{2,1,0:T(8,128)(2,1)S(1)}, u32[]{:S(2)}, u32[]{:S(2)}) collective-permute-start(bf16[3,64,512]{2,1,0:T(8,128)(2,1)S(1)} %add_convert_fusion.4), channel_id=1, source_target_pairs={{0,8},{1,3},{2,10},{3,1},{4,12},{5,7},{6,14},{7,5},{8,0},{9,11},{1... | collective-permute-start | bytes 589832 | tf_op jit(solution)/shard_map/ppermute | solution.py:213
  66.0 11.3 %collective-permute-start.12 = (bf16[3,64,512]{2,1,0:T(8,128)(2,1)S(1)}, bf16[3,64,512]{2,1,0:T(8,128)(2,1)S(1)}, u32[]{:S(2)}, u32[]{:S(2)}) collective-permute-start(bf16[3,64,512]{2,1,0:T(8,128)(2,1)S(1)} %add_convert_fusion.6), channel_id=1, source_target_pairs={{0,8},{1,3},{2,10},{3,1},{4,12},{5,7},{6,14},{7,5},{8,0},{9,11},{1... | collective-permute-start | bytes 589832 | tf_op jit(solution)/shard_map/ppermute | solution.py:213
  75.2 6.9 %collective-permute-start.20 = (bf16[3,64,512]{2,1,0:T(8,128)(2,1)S(1)}, bf16[3,64,512]{2,1,0:T(8,128)(2,1)S(1)}, u32[]{:S(2)}, u32[]{:S(2)}) collective-permute-start(bf16[3,64,512]{2,1,0:T(8,128)(2,1)S(1)} %add_convert_fusion.3.refs_4_), channel_id=1, source_target_pairs={{0,2},{1,5},{2,0},{3,7},{4,6},{5,1},{6,4},{7,3},{8,10},{9,13},{10,... | collective-permute-start | bytes 589832 | tf_op jit(solution)/shard_map/ppermute | solution.py:213
  77.4 6.2 %collective-permute-start.13 = (bf16[3,64,512]{2,1,0:T(8,128)(2,1)S(1)}, bf16[3,64,512]{2,1,0:T(8,128)(2,1)S(1)}, u32[]{:S(2)}, u32[]{:S(2)}) collective-permute-start(bf16[3,64,512]{2,1,0:T(8,128)(2,1)S(1)} %add_convert_fusion.5.refs_0_), channel_id=1, source_target_pairs={{0,2},{1,5},{2,0},{3,7},{4,6},{5,1},{6,4},{7,3},{8,10},{9,13},{10,... | collective-permute-start | bytes 589832 | tf_op jit(solution)/shard_map/ppermute | solution.py:213
  79.0 2.7 %collective-permute-start.7 = (bf16[1,128,512]{2,1,0:T(8,128)(2,1)S(1)}, bf16[1,128,512]{2,1,0:T(8,128)(2,1)S(1)}, u32[]{:S(2)}, u32[]{:S(2)}) collective-permute-start(bf16[1,128,512]{2,1,0:T(8,128)(2,1)S(1)} %add_convert_fusion.7.refs_0_), channel_id=1, source_target_pairs={{0,1},{1,0},{2,3},{3,2},{4,5},{5,4},{6,7},{7,6},{8,9},{9,8},{10,11... | collective-permute-start | bytes 393224 | tf_op jit(solution)/shard_map/ppermute | solution.py:202
  80.1 5.0 %collective-permute-start.6 = (bf16[1,128,512]{2,1,0:T(8,128)(2,1)S(1)}, bf16[1,128,512]{2,1,0:T(8,128)(2,1)S(1)}, u32[]{:S(2)}, u32[]{:S(2)}) collective-permute-start(bf16[1,128,512]{2,1,0:T(8,128)(2,1)S(1)} %add_convert_fusion.7.refs_0_), channel_id=1, source_target_pairs={{0,2},{1,5},{2,0},{3,7},{4,6},{5,1},{6,4},{7,3},{8,10},{9,13},{10,... | collective-permute-start | bytes 393224 | tf_op jit(solution)/shard_map/ppermute | solution.py:213
  81.6 6.9 %collective-permute-start.21 = (bf16[3,64,512]{2,1,0:T(8,128)(2,1)S(1)}, bf16[3,64,512]{2,1,0:T(8,128)(2,1)S(1)}, u32[]{:S(2)}, u32[]{:S(2)}) collective-permute-start(bf16[3,64,512]{2,1,0:T(8,128)(2,1)S(1)} %add_convert_fusion.3.refs_4_), channel_id=1, source_target_pairs={{0,1},{1,0},{2,3},{3,2},{4,5},{5,4},{6,7},{7,6},{8,9},{9,8},{10,11... | collective-permute-start | bytes 589832 | tf_op jit(solution)/shard_map/ppermute | solution.py:202
  81.7 6.9 %collective-permute-start.14 = (bf16[3,64,512]{2,1,0:T(8,128)(2,1)S(1)}, bf16[3,64,512]{2,1,0:T(8,128)(2,1)S(1)}, u32[]{:S(2)}, u32[]{:S(2)}) collective-permute-start(bf16[3,64,512]{2,1,0:T(8,128)(2,1)S(1)} %add_convert_fusion.5.refs_0_), channel_id=1, source_target_pairs={{0,1},{1,0},{2,3},{3,2},{4,5},{5,4},{6,7},{7,6},{8,9},{9,8},{10,11... | collective-permute-start | bytes 589832 | tf_op jit(solution)/shard_map/ppermute | solution.py:202
  82.1 6.4 %collective-permute-start.22 = (bf16[3,64,512]{2,1,0:T(8,128)(2,1)S(1)}, bf16[3,64,512]{2,1,0:T(8,128)(2,1)S(1)}, u32[]{:S(2)}, u32[]{:S(2)}) collective-permute-start(bf16[3,64,512]{2,1,0:T(8,128)(2,1)S(1)} %collective-permute-done.20.refs_5_), channel_id=1, source_target_pairs={{0,1},{1,0},{2,3},{3,2},{4,5},{5,4},{6,7},{7,6},{8,9},{9,8},{10,11... | collective-permute-start | bytes 589832 | tf_op jit(solution)/shard_map/ppermute | solution.py:202
  83.6 5.0 %collective-permute-start.15 = (bf16[3,64,512]{2,1,0:T(8,128)(2,1)S(1)}, bf16[3,64,512]{2,1,0:T(8,128)(2,1)S(1)}, u32[]{:S(2)}, u32[]{:S(2)}) collective-permute-start(bf16[3,64,512]{2,1,0:T(8,128)(2,1)S(1)} %collective-permute-done.13.refs_1_), channel_id=1, source_target_pairs={{0,1},{1,0},{2,3},{3,2},{4,5},{5,4},{6,7},{7,6},{8,9},{9,8},{10,11... | collective-permute-start | bytes 589832 | tf_op jit(solution)/shard_map/ppermute | solution.py:202
  85.1 1.8 %collective-permute-start.8 = (bf16[1,128,512]{2,1,0:T(8,128)(2,1)S(1)}, bf16[1,128,512]{2,1,0:T(8,128)(2,1)S(1)}, u32[]{:S(2)}, u32[]{:S(2)}) collective-permute-start(bf16[1,128,512]{2,1,0:T(8,128)(2,1)S(1)} %collective-permute-done.6.refs_1_), channel_id=1, source_target_pairs={{0,1},{1,0},{2,3},{3,2},{4,5},{5,4},{6,7},{7,6},{8,9},{9,8},{10,11... | collective-permute-start | bytes 393224 | tf_op jit(solution)/shard_map/ppermute | solution.py:202
  (11 other events, 61.6 us)

commit v3 on v2

--- a/solution.py
+++ b/solution.py
@@ -9,8 +9,10 @@
 BF = jnp.bfloat16
 F32 = jnp.float32
 MIB = 1024 * 1024
+PIECE = 128
 SMEM = pl.BlockSpec(memory_space=pltpu.SMEM)
 VMEM = pl.BlockSpec(memory_space=pltpu.VMEM)
+HBM = pl.BlockSpec(memory_space=pltpu.HBM)
 shape = jax.ShapeDtypeStruct
 
 
@@ -23,22 +25,33 @@
     return pre * sigma, sigma * (1.0 + pre * (1.0 - sigma))
 
 
-def pack_kernel(grid, to_west, to_east, wide):
+def pack_kernel(grid, to_west, to_east, held, wide, sems):
     features, rows, cols = grid.shape
     half = to_west.shape[1] // rows
     block = 2 * half
     last = cols // block - 1
-    for k in (0, last):
-        wide[k] = grid[:, :, k * block : (k + 1) * block].astype(F32).reshape(features * rows, block)
-    lane = lax.broadcasted_iota(jnp.int32, (features, block), 1)
-    for pair in range(rows // 2):
-        even = pl.ds(2 * pair, features, stride=rows)
-        odd = pl.ds(2 * pair + 1, features, stride=rows)
-        at = slice(pair * block, (pair + 1) * block)
-        head = jnp.where(lane < half, wide[0, even, :], pltpu.roll(wide[0, odd, :], half, 1))
-        tail = jnp.where(lane < half, pltpu.roll(wide[last, even, :], half, 1), wide[last, odd, :])
-        to_west[:, at] = head.astype(BF)
-        to_east[:, at] = tail.astype(BF)
+    pieces = []
+    for n, first in enumerate(range(0, features, PIECE)):
+        at = pl.ds(first, min(PIECE, features - first))
+        pieces.append((at, pltpu.make_async_copy(grid.at[at], held.at[at], sems.at[n])))
+    for _, copy in pieces:
+        copy.start()
+    for at, copy in pieces:
+        copy.wait()
+        size = at.size
+        for k in (0, last):
+            wide[k, pl.ds(at.start * rows, size * rows), :] = (
+                held[at, :, k * block : (k + 1) * block].astype(F32).reshape(size * rows, block)
+            )
+        lane = lax.broadcasted_iota(jnp.int32, (size, block), 1)
+        for pair in range(rows // 2):
+            even = pl.ds(at.start * rows + 2 * pair, size, stride=rows)
+            odd = pl.ds(at.start * rows + 2 * pair + 1, size, stride=rows)
+            to = slice(pair * block, (pair + 1) * block)
+            head = jnp.where(lane < half, wide[0, even, :], pltpu.roll(wide[0, odd, :], half, 1))
+            tail = jnp.where(lane < half, pltpu.roll(wide[last, even, :], half, 1), wide[last, odd, :])
+            to_west[at, to] = head.astype(BF)
+            to_east[at, to] = tail.astype(BF)
 
 
 def own_kernel(
@@ -115,78 +128,91 @@
     h_sum[...] = h_own[...] + halo_part(x, embed_t, weights_all[:, first : first + points], slope)
 
 
+def to_chunks(grads, stack, perm):
+    count, matrices, size, _ = grads.shape
+    for j in range(count):
+        at = pl.ds(pl.multiple_of(perm[j] * size, size), size)
+        for k in range(matrices):
+            grads[j, k] = stack[k, at, :]
+
+
+def from_chunks(outs, chunks, perm):
+    j = 0
+    for chunk in chunks:
+        for n in range(chunk.shape[0]):
+            size = chunk.shape[2]
+            at = pl.ds(pl.multiple_of(perm[j] * size, size), size)
+            for k, out in enumerate(outs):
+                out[at, :] = chunk[n, k].astype(F32)
+            j += 1
+
+
 def mesh_kernel(
-    perm, x, embed_t, weights_all, h_sum, message_w, up_w, out_w, gain, mesh_lat, cot, grad_update,
-    mesh_new, mesh_grad, grads_0, grads_1, grad_gain, back, slope, stack,
+    perm, x, embed_t, weights_all, h_sum, message_w, up_w, gain, mesh_lat, cot, grad_update,
+    grads, mesh_grad, grad_gain, grad_aggregate, update, slope, stack,
 ):
     points = x.shape[1]
     first = weights_all.shape[1] - points
     total = h_sum[...] + halo_part(x, embed_t, weights_all[:, first:], slope)
     gathered = total.astype(BF)
-    mesh_rows = mesh_lat[...].astype(F32)
-    summed = mesh_rows + contract(gathered, message_w[...], 1, 0)
+    summed = mesh_lat[...].astype(F32) + contract(gathered, message_w[...], 1, 0)
     rinv = lax.rsqrt(jnp.mean(summed * summed, axis=1, keepdims=True) + epsilon)
     qhat = summed * rinv
     gains = gain[...]
     normed = (qhat * gains).astype(BF)
     pre_up = contract(normed, up_w[...], 1, 0)
     silu_up, up_slope = silu_pair(pre_up)
-    update = silu_up.astype(BF)
+    update[...] = silu_up.astype(BF)
     grad_pre_up = (grad_update[...] * up_slope).astype(BF)
     grad_normed = contract(grad_pre_up, up_w[...], 1, 1)
     grad_gain[...] = jnp.sum(grad_normed * qhat, axis=0, keepdims=True)
     grad_qhat = grad_normed * gains
     grad_q = rinv * (grad_qhat - qhat * jnp.mean(grad_qhat * qhat, axis=1, keepdims=True))
-    grad_aggregate = grad_q.astype(BF)
-    back[...] = contract(message_w[...], grad_aggregate, 1, 1).astype(BF)
+    grad_aggregate[...] = grad_q.astype(BF)
     mesh_grad[...] = cot[...].astype(F32) + grad_q
-    mesh_new[...] = (mesh_rows + contract(update, out_w[...], 1, 0)).astype(BF)
-    stack[0] = contract(gathered, grad_aggregate, 0, 0).astype(BF)
+    stack[0] = contract(gathered, grad_q.astype(BF), 0, 0).astype(BF)
     stack[1] = contract(normed, grad_pre_up, 0, 0).astype(BF)
-    stack[2] = contract(update, cot[...], 0, 0).astype(BF)
-    _, matrices, size, _ = grads_0.shape
-    for j in range(4):
-        at = pl.multiple_of(perm[j] * (2 * size), 2 * size)
-        for k in range(matrices):
-            grads_0[j, k] = stack[k, pl.ds(at, size), :]
-            grads_1[j, k] = stack[k, pl.ds(at + size, size), :]
-
-
-def grid_kernel(perm, back, weights_all, slope_own, slope_west, slope_east, x_own, x_west, x_east, grad_gain, grads, total):
+    to_chunks(grads, stack, perm)
+
+
+def tail_kernel(grad_aggregate, update, message_w, out_w, mesh_lat, cot, back, mesh_new, grad_out):
+    back[...] = contract(message_w[...], grad_aggregate[...], 1, 1).astype(BF)
+    mesh_new[...] = (mesh_lat[...].astype(F32) + contract(update[...], out_w[...], 1, 0)).astype(BF)
+    grad_out[...] = contract(update[...], cot[...], 0, 0).astype(BF)
+
+
+def grid_kernel(
+    perm, back, weights_all, slope_own, slope_west, slope_east, x_own, x_west, x_east, grad_gain, grad_out, grads, stack
+):
     features = x_own.shape[0]
     tile = x_west.shape[1]
     pieces = []
     for x, slope in ((x_own, slope_own), (x_west, slope_west), (x_east, slope_east)):
         pieces += [(x, slope, k) for k in range(x.shape[1] // tile)]
-    sums = jnp.zeros((features, total.shape[1]), F32)
+    sums = jnp.zeros((features, stack.shape[2]), F32)
     for n, (x, slope, k) in enumerate(pieces):
         at = slice(k * tile, (k + 1) * tile)
         hidden = contract(back[...], weights_all[:, n * tile : (n + 1) * tile], 1, 0)
         grad_pre = (hidden * slope[:, at].astype(F32)).astype(BF)
         sums += contract(x[:, at], grad_pre, 1, 1)
-    total[...] = jnp.zeros(total.shape, F32)
-    total[:features, :] = sums
-    total[features : features + 1, :] = grad_gain[...]
-    size = grads.shape[2]
-    for j in range(4):
-        grads[j, 0] = total[pl.ds(pl.multiple_of(perm[j] * size, size), size), :].astype(BF)
+    stack[0] = grad_out[...].astype(F32)
+    stack[1] = jnp.zeros(stack.shape[1:], F32)
+    stack[1, :features, :] = sums
+    stack[1, features : features + 1, :] = grad_gain[...]
+    count, matrices, size, _ = grads.shape
+    for j in range(count):
+        at = pl.ds(pl.multiple_of(perm[j] * size, size), size)
+        for k in range(matrices):
+            grads[j, k] = stack[k, at, :].astype(BF)
 
 
 def order_mesh_kernel(perm, *refs):
-    chunks, outs = refs[:-3], refs[-3:]
-    for part in range(2):
-        for j, chunk in enumerate(chunks[4 * part : 4 * part + 4]):
-            size = chunk.shape[1]
-            at = pl.multiple_of(perm[j] * (2 * size), 2 * size) + part * size
-            for k, out in enumerate(outs):
-                out[pl.ds(at, size), :] = chunk[k].astype(F32)
+    from_chunks(refs[-2:], refs[:-2], perm)
 
 
 def order_grid_kernel(perm, *refs):
-    chunks, (grad_embed, grad_gain, total) = refs[:4], refs[4:]
-    for j, chunk in enumerate(chunks):
-        size = chunk.shape[1]
-        total[pl.ds(pl.multiple_of(perm[j] * size, size), size), :] = chunk[0].astype(F32)
+    grad_out, grad_embed, grad_gain, total = refs[-4:]
+    from_chunks((grad_out, total), refs[:-4], perm)
     features = grad_embed.shape[0]
     grad_embed[...] = total[:features, :]
     grad_gain[...] = total[features : features + 1, :]
@@ -215,23 +241,31 @@
 
 def chunk_order():
     core = lax.axis_index("lat") & 1
-    side = [((lax.axis_index(axis) & bit) != 0).astype(jnp.int32) for axis, bit in (s[0] for s in role_steps())]
-    mine = jnp.where(core == 0, side[0], side[1])
-    theirs = jnp.where(core == 0, side[1], side[0])
-    return jnp.stack([2 * core + mine, 2 * core + 1 - mine, 2 - 2 * core + theirs, 3 - 2 * core - theirs])
+    sides = []
+    for steps in role_steps():
+        low = [((lax.axis_index(axis) & bit) != 0).astype(jnp.int32) for axis, bit in steps[:2]]
+        sides.append(2 * low[0] + low[1])
+    mine = jnp.where(core == 0, sides[0], sides[1])
+    theirs = jnp.where(core == 0, sides[1], sides[0])
+    return jnp.stack([4 * core + (mine ^ j) for j in range(4)] + [4 - 4 * core + (theirs ^ j) for j in range(4)])
 
 
 def added(a, b):
     return (a.astype(F32) + b.astype(F32)).astype(BF)
 
 
-def all_summed(grads):
-    kept = added(grads[:2], core_swapped(grads[2:]))
-    mine = added(kept[0], swapped(kept[1], 0))
-    for step in range(1, len(role_steps()[0])):
+def core_summed(grads):
+    return added(grads[:4], core_swapped(grads[4:]))
+
+
+def all_summed(kept):
+    kept = added(kept[:2], swapped(kept[2:], 0))
+    mine = added(kept[:1], swapped(kept[1:], 1))
+    for step in range(2, len(role_steps()[0])):
         mine = added(mine, swapped(mine, step))
-    partners = swapped(mine, 0)
-    return mine, partners, core_swapped(mine), core_swapped(partners)
+    second = swapped(mine, 1)
+    first = swapped(jnp.concatenate([mine, second]), 0)
+    return mine, second, first, core_swapped(mine), core_swapped(second), core_swapped(first)
 
 
 def on_device(grid_in, mesh_lat, edge_w, edge_src, edge_dst, block_count, embed_w, message_w, up_w, out_w, gain, cot):
@@ -258,8 +292,12 @@
         )
 
     to_west, to_east = call(
-        pack_kernel, "pack", [VMEM], [shape((features, side), BF)] * 2, 0, 3 * MIB, 20,
-        [pltpu.VMEM((cols // block, features * rows, block), F32)],
+        pack_kernel, "pack", [HBM], [shape((features, side), BF)] * 2, 0, 3 * MIB, 20,
+        [
+            pltpu.VMEM((features, rows, cols), BF),
+            pltpu.VMEM((cols // block, features * rows, block), F32),
+            pltpu.SemaphoreType.DMA((-(-features // PIECE),)),
+        ],
     )(grid)
     count = lax.axis_size("lon")
     x_west = lax.ppermute(to_east, "lon", [(i, (i + 1) % count) for i in range(count)])
@@ -286,38 +324,43 @@
     )(x_west, embed_t, weights_all, h_own)
 
     perm = chunk_order()
-    mesh_new, mesh_grad, grads_0, grads_1, gain_term, back, slope_east = call(
-        mesh_kernel, "mesh_nodes", [SMEM] + [VMEM] * 11,
+    grads_a, mesh_grad, gain_term, grad_aggregate, update, slope_east = call(
+        mesh_kernel, "mesh_nodes", [SMEM] + [VMEM] * 10,
         [
+            shape((8, 2, latent // 8, latent), BF),
+            shape((nodes, latent), F32),
+            shape((1, latent), F32),
             shape((nodes, latent), BF),
-            shape((nodes, latent), F32),
-            shape((4, 3, latent // 8, latent), BF),
-            shape((4, 3, latent // 8, latent), BF),
-            shape((1, latent), F32),
-            shape((latent, nodes), BF),
+            shape((nodes, latent), BF),
             shape((latent, side), BF),
         ],
-        2_000_000_000, 8 * MIB, 16, [pltpu.VMEM((3, latent, latent), BF)],
-    )(
-        perm, x_east, embed_t, weights_all, h_sum, message_w, up_w, out_w, gain.reshape(1, latent),
-        mesh_lat, cot, grad_update,
-    )
-
+        2_000_000_000, 8 * MIB, 16, [pltpu.VMEM((2, latent, latent), BF)],
+    )(perm, x_east, embed_t, weights_all, h_sum, message_w, up_w, gain.reshape(1, latent), mesh_lat, cot, grad_update)
+    back, mesh_new, grad_out_term = call(
+        tail_kernel, "mesh_tail", [VMEM] * 6,
+        [shape((latent, nodes), BF), shape((nodes, latent), BF), shape((latent, latent), BF)],
+        400_000_000, 3 * MIB, 16,
+    )(grad_aggregate, update, message_w, out_w, mesh_lat, cot)
+
+    kept_a, back = lax.optimization_barrier((core_summed(grads_a), back))
     padded = -(-(features + 1) // 128) * 128
-    (grads_2,) = call(
-        grid_kernel, "grid_points", [SMEM] + [VMEM] * 9, [shape((4, 1, padded // 4, latent), BF)],
-        2_400_000_000, 9 * MIB, 16, [pltpu.VMEM((padded, latent), F32)],
-    )(perm, back, weights_all, slope_own, slope_west, slope_east, x_own, x_west, x_east, gain_term)
-
-    summed = [all_summed(grads) for grads in (grads_0, grads_1, grads_2)]
-    grad_message, grad_up, grad_out = call(
-        order_mesh_kernel, "order_mesh", [SMEM] + [VMEM] * 8, [shape((latent, latent), F32)] * 3, 0, 5 * MIB, 16
-    )(perm, *summed[0], *summed[1])
-    grad_embed, grad_gain = call(
-        order_grid_kernel, "order_grid", [SMEM] + [VMEM] * 4,
-        [shape((features, latent), F32), shape((1, latent), F32)], 0, 2 * MIB, 16,
-        [pltpu.VMEM((padded, latent), F32)],
-    )(perm, *summed[2])
+    assert padded == latent
+    (grads_b,) = call(
+        grid_kernel, "grid_points", [SMEM] + [VMEM] * 10, [shape((8, 2, latent // 8, latent), BF)],
+        2_400_000_000, 9 * MIB, 16, [pltpu.VMEM((2, latent, latent), F32)],
+    )(perm, back, weights_all, slope_own, slope_west, slope_east, x_own, x_west, x_east, gain_term, grad_out_term)
+
+    summed_a = all_summed(kept_a)
+    summed_b = all_summed(core_summed(grads_b))
+    square = shape((latent, latent), F32)
+    grad_message, grad_up = call(
+        order_mesh_kernel, "order_a", [SMEM] + [VMEM] * 6, [square, square], 0, 3 * MIB, 16
+    )(perm, *summed_a)
+    grad_out, grad_embed, grad_gain = call(
+        order_grid_kernel, "order_b", [SMEM] + [VMEM] * 6,
+        [square, shape((features, latent), F32), shape((1, latent), F32)], 0, 3 * MIB, 16,
+        [pltpu.VMEM((latent, latent), F32)],
+    )(perm, *summed_b)
     return (mesh_new, mesh_grad, grad_embed, grad_message, grad_up, grad_out, grad_gain[0])
 
 

time: 91.3 us -> 84.6 us (0.927)
  starting transfers between devices: 28.9 us -> 23.8 us
  waiting for transfers between devices: 31.9 us -> 30.7 us
    ppermute x1, waiting for transfers between devices: 9.13 us -> 0.15 us  [on_device(): lax.ppermute(to_east, 'lon', [(i, (i + 1) % count) for i in range(count)])]
    ppermute x1, waiting for transfers between devices: 0.01 us -> 8.01 us  [on_device(): lax.ppermute(to_west, 'lon', [((i + 1) % count, i) for i in range(count)])]
    ppermute x1, starting transfers between devices: 0.01 us -> 3.08 us  [on_device(): lax.ppermute(to_east, 'lon', [(i, (i + 1) % count) for i in range(count)])]
    ppermute x1, starting transfers between devices: 5.05 us -> 2.09 us  [on_device(): lax.ppermute(to_west, 'lon', [((i + 1) % count, i) for i in range(count)])]
    ppermute x9 -> x8, starting transfers between devices: 4.54 us -> 1.8 us  [core_swapped(): lax.ppermute(value, 'lat', [(i, i ^ 1) for i in range(lax.axis_size('lat'...]
    ppermute x12 -> x10, starting transfers between devices: 19.3 us -> 16.8 us  [swapped(): return lax.ppermute(value, ('lon', 'lat'), pairs)]
    pallas_call x5 -> x6, Pallas kernels: 13.3 us -> 13.8 us  [the longest x1 3.51 us: on_device(): call(grid_kernel, 'grid_points', [SMEM] + [VMEM] * 10, [shape((8, 2, late...]
    ppermute x9 -> x8, waiting for transfers between devices: 1.93 us -> 1.68 us  [core_swapped(): lax.ppermute(value, 'lat', [(i, i ^ 1) for i in range(lax.axis_size('lat'...]
  transfers between devices with their start and end apart: 23 -> 20, of which waited for: 12 -> 13; matrix products, arithmetic and copies ran while one was open for 1% -> 1% of each run, Pallas kernels for 11% -> 13%
where the time goes in v3:
time: 84.6 us; the launch traced here: 84.3 us
  waiting for transfers between devices  30.7 us (36%)
  starting transfers between devices  23.8 us (28%)
  Pallas kernels  21.6 us (26%)
  local copies, waits for them, and re-layouts  6.04 us (7%)
  between operations  1.53 us (2%)
    ppermute x10, waiting for transfers between devices, swapped(): return lax.ppermute(value, ('lon', 'lat'), pairs)  20.9 us
    ppermute x10, starting transfers between devices, swapped(): return lax.ppermute(value, ('lon', 'lat'), pairs)  16.8 us
    ppermute x1, waiting for transfers between devices, on_device(): lax.ppermute(to_west, 'lon', [((i + 1) % count, i) for i in range(count)])  8.01 us
    pallas_call x1, Pallas kernels, on_device(): call(own_kernel, 'own_points', [SMEM] * 3 + [VMEM] * 5, [shape((nodes, po...  7.03 us
    unnamed x24, local copies, waits for them, and re-layouts  5.82 us
    pallas_call x1, Pallas kernels, on_device(): call(grid_kernel, 'grid_points', [SMEM] + [VMEM] * 10, [shape((8, 2, late...  3.51 us
    pallas_call x1, Pallas kernels, on_device(): call(mesh_kernel, 'mesh_nodes', [SMEM] + [VMEM] * 10, [shape((8, 2, laten...  3.09 us
    ppermute x1, starting transfers between devices, on_device(): lax.ppermute(to_east, 'lon', [(i, (i + 1) % count) for i in range(count)])  3.08 us
  transfers between devices with their start and end apart: 20, of which 13 were waited for; matrix products, arithmetic and copies ran while one was open for 1% of the time, Pallas kernels for 13%

profile of v3, /device:TPU:0, one launch (start us, length us, event | category | flops | bytes accessed | tf_op | source)
XLA Modules:
  0.0 84.3 jit_solution(4800631269802872352)
XLA Ops:
  0.7 1.5 %copy-done = bf16[8,256,474]{1,0,2:T(8,128)(2,1)S(1)} copy-done((bf16[8,256,474]{1,0,2:T(8,128)(2,1)S(1)}, bf16[8,256,474]{1,0,2:T(8,128)(2,1)}, u32[]{:S(2)}) %copy-start) | copy-done | bytes 1941528
  2.2 2.0 %pack.1 = (bf16[474,512]{1,0:T(8,128)(2,1)S(1)}, bf16[474,512]{1,0:T(8,128)(2,1)}) custom-call(bf16[474,8,256]{2,1,0:T(8,128)(2,1)S(1)} %bitcast.11), custom_call_target="tpu_custom_call" | custom-call | bytes 3145728 | tf_op jit(solution)/shard_map/pack/pallas_call | solution.py:294
  4.2 3.1 %collective-permute-start.1 = (bf16[474,512]{1,0:T(8,128)(2,1)}, bf16[474,512]{1,0:T(8,128)(2,1)S(1)}, u32[]{:S(2)}, u32[]{:S(2)}) collective-permute-start(bf16[474,512]{1,0:T(8,128)(2,1)} %get-tuple-element.36), channel_id=1, source_target_pairs={{0,4},{4,8},{8,12},{12,0},{1,5},{5,9},{9,13},{13,1},{2,6},{6,10},{... | collective-permute-start | bytes 1456136 | tf_op jit(solution)/shard_map/ppermute | solution.py:303
  7.3 2.1 %collective-permute-start = (bf16[474,512]{1,0:T(8,128)(2,1)S(1)}, bf16[474,512]{1,0:T(8,128)(2,1)S(1)}, u32[]{:S(2)}, u32[]{:S(2)}) collective-permute-start(bf16[474,512]{1,0:T(8,128)(2,1)S(1)} %get-tuple-element.33), channel_id=1, source_target_pairs={{4,0},{8,4},{12,8},{0,12},{5,1},{9,5},{13,9},{1,13},{6,2},{10,6},{... | collective-permute-start | bytes 1456136 | tf_op jit(solution)/shard_map/ppermute | solution.py:304
  14.4 7.0 %own_points.1 = (bf16[256,3072]{1,0:T(8,128)(2,1)S(1)}, bf16[474,2048]{1,0:T(8,128)(2,1)S(1)}, bf16[512,474]{1,0:T(8,128)(2,1)S(1)}, f32[256,512]{1,0:T(8,128)S(...) custom-call(s32[32]{0:T(128)S(1)} %copy-done.10, s32[32]{0:T(128)S(1)} %copy-done.11, s32[1]{0:T(128)S(6)} %copy.19.count, ...), custom_call_target="tpu_custom_call" | custom-call | flops 4000000000 | bytes 12582912 | tf_op jit(solution)/shard_map/own_points/pallas_call | solution.py:306
  22.5 8.0 %collective-permute-done.x.x_east = bf16[474,512]{1,0:T(8,128)(2,1)S(1)} collective-permute-done((bf16[474,512]{1,0:T(8,128)(2,1)S(1)}, bf16[474,512]{1,0:T(8,128)(2,1)S(1)}, u32[]{:S(2)}, u32[]{:S(2)}) %collective-permute-start) | collective-permute-done | bytes 485408 | tf_op jit(solution)/shard_map/ppermute | solution.py:304
  30.5 3.1 %mesh_nodes.1 = (bf16[8,2,64,512]{3,2,1,0:T(8,128)(2,1)S(1)}, f32[256,512]{1,0:T(8,128)}, f32[1,512]{1,0:T(1,128)S(1)}, bf16[256,512]{1,0:T(8,128)(2,1)S(1)}, bf...) custom-call(s32[8]{0:T(128)S(1)} %stack.35.perm, bf16[474,512]{1,0:T(8,128)(2,1)S(1)} %collective-permute-done.x.x_east, ...), custom_call_target="tpu_custom_call" | custom-call | flops 2000000000 | bytes 8388608 | tf_op jit(solution)/shard_map/mesh_nodes/pallas_call | solution.py:327
  35.8 3.5 %grid_points.1 = bf16[8,2,64,512]{3,2,1,0:T(8,128)(2,1)S(1)} custom-call(s32[8]{0:T(128)S(1)} %stack.35.perm, bf16[512,256]{1,0:T(8,128)(2,1)S(1)} %get-tuple-element.46.back, bf16[256,3072]{1,0:T(8,128)(2,1)S(1)} %get-tuple-element.35.refs_2_.weights_all, bf16[512,2048]{1,0:T(8,128)(2,1)S(1)} %get-tuple-element.47.slope_own, ...), custom_call_target="tpu_custom_call" | custom-call | flops 2400000000 | bytes 9437184 | tf_op jit(solution)/shard_map/grid_points/pallas_call | solution.py:348
  39.6 1.6 %collective-permute-start.12 = (bf16[2,2,64,512]{3,2,1,0:T(8,128)(2,1)S(1)}, bf16[2,2,64,512]{3,2,1,0:T(8,128)(2,1)S(1)}, u32[]{:S(2)}, u32[]{:S(2)}) collective-permute-start(bf16[2,2,64,512]{3,2,1,0:T(8,128)(2,1)S(1)} %slice.45), channel_id=1, source_target_pairs={{0,2},{1,5},{2,0},{3,7},{4,6},{5,1},{6,4},{7,3},{8,10},{9,13},{10,... | collective-permute-start | bytes 786440 | tf_op jit(solution)/shard_map/ppermute | solution.py:239
  41.5 1.6 %collective-permute-start.4 = (bf16[2,2,64,512]{3,2,1,0:T(8,128)(2,1)S(1)}, bf16[2,2,64,512]{3,2,1,0:T(8,128)(2,1)S(1)}, u32[]{:S(2)}, u32[]{:S(2)}) collective-permute-start(bf16[2,2,64,512]{3,2,1,0:T(8,128)(2,1)S(1)} %slice.51), channel_id=1, source_target_pairs={{0,2},{1,5},{2,0},{3,7},{4,6},{5,1},{6,4},{7,3},{8,10},{9,13},{10,... | collective-permute-start | bytes 786440 | tf_op jit(solution)/shard_map/ppermute | solution.py:239
  43.1 3.0 %collective-permute-done.12 = bf16[2,2,64,512]{3,2,1,0:T(8,128)(2,1)S(1)} collective-permute-done((bf16[2,2,64,512]{3,2,1,0:T(8,128)(2,1)S(1)}, bf16[2,2,64,512]{3,2,1,0:T(8,128)(2,1)S(1)}, u32[]{:S(2)}, u32[]{:S(2)}) %collective-permute-start.12) | collective-permute-done | bytes 262176 | tf_op jit(solution)/shard_map/ppermute | solution.py:239
  46.1 1.4 %collective-permute-start.13 = (bf16[1,2,64,512]{3,2,1,0:T(8,128)(2,1)S(1)}, bf16[1,2,64,512]{3,2,1,0:T(8,128)(2,1)S(1)}, u32[]{:S(2)}, u32[]{:S(2)}) collective-permute-start(bf16[1,2,64,512]{3,2,1,0:T(8,128)(2,1)S(1)} %slice.55), channel_id=1, source_target_pairs={{0,4},{1,9},{2,6},{3,11},{4,0},{5,13},{6,2},{7,15},{8,12},{9,1},{1... | collective-permute-start | bytes 393224 | tf_op jit(solution)/shard_map/ppermute | solution.py:239
  47.5 1.3 %collective-permute-done.4 = bf16[2,2,64,512]{3,2,1,0:T(8,128)(2,1)S(1)} collective-permute-done((bf16[2,2,64,512]{3,2,1,0:T(8,128)(2,1)S(1)}, bf16[2,2,64,512]{3,2,1,0:T(8,128)(2,1)S(1)}, u32[]{:S(2)}, u32[]{:S(2)}) %collective-permute-start.4) | collective-permute-done | bytes 262176 | tf_op jit(solution)/shard_map/ppermute | solution.py:239
  48.9 1.4 %collective-permute-start.5 = (bf16[1,2,64,512]{3,2,1,0:T(8,128)(2,1)S(1)}, bf16[1,2,64,512]{3,2,1,0:T(8,128)(2,1)S(1)}, u32[]{:S(2)}, u32[]{:S(2)}) collective-permute-start(bf16[1,2,64,512]{3,2,1,0:T(8,128)(2,1)S(1)} %slice.53), channel_id=1, source_target_pairs={{0,4},{1,9},{2,6},{3,11},{4,0},{5,13},{6,2},{7,15},{8,12},{9,1},{1... | collective-permute-start | bytes 393224 | tf_op jit(solution)/shard_map/ppermute | solution.py:239
  51.6 2.4 %collective-permute-start.14 = (bf16[1,2,64,512]{3,2,1,0:T(8,128)(2,1)S(1)}, bf16[1,2,64,512]{3,2,1,0:T(8,128)(2,1)S(1)}, u32[]{:S(2)}, u32[]{:S(2)}) collective-permute-start(bf16[1,2,64,512]{3,2,1,0:T(8,128)(2,1)S(1)} %add_convert_fusion.5), channel_id=1, source_target_pairs={{0,8},{1,3},{2,10},{3,1},{4,12},{5,7},{6,14},{7,5},{8,0},{9,11},{1... | collective-permute-start | bytes 393224 | tf_op jit(solution)/shard_map/ppermute | solution.py:239
  54.5 2.3 %collective-permute-start.6 = (bf16[1,2,64,512]{3,2,1,0:T(8,128)(2,1)S(1)}, bf16[1,2,64,512]{3,2,1,0:T(8,128)(2,1)S(1)}, u32[]{:S(2)}, u32[]{:S(2)}) collective-permute-start(bf16[1,2,64,512]{3,2,1,0:T(8,128)(2,1)S(1)} %add_convert_fusion.7), channel_id=1, source_target_pairs={{0,8},{1,3},{2,10},{3,1},{4,12},{5,7},{6,14},{7,5},{8,0},{9,11},{1... | collective-permute-start | bytes 393224 | tf_op jit(solution)/shard_map/ppermute | solution.py:239
  57.6 2.1 %collective-permute-start.15 = (bf16[1,2,64,512]{3,2,1,0:T(8,128)(2,1)S(1)}, bf16[1,2,64,512]{3,2,1,0:T(8,128)(2,1)S(1)}, u32[]{:S(2)}, u32[]{:S(2)}) collective-permute-start(bf16[1,2,64,512]{3,2,1,0:T(8,128)(2,1)S(1)} %add_convert_fusion.4.refs_0_), channel_id=1, source_target_pairs={{0,4},{1,9},{2,6},{3,11},{4,0},{5,13},{6,2},{7,15},{8,12},{9,1},{1... | collective-permute-start | bytes 393224 | tf_op jit(solution)/shard_map/ppermute | solution.py:239
  59.7 6.0 %collective-permute-done.6 = bf16[1,2,64,512]{3,2,1,0:T(8,128)(2,1)S(1)} collective-permute-done((bf16[1,2,64,512]{3,2,1,0:T(8,128)(2,1)S(1)}, bf16[1,2,64,512]{3,2,1,0:T(8,128)(2,1)S(1)}, u32[]{:S(2)}, u32[]{:S(2)}) %collective-permute-start.6) | collective-permute-done | bytes 131104 | tf_op jit(solution)/shard_map/ppermute | solution.py:239
  66.6 1.6 %collective-permute-start.16 = (bf16[2,2,64,512]{3,2,1,0:T(8,128)(2,1)S(1)}, bf16[2,2,64,512]{3,2,1,0:T(8,128)(2,1)S(1)}, u32[]{:S(2)}, u32[]{:S(2)}) collective-permute-start(bf16[2,2,64,512]{3,2,1,0:T(8,128)(2,1)S(1)} %pad_maximum_fusion.1), channel_id=1, source_target_pairs={{0,2},{1,5},{2,0},{3,7},{4,6},{5,1},{6,4},{7,3},{8,10},{9,13},{10,... | collective-permute-start | bytes 786440 | tf_op jit(solution)/shard_map/ppermute | solution.py:239
  68.1 4.0 %collective-permute-done.7.refs_1_ = bf16[1,2,64,512]{3,2,1,0:T(8,128)(2,1)S(1)} collective-permute-done((bf16[1,2,64,512]{3,2,1,0:T(8,128)(2,1)S(1)}, bf16[1,2,64,512]{3,2,1,0:T(8,128)(2,1)S(1)}, u32[]{:S(2)}, u32[]{:S(2)}) %collective-permute-start.7) | collective-permute-done | bytes 131104 | tf_op jit(solution)/shard_map/ppermute | solution.py:239
  72.1 1.7 %collective-permute-start.8 = (bf16[2,2,64,512]{3,2,1,0:T(8,128)(2,1)S(1)}, bf16[2,2,64,512]{3,2,1,0:T(8,128)(2,1)S(1)}, u32[]{:S(2)}, u32[]{:S(2)}) collective-permute-start(bf16[2,2,64,512]{3,2,1,0:T(8,128)(2,1)S(1)} %pad_maximum_fusion), channel_id=1, source_target_pairs={{0,2},{1,5},{2,0},{3,7},{4,6},{5,1},{6,4},{7,3},{8,10},{9,13},{10,... | collective-permute-start | bytes 786440 | tf_op jit(solution)/shard_map/ppermute | solution.py:239
  74.4 4.2 %collective-permute-done.8.refs_2_ = bf16[2,2,64,512]{3,2,1,0:T(8,128)(2,1)S(1)} collective-permute-done((bf16[2,2,64,512]{3,2,1,0:T(8,128)(2,1)S(1)}, bf16[2,2,64,512]{3,2,1,0:T(8,128)(2,1)S(1)}, u32[]{:S(2)}, u32[]{:S(2)}) %collective-permute-start.8) | collective-permute-done | bytes 262176 | tf_op jit(solution)/shard_map/ppermute | solution.py:239
  80.3 2.0 %order_a.1 = (f32[512,512]{1,0:T(8,128)}, f32[512,512]{1,0:T(8,128)}) custom-call(s32[8]{0:T(128)S(1)} %stack.35.perm, bf16[1,2,64,512]{3,2,1,0:T(8,128)(2,1)S(1)} %add_convert_fusion.4.refs_0_, bf16[1,2,64,512]{3,2,1,0:T(8,128)(2,1)S(1)} %collective-permute-done.15.refs_1_, bf16[2,2,64,512]{3,2,1,0:T(8,128)(2,1)S(1)} %collective-permute-done.16.refs_2_, ...), custom_call_target="tpu_custom_call" | custom-call | bytes 3145728 | tf_op jit(solution)/shard_map/order_a/pallas_call | solution.py:356
  82.3 2.0 %order_b.1 = (f32[512,512]{1,0:T(8,128)}, f32[474,512]{1,0:T(8,128)}, f32[1,512]{1,0:T(1,128)}) custom-call(s32[8]{0:T(128)S(1)} %stack.35.perm, bf16[1,2,64,512]{3,2,1,0:T(8,128)(2,1)S(1)} %add_convert_fusion.6.refs_0_, bf16[1,2,64,512]{3,2,1,0:T(8,128)(2,1)S(1)} %collective-permute-done.7.refs_1_, ...), custom_call_target="tpu_custom_call" | custom-call | bytes 3145728 | tf_op jit(solution)/shard_map/order_b/pallas_call | solution.py:359
  (65 shorter events, 14.1 us)
Async XLA Ops:
  0.6 9.5 %copy-start.11 = (s32[32]{0:T(128)S(1)}, s32[32]{0:T(128)}, u32[]{:S(2)}) copy-start(s32[32]{0:T(128)} %dst.1) | copy-start | bytes 388
  0.6 9.5 %copy-start.10 = (s32[32]{0:T(128)S(1)}, s32[32]{0:T(128)}, u32[]{:S(2)}) copy-start(s32[32]{0:T(128)} %src.1) | copy-start | bytes 388
  4.2 17.4 %collective-permute-start.1 = (bf16[474,512]{1,0:T(8,128)(2,1)}, bf16[474,512]{1,0:T(8,128)(2,1)S(1)}, u32[]{:S(2)}, u32[]{:S(2)}) collective-permute-start(bf16[474,512]{1,0:T(8,128)(2,1)} %get-tuple-element.36), channel_id=1, source_target_pairs={{0,4},{4,8},{8,12},{12,0},{1,5},{5,9},{9,13},{13,1},{2,6},{6,10},{... | collective-permute-start | bytes 1456136 | tf_op jit(solution)/shard_map/ppermute | solution.py:303
  7.3 23.2 %collective-permute-start = (bf16[474,512]{1,0:T(8,128)(2,1)S(1)}, bf16[474,512]{1,0:T(8,128)(2,1)S(1)}, u32[]{:S(2)}, u32[]{:S(2)}) collective-permute-start(bf16[474,512]{1,0:T(8,128)(2,1)S(1)} %get-tuple-element.33), channel_id=1, source_target_pairs={{4,0},{8,4},{12,8},{0,12},{5,1},{9,5},{13,9},{1,13},{6,2},{10,6},{... | collective-permute-start | bytes 1456136 | tf_op jit(solution)/shard_map/ppermute | solution.py:304
  21.4 9.1 %copy-start.3 = (bf16[512,512]{1,0:T(8,128)(2,1)S(1)}, bf16[512,512]{1,0:T(8,128)(2,1)}, u32[]{:S(2)}) copy-start(bf16[512,512]{1,0:T(8,128)(2,1)} %message_w.3) | copy-start | bytes 1572868
  21.4 9.1 %copy-start.5 = (bf16[256,512]{1,0:T(8,128)(2,1)S(1)}, bf16[256,512]{1,0:T(8,128)(2,1)}, u32[]{:S(2)}) copy-start(bf16[256,512]{1,0:T(8,128)(2,1)} %mesh_lat.3) | copy-start | bytes 786436
  33.7 2.0 %collective-permute-start.2 = (bf16[4,2,64,512]{3,2,1,0:T(8,128)(2,1)S(1)}, bf16[4,2,64,512]{3,2,1,0:T(8,128)(2,1)S(1)}, u32[]{:S(2)}, u32[]{:S(2)}) collective-permute-start(bf16[4,2,64,512]{3,2,1,0:T(8,128)(2,1)S(1)} %slice.37), channel_id=1, source_target_pairs={{0,1},{1,0},{2,3},{3,2},{4,5},{5,4},{6,7},{7,6},{8,9},{9,8},{10,11... | collective-permute-start | bytes 1572872 | tf_op jit(solution)/shard_map/ppermute | solution.py:228
  39.4 2.0 %collective-permute-start.3 = (bf16[4,2,64,512]{3,2,1,0:T(8,128)(2,1)S(1)}, bf16[4,2,64,512]{3,2,1,0:T(8,128)(2,1)S(1)}, u32[]{:S(2)}, u32[]{:S(2)}) collective-permute-start(bf16[4,2,64,512]{3,2,1,0:T(8,128)(2,1)S(1)} %slice.49), channel_id=1, source_target_pairs={{0,1},{1,0},{2,3},{3,2},{4,5},{5,4},{6,7},{7,6},{8,9},{9,8},{10,11... | collective-permute-start | bytes 1572872 | tf_op jit(solution)/shard_map/ppermute | solution.py:228
  39.6 6.4 %collective-permute-start.12 = (bf16[2,2,64,512]{3,2,1,0:T(8,128)(2,1)S(1)}, bf16[2,2,64,512]{3,2,1,0:T(8,128)(2,1)S(1)}, u32[]{:S(2)}, u32[]{:S(2)}) collective-permute-start(bf16[2,2,64,512]{3,2,1,0:T(8,128)(2,1)S(1)} %slice.45), channel_id=1, source_target_pairs={{0,2},{1,5},{2,0},{3,7},{4,6},{5,1},{6,4},{7,3},{8,10},{9,13},{10,... | collective-permute-start | bytes 786440 | tf_op jit(solution)/shard_map/ppermute | solution.py:239
  41.5 7.3 %collective-permute-start.4 = (bf16[2,2,64,512]{3,2,1,0:T(8,128)(2,1)S(1)}, bf16[2,2,64,512]{3,2,1,0:T(8,128)(2,1)S(1)}, u32[]{:S(2)}, u32[]{:S(2)}) collective-permute-start(bf16[2,2,64,512]{3,2,1,0:T(8,128)(2,1)S(1)} %slice.51), channel_id=1, source_target_pairs={{0,2},{1,5},{2,0},{3,7},{4,6},{5,1},{6,4},{7,3},{8,10},{9,13},{10,... | collective-permute-start | bytes 786440 | tf_op jit(solution)/shard_map/ppermute | solution.py:239
  46.1 5.5 %collective-permute-start.13 = (bf16[1,2,64,512]{3,2,1,0:T(8,128)(2,1)S(1)}, bf16[1,2,64,512]{3,2,1,0:T(8,128)(2,1)S(1)}, u32[]{:S(2)}, u32[]{:S(2)}) collective-permute-start(bf16[1,2,64,512]{3,2,1,0:T(8,128)(2,1)S(1)} %slice.55), channel_id=1, source_target_pairs={{0,4},{1,9},{2,6},{3,11},{4,0},{5,13},{6,2},{7,15},{8,12},{9,1},{1... | collective-permute-start | bytes 393224 | tf_op jit(solution)/shard_map/ppermute | solution.py:239
  48.9 5.6 %collective-permute-start.5 = (bf16[1,2,64,512]{3,2,1,0:T(8,128)(2,1)S(1)}, bf16[1,2,64,512]{3,2,1,0:T(8,128)(2,1)S(1)}, u32[]{:S(2)}, u32[]{:S(2)}) collective-permute-start(bf16[1,2,64,512]{3,2,1,0:T(8,128)(2,1)S(1)} %slice.53), channel_id=1, source_target_pairs={{0,4},{1,9},{2,6},{3,11},{4,0},{5,13},{6,2},{7,15},{8,12},{9,1},{1... | collective-permute-start | bytes 393224 | tf_op jit(solution)/shard_map/ppermute | solution.py:239
  51.6 5.9 %collective-permute-start.14 = (bf16[1,2,64,512]{3,2,1,0:T(8,128)(2,1)S(1)}, bf16[1,2,64,512]{3,2,1,0:T(8,128)(2,1)S(1)}, u32[]{:S(2)}, u32[]{:S(2)}) collective-permute-start(bf16[1,2,64,512]{3,2,1,0:T(8,128)(2,1)S(1)} %add_convert_fusion.5), channel_id=1, source_target_pairs={{0,8},{1,3},{2,10},{3,1},{4,12},{5,7},{6,14},{7,5},{8,0},{9,11},{1... | collective-permute-start | bytes 393224 | tf_op jit(solution)/shard_map/ppermute | solution.py:239
  54.5 11.1 %collective-permute-start.6 = (bf16[1,2,64,512]{3,2,1,0:T(8,128)(2,1)S(1)}, bf16[1,2,64,512]{3,2,1,0:T(8,128)(2,1)S(1)}, u32[]{:S(2)}, u32[]{:S(2)}) collective-permute-start(bf16[1,2,64,512]{3,2,1,0:T(8,128)(2,1)S(1)} %add_convert_fusion.7), channel_id=1, source_target_pairs={{0,8},{1,3},{2,10},{3,1},{4,12},{5,7},{6,14},{7,5},{8,0},{9,11},{1... | collective-permute-start | bytes 393224 | tf_op jit(solution)/shard_map/ppermute | solution.py:239
  57.6 9.0 %collective-permute-start.15 = (bf16[1,2,64,512]{3,2,1,0:T(8,128)(2,1)S(1)}, bf16[1,2,64,512]{3,2,1,0:T(8,128)(2,1)S(1)}, u32[]{:S(2)}, u32[]{:S(2)}) collective-permute-start(bf16[1,2,64,512]{3,2,1,0:T(8,128)(2,1)S(1)} %add_convert_fusion.4.refs_0_), channel_id=1, source_target_pairs={{0,4},{1,9},{2,6},{3,11},{4,0},{5,13},{6,2},{7,15},{8,12},{9,1},{1... | collective-permute-start | bytes 393224 | tf_op jit(solution)/shard_map/ppermute | solution.py:239
  65.7 6.4 %collective-permute-start.7 = (bf16[1,2,64,512]{3,2,1,0:T(8,128)(2,1)S(1)}, bf16[1,2,64,512]{3,2,1,0:T(8,128)(2,1)S(1)}, u32[]{:S(2)}, u32[]{:S(2)}) collective-permute-start(bf16[1,2,64,512]{3,2,1,0:T(8,128)(2,1)S(1)} %add_convert_fusion.6.refs_0_), channel_id=1, source_target_pairs={{0,4},{1,9},{2,6},{3,11},{4,0},{5,13},{6,2},{7,15},{8,12},{9,1},{1... | collective-permute-start | bytes 393224 | tf_op jit(solution)/shard_map/ppermute | solution.py:239
  66.6 7.3 %collective-permute-start.16 = (bf16[2,2,64,512]{3,2,1,0:T(8,128)(2,1)S(1)}, bf16[2,2,64,512]{3,2,1,0:T(8,128)(2,1)S(1)}, u32[]{:S(2)}, u32[]{:S(2)}) collective-permute-start(bf16[2,2,64,512]{3,2,1,0:T(8,128)(2,1)S(1)} %pad_maximum_fusion.1), channel_id=1, source_target_pairs={{0,2},{1,5},{2,0},{3,7},{4,6},{5,1},{6,4},{7,3},{8,10},{9,13},{10,... | collective-permute-start | bytes 786440 | tf_op jit(solution)/shard_map/ppermute | solution.py:239
  72.1 6.4 %collective-permute-start.8 = (bf16[2,2,64,512]{3,2,1,0:T(8,128)(2,1)S(1)}, bf16[2,2,64,512]{3,2,1,0:T(8,128)(2,1)S(1)}, u32[]{:S(2)}, u32[]{:S(2)}) collective-permute-start(bf16[2,2,64,512]{3,2,1,0:T(8,128)(2,1)S(1)} %pad_maximum_fusion), channel_id=1, source_target_pairs={{0,2},{1,5},{2,0},{3,7},{4,6},{5,1},{6,4},{7,3},{8,10},{9,13},{10,... | collective-permute-start | bytes 786440 | tf_op jit(solution)/shard_map/ppermute | solution.py:239
  73.9 6.4 %collective-permute-start.19 = (bf16[2,2,64,512]{3,2,1,0:T(8,128)(2,1)S(1)}, bf16[2,2,64,512]{3,2,1,0:T(8,128)(2,1)S(1)}, u32[]{:S(2)}, u32[]{:S(2)}) collective-permute-start(bf16[2,2,64,512]{3,2,1,0:T(8,128)(2,1)S(1)} %collective-permute-done.16.refs_2_), channel_id=1, source_target_pairs={{0,1},{1,0},{2,3},{3,2},{4,5},{5,4},{6,7},{7,6},{8,9},{9,8},{10,11... | collective-permute-start | bytes 786440 | tf_op jit(solution)/shard_map/ppermute | solution.py:228
  73.9 5.2 %collective-permute-start.17 = (bf16[1,2,64,512]{3,2,1,0:T(8,128)(2,1)S(1)}, bf16[1,2,64,512]{3,2,1,0:T(8,128)(2,1)S(1)}, u32[]{:S(2)}, u32[]{:S(2)}) collective-permute-start(bf16[1,2,64,512]{3,2,1,0:T(8,128)(2,1)S(1)} %add_convert_fusion.4.refs_0_), channel_id=1, source_target_pairs={{0,1},{1,0},{2,3},{3,2},{4,5},{5,4},{6,7},{7,6},{8,9},{9,8},{10,11... | collective-permute-start | bytes 393224 | tf_op jit(solution)/shard_map/ppermute | solution.py:228
  78.6 3.7 %collective-permute-start.11 = (bf16[2,2,64,512]{3,2,1,0:T(8,128)(2,1)S(1)}, bf16[2,2,64,512]{3,2,1,0:T(8,128)(2,1)S(1)}, u32[]{:S(2)}, u32[]{:S(2)}) collective-permute-start(bf16[2,2,64,512]{3,2,1,0:T(8,128)(2,1)S(1)} %collective-permute-done.8.refs_2_), channel_id=1, source_target_pairs={{0,1},{1,0},{2,3},{3,2},{4,5},{5,4},{6,7},{7,6},{8,9},{9,8},{10,11... | collective-permute-start | bytes 786440 | tf_op jit(solution)/shard_map/ppermute | solution.py:228
  78.6 1.7 %collective-permute-start.18 = (bf16[1,2,64,512]{3,2,1,0:T(8,128)(2,1)S(1)}, bf16[1,2,64,512]{3,2,1,0:T(8,128)(2,1)S(1)}, u32[]{:S(2)}, u32[]{:S(2)}) collective-permute-start(bf16[1,2,64,512]{3,2,1,0:T(8,128)(2,1)S(1)} %collective-permute-done.15.refs_1_), channel_id=1, source_target_pairs={{0,1},{1,0},{2,3},{3,2},{4,5},{5,4},{6,7},{7,6},{8,9},{9,8},{10,11... | collective-permute-start | bytes 393224 | tf_op jit(solution)/shard_map/ppermute | solution.py:228
  79.1 3.2 %collective-permute-start.9 = (bf16[1,2,64,512]{3,2,1,0:T(8,128)(2,1)S(1)}, bf16[1,2,64,512]{3,2,1,0:T(8,128)(2,1)S(1)}, u32[]{:S(2)}, u32[]{:S(2)}) collective-permute-start(bf16[1,2,64,512]{3,2,1,0:T(8,128)(2,1)S(1)} %add_convert_fusion.6.refs_0_), channel_id=1, source_target_pairs={{0,1},{1,0},{2,3},{3,2},{4,5},{5,4},{6,7},{7,6},{8,9},{9,8},{10,11... | collective-permute-start | bytes 393224 | tf_op jit(solution)/shard_map/ppermute | solution.py:228
  79.1 3.2 %collective-permute-start.10 = (bf16[1,2,64,512]{3,2,1,0:T(8,128)(2,1)S(1)}, bf16[1,2,64,512]{3,2,1,0:T(8,128)(2,1)S(1)}, u32[]{:S(2)}, u32[]{:S(2)}) collective-permute-start(bf16[1,2,64,512]{3,2,1,0:T(8,128)(2,1)S(1)} %collective-permute-done.7.refs_1_), channel_id=1, source_target_pairs={{0,1},{1,0},{2,3},{3,2},{4,5},{5,4},{6,7},{7,6},{8,9},{9,8},{10,11... | collective-permute-start | bytes 393224 | tf_op jit(solution)/shard_map/ppermute | solution.py:228
  (8 other events, 31.8 us)

commit v4 on v3

--- a/solution.py
+++ b/solution.py
@@ -221,7 +221,8 @@
 def role_steps():
     lat = [("lat", 2 << k) for k in range(lax.axis_size("lat").bit_length() - 2)]
     lon = [("lon", 1 << k) for k in range(lax.axis_size("lon").bit_length() - 1)]
-    return (lat + lon, lon + lat)
+    rest = lat[1:] + lon[1:]
+    return ([lat[0], lon[0]] + rest, [lon[0], lat[0]] + rest)
 
 
 def core_swapped(value):
@@ -258,14 +259,20 @@
     return added(grads[:4], core_swapped(grads[4:]))
 
 
+def halved(kept):
+    return added(kept[:2], swapped(kept[2:], 0))
+
+
 def all_summed(kept):
-    kept = added(kept[:2], swapped(kept[2:], 0))
     mine = added(kept[:1], swapped(kept[1:], 1))
     for step in range(2, len(role_steps()[0])):
         mine = added(mine, swapped(mine, step))
     second = swapped(mine, 1)
-    first = swapped(jnp.concatenate([mine, second]), 0)
-    return mine, second, first, core_swapped(mine), core_swapped(second), core_swapped(first)
+    return mine, second, swapped(jnp.concatenate([mine, second]), 0)
+
+
+def from_both_cores(chunks):
+    return (*chunks, *(core_swapped(chunk) for chunk in chunks))
 
 
 def on_device(grid_in, mesh_lat, edge_w, edge_src, edge_dst, block_count, embed_w, message_w, up_w, out_w, gain, cot):
@@ -292,7 +299,7 @@
         )
 
     to_west, to_east = call(
-        pack_kernel, "pack", [HBM], [shape((features, side), BF)] * 2, 0, 3 * MIB, 20,
+        pack_kernel, "pack", [HBM], [shape((features, side), BF)] * 2, 0, 3 * MIB, 60,
         [
             pltpu.VMEM((features, rows, cols), BF),
             pltpu.VMEM((cols // block, features * rows, block), F32),
@@ -350,17 +357,19 @@
         2_400_000_000, 9 * MIB, 16, [pltpu.VMEM((2, latent, latent), F32)],
     )(perm, back, weights_all, slope_own, slope_west, slope_east, x_own, x_west, x_east, gain_term, grad_out_term)
 
+    kept_a, grads_b = lax.optimization_barrier((halved(kept_a), grads_b))
     summed_a = all_summed(kept_a)
-    summed_b = all_summed(core_summed(grads_b))
+    summed_b = all_summed(halved(core_summed(grads_b)))
     square = shape((latent, latent), F32)
     grad_message, grad_up = call(
         order_mesh_kernel, "order_a", [SMEM] + [VMEM] * 6, [square, square], 0, 3 * MIB, 16
-    )(perm, *summed_a)
+    )(perm, *from_both_cores(summed_a))
+    last, grad_message, grad_up = lax.optimization_barrier((summed_b[2], grad_message, grad_up))
     grad_out, grad_embed, grad_gain = call(
         order_grid_kernel, "order_b", [SMEM] + [VMEM] * 6,
         [square, shape((features, latent), F32), shape((1, latent), F32)], 0, 3 * MIB, 16,
         [pltpu.VMEM((latent, latent), F32)],
-    )(perm, *summed_b)
+    )(perm, *from_both_cores((*summed_b[:2], last)))
     return (mesh_new, mesh_grad, grad_embed, grad_message, grad_up, grad_out, grad_gain[0])
 
 

time: 84.6 us -> 81.5 us (0.963)
  starting transfers between devices: 23.8 us -> 19.2 us
  Pallas kernels: 21.6 us -> 23.2 us
  local copies, waits for them, and re-layouts: 6.04 us -> 4.5 us
  waiting for transfers between devices: 30.7 us -> 32.1 us
    ppermute x10, starting transfers between devices: 16.8 us -> 12.9 us  [swapped(): return lax.ppermute(value, ('lon', 'lat'), pairs)]
    ppermute x8, waiting for transfers between devices: 1.68 us -> 3.87 us  [core_swapped(): lax.ppermute(value, 'lat', [(i, i ^ 1) for i in range(lax.axis_size('lat'...]
    unnamed x24 -> x22, local copies, waits for them, and re-layouts: 5.82 us -> 4.28 us
    pallas_call x1, Pallas kernels: 2 us -> 3.08 us  [on_device(): call(pack_kernel, 'pack', [HBM], [shape((features, side), BF)] * 2, 0, 3...]
  transfers between devices with their start and end apart: 20 -> 20, of which waited for: 13 -> 17; matrix products, arithmetic and copies ran while one was open for 1% -> 1% of each run, Pallas kernels for 13% -> 18%
where the time goes in v4:
time: 81.5 us; the launch traced here: 81.2 us
  waiting for transfers between devices  32.1 us (39%)
  Pallas kernels  23.2 us (28%)
  starting transfers between devices  19.2 us (24%)
  local copies, waits for them, and re-layouts  4.5 us (6%)
  between operations  1.55 us (2%)
    ppermute x10, waiting for transfers between devices, swapped(): return lax.ppermute(value, ('lon', 'lat'), pairs)  20.4 us
    ppermute x10, starting transfers between devices, swapped(): return lax.ppermute(value, ('lon', 'lat'), pairs)  12.9 us
    ppermute x1, waiting for transfers between devices, on_device(): lax.ppermute(to_west, 'lon', [((i + 1) % count, i) for i in range(count)])  7.86 us
    pallas_call x1, Pallas kernels, on_device(): call(own_kernel, 'own_points', [SMEM] * 3 + [VMEM] * 5, [shape((nodes, po...  7.53 us
    unnamed x22, local copies, waits for them, and re-layouts  4.28 us
    ppermute x8, waiting for transfers between devices, core_swapped(): lax.ppermute(value, 'lat', [(i, i ^ 1) for i in range(lax.axis_size('lat'...  3.87 us
    pallas_call x1, Pallas kernels, on_device(): call(grid_kernel, 'grid_points', [SMEM] + [VMEM] * 10, [shape((8, 2, late...  3.5 us
    pallas_call x1, Pallas kernels, on_device(): call(mesh_kernel, 'mesh_nodes', [SMEM] + [VMEM] * 10, [shape((8, 2, laten...  3.09 us
  transfers between devices with their start and end apart: 20, of which 17 were waited for; matrix products, arithmetic and copies ran while one was open for 1% of the time, Pallas kernels for 18%

profile of v4, /device:TPU:0, one launch (start us, length us, event | category | flops | bytes accessed | tf_op | source)
XLA Modules:
  0.0 81.2 jit_solution(18137115346319511965)
XLA Ops:
  0.7 3.1 %pack.1 = (bf16[474,512]{1,0:T(8,128)(2,1)}, bf16[474,512]{1,0:T(8,128)(2,1)}) custom-call(bf16[474,8,256]{2,1,0:T(8,128)(2,1)} %bitcast.11), custom_call_target="tpu_custom_call" | custom-call | bytes 3145728 | tf_op jit(solution)/shard_map/pack/pallas_call | solution.py:301
  3.7 3.1 %collective-permute-start.1 = (bf16[474,512]{1,0:T(8,128)(2,1)}, bf16[474,512]{1,0:T(8,128)(2,1)S(1)}, u32[]{:S(2)}, u32[]{:S(2)}) collective-permute-start(bf16[474,512]{1,0:T(8,128)(2,1)} %get-tuple-element.41), channel_id=1, source_target_pairs={{0,4},{4,8},{8,12},{12,0},{1,5},{5,9},{9,13},{13,1},{2,6},{6,10},{... | collective-permute-start | bytes 1456136 | tf_op jit(solution)/shard_map/ppermute | solution.py:310
  6.8 2.1 %collective-permute-start = (bf16[474,512]{1,0:T(8,128)(2,1)}, bf16[474,512]{1,0:T(8,128)(2,1)S(1)}, u32[]{:S(2)}, u32[]{:S(2)}) collective-permute-start(bf16[474,512]{1,0:T(8,128)(2,1)} %get-tuple-element.38), channel_id=1, source_target_pairs={{4,0},{8,4},{12,8},{0,12},{5,1},{9,5},{13,9},{1,13},{6,2},{10,6},{... | collective-permute-start | bytes 1456136 | tf_op jit(solution)/shard_map/ppermute | solution.py:311
  11.7 1.2 %copy-done.5 = bf16[32,128,128]{2,1,0:T(8,128)(2,1)S(1)} copy-done((bf16[32,128,128]{2,1,0:T(8,128)(2,1)S(1)}, bf16[32,128,128]{2,1,0:T(8,128)(2,1)}, u32[]{:S(2)}) %copy-start.5) | copy-done | bytes 1048600
  13.9 7.5 %own_points.1 = (bf16[256,3072]{1,0:T(8,128)(2,1)S(1)}, bf16[474,2048]{1,0:T(8,128)(2,1)S(1)}, bf16[512,474]{1,0:T(8,128)(2,1)S(1)}, f32[256,512]{1,0:T(8,128)S(...) custom-call(s32[32]{0:T(128)S(1)} %copy-done.9, s32[32]{0:T(128)S(1)} %copy-done.10, s32[1]{0:T(128)S(6)} %copy.19.count, ...), custom_call_target="tpu_custom_call" | custom-call | flops 4000000000 | bytes 12582912 | tf_op jit(solution)/shard_map/own_points/pallas_call | solution.py:313
  22.4 7.9 %collective-permute-done.x.x_east = bf16[474,512]{1,0:T(8,128)(2,1)S(1)} collective-permute-done((bf16[474,512]{1,0:T(8,128)(2,1)}, bf16[474,512]{1,0:T(8,128)(2,1)S(1)}, u32[]{:S(2)}, u32[]{:S(2)}) %collective-permute-start) | collective-permute-done | bytes 485408 | tf_op jit(solution)/shard_map/ppermute | solution.py:311
  30.3 3.1 %mesh_nodes.1 = (bf16[8,2,64,512]{3,2,1,0:T(8,128)(2,1)S(1)}, f32[256,512]{1,0:T(8,128)}, f32[1,512]{1,0:T(1,128)S(1)}, bf16[256,512]{1,0:T(8,128)(2,1)S(1)}, bf...) custom-call(s32[8]{0:T(128)S(1)} %stack.35.perm, bf16[474,512]{1,0:T(8,128)(2,1)S(1)} %collective-permute-done.x.x_east, ...), custom_call_target="tpu_custom_call" | custom-call | flops 2000000000 | bytes 8388608 | tf_op jit(solution)/shard_map/mesh_nodes/pallas_call | solution.py:334
  35.6 1.6 %collective-permute-start.3 = (bf16[2,2,64,512]{3,2,1,0:T(8,128)(2,1)S(1)}, bf16[2,2,64,512]{3,2,1,0:T(8,128)(2,1)S(1)}, u32[]{:S(2)}, u32[]{:S(2)}) collective-permute-start(bf16[2,2,64,512]{3,2,1,0:T(8,128)(2,1)S(1)} %slice.39), channel_id=1, source_target_pairs={{0,2},{1,5},{2,0},{3,7},{4,6},{5,1},{6,4},{7,3},{8,10},{9,13},{10,... | collective-permute-start | bytes 786440 | tf_op jit(solution)/shard_map/ppermute | solution.py:240
  37.1 3.5 %grid_points.1 = bf16[8,2,64,512]{3,2,1,0:T(8,128)(2,1)S(1)} custom-call(s32[8]{0:T(128)S(1)} %stack.35.perm, bf16[512,256]{1,0:T(8,128)(2,1)S(1)} %get-tuple-element.52.back, bf16[256,3072]{1,0:T(8,128)(2,1)S(1)} %get-tuple-element.40.refs_2_.weights_all, bf16[512,2048]{1,0:T(8,128)(2,1)S(1)} %get-tuple-element.53.slope_own, ...), custom_call_target="tpu_custom_call" | custom-call | flops 2400000000 | bytes 9437184 | tf_op jit(solution)/shard_map/grid_points/pallas_call | solution.py:355
  40.6 1.4 %collective-permute-done.3 = bf16[2,2,64,512]{3,2,1,0:T(8,128)(2,1)S(1)} collective-permute-done((bf16[2,2,64,512]{3,2,1,0:T(8,128)(2,1)S(1)}, bf16[2,2,64,512]{3,2,1,0:T(8,128)(2,1)S(1)}, u32[]{:S(2)}, u32[]{:S(2)}) %collective-permute-start.3) | collective-permute-done | bytes 262176 | tf_op jit(solution)/shard_map/ppermute | solution.py:240
  44.3 1.6 %collective-permute-start.5 = (bf16[2,2,64,512]{3,2,1,0:T(8,128)(2,1)S(1)}, bf16[2,2,64,512]{3,2,1,0:T(8,128)(2,1)S(1)}, u32[]{:S(2)}, u32[]{:S(2)}) collective-permute-start(bf16[2,2,64,512]{3,2,1,0:T(8,128)(2,1)S(1)} %slice.49), channel_id=1, source_target_pairs={{0,2},{1,5},{2,0},{3,7},{4,6},{5,1},{6,4},{7,3},{8,10},{9,13},{10,... | collective-permute-start | bytes 786440 | tf_op jit(solution)/shard_map/ppermute | solution.py:240
  45.8 1.6 %collective-permute-done.10 = bf16[1,2,64,512]{3,2,1,0:T(8,128)(2,1)S(1)} collective-permute-done((bf16[1,2,64,512]{3,2,1,0:T(8,128)(2,1)S(1)}, bf16[1,2,64,512]{3,2,1,0:T(8,128)(2,1)S(1)}, u32[]{:S(2)}, u32[]{:S(2)}) %collective-permute-start.10) | collective-permute-done | bytes 131104 | tf_op jit(solution)/shard_map/ppermute | solution.py:240
  47.4 2.3 %collective-permute-start.11 = (bf16[1,2,64,512]{3,2,1,0:T(8,128)(2,1)S(1)}, bf16[1,2,64,512]{3,2,1,0:T(8,128)(2,1)S(1)}, u32[]{:S(2)}, u32[]{:S(2)}) collective-permute-start(bf16[1,2,64,512]{3,2,1,0:T(8,128)(2,1)S(1)} %add_convert_fusion.5), channel_id=1, source_target_pairs={{0,8},{1,9},{2,10},{3,11},{4,12},{5,13},{6,14},{7,15},{8,0},{9,1},... | collective-permute-start | bytes 393224 | tf_op jit(solution)/shard_map/ppermute | solution.py:240
  50.8 1.2 %collective-permute-start.6 = (bf16[1,2,64,512]{3,2,1,0:T(8,128)(2,1)S(1)}, bf16[1,2,64,512]{3,2,1,0:T(8,128)(2,1)S(1)}, u32[]{:S(2)}, u32[]{:S(2)}) collective-permute-start(bf16[1,2,64,512]{3,2,1,0:T(8,128)(2,1)S(1)} %slice.51), channel_id=1, source_target_pairs={{0,4},{1,3},{2,6},{3,1},{4,0},{5,7},{6,2},{7,5},{8,12},{9,11},{10,... | collective-permute-start | bytes 393224 | tf_op jit(solution)/shard_map/ppermute | solution.py:240
  52.0 4.2 %collective-permute-done.11 = bf16[1,2,64,512]{3,2,1,0:T(8,128)(2,1)S(1)} collective-permute-done((bf16[1,2,64,512]{3,2,1,0:T(8,128)(2,1)S(1)}, bf16[1,2,64,512]{3,2,1,0:T(8,128)(2,1)S(1)}, u32[]{:S(2)}, u32[]{:S(2)}) %collective-permute-start.11) | collective-permute-done | bytes 131104 | tf_op jit(solution)/shard_map/ppermute | solution.py:240
  57.4 2.7 %collective-permute-start.7 = (bf16[1,2,64,512]{3,2,1,0:T(8,128)(2,1)S(1)}, bf16[1,2,64,512]{3,2,1,0:T(8,128)(2,1)S(1)}, u32[]{:S(2)}, u32[]{:S(2)}) collective-permute-start(bf16[1,2,64,512]{3,2,1,0:T(8,128)(2,1)S(1)} %add_convert_fusion.7), channel_id=1, source_target_pairs={{0,8},{1,9},{2,10},{3,11},{4,12},{5,13},{6,14},{7,15},{8,0},{9,1},... | collective-permute-start | bytes 393224 | tf_op jit(solution)/shard_map/ppermute | solution.py:240
  60.1 4.0 %collective-permute-done.12.refs_1_ = bf16[1,2,64,512]{3,2,1,0:T(8,128)(2,1)S(1)} collective-permute-done((bf16[1,2,64,512]{3,2,1,0:T(8,128)(2,1)S(1)}, bf16[1,2,64,512]{3,2,1,0:T(8,128)(2,1)S(1)}, u32[]{:S(2)}, u32[]{:S(2)}) %collective-permute-start.12) | collective-permute-done | bytes 131104 | tf_op jit(solution)/shard_map/ppermute | solution.py:240
  64.1 1.6 %collective-permute-done.7 = bf16[1,2,64,512]{3,2,1,0:T(8,128)(2,1)S(1)} collective-permute-done((bf16[1,2,64,512]{3,2,1,0:T(8,128)(2,1)S(1)}, bf16[1,2,64,512]{3,2,1,0:T(8,128)(2,1)S(1)}, u32[]{:S(2)}, u32[]{:S(2)}) %collective-permute-start.7) | collective-permute-done | bytes 131104 | tf_op jit(solution)/shard_map/ppermute | solution.py:240
  66.6 3.9 %collective-permute-done.13.refs_2_ = bf16[2,2,64,512]{3,2,1,0:T(8,128)(2,1)S(1)} collective-permute-done((bf16[2,2,64,512]{3,2,1,0:T(8,128)(2,1)S(1)}, bf16[2,2,64,512]{3,2,1,0:T(8,128)(2,1)S(1)}, u32[]{:S(2)}, u32[]{:S(2)}) %collective-permute-start.13) | collective-permute-done | bytes 262176 | tf_op jit(solution)/shard_map/ppermute | solution.py:240
  70.8 1.2 %collective-permute-start.9 = (bf16[2,2,64,512]{3,2,1,0:T(8,128)(2,1)S(1)}, bf16[2,2,64,512]{3,2,1,0:T(8,128)(2,1)S(1)}, u32[]{:S(2)}, u32[]{:S(2)}) collective-permute-start(bf16[2,2,64,512]{3,2,1,0:T(8,128)(2,1)S(1)} %pad_maximum_fusion), channel_id=1, source_target_pairs={{0,2},{1,5},{2,0},{3,7},{4,6},{5,1},{6,4},{7,3},{8,10},{9,13},{10,... | collective-permute-start | bytes 786440 | tf_op jit(solution)/shard_map/ppermute | solution.py:240
  73.6 2.0 %order_a.1 = (f32[512,512]{1,0:T(8,128)}, f32[512,512]{1,0:T(8,128)}) custom-call(s32[8]{0:T(128)S(1)} %stack.35.perm, bf16[1,2,64,512]{3,2,1,0:T(8,128)(2,1)S(1)} %add_convert_fusion.4.refs_0_, bf16[1,2,64,512]{3,2,1,0:T(8,128)(2,1)S(1)} %collective-permute-done.12.refs_1_, bf16[2,2,64,512]{3,2,1,0:T(8,128)(2,1)S(1)} %collective-permute-done.13.refs_2_, ...), custom_call_target="tpu_custom_call" | custom-call | bytes 3145728 | tf_op jit(solution)/shard_map/order_a/pallas_call | solution.py:364
  75.6 1.7 %collective-permute-done.9.refs_2_ = bf16[2,2,64,512]{3,2,1,0:T(8,128)(2,1)S(1)} collective-permute-done((bf16[2,2,64,512]{3,2,1,0:T(8,128)(2,1)S(1)}, bf16[2,2,64,512]{3,2,1,0:T(8,128)(2,1)S(1)}, u32[]{:S(2)}, u32[]{:S(2)}) %collective-permute-start.9) | collective-permute-done | bytes 262176 | tf_op jit(solution)/shard_map/ppermute | solution.py:240
  77.8 1.2 %collective-permute-done.17.refs_3_ = bf16[1,2,64,512]{3,2,1,0:T(8,128)(2,1)S(1)} collective-permute-done((bf16[1,2,64,512]{3,2,1,0:T(8,128)(2,1)S(1)}, bf16[1,2,64,512]{3,2,1,0:T(8,128)(2,1)S(1)}, u32[]{:S(2)}, u32[]{:S(2)}) %collective-permute-start.17) | collective-permute-done | bytes 131104 | tf_op jit(solution)/shard_map/ppermute | solution.py:229
  79.2 2.0 %order_b.1 = (f32[512,512]{1,0:T(8,128)}, f32[474,512]{1,0:T(8,128)}, f32[1,512]{1,0:T(1,128)}) custom-call(s32[8]{0:T(128)S(1)} %stack.35.perm, bf16[1,2,64,512]{3,2,1,0:T(8,128)(2,1)S(1)} %add_convert_fusion.6.refs_0_, bf16[1,2,64,512]{3,2,1,0:T(8,128)(2,1)S(1)} %collective-permute-done.8.refs_1_, ...), custom_call_target="tpu_custom_call" | custom-call | bytes 3145728 | tf_op jit(solution)/shard_map/order_b/pallas_call | solution.py:368
  (63 shorter events, 14.2 us)
Async XLA Ops:
  0.6 9.0 %copy-start = (bf16[8,256,474]{1,0,2:T(8,128)(2,1)S(1)}, bf16[8,256,474]{1,0,2:T(8,128)(2,1)}, u32[]{:S(2)}) copy-start(bf16[8,256,474]{1,0,2:T(8,128)(2,1)} %param.12) | copy-start | bytes 5824516
  0.6 9.0 %copy-start.9 = (s32[32]{0:T(128)S(1)}, s32[32]{0:T(128)}, u32[]{:S(2)}) copy-start(s32[32]{0:T(128)} %src.1) | copy-start | bytes 388
  0.7 9.0 %copy-start.10 = (s32[32]{0:T(128)S(1)}, s32[32]{0:T(128)}, u32[]{:S(2)}) copy-start(s32[32]{0:T(128)} %dst.1) | copy-start | bytes 388
  3.7 17.8 %collective-permute-start.1 = (bf16[474,512]{1,0:T(8,128)(2,1)}, bf16[474,512]{1,0:T(8,128)(2,1)S(1)}, u32[]{:S(2)}, u32[]{:S(2)}) collective-permute-start(bf16[474,512]{1,0:T(8,128)(2,1)} %get-tuple-element.41), channel_id=1, source_target_pairs={{0,4},{4,8},{8,12},{12,0},{1,5},{5,9},{9,13},{13,1},{2,6},{6,10},{... | collective-permute-start | bytes 1456136 | tf_op jit(solution)/shard_map/ppermute | solution.py:310
  6.8 23.4 %collective-permute-start = (bf16[474,512]{1,0:T(8,128)(2,1)}, bf16[474,512]{1,0:T(8,128)(2,1)S(1)}, u32[]{:S(2)}, u32[]{:S(2)}) collective-permute-start(bf16[474,512]{1,0:T(8,128)(2,1)} %get-tuple-element.38), channel_id=1, source_target_pairs={{4,0},{8,4},{12,8},{0,12},{5,1},{9,5},{13,9},{1,13},{6,2},{10,6},{... | collective-permute-start | bytes 1456136 | tf_op jit(solution)/shard_map/ppermute | solution.py:311
  21.5 8.8 %copy-start.2 = (bf16[512,512]{1,0:T(8,128)(2,1)S(1)}, bf16[512,512]{1,0:T(8,128)(2,1)}, u32[]{:S(2)}) copy-start(bf16[512,512]{1,0:T(8,128)(2,1)} %message_w.3) | copy-start | bytes 1572868
  33.4 2.0 %collective-permute-start.2 = (bf16[4,2,64,512]{3,2,1,0:T(8,128)(2,1)S(1)}, bf16[4,2,64,512]{3,2,1,0:T(8,128)(2,1)S(1)}, u32[]{:S(2)}, u32[]{:S(2)}) collective-permute-start(bf16[4,2,64,512]{3,2,1,0:T(8,128)(2,1)S(1)} %slice.37), channel_id=1, source_target_pairs={{0,1},{1,0},{2,3},{3,2},{4,5},{5,4},{6,7},{7,6},{8,9},{9,8},{10,11... | collective-permute-start | bytes 1572872 | tf_op jit(solution)/shard_map/ppermute | solution.py:229
  35.6 6.4 %collective-permute-start.3 = (bf16[2,2,64,512]{3,2,1,0:T(8,128)(2,1)S(1)}, bf16[2,2,64,512]{3,2,1,0:T(8,128)(2,1)S(1)}, u32[]{:S(2)}, u32[]{:S(2)}) collective-permute-start(bf16[2,2,64,512]{3,2,1,0:T(8,128)(2,1)S(1)} %slice.39), channel_id=1, source_target_pairs={{0,2},{1,5},{2,0},{3,7},{4,6},{5,1},{6,4},{7,3},{8,10},{9,13},{10,... | collective-permute-start | bytes 786440 | tf_op jit(solution)/shard_map/ppermute | solution.py:240
  42.1 2.0 %collective-permute-start.4 = (bf16[4,2,64,512]{3,2,1,0:T(8,128)(2,1)S(1)}, bf16[4,2,64,512]{3,2,1,0:T(8,128)(2,1)S(1)}, u32[]{:S(2)}, u32[]{:S(2)}) collective-permute-start(bf16[4,2,64,512]{3,2,1,0:T(8,128)(2,1)S(1)} %slice.41), channel_id=1, source_target_pairs={{0,1},{1,0},{2,3},{3,2},{4,5},{5,4},{6,7},{7,6},{8,9},{9,8},{10,11... | collective-permute-start | bytes 1572872 | tf_op jit(solution)/shard_map/ppermute | solution.py:229
  42.2 5.2 %collective-permute-start.10 = (bf16[1,2,64,512]{3,2,1,0:T(8,128)(2,1)S(1)}, bf16[1,2,64,512]{3,2,1,0:T(8,128)(2,1)S(1)}, u32[]{:S(2)}, u32[]{:S(2)}) collective-permute-start(bf16[1,2,64,512]{3,2,1,0:T(8,128)(2,1)S(1)} %slice.47), channel_id=1, source_target_pairs={{0,4},{1,3},{2,6},{3,1},{4,0},{5,7},{6,2},{7,5},{8,12},{9,11},{10,... | collective-permute-start | bytes 393224 | tf_op jit(solution)/shard_map/ppermute | solution.py:240
  44.3 6.4 %collective-permute-start.5 = (bf16[2,2,64,512]{3,2,1,0:T(8,128)(2,1)S(1)}, bf16[2,2,64,512]{3,2,1,0:T(8,128)(2,1)S(1)}, u32[]{:S(2)}, u32[]{:S(2)}) collective-permute-start(bf16[2,2,64,512]{3,2,1,0:T(8,128)(2,1)S(1)} %slice.49), channel_id=1, source_target_pairs={{0,2},{1,5},{2,0},{3,7},{4,6},{5,1},{6,4},{7,3},{8,10},{9,13},{10,... | collective-permute-start | bytes 786440 | tf_op jit(solution)/shard_map/ppermute | solution.py:240
  47.4 8.8 %collective-permute-start.11 = (bf16[1,2,64,512]{3,2,1,0:T(8,128)(2,1)S(1)}, bf16[1,2,64,512]{3,2,1,0:T(8,128)(2,1)S(1)}, u32[]{:S(2)}, u32[]{:S(2)}) collective-permute-start(bf16[1,2,64,512]{3,2,1,0:T(8,128)(2,1)S(1)} %add_convert_fusion.5), channel_id=1, source_target_pairs={{0,8},{1,9},{2,10},{3,11},{4,12},{5,13},{6,14},{7,15},{8,0},{9,1},... | collective-permute-start | bytes 393224 | tf_op jit(solution)/shard_map/ppermute | solution.py:240
  50.8 6.5 %collective-permute-start.6 = (bf16[1,2,64,512]{3,2,1,0:T(8,128)(2,1)S(1)}, bf16[1,2,64,512]{3,2,1,0:T(8,128)(2,1)S(1)}, u32[]{:S(2)}, u32[]{:S(2)}) collective-permute-start(bf16[1,2,64,512]{3,2,1,0:T(8,128)(2,1)S(1)} %slice.51), channel_id=1, source_target_pairs={{0,4},{1,3},{2,6},{3,1},{4,0},{5,7},{6,2},{7,5},{8,12},{9,11},{10,... | collective-permute-start | bytes 393224 | tf_op jit(solution)/shard_map/ppermute | solution.py:240
  56.2 7.8 %collective-permute-start.12 = (bf16[1,2,64,512]{3,2,1,0:T(8,128)(2,1)S(1)}, bf16[1,2,64,512]{3,2,1,0:T(8,128)(2,1)S(1)}, u32[]{:S(2)}, u32[]{:S(2)}) collective-permute-start(bf16[1,2,64,512]{3,2,1,0:T(8,128)(2,1)S(1)} %add_convert_fusion.4.refs_0_), channel_id=1, source_target_pairs={{0,4},{1,3},{2,6},{3,1},{4,0},{5,7},{6,2},{7,5},{8,12},{9,11},{10,... | collective-permute-start | bytes 393224 | tf_op jit(solution)/shard_map/ppermute | solution.py:240
  57.4 8.4 %collective-permute-start.7 = (bf16[1,2,64,512]{3,2,1,0:T(8,128)(2,1)S(1)}, bf16[1,2,64,512]{3,2,1,0:T(8,128)(2,1)S(1)}, u32[]{:S(2)}, u32[]{:S(2)}) collective-permute-start(bf16[1,2,64,512]{3,2,1,0:T(8,128)(2,1)S(1)} %add_convert_fusion.7), channel_id=1, source_target_pairs={{0,8},{1,9},{2,10},{3,11},{4,12},{5,13},{6,14},{7,15},{8,0},{9,1},... | collective-permute-start | bytes 393224 | tf_op jit(solution)/shard_map/ppermute | solution.py:240
  64.1 6.4 %collective-permute-start.13 = (bf16[2,2,64,512]{3,2,1,0:T(8,128)(2,1)S(1)}, bf16[2,2,64,512]{3,2,1,0:T(8,128)(2,1)S(1)}, u32[]{:S(2)}, u32[]{:S(2)}) collective-permute-start(bf16[2,2,64,512]{3,2,1,0:T(8,128)(2,1)S(1)} %pad_maximum_fusion.1), channel_id=1, source_target_pairs={{0,2},{1,5},{2,0},{3,7},{4,6},{5,1},{6,4},{7,3},{8,10},{9,13},{10,... | collective-permute-start | bytes 786440 | tf_op jit(solution)/shard_map/ppermute | solution.py:240
  65.8 5.0 %collective-permute-start.8 = (bf16[1,2,64,512]{3,2,1,0:T(8,128)(2,1)S(1)}, bf16[1,2,64,512]{3,2,1,0:T(8,128)(2,1)S(1)}, u32[]{:S(2)}, u32[]{:S(2)}) collective-permute-start(bf16[1,2,64,512]{3,2,1,0:T(8,128)(2,1)S(1)} %add_convert_fusion.6.refs_0_), channel_id=1, source_target_pairs={{0,4},{1,3},{2,6},{3,1},{4,0},{5,7},{6,2},{7,5},{8,12},{9,11},{10,... | collective-permute-start | bytes 393224 | tf_op jit(solution)/shard_map/ppermute | solution.py:240
  70.5 3.1 %collective-permute-start.16 = (bf16[2,2,64,512]{3,2,1,0:T(8,128)(2,1)S(1)}, bf16[2,2,64,512]{3,2,1,0:T(8,128)(2,1)S(1)}, u32[]{:S(2)}, u32[]{:S(2)}) collective-permute-start(bf16[2,2,64,512]{3,2,1,0:T(8,128)(2,1)S(1)} %collective-permute-done.13.refs_2_), channel_id=1, source_target_pairs={{0,1},{1,0},{2,3},{3,2},{4,5},{5,4},{6,7},{7,6},{8,9},{9,8},{10,11... | collective-permute-start | bytes 786440 | tf_op jit(solution)/shard_map/ppermute | solution.py:229
  70.8 6.4 %collective-permute-start.9 = (bf16[2,2,64,512]{3,2,1,0:T(8,128)(2,1)S(1)}, bf16[2,2,64,512]{3,2,1,0:T(8,128)(2,1)S(1)}, u32[]{:S(2)}, u32[]{:S(2)}) collective-permute-start(bf16[2,2,64,512]{3,2,1,0:T(8,128)(2,1)S(1)} %pad_maximum_fusion), channel_id=1, source_target_pairs={{0,2},{1,5},{2,0},{3,7},{4,6},{5,1},{6,4},{7,3},{8,10},{9,13},{10,... | collective-permute-start | bytes 786440 | tf_op jit(solution)/shard_map/ppermute | solution.py:240
  72.0 1.3 %collective-permute-start.14 = (bf16[1,2,64,512]{3,2,1,0:T(8,128)(2,1)S(1)}, bf16[1,2,64,512]{3,2,1,0:T(8,128)(2,1)S(1)}, u32[]{:S(2)}, u32[]{:S(2)}) collective-permute-start(bf16[1,2,64,512]{3,2,1,0:T(8,128)(2,1)S(1)} %add_convert_fusion.4.refs_0_), channel_id=1, source_target_pairs={{0,1},{1,0},{2,3},{3,2},{4,5},{5,4},{6,7},{7,6},{8,9},{9,8},{10,11... | collective-permute-start | bytes 393224 | tf_op jit(solution)/shard_map/ppermute | solution.py:229
  72.0 1.5 %collective-permute-start.15 = (bf16[1,2,64,512]{3,2,1,0:T(8,128)(2,1)S(1)}, bf16[1,2,64,512]{3,2,1,0:T(8,128)(2,1)S(1)}, u32[]{:S(2)}, u32[]{:S(2)}) collective-permute-start(bf16[1,2,64,512]{3,2,1,0:T(8,128)(2,1)S(1)} %collective-permute-done.12.refs_1_), channel_id=1, source_target_pairs={{0,1},{1,0},{2,3},{3,2},{4,5},{5,4},{6,7},{7,6},{8,9},{9,8},{10,11... | collective-permute-start | bytes 393224 | tf_op jit(solution)/shard_map/ppermute | solution.py:229
  77.3 1.9 %collective-permute-start.19 = (bf16[2,2,64,512]{3,2,1,0:T(8,128)(2,1)S(1)}, bf16[2,2,64,512]{3,2,1,0:T(8,128)(2,1)S(1)}, u32[]{:S(2)}, u32[]{:S(2)}) collective-permute-start(bf16[2,2,64,512]{3,2,1,0:T(8,128)(2,1)S(1)} %collective-permute-done.9.refs_2_), channel_id=1, source_target_pairs={{0,1},{1,0},{2,3},{3,2},{4,5},{5,4},{6,7},{7,6},{8,9},{9,8},{10,11... | collective-permute-start | bytes 786440 | tf_op jit(solution)/shard_map/ppermute | solution.py:229
  77.3 1.7 %collective-permute-start.17 = (bf16[1,2,64,512]{3,2,1,0:T(8,128)(2,1)S(1)}, bf16[1,2,64,512]{3,2,1,0:T(8,128)(2,1)S(1)}, u32[]{:S(2)}, u32[]{:S(2)}) collective-permute-start(bf16[1,2,64,512]{3,2,1,0:T(8,128)(2,1)S(1)} %add_convert_fusion.6.refs_0_), channel_id=1, source_target_pairs={{0,1},{1,0},{2,3},{3,2},{4,5},{5,4},{6,7},{7,6},{8,9},{9,8},{10,11... | collective-permute-start | bytes 393224 | tf_op jit(solution)/shard_map/ppermute | solution.py:229
  77.8 1.4 %collective-permute-start.18 = (bf16[1,2,64,512]{3,2,1,0:T(8,128)(2,1)S(1)}, bf16[1,2,64,512]{3,2,1,0:T(8,128)(2,1)S(1)}, u32[]{:S(2)}, u32[]{:S(2)}) collective-permute-start(bf16[1,2,64,512]{3,2,1,0:T(8,128)(2,1)S(1)} %collective-permute-done.8.refs_1_), channel_id=1, source_target_pairs={{0,1},{1,0},{2,3},{3,2},{4,5},{5,4},{6,7},{7,6},{8,9},{9,8},{10,11... | collective-permute-start | bytes 393224 | tf_op jit(solution)/shard_map/ppermute | solution.py:229
  (7 other events, 30.6 us)

commit v5 on v4

--- a/solution.py
+++ b/solution.py
@@ -25,33 +25,41 @@
     return pre * sigma, sigma * (1.0 + pre * (1.0 - sigma))
 
 
-def pack_kernel(grid, to_west, to_east, held, wide, sems):
+def pack_rows(wide, out, rows, first, size, from_high):
+    block = wide.shape[1]
+    half = block // 2
+    lane = lax.broadcasted_iota(jnp.int32, (size, block), 1)
+    for pair in range(rows // 2):
+        even = wide[pl.ds(first * rows + 2 * pair, size, stride=rows), :]
+        odd = wide[pl.ds(first * rows + 2 * pair + 1, size, stride=rows), :]
+        if from_high:
+            even = pltpu.roll(even, half, 1)
+        else:
+            odd = pltpu.roll(odd, half, 1)
+        out[pl.ds(first, size), pair * block : (pair + 1) * block] = jnp.where(lane < half, even, odd).astype(BF)
+
+
+def pack_east_kernel(grid, to_east, held, wide, sems):
     features, rows, cols = grid.shape
-    half = to_west.shape[1] // rows
-    block = 2 * half
-    last = cols // block - 1
+    block = wide.shape[1]
     pieces = []
     for n, first in enumerate(range(0, features, PIECE)):
         at = pl.ds(first, min(PIECE, features - first))
-        pieces.append((at, pltpu.make_async_copy(grid.at[at], held.at[at], sems.at[n])))
+        source = grid.at[at, :, pl.ds(cols - block, block)]
+        pieces.append((at, pltpu.make_async_copy(source, held.at[at], sems.at[n])))
     for _, copy in pieces:
         copy.start()
     for at, copy in pieces:
         copy.wait()
-        size = at.size
-        for k in (0, last):
-            wide[k, pl.ds(at.start * rows, size * rows), :] = (
-                held[at, :, k * block : (k + 1) * block].astype(F32).reshape(size * rows, block)
-            )
-        lane = lax.broadcasted_iota(jnp.int32, (size, block), 1)
-        for pair in range(rows // 2):
-            even = pl.ds(at.start * rows + 2 * pair, size, stride=rows)
-            odd = pl.ds(at.start * rows + 2 * pair + 1, size, stride=rows)
-            to = slice(pair * block, (pair + 1) * block)
-            head = jnp.where(lane < half, wide[0, even, :], pltpu.roll(wide[0, odd, :], half, 1))
-            tail = jnp.where(lane < half, pltpu.roll(wide[last, even, :], half, 1), wide[last, odd, :])
-            to_west[at, to] = head.astype(BF)
-            to_east[at, to] = tail.astype(BF)
+        wide[pl.ds(at.start * rows, at.size * rows), :] = held[at].astype(F32).reshape(at.size * rows, block)
+        pack_rows(wide, to_east, rows, at.start, at.size, True)
+
+
+def pack_west_kernel(grid, to_west, wide):
+    features, rows, _ = grid.shape
+    block = wide.shape[1]
+    wide[...] = grid[:, :, :block].astype(F32).reshape(features * rows, block)
+    pack_rows(wide, to_west, rows, 0, features, False)
 
 
 def own_kernel(
@@ -129,11 +137,11 @@
 
 
 def to_chunks(grads, stack, perm):
-    count, matrices, size, _ = grads.shape
+    count, parts, size, _ = grads.shape
     for j in range(count):
         at = pl.ds(pl.multiple_of(perm[j] * size, size), size)
-        for k in range(matrices):
-            grads[j, k] = stack[k, at, :]
+        for k in range(parts):
+            grads[j, k] = stack[k, at, :].astype(BF)
 
 
 def from_chunks(outs, chunks, perm):
@@ -141,9 +149,8 @@
     for chunk in chunks:
         for n in range(chunk.shape[0]):
             size = chunk.shape[2]
-            at = pl.ds(pl.multiple_of(perm[j] * size, size), size)
-            for k, out in enumerate(outs):
-                out[at, :] = chunk[n, k].astype(F32)
+            for k, (out, first) in enumerate(outs):
+                out[pl.ds(pl.multiple_of(first + perm[j] * size, size), size), :] = chunk[n, k].astype(F32)
             j += 1
 
 
@@ -170,15 +177,23 @@
     grad_q = rinv * (grad_qhat - qhat * jnp.mean(grad_qhat * qhat, axis=1, keepdims=True))
     grad_aggregate[...] = grad_q.astype(BF)
     mesh_grad[...] = cot[...].astype(F32) + grad_q
-    stack[0] = contract(gathered, grad_q.astype(BF), 0, 0).astype(BF)
-    stack[1] = contract(normed, grad_pre_up, 0, 0).astype(BF)
+    rows = stack.shape[1]
+    for k, grad in enumerate(
+        (
+            contract(gathered, grad_q.astype(BF), 0, 0),
+            contract(normed, grad_pre_up, 0, 0),
+            contract(update[:, :rows], cot[...], 0, 0),
+        )
+    ):
+        for n in range(grad.shape[0] // rows):
+            stack[2 * k + n] = grad[n * rows : (n + 1) * rows].astype(BF)
     to_chunks(grads, stack, perm)
 
 
 def tail_kernel(grad_aggregate, update, message_w, out_w, mesh_lat, cot, back, mesh_new, grad_out):
     back[...] = contract(message_w[...], grad_aggregate[...], 1, 1).astype(BF)
     mesh_new[...] = (mesh_lat[...].astype(F32) + contract(update[...], out_w[...], 1, 0)).astype(BF)
-    grad_out[...] = contract(update[...], cot[...], 0, 0).astype(BF)
+    grad_out[...] = contract(update[:, grad_out.shape[0] :], cot[...], 0, 0)
 
 
 def grid_kernel(
@@ -195,27 +210,37 @@
         hidden = contract(back[...], weights_all[:, n * tile : (n + 1) * tile], 1, 0)
         grad_pre = (hidden * slope[:, at].astype(F32)).astype(BF)
         sums += contract(x[:, at], grad_pre, 1, 1)
-    stack[0] = grad_out[...].astype(F32)
-    stack[1] = jnp.zeros(stack.shape[1:], F32)
-    stack[1, :features, :] = sums
-    stack[1, features : features + 1, :] = grad_gain[...]
-    count, matrices, size, _ = grads.shape
-    for j in range(count):
-        at = pl.ds(pl.multiple_of(perm[j] * size, size), size)
-        for k in range(matrices):
-            grads[j, k] = stack[k, at, :].astype(BF)
-
-
-def order_mesh_kernel(perm, *refs):
-    from_chunks(refs[-2:], refs[:-2], perm)
-
-
-def order_grid_kernel(perm, *refs):
-    grad_out, grad_embed, grad_gain, total = refs[-4:]
-    from_chunks((grad_out, total), refs[:-4], perm)
+    rows = stack.shape[1]
+    stack[0] = grad_out[...]
+    stack[1] = sums[:rows]
+    stack[2] = jnp.zeros(stack.shape[1:], F32)
+    stack[2, : features - rows, :] = sums[rows:]
+    stack[2, features - rows : features - rows + 1, :] = grad_gain[...]
+    to_chunks(grads, stack, perm)
+
+
+def order_a_kernel(perm, *refs):
+    chunks, (grad_message, grad_up, grad_out, half, sem) = refs[:6], refs[6:]
+    rows = half.shape[0]
+    from_chunks(((half, 0),), [chunk.at[:, 4:] for chunk in chunks], perm)
+    copy = pltpu.make_async_copy(half, grad_out.at[pl.ds(0, rows)], sem)
+    copy.start()
+    outs = ((grad_message, 0), (grad_message, rows), (grad_up, 0), (grad_up, rows))
+    from_chunks(outs, [chunk.at[:, :4] for chunk in chunks], perm)
+    copy.wait()
+
+
+def order_b_kernel(perm, *refs):
+    chunks, (_, grad_out, grad_embed, grad_gain, half, total, sem) = refs[:6], refs[6:]
+    rows = half.shape[0]
+    from_chunks(((half, 0),), [chunk.at[:, :1] for chunk in chunks], perm)
+    copy = pltpu.make_async_copy(half, grad_out.at[pl.ds(rows, rows)], sem)
+    copy.start()
+    from_chunks(((total, 0), (total, rows)), [chunk.at[:, 1:] for chunk in chunks], perm)
     features = grad_embed.shape[0]
     grad_embed[...] = total[:features, :]
     grad_gain[...] = total[features : features + 1, :]
+    copy.wait()
 
 
 def role_steps():
@@ -286,28 +311,29 @@
     points = own + 2 * side
     grid = jnp.transpose(grid_in, (2, 0, 1))
 
-    def call(kernel, name, in_specs, out_shape, flops, bytes_accessed, limit, scratch_shapes=()):
+    def call(kernel, name, in_specs, out_shape, flops, bytes_accessed, limit, scratch_shapes=(), out_specs=None, **more):
         return pl.pallas_call(
             kernel,
             name=name,
             in_specs=in_specs,
-            out_specs=[VMEM] * len(out_shape),
+            out_specs=out_specs or [VMEM] * len(out_shape),
             out_shape=out_shape,
             scratch_shapes=list(scratch_shapes),
             compiler_params=pltpu.CompilerParams(vmem_limit_bytes=limit * MIB),
             cost_estimate=pl.CostEstimate(flops=flops, bytes_accessed=bytes_accessed, transcendentals=0),
+            **more,
         )
 
-    to_west, to_east = call(
-        pack_kernel, "pack", [HBM], [shape((features, side), BF)] * 2, 0, 3 * MIB, 60,
-        [
-            pltpu.VMEM((features, rows, cols), BF),
-            pltpu.VMEM((cols // block, features * rows, block), F32),
-            pltpu.SemaphoreType.DMA((-(-features // PIECE),)),
-        ],
+    strip = shape((features, side), BF)
+    wide = pltpu.VMEM((features * rows, block), F32)
+    (to_east,) = call(
+        pack_east_kernel, "pack_east", [HBM], [strip], 0, MIB, 60,
+        [pltpu.VMEM((features, rows, block), BF), wide, pltpu.SemaphoreType.DMA((-(-features // PIECE),))],
     )(grid)
     count = lax.axis_size("lon")
     x_west = lax.ppermute(to_east, "lon", [(i, (i + 1) % count) for i in range(count)])
+    to_east, later = lax.optimization_barrier((to_east, grid))
+    (to_west,) = call(pack_west_kernel, "pack_west", [VMEM], [strip], 0, MIB, 20, [wide])(later)
     x_east = lax.ppermute(to_west, "lon", [((i + 1) % count, i) for i in range(count)])
 
     weights_all, x_own, embed_t, h_own, slope_own, grad_update = call(
@@ -334,18 +360,18 @@
     grads_a, mesh_grad, gain_term, grad_aggregate, update, slope_east = call(
         mesh_kernel, "mesh_nodes", [SMEM] + [VMEM] * 10,
         [
-            shape((8, 2, latent // 8, latent), BF),
+            shape((8, 5, latent // 16, latent), BF),
             shape((nodes, latent), F32),
             shape((1, latent), F32),
             shape((nodes, latent), BF),
             shape((nodes, latent), BF),
             shape((latent, side), BF),
         ],
-        2_000_000_000, 8 * MIB, 16, [pltpu.VMEM((2, latent, latent), BF)],
+        2_000_000_000, 8 * MIB, 16, [pltpu.VMEM((5, latent // 2, latent), BF)],
     )(perm, x_east, embed_t, weights_all, h_sum, message_w, up_w, gain.reshape(1, latent), mesh_lat, cot, grad_update)
     back, mesh_new, grad_out_term = call(
         tail_kernel, "mesh_tail", [VMEM] * 6,
-        [shape((latent, nodes), BF), shape((nodes, latent), BF), shape((latent, latent), BF)],
+        [shape((latent, nodes), BF), shape((nodes, latent), BF), shape((latent // 2, latent), F32)],
         400_000_000, 3 * MIB, 16,
     )(grad_aggregate, update, message_w, out_w, mesh_lat, cot)
 
@@ -353,23 +379,26 @@
     padded = -(-(features + 1) // 128) * 128
     assert padded == latent
     (grads_b,) = call(
-        grid_kernel, "grid_points", [SMEM] + [VMEM] * 10, [shape((8, 2, latent // 8, latent), BF)],
-        2_400_000_000, 9 * MIB, 16, [pltpu.VMEM((2, latent, latent), F32)],
+        grid_kernel, "grid_points", [SMEM] + [VMEM] * 10, [shape((8, 3, latent // 16, latent), BF)],
+        2_400_000_000, 9 * MIB, 16, [pltpu.VMEM((3, latent // 2, latent), F32)],
     )(perm, back, weights_all, slope_own, slope_west, slope_east, x_own, x_west, x_east, gain_term, grad_out_term)
 
     kept_a, grads_b = lax.optimization_barrier((halved(kept_a), grads_b))
     summed_a = all_summed(kept_a)
     summed_b = all_summed(halved(core_summed(grads_b)))
     square = shape((latent, latent), F32)
-    grad_message, grad_up = call(
-        order_mesh_kernel, "order_a", [SMEM] + [VMEM] * 6, [square, square], 0, 3 * MIB, 16
+    half_square = pltpu.VMEM((latent // 2, latent), F32)
+    grad_message, grad_up, grad_out = call(
+        order_a_kernel, "order_a", [SMEM] + [VMEM] * 6, [square, square, square], 0, 4 * MIB, 16,
+        [half_square, pltpu.SemaphoreType.DMA], out_specs=[VMEM, VMEM, HBM],
     )(perm, *from_both_cores(summed_a))
-    last, grad_message, grad_up = lax.optimization_barrier((summed_b[2], grad_message, grad_up))
+    last, grad_message, grad_up, grad_out = lax.optimization_barrier((summed_b[2], grad_message, grad_up, grad_out))
     grad_out, grad_embed, grad_gain = call(
-        order_grid_kernel, "order_b", [SMEM] + [VMEM] * 6,
+        order_b_kernel, "order_b", [SMEM] + [VMEM] * 6 + [HBM],
         [square, shape((features, latent), F32), shape((1, latent), F32)], 0, 3 * MIB, 16,
-        [pltpu.VMEM((latent, latent), F32)],
-    )(perm, *from_both_cores((*summed_b[:2], last)))
+        [half_square, pltpu.VMEM((latent, latent), F32), pltpu.SemaphoreType.DMA],
+        out_specs=[HBM, VMEM, VMEM], input_output_aliases={7: 0},
+    )(perm, *from_both_cores((*summed_b[:2], last)), grad_out)
     return (mesh_new, mesh_grad, grad_embed, grad_message, grad_up, grad_out, grad_gain[0])
 
 

time: 81.5 us -> 85.1 us (1.044)
  starting transfers between devices: 19.2 us -> 21.6 us
  Pallas kernels: 23.2 us -> 25.4 us
  local copies, waits for them, and re-layouts: 4.5 us -> 3.46 us
    pallas_call x5 -> x6, Pallas kernels: 13.7 us -> 15.9 us  [the longest x1 3.96 us: on_device(): call(grid_kernel, 'grid_points', [SMEM] + [VMEM] * 10, [shape((8, 3, late...]
    ppermute x10, starting transfers between devices: 12.9 us -> 14.9 us  [swapped(): return lax.ppermute(value, ('lon', 'lat'), pairs)]
    ppermute x10, waiting for transfers between devices: 20.4 us -> 19.2 us  [swapped(): return lax.ppermute(value, ('lon', 'lat'), pairs)]
    unnamed x22, local copies, waits for them, and re-layouts: 4.28 us -> 3.24 us
  transfers between devices with their start and end apart: 20 -> 20, of which waited for: 17 -> 14; matrix products, arithmetic and copies ran while one was open for 1% -> 1% of each run, Pallas kernels for 18% -> 20%
where the time goes in v5:
time: 85.1 us; the launch traced here: 84.8 us
  waiting for transfers between devices  32.2 us (38%)
  Pallas kernels  25.4 us (30%)
  starting transfers between devices  21.6 us (25%)
  local copies, waits for them, and re-layouts  3.46 us (4%)
  between operations  1.54 us (2%)
    ppermute x10, waiting for transfers between devices, swapped(): return lax.ppermute(value, ('lon', 'lat'), pairs)  19.2 us
    ppermute x10, starting transfers between devices, swapped(): return lax.ppermute(value, ('lon', 'lat'), pairs)  14.9 us
    ppermute x1, waiting for transfers between devices, on_device(): lax.ppermute(to_west, 'lon', [((i + 1) % count, i) for i in range(count)])  8.67 us
    pallas_call x1, Pallas kernels, on_device(): call(own_kernel, 'own_points', [SMEM] * 3 + [VMEM] * 5, [shape((nodes, po...  7.41 us
    pallas_call x1, Pallas kernels, on_device(): call(grid_kernel, 'grid_points', [SMEM] + [VMEM] * 10, [shape((8, 3, late...  3.96 us
    ppermute x8, waiting for transfers between devices, core_swapped(): lax.ppermute(value, 'lat', [(i, i ^ 1) for i in range(lax.axis_size('lat'...  3.93 us
    pallas_call x1, Pallas kernels, on_device(): call(mesh_kernel, 'mesh_nodes', [SMEM] + [VMEM] * 10, [shape((8, 5, laten...  3.83 us
    unnamed x22, local copies, waits for them, and re-layouts  3.24 us
  transfers between devices with their start and end apart: 20, of which 14 were waited for; matrix products, arithmetic and copies ran while one was open for 1% of the time, Pallas kernels for 20%

profile of v5, /device:TPU:0, one launch (start us, length us, event | category | flops | bytes accessed | tf_op | source)
XLA Modules:
  0.0 84.8 jit_solution(228345878712904628)
XLA Ops:
  0.6 2.5 %pack_east.1 = bf16[474,512]{1,0:T(8,128)(2,1)} custom-call(bf16[474,8,256]{2,1,0:T(8,128)(2,1)} %bitcast.11), custom_call_target="tpu_custom_call" | custom-call | bytes 1048576 | tf_op jit(solution)/shard_map/pack_east/pallas_call | solution.py:329
  3.2 3.1 %collective-permute-start.1 = (bf16[474,512]{1,0:T(8,128)(2,1)}, bf16[474,512]{1,0:T(8,128)(2,1)S(1)}, u32[]{:S(2)}, u32[]{:S(2)}) collective-permute-start(bf16[474,512]{1,0:T(8,128)(2,1)} %pack_east.1), channel_id=1, source_target_pairs={{0,4},{4,8},{8,12},{12,0},{1,5},{5,9},{9,13},{13,1},{2,6},{6,10},{... | collective-permute-start | bytes 1456136 | tf_op jit(solution)/shard_map/ppermute | solution.py:334
  6.8 2.1 %collective-permute-start = (bf16[474,512]{1,0:T(8,128)(2,1)S(1)}, bf16[474,512]{1,0:T(8,128)(2,1)}, u32[]{:S(2)}, u32[]{:S(2)}) collective-permute-start(bf16[474,512]{1,0:T(8,128)(2,1)S(1)} %pack_west.1), channel_id=1, source_target_pairs={{4,0},{8,4},{12,8},{0,12},{5,1},{9,5},{13,9},{1,13},{6,2},{10,6},{... | collective-permute-start | bytes 1456136 | tf_op jit(solution)/shard_map/ppermute | solution.py:337
  10.6 1.2 %copy-done.5 = bf16[32,128,128]{2,1,0:T(8,128)(2,1)S(1)} copy-done((bf16[32,128,128]{2,1,0:T(8,128)(2,1)S(1)}, bf16[32,128,128]{2,1,0:T(8,128)(2,1)}, u32[]{:S(2)}) %copy-start.5) | copy-done | bytes 1048600
  11.8 1.0 %copy-done.7 = bf16[474,512]{1,0:T(8,128)(2,1)S(1)} copy-done((bf16[474,512]{1,0:T(8,128)(2,1)S(1)}, bf16[474,512]{1,0:T(8,128)(2,1)}, u32[]{:S(2)}) %copy-start.7) | copy-done | bytes 485400
  12.9 7.4 %own_points.1 = (bf16[256,3072]{1,0:T(8,128)(2,1)S(1)}, bf16[474,2048]{1,0:T(8,128)(2,1)S(1)}, bf16[512,474]{1,0:T(8,128)(2,1)S(1)}, f32[256,512]{1,0:T(8,128)S(...) custom-call(s32[32]{0:T(128)S(1)} %copy-done.9, s32[32]{0:T(128)S(1)} %copy-done.10, s32[1]{0:T(128)S(6)} %copy.21.count, ...), custom_call_target="tpu_custom_call" | custom-call | flops 4000000000 | bytes 12582912 | tf_op jit(solution)/shard_map/own_points/pallas_call | solution.py:339
  21.5 8.7 %collective-permute-done.x.x_east = bf16[474,512]{1,0:T(8,128)(2,1)} collective-permute-done((bf16[474,512]{1,0:T(8,128)(2,1)S(1)}, bf16[474,512]{1,0:T(8,128)(2,1)}, u32[]{:S(2)}, u32[]{:S(2)}) %collective-permute-start) | collective-permute-done | bytes 485408 | tf_op jit(solution)/shard_map/ppermute | solution.py:337
  30.2 3.8 %mesh_nodes.1 = (bf16[8,5,32,512]{3,2,1,0:T(8,128)(2,1)S(1)}, f32[256,512]{1,0:T(8,128)}, f32[1,512]{1,0:T(1,128)S(1)}, bf16[256,512]{1,0:T(8,128)(2,1)S(1)}, bf...) custom-call(s32[8]{0:T(128)S(1)} %stack.35.perm, bf16[474,512]{1,0:T(8,128)(2,1)} %collective-permute-done.x.x_east, ...), custom_call_target="tpu_custom_call" | custom-call | flops 2000000000 | bytes 8388608 | tf_op jit(solution)/shard_map/mesh_nodes/pallas_call | solution.py:360
  34.1 1.1 %mesh_tail.1 = (bf16[512,256]{1,0:T(8,128)(2,1)S(1)}, bf16[256,512]{1,0:T(8,128)(2,1)}, f32[256,512]{1,0:T(8,128)S(1)}) custom-call(bf16[256,512]{1,0:T(8,128)(2,1)S(1)} %get-tuple-element.45.grad_aggregate, bf16[256,512]{1,0:T(8,128)(2,1)S(1)} %get-tuple-element.46.update, bf16[512,512]{1,0:T(8,128)(2,1)S(1)} %copy-done.2, bf16[512,512]{1,0:T(8,128)(2,1)S(1)} %copy-done.1, ...), custom_call_target="tpu_custom_call" | custom-call | flops 400000000 | bytes 3145728 | tf_op jit(solution)/shard_map/mesh_tail/pallas_call | solution.py:372
  36.5 1.6 %collective-permute-start.3 = (bf16[2,5,32,512]{3,2,1,0:T(8,128)(2,1)S(1)}, bf16[2,5,32,512]{3,2,1,0:T(8,128)(2,1)S(1)}, u32[]{:S(2)}, u32[]{:S(2)}) collective-permute-start(bf16[2,5,32,512]{3,2,1,0:T(8,128)(2,1)S(1)} %slice.39), channel_id=1, source_target_pairs={{0,2},{1,5},{2,0},{3,7},{4,6},{5,1},{6,4},{7,3},{8,10},{9,13},{10,... | collective-permute-start | bytes 983048 | tf_op jit(solution)/shard_map/ppermute | solution.py:265
  38.1 4.0 %grid_points.1 = bf16[8,3,32,512]{3,2,1,0:T(8,128)(2,1)S(1)} custom-call(s32[8]{0:T(128)S(1)} %stack.35.perm, bf16[512,256]{1,0:T(8,128)(2,1)S(1)} %get-tuple-element.52.back, bf16[256,3072]{1,0:T(8,128)(2,1)S(1)} %get-tuple-element.41.refs_2_.weights_all, bf16[512,2048]{1,0:T(8,128)(2,1)S(1)} %get-tuple-element.53.slope_own, ...), custom_call_target="tpu_custom_call" | custom-call | flops 2400000000 | bytes 9437184 | tf_op jit(solution)/shard_map/grid_points/pallas_call | solution.py:381
  42.0 1.6 %collective-permute-done.3 = bf16[2,5,32,512]{3,2,1,0:T(8,128)(2,1)S(1)} collective-permute-done((bf16[2,5,32,512]{3,2,1,0:T(8,128)(2,1)S(1)}, bf16[2,5,32,512]{3,2,1,0:T(8,128)(2,1)S(1)}, u32[]{:S(2)}, u32[]{:S(2)}) %collective-permute-start.3) | collective-permute-done | bytes 327712 | tf_op jit(solution)/shard_map/ppermute | solution.py:265
  45.7 1.6 %collective-permute-start.5 = (bf16[2,3,32,512]{3,2,1,0:T(8,128)(2,1)S(1)}, bf16[2,3,32,512]{3,2,1,0:T(8,128)(2,1)S(1)}, u32[]{:S(2)}, u32[]{:S(2)}) collective-permute-start(bf16[2,3,32,512]{3,2,1,0:T(8,128)(2,1)S(1)} %slice.49), channel_id=1, source_target_pairs={{0,2},{1,5},{2,0},{3,7},{4,6},{5,1},{6,4},{7,3},{8,10},{9,13},{10,... | collective-permute-start | bytes 589832 | tf_op jit(solution)/shard_map/ppermute | solution.py:265
  47.3 2.7 %collective-permute-done.10 = bf16[1,5,32,512]{3,2,1,0:T(8,128)(2,1)S(1)} collective-permute-done((bf16[1,5,32,512]{3,2,1,0:T(8,128)(2,1)S(1)}, bf16[1,5,32,512]{3,2,1,0:T(8,128)(2,1)S(1)}, u32[]{:S(2)}, u32[]{:S(2)}) %collective-permute-start.10) | collective-permute-done | bytes 163872 | tf_op jit(solution)/shard_map/ppermute | solution.py:265
  50.0 2.2 %collective-permute-start.11 = (bf16[1,5,32,512]{3,2,1,0:T(8,128)(2,1)S(1)}, bf16[1,5,32,512]{3,2,1,0:T(8,128)(2,1)S(1)}, u32[]{:S(2)}, u32[]{:S(2)}) collective-permute-start(bf16[1,5,32,512]{3,2,1,0:T(8,128)(2,1)S(1)} %add_convert_fusion.5), channel_id=1, source_target_pairs={{0,8},{1,9},{2,10},{3,11},{4,12},{5,13},{6,14},{7,15},{8,0},{9,1},... | collective-permute-start | bytes 491528 | tf_op jit(solution)/shard_map/ppermute | solution.py:265
  52.3 1.6 %collective-permute-start.6 = (bf16[1,3,32,512]{3,2,1,0:T(8,128)(2,1)S(1)}, bf16[1,3,32,512]{3,2,1,0:T(8,128)(2,1)S(1)}, u32[]{:S(2)}, u32[]{:S(2)}) collective-permute-start(bf16[1,3,32,512]{3,2,1,0:T(8,128)(2,1)S(1)} %slice.51), channel_id=1, source_target_pairs={{0,4},{1,3},{2,6},{3,1},{4,0},{5,7},{6,2},{7,5},{8,12},{9,11},{10,... | collective-permute-start | bytes 294920 | tf_op jit(solution)/shard_map/ppermute | solution.py:265
  53.9 5.7 %collective-permute-done.11 = bf16[1,5,32,512]{3,2,1,0:T(8,128)(2,1)S(1)} collective-permute-done((bf16[1,5,32,512]{3,2,1,0:T(8,128)(2,1)S(1)}, bf16[1,5,32,512]{3,2,1,0:T(8,128)(2,1)S(1)}, u32[]{:S(2)}, u32[]{:S(2)}) %collective-permute-start.11) | collective-permute-done | bytes 163872 | tf_op jit(solution)/shard_map/ppermute | solution.py:265
  59.9 3.3 %collective-permute-start.7 = (bf16[1,3,32,512]{3,2,1,0:T(8,128)(2,1)S(1)}, bf16[1,3,32,512]{3,2,1,0:T(8,128)(2,1)S(1)}, u32[]{:S(2)}, u32[]{:S(2)}) collective-permute-start(bf16[1,3,32,512]{3,2,1,0:T(8,128)(2,1)S(1)} %add_convert_fusion.7), channel_id=1, source_target_pairs={{0,8},{1,9},{2,10},{3,11},{4,12},{5,13},{6,14},{7,15},{8,0},{9,1},... | collective-permute-start | bytes 294920 | tf_op jit(solution)/shard_map/ppermute | solution.py:265
  63.3 3.8 %collective-permute-done.12.refs_1_ = bf16[1,5,32,512]{3,2,1,0:T(8,128)(2,1)S(1)} collective-permute-done((bf16[1,5,32,512]{3,2,1,0:T(8,128)(2,1)S(1)}, bf16[1,5,32,512]{3,2,1,0:T(8,128)(2,1)S(1)}, u32[]{:S(2)}, u32[]{:S(2)}) %collective-permute-start.12) | collective-permute-done | bytes 163872 | tf_op jit(solution)/shard_map/ppermute | solution.py:265
  67.1 1.8 %collective-permute-start.13 = (bf16[2,5,32,512]{3,2,1,0:T(8,128)(2,1)S(1)}, bf16[2,5,32,512]{3,2,1,0:T(8,128)(2,1)S(1)}, u32[]{:S(2)}, u32[]{:S(2)}) collective-permute-start(bf16[2,5,32,512]{3,2,1,0:T(8,128)(2,1)S(1)} %pad_maximum_fusion), channel_id=1, source_target_pairs={{0,2},{1,5},{2,0},{3,7},{4,6},{5,1},{6,4},{7,3},{8,10},{9,13},{10,... | collective-permute-start | bytes 983048 | tf_op jit(solution)/shard_map/ppermute | solution.py:265
  69.0 5.2 %collective-permute-done.13.refs_2_ = bf16[2,5,32,512]{3,2,1,0:T(8,128)(2,1)S(1)} collective-permute-done((bf16[2,5,32,512]{3,2,1,0:T(8,128)(2,1)S(1)}, bf16[2,5,32,512]{3,2,1,0:T(8,128)(2,1)S(1)}, u32[]{:S(2)}, u32[]{:S(2)}) %collective-permute-start.13) | collective-permute-done | bytes 327712 | tf_op jit(solution)/shard_map/ppermute | solution.py:265
  74.3 1.8 %collective-permute-start.9 = (bf16[2,3,32,512]{3,2,1,0:T(8,128)(2,1)S(1)}, bf16[2,3,32,512]{3,2,1,0:T(8,128)(2,1)S(1)}, u32[]{:S(2)}, u32[]{:S(2)}) collective-permute-start(bf16[2,3,32,512]{3,2,1,0:T(8,128)(2,1)S(1)} %pad_maximum_fusion.1), channel_id=1, source_target_pairs={{0,2},{1,5},{2,0},{3,7},{4,6},{5,1},{6,4},{7,3},{8,10},{9,13},{10,... | collective-permute-start | bytes 589832 | tf_op jit(solution)/shard_map/ppermute | solution.py:265
  77.7 2.8 %order_a.1 = (f32[512,512]{1,0:T(8,128)}, f32[512,512]{1,0:T(8,128)}, f32[512,512]{1,0:T(8,128)}) custom-call(s32[8]{0:T(128)S(1)} %stack.35.perm, bf16[1,5,32,512]{3,2,1,0:T(8,128)(2,1)S(1)} %add_convert_fusion.4.refs_0_, bf16[1,5,32,512]{3,2,1,0:T(8,128)(2,1)S(1)} %collective-permute-done.12.refs_1_, ...), custom_call_target="tpu_custom_call" | custom-call | bytes 4194304 | tf_op jit(solution)/shard_map/order_a/pallas_call | solution.py:391
  82.4 2.3 %order_b.1 = (f32[512,512]{1,0:T(8,128)}, f32[474,512]{1,0:T(8,128)}, f32[1,512]{1,0:T(1,128)}) custom-call(s32[8]{0:T(128)S(1)} %stack.35.perm, bf16[1,3,32,512]{3,2,1,0:T(8,128)(2,1)S(1)} %add_convert_fusion.6.refs_0_, bf16[1,3,32,512]{3,2,1,0:T(8,128)(2,1)S(1)} %collective-permute-done.8.refs_1_, ...), custom_call_target="tpu_custom_call", output_to_operand_aliasing={{0}: (7, {})} | custom-call | bytes 3145728 | tf_op jit(solution)/shard_map/order_b/pallas_call | solution.py:396
  (64 shorter events, 10.2 us)
Async XLA Ops:
  3.2 17.4 %collective-permute-start.1 = (bf16[474,512]{1,0:T(8,128)(2,1)}, bf16[474,512]{1,0:T(8,128)(2,1)S(1)}, u32[]{:S(2)}, u32[]{:S(2)}) collective-permute-start(bf16[474,512]{1,0:T(8,128)(2,1)} %pack_east.1), channel_id=1, source_target_pairs={{0,4},{4,8},{8,12},{12,0},{1,5},{5,9},{9,13},{13,1},{2,6},{6,10},{... | collective-permute-start | bytes 1456136 | tf_op jit(solution)/shard_map/ppermute | solution.py:334
  6.8 23.4 %collective-permute-start = (bf16[474,512]{1,0:T(8,128)(2,1)S(1)}, bf16[474,512]{1,0:T(8,128)(2,1)}, u32[]{:S(2)}, u32[]{:S(2)}) collective-permute-start(bf16[474,512]{1,0:T(8,128)(2,1)S(1)} %pack_west.1), channel_id=1, source_target_pairs={{4,0},{8,4},{12,8},{0,12},{5,1},{9,5},{13,9},{1,13},{6,2},{10,6},{... | collective-permute-start | bytes 1456136 | tf_op jit(solution)/shard_map/ppermute | solution.py:337
  20.6 9.6 %copy-start.2 = (bf16[512,512]{1,0:T(8,128)(2,1)S(1)}, bf16[512,512]{1,0:T(8,128)(2,1)}, u32[]{:S(2)}) copy-start(bf16[512,512]{1,0:T(8,128)(2,1)} %message_w.3) | copy-start | bytes 1572868
  20.6 9.6 %copy-start.4 = (bf16[256,512]{1,0:T(8,128)(2,1)S(1)}, bf16[256,512]{1,0:T(8,128)(2,1)}, u32[]{:S(2)}) copy-start(bf16[256,512]{1,0:T(8,128)(2,1)} %mesh_lat.3) | copy-start | bytes 786436
  20.6 9.6 %copy-start.6 = (bf16[512,512]{1,0:T(8,128)(2,1)S(1)}, bf16[512,512]{1,0:T(8,128)(2,1)}, u32[]{:S(2)}) copy-start(bf16[512,512]{1,0:T(8,128)(2,1)} %up_w.1) | copy-start | bytes 1572868
  20.6 9.6 %copy-start.8 = (f32[512]{0:T(512)S(1)}, f32[512]{0:T(512)}, u32[]{:S(2)}) copy-start(f32[512]{0:T(512)} %param.22) | copy-start | bytes 6148
  34.1 2.2 %collective-permute-start.2 = (bf16[4,5,32,512]{3,2,1,0:T(8,128)(2,1)S(1)}, bf16[4,5,32,512]{3,2,1,0:T(8,128)(2,1)S(1)}, u32[]{:S(2)}, u32[]{:S(2)}) collective-permute-start(bf16[4,5,32,512]{3,2,1,0:T(8,128)(2,1)S(1)} %slice.37), channel_id=1, source_target_pairs={{0,1},{1,0},{2,3},{3,2},{4,5},{5,4},{6,7},{7,6},{8,9},{9,8},{10,11... | collective-permute-start | bytes 1966088 | tf_op jit(solution)/shard_map/ppermute | solution.py:254
  36.5 7.1 %collective-permute-start.3 = (bf16[2,5,32,512]{3,2,1,0:T(8,128)(2,1)S(1)}, bf16[2,5,32,512]{3,2,1,0:T(8,128)(2,1)S(1)}, u32[]{:S(2)}, u32[]{:S(2)}) collective-permute-start(bf16[2,5,32,512]{3,2,1,0:T(8,128)(2,1)S(1)} %slice.39), channel_id=1, source_target_pairs={{0,2},{1,5},{2,0},{3,7},{4,6},{5,1},{6,4},{7,3},{8,10},{9,13},{10,... | collective-permute-start | bytes 983048 | tf_op jit(solution)/shard_map/ppermute | solution.py:265
  43.8 1.8 %collective-permute-start.4 = (bf16[4,3,32,512]{3,2,1,0:T(8,128)(2,1)S(1)}, bf16[4,3,32,512]{3,2,1,0:T(8,128)(2,1)S(1)}, u32[]{:S(2)}, u32[]{:S(2)}) collective-permute-start(bf16[4,3,32,512]{3,2,1,0:T(8,128)(2,1)S(1)} %slice.41), channel_id=1, source_target_pairs={{0,1},{1,0},{2,3},{3,2},{4,5},{5,4},{6,7},{7,6},{8,9},{9,8},{10,11... | collective-permute-start | bytes 1179656 | tf_op jit(solution)/shard_map/ppermute | solution.py:254
  43.9 6.1 %collective-permute-start.10 = (bf16[1,5,32,512]{3,2,1,0:T(8,128)(2,1)S(1)}, bf16[1,5,32,512]{3,2,1,0:T(8,128)(2,1)S(1)}, u32[]{:S(2)}, u32[]{:S(2)}) collective-permute-start(bf16[1,5,32,512]{3,2,1,0:T(8,128)(2,1)S(1)} %slice.47), channel_id=1, source_target_pairs={{0,4},{1,3},{2,6},{3,1},{4,0},{5,7},{6,2},{7,5},{8,12},{9,11},{10,... | collective-permute-start | bytes 491528 | tf_op jit(solution)/shard_map/ppermute | solution.py:265
  45.7 6.5 %collective-permute-start.5 = (bf16[2,3,32,512]{3,2,1,0:T(8,128)(2,1)S(1)}, bf16[2,3,32,512]{3,2,1,0:T(8,128)(2,1)S(1)}, u32[]{:S(2)}, u32[]{:S(2)}) collective-permute-start(bf16[2,3,32,512]{3,2,1,0:T(8,128)(2,1)S(1)} %slice.49), channel_id=1, source_target_pairs={{0,2},{1,5},{2,0},{3,7},{4,6},{5,1},{6,4},{7,3},{8,10},{9,13},{10,... | collective-permute-start | bytes 589832 | tf_op jit(solution)/shard_map/ppermute | solution.py:265
  50.0 9.6 %collective-permute-start.11 = (bf16[1,5,32,512]{3,2,1,0:T(8,128)(2,1)S(1)}, bf16[1,5,32,512]{3,2,1,0:T(8,128)(2,1)S(1)}, u32[]{:S(2)}, u32[]{:S(2)}) collective-permute-start(bf16[1,5,32,512]{3,2,1,0:T(8,128)(2,1)S(1)} %add_convert_fusion.5), channel_id=1, source_target_pairs={{0,8},{1,9},{2,10},{3,11},{4,12},{5,13},{6,14},{7,15},{8,0},{9,1},... | collective-permute-start | bytes 491528 | tf_op jit(solution)/shard_map/ppermute | solution.py:265
  52.3 7.6 %collective-permute-start.6 = (bf16[1,3,32,512]{3,2,1,0:T(8,128)(2,1)S(1)}, bf16[1,3,32,512]{3,2,1,0:T(8,128)(2,1)S(1)}, u32[]{:S(2)}, u32[]{:S(2)}) collective-permute-start(bf16[1,3,32,512]{3,2,1,0:T(8,128)(2,1)S(1)} %slice.51), channel_id=1, source_target_pairs={{0,4},{1,3},{2,6},{3,1},{4,0},{5,7},{6,2},{7,5},{8,12},{9,11},{10,... | collective-permute-start | bytes 294920 | tf_op jit(solution)/shard_map/ppermute | solution.py:265
  59.7 7.4 %collective-permute-start.12 = (bf16[1,5,32,512]{3,2,1,0:T(8,128)(2,1)S(1)}, bf16[1,5,32,512]{3,2,1,0:T(8,128)(2,1)S(1)}, u32[]{:S(2)}, u32[]{:S(2)}) collective-permute-start(bf16[1,5,32,512]{3,2,1,0:T(8,128)(2,1)S(1)} %add_convert_fusion.4.refs_0_), channel_id=1, source_target_pairs={{0,4},{1,3},{2,6},{3,1},{4,0},{5,7},{6,2},{7,5},{8,12},{9,11},{10,... | collective-permute-start | bytes 491528 | tf_op jit(solution)/shard_map/ppermute | solution.py:265
  59.9 9.0 %collective-permute-start.7 = (bf16[1,3,32,512]{3,2,1,0:T(8,128)(2,1)S(1)}, bf16[1,3,32,512]{3,2,1,0:T(8,128)(2,1)S(1)}, u32[]{:S(2)}, u32[]{:S(2)}) collective-permute-start(bf16[1,3,32,512]{3,2,1,0:T(8,128)(2,1)S(1)} %add_convert_fusion.7), channel_id=1, source_target_pairs={{0,8},{1,9},{2,10},{3,11},{4,12},{5,13},{6,14},{7,15},{8,0},{9,1},... | collective-permute-start | bytes 294920 | tf_op jit(solution)/shard_map/ppermute | solution.py:265
  67.1 7.1 %collective-permute-start.13 = (bf16[2,5,32,512]{3,2,1,0:T(8,128)(2,1)S(1)}, bf16[2,5,32,512]{3,2,1,0:T(8,128)(2,1)S(1)}, u32[]{:S(2)}, u32[]{:S(2)}) collective-permute-start(bf16[2,5,32,512]{3,2,1,0:T(8,128)(2,1)S(1)} %pad_maximum_fusion), channel_id=1, source_target_pairs={{0,2},{1,5},{2,0},{3,7},{4,6},{5,1},{6,4},{7,3},{8,10},{9,13},{10,... | collective-permute-start | bytes 983048 | tf_op jit(solution)/shard_map/ppermute | solution.py:265
  69.0 5.3 %collective-permute-start.8 = (bf16[1,3,32,512]{3,2,1,0:T(8,128)(2,1)S(1)}, bf16[1,3,32,512]{3,2,1,0:T(8,128)(2,1)S(1)}, u32[]{:S(2)}, u32[]{:S(2)}) collective-permute-start(bf16[1,3,32,512]{3,2,1,0:T(8,128)(2,1)S(1)} %add_convert_fusion.6.refs_0_), channel_id=1, source_target_pairs={{0,4},{1,3},{2,6},{3,1},{4,0},{5,7},{6,2},{7,5},{8,12},{9,11},{10,... | collective-permute-start | bytes 294920 | tf_op jit(solution)/shard_map/ppermute | solution.py:265
  74.3 3.5 %collective-permute-start.16 = (bf16[2,5,32,512]{3,2,1,0:T(8,128)(2,1)S(1)}, bf16[2,5,32,512]{3,2,1,0:T(8,128)(2,1)S(1)}, u32[]{:S(2)}, u32[]{:S(2)}) collective-permute-start(bf16[2,5,32,512]{3,2,1,0:T(8,128)(2,1)S(1)} %collective-permute-done.13.refs_2_), channel_id=1, source_target_pairs={{0,1},{1,0},{2,3},{3,2},{4,5},{5,4},{6,7},{7,6},{8,9},{9,8},{10,11... | collective-permute-start | bytes 983048 | tf_op jit(solution)/shard_map/ppermute | solution.py:254
  74.3 6.3 %collective-permute-start.9 = (bf16[2,3,32,512]{3,2,1,0:T(8,128)(2,1)S(1)}, bf16[2,3,32,512]{3,2,1,0:T(8,128)(2,1)S(1)}, u32[]{:S(2)}, u32[]{:S(2)}) collective-permute-start(bf16[2,3,32,512]{3,2,1,0:T(8,128)(2,1)S(1)} %pad_maximum_fusion.1), channel_id=1, source_target_pairs={{0,2},{1,5},{2,0},{3,7},{4,6},{5,1},{6,4},{7,3},{8,10},{9,13},{10,... | collective-permute-start | bytes 589832 | tf_op jit(solution)/shard_map/ppermute | solution.py:265
  76.1 1.4 %collective-permute-start.14 = (bf16[1,5,32,512]{3,2,1,0:T(8,128)(2,1)S(1)}, bf16[1,5,32,512]{3,2,1,0:T(8,128)(2,1)S(1)}, u32[]{:S(2)}, u32[]{:S(2)}) collective-permute-start(bf16[1,5,32,512]{3,2,1,0:T(8,128)(2,1)S(1)} %add_convert_fusion.4.refs_0_), channel_id=1, source_target_pairs={{0,1},{1,0},{2,3},{3,2},{4,5},{5,4},{6,7},{7,6},{8,9},{9,8},{10,11... | collective-permute-start | bytes 491528 | tf_op jit(solution)/shard_map/ppermute | solution.py:254
  76.1 1.6 %collective-permute-start.15 = (bf16[1,5,32,512]{3,2,1,0:T(8,128)(2,1)S(1)}, bf16[1,5,32,512]{3,2,1,0:T(8,128)(2,1)S(1)}, u32[]{:S(2)}, u32[]{:S(2)}) collective-permute-start(bf16[1,5,32,512]{3,2,1,0:T(8,128)(2,1)S(1)} %collective-permute-done.12.refs_1_), channel_id=1, source_target_pairs={{0,1},{1,0},{2,3},{3,2},{4,5},{5,4},{6,7},{7,6},{8,9},{9,8},{10,11... | collective-permute-start | bytes 491528 | tf_op jit(solution)/shard_map/ppermute | solution.py:254
  80.6 1.9 %collective-permute-start.19 = (bf16[2,3,32,512]{3,2,1,0:T(8,128)(2,1)S(1)}, bf16[2,3,32,512]{3,2,1,0:T(8,128)(2,1)S(1)}, u32[]{:S(2)}, u32[]{:S(2)}) collective-permute-start(bf16[2,3,32,512]{3,2,1,0:T(8,128)(2,1)S(1)} %collective-permute-done.9.refs_2_), channel_id=1, source_target_pairs={{0,1},{1,0},{2,3},{3,2},{4,5},{5,4},{6,7},{7,6},{8,9},{9,8},{10,11... | collective-permute-start | bytes 589832 | tf_op jit(solution)/shard_map/ppermute | solution.py:254
  80.9 1.3 %collective-permute-start.17 = (bf16[1,3,32,512]{3,2,1,0:T(8,128)(2,1)S(1)}, bf16[1,3,32,512]{3,2,1,0:T(8,128)(2,1)S(1)}, u32[]{:S(2)}, u32[]{:S(2)}) collective-permute-start(bf16[1,3,32,512]{3,2,1,0:T(8,128)(2,1)S(1)} %add_convert_fusion.6.refs_0_), channel_id=1, source_target_pairs={{0,1},{1,0},{2,3},{3,2},{4,5},{5,4},{6,7},{7,6},{8,9},{9,8},{10,11... | collective-permute-start | bytes 294920 | tf_op jit(solution)/shard_map/ppermute | solution.py:254
  81.1 1.3 %collective-permute-start.18 = (bf16[1,3,32,512]{3,2,1,0:T(8,128)(2,1)S(1)}, bf16[1,3,32,512]{3,2,1,0:T(8,128)(2,1)S(1)}, u32[]{:S(2)}, u32[]{:S(2)}) collective-permute-start(bf16[1,3,32,512]{3,2,1,0:T(8,128)(2,1)S(1)} %collective-permute-done.8.refs_1_), channel_id=1, source_target_pairs={{0,1},{1,0},{2,3},{3,2},{4,5},{5,4},{6,7},{7,6},{8,9},{9,8},{10,11... | collective-permute-start | bytes 294920 | tf_op jit(solution)/shard_map/ppermute | solution.py:254
  (7 other events, 28.2 us)

commit v6 on v4

--- a/solution.py
+++ b/solution.py
@@ -9,7 +9,6 @@
 BF = jnp.bfloat16
 F32 = jnp.float32
 MIB = 1024 * 1024
-PIECE = 128
 SMEM = pl.BlockSpec(memory_space=pltpu.SMEM)
 VMEM = pl.BlockSpec(memory_space=pltpu.VMEM)
 HBM = pl.BlockSpec(memory_space=pltpu.HBM)
@@ -25,33 +24,21 @@
     return pre * sigma, sigma * (1.0 + pre * (1.0 - sigma))
 
 
-def pack_kernel(grid, to_west, to_east, held, wide, sems):
+def pack_kernel(from_high, grid, out, wide):
     features, rows, cols = grid.shape
-    half = to_west.shape[1] // rows
-    block = 2 * half
-    last = cols // block - 1
-    pieces = []
-    for n, first in enumerate(range(0, features, PIECE)):
-        at = pl.ds(first, min(PIECE, features - first))
-        pieces.append((at, pltpu.make_async_copy(grid.at[at], held.at[at], sems.at[n])))
-    for _, copy in pieces:
-        copy.start()
-    for at, copy in pieces:
-        copy.wait()
-        size = at.size
-        for k in (0, last):
-            wide[k, pl.ds(at.start * rows, size * rows), :] = (
-                held[at, :, k * block : (k + 1) * block].astype(F32).reshape(size * rows, block)
-            )
-        lane = lax.broadcasted_iota(jnp.int32, (size, block), 1)
-        for pair in range(rows // 2):
-            even = pl.ds(at.start * rows + 2 * pair, size, stride=rows)
-            odd = pl.ds(at.start * rows + 2 * pair + 1, size, stride=rows)
-            to = slice(pair * block, (pair + 1) * block)
-            head = jnp.where(lane < half, wide[0, even, :], pltpu.roll(wide[0, odd, :], half, 1))
-            tail = jnp.where(lane < half, pltpu.roll(wide[last, even, :], half, 1), wide[last, odd, :])
-            to_west[at, to] = head.astype(BF)
-            to_east[at, to] = tail.astype(BF)
+    block = wide.shape[1]
+    half = block // 2
+    start = cols - block if from_high else 0
+    wide[...] = grid[:, :, start : start + block].astype(F32).reshape(features * rows, block)
+    lane = lax.broadcasted_iota(jnp.int32, (features, block), 1)
+    for pair in range(rows // 2):
+        even = wide[pl.ds(2 * pair, features, stride=rows), :]
+        odd = wide[pl.ds(2 * pair + 1, features, stride=rows), :]
+        if from_high:
+            even = pltpu.roll(even, half, 1)
+        else:
+            odd = pltpu.roll(odd, half, 1)
+        out[:, pair * block : (pair + 1) * block] = jnp.where(lane < half, even, odd).astype(BF)
 
 
 def own_kernel(
@@ -211,18 +198,29 @@
 
 
 def order_grid_kernel(perm, *refs):
-    grad_out, grad_embed, grad_gain, total = refs[-4:]
-    from_chunks((grad_out, total), refs[:-4], perm)
+    grad_out, grad_embed, grad_gain, held, total, sems = refs[-6:]
+    copies = []
+    chunks = [(chunk, n) for chunk in refs[:-6] for n in range(chunk.shape[0])]
+    size = held.shape[1]
+    for j, (chunk, n) in enumerate(chunks):
+        held[j] = chunk[n, 0].astype(F32)
+        at = pl.ds(pl.multiple_of(perm[j] * size, size), size)
+        copies.append(pltpu.make_async_copy(held.at[j], grad_out.at[at], sems.at[j]))
+        copies[-1].start()
+    for j, (chunk, n) in enumerate(chunks):
+        total[pl.ds(pl.multiple_of(perm[j] * size, size), size), :] = chunk[n, 1].astype(F32)
     features = grad_embed.shape[0]
     grad_embed[...] = total[:features, :]
     grad_gain[...] = total[features : features + 1, :]
+    for copy in copies:
+        copy.wait()
 
 
 def role_steps():
     lat = [("lat", 2 << k) for k in range(lax.axis_size("lat").bit_length() - 2)]
     lon = [("lon", 1 << k) for k in range(lax.axis_size("lon").bit_length() - 1)]
-    rest = lat[1:] + lon[1:]
-    return ([lat[0], lon[0]] + rest, [lon[0], lat[0]] + rest)
+    rest = lat[1:] + lon[2:]
+    return ([lat[0], lon[1], lon[0]] + rest, [lon[0], lat[0], lon[1]] + rest)
 
 
 def core_swapped(value):
@@ -286,28 +284,25 @@
     points = own + 2 * side
     grid = jnp.transpose(grid_in, (2, 0, 1))
 
-    def call(kernel, name, in_specs, out_shape, flops, bytes_accessed, limit, scratch_shapes=()):
+    def call(kernel, name, in_specs, out_shape, flops, bytes_accessed, limit, scratch_shapes=(), out_specs=None):
         return pl.pallas_call(
             kernel,
             name=name,
             in_specs=in_specs,
-            out_specs=[VMEM] * len(out_shape),
+            out_specs=out_specs or [VMEM] * len(out_shape),
             out_shape=out_shape,
             scratch_shapes=list(scratch_shapes),
             compiler_params=pltpu.CompilerParams(vmem_limit_bytes=limit * MIB),
             cost_estimate=pl.CostEstimate(flops=flops, bytes_accessed=bytes_accessed, transcendentals=0),
         )
 
-    to_west, to_east = call(
-        pack_kernel, "pack", [HBM], [shape((features, side), BF)] * 2, 0, 3 * MIB, 60,
-        [
-            pltpu.VMEM((features, rows, cols), BF),
-            pltpu.VMEM((cols // block, features * rows, block), F32),
-            pltpu.SemaphoreType.DMA((-(-features // PIECE),)),
-        ],
-    )(grid)
+    strip = shape((features, side), BF)
+    wide = pltpu.VMEM((features * rows, block), F32)
     count = lax.axis_size("lon")
+    (to_east,) = call(lambda *refs: pack_kernel(True, *refs), "pack_east", [VMEM], [strip], 0, MIB, 20, [wide])(grid)
     x_west = lax.ppermute(to_east, "lon", [(i, (i + 1) % count) for i in range(count)])
+    to_east, later = lax.optimization_barrier((to_east, grid))
+    (to_west,) = call(lambda *refs: pack_kernel(False, *refs), "pack_west", [VMEM], [strip], 0, MIB, 20, [wide])(later)
     x_east = lax.ppermute(to_west, "lon", [((i + 1) % count, i) for i in range(count)])
 
     weights_all, x_own, embed_t, h_own, slope_own, grad_update = call(
@@ -368,7 +363,8 @@
     grad_out, grad_embed, grad_gain = call(
         order_grid_kernel, "order_b", [SMEM] + [VMEM] * 6,
         [square, shape((features, latent), F32), shape((1, latent), F32)], 0, 3 * MIB, 16,
-        [pltpu.VMEM((latent, latent), F32)],
+        [pltpu.VMEM((8, latent // 8, latent), F32), pltpu.VMEM((latent, latent), F32), pltpu.SemaphoreType.DMA((8,))],
+        out_specs=[HBM, VMEM, VMEM],
     )(perm, *from_both_cores((*summed_b[:2], last)))
     return (mesh_new, mesh_grad, grad_embed, grad_message, grad_up, grad_out, grad_gain[0])
 

time: 81.5 us -> 86.1 us (1.056)
  waiting for transfers between devices: 32.1 us -> 36.2 us
    ppermute x10, waiting for transfers between devices: 20.4 us -> 23.8 us  [swapped(): return lax.ppermute(value, ('lon', 'lat'), pairs)]
    pallas_call x1 -> x2, Pallas kernels: 3.08 us -> 1.78 us  [the longest x1 1.28 us: on_device(): call(lambda *refs: pack_kernel(True, *refs), 'pack_east', [VMEM], [strip]...]
    unnamed x22 -> x24, local copies, waits for them, and re-layouts: 4.28 us -> 4.77 us
  transfers between devices with their start and end apart: 20 -> 20, of which waited for: 17 -> 18; matrix products, arithmetic and copies ran while one was open for 1% -> 1% of each run, Pallas kernels for 18% -> 18%
where the time goes in v6:
time: 86.1 us; the launch traced here: 85.8 us
  waiting for transfers between devices  36.2 us (42%)
  Pallas kernels  23.1 us (27%)
  starting transfers between devices  19.3 us (22%)
  local copies, waits for them, and re-layouts  4.98 us (6%)
  between operations  1.53 us (2%)
    ppermute x10, waiting for transfers between devices, swapped(): return lax.ppermute(value, ('lon', 'lat'), pairs)  23.8 us
    ppermute x10, starting transfers between devices, swapped(): return lax.ppermute(value, ('lon', 'lat'), pairs)  13 us
    ppermute x1, waiting for transfers between devices, on_device(): lax.ppermute(to_west, 'lon', [((i + 1) % count, i) for i in range(count)])  8.68 us
    pallas_call x1, Pallas kernels, on_device(): call(own_kernel, 'own_points', [SMEM] * 3 + [VMEM] * 5, [shape((nodes, po...  7.22 us
    unnamed x24, local copies, waits for them, and re-layouts  4.77 us
    pallas_call x1, Pallas kernels, on_device(): call(grid_kernel, 'grid_points', [SMEM] + [VMEM] * 10, [shape((8, 2, late...  4.02 us
    pallas_call x1, Pallas kernels, on_device(): call(mesh_kernel, 'mesh_nodes', [SMEM] + [VMEM] * 10, [shape((8, 2, laten...  3.59 us
    ppermute x8, waiting for transfers between devices, core_swapped(): lax.ppermute(value, 'lat', [(i, i ^ 1) for i in range(lax.axis_size('lat'...  3.26 us
  transfers between devices with their start and end apart: 20, of which 18 were waited for; matrix products, arithmetic and copies ran while one was open for 1% of the time, Pallas kernels for 18%

profile of v6, /device:TPU:0, one launch (start us, length us, event | category | flops | bytes accessed | tf_op | source)
XLA Modules:
  0.0 85.8 jit_solution(16454798183036636247)
XLA Ops:
  0.6 1.5 %copy-done = bf16[8,256,474]{1,0,2:T(8,128)(2,1)S(1)} copy-done((bf16[8,256,474]{1,0,2:T(8,128)(2,1)S(1)}, bf16[8,256,474]{1,0,2:T(8,128)(2,1)}, u32[]{:S(2)}) %copy-start) | copy-done | bytes 1941528
  2.2 1.3 %pack_east.1 = bf16[474,512]{1,0:T(8,128)(2,1)} custom-call(bf16[474,8,256]{2,1,0:T(8,128)(2,1)S(1)} %bitcast.11), custom_call_target="tpu_custom_call" | custom-call | bytes 1048576 | tf_op jit(solution)/shard_map/pack_east/pallas_call | solution.py:302
  3.5 3.0 %collective-permute-start.1 = (bf16[474,512]{1,0:T(8,128)(2,1)}, bf16[474,512]{1,0:T(8,128)(2,1)S(1)}, u32[]{:S(2)}, u32[]{:S(2)}) collective-permute-start(bf16[474,512]{1,0:T(8,128)(2,1)} %pack_east.1), channel_id=1, source_target_pairs={{0,4},{4,8},{8,12},{12,0},{1,5},{5,9},{9,13},{13,1},{2,6},{6,10},{... | collective-permute-start | bytes 1456136 | tf_op jit(solution)/shard_map/ppermute | solution.py:303
  7.0 2.1 %collective-permute-start = (bf16[474,512]{1,0:T(8,128)(2,1)S(1)}, bf16[474,512]{1,0:T(8,128)(2,1)}, u32[]{:S(2)}, u32[]{:S(2)}) collective-permute-start(bf16[474,512]{1,0:T(8,128)(2,1)S(1)} %pack_west.1), channel_id=1, source_target_pairs={{4,0},{8,4},{12,8},{0,12},{5,1},{9,5},{13,9},{1,13},{6,2},{10,6},{... | collective-permute-start | bytes 1456136 | tf_op jit(solution)/shard_map/ppermute | solution.py:306
  13.0 7.2 %own_points.1 = (bf16[256,3072]{1,0:T(8,128)(2,1)S(1)}, bf16[474,2048]{1,0:T(8,128)(2,1)S(1)}, bf16[512,474]{1,0:T(8,128)(2,1)S(1)}, f32[256,512]{1,0:T(8,128)S(...) custom-call(s32[32]{0:T(128)S(1)} %copy-done.10, s32[32]{0:T(128)S(1)} %copy-done.11, s32[1]{0:T(128)S(6)} %copy.19.count, ...), custom_call_target="tpu_custom_call" | custom-call | flops 4000000000 | bytes 12582912 | tf_op jit(solution)/shard_map/own_points/pallas_call | solution.py:308
  21.7 8.7 %collective-permute-done.x.x_east = bf16[474,512]{1,0:T(8,128)(2,1)} collective-permute-done((bf16[474,512]{1,0:T(8,128)(2,1)S(1)}, bf16[474,512]{1,0:T(8,128)(2,1)}, u32[]{:S(2)}, u32[]{:S(2)}) %collective-permute-start) | collective-permute-done | bytes 485408 | tf_op jit(solution)/shard_map/ppermute | solution.py:306
  30.4 3.6 %mesh_nodes.1 = (bf16[8,2,64,512]{3,2,1,0:T(8,128)(2,1)S(1)}, f32[256,512]{1,0:T(8,128)}, f32[1,512]{1,0:T(1,128)S(1)}, bf16[256,512]{1,0:T(8,128)(2,1)S(1)}, bf...) custom-call(s32[8]{0:T(128)S(1)} %stack.35.perm, bf16[474,512]{1,0:T(8,128)(2,1)} %collective-permute-done.x.x_east, ...), custom_call_target="tpu_custom_call" | custom-call | flops 2000000000 | bytes 8388608 | tf_op jit(solution)/shard_map/mesh_nodes/pallas_call | solution.py:329
  36.2 1.6 %collective-permute-start.3 = (bf16[2,2,64,512]{3,2,1,0:T(8,128)(2,1)S(1)}, bf16[2,2,64,512]{3,2,1,0:T(8,128)(2,1)S(1)}, u32[]{:S(2)}, u32[]{:S(2)}) collective-permute-start(bf16[2,2,64,512]{3,2,1,0:T(8,128)(2,1)S(1)} %slice.39), channel_id=1, source_target_pairs={{0,2},{1,5},{2,0},{3,7},{4,6},{5,1},{6,4},{7,3},{8,10},{9,13},{10,... | collective-permute-start | bytes 786440 | tf_op jit(solution)/shard_map/ppermute | solution.py:238
  37.7 4.0 %grid_points.1 = bf16[8,2,64,512]{3,2,1,0:T(8,128)(2,1)S(1)} custom-call(s32[8]{0:T(128)S(1)} %stack.35.perm, bf16[512,256]{1,0:T(8,128)(2,1)S(1)} %get-tuple-element.50.back, bf16[256,3072]{1,0:T(8,128)(2,1)S(1)} %get-tuple-element.39.refs_2_.weights_all, bf16[512,2048]{1,0:T(8,128)(2,1)S(1)} %get-tuple-element.51.slope_own, ...), custom_call_target="tpu_custom_call" | custom-call | flops 2400000000 | bytes 9437184 | tf_op jit(solution)/shard_map/grid_points/pallas_call | solution.py:350
  42.8 1.8 %collective-permute-start.10 = (bf16[1,2,64,512]{3,2,1,0:T(8,128)(2,1)S(1)}, bf16[1,2,64,512]{3,2,1,0:T(8,128)(2,1)S(1)}, u32[]{:S(2)}, u32[]{:S(2)}) collective-permute-start(bf16[1,2,64,512]{3,2,1,0:T(8,128)(2,1)S(1)} %slice.47), channel_id=1, source_target_pairs={{0,8},{1,3},{2,10},{3,1},{4,12},{5,7},{6,14},{7,5},{8,0},{9,11},{1... | collective-permute-start | bytes 393224 | tf_op jit(solution)/shard_map/ppermute | solution.py:238
  44.9 1.6 %collective-permute-start.5 = (bf16[2,2,64,512]{3,2,1,0:T(8,128)(2,1)S(1)}, bf16[2,2,64,512]{3,2,1,0:T(8,128)(2,1)S(1)}, u32[]{:S(2)}, u32[]{:S(2)}) collective-permute-start(bf16[2,2,64,512]{3,2,1,0:T(8,128)(2,1)S(1)} %slice.49), channel_id=1, source_target_pairs={{0,2},{1,5},{2,0},{3,7},{4,6},{5,1},{6,4},{7,3},{8,10},{9,13},{10,... | collective-permute-start | bytes 786440 | tf_op jit(solution)/shard_map/ppermute | solution.py:238
  46.4 3.8 %collective-permute-done.10 = bf16[1,2,64,512]{3,2,1,0:T(8,128)(2,1)S(1)} collective-permute-done((bf16[1,2,64,512]{3,2,1,0:T(8,128)(2,1)S(1)}, bf16[1,2,64,512]{3,2,1,0:T(8,128)(2,1)S(1)}, u32[]{:S(2)}, u32[]{:S(2)}) %collective-permute-start.10) | collective-permute-done | bytes 131104 | tf_op jit(solution)/shard_map/ppermute | solution.py:238
  51.4 2.3 %collective-permute-start.6 = (bf16[1,2,64,512]{3,2,1,0:T(8,128)(2,1)S(1)}, bf16[1,2,64,512]{3,2,1,0:T(8,128)(2,1)S(1)}, u32[]{:S(2)}, u32[]{:S(2)}) collective-permute-start(bf16[1,2,64,512]{3,2,1,0:T(8,128)(2,1)S(1)} %slice.51), channel_id=1, source_target_pairs={{0,8},{1,3},{2,10},{3,1},{4,12},{5,7},{6,14},{7,5},{8,0},{9,11},{1... | collective-permute-start | bytes 393224 | tf_op jit(solution)/shard_map/ppermute | solution.py:238
  53.7 1.6 %collective-permute-done.11 = bf16[1,2,64,512]{3,2,1,0:T(8,128)(2,1)S(1)} collective-permute-done((bf16[1,2,64,512]{3,2,1,0:T(8,128)(2,1)S(1)}, bf16[1,2,64,512]{3,2,1,0:T(8,128)(2,1)S(1)}, u32[]{:S(2)}, u32[]{:S(2)}) %collective-permute-start.11) | collective-permute-done | bytes 131104 | tf_op jit(solution)/shard_map/ppermute | solution.py:238
  55.4 1.4 %collective-permute-start.12 = (bf16[1,2,64,512]{3,2,1,0:T(8,128)(2,1)S(1)}, bf16[1,2,64,512]{3,2,1,0:T(8,128)(2,1)S(1)}, u32[]{:S(2)}, u32[]{:S(2)}) collective-permute-start(bf16[1,2,64,512]{3,2,1,0:T(8,128)(2,1)S(1)} %add_convert_fusion.4.refs_0_), channel_id=1, source_target_pairs={{0,8},{1,3},{2,10},{3,1},{4,12},{5,7},{6,14},{7,5},{8,0},{9,11},{1... | collective-permute-start | bytes 393224 | tf_op jit(solution)/shard_map/ppermute | solution.py:238
  56.8 1.9 %collective-permute-done.6 = bf16[1,2,64,512]{3,2,1,0:T(8,128)(2,1)S(1)} collective-permute-done((bf16[1,2,64,512]{3,2,1,0:T(8,128)(2,1)S(1)}, bf16[1,2,64,512]{3,2,1,0:T(8,128)(2,1)S(1)}, u32[]{:S(2)}, u32[]{:S(2)}) %collective-permute-start.6) | collective-permute-done | bytes 131104 | tf_op jit(solution)/shard_map/ppermute | solution.py:238
  59.0 6.3 %collective-permute-done.12.refs_1_ = bf16[1,2,64,512]{3,2,1,0:T(8,128)(2,1)S(1)} collective-permute-done((bf16[1,2,64,512]{3,2,1,0:T(8,128)(2,1)S(1)}, bf16[1,2,64,512]{3,2,1,0:T(8,128)(2,1)S(1)}, u32[]{:S(2)}, u32[]{:S(2)}) %collective-permute-start.12) | collective-permute-done | bytes 131104 | tf_op jit(solution)/shard_map/ppermute | solution.py:238
  65.3 1.6 %collective-permute-start.13 = (bf16[2,2,64,512]{3,2,1,0:T(8,128)(2,1)S(1)}, bf16[2,2,64,512]{3,2,1,0:T(8,128)(2,1)S(1)}, u32[]{:S(2)}, u32[]{:S(2)}) collective-permute-start(bf16[2,2,64,512]{3,2,1,0:T(8,128)(2,1)S(1)} %pad_maximum_fusion.1), channel_id=1, source_target_pairs={{0,2},{1,5},{2,0},{3,7},{4,6},{5,1},{6,4},{7,3},{8,10},{9,13},{10,... | collective-permute-start | bytes 786440 | tf_op jit(solution)/shard_map/ppermute | solution.py:238
  68.6 3.7 %collective-permute-done.13.refs_2_ = bf16[2,2,64,512]{3,2,1,0:T(8,128)(2,1)S(1)} collective-permute-done((bf16[2,2,64,512]{3,2,1,0:T(8,128)(2,1)S(1)}, bf16[2,2,64,512]{3,2,1,0:T(8,128)(2,1)S(1)}, u32[]{:S(2)}, u32[]{:S(2)}) %collective-permute-start.13) | collective-permute-done | bytes 262176 | tf_op jit(solution)/shard_map/ppermute | solution.py:238
  72.3 2.6 %collective-permute-done.8.refs_1_ = bf16[1,2,64,512]{3,2,1,0:T(8,128)(2,1)S(1)} collective-permute-done((bf16[1,2,64,512]{3,2,1,0:T(8,128)(2,1)S(1)}, bf16[1,2,64,512]{3,2,1,0:T(8,128)(2,1)S(1)}, u32[]{:S(2)}, u32[]{:S(2)}) %collective-permute-start.8) | collective-permute-done | bytes 131104 | tf_op jit(solution)/shard_map/ppermute | solution.py:238
  74.9 1.6 %collective-permute-start.9 = (bf16[2,2,64,512]{3,2,1,0:T(8,128)(2,1)S(1)}, bf16[2,2,64,512]{3,2,1,0:T(8,128)(2,1)S(1)}, u32[]{:S(2)}, u32[]{:S(2)}) collective-permute-start(bf16[2,2,64,512]{3,2,1,0:T(8,128)(2,1)S(1)} %pad_maximum_fusion), channel_id=1, source_target_pairs={{0,2},{1,5},{2,0},{3,7},{4,6},{5,1},{6,4},{7,3},{8,10},{9,13},{10,... | collective-permute-start | bytes 786440 | tf_op jit(solution)/shard_map/ppermute | solution.py:238
  78.0 2.0 %order_a.1 = (f32[512,512]{1,0:T(8,128)}, f32[512,512]{1,0:T(8,128)}) custom-call(s32[8]{0:T(128)S(1)} %stack.35.perm, bf16[1,2,64,512]{3,2,1,0:T(8,128)(2,1)S(1)} %add_convert_fusion.4.refs_0_, bf16[1,2,64,512]{3,2,1,0:T(8,128)(2,1)S(1)} %collective-permute-done.12.refs_1_, bf16[2,2,64,512]{3,2,1,0:T(8,128)(2,1)S(1)} %collective-permute-done.13.refs_2_, ...), custom_call_target="tpu_custom_call" | custom-call | bytes 3145728 | tf_op jit(solution)/shard_map/order_a/pallas_call | solution.py:359
  80.0 1.4 %collective-permute-done.9.refs_2_ = bf16[2,2,64,512]{3,2,1,0:T(8,128)(2,1)S(1)} collective-permute-done((bf16[2,2,64,512]{3,2,1,0:T(8,128)(2,1)S(1)}, bf16[2,2,64,512]{3,2,1,0:T(8,128)(2,1)S(1)}, u32[]{:S(2)}, u32[]{:S(2)}) %collective-permute-start.9) | collective-permute-done | bytes 262176 | tf_op jit(solution)/shard_map/ppermute | solution.py:238
  83.2 2.5 %order_b.1 = (f32[512,512]{1,0:T(8,128)}, f32[474,512]{1,0:T(8,128)}, f32[1,512]{1,0:T(1,128)}) custom-call(s32[8]{0:T(128)S(1)} %stack.35.perm, bf16[1,2,64,512]{3,2,1,0:T(8,128)(2,1)S(1)} %add_convert_fusion.6.refs_0_, bf16[1,2,64,512]{3,2,1,0:T(8,128)(2,1)S(1)} %collective-permute-done.8.refs_1_, ...), custom_call_target="tpu_custom_call" | custom-call | bytes 3145728 | tf_op jit(solution)/shard_map/order_b/pallas_call | solution.py:363
  (66 shorter events, 15.3 us)
Async XLA Ops:
  3.5 17.4 %collective-permute-start.1 = (bf16[474,512]{1,0:T(8,128)(2,1)}, bf16[474,512]{1,0:T(8,128)(2,1)S(1)}, u32[]{:S(2)}, u32[]{:S(2)}) collective-permute-start(bf16[474,512]{1,0:T(8,128)(2,1)} %pack_east.1), channel_id=1, source_target_pairs={{0,4},{4,8},{8,12},{12,0},{1,5},{5,9},{9,13},{13,1},{2,6},{6,10},{... | collective-permute-start | bytes 1456136 | tf_op jit(solution)/shard_map/ppermute | solution.py:303
  7.0 23.4 %collective-permute-start = (bf16[474,512]{1,0:T(8,128)(2,1)S(1)}, bf16[474,512]{1,0:T(8,128)(2,1)}, u32[]{:S(2)}, u32[]{:S(2)}) collective-permute-start(bf16[474,512]{1,0:T(8,128)(2,1)S(1)} %pack_west.1), channel_id=1, source_target_pairs={{4,0},{8,4},{12,8},{0,12},{5,1},{9,5},{13,9},{1,13},{6,2},{10,6},{... | collective-permute-start | bytes 1456136 | tf_op jit(solution)/shard_map/ppermute | solution.py:306
  20.3 10.1 %copy-start.3 = (bf16[512,512]{1,0:T(8,128)(2,1)S(1)}, bf16[512,512]{1,0:T(8,128)(2,1)}, u32[]{:S(2)}) copy-start(bf16[512,512]{1,0:T(8,128)(2,1)} %message_w.3) | copy-start | bytes 1572868
  20.3 10.1 %copy-start.5 = (bf16[256,512]{1,0:T(8,128)(2,1)S(1)}, bf16[256,512]{1,0:T(8,128)(2,1)}, u32[]{:S(2)}) copy-start(bf16[256,512]{1,0:T(8,128)(2,1)} %mesh_lat.3) | copy-start | bytes 786436
  20.3 10.1 %copy-start.7 = (bf16[512,512]{1,0:T(8,128)(2,1)S(1)}, bf16[512,512]{1,0:T(8,128)(2,1)}, u32[]{:S(2)}) copy-start(bf16[512,512]{1,0:T(8,128)(2,1)} %up_w.1) | copy-start | bytes 1572868
  20.3 10.1 %copy-start.9 = (f32[512]{0:T(512)S(1)}, f32[512]{0:T(512)}, u32[]{:S(2)}) copy-start(f32[512]{0:T(512)} %param.22) | copy-start | bytes 6148
  34.0 2.0 %collective-permute-start.2 = (bf16[4,2,64,512]{3,2,1,0:T(8,128)(2,1)S(1)}, bf16[4,2,64,512]{3,2,1,0:T(8,128)(2,1)S(1)}, u32[]{:S(2)}, u32[]{:S(2)}) collective-permute-start(bf16[4,2,64,512]{3,2,1,0:T(8,128)(2,1)S(1)} %slice.37), channel_id=1, source_target_pairs={{0,1},{1,0},{2,3},{3,2},{4,5},{5,4},{6,7},{7,6},{8,9},{9,8},{10,11... | collective-permute-start | bytes 1572872 | tf_op jit(solution)/shard_map/ppermute | solution.py:227
  36.2 6.4 %collective-permute-start.3 = (bf16[2,2,64,512]{3,2,1,0:T(8,128)(2,1)S(1)}, bf16[2,2,64,512]{3,2,1,0:T(8,128)(2,1)S(1)}, u32[]{:S(2)}, u32[]{:S(2)}) collective-permute-start(bf16[2,2,64,512]{3,2,1,0:T(8,128)(2,1)S(1)} %slice.39), channel_id=1, source_target_pairs={{0,2},{1,5},{2,0},{3,7},{4,6},{5,1},{6,4},{7,3},{8,10},{9,13},{10,... | collective-permute-start | bytes 786440 | tf_op jit(solution)/shard_map/ppermute | solution.py:238
  42.7 2.0 %collective-permute-start.4 = (bf16[4,2,64,512]{3,2,1,0:T(8,128)(2,1)S(1)}, bf16[4,2,64,512]{3,2,1,0:T(8,128)(2,1)S(1)}, u32[]{:S(2)}, u32[]{:S(2)}) collective-permute-start(bf16[4,2,64,512]{3,2,1,0:T(8,128)(2,1)S(1)} %slice.41), channel_id=1, source_target_pairs={{0,1},{1,0},{2,3},{3,2},{4,5},{5,4},{6,7},{7,6},{8,9},{9,8},{10,11... | collective-permute-start | bytes 1572872 | tf_op jit(solution)/shard_map/ppermute | solution.py:227
  42.8 7.4 %collective-permute-start.10 = (bf16[1,2,64,512]{3,2,1,0:T(8,128)(2,1)S(1)}, bf16[1,2,64,512]{3,2,1,0:T(8,128)(2,1)S(1)}, u32[]{:S(2)}, u32[]{:S(2)}) collective-permute-start(bf16[1,2,64,512]{3,2,1,0:T(8,128)(2,1)S(1)} %slice.47), channel_id=1, source_target_pairs={{0,8},{1,3},{2,10},{3,1},{4,12},{5,7},{6,14},{7,5},{8,0},{9,11},{1... | collective-permute-start | bytes 393224 | tf_op jit(solution)/shard_map/ppermute | solution.py:238
  44.9 6.4 %collective-permute-start.5 = (bf16[2,2,64,512]{3,2,1,0:T(8,128)(2,1)S(1)}, bf16[2,2,64,512]{3,2,1,0:T(8,128)(2,1)S(1)}, u32[]{:S(2)}, u32[]{:S(2)}) collective-permute-start(bf16[2,2,64,512]{3,2,1,0:T(8,128)(2,1)S(1)} %slice.49), channel_id=1, source_target_pairs={{0,2},{1,5},{2,0},{3,7},{4,6},{5,1},{6,4},{7,3},{8,10},{9,13},{10,... | collective-permute-start | bytes 786440 | tf_op jit(solution)/shard_map/ppermute | solution.py:238
  50.3 5.0 %collective-permute-start.11 = (bf16[1,2,64,512]{3,2,1,0:T(8,128)(2,1)S(1)}, bf16[1,2,64,512]{3,2,1,0:T(8,128)(2,1)S(1)}, u32[]{:S(2)}, u32[]{:S(2)}) collective-permute-start(bf16[1,2,64,512]{3,2,1,0:T(8,128)(2,1)S(1)} %add_convert_fusion.5), channel_id=1, source_target_pairs={{0,4},{1,9},{2,6},{3,11},{4,0},{5,13},{6,2},{7,15},{8,12},{9,1},{1... | collective-permute-start | bytes 393224 | tf_op jit(solution)/shard_map/ppermute | solution.py:238
  51.4 7.3 %collective-permute-start.6 = (bf16[1,2,64,512]{3,2,1,0:T(8,128)(2,1)S(1)}, bf16[1,2,64,512]{3,2,1,0:T(8,128)(2,1)S(1)}, u32[]{:S(2)}, u32[]{:S(2)}) collective-permute-start(bf16[1,2,64,512]{3,2,1,0:T(8,128)(2,1)S(1)} %slice.51), channel_id=1, source_target_pairs={{0,8},{1,3},{2,10},{3,1},{4,12},{5,7},{6,14},{7,5},{8,0},{9,11},{1... | collective-permute-start | bytes 393224 | tf_op jit(solution)/shard_map/ppermute | solution.py:238
  55.4 10.0 %collective-permute-start.12 = (bf16[1,2,64,512]{3,2,1,0:T(8,128)(2,1)S(1)}, bf16[1,2,64,512]{3,2,1,0:T(8,128)(2,1)S(1)}, u32[]{:S(2)}, u32[]{:S(2)}) collective-permute-start(bf16[1,2,64,512]{3,2,1,0:T(8,128)(2,1)S(1)} %add_convert_fusion.4.refs_0_), channel_id=1, source_target_pairs={{0,8},{1,3},{2,10},{3,1},{4,12},{5,7},{6,14},{7,5},{8,0},{9,11},{1... | collective-permute-start | bytes 393224 | tf_op jit(solution)/shard_map/ppermute | solution.py:238
  58.8 8.9 %collective-permute-start.7 = (bf16[1,2,64,512]{3,2,1,0:T(8,128)(2,1)S(1)}, bf16[1,2,64,512]{3,2,1,0:T(8,128)(2,1)S(1)}, u32[]{:S(2)}, u32[]{:S(2)}) collective-permute-start(bf16[1,2,64,512]{3,2,1,0:T(8,128)(2,1)S(1)} %add_convert_fusion.7), channel_id=1, source_target_pairs={{0,4},{1,9},{2,6},{3,11},{4,0},{5,13},{6,2},{7,15},{8,12},{9,1},{1... | collective-permute-start | bytes 393224 | tf_op jit(solution)/shard_map/ppermute | solution.py:238
  65.3 6.9 %collective-permute-start.13 = (bf16[2,2,64,512]{3,2,1,0:T(8,128)(2,1)S(1)}, bf16[2,2,64,512]{3,2,1,0:T(8,128)(2,1)S(1)}, u32[]{:S(2)}, u32[]{:S(2)}) collective-permute-start(bf16[2,2,64,512]{3,2,1,0:T(8,128)(2,1)S(1)} %pad_maximum_fusion.1), channel_id=1, source_target_pairs={{0,2},{1,5},{2,0},{3,7},{4,6},{5,1},{6,4},{7,3},{8,10},{9,13},{10,... | collective-permute-start | bytes 786440 | tf_op jit(solution)/shard_map/ppermute | solution.py:238
  67.7 7.2 %collective-permute-start.8 = (bf16[1,2,64,512]{3,2,1,0:T(8,128)(2,1)S(1)}, bf16[1,2,64,512]{3,2,1,0:T(8,128)(2,1)S(1)}, u32[]{:S(2)}, u32[]{:S(2)}) collective-permute-start(bf16[1,2,64,512]{3,2,1,0:T(8,128)(2,1)S(1)} %add_convert_fusion.6.refs_0_), channel_id=1, source_target_pairs={{0,8},{1,3},{2,10},{3,1},{4,12},{5,7},{6,14},{7,5},{8,0},{9,11},{1... | collective-permute-start | bytes 393224 | tf_op jit(solution)/shard_map/ppermute | solution.py:238
  72.3 5.7 %collective-permute-start.16 = (bf16[2,2,64,512]{3,2,1,0:T(8,128)(2,1)S(1)}, bf16[2,2,64,512]{3,2,1,0:T(8,128)(2,1)S(1)}, u32[]{:S(2)}, u32[]{:S(2)}) collective-permute-start(bf16[2,2,64,512]{3,2,1,0:T(8,128)(2,1)S(1)} %collective-permute-done.13.refs_2_), channel_id=1, source_target_pairs={{0,1},{1,0},{2,3},{3,2},{4,5},{5,4},{6,7},{7,6},{8,9},{9,8},{10,11... | collective-permute-start | bytes 786440 | tf_op jit(solution)/shard_map/ppermute | solution.py:227
  74.9 6.4 %collective-permute-start.9 = (bf16[2,2,64,512]{3,2,1,0:T(8,128)(2,1)S(1)}, bf16[2,2,64,512]{3,2,1,0:T(8,128)(2,1)S(1)}, u32[]{:S(2)}, u32[]{:S(2)}) collective-permute-start(bf16[2,2,64,512]{3,2,1,0:T(8,128)(2,1)S(1)} %pad_maximum_fusion), channel_id=1, source_target_pairs={{0,2},{1,5},{2,0},{3,7},{4,6},{5,1},{6,4},{7,3},{8,10},{9,13},{10,... | collective-permute-start | bytes 786440 | tf_op jit(solution)/shard_map/ppermute | solution.py:238
  76.4 1.3 %collective-permute-start.14 = (bf16[1,2,64,512]{3,2,1,0:T(8,128)(2,1)S(1)}, bf16[1,2,64,512]{3,2,1,0:T(8,128)(2,1)S(1)}, u32[]{:S(2)}, u32[]{:S(2)}) collective-permute-start(bf16[1,2,64,512]{3,2,1,0:T(8,128)(2,1)S(1)} %add_convert_fusion.4.refs_0_), channel_id=1, source_target_pairs={{0,1},{1,0},{2,3},{3,2},{4,5},{5,4},{6,7},{7,6},{8,9},{9,8},{10,11... | collective-permute-start | bytes 393224 | tf_op jit(solution)/shard_map/ppermute | solution.py:227
  76.4 1.5 %collective-permute-start.15 = (bf16[1,2,64,512]{3,2,1,0:T(8,128)(2,1)S(1)}, bf16[1,2,64,512]{3,2,1,0:T(8,128)(2,1)S(1)}, u32[]{:S(2)}, u32[]{:S(2)}) collective-permute-start(bf16[1,2,64,512]{3,2,1,0:T(8,128)(2,1)S(1)} %collective-permute-done.12.refs_1_), channel_id=1, source_target_pairs={{0,1},{1,0},{2,3},{3,2},{4,5},{5,4},{6,7},{7,6},{8,9},{9,8},{10,11... | collective-permute-start | bytes 393224 | tf_op jit(solution)/shard_map/ppermute | solution.py:227
  81.3 1.9 %collective-permute-start.19 = (bf16[2,2,64,512]{3,2,1,0:T(8,128)(2,1)S(1)}, bf16[2,2,64,512]{3,2,1,0:T(8,128)(2,1)S(1)}, u32[]{:S(2)}, u32[]{:S(2)}) collective-permute-start(bf16[2,2,64,512]{3,2,1,0:T(8,128)(2,1)S(1)} %collective-permute-done.9.refs_2_), channel_id=1, source_target_pairs={{0,1},{1,0},{2,3},{3,2},{4,5},{5,4},{6,7},{7,6},{8,9},{9,8},{10,11... | collective-permute-start | bytes 786440 | tf_op jit(solution)/shard_map/ppermute | solution.py:227
  81.3 1.7 %collective-permute-start.17 = (bf16[1,2,64,512]{3,2,1,0:T(8,128)(2,1)S(1)}, bf16[1,2,64,512]{3,2,1,0:T(8,128)(2,1)S(1)}, u32[]{:S(2)}, u32[]{:S(2)}) collective-permute-start(bf16[1,2,64,512]{3,2,1,0:T(8,128)(2,1)S(1)} %add_convert_fusion.6.refs_0_), channel_id=1, source_target_pairs={{0,1},{1,0},{2,3},{3,2},{4,5},{5,4},{6,7},{7,6},{8,9},{9,8},{10,11... | collective-permute-start | bytes 393224 | tf_op jit(solution)/shard_map/ppermute | solution.py:227
  81.8 1.4 %collective-permute-start.18 = (bf16[1,2,64,512]{3,2,1,0:T(8,128)(2,1)S(1)}, bf16[1,2,64,512]{3,2,1,0:T(8,128)(2,1)S(1)}, u32[]{:S(2)}, u32[]{:S(2)}) collective-permute-start(bf16[1,2,64,512]{3,2,1,0:T(8,128)(2,1)S(1)} %collective-permute-done.8.refs_1_), channel_id=1, source_target_pairs={{0,1},{1,0},{2,3},{3,2},{4,5},{5,4},{6,7},{7,6},{8,9},{9,8},{10,11... | collective-permute-start | bytes 393224 | tf_op jit(solution)/shard_map/ppermute | solution.py:227
  (8 other events, 35.3 us)

commit v7 on v6

--- a/solution.py
+++ b/solution.py
@@ -11,7 +11,6 @@
 MIB = 1024 * 1024
 SMEM = pl.BlockSpec(memory_space=pltpu.SMEM)
 VMEM = pl.BlockSpec(memory_space=pltpu.VMEM)
-HBM = pl.BlockSpec(memory_space=pltpu.HBM)
 shape = jax.ShapeDtypeStruct
 
 
@@ -198,29 +197,18 @@
 
 
 def order_grid_kernel(perm, *refs):
-    grad_out, grad_embed, grad_gain, held, total, sems = refs[-6:]
-    copies = []
-    chunks = [(chunk, n) for chunk in refs[:-6] for n in range(chunk.shape[0])]
-    size = held.shape[1]
-    for j, (chunk, n) in enumerate(chunks):
-        held[j] = chunk[n, 0].astype(F32)
-        at = pl.ds(pl.multiple_of(perm[j] * size, size), size)
-        copies.append(pltpu.make_async_copy(held.at[j], grad_out.at[at], sems.at[j]))
-        copies[-1].start()
-    for j, (chunk, n) in enumerate(chunks):
-        total[pl.ds(pl.multiple_of(perm[j] * size, size), size), :] = chunk[n, 1].astype(F32)
+    grad_out, grad_embed, grad_gain, total = refs[-4:]
+    from_chunks((grad_out, total), refs[:-4], perm)
     features = grad_embed.shape[0]
     grad_embed[...] = total[:features, :]
     grad_gain[...] = total[features : features + 1, :]
-    for copy in copies:
-        copy.wait()
 
 
 def role_steps():
     lat = [("lat", 2 << k) for k in range(lax.axis_size("lat").bit_length() - 2)]
     lon = [("lon", 1 << k) for k in range(lax.axis_size("lon").bit_length() - 1)]
-    rest = lat[1:] + lon[2:]
-    return ([lat[0], lon[1], lon[0]] + rest, [lon[0], lat[0], lon[1]] + rest)
+    rest = lat[1:] + lon[1:]
+    return ([lat[0], lon[0]] + rest, [lon[0], lat[0]] + rest)
 
 
 def core_swapped(value):
@@ -284,12 +272,12 @@
     points = own + 2 * side
     grid = jnp.transpose(grid_in, (2, 0, 1))
 
-    def call(kernel, name, in_specs, out_shape, flops, bytes_accessed, limit, scratch_shapes=(), out_specs=None):
+    def call(kernel, name, in_specs, out_shape, flops, bytes_accessed, limit, scratch_shapes=()):
         return pl.pallas_call(
             kernel,
             name=name,
             in_specs=in_specs,
-            out_specs=out_specs or [VMEM] * len(out_shape),
+            out_specs=[VMEM] * len(out_shape),
             out_shape=out_shape,
             scratch_shapes=list(scratch_shapes),
             compiler_params=pltpu.CompilerParams(vmem_limit_bytes=limit * MIB),
@@ -299,10 +287,10 @@
     strip = shape((features, side), BF)
     wide = pltpu.VMEM((features * rows, block), F32)
     count = lax.axis_size("lon")
-    (to_east,) = call(lambda *refs: pack_kernel(True, *refs), "pack_east", [VMEM], [strip], 0, MIB, 20, [wide])(grid)
+    (to_east,) = call(lambda *refs: pack_kernel(True, *refs), "pack_east", [VMEM], [strip], 0, MIB, 8, [wide])(grid)
     x_west = lax.ppermute(to_east, "lon", [(i, (i + 1) % count) for i in range(count)])
     to_east, later = lax.optimization_barrier((to_east, grid))
-    (to_west,) = call(lambda *refs: pack_kernel(False, *refs), "pack_west", [VMEM], [strip], 0, MIB, 20, [wide])(later)
+    (to_west,) = call(lambda *refs: pack_kernel(False, *refs), "pack_west", [VMEM], [strip], 0, MIB, 8, [wide])(later)
     x_east = lax.ppermute(to_west, "lon", [((i + 1) % count, i) for i in range(count)])
 
     weights_all, x_own, embed_t, h_own, slope_own, grad_update = call(
@@ -315,7 +303,7 @@
             shape((latent, own), BF),
             shape((nodes, latent), F32),
         ],
-        4_000_000_000, 12 * MIB, 32,
+        4_000_000_000, 12 * MIB, 24,
         [pltpu.VMEM((points // block, nodes, block), F32), pltpu.VMEM((cols // block, features * rows, block), F32)],
     )(edge_src, edge_dst, block_count, grid, embed_w, edge_w, cot, out_w)
 
@@ -363,8 +351,7 @@
     grad_out, grad_embed, grad_gain = call(
         order_grid_kernel, "order_b", [SMEM] + [VMEM] * 6,
         [square, shape((features, latent), F32), shape((1, latent), F32)], 0, 3 * MIB, 16,
-        [pltpu.VMEM((8, latent // 8, latent), F32), pltpu.VMEM((latent, latent), F32), pltpu.SemaphoreType.DMA((8,))],
-        out_specs=[HBM, VMEM, VMEM],
+        [pltpu.VMEM((latent, latent), F32)],
     )(perm, *from_both_cores((*summed_b[:2], last)))
     return (mesh_new, mesh_grad, grad_embed, grad_message, grad_up, grad_out, grad_gain[0])
 

time: 86.1 us -> 82.4 us (0.957)
  starting transfers between devices: 19.3 us -> 16.3 us
    ppermute x10, starting transfers between devices: 13 us -> 10 us  [swapped(): return lax.ppermute(value, ('lon', 'lat'), pairs)]
    ppermute x10, waiting for transfers between devices: 23.8 us -> 22.6 us  [swapped(): return lax.ppermute(value, ('lon', 'lat'), pairs)]
    ppermute x8, waiting for transfers between devices: 3.26 us -> 4.21 us  [core_swapped(): lax.ppermute(value, 'lat', [(i, i ^ 1) for i in range(lax.axis_size('lat'...]
  transfers between devices with their start and end apart: 20 -> 20, of which waited for: 18 -> 18; matrix products, arithmetic and copies ran while one was open for 1% -> 1% of each run, Pallas kernels for 18% -> 20%
where the time goes in v7:
time: 82.4 us; the launch traced here: 82 us
  waiting for transfers between devices  35.7 us (43%)
  Pallas kernels  22.9 us (28%)
  starting transfers between devices  16.3 us (20%)
  local copies, waits for them, and re-layouts  4.98 us (6%)
  between operations  1.53 us (2%)
    ppermute x10, waiting for transfers between devices, swapped(): return lax.ppermute(value, ('lon', 'lat'), pairs)  22.6 us
    ppermute x10, starting transfers between devices, swapped(): return lax.ppermute(value, ('lon', 'lat'), pairs)  10 us
    ppermute x1, waiting for transfers between devices, on_device(): lax.ppermute(to_west, 'lon', [((i + 1) % count, i) for i in range(count)])  8.68 us
    pallas_call x1, Pallas kernels, on_device(): call(own_kernel, 'own_points', [SMEM] * 3 + [VMEM] * 5, [shape((nodes, po...  7.53 us
    unnamed x24, local copies, waits for them, and re-layouts  4.77 us
    ppermute x8, waiting for transfers between devices, core_swapped(): lax.ppermute(value, 'lat', [(i, i ^ 1) for i in range(lax.axis_size('lat'...  4.21 us
    pallas_call x1, Pallas kernels, on_device(): call(grid_kernel, 'grid_points', [SMEM] + [VMEM] * 10, [shape((8, 2, late...  4.02 us
    pallas_call x1, Pallas kernels, on_device(): call(mesh_kernel, 'mesh_nodes', [SMEM] + [VMEM] * 10, [shape((8, 2, laten...  3.59 us
  transfers between devices with their start and end apart: 20, of which 18 were waited for; matrix products, arithmetic and copies ran while one was open for 1% of the time, Pallas kernels for 20%

profile of v7, /device:TPU:0, one launch (start us, length us, event | category | flops | bytes accessed | tf_op | source)
XLA Modules:
  0.0 82.0 jit_solution(13092947407296356709)
XLA Ops:
  0.6 1.5 %copy-done = bf16[8,256,474]{1,0,2:T(8,128)(2,1)S(1)} copy-done((bf16[8,256,474]{1,0,2:T(8,128)(2,1)S(1)}, bf16[8,256,474]{1,0,2:T(8,128)(2,1)}, u32[]{:S(2)}) %copy-start) | copy-done | bytes 1941528
  2.2 1.3 %pack_east.1 = bf16[474,512]{1,0:T(8,128)(2,1)} custom-call(bf16[474,8,256]{2,1,0:T(8,128)(2,1)S(1)} %bitcast.11), custom_call_target="tpu_custom_call" | custom-call | bytes 1048576 | tf_op jit(solution)/shard_map/pack_east/pallas_call | solution.py:290
  3.5 3.0 %collective-permute-start.1 = (bf16[474,512]{1,0:T(8,128)(2,1)}, bf16[474,512]{1,0:T(8,128)(2,1)S(1)}, u32[]{:S(2)}, u32[]{:S(2)}) collective-permute-start(bf16[474,512]{1,0:T(8,128)(2,1)} %pack_east.1), channel_id=1, source_target_pairs={{0,4},{4,8},{8,12},{12,0},{1,5},{5,9},{9,13},{13,1},{2,6},{6,10},{... | collective-permute-start | bytes 1456136 | tf_op jit(solution)/shard_map/ppermute | solution.py:291
  7.0 2.1 %collective-permute-start = (bf16[474,512]{1,0:T(8,128)(2,1)S(1)}, bf16[474,512]{1,0:T(8,128)(2,1)}, u32[]{:S(2)}, u32[]{:S(2)}) collective-permute-start(bf16[474,512]{1,0:T(8,128)(2,1)S(1)} %pack_west.1), channel_id=1, source_target_pairs={{4,0},{8,4},{12,8},{0,12},{5,1},{9,5},{13,9},{1,13},{6,2},{10,6},{... | collective-permute-start | bytes 1456136 | tf_op jit(solution)/shard_map/ppermute | solution.py:294
  10.8 1.2 %copy-done.6 = bf16[32,128,128]{2,1,0:T(8,128)(2,1)S(1)} copy-done((bf16[32,128,128]{2,1,0:T(8,128)(2,1)S(1)}, bf16[32,128,128]{2,1,0:T(8,128)(2,1)}, u32[]{:S(2)}) %copy-start.6) | copy-done | bytes 1048600
  13.1 7.5 %own_points.1 = (bf16[256,3072]{1,0:T(8,128)(2,1)S(1)}, bf16[474,2048]{1,0:T(8,128)(2,1)S(1)}, bf16[512,474]{1,0:T(8,128)(2,1)S(1)}, f32[256,512]{1,0:T(8,128)S(...) custom-call(s32[32]{0:T(128)S(1)} %copy-done.10, s32[32]{0:T(128)S(1)} %copy-done.11, s32[1]{0:T(128)S(6)} %copy.19.count, ...), custom_call_target="tpu_custom_call" | custom-call | flops 4000000000 | bytes 12582912 | tf_op jit(solution)/shard_map/own_points/pallas_call | solution.py:296
  21.7 8.7 %collective-permute-done.x.x_east = bf16[474,512]{1,0:T(8,128)(2,1)} collective-permute-done((bf16[474,512]{1,0:T(8,128)(2,1)S(1)}, bf16[474,512]{1,0:T(8,128)(2,1)}, u32[]{:S(2)}, u32[]{:S(2)}) %collective-permute-start) | collective-permute-done | bytes 485408 | tf_op jit(solution)/shard_map/ppermute | solution.py:294
  30.4 3.6 %mesh_nodes.1 = (bf16[8,2,64,512]{3,2,1,0:T(8,128)(2,1)S(1)}, f32[256,512]{1,0:T(8,128)}, f32[1,512]{1,0:T(1,128)S(1)}, bf16[256,512]{1,0:T(8,128)(2,1)S(1)}, bf...) custom-call(s32[8]{0:T(128)S(1)} %stack.35.perm, bf16[474,512]{1,0:T(8,128)(2,1)} %collective-permute-done.x.x_east, ...), custom_call_target="tpu_custom_call" | custom-call | flops 2000000000 | bytes 8388608 | tf_op jit(solution)/shard_map/mesh_nodes/pallas_call | solution.py:317
  36.2 1.6 %collective-permute-start.3 = (bf16[2,2,64,512]{3,2,1,0:T(8,128)(2,1)S(1)}, bf16[2,2,64,512]{3,2,1,0:T(8,128)(2,1)S(1)}, u32[]{:S(2)}, u32[]{:S(2)}) collective-permute-start(bf16[2,2,64,512]{3,2,1,0:T(8,128)(2,1)S(1)} %slice.39), channel_id=1, source_target_pairs={{0,2},{1,5},{2,0},{3,7},{4,6},{5,1},{6,4},{7,3},{8,10},{9,13},{10,... | collective-permute-start | bytes 786440 | tf_op jit(solution)/shard_map/ppermute | solution.py:226
  37.7 4.0 %grid_points.1 = bf16[8,2,64,512]{3,2,1,0:T(8,128)(2,1)S(1)} custom-call(s32[8]{0:T(128)S(1)} %stack.35.perm, bf16[512,256]{1,0:T(8,128)(2,1)S(1)} %get-tuple-element.50.back, bf16[256,3072]{1,0:T(8,128)(2,1)S(1)} %get-tuple-element.39.refs_2_.weights_all, bf16[512,2048]{1,0:T(8,128)(2,1)S(1)} %get-tuple-element.51.slope_own, ...), custom_call_target="tpu_custom_call" | custom-call | flops 2400000000 | bytes 9437184 | tf_op jit(solution)/shard_map/grid_points/pallas_call | solution.py:338
  44.9 1.6 %collective-permute-start.5 = (bf16[2,2,64,512]{3,2,1,0:T(8,128)(2,1)S(1)}, bf16[2,2,64,512]{3,2,1,0:T(8,128)(2,1)S(1)}, u32[]{:S(2)}, u32[]{:S(2)}) collective-permute-start(bf16[2,2,64,512]{3,2,1,0:T(8,128)(2,1)S(1)} %slice.49), channel_id=1, source_target_pairs={{0,2},{1,5},{2,0},{3,7},{4,6},{5,1},{6,4},{7,3},{8,10},{9,13},{10,... | collective-permute-start | bytes 786440 | tf_op jit(solution)/shard_map/ppermute | solution.py:226
  46.4 1.6 %collective-permute-done.10 = bf16[1,2,64,512]{3,2,1,0:T(8,128)(2,1)S(1)} collective-permute-done((bf16[1,2,64,512]{3,2,1,0:T(8,128)(2,1)S(1)}, bf16[1,2,64,512]{3,2,1,0:T(8,128)(2,1)S(1)}, u32[]{:S(2)}, u32[]{:S(2)}) %collective-permute-start.10) | collective-permute-done | bytes 131104 | tf_op jit(solution)/shard_map/ppermute | solution.py:226
  48.0 1.8 %collective-permute-start.11 = (bf16[1,2,64,512]{3,2,1,0:T(8,128)(2,1)S(1)}, bf16[1,2,64,512]{3,2,1,0:T(8,128)(2,1)S(1)}, u32[]{:S(2)}, u32[]{:S(2)}) collective-permute-start(bf16[1,2,64,512]{3,2,1,0:T(8,128)(2,1)S(1)} %add_convert_fusion.5), channel_id=1, source_target_pairs={{0,8},{1,9},{2,10},{3,11},{4,12},{5,13},{6,14},{7,15},{8,0},{9,1},... | collective-permute-start | bytes 393224 | tf_op jit(solution)/shard_map/ppermute | solution.py:226
  49.8 1.5 %collective-permute-done.5 = bf16[2,2,64,512]{3,2,1,0:T(8,128)(2,1)S(1)} collective-permute-done((bf16[2,2,64,512]{3,2,1,0:T(8,128)(2,1)S(1)}, bf16[2,2,64,512]{3,2,1,0:T(8,128)(2,1)S(1)}, u32[]{:S(2)}, u32[]{:S(2)}) %collective-permute-start.5) | collective-permute-done | bytes 262176 | tf_op jit(solution)/shard_map/ppermute | solution.py:226
  52.3 4.6 %collective-permute-done.11 = bf16[1,2,64,512]{3,2,1,0:T(8,128)(2,1)S(1)} collective-permute-done((bf16[1,2,64,512]{3,2,1,0:T(8,128)(2,1)S(1)}, bf16[1,2,64,512]{3,2,1,0:T(8,128)(2,1)S(1)}, u32[]{:S(2)}, u32[]{:S(2)}) %collective-permute-start.11) | collective-permute-done | bytes 131104 | tf_op jit(solution)/shard_map/ppermute | solution.py:226
  56.9 1.2 %collective-permute-done.6 = bf16[1,2,64,512]{3,2,1,0:T(8,128)(2,1)S(1)} collective-permute-done((bf16[1,2,64,512]{3,2,1,0:T(8,128)(2,1)S(1)}, bf16[1,2,64,512]{3,2,1,0:T(8,128)(2,1)S(1)}, u32[]{:S(2)}, u32[]{:S(2)}) %collective-permute-start.6) | collective-permute-done | bytes 131104 | tf_op jit(solution)/shard_map/ppermute | solution.py:226
  58.1 2.1 %collective-permute-start.7 = (bf16[1,2,64,512]{3,2,1,0:T(8,128)(2,1)S(1)}, bf16[1,2,64,512]{3,2,1,0:T(8,128)(2,1)S(1)}, u32[]{:S(2)}, u32[]{:S(2)}) collective-permute-start(bf16[1,2,64,512]{3,2,1,0:T(8,128)(2,1)S(1)} %add_convert_fusion.7), channel_id=1, source_target_pairs={{0,8},{1,9},{2,10},{3,11},{4,12},{5,13},{6,14},{7,15},{8,0},{9,1},... | collective-permute-start | bytes 393224 | tf_op jit(solution)/shard_map/ppermute | solution.py:226
  60.2 3.8 %collective-permute-done.12.refs_1_ = bf16[1,2,64,512]{3,2,1,0:T(8,128)(2,1)S(1)} collective-permute-done((bf16[1,2,64,512]{3,2,1,0:T(8,128)(2,1)S(1)}, bf16[1,2,64,512]{3,2,1,0:T(8,128)(2,1)S(1)}, u32[]{:S(2)}, u32[]{:S(2)}) %collective-permute-start.12) | collective-permute-done | bytes 131104 | tf_op jit(solution)/shard_map/ppermute | solution.py:226
  64.4 2.2 %collective-permute-done.7 = bf16[1,2,64,512]{3,2,1,0:T(8,128)(2,1)S(1)} collective-permute-done((bf16[1,2,64,512]{3,2,1,0:T(8,128)(2,1)S(1)}, bf16[1,2,64,512]{3,2,1,0:T(8,128)(2,1)S(1)}, u32[]{:S(2)}, u32[]{:S(2)}) %collective-permute-start.7) | collective-permute-done | bytes 131104 | tf_op jit(solution)/shard_map/ppermute | solution.py:226
  66.7 3.8 %collective-permute-done.13.refs_2_ = bf16[2,2,64,512]{3,2,1,0:T(8,128)(2,1)S(1)} collective-permute-done((bf16[2,2,64,512]{3,2,1,0:T(8,128)(2,1)S(1)}, bf16[2,2,64,512]{3,2,1,0:T(8,128)(2,1)S(1)}, u32[]{:S(2)}, u32[]{:S(2)}) %collective-permute-start.13) | collective-permute-done | bytes 262176 | tf_op jit(solution)/shard_map/ppermute | solution.py:226
  74.0 2.0 %order_a.1 = (f32[512,512]{1,0:T(8,128)}, f32[512,512]{1,0:T(8,128)}) custom-call(s32[8]{0:T(128)S(1)} %stack.35.perm, bf16[1,2,64,512]{3,2,1,0:T(8,128)(2,1)S(1)} %add_convert_fusion.4.refs_0_, bf16[1,2,64,512]{3,2,1,0:T(8,128)(2,1)S(1)} %collective-permute-done.12.refs_1_, bf16[2,2,64,512]{3,2,1,0:T(8,128)(2,1)S(1)} %collective-permute-done.13.refs_2_, ...), custom_call_target="tpu_custom_call" | custom-call | bytes 3145728 | tf_op jit(solution)/shard_map/order_a/pallas_call | solution.py:347
  76.0 2.1 %collective-permute-done.9.refs_2_ = bf16[2,2,64,512]{3,2,1,0:T(8,128)(2,1)S(1)} collective-permute-done((bf16[2,2,64,512]{3,2,1,0:T(8,128)(2,1)S(1)}, bf16[2,2,64,512]{3,2,1,0:T(8,128)(2,1)S(1)}, u32[]{:S(2)}, u32[]{:S(2)}) %collective-permute-start.9) | collective-permute-done | bytes 262176 | tf_op jit(solution)/shard_map/ppermute | solution.py:226
  78.6 1.2 %collective-permute-done.17.refs_3_ = bf16[1,2,64,512]{3,2,1,0:T(8,128)(2,1)S(1)} collective-permute-done((bf16[1,2,64,512]{3,2,1,0:T(8,128)(2,1)S(1)}, bf16[1,2,64,512]{3,2,1,0:T(8,128)(2,1)S(1)}, u32[]{:S(2)}, u32[]{:S(2)}) %collective-permute-start.17) | collective-permute-done | bytes 131104 | tf_op jit(solution)/shard_map/ppermute | solution.py:215
  80.0 2.0 %order_b.1 = (f32[512,512]{1,0:T(8,128)}, f32[474,512]{1,0:T(8,128)}, f32[1,512]{1,0:T(1,128)}) custom-call(s32[8]{0:T(128)S(1)} %stack.35.perm, bf16[1,2,64,512]{3,2,1,0:T(8,128)(2,1)S(1)} %add_convert_fusion.6.refs_0_, bf16[1,2,64,512]{3,2,1,0:T(8,128)(2,1)S(1)} %collective-permute-done.8.refs_1_, ...), custom_call_target="tpu_custom_call" | custom-call | bytes 3145728 | tf_op jit(solution)/shard_map/order_b/pallas_call | solution.py:351
  (66 shorter events, 14.7 us)
Async XLA Ops:
  3.5 17.4 %collective-permute-start.1 = (bf16[474,512]{1,0:T(8,128)(2,1)}, bf16[474,512]{1,0:T(8,128)(2,1)S(1)}, u32[]{:S(2)}, u32[]{:S(2)}) collective-permute-start(bf16[474,512]{1,0:T(8,128)(2,1)} %pack_east.1), channel_id=1, source_target_pairs={{0,4},{4,8},{8,12},{12,0},{1,5},{5,9},{9,13},{13,1},{2,6},{6,10},{... | collective-permute-start | bytes 1456136 | tf_op jit(solution)/shard_map/ppermute | solution.py:291
  7.0 23.4 %collective-permute-start = (bf16[474,512]{1,0:T(8,128)(2,1)S(1)}, bf16[474,512]{1,0:T(8,128)(2,1)}, u32[]{:S(2)}, u32[]{:S(2)}) collective-permute-start(bf16[474,512]{1,0:T(8,128)(2,1)S(1)} %pack_west.1), channel_id=1, source_target_pairs={{4,0},{8,4},{12,8},{0,12},{5,1},{9,5},{13,9},{1,13},{6,2},{10,6},{... | collective-permute-start | bytes 1456136 | tf_op jit(solution)/shard_map/ppermute | solution.py:294
  20.6 9.8 %copy-start.3 = (bf16[512,512]{1,0:T(8,128)(2,1)S(1)}, bf16[512,512]{1,0:T(8,128)(2,1)}, u32[]{:S(2)}) copy-start(bf16[512,512]{1,0:T(8,128)(2,1)} %message_w.3) | copy-start | bytes 1572868
  20.6 9.8 %copy-start.5 = (bf16[256,512]{1,0:T(8,128)(2,1)S(1)}, bf16[256,512]{1,0:T(8,128)(2,1)}, u32[]{:S(2)}) copy-start(bf16[256,512]{1,0:T(8,128)(2,1)} %mesh_lat.3) | copy-start | bytes 786436
  20.6 9.8 %copy-start.7 = (bf16[512,512]{1,0:T(8,128)(2,1)S(1)}, bf16[512,512]{1,0:T(8,128)(2,1)}, u32[]{:S(2)}) copy-start(bf16[512,512]{1,0:T(8,128)(2,1)} %up_w.1) | copy-start | bytes 1572868
  20.6 9.8 %copy-start.9 = (f32[512]{0:T(512)S(1)}, f32[512]{0:T(512)}, u32[]{:S(2)}) copy-start(f32[512]{0:T(512)} %param.22) | copy-start | bytes 6148
  34.0 2.0 %collective-permute-start.2 = (bf16[4,2,64,512]{3,2,1,0:T(8,128)(2,1)S(1)}, bf16[4,2,64,512]{3,2,1,0:T(8,128)(2,1)S(1)}, u32[]{:S(2)}, u32[]{:S(2)}) collective-permute-start(bf16[4,2,64,512]{3,2,1,0:T(8,128)(2,1)S(1)} %slice.37), channel_id=1, source_target_pairs={{0,1},{1,0},{2,3},{3,2},{4,5},{5,4},{6,7},{7,6},{8,9},{9,8},{10,11... | collective-permute-start | bytes 1572872 | tf_op jit(solution)/shard_map/ppermute | solution.py:215
  36.2 6.4 %collective-permute-start.3 = (bf16[2,2,64,512]{3,2,1,0:T(8,128)(2,1)S(1)}, bf16[2,2,64,512]{3,2,1,0:T(8,128)(2,1)S(1)}, u32[]{:S(2)}, u32[]{:S(2)}) collective-permute-start(bf16[2,2,64,512]{3,2,1,0:T(8,128)(2,1)S(1)} %slice.39), channel_id=1, source_target_pairs={{0,2},{1,5},{2,0},{3,7},{4,6},{5,1},{6,4},{7,3},{8,10},{9,13},{10,... | collective-permute-start | bytes 786440 | tf_op jit(solution)/shard_map/ppermute | solution.py:226
  42.7 2.0 %collective-permute-start.4 = (bf16[4,2,64,512]{3,2,1,0:T(8,128)(2,1)S(1)}, bf16[4,2,64,512]{3,2,1,0:T(8,128)(2,1)S(1)}, u32[]{:S(2)}, u32[]{:S(2)}) collective-permute-start(bf16[4,2,64,512]{3,2,1,0:T(8,128)(2,1)S(1)} %slice.41), channel_id=1, source_target_pairs={{0,1},{1,0},{2,3},{3,2},{4,5},{5,4},{6,7},{7,6},{8,9},{9,8},{10,11... | collective-permute-start | bytes 1572872 | tf_op jit(solution)/shard_map/ppermute | solution.py:215
  42.8 5.2 %collective-permute-start.10 = (bf16[1,2,64,512]{3,2,1,0:T(8,128)(2,1)S(1)}, bf16[1,2,64,512]{3,2,1,0:T(8,128)(2,1)S(1)}, u32[]{:S(2)}, u32[]{:S(2)}) collective-permute-start(bf16[1,2,64,512]{3,2,1,0:T(8,128)(2,1)S(1)} %slice.47), channel_id=1, source_target_pairs={{0,4},{1,3},{2,6},{3,1},{4,0},{5,7},{6,2},{7,5},{8,12},{9,11},{10,... | collective-permute-start | bytes 393224 | tf_op jit(solution)/shard_map/ppermute | solution.py:226
  44.9 6.4 %collective-permute-start.5 = (bf16[2,2,64,512]{3,2,1,0:T(8,128)(2,1)S(1)}, bf16[2,2,64,512]{3,2,1,0:T(8,128)(2,1)S(1)}, u32[]{:S(2)}, u32[]{:S(2)}) collective-permute-start(bf16[2,2,64,512]{3,2,1,0:T(8,128)(2,1)S(1)} %slice.49), channel_id=1, source_target_pairs={{0,2},{1,5},{2,0},{3,7},{4,6},{5,1},{6,4},{7,3},{8,10},{9,13},{10,... | collective-permute-start | bytes 786440 | tf_op jit(solution)/shard_map/ppermute | solution.py:226
  48.0 8.8 %collective-permute-start.11 = (bf16[1,2,64,512]{3,2,1,0:T(8,128)(2,1)S(1)}, bf16[1,2,64,512]{3,2,1,0:T(8,128)(2,1)S(1)}, u32[]{:S(2)}, u32[]{:S(2)}) collective-permute-start(bf16[1,2,64,512]{3,2,1,0:T(8,128)(2,1)S(1)} %add_convert_fusion.5), channel_id=1, source_target_pairs={{0,8},{1,9},{2,10},{3,11},{4,12},{5,13},{6,14},{7,15},{8,0},{9,1},... | collective-permute-start | bytes 393224 | tf_op jit(solution)/shard_map/ppermute | solution.py:226
  51.4 6.7 %collective-permute-start.6 = (bf16[1,2,64,512]{3,2,1,0:T(8,128)(2,1)S(1)}, bf16[1,2,64,512]{3,2,1,0:T(8,128)(2,1)S(1)}, u32[]{:S(2)}, u32[]{:S(2)}) collective-permute-start(bf16[1,2,64,512]{3,2,1,0:T(8,128)(2,1)S(1)} %slice.51), channel_id=1, source_target_pairs={{0,4},{1,3},{2,6},{3,1},{4,0},{5,7},{6,2},{7,5},{8,12},{9,11},{10,... | collective-permute-start | bytes 393224 | tf_op jit(solution)/shard_map/ppermute | solution.py:226
  56.8 7.2 %collective-permute-start.12 = (bf16[1,2,64,512]{3,2,1,0:T(8,128)(2,1)S(1)}, bf16[1,2,64,512]{3,2,1,0:T(8,128)(2,1)S(1)}, u32[]{:S(2)}, u32[]{:S(2)}) collective-permute-start(bf16[1,2,64,512]{3,2,1,0:T(8,128)(2,1)S(1)} %add_convert_fusion.4.refs_0_), channel_id=1, source_target_pairs={{0,4},{1,3},{2,6},{3,1},{4,0},{5,7},{6,2},{7,5},{8,12},{9,11},{10,... | collective-permute-start | bytes 393224 | tf_op jit(solution)/shard_map/ppermute | solution.py:226
  58.1 8.4 %collective-permute-start.7 = (bf16[1,2,64,512]{3,2,1,0:T(8,128)(2,1)S(1)}, bf16[1,2,64,512]{3,2,1,0:T(8,128)(2,1)S(1)}, u32[]{:S(2)}, u32[]{:S(2)}) collective-permute-start(bf16[1,2,64,512]{3,2,1,0:T(8,128)(2,1)S(1)} %add_convert_fusion.7), channel_id=1, source_target_pairs={{0,8},{1,9},{2,10},{3,11},{4,12},{5,13},{6,14},{7,15},{8,0},{9,1},... | collective-permute-start | bytes 393224 | tf_op jit(solution)/shard_map/ppermute | solution.py:226
  64.1 6.4 %collective-permute-start.13 = (bf16[2,2,64,512]{3,2,1,0:T(8,128)(2,1)S(1)}, bf16[2,2,64,512]{3,2,1,0:T(8,128)(2,1)S(1)}, u32[]{:S(2)}, u32[]{:S(2)}) collective-permute-start(bf16[2,2,64,512]{3,2,1,0:T(8,128)(2,1)S(1)} %pad_maximum_fusion.1), channel_id=1, source_target_pairs={{0,2},{1,5},{2,0},{3,7},{4,6},{5,1},{6,4},{7,3},{8,10},{9,13},{10,... | collective-permute-start | bytes 786440 | tf_op jit(solution)/shard_map/ppermute | solution.py:226
  66.6 5.0 %collective-permute-start.8 = (bf16[1,2,64,512]{3,2,1,0:T(8,128)(2,1)S(1)}, bf16[1,2,64,512]{3,2,1,0:T(8,128)(2,1)S(1)}, u32[]{:S(2)}, u32[]{:S(2)}) collective-permute-start(bf16[1,2,64,512]{3,2,1,0:T(8,128)(2,1)S(1)} %add_convert_fusion.6.refs_0_), channel_id=1, source_target_pairs={{0,4},{1,3},{2,6},{3,1},{4,0},{5,7},{6,2},{7,5},{8,12},{9,11},{10,... | collective-permute-start | bytes 393224 | tf_op jit(solution)/shard_map/ppermute | solution.py:226
  70.5 3.5 %collective-permute-start.16 = (bf16[2,2,64,512]{3,2,1,0:T(8,128)(2,1)S(1)}, bf16[2,2,64,512]{3,2,1,0:T(8,128)(2,1)S(1)}, u32[]{:S(2)}, u32[]{:S(2)}) collective-permute-start(bf16[2,2,64,512]{3,2,1,0:T(8,128)(2,1)S(1)} %collective-permute-done.13.refs_2_), channel_id=1, source_target_pairs={{0,1},{1,0},{2,3},{3,2},{4,5},{5,4},{6,7},{7,6},{8,9},{9,8},{10,11... | collective-permute-start | bytes 786440 | tf_op jit(solution)/shard_map/ppermute | solution.py:215
  71.7 6.4 %collective-permute-start.9 = (bf16[2,2,64,512]{3,2,1,0:T(8,128)(2,1)S(1)}, bf16[2,2,64,512]{3,2,1,0:T(8,128)(2,1)S(1)}, u32[]{:S(2)}, u32[]{:S(2)}) collective-permute-start(bf16[2,2,64,512]{3,2,1,0:T(8,128)(2,1)S(1)} %pad_maximum_fusion), channel_id=1, source_target_pairs={{0,2},{1,5},{2,0},{3,7},{4,6},{5,1},{6,4},{7,3},{8,10},{9,13},{10,... | collective-permute-start | bytes 786440 | tf_op jit(solution)/shard_map/ppermute | solution.py:226
  72.5 1.3 %collective-permute-start.14 = (bf16[1,2,64,512]{3,2,1,0:T(8,128)(2,1)S(1)}, bf16[1,2,64,512]{3,2,1,0:T(8,128)(2,1)S(1)}, u32[]{:S(2)}, u32[]{:S(2)}) collective-permute-start(bf16[1,2,64,512]{3,2,1,0:T(8,128)(2,1)S(1)} %add_convert_fusion.4.refs_0_), channel_id=1, source_target_pairs={{0,1},{1,0},{2,3},{3,2},{4,5},{5,4},{6,7},{7,6},{8,9},{9,8},{10,11... | collective-permute-start | bytes 393224 | tf_op jit(solution)/shard_map/ppermute | solution.py:215
  72.5 1.5 %collective-permute-start.15 = (bf16[1,2,64,512]{3,2,1,0:T(8,128)(2,1)S(1)}, bf16[1,2,64,512]{3,2,1,0:T(8,128)(2,1)S(1)}, u32[]{:S(2)}, u32[]{:S(2)}) collective-permute-start(bf16[1,2,64,512]{3,2,1,0:T(8,128)(2,1)S(1)} %collective-permute-done.12.refs_1_), channel_id=1, source_target_pairs={{0,1},{1,0},{2,3},{3,2},{4,5},{5,4},{6,7},{7,6},{8,9},{9,8},{10,11... | collective-permute-start | bytes 393224 | tf_op jit(solution)/shard_map/ppermute | solution.py:215
  78.1 1.9 %collective-permute-start.19 = (bf16[2,2,64,512]{3,2,1,0:T(8,128)(2,1)S(1)}, bf16[2,2,64,512]{3,2,1,0:T(8,128)(2,1)S(1)}, u32[]{:S(2)}, u32[]{:S(2)}) collective-permute-start(bf16[2,2,64,512]{3,2,1,0:T(8,128)(2,1)S(1)} %collective-permute-done.9.refs_2_), channel_id=1, source_target_pairs={{0,1},{1,0},{2,3},{3,2},{4,5},{5,4},{6,7},{7,6},{8,9},{9,8},{10,11... | collective-permute-start | bytes 786440 | tf_op jit(solution)/shard_map/ppermute | solution.py:215
  78.1 1.7 %collective-permute-start.17 = (bf16[1,2,64,512]{3,2,1,0:T(8,128)(2,1)S(1)}, bf16[1,2,64,512]{3,2,1,0:T(8,128)(2,1)S(1)}, u32[]{:S(2)}, u32[]{:S(2)}) collective-permute-start(bf16[1,2,64,512]{3,2,1,0:T(8,128)(2,1)S(1)} %add_convert_fusion.6.refs_0_), channel_id=1, source_target_pairs={{0,1},{1,0},{2,3},{3,2},{4,5},{5,4},{6,7},{7,6},{8,9},{9,8},{10,11... | collective-permute-start | bytes 393224 | tf_op jit(solution)/shard_map/ppermute | solution.py:215
  78.6 1.4 %collective-permute-start.18 = (bf16[1,2,64,512]{3,2,1,0:T(8,128)(2,1)S(1)}, bf16[1,2,64,512]{3,2,1,0:T(8,128)(2,1)S(1)}, u32[]{:S(2)}, u32[]{:S(2)}) collective-permute-start(bf16[1,2,64,512]{3,2,1,0:T(8,128)(2,1)S(1)} %collective-permute-done.8.refs_1_), channel_id=1, source_target_pairs={{0,1},{1,0},{2,3},{3,2},{4,5},{5,4},{6,7},{7,6},{8,9},{9,8},{10,11... | collective-permute-start | bytes 393224 | tf_op jit(solution)/shard_map/ppermute | solution.py:215
  (8 other events, 35.3 us)

commit v8 on v7

--- a/solution.py
+++ b/solution.py
@@ -114,12 +114,12 @@
     h_sum[...] = h_own[...] + halo_part(x, embed_t, weights_all[:, first : first + points], slope)
 
 
-def to_chunks(grads, stack, perm):
+def to_chunks(grads, stack, perm, start):
     count, matrices, size, _ = grads.shape
     for j in range(count):
-        at = pl.ds(pl.multiple_of(perm[j] * size, size), size)
+        at = pl.ds(pl.multiple_of((perm[start + j] & (count - 1)) * size, size), size)
         for k in range(matrices):
-            grads[j, k] = stack[k, at, :]
+            grads[j, k] = stack[k, at, :].astype(BF)
 
 
 def from_chunks(outs, chunks, perm):
@@ -133,63 +133,95 @@
             j += 1
 
 
+def rows_of_half(half, rows):
+    return pl.ds(pl.multiple_of(half * rows, rows), rows)
+
+
 def mesh_kernel(
     perm, x, embed_t, weights_all, h_sum, message_w, up_w, gain, mesh_lat, cot, grad_update,
-    grads, mesh_grad, grad_gain, grad_aggregate, update, slope, stack,
+    sent, mesh_grad, grad_gain, gathered, grad_aggregate, normed, grad_pre_up, update, slope, stack,
 ):
     points = x.shape[1]
     first = weights_all.shape[1] - points
     total = h_sum[...] + halo_part(x, embed_t, weights_all[:, first:], slope)
-    gathered = total.astype(BF)
-    summed = mesh_lat[...].astype(F32) + contract(gathered, message_w[...], 1, 0)
+    gathered[...] = total.astype(BF)
+    summed = mesh_lat[...].astype(F32) + contract(gathered[...], message_w[...], 1, 0)
     rinv = lax.rsqrt(jnp.mean(summed * summed, axis=1, keepdims=True) + epsilon)
     qhat = summed * rinv
     gains = gain[...]
-    normed = (qhat * gains).astype(BF)
-    pre_up = contract(normed, up_w[...], 1, 0)
+    normed[...] = (qhat * gains).astype(BF)
+    pre_up = contract(normed[...], up_w[...], 1, 0)
     silu_up, up_slope = silu_pair(pre_up)
     update[...] = silu_up.astype(BF)
-    grad_pre_up = (grad_update[...] * up_slope).astype(BF)
-    grad_normed = contract(grad_pre_up, up_w[...], 1, 1)
+    grad_pre_up[...] = (grad_update[...] * up_slope).astype(BF)
+    grad_normed = contract(grad_pre_up[...], up_w[...], 1, 1)
     grad_gain[...] = jnp.sum(grad_normed * qhat, axis=0, keepdims=True)
     grad_qhat = grad_normed * gains
     grad_q = rinv * (grad_qhat - qhat * jnp.mean(grad_qhat * qhat, axis=1, keepdims=True))
     grad_aggregate[...] = grad_q.astype(BF)
     mesh_grad[...] = cot[...].astype(F32) + grad_q
-    stack[0] = contract(gathered, grad_q.astype(BF), 0, 0).astype(BF)
-    stack[1] = contract(normed, grad_pre_up, 0, 0).astype(BF)
-    to_chunks(grads, stack, perm)
-
-
-def tail_kernel(grad_aggregate, update, message_w, out_w, mesh_lat, cot, back, mesh_new, grad_out):
+    theirs = rows_of_half(1 - perm[0] // 4, stack.shape[1])
+    stack[0] = contract(gathered[:, theirs], grad_aggregate[...], 0, 0).astype(BF)
+    stack[1] = contract(normed[:, theirs], grad_pre_up[...], 0, 0).astype(BF)
+    to_chunks(sent, stack, perm, 4)
+
+
+def tail_kernel(
+    perm, gathered, grad_aggregate, normed, grad_pre_up, update, message_w, out_w, mesh_lat, cot,
+    kept, back, mesh_new, grad_out, stack,
+):
+    mine = rows_of_half(perm[0] // 4, stack.shape[1])
+    stack[0] = contract(gathered[:, mine], grad_aggregate[...], 0, 0).astype(BF)
+    stack[1] = contract(normed[:, mine], grad_pre_up[...], 0, 0).astype(BF)
+    to_chunks(kept, stack, perm, 0)
     back[...] = contract(message_w[...], grad_aggregate[...], 1, 1).astype(BF)
     mesh_new[...] = (mesh_lat[...].astype(F32) + contract(update[...], out_w[...], 1, 0)).astype(BF)
     grad_out[...] = contract(update[...], cot[...], 0, 0).astype(BF)
 
 
-def grid_kernel(
-    perm, back, weights_all, slope_own, slope_west, slope_east, x_own, x_west, x_east, grad_gain, grad_out, grads, stack
-):
-    features = x_own.shape[0]
+def points_of(x_own, x_west, x_east):
     tile = x_west.shape[1]
     pieces = []
-    for x, slope in ((x_own, slope_own), (x_west, slope_west), (x_east, slope_east)):
-        pieces += [(x, slope, k) for k in range(x.shape[1] // tile)]
-    sums = jnp.zeros((features, stack.shape[2]), F32)
-    for n, (x, slope, k) in enumerate(pieces):
-        at = slice(k * tile, (k + 1) * tile)
-        hidden = contract(back[...], weights_all[:, n * tile : (n + 1) * tile], 1, 0)
-        grad_pre = (hidden * slope[:, at].astype(F32)).astype(BF)
-        sums += contract(x[:, at], grad_pre, 1, 1)
-    stack[0] = grad_out[...].astype(F32)
-    stack[1] = jnp.zeros(stack.shape[1:], F32)
-    stack[1, :features, :] = sums
-    stack[1, features : features + 1, :] = grad_gain[...]
-    count, matrices, size, _ = grads.shape
-    for j in range(count):
-        at = pl.ds(pl.multiple_of(perm[j] * size, size), size)
-        for k in range(matrices):
-            grads[j, k] = stack[k, at, :].astype(BF)
+    for x in (x_own, x_west, x_east):
+        pieces += [(x, slice(k * tile, (k + 1) * tile)) for k in range(x.shape[1] // tile)]
+    return [(x, at, slice(n * tile, (n + 1) * tile)) for n, (x, at) in enumerate(pieces)]
+
+
+def embed_rows(half, x_parts, grad_pre, grad_gain, out):
+    rows = out.shape[0]
+    features = x_parts[0].shape[0]
+    for side in range(2):
+        count = min(rows, features - side * rows)
+
+        @pl.when(half == side)
+        def _():
+            sums = jnp.zeros((count, out.shape[1]), F32)
+            for x, at, all_at in points_of(*x_parts):
+                sums += contract(x[side * rows : side * rows + count, at], grad_pre[:, all_at], 1, 1)
+            if count < rows:
+                out[...] = jnp.zeros(out.shape, F32)
+                out[count : count + 1, :] = grad_gain[...]
+            out[:count, :] = sums
+
+
+def grid_kernel(
+    perm, back, weights_all, slope_own, slope_west, slope_east, x_own, x_west, x_east, grad_gain, grad_out,
+    sent, grad_pre, stack,
+):
+    for slope, at, all_at in points_of(slope_own, slope_west, slope_east):
+        hidden = contract(back[...], weights_all[:, all_at], 1, 0)
+        grad_pre[:, all_at] = (hidden * slope[:, at].astype(F32)).astype(BF)
+    half = 1 - perm[0] // 4
+    stack[0] = grad_out[rows_of_half(half, stack.shape[1]), :].astype(F32)
+    embed_rows(half, (x_own, x_west, x_east), grad_pre, grad_gain, stack.at[1])
+    to_chunks(sent, stack, perm, 4)
+
+
+def grid_kept_kernel(perm, grad_pre, x_own, x_west, x_east, grad_gain, grad_out, kept, stack):
+    half = perm[0] // 4
+    stack[0] = grad_out[rows_of_half(half, stack.shape[1]), :].astype(F32)
+    embed_rows(half, (x_own, x_west, x_east), grad_pre, grad_gain, stack.at[1])
+    to_chunks(kept, stack, perm, 0)
 
 
 def order_mesh_kernel(perm, *refs):
@@ -239,10 +271,6 @@
 
 def added(a, b):
     return (a.astype(F32) + b.astype(F32)).astype(BF)
-
-
-def core_summed(grads):
-    return added(grads[:4], core_swapped(grads[4:]))
 
 
 def halved(kept):
@@ -290,7 +318,7 @@
     (to_east,) = call(lambda *refs: pack_kernel(True, *refs), "pack_east", [VMEM], [strip], 0, MIB, 8, [wide])(grid)
     x_west = lax.ppermute(to_east, "lon", [(i, (i + 1) % count) for i in range(count)])
     to_east, later = lax.optimization_barrier((to_east, grid))
-    (to_west,) = call(lambda *refs: pack_kernel(False, *refs), "pack_west", [VMEM], [strip], 0, MIB, 8, [wide])(later)
+    (to_west,) = call(lambda *refs: pack_kernel(False, *refs), "pack_west", [VMEM], [strip], 0, MIB, 60, [wide])(later)
     x_east = lax.ppermute(to_west, "lon", [((i + 1) % count, i) for i in range(count)])
 
     weights_all, x_own, embed_t, h_own, slope_own, grad_update = call(
@@ -314,35 +342,41 @@
     )(x_west, embed_t, weights_all, h_own)
 
     perm = chunk_order()
-    grads_a, mesh_grad, gain_term, grad_aggregate, update, slope_east = call(
+    half_chunks = shape((4, 2, latent // 8, latent), BF)
+    node_rows = shape((nodes, latent), BF)
+    (
+        sent_a, mesh_grad, gain_term, gathered, grad_aggregate, normed, grad_pre_up, update, slope_east
+    ) = call(
         mesh_kernel, "mesh_nodes", [SMEM] + [VMEM] * 10,
-        [
-            shape((8, 2, latent // 8, latent), BF),
-            shape((nodes, latent), F32),
-            shape((1, latent), F32),
-            shape((nodes, latent), BF),
-            shape((nodes, latent), BF),
-            shape((latent, side), BF),
-        ],
-        2_000_000_000, 8 * MIB, 16, [pltpu.VMEM((2, latent, latent), BF)],
+        [half_chunks, shape((nodes, latent), F32), shape((1, latent), F32)]
+        + [node_rows] * 5
+        + [shape((latent, side), BF)],
+        2_000_000_000, 8 * MIB, 16, [pltpu.VMEM((2, latent // 2, latent), BF)],
     )(perm, x_east, embed_t, weights_all, h_sum, message_w, up_w, gain.reshape(1, latent), mesh_lat, cot, grad_update)
-    back, mesh_new, grad_out_term = call(
-        tail_kernel, "mesh_tail", [VMEM] * 6,
-        [shape((latent, nodes), BF), shape((nodes, latent), BF), shape((latent, latent), BF)],
-        400_000_000, 3 * MIB, 16,
-    )(grad_aggregate, update, message_w, out_w, mesh_lat, cot)
-
-    kept_a, back = lax.optimization_barrier((core_summed(grads_a), back))
+    got_a = core_swapped(sent_a)
+    kept_a, back, mesh_new, grad_out_term = call(
+        tail_kernel, "mesh_tail", [SMEM] + [VMEM] * 9,
+        [half_chunks, shape((latent, nodes), BF), node_rows, shape((latent, latent), BF)],
+        500_000_000, 3 * MIB, 16, [pltpu.VMEM((2, latent // 2, latent), BF)],
+    )(perm, gathered, grad_aggregate, normed, grad_pre_up, update, message_w, out_w, mesh_lat, cot)
+
+    kept_a, back = lax.optimization_barrier((added(kept_a, got_a), back))
     padded = -(-(features + 1) // 128) * 128
     assert padded == latent
-    (grads_b,) = call(
-        grid_kernel, "grid_points", [SMEM] + [VMEM] * 10, [shape((8, 2, latent // 8, latent), BF)],
-        2_400_000_000, 9 * MIB, 16, [pltpu.VMEM((2, latent, latent), F32)],
-    )(perm, back, weights_all, slope_own, slope_west, slope_east, x_own, x_west, x_east, gain_term, grad_out_term)
-
-    kept_a, grads_b = lax.optimization_barrier((halved(kept_a), grads_b))
+    x_parts = (x_own, x_west, x_east)
+    stack = pltpu.VMEM((2, latent // 2, latent), F32)
+    sent_b, grad_pre = call(
+        grid_kernel, "grid_points", [SMEM] + [VMEM] * 10, [half_chunks, shape((latent, points), BF)],
+        1_600_000_000, 9 * MIB, 20, [stack],
+    )(perm, back, weights_all, slope_own, slope_west, slope_east, *x_parts, gain_term, grad_out_term)
+    got_b = core_swapped(sent_b)
+    kept_a, grad_pre = lax.optimization_barrier((halved(kept_a), grad_pre))
+    (kept_b,) = call(
+        grid_kept_kernel, "grid_kept", [SMEM] + [VMEM] * 6, [half_chunks], 800_000_000, 6 * MIB, 16, [stack]
+    )(perm, grad_pre, *x_parts, gain_term, grad_out_term)
+
     summed_a = all_summed(kept_a)
-    summed_b = all_summed(halved(core_summed(grads_b)))
+    summed_b = all_summed(halved(added(kept_b, got_b)))
     square = shape((latent, latent), F32)
     grad_message, grad_up = call(
         order_mesh_kernel, "order_a", [SMEM] + [VMEM] * 6, [square, square], 0, 3 * MIB, 16

time: 82.4 us -> 81.9 us (level)
  waiting for transfers between devices: 35.7 us -> 30.7 us
  Pallas kernels: 22.9 us -> 26.4 us
  starting transfers between devices: 16.3 us -> 17.5 us
    pallas_call x1, Pallas kernels: 0.5 us -> 2.81 us  [on_device(): call(lambda *refs: pack_kernel(False, *refs), 'pack_west', [VMEM], [strip...]
    ppermute x1, waiting for transfers between devices: 8.68 us -> 6.41 us  [on_device(): lax.ppermute(to_west, 'lon', [((i + 1) % count, i) for i in range(count)])]
    ppermute x8, waiting for transfers between devices: 4.21 us -> 2.43 us  [core_swapped(): lax.ppermute(value, 'lat', [(i, i ^ 1) for i in range(lax.axis_size('lat'...]
    ppermute x10, starting transfers between devices: 10 us -> 11.3 us  [swapped(): return lax.ppermute(value, ('lon', 'lat'), pairs)]
    pallas_call x3 -> x4, Pallas kernels: 8.74 us -> 9.58 us  [the longest x1 3.17 us: on_device(): call(mesh_kernel, 'mesh_nodes', [SMEM] + [VMEM] * 10, [half_chunks, shape...]
  transfers between devices with their start and end apart: 20 -> 20, of which waited for: 18 -> 13; matrix products, arithmetic and copies ran while one was open for 1% -> 1% of each run, Pallas kernels for 20% -> 24%
where the time goes in v8:
time: 81.9 us; the launch traced here: 81.6 us
  waiting for transfers between devices  30.7 us (37%)
  Pallas kernels  26.4 us (32%)
  starting transfers between devices  17.5 us (21%)
  local copies, waits for them, and re-layouts  4.91 us (6%)
  between operations  1.53 us (2%)
    ppermute x10, waiting for transfers between devices, swapped(): return lax.ppermute(value, ('lon', 'lat'), pairs)  21.8 us
    ppermute x10, starting transfers between devices, swapped(): return lax.ppermute(value, ('lon', 'lat'), pairs)  11.3 us
    pallas_call x1, Pallas kernels, on_device(): call(own_kernel, 'own_points', [SMEM] * 3 + [VMEM] * 5, [shape((nodes, po...  7.82 us
    ppermute x1, waiting for transfers between devices, on_device(): lax.ppermute(to_west, 'lon', [((i + 1) % count, i) for i in range(count)])  6.41 us
    unnamed x24, local copies, waits for them, and re-layouts  4.77 us
    pallas_call x1, Pallas kernels, on_device(): call(mesh_kernel, 'mesh_nodes', [SMEM] + [VMEM] * 10, [half_chunks, shape...  3.17 us
    ppermute x1, starting transfers between devices, on_device(): lax.ppermute(to_east, 'lon', [(i, (i + 1) % count) for i in range(count)])  3.02 us
    pallas_call x1, Pallas kernels, on_device(): call(lambda *refs: pack_kernel(False, *refs), 'pack_west', [VMEM], [strip...  2.81 us
  transfers between devices with their start and end apart: 20, of which 13 were waited for; matrix products, arithmetic and copies ran while one was open for 1% of the time, Pallas kernels for 24%

profile of v8, /device:TPU:0, one launch (start us, length us, event | category | flops | bytes accessed | tf_op | source)
XLA Modules:
  0.0 81.6 jit_solution(6920534143976091573)
XLA Ops:
  0.6 1.5 %copy-done = bf16[8,256,474]{1,0,2:T(8,128)(2,1)S(1)} copy-done((bf16[8,256,474]{1,0,2:T(8,128)(2,1)S(1)}, bf16[8,256,474]{1,0,2:T(8,128)(2,1)}, u32[]{:S(2)}) %copy-start) | copy-done | bytes 1941528
  2.2 1.3 %pack_east.1 = bf16[474,512]{1,0:T(8,128)(2,1)} custom-call(bf16[474,8,256]{2,1,0:T(8,128)(2,1)S(1)} %bitcast.12), custom_call_target="tpu_custom_call" | custom-call | bytes 1048576 | tf_op jit(solution)/shard_map/pack_east/pallas_call | solution.py:318
  3.5 3.0 %collective-permute-start.1 = (bf16[474,512]{1,0:T(8,128)(2,1)}, bf16[474,512]{1,0:T(8,128)(2,1)S(1)}, u32[]{:S(2)}, u32[]{:S(2)}) collective-permute-start(bf16[474,512]{1,0:T(8,128)(2,1)} %pack_east.1), channel_id=1, source_target_pairs={{0,4},{4,8},{8,12},{12,0},{1,5},{5,9},{9,13},{13,1},{2,6},{6,10},{... | collective-permute-start | bytes 1456136 | tf_op jit(solution)/shard_map/ppermute | solution.py:319
  6.5 2.8 %pack_west.1 = bf16[474,512]{1,0:T(8,128)(2,1)} custom-call(bf16[474,8,256]{2,1,0:T(8,128)(2,1)} %bitcast.11), custom_call_target="tpu_custom_call" | custom-call | bytes 1048576 | tf_op jit(solution)/shard_map/pack_west/pallas_call | solution.py:321
  9.3 2.0 %collective-permute-start = (bf16[474,512]{1,0:T(8,128)(2,1)}, bf16[474,512]{1,0:T(8,128)(2,1)S(1)}, u32[]{:S(2)}, u32[]{:S(2)}) collective-permute-start(bf16[474,512]{1,0:T(8,128)(2,1)} %pack_west.1), channel_id=1, source_target_pairs={{4,0},{8,4},{12,8},{0,12},{5,1},{9,5},{13,9},{1,13},{6,2},{10,6},{... | collective-permute-start | bytes 1456136 | tf_op jit(solution)/shard_map/ppermute | solution.py:322
  15.3 7.8 %own_points.1 = (bf16[256,3072]{1,0:T(8,128)(2,1)S(1)}, bf16[474,2048]{1,0:T(8,128)(2,1)S(1)}, bf16[512,474]{1,0:T(8,128)(2,1)S(1)}, f32[256,512]{1,0:T(8,128)S(...) custom-call(s32[32]{0:T(128)S(1)} %copy-done.10, s32[32]{0:T(128)S(1)} %copy-done.11, s32[1]{0:T(128)S(6)} %copy.19.count, ...), custom_call_target="tpu_custom_call" | custom-call | flops 4000000000 | bytes 12582912 | tf_op jit(solution)/shard_map/own_points/pallas_call | solution.py:324
  24.1 6.4 %collective-permute-done.x.x_east = bf16[474,512]{1,0:T(8,128)(2,1)S(1)} collective-permute-done((bf16[474,512]{1,0:T(8,128)(2,1)}, bf16[474,512]{1,0:T(8,128)(2,1)S(1)}, u32[]{:S(2)}, u32[]{:S(2)}) %collective-permute-start) | collective-permute-done | bytes 485408 | tf_op jit(solution)/shard_map/ppermute | solution.py:322
  30.5 3.2 %mesh_nodes.1 = (bf16[4,2,64,512]{3,2,1,0:T(8,128)(2,1)S(1)}, f32[256,512]{1,0:T(8,128)}, f32[1,512]{1,0:T(1,128)S(1)}, bf16[256,512]{1,0:T(8,128)(2,1)S(1)}, bf...) custom-call(s32[8]{0:T(128)S(1)} %stack.35.perm, ...), custom_call_target="tpu_custom_call" | custom-call | flops 2000000000 | bytes 8388608 | tf_op jit(solution)/shard_map/mesh_nodes/pallas_call | solution.py:349
  33.7 1.9 %mesh_tail.1 = (bf16[4,2,64,512]{3,2,1,0:T(8,128)(2,1)S(1)}, bf16[512,256]{1,0:T(8,128)(2,1)S(1)}, bf16[256,512]{1,0:T(8,128)(2,1)}, bf16[512,512]{1,0:T(8,128)(2,1)S(1)}) custom-call(s32[8]{0:T(128)S(1)} %stack.35.perm, bf16[256,512]{1,0:T(8,128)(2,1)S(1)} %get-tuple-element.49.gathered, bf16[256,512]{1,0:T(8,128)(2,1)S(1)} %get-tuple-element.50.grad_aggregate, ...), custom_call_target="tpu_custom_call" | custom-call | flops 500000000 | bytes 3145728 | tf_op jit(solution)/shard_map/mesh_tail/pallas_call | solution.py:357
  35.8 1.5 %collective-permute-start.3 = (bf16[2,2,64,512]{3,2,1,0:T(8,128)(2,1)S(1)}, bf16[2,2,64,512]{3,2,1,0:T(8,128)(2,1)S(1)}, u32[]{:S(2)}, u32[]{:S(2)}) collective-permute-start(bf16[2,2,64,512]{3,2,1,0:T(8,128)(2,1)S(1)} %slice.25), channel_id=1, source_target_pairs={{0,2},{1,5},{2,0},{3,7},{4,6},{5,1},{6,4},{7,3},{8,10},{9,13},{10,... | collective-permute-start | bytes 786440 | tf_op jit(solution)/shard_map/ppermute | solution.py:258
  37.3 2.7 %grid_points.1 = (bf16[4,2,64,512]{3,2,1,0:T(8,128)(2,1)S(1)}, bf16[512,3072]{1,0:T(8,128)(2,1)S(1)}) custom-call(s32[8]{0:T(128)S(1)} %stack.35.perm, bf16[512,256]{1,0:T(8,128)(2,1)S(1)} %get-tuple-element.60.back, bf16[256,3072]{1,0:T(8,128)(2,1)S(1)} %get-tuple-element.45.refs_2_.weights_all, bf16[512,2048]{1,0:T(8,128)(2,1)S(1)} %get-tuple-element.61.slope_own, ...), custom_call_target="tpu_custom_call" | custom-call | flops 1600000000 | bytes 9437184 | tf_op jit(solution)/shard_map/grid_points/pallas_call | solution.py:368
  40.1 2.1 %collective-permute-done.3 = bf16[2,2,64,512]{3,2,1,0:T(8,128)(2,1)S(1)} collective-permute-done((bf16[2,2,64,512]{3,2,1,0:T(8,128)(2,1)S(1)}, bf16[2,2,64,512]{3,2,1,0:T(8,128)(2,1)S(1)}, u32[]{:S(2)}, u32[]{:S(2)}) %collective-permute-start.3) | collective-permute-done | bytes 262176 | tf_op jit(solution)/shard_map/ppermute | solution.py:258
  42.9 1.8 %grid_kept.1 = bf16[4,2,64,512]{3,2,1,0:T(8,128)(2,1)S(1)} custom-call(s32[8]{0:T(128)S(1)} %stack.35.perm, bf16[512,3072]{1,0:T(8,128)(2,1)S(1)} %get-tuple-element.68.grad_pre, bf16[474,2048]{1,0:T(8,128)(2,1)S(1)} %get-tuple-element.64.x_own, bf16[474,512]{1,0:T(8,128)(2,1)S(1)} %collective-permute-done.1.refs_0_.x_west, ...), custom_call_target="tpu_custom_call" | custom-call | flops 800000000 | bytes 6291456 | tf_op jit(solution)/shard_map/grid_kept/pallas_call | solution.py:374
  44.9 1.6 %collective-permute-start.5 = (bf16[2,2,64,512]{3,2,1,0:T(8,128)(2,1)S(1)}, bf16[2,2,64,512]{3,2,1,0:T(8,128)(2,1)S(1)}, u32[]{:S(2)}, u32[]{:S(2)}) collective-permute-start(bf16[2,2,64,512]{3,2,1,0:T(8,128)(2,1)S(1)} %slice.33), channel_id=1, source_target_pairs={{0,2},{1,5},{2,0},{3,7},{4,6},{5,1},{6,4},{7,3},{8,10},{9,13},{10,... | collective-permute-start | bytes 786440 | tf_op jit(solution)/shard_map/ppermute | solution.py:258
  47.4 1.9 %collective-permute-start.11 = (bf16[1,2,64,512]{3,2,1,0:T(8,128)(2,1)S(1)}, bf16[1,2,64,512]{3,2,1,0:T(8,128)(2,1)S(1)}, u32[]{:S(2)}, u32[]{:S(2)}) collective-permute-start(bf16[1,2,64,512]{3,2,1,0:T(8,128)(2,1)S(1)} %add_convert_fusion.5), channel_id=1, source_target_pairs={{0,8},{1,9},{2,10},{3,11},{4,12},{5,13},{6,14},{7,15},{8,0},{9,1},... | collective-permute-start | bytes 393224 | tf_op jit(solution)/shard_map/ppermute | solution.py:258
  49.2 2.1 %collective-permute-done.5 = bf16[2,2,64,512]{3,2,1,0:T(8,128)(2,1)S(1)} collective-permute-done((bf16[2,2,64,512]{3,2,1,0:T(8,128)(2,1)S(1)}, bf16[2,2,64,512]{3,2,1,0:T(8,128)(2,1)S(1)}, u32[]{:S(2)}, u32[]{:S(2)}) %collective-permute-start.5) | collective-permute-done | bytes 262176 | tf_op jit(solution)/shard_map/ppermute | solution.py:258
  51.5 1.5 %collective-permute-start.6 = (bf16[1,2,64,512]{3,2,1,0:T(8,128)(2,1)S(1)}, bf16[1,2,64,512]{3,2,1,0:T(8,128)(2,1)S(1)}, u32[]{:S(2)}, u32[]{:S(2)}) collective-permute-start(bf16[1,2,64,512]{3,2,1,0:T(8,128)(2,1)S(1)} %slice.35), channel_id=1, source_target_pairs={{0,4},{1,3},{2,6},{3,1},{4,0},{5,7},{6,2},{7,5},{8,12},{9,11},{10,... | collective-permute-start | bytes 393224 | tf_op jit(solution)/shard_map/ppermute | solution.py:258
  53.0 3.2 %collective-permute-done.11 = bf16[1,2,64,512]{3,2,1,0:T(8,128)(2,1)S(1)} collective-permute-done((bf16[1,2,64,512]{3,2,1,0:T(8,128)(2,1)S(1)}, bf16[1,2,64,512]{3,2,1,0:T(8,128)(2,1)S(1)}, u32[]{:S(2)}, u32[]{:S(2)}) %collective-permute-start.11) | collective-permute-done | bytes 131104 | tf_op jit(solution)/shard_map/ppermute | solution.py:258
  57.5 1.7 %collective-permute-start.7 = (bf16[1,2,64,512]{3,2,1,0:T(8,128)(2,1)S(1)}, bf16[1,2,64,512]{3,2,1,0:T(8,128)(2,1)S(1)}, u32[]{:S(2)}, u32[]{:S(2)}) collective-permute-start(bf16[1,2,64,512]{3,2,1,0:T(8,128)(2,1)S(1)} %add_convert_fusion.7), channel_id=1, source_target_pairs={{0,8},{1,9},{2,10},{3,11},{4,12},{5,13},{6,14},{7,15},{8,0},{9,1},... | collective-permute-start | bytes 393224 | tf_op jit(solution)/shard_map/ppermute | solution.py:258
  59.2 5.5 %collective-permute-done.12.refs_1_ = bf16[1,2,64,512]{3,2,1,0:T(8,128)(2,1)S(1)} collective-permute-done((bf16[1,2,64,512]{3,2,1,0:T(8,128)(2,1)S(1)}, bf16[1,2,64,512]{3,2,1,0:T(8,128)(2,1)S(1)}, u32[]{:S(2)}, u32[]{:S(2)}) %collective-permute-start.12) | collective-permute-done | bytes 131104 | tf_op jit(solution)/shard_map/ppermute | solution.py:258
  66.0 5.2 %collective-permute-done.13.refs_2_ = bf16[2,2,64,512]{3,2,1,0:T(8,128)(2,1)S(1)} collective-permute-done((bf16[2,2,64,512]{3,2,1,0:T(8,128)(2,1)S(1)}, bf16[2,2,64,512]{3,2,1,0:T(8,128)(2,1)S(1)}, u32[]{:S(2)}, u32[]{:S(2)}) %collective-permute-start.13) | collective-permute-done | bytes 262176 | tf_op jit(solution)/shard_map/ppermute | solution.py:258
  73.9 2.0 %order_a.1 = (f32[512,512]{1,0:T(8,128)}, f32[512,512]{1,0:T(8,128)}) custom-call(s32[8]{0:T(128)S(1)} %stack.35.perm, bf16[1,2,64,512]{3,2,1,0:T(8,128)(2,1)S(1)} %add_convert_fusion.4.refs_0_, bf16[1,2,64,512]{3,2,1,0:T(8,128)(2,1)S(1)} %collective-permute-done.12.refs_1_, bf16[2,2,64,512]{3,2,1,0:T(8,128)(2,1)S(1)} %collective-permute-done.13.refs_2_, ...), custom_call_target="tpu_custom_call" | custom-call | bytes 3145728 | tf_op jit(solution)/shard_map/order_a/pallas_call | solution.py:381
  75.9 1.8 %collective-permute-done.9.refs_2_ = bf16[2,2,64,512]{3,2,1,0:T(8,128)(2,1)S(1)} collective-permute-done((bf16[2,2,64,512]{3,2,1,0:T(8,128)(2,1)S(1)}, bf16[2,2,64,512]{3,2,1,0:T(8,128)(2,1)S(1)}, u32[]{:S(2)}, u32[]{:S(2)}) %collective-permute-start.9) | collective-permute-done | bytes 262176 | tf_op jit(solution)/shard_map/ppermute | solution.py:258
  79.6 2.0 %order_b.1 = (f32[512,512]{1,0:T(8,128)}, f32[474,512]{1,0:T(8,128)}, f32[1,512]{1,0:T(1,128)}) custom-call(s32[8]{0:T(128)S(1)} %stack.35.perm, bf16[1,2,64,512]{3,2,1,0:T(8,128)(2,1)S(1)} %add_convert_fusion.6.refs_0_, bf16[1,2,64,512]{3,2,1,0:T(8,128)(2,1)S(1)} %collective-permute-done.8.refs_1_, ...), custom_call_target="tpu_custom_call" | custom-call | bytes 3145728 | tf_op jit(solution)/shard_map/order_b/pallas_call | solution.py:385
  (65 shorter events, 13.5 us)
Async XLA Ops:
  2.2 9.9 %copy-start.1 = (bf16[8,256,474]{1,0,2:T(8,128)(2,1)S(1)}, bf16[8,256,474]{1,0,2:T(8,128)(2,1)}, u32[]{:S(2)}) copy-start(bf16[8,256,474]{1,0,2:T(8,128)(2,1)} %param.12) | copy-start | bytes 5824516
  2.2 9.9 %copy-start.2 = (bf16[512,512]{1,0:T(8,128)(2,1)S(1)}, bf16[512,512]{1,0:T(8,128)(2,1)}, u32[]{:S(2)}) copy-start(bf16[512,512]{1,0:T(8,128)(2,1)} %out_w.3) | copy-start | bytes 1572868
  2.2 9.9 %copy-start.10 = (s32[32]{0:T(128)S(1)}, s32[32]{0:T(128)}, u32[]{:S(2)}) copy-start(s32[32]{0:T(128)} %src.1) | copy-start | bytes 388
  2.2 9.9 %copy-start.11 = (s32[32]{0:T(128)S(1)}, s32[32]{0:T(128)}, u32[]{:S(2)}) copy-start(s32[32]{0:T(128)} %dst.1) | copy-start | bytes 388
  3.5 19.7 %collective-permute-start.1 = (bf16[474,512]{1,0:T(8,128)(2,1)}, bf16[474,512]{1,0:T(8,128)(2,1)S(1)}, u32[]{:S(2)}, u32[]{:S(2)}) collective-permute-start(bf16[474,512]{1,0:T(8,128)(2,1)} %pack_east.1), channel_id=1, source_target_pairs={{0,4},{4,8},{8,12},{12,0},{1,5},{5,9},{9,13},{13,1},{2,6},{6,10},{... | collective-permute-start | bytes 1456136 | tf_op jit(solution)/shard_map/ppermute | solution.py:319
  9.3 21.2 %collective-permute-start = (bf16[474,512]{1,0:T(8,128)(2,1)}, bf16[474,512]{1,0:T(8,128)(2,1)S(1)}, u32[]{:S(2)}, u32[]{:S(2)}) collective-permute-start(bf16[474,512]{1,0:T(8,128)(2,1)} %pack_west.1), channel_id=1, source_target_pairs={{4,0},{8,4},{12,8},{0,12},{5,1},{9,5},{13,9},{1,13},{6,2},{10,6},{... | collective-permute-start | bytes 1456136 | tf_op jit(solution)/shard_map/ppermute | solution.py:322
  33.7 1.9 %collective-permute-start.2 = (bf16[4,2,64,512]{3,2,1,0:T(8,128)(2,1)S(1)}, bf16[4,2,64,512]{3,2,1,0:T(8,128)(2,1)S(1)}, u32[]{:S(2)}, u32[]{:S(2)}) collective-permute-start(bf16[4,2,64,512]{3,2,1,0:T(8,128)(2,1)S(1)} %get-tuple-element.57), channel_id=1, source_target_pairs={{0,1},{1,0},{2,3},{3,2},{4,5},{5,4},{6,7},{7,6},{8,9},{9,8},{10,11... | collective-permute-start | bytes 1572872 | tf_op jit(solution)/shard_map/ppermute | solution.py:247
  35.8 6.4 %collective-permute-start.3 = (bf16[2,2,64,512]{3,2,1,0:T(8,128)(2,1)S(1)}, bf16[2,2,64,512]{3,2,1,0:T(8,128)(2,1)S(1)}, u32[]{:S(2)}, u32[]{:S(2)}) collective-permute-start(bf16[2,2,64,512]{3,2,1,0:T(8,128)(2,1)S(1)} %slice.25), channel_id=1, source_target_pairs={{0,2},{1,5},{2,0},{3,7},{4,6},{5,1},{6,4},{7,3},{8,10},{9,13},{10,... | collective-permute-start | bytes 786440 | tf_op jit(solution)/shard_map/ppermute | solution.py:258
  40.0 4.7 %collective-permute-start.4 = (bf16[4,2,64,512]{3,2,1,0:T(8,128)(2,1)S(1)}, bf16[4,2,64,512]{3,2,1,0:T(8,128)(2,1)S(1)}, u32[]{:S(2)}, u32[]{:S(2)}) collective-permute-start(bf16[4,2,64,512]{3,2,1,0:T(8,128)(2,1)S(1)} %get-tuple-element.69), channel_id=1, source_target_pairs={{0,1},{1,0},{2,3},{3,2},{4,5},{5,4},{6,7},{7,6},{8,9},{9,8},{10,11... | collective-permute-start | bytes 1572872 | tf_op jit(solution)/shard_map/ppermute | solution.py:247
  42.3 5.0 %collective-permute-start.10 = (bf16[1,2,64,512]{3,2,1,0:T(8,128)(2,1)S(1)}, bf16[1,2,64,512]{3,2,1,0:T(8,128)(2,1)S(1)}, u32[]{:S(2)}, u32[]{:S(2)}) collective-permute-start(bf16[1,2,64,512]{3,2,1,0:T(8,128)(2,1)S(1)} %slice.31), channel_id=1, source_target_pairs={{0,4},{1,3},{2,6},{3,1},{4,0},{5,7},{6,2},{7,5},{8,12},{9,11},{10,... | collective-permute-start | bytes 393224 | tf_op jit(solution)/shard_map/ppermute | solution.py:258
  44.9 6.4 %collective-permute-start.5 = (bf16[2,2,64,512]{3,2,1,0:T(8,128)(2,1)S(1)}, bf16[2,2,64,512]{3,2,1,0:T(8,128)(2,1)S(1)}, u32[]{:S(2)}, u32[]{:S(2)}) collective-permute-start(bf16[2,2,64,512]{3,2,1,0:T(8,128)(2,1)S(1)} %slice.33), channel_id=1, source_target_pairs={{0,2},{1,5},{2,0},{3,7},{4,6},{5,1},{6,4},{7,3},{8,10},{9,13},{10,... | collective-permute-start | bytes 786440 | tf_op jit(solution)/shard_map/ppermute | solution.py:258
  47.4 8.8 %collective-permute-start.11 = (bf16[1,2,64,512]{3,2,1,0:T(8,128)(2,1)S(1)}, bf16[1,2,64,512]{3,2,1,0:T(8,128)(2,1)S(1)}, u32[]{:S(2)}, u32[]{:S(2)}) collective-permute-start(bf16[1,2,64,512]{3,2,1,0:T(8,128)(2,1)S(1)} %add_convert_fusion.5), channel_id=1, source_target_pairs={{0,8},{1,9},{2,10},{3,11},{4,12},{5,13},{6,14},{7,15},{8,0},{9,1},... | collective-permute-start | bytes 393224 | tf_op jit(solution)/shard_map/ppermute | solution.py:258
  51.5 6.0 %collective-permute-start.6 = (bf16[1,2,64,512]{3,2,1,0:T(8,128)(2,1)S(1)}, bf16[1,2,64,512]{3,2,1,0:T(8,128)(2,1)S(1)}, u32[]{:S(2)}, u32[]{:S(2)}) collective-permute-start(bf16[1,2,64,512]{3,2,1,0:T(8,128)(2,1)S(1)} %slice.35), channel_id=1, source_target_pairs={{0,4},{1,3},{2,6},{3,1},{4,0},{5,7},{6,2},{7,5},{8,12},{9,11},{10,... | collective-permute-start | bytes 393224 | tf_op jit(solution)/shard_map/ppermute | solution.py:258
  56.2 8.5 %collective-permute-start.12 = (bf16[1,2,64,512]{3,2,1,0:T(8,128)(2,1)S(1)}, bf16[1,2,64,512]{3,2,1,0:T(8,128)(2,1)S(1)}, u32[]{:S(2)}, u32[]{:S(2)}) collective-permute-start(bf16[1,2,64,512]{3,2,1,0:T(8,128)(2,1)S(1)} %add_convert_fusion.4.refs_0_), channel_id=1, source_target_pairs={{0,4},{1,3},{2,6},{3,1},{4,0},{5,7},{6,2},{7,5},{8,12},{9,11},{10,... | collective-permute-start | bytes 393224 | tf_op jit(solution)/shard_map/ppermute | solution.py:258
  57.5 8.4 %collective-permute-start.7 = (bf16[1,2,64,512]{3,2,1,0:T(8,128)(2,1)S(1)}, bf16[1,2,64,512]{3,2,1,0:T(8,128)(2,1)S(1)}, u32[]{:S(2)}, u32[]{:S(2)}) collective-permute-start(bf16[1,2,64,512]{3,2,1,0:T(8,128)(2,1)S(1)} %add_convert_fusion.7), channel_id=1, source_target_pairs={{0,8},{1,9},{2,10},{3,11},{4,12},{5,13},{6,14},{7,15},{8,0},{9,1},... | collective-permute-start | bytes 393224 | tf_op jit(solution)/shard_map/ppermute | solution.py:258
  64.7 6.4 %collective-permute-start.13 = (bf16[2,2,64,512]{3,2,1,0:T(8,128)(2,1)S(1)}, bf16[2,2,64,512]{3,2,1,0:T(8,128)(2,1)S(1)}, u32[]{:S(2)}, u32[]{:S(2)}) collective-permute-start(bf16[2,2,64,512]{3,2,1,0:T(8,128)(2,1)S(1)} %pad_maximum_fusion.1), channel_id=1, source_target_pairs={{0,2},{1,5},{2,0},{3,7},{4,6},{5,1},{6,4},{7,3},{8,10},{9,13},{10,... | collective-permute-start | bytes 786440 | tf_op jit(solution)/shard_map/ppermute | solution.py:258
  65.9 5.3 %collective-permute-start.8 = (bf16[1,2,64,512]{3,2,1,0:T(8,128)(2,1)S(1)}, bf16[1,2,64,512]{3,2,1,0:T(8,128)(2,1)S(1)}, u32[]{:S(2)}, u32[]{:S(2)}) collective-permute-start(bf16[1,2,64,512]{3,2,1,0:T(8,128)(2,1)S(1)} %add_convert_fusion.6.refs_0_), channel_id=1, source_target_pairs={{0,4},{1,3},{2,6},{3,1},{4,0},{5,7},{6,2},{7,5},{8,12},{9,11},{10,... | collective-permute-start | bytes 393224 | tf_op jit(solution)/shard_map/ppermute | solution.py:258
  71.2 2.7 %collective-permute-start.16 = (bf16[2,2,64,512]{3,2,1,0:T(8,128)(2,1)S(1)}, bf16[2,2,64,512]{3,2,1,0:T(8,128)(2,1)S(1)}, u32[]{:S(2)}, u32[]{:S(2)}) collective-permute-start(bf16[2,2,64,512]{3,2,1,0:T(8,128)(2,1)S(1)} %collective-permute-done.13.refs_2_), channel_id=1, source_target_pairs={{0,1},{1,0},{2,3},{3,2},{4,5},{5,4},{6,7},{7,6},{8,9},{9,8},{10,11... | collective-permute-start | bytes 786440 | tf_op jit(solution)/shard_map/ppermute | solution.py:247
  71.2 6.4 %collective-permute-start.9 = (bf16[2,2,64,512]{3,2,1,0:T(8,128)(2,1)S(1)}, bf16[2,2,64,512]{3,2,1,0:T(8,128)(2,1)S(1)}, u32[]{:S(2)}, u32[]{:S(2)}) collective-permute-start(bf16[2,2,64,512]{3,2,1,0:T(8,128)(2,1)S(1)} %pad_maximum_fusion), channel_id=1, source_target_pairs={{0,2},{1,5},{2,0},{3,7},{4,6},{5,1},{6,4},{7,3},{8,10},{9,13},{10,... | collective-permute-start | bytes 786440 | tf_op jit(solution)/shard_map/ppermute | solution.py:258
  72.4 1.3 %collective-permute-start.14 = (bf16[1,2,64,512]{3,2,1,0:T(8,128)(2,1)S(1)}, bf16[1,2,64,512]{3,2,1,0:T(8,128)(2,1)S(1)}, u32[]{:S(2)}, u32[]{:S(2)}) collective-permute-start(bf16[1,2,64,512]{3,2,1,0:T(8,128)(2,1)S(1)} %add_convert_fusion.4.refs_0_), channel_id=1, source_target_pairs={{0,1},{1,0},{2,3},{3,2},{4,5},{5,4},{6,7},{7,6},{8,9},{9,8},{10,11... | collective-permute-start | bytes 393224 | tf_op jit(solution)/shard_map/ppermute | solution.py:247
  72.4 1.5 %collective-permute-start.15 = (bf16[1,2,64,512]{3,2,1,0:T(8,128)(2,1)S(1)}, bf16[1,2,64,512]{3,2,1,0:T(8,128)(2,1)S(1)}, u32[]{:S(2)}, u32[]{:S(2)}) collective-permute-start(bf16[1,2,64,512]{3,2,1,0:T(8,128)(2,1)S(1)} %collective-permute-done.12.refs_1_), channel_id=1, source_target_pairs={{0,1},{1,0},{2,3},{3,2},{4,5},{5,4},{6,7},{7,6},{8,9},{9,8},{10,11... | collective-permute-start | bytes 393224 | tf_op jit(solution)/shard_map/ppermute | solution.py:247
  77.7 1.9 %collective-permute-start.19 = (bf16[2,2,64,512]{3,2,1,0:T(8,128)(2,1)S(1)}, bf16[2,2,64,512]{3,2,1,0:T(8,128)(2,1)S(1)}, u32[]{:S(2)}, u32[]{:S(2)}) collective-permute-start(bf16[2,2,64,512]{3,2,1,0:T(8,128)(2,1)S(1)} %collective-permute-done.9.refs_2_), channel_id=1, source_target_pairs={{0,1},{1,0},{2,3},{3,2},{4,5},{5,4},{6,7},{7,6},{8,9},{9,8},{10,11... | collective-permute-start | bytes 786440 | tf_op jit(solution)/shard_map/ppermute | solution.py:247
  77.7 1.7 %collective-permute-start.17 = (bf16[1,2,64,512]{3,2,1,0:T(8,128)(2,1)S(1)}, bf16[1,2,64,512]{3,2,1,0:T(8,128)(2,1)S(1)}, u32[]{:S(2)}, u32[]{:S(2)}) collective-permute-start(bf16[1,2,64,512]{3,2,1,0:T(8,128)(2,1)S(1)} %add_convert_fusion.6.refs_0_), channel_id=1, source_target_pairs={{0,1},{1,0},{2,3},{3,2},{4,5},{5,4},{6,7},{7,6},{8,9},{9,8},{10,11... | collective-permute-start | bytes 393224 | tf_op jit(solution)/shard_map/ppermute | solution.py:247
  78.2 1.4 %collective-permute-start.18 = (bf16[1,2,64,512]{3,2,1,0:T(8,128)(2,1)S(1)}, bf16[1,2,64,512]{3,2,1,0:T(8,128)(2,1)S(1)}, u32[]{:S(2)}, u32[]{:S(2)}) collective-permute-start(bf16[1,2,64,512]{3,2,1,0:T(8,128)(2,1)S(1)} %collective-permute-done.8.refs_1_), channel_id=1, source_target_pairs={{0,1},{1,0},{2,3},{3,2},{4,5},{5,4},{6,7},{7,6},{8,9},{9,8},{10,11... | collective-permute-start | bytes 393224 | tf_op jit(solution)/shard_map/ppermute | solution.py:247
  (8 other events, 34.1 us)

commit v9 on v8

--- a/solution.py
+++ b/solution.py
@@ -40,14 +40,9 @@
         out[:, pair * block : (pair + 1) * block] = jnp.where(lane < half, even, odd).astype(BF)
 
 
-def own_kernel(
-    src, dst, count, grid, embed_w, edge_w, cot, out_w,
-    weights_all, x_t, embed_t, h_own, slope, grad_update, acc, wide,
-):
-    features, rows, cols = grid.shape
+def weights_kernel(rows, own_blocks, src, dst, count, edge_w, cot, out_w, weights_all, grad_update, acc):
     block = edge_w.shape[1]
     half = block // 2
-    own_blocks = cols // block
     windows = 2 * own_blocks + 1
     west_base = rows * own_blocks
     east_base = west_base + rows // 2
@@ -86,21 +81,31 @@
     lax.fori_loop(0, count[0], slot, 0)
     for k in range(acc.shape[0]):
         weights_all[:, k * block : (k + 1) * block] = acc[k].astype(BF)
-    for k in range(own_blocks):
+    grad_update[...] = contract(cot[...], out_w[...], 1, 1)
+
+
+def rows_kernel(grid, embed_w, x_t, embed_t, wide):
+    features, rows, cols = grid.shape
+    block = wide.shape[2]
+    for k in range(cols // block):
         wide[k] = grid[:, :, k * block : (k + 1) * block].astype(F32).reshape(features * rows, block)
-    embed_t[...] = embed_w[...].T
-    total = jnp.zeros(h_own.shape, F32)
-    for r in range(rows):
-        at = slice(r * cols, (r + 1) * cols)
-        for k in range(own_blocks):
+        for r in range(rows):
             x_t[:, r * cols + k * block : r * cols + (k + 1) * block] = wide[
                 k, pl.ds(r, features, stride=rows), :
             ].astype(BF)
+    embed_t[...] = embed_w[...].T
+
+
+def own_kernel(x_t, embed_t, weights_all, h_own, slope):
+    points = x_t.shape[1]
+    tile = points // 8
+    total = jnp.zeros(h_own.shape, F32)
+    for r in range(8):
+        at = slice(r * tile, (r + 1) * tile)
         hidden, hidden_slope = silu_pair(contract(embed_t[...], x_t[:, at], 1, 0))
         slope[:, at] = hidden_slope.astype(BF)
         total += contract(weights_all[:, at], hidden.astype(BF), 1, 1)
     h_own[...] = total
-    grad_update[...] = contract(cot[...], out_w[...], 1, 1)
 
 
 def halo_part(x, embed_t, weights, slope):
@@ -228,12 +233,18 @@
     from_chunks(refs[-2:], refs[:-2], perm)
 
 
-def order_grid_kernel(perm, *refs):
-    grad_out, grad_embed, grad_gain, total = refs[-4:]
-    from_chunks((grad_out, total), refs[:-4], perm)
-    features = grad_embed.shape[0]
-    grad_embed[...] = total[:features, :]
-    grad_gain[...] = total[features : features + 1, :]
+def order_grid_kernel(half, behind, perm, *refs):
+    chunks, others, (grad_out, grad_embed, grad_gain) = refs[:3], refs[3:-3], refs[-3:]
+    j = 4 * half
+    for chunk in chunks:
+        for n in range(chunk.shape[0]):
+            size = chunk.shape[2]
+            at = pl.ds(pl.multiple_of((perm[j] & 3) * size, size), size)
+            grad_out[at, :] = chunk[n, 0].astype(F32)
+            grad_embed[at, :] = chunk[n, 1].astype(F32)
+            j += 1
+    row = others[0][...] if others else jnp.zeros(grad_gain.shape, F32)
+    grad_gain[...] = jnp.where(perm[4 * half] >= 4, grad_embed[behind : behind + 1, :], row)
 
 
 def role_steps():
@@ -318,22 +329,22 @@
     (to_east,) = call(lambda *refs: pack_kernel(True, *refs), "pack_east", [VMEM], [strip], 0, MIB, 8, [wide])(grid)
     x_west = lax.ppermute(to_east, "lon", [(i, (i + 1) % count) for i in range(count)])
     to_east, later = lax.optimization_barrier((to_east, grid))
-    (to_west,) = call(lambda *refs: pack_kernel(False, *refs), "pack_west", [VMEM], [strip], 0, MIB, 60, [wide])(later)
+    (to_west,) = call(lambda *refs: pack_kernel(False, *refs), "pack_west", [VMEM], [strip], 0, MIB, 8, [wide])(later)
     x_east = lax.ppermute(to_west, "lon", [((i + 1) % count, i) for i in range(count)])
 
-    weights_all, x_own, embed_t, h_own, slope_own, grad_update = call(
-        own_kernel, "own_points", [SMEM] * 3 + [VMEM] * 5,
-        [
-            shape((nodes, points), BF),
-            shape((features, own), BF),
-            shape((latent, features), BF),
-            shape((nodes, latent), F32),
-            shape((latent, own), BF),
-            shape((nodes, latent), F32),
-        ],
-        4_000_000_000, 12 * MIB, 24,
-        [pltpu.VMEM((points // block, nodes, block), F32), pltpu.VMEM((cols // block, features * rows, block), F32)],
-    )(edge_src, edge_dst, block_count, grid, embed_w, edge_w, cot, out_w)
+    weights_all, grad_update = call(
+        lambda *refs: weights_kernel(rows, cols // block, *refs), "slot_weights", [SMEM] * 3 + [VMEM] * 3,
+        [shape((nodes, points), BF), shape((nodes, latent), F32)],
+        200_000_000, 4 * MIB, 16, [pltpu.VMEM((points // block, nodes, block), F32)],
+    )(edge_src, edge_dst, block_count, edge_w, cot, out_w)
+    x_own, embed_t = call(
+        rows_kernel, "own_rows", [VMEM] * 2, [shape((features, own), BF), shape((latent, features), BF)],
+        1_000_000_000, 5 * MIB, 16, [pltpu.VMEM((cols // block, features * rows, block), F32)],
+    )(later, embed_w)
+    h_own, slope_own = call(
+        own_kernel, "own_points", [VMEM] * 3, [shape((nodes, latent), F32), shape((latent, own), BF)],
+        2_000_000_000, 7 * MIB, 16,
+    )(x_own, embed_t, weights_all)
 
     h_sum, slope_west = call(
         lambda *refs: west_kernel(own, *refs), "west_points", [VMEM] * 4,
@@ -382,11 +393,33 @@
         order_mesh_kernel, "order_a", [SMEM] + [VMEM] * 6, [square, square], 0, 3 * MIB, 16
     )(perm, *from_both_cores(summed_a))
     last, grad_message, grad_up = lax.optimization_barrier((summed_b[2], grad_message, grad_up))
-    grad_out, grad_embed, grad_gain = call(
-        order_grid_kernel, "order_b", [SMEM] + [VMEM] * 6,
-        [square, shape((features, latent), F32), shape((1, latent), F32)], 0, 3 * MIB, 16,
-        [pltpu.VMEM((latent, latent), F32)],
-    )(perm, *from_both_cores((*summed_b[:2], last)))
+    summed_b = (*summed_b[:2], last)
+    rows_half = latent // 2
+    behind = features - rows_half
+    outs = [square, shape((features, latent), F32), shape((1, latent), F32)]
+
+    def order_b(half, chunks, more, more_specs, aliases):
+        block_of = pl.BlockSpec((rows_half, latent), lambda i, perm: (perm[4 * half] // 4, 0))
+        return pl.pallas_call(
+            lambda *refs: order_grid_kernel(half, behind, *refs),
+            name="order_b",
+            grid_spec=pltpu.PrefetchScalarGridSpec(
+                num_scalar_prefetch=1,
+                grid=(1,),
+                in_specs=[VMEM] * 3 + more_specs,
+                out_specs=[block_of, block_of, VMEM],
+            ),
+            out_shape=outs,
+            input_output_aliases=aliases,
+            compiler_params=pltpu.CompilerParams(vmem_limit_bytes=16 * MIB),
+            cost_estimate=pl.CostEstimate(flops=0, bytes_accessed=2 * MIB, transcendentals=0),
+        )(perm, *chunks, *more)
+
+    from_other = [core_swapped(chunk) for chunk in summed_b]
+    held = order_b(0, summed_b, (), [], {})
+    grad_out, grad_embed, grad_gain = order_b(
+        1, from_other, (held[2], held[0], held[1]), [VMEM] + [pl.BlockSpec(memory_space=pl.ANY)] * 2, {5: 0, 6: 1}
+    )
     return (mesh_new, mesh_grad, grad_embed, grad_message, grad_up, grad_out, grad_gain[0])
 
 

time: 81.9 us -> 81.7 us (level)
  waiting for transfers between devices: 30.7 us -> 29.7 us
    pallas_call x2 -> x5, Pallas kernels: 9.84 us -> 12.1 us  [the longest x1 4.12 us: on_device(): call(lambda *refs: weights_kernel(rows, cols // block, *refs), 'slot_weig...]
    pallas_call x1, Pallas kernels: 2.81 us -> 1.28 us  [on_device(): call(lambda *refs: pack_kernel(False, *refs), 'pack_west', [VMEM], [strip...]
    ppermute x8, waiting for transfers between devices: 2.43 us -> 1.04 us  [core_swapped(): lax.ppermute(value, 'lat', [(i, i ^ 1) for i in range(lax.axis_size('lat'...]
    unnamed x24 -> x26, local copies, waits for them, and re-layouts: 4.77 us -> 4.77 us
  transfers between devices with their start and end apart: 20 -> 20, of which waited for: 13 -> 11; matrix products, arithmetic and copies ran while one was open for 1% -> 1% of each run, Pallas kernels for 24% -> 26%
where the time goes in v9:
time: 81.7 us; the launch traced here: 81.4 us
  waiting for transfers between devices  29.7 us (36%)
  Pallas kernels  27.1 us (33%)
  starting transfers between devices  17.4 us (21%)
  local copies, waits for them, and re-layouts  4.92 us (6%)
  between operations  1.57 us (2%)
    ppermute x10, waiting for transfers between devices, swapped(): return lax.ppermute(value, ('lon', 'lat'), pairs)  21.9 us
    ppermute x10, starting transfers between devices, swapped(): return lax.ppermute(value, ('lon', 'lat'), pairs)  11.2 us
    ppermute x1, waiting for transfers between devices, on_device(): lax.ppermute(to_west, 'lon', [((i + 1) % count, i) for i in range(count)])  6.76 us
    unnamed x26, local copies, waits for them, and re-layouts  4.77 us
    pallas_call x1, Pallas kernels, on_device(): call(lambda *refs: weights_kernel(rows, cols // block, *refs), 'slot_weig...  4.12 us
    pallas_call x1, Pallas kernels, on_device(): call(own_kernel, 'own_points', [VMEM] * 3, [shape((nodes, latent), F32),...  3.54 us
    pallas_call x1, Pallas kernels, on_device(): call(mesh_kernel, 'mesh_nodes', [SMEM] + [VMEM] * 10, [half_chunks, shape...  3.19 us
    pallas_call x2, Pallas kernels, order_b(): pl.pallas_call(lambda *refs: order_grid_kernel(half, behind, *refs), name...  3.12 us
  transfers between devices with their start and end apart: 20, of which 11 were waited for; matrix products, arithmetic and copies ran while one was open for 1% of the time, Pallas kernels for 26%

profile of v9, /device:TPU:0, one launch (start us, length us, event | category | flops | bytes accessed | tf_op | source)
XLA Modules:
  0.0 81.4 jit_solution(10959070146586609818)
XLA Ops:
  0.6 1.5 %copy-done = bf16[8,256,474]{1,0,2:T(8,128)(2,1)S(1)} copy-done((bf16[8,256,474]{1,0,2:T(8,128)(2,1)S(1)}, bf16[8,256,474]{1,0,2:T(8,128)(2,1)}, u32[]{:S(2)}) %copy-start) | copy-done | bytes 1941528
  3.5 3.0 %collective-permute-start.1 = (bf16[474,512]{1,0:T(8,128)(2,1)}, bf16[474,512]{1,0:T(8,128)(2,1)S(1)}, u32[]{:S(2)}, u32[]{:S(2)}) collective-permute-start(bf16[474,512]{1,0:T(8,128)(2,1)} %pack_east.1), channel_id=1, source_target_pairs={{0,4},{4,8},{8,12},{12,0},{1,5},{5,9},{9,13},{13,1},{2,6},{6,10},{... | collective-permute-start | bytes 1456136 | tf_op jit(solution)/shard_map/ppermute | solution.py:330
  7.8 2.0 %collective-permute-start = (bf16[474,512]{1,0:T(8,128)(2,1)}, bf16[474,512]{1,0:T(8,128)(2,1)S(1)}, u32[]{:S(2)}, u32[]{:S(2)}) collective-permute-start(bf16[474,512]{1,0:T(8,128)(2,1)} %pack_west.1), channel_id=1, source_target_pairs={{4,0},{8,4},{12,8},{0,12},{5,1},{9,5},{13,9},{1,13},{6,2},{10,6},{... | collective-permute-start | bytes 1456136 | tf_op jit(solution)/shard_map/ppermute | solution.py:333
  12.7 4.1 %slot_weights.1 = (bf16[256,3072]{1,0:T(8,128)(2,1)S(1)}, f32[256,512]{1,0:T(8,128)S(1)}) custom-call(s32[32]{0:T(128)S(1)} %copy-done.8, s32[32]{0:T(128)S(1)} %copy-done.9, s32[1]{0:T(128)S(6)} %copy.23.refs_2_, bf16[32,128,128]{2,1,0:T(8,128)(2,1)S(1)} %copy-done.3, bf16[256,512]{1,0:T(8,128)(2,1)S(1)} %copy-done.4, bf16[512,512]{1,0:T(8,128)(2,1)S(1)} %copy-done.2), custom_call_target="tpu_custom_call" | custom-call | flops 200000000 | bytes 4194304 | tf_op jit(solution)/shard_map/slot_weights/pallas_call | solution.py:335
  19.2 3.5 %own_points.1 = (f32[256,512]{1,0:T(8,128)S(1)}, bf16[512,2048]{1,0:T(8,128)(2,1)S(1)}) custom-call(bf16[474,2048]{1,0:T(8,128)(2,1)S(1)} %get-tuple-element.49.x_t.x_own, bf16[512,474]{1,0:T(8,128)(2,1)S(1)} %get-tuple-element.47.embed_t.refs_1_, bf16[256,3072]{1,0:T(8,128)(2,1)S(1)} %get-tuple-element.48.weights_all.refs_2_), custom_call_target="tpu_custom_call" | custom-call | flops 2000000000 | bytes 7340032 | tf_op jit(solution)/shard_map/own_points/pallas_call | solution.py:344
  23.7 6.8 %collective-permute-done.x.x_east = bf16[474,512]{1,0:T(8,128)(2,1)S(1)} collective-permute-done((bf16[474,512]{1,0:T(8,128)(2,1)}, bf16[474,512]{1,0:T(8,128)(2,1)S(1)}, u32[]{:S(2)}, u32[]{:S(2)}) %collective-permute-start) | collective-permute-done | bytes 485408 | tf_op jit(solution)/shard_map/ppermute | solution.py:333
  30.5 3.2 %mesh_nodes.1 = (bf16[4,2,64,512]{3,2,1,0:T(8,128)(2,1)S(1)}, f32[256,512]{1,0:T(8,128)}, f32[1,512]{1,0:T(1,128)S(1)}, bf16[256,512]{1,0:T(8,128)(2,1)S(1)}, bf...) custom-call(s32[8]{0:T(128)S(1)} %stack.35.perm.refs_0_, ...), custom_call_target="tpu_custom_call" | custom-call | flops 2000000000 | bytes 8388608 | tf_op jit(solution)/shard_map/mesh_nodes/pallas_call | solution.py:360
  33.7 1.9 %mesh_tail.1 = (bf16[4,2,64,512]{3,2,1,0:T(8,128)(2,1)S(1)}, bf16[512,256]{1,0:T(8,128)(2,1)S(1)}, bf16[256,512]{1,0:T(8,128)(2,1)}, bf16[512,512]{1,0:T(8,128)(2,1)S(1)}) custom-call(s32[8]{0:T(128)S(1)} %stack.35.perm.refs_0_, bf16[256,512]{1,0:T(8,128)(2,1)S(1)} %get-tuple-element.53.gathered, bf16[256,512]{1,0:T(8,128)(2,1)S(1)} %get-tuple-element.54.grad_aggregate, ...), custom_call_target="tpu_custom_call" | custom-call | flops 500000000 | bytes 3145728 | tf_op jit(solution)/shard_map/mesh_tail/pallas_call | solution.py:368
  35.8 1.6 %collective-permute-start.3 = (bf16[2,2,64,512]{3,2,1,0:T(8,128)(2,1)S(1)}, bf16[2,2,64,512]{3,2,1,0:T(8,128)(2,1)S(1)}, u32[]{:S(2)}, u32[]{:S(2)}) collective-permute-start(bf16[2,2,64,512]{3,2,1,0:T(8,128)(2,1)S(1)} %slice.25), channel_id=1, source_target_pairs={{0,2},{1,5},{2,0},{3,7},{4,6},{5,1},{6,4},{7,3},{8,10},{9,13},{10,... | collective-permute-start | bytes 786440 | tf_op jit(solution)/shard_map/ppermute | solution.py:269
  37.4 2.7 %grid_points.1 = (bf16[4,2,64,512]{3,2,1,0:T(8,128)(2,1)S(1)}, bf16[512,3072]{1,0:T(8,128)(2,1)S(1)}) custom-call(s32[8]{0:T(128)S(1)} %stack.35.perm.refs_0_, bf16[512,256]{1,0:T(8,128)(2,1)S(1)} %get-tuple-element.64.back, bf16[256,3072]{1,0:T(8,128)(2,1)S(1)} %get-tuple-element.48.weights_all.refs_2_, bf16[512,2048]{1,0:T(8,128)(2,1)S(1)} %get-tuple-element.65.slope_own, ...), custom_call_target="tpu_custom_call" | custom-call | flops 1600000000 | bytes 9437184 | tf_op jit(solution)/shard_map/grid_points/pallas_call | solution.py:379
  40.2 2.1 %collective-permute-done.3 = bf16[2,2,64,512]{3,2,1,0:T(8,128)(2,1)S(1)} collective-permute-done((bf16[2,2,64,512]{3,2,1,0:T(8,128)(2,1)S(1)}, bf16[2,2,64,512]{3,2,1,0:T(8,128)(2,1)S(1)}, u32[]{:S(2)}, u32[]{:S(2)}) %collective-permute-start.3) | collective-permute-done | bytes 262176 | tf_op jit(solution)/shard_map/ppermute | solution.py:269
  42.9 1.8 %grid_kept.1 = bf16[4,2,64,512]{3,2,1,0:T(8,128)(2,1)S(1)} custom-call(s32[8]{0:T(128)S(1)} %stack.35.perm.refs_0_, bf16[512,3072]{1,0:T(8,128)(2,1)S(1)} %get-tuple-element.71.grad_pre, bf16[474,2048]{1,0:T(8,128)(2,1)S(1)} %get-tuple-element.49.x_t.x_own, bf16[474,512]{1,0:T(8,128)(2,1)S(1)} %collective-permute-done.1.refs_0_.x_west, ...), custom_call_target="tpu_custom_call" | custom-call | flops 800000000 | bytes 6291456 | tf_op jit(solution)/shard_map/grid_kept/pallas_call | solution.py:385
  45.0 1.6 %collective-permute-start.5 = (bf16[2,2,64,512]{3,2,1,0:T(8,128)(2,1)S(1)}, bf16[2,2,64,512]{3,2,1,0:T(8,128)(2,1)S(1)}, u32[]{:S(2)}, u32[]{:S(2)}) collective-permute-start(bf16[2,2,64,512]{3,2,1,0:T(8,128)(2,1)S(1)} %slice.33), channel_id=1, source_target_pairs={{0,2},{1,5},{2,0},{3,7},{4,6},{5,1},{6,4},{7,3},{8,10},{9,13},{10,... | collective-permute-start | bytes 786440 | tf_op jit(solution)/shard_map/ppermute | solution.py:269
  47.4 1.9 %collective-permute-start.13 = (bf16[1,2,64,512]{3,2,1,0:T(8,128)(2,1)S(1)}, bf16[1,2,64,512]{3,2,1,0:T(8,128)(2,1)S(1)}, u32[]{:S(2)}, u32[]{:S(2)}) collective-permute-start(bf16[1,2,64,512]{3,2,1,0:T(8,128)(2,1)S(1)} %add_convert_fusion.5), channel_id=1, source_target_pairs={{0,8},{1,9},{2,10},{3,11},{4,12},{5,13},{6,14},{7,15},{8,0},{9,1},... | collective-permute-start | bytes 393224 | tf_op jit(solution)/shard_map/ppermute | solution.py:269
  49.3 2.1 %collective-permute-done.5 = bf16[2,2,64,512]{3,2,1,0:T(8,128)(2,1)S(1)} collective-permute-done((bf16[2,2,64,512]{3,2,1,0:T(8,128)(2,1)S(1)}, bf16[2,2,64,512]{3,2,1,0:T(8,128)(2,1)S(1)}, u32[]{:S(2)}, u32[]{:S(2)}) %collective-permute-start.5) | collective-permute-done | bytes 262176 | tf_op jit(solution)/shard_map/ppermute | solution.py:269
  51.5 1.5 %collective-permute-start.6 = (bf16[1,2,64,512]{3,2,1,0:T(8,128)(2,1)S(1)}, bf16[1,2,64,512]{3,2,1,0:T(8,128)(2,1)S(1)}, u32[]{:S(2)}, u32[]{:S(2)}) collective-permute-start(bf16[1,2,64,512]{3,2,1,0:T(8,128)(2,1)S(1)} %slice.35), channel_id=1, source_target_pairs={{0,4},{1,3},{2,6},{3,1},{4,0},{5,7},{6,2},{7,5},{8,12},{9,11},{10,... | collective-permute-start | bytes 393224 | tf_op jit(solution)/shard_map/ppermute | solution.py:269
  53.0 3.2 %collective-permute-done.13 = bf16[1,2,64,512]{3,2,1,0:T(8,128)(2,1)S(1)} collective-permute-done((bf16[1,2,64,512]{3,2,1,0:T(8,128)(2,1)S(1)}, bf16[1,2,64,512]{3,2,1,0:T(8,128)(2,1)S(1)}, u32[]{:S(2)}, u32[]{:S(2)}) %collective-permute-start.13) | collective-permute-done | bytes 131104 | tf_op jit(solution)/shard_map/ppermute | solution.py:269
  57.5 1.8 %collective-permute-start.7 = (bf16[1,2,64,512]{3,2,1,0:T(8,128)(2,1)S(1)}, bf16[1,2,64,512]{3,2,1,0:T(8,128)(2,1)S(1)}, u32[]{:S(2)}, u32[]{:S(2)}) collective-permute-start(bf16[1,2,64,512]{3,2,1,0:T(8,128)(2,1)S(1)} %add_convert_fusion.7), channel_id=1, source_target_pairs={{0,8},{1,9},{2,10},{3,11},{4,12},{5,13},{6,14},{7,15},{8,0},{9,1},... | collective-permute-start | bytes 393224 | tf_op jit(solution)/shard_map/ppermute | solution.py:269
  59.3 5.5 %collective-permute-done.14.refs_1_ = bf16[1,2,64,512]{3,2,1,0:T(8,128)(2,1)S(1)} collective-permute-done((bf16[1,2,64,512]{3,2,1,0:T(8,128)(2,1)S(1)}, bf16[1,2,64,512]{3,2,1,0:T(8,128)(2,1)S(1)}, u32[]{:S(2)}, u32[]{:S(2)}) %collective-permute-start.14) | collective-permute-done | bytes 131104 | tf_op jit(solution)/shard_map/ppermute | solution.py:269
  66.0 5.2 %collective-permute-done.15.refs_2_ = bf16[2,2,64,512]{3,2,1,0:T(8,128)(2,1)S(1)} collective-permute-done((bf16[2,2,64,512]{3,2,1,0:T(8,128)(2,1)S(1)}, bf16[2,2,64,512]{3,2,1,0:T(8,128)(2,1)S(1)}, u32[]{:S(2)}, u32[]{:S(2)}) %collective-permute-start.15) | collective-permute-done | bytes 262176 | tf_op jit(solution)/shard_map/ppermute | solution.py:269
  73.9 2.0 %order_a.1 = (f32[512,512]{1,0:T(8,128)}, f32[512,512]{1,0:T(8,128)}) custom-call(s32[8]{0:T(128)S(1)} %stack.35.perm.refs_0_, bf16[1,2,64,512]{3,2,1,0:T(8,128)(2,1)S(1)} %add_convert_fusion.4.refs_0_, bf16[1,2,64,512]{3,2,1,0:T(8,128)(2,1)S(1)} %collective-permute-done.14.refs_1_, bf16[2,2,64,512]{3,2,1,0:T(8,128)(2,1)S(1)} %collective-permute-done.15.refs_2_, ...), custom_call_target="tpu_custom_call" | custom-call | bytes 3145728 | tf_op jit(solution)/shard_map/order_a/pallas_call | solution.py:392
  75.9 1.8 %collective-permute-done.11.refs_3_ = bf16[2,2,64,512]{3,2,1,0:T(8,128)(2,1)S(1)} collective-permute-done((bf16[2,2,64,512]{3,2,1,0:T(8,128)(2,1)S(1)}, bf16[2,2,64,512]{3,2,1,0:T(8,128)(2,1)S(1)}, u32[]{:S(2)}, u32[]{:S(2)}) %collective-permute-start.11) | collective-permute-done | bytes 262176 | tf_op jit(solution)/shard_map/ppermute | solution.py:269
  78.2 1.6 %order_b.2 = (f32[512,512]{1,0:T(8,128)}, f32[474,512]{1,0:T(8,128)}, f32[1,512]{1,0:T(1,128)S(1)}) custom-call(s32[8]{0:T(128)S(1)} %stack.35.perm.refs_0_, bf16[1,2,64,512]{3,2,1,0:T(8,128)(2,1)S(1)} %add_convert_fusion.6.refs_1_, bf16[1,2,64,512]{3,2,1,0:T(8,128)(2,1)S(1)} %collective-permute-done.9.refs_2_, ...), custom_call_target="tpu_custom_call" | custom-call | bytes 2097152 | tf_op jit(solution)/shard_map/order_b/pallas_call | solution.py:403
  79.8 1.6 %order_b.3 = (f32[512,512]{1,0:T(8,128)}, f32[474,512]{1,0:T(8,128)}, f32[1,512]{1,0:T(1,128)}) custom-call(s32[8]{0:T(128)S(1)} %stack.35.perm.refs_0_, bf16[1,2,64,512]{3,2,1,0:T(8,128)(2,1)S(1)} %collective-permute-done.8.refs_1_, bf16[1,2,64,512]{3,2,1,0:T(8,128)(2,1)S(1)} %collective-permute-done.10.refs_2_, ...), custom_call_target="tpu_custom_call", output_to_operand_aliasing={{0}: (5, {}), {1}: (6, {})} | custom-call | bytes 2097152 | tf_op jit(solution)/shard_map/order_b/pallas_call | solution.py:403
  (70 shorter events, 15.9 us)
Async XLA Ops:
  2.2 8.4 %copy-start.2 = (bf16[512,512]{1,0:T(8,128)(2,1)S(1)}, bf16[512,512]{1,0:T(8,128)(2,1)}, u32[]{:S(2)}) copy-start(bf16[512,512]{1,0:T(8,128)(2,1)} %out_w.1) | copy-start | bytes 1572868
  2.2 8.4 %copy-start.8 = (s32[32]{0:T(128)S(1)}, s32[32]{0:T(128)}, u32[]{:S(2)}) copy-start(s32[32]{0:T(128)} %refs_0_.1) | copy-start | bytes 388
  2.2 8.4 %copy-start.9 = (s32[32]{0:T(128)S(1)}, s32[32]{0:T(128)}, u32[]{:S(2)}) copy-start(s32[32]{0:T(128)} %refs_1_.1) | copy-start | bytes 388
  3.5 13.4 %copy-start.1 = (bf16[8,256,474]{1,0,2:T(8,128)(2,1)S(1)}, bf16[8,256,474]{1,0,2:T(8,128)(2,1)}, u32[]{:S(2)}) copy-start(bf16[8,256,474]{1,0,2:T(8,128)(2,1)} %param.12) | copy-start | bytes 5824516
  3.5 19.4 %collective-permute-start.1 = (bf16[474,512]{1,0:T(8,128)(2,1)}, bf16[474,512]{1,0:T(8,128)(2,1)S(1)}, u32[]{:S(2)}, u32[]{:S(2)}) collective-permute-start(bf16[474,512]{1,0:T(8,128)(2,1)} %pack_east.1), channel_id=1, source_target_pairs={{0,4},{4,8},{8,12},{12,0},{1,5},{5,9},{9,13},{13,1},{2,6},{6,10},{... | collective-permute-start | bytes 1456136 | tf_op jit(solution)/shard_map/ppermute | solution.py:330
  7.8 22.7 %collective-permute-start = (bf16[474,512]{1,0:T(8,128)(2,1)}, bf16[474,512]{1,0:T(8,128)(2,1)S(1)}, u32[]{:S(2)}, u32[]{:S(2)}) collective-permute-start(bf16[474,512]{1,0:T(8,128)(2,1)} %pack_west.1), channel_id=1, source_target_pairs={{4,0},{8,4},{12,8},{0,12},{5,1},{9,5},{13,9},{1,13},{6,2},{10,6},{... | collective-permute-start | bytes 1456136 | tf_op jit(solution)/shard_map/ppermute | solution.py:333
  33.7 1.9 %collective-permute-start.2 = (bf16[4,2,64,512]{3,2,1,0:T(8,128)(2,1)S(1)}, bf16[4,2,64,512]{3,2,1,0:T(8,128)(2,1)S(1)}, u32[]{:S(2)}, u32[]{:S(2)}) collective-permute-start(bf16[4,2,64,512]{3,2,1,0:T(8,128)(2,1)S(1)} %get-tuple-element.61), channel_id=1, source_target_pairs={{0,1},{1,0},{2,3},{3,2},{4,5},{5,4},{6,7},{7,6},{8,9},{9,8},{10,11... | collective-permute-start | bytes 1572872 | tf_op jit(solution)/shard_map/ppermute | solution.py:258
  35.8 6.4 %collective-permute-start.3 = (bf16[2,2,64,512]{3,2,1,0:T(8,128)(2,1)S(1)}, bf16[2,2,64,512]{3,2,1,0:T(8,128)(2,1)S(1)}, u32[]{:S(2)}, u32[]{:S(2)}) collective-permute-start(bf16[2,2,64,512]{3,2,1,0:T(8,128)(2,1)S(1)} %slice.25), channel_id=1, source_target_pairs={{0,2},{1,5},{2,0},{3,7},{4,6},{5,1},{6,4},{7,3},{8,10},{9,13},{10,... | collective-permute-start | bytes 786440 | tf_op jit(solution)/shard_map/ppermute | solution.py:269
  40.1 4.7 %collective-permute-start.4 = (bf16[4,2,64,512]{3,2,1,0:T(8,128)(2,1)S(1)}, bf16[4,2,64,512]{3,2,1,0:T(8,128)(2,1)S(1)}, u32[]{:S(2)}, u32[]{:S(2)}) collective-permute-start(bf16[4,2,64,512]{3,2,1,0:T(8,128)(2,1)S(1)} %get-tuple-element.72), channel_id=1, source_target_pairs={{0,1},{1,0},{2,3},{3,2},{4,5},{5,4},{6,7},{7,6},{8,9},{9,8},{10,11... | collective-permute-start | bytes 1572872 | tf_op jit(solution)/shard_map/ppermute | solution.py:258
  42.3 5.0 %collective-permute-start.12 = (bf16[1,2,64,512]{3,2,1,0:T(8,128)(2,1)S(1)}, bf16[1,2,64,512]{3,2,1,0:T(8,128)(2,1)S(1)}, u32[]{:S(2)}, u32[]{:S(2)}) collective-permute-start(bf16[1,2,64,512]{3,2,1,0:T(8,128)(2,1)S(1)} %slice.31), channel_id=1, source_target_pairs={{0,4},{1,3},{2,6},{3,1},{4,0},{5,7},{6,2},{7,5},{8,12},{9,11},{10,... | collective-permute-start | bytes 393224 | tf_op jit(solution)/shard_map/ppermute | solution.py:269
  45.0 6.4 %collective-permute-start.5 = (bf16[2,2,64,512]{3,2,1,0:T(8,128)(2,1)S(1)}, bf16[2,2,64,512]{3,2,1,0:T(8,128)(2,1)S(1)}, u32[]{:S(2)}, u32[]{:S(2)}) collective-permute-start(bf16[2,2,64,512]{3,2,1,0:T(8,128)(2,1)S(1)} %slice.33), channel_id=1, source_target_pairs={{0,2},{1,5},{2,0},{3,7},{4,6},{5,1},{6,4},{7,3},{8,10},{9,13},{10,... | collective-permute-start | bytes 786440 | tf_op jit(solution)/shard_map/ppermute | solution.py:269
  47.4 8.8 %collective-permute-start.13 = (bf16[1,2,64,512]{3,2,1,0:T(8,128)(2,1)S(1)}, bf16[1,2,64,512]{3,2,1,0:T(8,128)(2,1)S(1)}, u32[]{:S(2)}, u32[]{:S(2)}) collective-permute-start(bf16[1,2,64,512]{3,2,1,0:T(8,128)(2,1)S(1)} %add_convert_fusion.5), channel_id=1, source_target_pairs={{0,8},{1,9},{2,10},{3,11},{4,12},{5,13},{6,14},{7,15},{8,0},{9,1},... | collective-permute-start | bytes 393224 | tf_op jit(solution)/shard_map/ppermute | solution.py:269
  51.5 6.0 %collective-permute-start.6 = (bf16[1,2,64,512]{3,2,1,0:T(8,128)(2,1)S(1)}, bf16[1,2,64,512]{3,2,1,0:T(8,128)(2,1)S(1)}, u32[]{:S(2)}, u32[]{:S(2)}) collective-permute-start(bf16[1,2,64,512]{3,2,1,0:T(8,128)(2,1)S(1)} %slice.35), channel_id=1, source_target_pairs={{0,4},{1,3},{2,6},{3,1},{4,0},{5,7},{6,2},{7,5},{8,12},{9,11},{10,... | collective-permute-start | bytes 393224 | tf_op jit(solution)/shard_map/ppermute | solution.py:269
  56.2 8.6 %collective-permute-start.14 = (bf16[1,2,64,512]{3,2,1,0:T(8,128)(2,1)S(1)}, bf16[1,2,64,512]{3,2,1,0:T(8,128)(2,1)S(1)}, u32[]{:S(2)}, u32[]{:S(2)}) collective-permute-start(bf16[1,2,64,512]{3,2,1,0:T(8,128)(2,1)S(1)} %add_convert_fusion.4.refs_0_), channel_id=1, source_target_pairs={{0,4},{1,3},{2,6},{3,1},{4,0},{5,7},{6,2},{7,5},{8,12},{9,11},{10,... | collective-permute-start | bytes 393224 | tf_op jit(solution)/shard_map/ppermute | solution.py:269
  57.5 8.4 %collective-permute-start.7 = (bf16[1,2,64,512]{3,2,1,0:T(8,128)(2,1)S(1)}, bf16[1,2,64,512]{3,2,1,0:T(8,128)(2,1)S(1)}, u32[]{:S(2)}, u32[]{:S(2)}) collective-permute-start(bf16[1,2,64,512]{3,2,1,0:T(8,128)(2,1)S(1)} %add_convert_fusion.7), channel_id=1, source_target_pairs={{0,8},{1,9},{2,10},{3,11},{4,12},{5,13},{6,14},{7,15},{8,0},{9,1},... | collective-permute-start | bytes 393224 | tf_op jit(solution)/shard_map/ppermute | solution.py:269
  64.8 6.4 %collective-permute-start.15 = (bf16[2,2,64,512]{3,2,1,0:T(8,128)(2,1)S(1)}, bf16[2,2,64,512]{3,2,1,0:T(8,128)(2,1)S(1)}, u32[]{:S(2)}, u32[]{:S(2)}) collective-permute-start(bf16[2,2,64,512]{3,2,1,0:T(8,128)(2,1)S(1)} %pad_maximum_fusion.1), channel_id=1, source_target_pairs={{0,2},{1,5},{2,0},{3,7},{4,6},{5,1},{6,4},{7,3},{8,10},{9,13},{10,... | collective-permute-start | bytes 786440 | tf_op jit(solution)/shard_map/ppermute | solution.py:269
  66.0 5.3 %collective-permute-start.9 = (bf16[1,2,64,512]{3,2,1,0:T(8,128)(2,1)S(1)}, bf16[1,2,64,512]{3,2,1,0:T(8,128)(2,1)S(1)}, u32[]{:S(2)}, u32[]{:S(2)}) collective-permute-start(bf16[1,2,64,512]{3,2,1,0:T(8,128)(2,1)S(1)} %add_convert_fusion.6.refs_1_), channel_id=1, source_target_pairs={{0,4},{1,3},{2,6},{3,1},{4,0},{5,7},{6,2},{7,5},{8,12},{9,11},{10,... | collective-permute-start | bytes 393224 | tf_op jit(solution)/shard_map/ppermute | solution.py:269
  71.3 2.7 %collective-permute-start.18 = (bf16[2,2,64,512]{3,2,1,0:T(8,128)(2,1)S(1)}, bf16[2,2,64,512]{3,2,1,0:T(8,128)(2,1)S(1)}, u32[]{:S(2)}, u32[]{:S(2)}) collective-permute-start(bf16[2,2,64,512]{3,2,1,0:T(8,128)(2,1)S(1)} %collective-permute-done.15.refs_2_), channel_id=1, source_target_pairs={{0,1},{1,0},{2,3},{3,2},{4,5},{5,4},{6,7},{7,6},{8,9},{9,8},{10,11... | collective-permute-start | bytes 786440 | tf_op jit(solution)/shard_map/ppermute | solution.py:258
  71.3 6.4 %collective-permute-start.11 = (bf16[2,2,64,512]{3,2,1,0:T(8,128)(2,1)S(1)}, bf16[2,2,64,512]{3,2,1,0:T(8,128)(2,1)S(1)}, u32[]{:S(2)}, u32[]{:S(2)}) collective-permute-start(bf16[2,2,64,512]{3,2,1,0:T(8,128)(2,1)S(1)} %pad_maximum_fusion), channel_id=1, source_target_pairs={{0,2},{1,5},{2,0},{3,7},{4,6},{5,1},{6,4},{7,3},{8,10},{9,13},{10,... | collective-permute-start | bytes 786440 | tf_op jit(solution)/shard_map/ppermute | solution.py:269
  72.4 1.3 %collective-permute-start.16 = (bf16[1,2,64,512]{3,2,1,0:T(8,128)(2,1)S(1)}, bf16[1,2,64,512]{3,2,1,0:T(8,128)(2,1)S(1)}, u32[]{:S(2)}, u32[]{:S(2)}) collective-permute-start(bf16[1,2,64,512]{3,2,1,0:T(8,128)(2,1)S(1)} %add_convert_fusion.4.refs_0_), channel_id=1, source_target_pairs={{0,1},{1,0},{2,3},{3,2},{4,5},{5,4},{6,7},{7,6},{8,9},{9,8},{10,11... | collective-permute-start | bytes 393224 | tf_op jit(solution)/shard_map/ppermute | solution.py:258
  72.4 1.5 %collective-permute-start.17 = (bf16[1,2,64,512]{3,2,1,0:T(8,128)(2,1)S(1)}, bf16[1,2,64,512]{3,2,1,0:T(8,128)(2,1)S(1)}, u32[]{:S(2)}, u32[]{:S(2)}) collective-permute-start(bf16[1,2,64,512]{3,2,1,0:T(8,128)(2,1)S(1)} %collective-permute-done.14.refs_1_), channel_id=1, source_target_pairs={{0,1},{1,0},{2,3},{3,2},{4,5},{5,4},{6,7},{7,6},{8,9},{9,8},{10,11... | collective-permute-start | bytes 393224 | tf_op jit(solution)/shard_map/ppermute | solution.py:258
  77.7 2.1 %collective-permute-start.19 = (bf16[2,2,64,512]{3,2,1,0:T(8,128)(2,1)S(1)}, bf16[2,2,64,512]{3,2,1,0:T(8,128)(2,1)S(1)}, u32[]{:S(2)}, u32[]{:S(2)}) collective-permute-start(bf16[2,2,64,512]{3,2,1,0:T(8,128)(2,1)S(1)} %collective-permute-done.11.refs_3_), channel_id=1, source_target_pairs={{0,1},{1,0},{2,3},{3,2},{4,5},{5,4},{6,7},{7,6},{8,9},{9,8},{10,11... | collective-permute-start | bytes 786440 | tf_op jit(solution)/shard_map/ppermute | solution.py:258
  77.7 2.1 %collective-permute-start.8 = (bf16[1,2,64,512]{3,2,1,0:T(8,128)(2,1)S(1)}, bf16[1,2,64,512]{3,2,1,0:T(8,128)(2,1)S(1)}, u32[]{:S(2)}, u32[]{:S(2)}) collective-permute-start(bf16[1,2,64,512]{3,2,1,0:T(8,128)(2,1)S(1)} %add_convert_fusion.6.refs_1_), channel_id=1, source_target_pairs={{0,1},{1,0},{2,3},{3,2},{4,5},{5,4},{6,7},{7,6},{8,9},{9,8},{10,11... | collective-permute-start | bytes 393224 | tf_op jit(solution)/shard_map/ppermute | solution.py:258
  78.2 1.6 %collective-permute-start.10 = (bf16[1,2,64,512]{3,2,1,0:T(8,128)(2,1)S(1)}, bf16[1,2,64,512]{3,2,1,0:T(8,128)(2,1)S(1)}, u32[]{:S(2)}, u32[]{:S(2)}) collective-permute-start(bf16[1,2,64,512]{3,2,1,0:T(8,128)(2,1)S(1)} %collective-permute-done.9.refs_2_), channel_id=1, source_target_pairs={{0,1},{1,0},{2,3},{3,2},{4,5},{5,4},{6,7},{7,6},{8,9},{9,8},{10,11... | collective-permute-start | bytes 393224 | tf_op jit(solution)/shard_map/ppermute | solution.py:258
  (9 other events, 38.7 us)

commit v10 on v9

--- a/solution.py
+++ b/solution.py
@@ -143,9 +143,10 @@
 
 
 def mesh_kernel(
-    perm, x, embed_t, weights_all, h_sum, message_w, up_w, gain, mesh_lat, cot, grad_update,
+    x, embed_t, weights_all, h_sum, message_w, up_w, gain, mesh_lat, cot, grad_update,
     sent, mesh_grad, grad_gain, gathered, grad_aggregate, normed, grad_pre_up, update, slope, stack,
 ):
+    perm = chunk_order()
     points = x.shape[1]
     first = weights_all.shape[1] - points
     total = h_sum[...] + halo_part(x, embed_t, weights_all[:, first:], slope)
@@ -172,9 +173,10 @@
 
 
 def tail_kernel(
-    perm, gathered, grad_aggregate, normed, grad_pre_up, update, message_w, out_w, mesh_lat, cot,
+    gathered, grad_aggregate, normed, grad_pre_up, update, message_w, out_w, mesh_lat, cot,
     kept, back, mesh_new, grad_out, stack,
 ):
+    perm = chunk_order()
     mine = rows_of_half(perm[0] // 4, stack.shape[1])
     stack[0] = contract(gathered[:, mine], grad_aggregate[...], 0, 0).astype(BF)
     stack[1] = contract(normed[:, mine], grad_pre_up[...], 0, 0).astype(BF)
@@ -210,9 +212,10 @@
 
 
 def grid_kernel(
-    perm, back, weights_all, slope_own, slope_west, slope_east, x_own, x_west, x_east, grad_gain, grad_out,
+    back, weights_all, slope_own, slope_west, slope_east, x_own, x_west, x_east, grad_gain, grad_out,
     sent, grad_pre, stack,
 ):
+    perm = chunk_order()
     for slope, at, all_at in points_of(slope_own, slope_west, slope_east):
         hidden = contract(back[...], weights_all[:, all_at], 1, 0)
         grad_pre[:, all_at] = (hidden * slope[:, at].astype(F32)).astype(BF)
@@ -222,18 +225,25 @@
     to_chunks(sent, stack, perm, 4)
 
 
-def grid_kept_kernel(perm, grad_pre, x_own, x_west, x_east, grad_gain, grad_out, kept, stack):
-    half = perm[0] // 4
-    stack[0] = grad_out[rows_of_half(half, stack.shape[1]), :].astype(F32)
-    embed_rows(half, (x_own, x_west, x_east), grad_pre, grad_gain, stack.at[1])
-    to_chunks(kept, stack, perm, 0)
-
-
-def order_mesh_kernel(perm, *refs):
-    from_chunks(refs[-2:], refs[:-2], perm)
-
-
-def order_grid_kernel(half, behind, perm, *refs):
+def grid_kept_kernel(grad_pre, x_own, x_west, x_east, grad_gain, sums):
+    perm = chunk_order()
+    embed_rows(perm[0] // 4, (x_own, x_west, x_east), grad_pre, grad_gain, sums)
+
+
+def kept_chunks_kernel(grad_out, sums, kept):
+    perm = chunk_order()
+    count, _, size, _ = kept.shape
+    for j in range(count):
+        kept[j, 0] = grad_out[pl.ds(pl.multiple_of(perm[j] * size, size), size), :]
+        kept[j, 1] = sums[pl.ds(pl.multiple_of((perm[j] & (count - 1)) * size, size), size), :].astype(BF)
+
+
+def order_mesh_kernel(*refs):
+    from_chunks(refs[-2:], refs[:-2], chunk_order())
+
+
+def order_grid_kernel(half, behind, *refs):
+    perm = chunk_order()
     chunks, others, (grad_out, grad_embed, grad_gain) = refs[:3], refs[3:-3], refs[-3:]
     j = 4 * half
     for chunk in chunks:
@@ -277,7 +287,7 @@
         sides.append(2 * low[0] + low[1])
     mine = jnp.where(core == 0, sides[0], sides[1])
     theirs = jnp.where(core == 0, sides[1], sides[0])
-    return jnp.stack([4 * core + (mine ^ j) for j in range(4)] + [4 - 4 * core + (theirs ^ j) for j in range(4)])
+    return [4 * core + (mine ^ j) for j in range(4)] + [4 - 4 * core + (theirs ^ j) for j in range(4)]
 
 
 def added(a, b):
@@ -352,24 +362,23 @@
         600_000_000, 3 * MIB, 16,
     )(x_west, embed_t, weights_all, h_own)
 
-    perm = chunk_order()
     half_chunks = shape((4, 2, latent // 8, latent), BF)
     node_rows = shape((nodes, latent), BF)
     (
         sent_a, mesh_grad, gain_term, gathered, grad_aggregate, normed, grad_pre_up, update, slope_east
     ) = call(
-        mesh_kernel, "mesh_nodes", [SMEM] + [VMEM] * 10,
+        mesh_kernel, "mesh_nodes", [VMEM] * 10,
         [half_chunks, shape((nodes, latent), F32), shape((1, latent), F32)]
         + [node_rows] * 5
         + [shape((latent, side), BF)],
         2_000_000_000, 8 * MIB, 16, [pltpu.VMEM((2, latent // 2, latent), BF)],
-    )(perm, x_east, embed_t, weights_all, h_sum, message_w, up_w, gain.reshape(1, latent), mesh_lat, cot, grad_update)
+    )(x_east, embed_t, weights_all, h_sum, message_w, up_w, gain.reshape(1, latent), mesh_lat, cot, grad_update)
     got_a = core_swapped(sent_a)
     kept_a, back, mesh_new, grad_out_term = call(
-        tail_kernel, "mesh_tail", [SMEM] + [VMEM] * 9,
+        tail_kernel, "mesh_tail", [VMEM] * 9,
         [half_chunks, shape((latent, nodes), BF), node_rows, shape((latent, latent), BF)],
         500_000_000, 3 * MIB, 16, [pltpu.VMEM((2, latent // 2, latent), BF)],
-    )(perm, gathered, grad_aggregate, normed, grad_pre_up, update, message_w, out_w, mesh_lat, cot)
+    )(gathered, grad_aggregate, normed, grad_pre_up, update, message_w, out_w, mesh_lat, cot)
 
     kept_a, back = lax.optimization_barrier((added(kept_a, got_a), back))
     padded = -(-(features + 1) // 128) * 128
@@ -377,21 +386,24 @@
     x_parts = (x_own, x_west, x_east)
     stack = pltpu.VMEM((2, latent // 2, latent), F32)
     sent_b, grad_pre = call(
-        grid_kernel, "grid_points", [SMEM] + [VMEM] * 10, [half_chunks, shape((latent, points), BF)],
+        grid_kernel, "grid_points", [VMEM] * 10, [half_chunks, shape((latent, points), BF)],
         1_600_000_000, 9 * MIB, 20, [stack],
-    )(perm, back, weights_all, slope_own, slope_west, slope_east, *x_parts, gain_term, grad_out_term)
+    )(back, weights_all, slope_own, slope_west, slope_east, *x_parts, gain_term, grad_out_term)
     got_b = core_swapped(sent_b)
-    kept_a, grad_pre = lax.optimization_barrier((halved(kept_a), grad_pre))
+    (sums_b,) = call(
+        grid_kept_kernel, "grid_kept", [VMEM] * 5, [shape((latent // 2, latent), F32)], 800_000_000, 6 * MIB, 16
+    )(grad_pre, *x_parts, gain_term)
+    kept_a, sums_b = lax.optimization_barrier((halved(kept_a), sums_b))
     (kept_b,) = call(
-        grid_kept_kernel, "grid_kept", [SMEM] + [VMEM] * 6, [half_chunks], 800_000_000, 6 * MIB, 16, [stack]
-    )(perm, grad_pre, *x_parts, gain_term, grad_out_term)
+        kept_chunks_kernel, "kept_chunks", [VMEM] * 2, [half_chunks], 8_000_000_000, MIB, 16
+    )(grad_out_term, sums_b)
 
     summed_a = all_summed(kept_a)
     summed_b = all_summed(halved(added(kept_b, got_b)))
     square = shape((latent, latent), F32)
     grad_message, grad_up = call(
-        order_mesh_kernel, "order_a", [SMEM] + [VMEM] * 6, [square, square], 0, 3 * MIB, 16
-    )(perm, *from_both_cores(summed_a))
+        order_mesh_kernel, "order_a", [VMEM] * 6, [square, square], 0, 3 * MIB, 16
+    )(*from_both_cores(summed_a))
     last, grad_message, grad_up = lax.optimization_barrier((summed_b[2], grad_message, grad_up))
     summed_b = (*summed_b[:2], last)
     rows_half = latent // 2
@@ -399,26 +411,23 @@
     outs = [square, shape((features, latent), F32), shape((1, latent), F32)]
 
     def order_b(half, chunks, more, more_specs, aliases):
-        block_of = pl.BlockSpec((rows_half, latent), lambda i, perm: (perm[4 * half] // 4, 0))
+        block_of = pl.BlockSpec((rows_half, latent), lambda i: ((lax.axis_index("lat") & 1) ^ half, 0))
         return pl.pallas_call(
             lambda *refs: order_grid_kernel(half, behind, *refs),
             name="order_b",
-            grid_spec=pltpu.PrefetchScalarGridSpec(
-                num_scalar_prefetch=1,
-                grid=(1,),
-                in_specs=[VMEM] * 3 + more_specs,
-                out_specs=[block_of, block_of, VMEM],
-            ),
+            grid=(1,),
+            in_specs=[VMEM] * 3 + more_specs,
+            out_specs=[block_of, block_of, VMEM],
             out_shape=outs,
             input_output_aliases=aliases,
             compiler_params=pltpu.CompilerParams(vmem_limit_bytes=16 * MIB),
             cost_estimate=pl.CostEstimate(flops=0, bytes_accessed=2 * MIB, transcendentals=0),
-        )(perm, *chunks, *more)
+        )(*chunks, *more)
 
     from_other = [core_swapped(chunk) for chunk in summed_b]
     held = order_b(0, summed_b, (), [], {})
     grad_out, grad_embed, grad_gain = order_b(
-        1, from_other, (held[2], held[0], held[1]), [VMEM] + [pl.BlockSpec(memory_space=pl.ANY)] * 2, {5: 0, 6: 1}
+        1, from_other, (held[2], held[0], held[1]), [VMEM] + [pl.BlockSpec(memory_space=pl.ANY)] * 2, {4: 0, 5: 1}
     )
     return (mesh_new, mesh_grad, grad_embed, grad_message, grad_up, grad_out, grad_gain[0])
 

time: 81.7 us -> 80 us (0.979)
  waiting for transfers between devices: 29.7 us -> 36.5 us
  Pallas kernels: 27.1 us -> 21.6 us
  local copies, waits for them, and re-layouts: 4.92 us -> 1.65 us
    unnamed x26 -> x24, local copies, waits for them, and re-layouts: 4.77 us -> 1.59 us
    pallas_call x5 -> x6, Pallas kernels: 11.6 us -> 8.86 us  [the longest x1 2.66 us: on_device(): call(mesh_kernel, 'mesh_nodes', [VMEM] * 10, [half_chunks, shape((nodes,...]
    ppermute x1, waiting for transfers between devices: 0.01 us -> 1.97 us  [on_device(): lax.ppermute(to_east, 'lon', [(i, (i + 1) % count) for i in range(count)])]
    ppermute x1, waiting for transfers between devices: 6.76 us -> 8.71 us  [on_device(): lax.ppermute(to_west, 'lon', [((i + 1) % count, i) for i in range(count)])]
    ppermute x10, waiting for transfers between devices: 21.9 us -> 23.9 us  [swapped(): return lax.ppermute(value, ('lon', 'lat'), pairs)]
    pallas_call x2, Pallas kernels: 3.12 us -> 2.06 us  [order_b(): pl.pallas_call(lambda *refs: order_grid_kernel(half, behind, *refs), name...]
    ppermute x8, waiting for transfers between devices: 1.04 us -> 1.94 us  [core_swapped(): lax.ppermute(value, 'lat', [(i, i ^ 1) for i in range(lax.axis_size('lat'...]
  transfers between devices with their start and end apart: 20 -> 20, of which waited for: 11 -> 14; matrix products, arithmetic and copies ran while one was open for 1% -> 1% of each run, Pallas kernels for 26% -> 22%
where the time goes in v10:
time: 80 us; the launch traced here: 79.9 us
  waiting for transfers between devices  36.5 us (46%)
  Pallas kernels  21.6 us (27%)
  starting transfers between devices  17.9 us (22%)
  local copies, waits for them, and re-layouts  1.65 us (2%)
  between operations  1.61 us (2%)
    ppermute x10, waiting for transfers between devices, swapped(): return lax.ppermute(value, ('lon', 'lat'), pairs)  23.9 us
    ppermute x10, starting transfers between devices, swapped(): return lax.ppermute(value, ('lon', 'lat'), pairs)  11.6 us
    ppermute x1, waiting for transfers between devices, on_device(): lax.ppermute(to_west, 'lon', [((i + 1) % count, i) for i in range(count)])  8.71 us
    pallas_call x1, Pallas kernels, on_device(): call(lambda *refs: weights_kernel(rows, cols // block, *refs), 'slot_weig...  3.93 us
    pallas_call x1, Pallas kernels, on_device(): call(own_kernel, 'own_points', [VMEM] * 3, [shape((nodes, latent), F32),...  3.55 us
    ppermute x1, starting transfers between devices, on_device(): lax.ppermute(to_east, 'lon', [(i, (i + 1) % count) for i in range(count)])  3.08 us
    pallas_call x1, Pallas kernels, on_device(): call(mesh_kernel, 'mesh_nodes', [VMEM] * 10, [half_chunks, shape((nodes,...  2.66 us
    pallas_call x1, Pallas kernels, on_device(): call(grid_kernel, 'grid_points', [VMEM] * 10, [half_chunks, shape((latent...  2.14 us
  transfers between devices with their start and end apart: 20, of which 14 were waited for; matrix products, arithmetic and copies ran while one was open for 1% of the time, Pallas kernels for 22%

profile of v10, /device:TPU:0, one launch (start us, length us, event | category | flops | bytes accessed | tf_op | source)
XLA Modules:
  0.0 79.9 jit_solution(11527866834337696592)
XLA Ops:
  0.6 1.5 %copy-done = bf16[8,256,474]{1,0,2:T(8,128)(2,1)S(1)} copy-done((bf16[8,256,474]{1,0,2:T(8,128)(2,1)S(1)}, bf16[8,256,474]{1,0,2:T(8,128)(2,1)}, u32[]{:S(2)}) %copy-start) | copy-done | bytes 1941528
  2.7 3.1 %collective-permute-start.1 = (bf16[474,512]{1,0:T(8,128)(2,1)S(1)}, bf16[474,512]{1,0:T(8,128)(2,1)S(1)}, u32[]{:S(2)}, u32[]{:S(2)}) collective-permute-start(bf16[474,512]{1,0:T(8,128)(2,1)S(1)} %pack_east.1), channel_id=1, source_target_pairs={{0,4},{4,8},{8,12},{12,0},{1,5},{5,9},{9,13},{13,1},{2,6},{6,10},{... | collective-permute-start | bytes 1456136 | tf_op jit(solution)/shard_map/ppermute | solution.py:340
  6.3 2.1 %collective-permute-start = (bf16[474,512]{1,0:T(8,128)(2,1)S(1)}, bf16[474,512]{1,0:T(8,128)(2,1)S(1)}, u32[]{:S(2)}, u32[]{:S(2)}) collective-permute-start(bf16[474,512]{1,0:T(8,128)(2,1)S(1)} %pack_west.1), channel_id=1, source_target_pairs={{4,0},{8,4},{12,8},{0,12},{5,1},{9,5},{13,9},{1,13},{6,2},{10,6},{... | collective-permute-start | bytes 1456136 | tf_op jit(solution)/shard_map/ppermute | solution.py:343
  9.1 3.9 %slot_weights.1 = (bf16[256,3072]{1,0:T(8,128)(2,1)S(1)}, f32[256,512]{1,0:T(8,128)S(1)}) custom-call(s32[32]{0:T(128)S(1)} %copy-done.7, s32[32]{0:T(128)S(1)} %copy-done.8, s32[1]{0:T(128)S(6)} %copy.23.refs_2_, bf16[32,128,128]{2,1,0:T(8,128)(2,1)S(1)} %copy-done.3, bf16[256,512]{1,0:T(8,128)(2,1)S(1)} %copy-done.4, bf16[512,512]{1,0:T(8,128)(2,1)S(1)} %copy-done.2), custom_call_target="tpu_custom_call" | custom-call | flops 200000000 | bytes 4194304 | tf_op jit(solution)/shard_map/slot_weights/pallas_call | solution.py:345
  13.1 1.3 %own_rows.1 = (bf16[474,2048]{1,0:T(8,128)(2,1)S(1)}, bf16[512,474]{1,0:T(8,128)(2,1)S(1)}) custom-call(bf16[474,8,256]{2,1,0:T(8,128)(2,1)S(1)} %bitcast.5, bf16[474,512]{1,0:T(8,128)(2,1)S(1)} %copy-done.10), custom_call_target="tpu_custom_call" | custom-call | flops 1000000000 | bytes 5242880 | tf_op jit(solution)/shard_map/own_rows/pallas_call | solution.py:350
  14.4 3.6 %own_points.1 = (f32[256,512]{1,0:T(8,128)S(1)}, bf16[512,2048]{1,0:T(8,128)(2,1)S(1)}) custom-call(bf16[474,2048]{1,0:T(8,128)(2,1)S(1)} %get-tuple-element.49.x_t.x_own, bf16[512,474]{1,0:T(8,128)(2,1)S(1)} %get-tuple-element.47.embed_t.refs_1_, bf16[256,3072]{1,0:T(8,128)(2,1)S(1)} %get-tuple-element.48.weights_all.refs_2_), custom_call_target="tpu_custom_call" | custom-call | flops 2000000000 | bytes 7340032 | tf_op jit(solution)/shard_map/own_points/pallas_call | solution.py:354
  18.0 2.0 %collective-permute-done.1.refs_0_.x_west = bf16[474,512]{1,0:T(8,128)(2,1)S(1)} collective-permute-done((bf16[474,512]{1,0:T(8,128)(2,1)S(1)}, bf16[474,512]{1,0:T(8,128)(2,1)S(1)}, u32[]{:S(2)}, u32[]{:S(2)}) %collective-permute-start.1) | collective-permute-done | bytes 485408 | tf_op jit(solution)/shard_map/ppermute | solution.py:340
  20.9 8.7 %collective-permute-done.x.x_east = bf16[474,512]{1,0:T(8,128)(2,1)S(1)} collective-permute-done((bf16[474,512]{1,0:T(8,128)(2,1)S(1)}, bf16[474,512]{1,0:T(8,128)(2,1)S(1)}, u32[]{:S(2)}, u32[]{:S(2)}) %collective-permute-start) | collective-permute-done | bytes 485408 | tf_op jit(solution)/shard_map/ppermute | solution.py:343
  29.6 2.7 %mesh_nodes.1 = (bf16[4,2,64,512]{3,2,1,0:T(8,128)(2,1)S(1)}, f32[256,512]{1,0:T(8,128)}, f32[1,512]{1,0:T(1,128)S(1)}, bf16[256,512]{1,0:T(8,128)(2,1)S(1)}, bf...) custom-call(bf16[474,512]{1,0:T(8,128)(2,1)S(1)} %collective-permute, ...), custom_call_target="tpu_custom_call" | custom-call | flops 2000000000 | bytes 8388608 | tf_op jit(solution)/shard_map/mesh_nodes/pallas_call | solution.py:369
  32.3 1.4 %mesh_tail.1 = (bf16[4,2,64,512]{3,2,1,0:T(8,128)(2,1)S(1)}, bf16[512,256]{1,0:T(8,128)(2,1)S(1)}, bf16[256,512]{1,0:T(8,128)(2,1)}, bf16[512,512]{1,0:T(8,128)(2,1)S(1)}) custom-call(bf16[256,512]{1,0:T(8,128)(2,1)S(1)} %get-tuple-element.53.gathered, bf16[256,512]{1,0:T(8,128)(2,1)S(1)} %get-tuple-element.54.grad_aggregate, ...), custom_call_target="tpu_custom_call" | custom-call | flops 500000000 | bytes 3145728 | tf_op jit(solution)/shard_map/mesh_tail/pallas_call | solution.py:377
  34.3 1.6 %collective-permute-start.3 = (bf16[2,2,64,512]{3,2,1,0:T(8,128)(2,1)S(1)}, bf16[2,2,64,512]{3,2,1,0:T(8,128)(2,1)S(1)}, u32[]{:S(2)}, u32[]{:S(2)}) collective-permute-start(bf16[2,2,64,512]{3,2,1,0:T(8,128)(2,1)S(1)} %slice.25), channel_id=1, source_target_pairs={{0,2},{1,5},{2,0},{3,7},{4,6},{5,1},{6,4},{7,3},{8,10},{9,13},{10,... | collective-permute-start | bytes 786440 | tf_op jit(solution)/shard_map/ppermute | solution.py:279
  35.9 2.1 %grid_points.1 = (bf16[4,2,64,512]{3,2,1,0:T(8,128)(2,1)S(1)}, bf16[512,3072]{1,0:T(8,128)(2,1)S(1)}) custom-call(bf16[512,256]{1,0:T(8,128)(2,1)S(1)} %get-tuple-element.65.back, bf16[256,3072]{1,0:T(8,128)(2,1)S(1)} %get-tuple-element.48.weights_all.refs_2_, bf16[512,2048]{1,0:T(8,128)(2,1)S(1)} %get-tuple-element.66.slope_own, ...), custom_call_target="tpu_custom_call" | custom-call | flops 1600000000 | bytes 9437184 | tf_op jit(solution)/shard_map/grid_points/pallas_call | solution.py:388
  38.1 1.2 %grid_kept.1.sums = f32[256,512]{1,0:T(8,128)S(1)} custom-call(bf16[512,3072]{1,0:T(8,128)(2,1)S(1)} %get-tuple-element.70.grad_pre, bf16[474,2048]{1,0:T(8,128)(2,1)S(1)} %get-tuple-element.49.x_t.x_own, bf16[474,512]{1,0:T(8,128)(2,1)S(1)} %collective-permute-done.1.refs_0_.x_west, bf16[474,512]{1,0:T(8,128)(2,1)S(1)} %collective-permute-done.x.x_east, ...), custom_call_target="tpu_custom_call" | custom-call | flops 800000000 | bytes 6291456 | tf_op jit(solution)/shard_map/grid_kept/pallas_call | solution.py:393
  39.3 1.4 %collective-permute-done.3 = bf16[2,2,64,512]{3,2,1,0:T(8,128)(2,1)S(1)} collective-permute-done((bf16[2,2,64,512]{3,2,1,0:T(8,128)(2,1)S(1)}, bf16[2,2,64,512]{3,2,1,0:T(8,128)(2,1)S(1)}, u32[]{:S(2)}, u32[]{:S(2)}) %collective-permute-start.3) | collective-permute-done | bytes 262176 | tf_op jit(solution)/shard_map/ppermute | solution.py:279
  41.8 1.6 %collective-permute-start.5 = (bf16[2,2,64,512]{3,2,1,0:T(8,128)(2,1)S(1)}, bf16[2,2,64,512]{3,2,1,0:T(8,128)(2,1)S(1)}, u32[]{:S(2)}, u32[]{:S(2)}) collective-permute-start(bf16[2,2,64,512]{3,2,1,0:T(8,128)(2,1)S(1)} %slice.33), channel_id=1, source_target_pairs={{0,2},{1,5},{2,0},{3,7},{4,6},{5,1},{6,4},{7,3},{8,10},{9,13},{10,... | collective-permute-start | bytes 786440 | tf_op jit(solution)/shard_map/ppermute | solution.py:279
  43.3 4.0 %collective-permute-done.12 = bf16[1,2,64,512]{3,2,1,0:T(8,128)(2,1)S(1)} collective-permute-done((bf16[1,2,64,512]{3,2,1,0:T(8,128)(2,1)S(1)}, bf16[1,2,64,512]{3,2,1,0:T(8,128)(2,1)S(1)}, u32[]{:S(2)}, u32[]{:S(2)}) %collective-permute-start.12) | collective-permute-done | bytes 131104 | tf_op jit(solution)/shard_map/ppermute | solution.py:279
  47.3 1.7 %collective-permute-start.13 = (bf16[1,2,64,512]{3,2,1,0:T(8,128)(2,1)S(1)}, bf16[1,2,64,512]{3,2,1,0:T(8,128)(2,1)S(1)}, u32[]{:S(2)}, u32[]{:S(2)}) collective-permute-start(bf16[1,2,64,512]{3,2,1,0:T(8,128)(2,1)S(1)} %add_convert_fusion.5), channel_id=1, source_target_pairs={{0,8},{1,9},{2,10},{3,11},{4,12},{5,13},{6,14},{7,15},{8,0},{9,1},... | collective-permute-start | bytes 393224 | tf_op jit(solution)/shard_map/ppermute | solution.py:279
  49.1 1.6 %collective-permute-start.6 = (bf16[1,2,64,512]{3,2,1,0:T(8,128)(2,1)S(1)}, bf16[1,2,64,512]{3,2,1,0:T(8,128)(2,1)S(1)}, u32[]{:S(2)}, u32[]{:S(2)}) collective-permute-start(bf16[1,2,64,512]{3,2,1,0:T(8,128)(2,1)S(1)} %slice.35), channel_id=1, source_target_pairs={{0,4},{1,3},{2,6},{3,1},{4,0},{5,7},{6,2},{7,5},{8,12},{9,11},{10,... | collective-permute-start | bytes 393224 | tf_op jit(solution)/shard_map/ppermute | solution.py:279
  50.8 4.0 %collective-permute-done.13 = bf16[1,2,64,512]{3,2,1,0:T(8,128)(2,1)S(1)} collective-permute-done((bf16[1,2,64,512]{3,2,1,0:T(8,128)(2,1)S(1)}, bf16[1,2,64,512]{3,2,1,0:T(8,128)(2,1)S(1)}, u32[]{:S(2)}, u32[]{:S(2)}) %collective-permute-start.13) | collective-permute-done | bytes 131104 | tf_op jit(solution)/shard_map/ppermute | solution.py:279
  55.5 2.5 %collective-permute-start.7 = (bf16[1,2,64,512]{3,2,1,0:T(8,128)(2,1)S(1)}, bf16[1,2,64,512]{3,2,1,0:T(8,128)(2,1)S(1)}, u32[]{:S(2)}, u32[]{:S(2)}) collective-permute-start(bf16[1,2,64,512]{3,2,1,0:T(8,128)(2,1)S(1)} %add_convert_fusion.7), channel_id=1, source_target_pairs={{0,8},{1,9},{2,10},{3,11},{4,12},{5,13},{6,14},{7,15},{8,0},{9,1},... | collective-permute-start | bytes 393224 | tf_op jit(solution)/shard_map/ppermute | solution.py:279
  58.0 6.0 %collective-permute-done.14.refs_1_ = bf16[1,2,64,512]{3,2,1,0:T(8,128)(2,1)S(1)} collective-permute-done((bf16[1,2,64,512]{3,2,1,0:T(8,128)(2,1)S(1)}, bf16[1,2,64,512]{3,2,1,0:T(8,128)(2,1)S(1)}, u32[]{:S(2)}, u32[]{:S(2)}) %collective-permute-start.14) | collective-permute-done | bytes 131104 | tf_op jit(solution)/shard_map/ppermute | solution.py:279
  65.2 5.3 %collective-permute-done.15.refs_2_ = bf16[2,2,64,512]{3,2,1,0:T(8,128)(2,1)S(1)} collective-permute-done((bf16[2,2,64,512]{3,2,1,0:T(8,128)(2,1)S(1)}, bf16[2,2,64,512]{3,2,1,0:T(8,128)(2,1)S(1)}, u32[]{:S(2)}, u32[]{:S(2)}) %collective-permute-start.15) | collective-permute-done | bytes 262176 | tf_op jit(solution)/shard_map/ppermute | solution.py:279
  72.8 1.5 %order_a.1 = (f32[512,512]{1,0:T(8,128)}, f32[512,512]{1,0:T(8,128)}) custom-call(bf16[1,2,64,512]{3,2,1,0:T(8,128)(2,1)S(1)} %add_convert_fusion.4.refs_0_, bf16[1,2,64,512]{3,2,1,0:T(8,128)(2,1)S(1)} %collective-permute-done.14.refs_1_, bf16[2,2,64,512]{3,2,1,0:T(8,128)(2,1)S(1)} %collective-permute-done.15.refs_2_, ...), custom_call_target="tpu_custom_call" | custom-call | bytes 3145728 | tf_op jit(solution)/shard_map/order_a/pallas_call | solution.py:404
  74.3 2.7 %collective-permute-done.11.refs_2_ = bf16[2,2,64,512]{3,2,1,0:T(8,128)(2,1)S(1)} collective-permute-done((bf16[2,2,64,512]{3,2,1,0:T(8,128)(2,1)S(1)}, bf16[2,2,64,512]{3,2,1,0:T(8,128)(2,1)S(1)}, u32[]{:S(2)}, u32[]{:S(2)}) %collective-permute-start.11) | collective-permute-done | bytes 262176 | tf_op jit(solution)/shard_map/ppermute | solution.py:279
  (68 shorter events, 10.9 us)
Async XLA Ops:
  2.7 17.2 %collective-permute-start.1 = (bf16[474,512]{1,0:T(8,128)(2,1)S(1)}, bf16[474,512]{1,0:T(8,128)(2,1)S(1)}, u32[]{:S(2)}, u32[]{:S(2)}) collective-permute-start(bf16[474,512]{1,0:T(8,128)(2,1)S(1)} %pack_east.1), channel_id=1, source_target_pairs={{0,4},{4,8},{8,12},{12,0},{1,5},{5,9},{9,13},{13,1},{2,6},{6,10},{... | collective-permute-start | bytes 1456136 | tf_op jit(solution)/shard_map/ppermute | solution.py:340
  6.3 23.3 %collective-permute-start = (bf16[474,512]{1,0:T(8,128)(2,1)S(1)}, bf16[474,512]{1,0:T(8,128)(2,1)S(1)}, u32[]{:S(2)}, u32[]{:S(2)}) collective-permute-start(bf16[474,512]{1,0:T(8,128)(2,1)S(1)} %pack_west.1), channel_id=1, source_target_pairs={{4,0},{8,4},{12,8},{0,12},{5,1},{9,5},{13,9},{1,13},{6,2},{10,6},{... | collective-permute-start | bytes 1456136 | tf_op jit(solution)/shard_map/ppermute | solution.py:343
  18.0 11.6 %copy-start.5 = (bf16[512,512]{1,0:T(8,128)(2,1)S(1)}, bf16[512,512]{1,0:T(8,128)(2,1)}, u32[]{:S(2)}) copy-start(bf16[512,512]{1,0:T(8,128)(2,1)} %message_w.3) | copy-start | bytes 1572868
  18.0 11.6 %copy-start.6 = (bf16[256,512]{1,0:T(8,128)(2,1)S(1)}, bf16[256,512]{1,0:T(8,128)(2,1)}, u32[]{:S(2)}) copy-start(bf16[256,512]{1,0:T(8,128)(2,1)} %mesh_lat.3) | copy-start | bytes 786436
  18.0 11.6 %copy-start.9 = (bf16[512,512]{1,0:T(8,128)(2,1)S(1)}, bf16[512,512]{1,0:T(8,128)(2,1)}, u32[]{:S(2)}) copy-start(bf16[512,512]{1,0:T(8,128)(2,1)} %up_w.1) | copy-start | bytes 1572868
  18.0 11.6 %copy-start.11 = (f32[512]{0:T(512)S(1)}, f32[512]{0:T(512)}, u32[]{:S(2)}) copy-start(f32[512]{0:T(512)} %param.22) | copy-start | bytes 6148
  32.3 1.9 %collective-permute-start.2 = (bf16[4,2,64,512]{3,2,1,0:T(8,128)(2,1)S(1)}, bf16[4,2,64,512]{3,2,1,0:T(8,128)(2,1)S(1)}, u32[]{:S(2)}, u32[]{:S(2)}) collective-permute-start(bf16[4,2,64,512]{3,2,1,0:T(8,128)(2,1)S(1)} %get-tuple-element.62), channel_id=1, source_target_pairs={{0,1},{1,0},{2,3},{3,2},{4,5},{5,4},{6,7},{7,6},{8,9},{9,8},{10,11... | collective-permute-start | bytes 1572872 | tf_op jit(solution)/shard_map/ppermute | solution.py:268
  34.3 6.4 %collective-permute-start.3 = (bf16[2,2,64,512]{3,2,1,0:T(8,128)(2,1)S(1)}, bf16[2,2,64,512]{3,2,1,0:T(8,128)(2,1)S(1)}, u32[]{:S(2)}, u32[]{:S(2)}) collective-permute-start(bf16[2,2,64,512]{3,2,1,0:T(8,128)(2,1)S(1)} %slice.25), channel_id=1, source_target_pairs={{0,2},{1,5},{2,0},{3,7},{4,6},{5,1},{6,4},{7,3},{8,10},{9,13},{10,... | collective-permute-start | bytes 786440 | tf_op jit(solution)/shard_map/ppermute | solution.py:279
  38.0 3.5 %collective-permute-start.4 = (bf16[4,2,64,512]{3,2,1,0:T(8,128)(2,1)S(1)}, bf16[4,2,64,512]{3,2,1,0:T(8,128)(2,1)S(1)}, u32[]{:S(2)}, u32[]{:S(2)}) collective-permute-start(bf16[4,2,64,512]{3,2,1,0:T(8,128)(2,1)S(1)} %get-tuple-element.72), channel_id=1, source_target_pairs={{0,1},{1,0},{2,3},{3,2},{4,5},{5,4},{6,7},{7,6},{8,9},{9,8},{10,11... | collective-permute-start | bytes 1572872 | tf_op jit(solution)/shard_map/ppermute | solution.py:268
  40.9 6.4 %collective-permute-start.12 = (bf16[1,2,64,512]{3,2,1,0:T(8,128)(2,1)S(1)}, bf16[1,2,64,512]{3,2,1,0:T(8,128)(2,1)S(1)}, u32[]{:S(2)}, u32[]{:S(2)}) collective-permute-start(bf16[1,2,64,512]{3,2,1,0:T(8,128)(2,1)S(1)} %slice.31), channel_id=1, source_target_pairs={{0,4},{1,3},{2,6},{3,1},{4,0},{5,7},{6,2},{7,5},{8,12},{9,11},{10,... | collective-permute-start | bytes 393224 | tf_op jit(solution)/shard_map/ppermute | solution.py:279
  41.8 7.3 %collective-permute-start.5 = (bf16[2,2,64,512]{3,2,1,0:T(8,128)(2,1)S(1)}, bf16[2,2,64,512]{3,2,1,0:T(8,128)(2,1)S(1)}, u32[]{:S(2)}, u32[]{:S(2)}) collective-permute-start(bf16[2,2,64,512]{3,2,1,0:T(8,128)(2,1)S(1)} %slice.33), channel_id=1, source_target_pairs={{0,2},{1,5},{2,0},{3,7},{4,6},{5,1},{6,4},{7,3},{8,10},{9,13},{10,... | collective-permute-start | bytes 786440 | tf_op jit(solution)/shard_map/ppermute | solution.py:279
  47.3 7.4 %collective-permute-start.13 = (bf16[1,2,64,512]{3,2,1,0:T(8,128)(2,1)S(1)}, bf16[1,2,64,512]{3,2,1,0:T(8,128)(2,1)S(1)}, u32[]{:S(2)}, u32[]{:S(2)}) collective-permute-start(bf16[1,2,64,512]{3,2,1,0:T(8,128)(2,1)S(1)} %add_convert_fusion.5), channel_id=1, source_target_pairs={{0,8},{1,9},{2,10},{3,11},{4,12},{5,13},{6,14},{7,15},{8,0},{9,1},... | collective-permute-start | bytes 393224 | tf_op jit(solution)/shard_map/ppermute | solution.py:279
  49.1 6.3 %collective-permute-start.6 = (bf16[1,2,64,512]{3,2,1,0:T(8,128)(2,1)S(1)}, bf16[1,2,64,512]{3,2,1,0:T(8,128)(2,1)S(1)}, u32[]{:S(2)}, u32[]{:S(2)}) collective-permute-start(bf16[1,2,64,512]{3,2,1,0:T(8,128)(2,1)S(1)} %slice.35), channel_id=1, source_target_pairs={{0,4},{1,3},{2,6},{3,1},{4,0},{5,7},{6,2},{7,5},{8,12},{9,11},{10,... | collective-permute-start | bytes 393224 | tf_op jit(solution)/shard_map/ppermute | solution.py:279
  54.8 9.2 %collective-permute-start.14 = (bf16[1,2,64,512]{3,2,1,0:T(8,128)(2,1)S(1)}, bf16[1,2,64,512]{3,2,1,0:T(8,128)(2,1)S(1)}, u32[]{:S(2)}, u32[]{:S(2)}) collective-permute-start(bf16[1,2,64,512]{3,2,1,0:T(8,128)(2,1)S(1)} %add_convert_fusion.4.refs_0_), channel_id=1, source_target_pairs={{0,4},{1,3},{2,6},{3,1},{4,0},{5,7},{6,2},{7,5},{8,12},{9,11},{10,... | collective-permute-start | bytes 393224 | tf_op jit(solution)/shard_map/ppermute | solution.py:279
  55.5 9.0 %collective-permute-start.7 = (bf16[1,2,64,512]{3,2,1,0:T(8,128)(2,1)S(1)}, bf16[1,2,64,512]{3,2,1,0:T(8,128)(2,1)S(1)}, u32[]{:S(2)}, u32[]{:S(2)}) collective-permute-start(bf16[1,2,64,512]{3,2,1,0:T(8,128)(2,1)S(1)} %add_convert_fusion.7), channel_id=1, source_target_pairs={{0,8},{1,9},{2,10},{3,11},{4,12},{5,13},{6,14},{7,15},{8,0},{9,1},... | collective-permute-start | bytes 393224 | tf_op jit(solution)/shard_map/ppermute | solution.py:279
  64.0 6.4 %collective-permute-start.15 = (bf16[2,2,64,512]{3,2,1,0:T(8,128)(2,1)S(1)}, bf16[2,2,64,512]{3,2,1,0:T(8,128)(2,1)S(1)}, u32[]{:S(2)}, u32[]{:S(2)}) collective-permute-start(bf16[2,2,64,512]{3,2,1,0:T(8,128)(2,1)S(1)} %pad_maximum_fusion.1), channel_id=1, source_target_pairs={{0,2},{1,5},{2,0},{3,7},{4,6},{5,1},{6,4},{7,3},{8,10},{9,13},{10,... | collective-permute-start | bytes 786440 | tf_op jit(solution)/shard_map/ppermute | solution.py:279
  64.5 5.9 %collective-permute-start.9 = (bf16[1,2,64,512]{3,2,1,0:T(8,128)(2,1)S(1)}, bf16[1,2,64,512]{3,2,1,0:T(8,128)(2,1)S(1)}, u32[]{:S(2)}, u32[]{:S(2)}) collective-permute-start(bf16[1,2,64,512]{3,2,1,0:T(8,128)(2,1)S(1)} %add_convert_fusion.6.refs_0_), channel_id=1, source_target_pairs={{0,4},{1,3},{2,6},{3,1},{4,0},{5,7},{6,2},{7,5},{8,12},{9,11},{10,... | collective-permute-start | bytes 393224 | tf_op jit(solution)/shard_map/ppermute | solution.py:279
  70.5 2.4 %collective-permute-start.18 = (bf16[2,2,64,512]{3,2,1,0:T(8,128)(2,1)S(1)}, bf16[2,2,64,512]{3,2,1,0:T(8,128)(2,1)S(1)}, u32[]{:S(2)}, u32[]{:S(2)}) collective-permute-start(bf16[2,2,64,512]{3,2,1,0:T(8,128)(2,1)S(1)} %collective-permute-done.15.refs_2_), channel_id=1, source_target_pairs={{0,1},{1,0},{2,3},{3,2},{4,5},{5,4},{6,7},{7,6},{8,9},{9,8},{10,11... | collective-permute-start | bytes 786440 | tf_op jit(solution)/shard_map/ppermute | solution.py:268
  70.5 6.4 %collective-permute-start.11 = (bf16[2,2,64,512]{3,2,1,0:T(8,128)(2,1)S(1)}, bf16[2,2,64,512]{3,2,1,0:T(8,128)(2,1)S(1)}, u32[]{:S(2)}, u32[]{:S(2)}) collective-permute-start(bf16[2,2,64,512]{3,2,1,0:T(8,128)(2,1)S(1)} %pad_maximum_fusion), channel_id=1, source_target_pairs={{0,2},{1,5},{2,0},{3,7},{4,6},{5,1},{6,4},{7,3},{8,10},{9,13},{10,... | collective-permute-start | bytes 786440 | tf_op jit(solution)/shard_map/ppermute | solution.py:279
  71.3 1.3 %collective-permute-start.16 = (bf16[1,2,64,512]{3,2,1,0:T(8,128)(2,1)S(1)}, bf16[1,2,64,512]{3,2,1,0:T(8,128)(2,1)S(1)}, u32[]{:S(2)}, u32[]{:S(2)}) collective-permute-start(bf16[1,2,64,512]{3,2,1,0:T(8,128)(2,1)S(1)} %add_convert_fusion.4.refs_0_), channel_id=1, source_target_pairs={{0,1},{1,0},{2,3},{3,2},{4,5},{5,4},{6,7},{7,6},{8,9},{9,8},{10,11... | collective-permute-start | bytes 393224 | tf_op jit(solution)/shard_map/ppermute | solution.py:268
  71.3 1.5 %collective-permute-start.17 = (bf16[1,2,64,512]{3,2,1,0:T(8,128)(2,1)S(1)}, bf16[1,2,64,512]{3,2,1,0:T(8,128)(2,1)S(1)}, u32[]{:S(2)}, u32[]{:S(2)}) collective-permute-start(bf16[1,2,64,512]{3,2,1,0:T(8,128)(2,1)S(1)} %collective-permute-done.14.refs_1_), channel_id=1, source_target_pairs={{0,1},{1,0},{2,3},{3,2},{4,5},{5,4},{6,7},{7,6},{8,9},{9,8},{10,11... | collective-permute-start | bytes 393224 | tf_op jit(solution)/shard_map/ppermute | solution.py:268
  76.9 1.9 %collective-permute-start.19 = (bf16[2,2,64,512]{3,2,1,0:T(8,128)(2,1)S(1)}, bf16[2,2,64,512]{3,2,1,0:T(8,128)(2,1)S(1)}, u32[]{:S(2)}, u32[]{:S(2)}) collective-permute-start(bf16[2,2,64,512]{3,2,1,0:T(8,128)(2,1)S(1)} %collective-permute-done.11.refs_2_), channel_id=1, source_target_pairs={{0,1},{1,0},{2,3},{3,2},{4,5},{5,4},{6,7},{7,6},{8,9},{9,8},{10,11... | collective-permute-start | bytes 786440 | tf_op jit(solution)/shard_map/ppermute | solution.py:268
  76.9 1.7 %collective-permute-start.8 = (bf16[1,2,64,512]{3,2,1,0:T(8,128)(2,1)S(1)}, bf16[1,2,64,512]{3,2,1,0:T(8,128)(2,1)S(1)}, u32[]{:S(2)}, u32[]{:S(2)}) collective-permute-start(bf16[1,2,64,512]{3,2,1,0:T(8,128)(2,1)S(1)} %add_convert_fusion.6.refs_0_), channel_id=1, source_target_pairs={{0,1},{1,0},{2,3},{3,2},{4,5},{5,4},{6,7},{7,6},{8,9},{9,8},{10,11... | collective-permute-start | bytes 393224 | tf_op jit(solution)/shard_map/ppermute | solution.py:268
  77.4 1.4 %collective-permute-start.10 = (bf16[1,2,64,512]{3,2,1,0:T(8,128)(2,1)S(1)}, bf16[1,2,64,512]{3,2,1,0:T(8,128)(2,1)S(1)}, u32[]{:S(2)}, u32[]{:S(2)}) collective-permute-start(bf16[1,2,64,512]{3,2,1,0:T(8,128)(2,1)S(1)} %collective-permute-done.9.refs_1_), channel_id=1, source_target_pairs={{0,1},{1,0},{2,3},{3,2},{4,5},{5,4},{6,7},{7,6},{8,9},{9,8},{10,11... | collective-permute-start | bytes 393224 | tf_op jit(solution)/shard_map/ppermute | solution.py:268
  (8 other events, 56.7 us)

commit v11 on v10

--- a/solution.py
+++ b/solution.py
@@ -298,11 +298,17 @@
     return added(kept[:2], swapped(kept[2:], 0))
 
 
-def all_summed(kept):
-    mine = added(kept[:1], swapped(kept[1:], 1))
+def quartered(kept):
+    return added(kept[:1], swapped(kept[1:], 1))
+
+
+def exchanged(mine):
     for step in range(2, len(role_steps()[0])):
         mine = added(mine, swapped(mine, step))
-    second = swapped(mine, 1)
+    return mine
+
+
+def gathered_back(mine, second):
     return mine, second, swapped(jnp.concatenate([mine, second]), 0)
 
 
@@ -398,8 +404,14 @@
         kept_chunks_kernel, "kept_chunks", [VMEM] * 2, [half_chunks], 8_000_000_000, MIB, 16
     )(grad_out_term, sums_b)
 
-    summed_a = all_summed(kept_a)
-    summed_b = all_summed(halved(added(kept_b, got_b)))
+    mine_a = exchanged(quartered(kept_a))
+    mine_b = quartered(halved(added(kept_b, got_b)))
+    mine_a, _ = lax.optimization_barrier((mine_a, mine_b))
+    second_a = swapped(mine_a, 1)
+    mine_b = exchanged(mine_b)
+    second_a, _ = lax.optimization_barrier((second_a, mine_b))
+    summed_a = gathered_back(mine_a, second_a)
+    summed_b = gathered_back(mine_b, swapped(mine_b, 1))
     square = shape((latent, latent), F32)
     grad_message, grad_up = call(
         order_mesh_kernel, "order_a", [VMEM] * 6, [square, square], 0, 3 * MIB, 16

time: 80 us -> 83.4 us (1.042)
  waiting for transfers between devices: 36.5 us -> 38.9 us
  starting transfers between devices: 17.9 us -> 19.5 us
    ppermute x10, waiting for transfers between devices: 23.9 us -> 25.6 us  [swapped(): return lax.ppermute(value, ('lon', 'lat'), pairs)]
    ppermute x10, starting transfers between devices: 11.6 us -> 13.3 us  [swapped(): return lax.ppermute(value, ('lon', 'lat'), pairs)]
  transfers between devices with their start and end apart: 20 -> 20, of which waited for: 14 -> 15; matrix products, arithmetic and copies ran while one was open for 1% -> 0% of each run, Pallas kernels for 22% -> 20%
where the time goes in v11:
time: 83.4 us; the launch traced here: 83.2 us
  waiting for transfers between devices  38.9 us (47%)
  Pallas kernels  21 us (25%)
  starting transfers between devices  19.5 us (23%)
  local copies, waits for them, and re-layouts  1.65 us (2%)
  between operations  1.61 us (2%)
    ppermute x10, waiting for transfers between devices, swapped(): return lax.ppermute(value, ('lon', 'lat'), pairs)  25.6 us
    ppermute x10, starting transfers between devices, swapped(): return lax.ppermute(value, ('lon', 'lat'), pairs)  13.3 us
    ppermute x1, waiting for transfers between devices, on_device(): lax.ppermute(to_west, 'lon', [((i + 1) % count, i) for i in range(count)])  8.71 us
    pallas_call x1, Pallas kernels, on_device(): call(own_kernel, 'own_points', [VMEM] * 3, [shape((nodes, latent), F32),...  3.56 us
    pallas_call x1, Pallas kernels, on_device(): call(lambda *refs: weights_kernel(rows, cols // block, *refs), 'slot_weig...  3.27 us
    ppermute x1, starting transfers between devices, on_device(): lax.ppermute(to_east, 'lon', [(i, (i + 1) % count) for i in range(count)])  3.08 us
    pallas_call x1, Pallas kernels, on_device(): call(mesh_kernel, 'mesh_nodes', [VMEM] * 10, [half_chunks, shape((nodes,...  2.66 us
    ppermute x1, waiting for transfers between devices, on_device(): lax.ppermute(to_east, 'lon', [(i, (i + 1) % count) for i in range(count)])  2.62 us
  transfers between devices with their start and end apart: 20, of which 15 were waited for; matrix products, arithmetic and copies ran while one was open for 0% of the time, Pallas kernels for 20%

profile of v11, /device:TPU:0, one launch (start us, length us, event | category | flops | bytes accessed | tf_op | source)
XLA Modules:
  0.0 83.2 jit_solution(366675032039896442)
XLA Ops:
  0.6 1.5 %copy-done = bf16[8,256,474]{1,0,2:T(8,128)(2,1)S(1)} copy-done((bf16[8,256,474]{1,0,2:T(8,128)(2,1)S(1)}, bf16[8,256,474]{1,0,2:T(8,128)(2,1)}, u32[]{:S(2)}) %copy-start) | copy-done | bytes 1941528
  2.7 3.1 %collective-permute-start.1 = (bf16[474,512]{1,0:T(8,128)(2,1)S(1)}, bf16[474,512]{1,0:T(8,128)(2,1)S(1)}, u32[]{:S(2)}, u32[]{:S(2)}) collective-permute-start(bf16[474,512]{1,0:T(8,128)(2,1)S(1)} %pack_east.1), channel_id=1, source_target_pairs={{0,4},{4,8},{8,12},{12,0},{1,5},{5,9},{9,13},{13,1},{2,6},{6,10},{... | collective-permute-start | bytes 1456136 | tf_op jit(solution)/shard_map/ppermute | solution.py:346
  6.3 2.1 %collective-permute-start = (bf16[474,512]{1,0:T(8,128)(2,1)S(1)}, bf16[474,512]{1,0:T(8,128)(2,1)S(1)}, u32[]{:S(2)}, u32[]{:S(2)}) collective-permute-start(bf16[474,512]{1,0:T(8,128)(2,1)S(1)} %pack_west.1), channel_id=1, source_target_pairs={{4,0},{8,4},{12,8},{0,12},{5,1},{9,5},{13,9},{1,13},{6,2},{10,6},{... | collective-permute-start | bytes 1456136 | tf_op jit(solution)/shard_map/ppermute | solution.py:349
  9.1 3.3 %slot_weights.1 = (bf16[256,3072]{1,0:T(8,128)(2,1)S(1)}, f32[256,512]{1,0:T(8,128)S(1)}) custom-call(s32[32]{0:T(128)S(1)} %copy-done.7, s32[32]{0:T(128)S(1)} %copy-done.8, s32[1]{0:T(128)S(6)} %copy.23.refs_2_, bf16[32,128,128]{2,1,0:T(8,128)(2,1)S(1)} %copy-done.3, bf16[256,512]{1,0:T(8,128)(2,1)S(1)} %copy-done.4, bf16[512,512]{1,0:T(8,128)(2,1)S(1)} %copy-done.2), custom_call_target="tpu_custom_call" | custom-call | flops 200000000 | bytes 4194304 | tf_op jit(solution)/shard_map/slot_weights/pallas_call | solution.py:351
  13.7 3.6 %own_points.1 = (f32[256,512]{1,0:T(8,128)S(1)}, bf16[512,2048]{1,0:T(8,128)(2,1)S(1)}) custom-call(bf16[474,2048]{1,0:T(8,128)(2,1)S(1)} %get-tuple-element.51.x_t.x_own, bf16[512,474]{1,0:T(8,128)(2,1)S(1)} %get-tuple-element.49.embed_t.refs_1_, bf16[256,3072]{1,0:T(8,128)(2,1)S(1)} %get-tuple-element.50.weights_all.refs_2_), custom_call_target="tpu_custom_call" | custom-call | flops 2000000000 | bytes 7340032 | tf_op jit(solution)/shard_map/own_points/pallas_call | solution.py:360
  17.4 2.6 %collective-permute-done.1.refs_0_.x_west = bf16[474,512]{1,0:T(8,128)(2,1)S(1)} collective-permute-done((bf16[474,512]{1,0:T(8,128)(2,1)S(1)}, bf16[474,512]{1,0:T(8,128)(2,1)S(1)}, u32[]{:S(2)}, u32[]{:S(2)}) %collective-permute-start.1) | collective-permute-done | bytes 485408 | tf_op jit(solution)/shard_map/ppermute | solution.py:346
  20.9 8.7 %collective-permute-done.x.x_east = bf16[474,512]{1,0:T(8,128)(2,1)S(1)} collective-permute-done((bf16[474,512]{1,0:T(8,128)(2,1)S(1)}, bf16[474,512]{1,0:T(8,128)(2,1)S(1)}, u32[]{:S(2)}, u32[]{:S(2)}) %collective-permute-start) | collective-permute-done | bytes 485408 | tf_op jit(solution)/shard_map/ppermute | solution.py:349
  29.6 2.7 %mesh_nodes.1 = (bf16[4,2,64,512]{3,2,1,0:T(8,128)(2,1)S(1)}, f32[256,512]{1,0:T(8,128)}, f32[1,512]{1,0:T(1,128)S(1)}, bf16[256,512]{1,0:T(8,128)(2,1)S(1)}, bf...) custom-call(bf16[474,512]{1,0:T(8,128)(2,1)S(1)} %collective-permute, ...), custom_call_target="tpu_custom_call" | custom-call | flops 2000000000 | bytes 8388608 | tf_op jit(solution)/shard_map/mesh_nodes/pallas_call | solution.py:375
  32.3 1.4 %mesh_tail.1 = (bf16[4,2,64,512]{3,2,1,0:T(8,128)(2,1)S(1)}, bf16[512,256]{1,0:T(8,128)(2,1)S(1)}, bf16[256,512]{1,0:T(8,128)(2,1)}, bf16[512,512]{1,0:T(8,128)(2,1)S(1)}) custom-call(bf16[256,512]{1,0:T(8,128)(2,1)S(1)} %get-tuple-element.55.gathered, bf16[256,512]{1,0:T(8,128)(2,1)S(1)} %get-tuple-element.56.grad_aggregate, ...), custom_call_target="tpu_custom_call" | custom-call | flops 500000000 | bytes 3145728 | tf_op jit(solution)/shard_map/mesh_tail/pallas_call | solution.py:383
  34.3 1.6 %collective-permute-start.3 = (bf16[2,2,64,512]{3,2,1,0:T(8,128)(2,1)S(1)}, bf16[2,2,64,512]{3,2,1,0:T(8,128)(2,1)S(1)}, u32[]{:S(2)}, u32[]{:S(2)}) collective-permute-start(bf16[2,2,64,512]{3,2,1,0:T(8,128)(2,1)S(1)} %slice.25), channel_id=1, source_target_pairs={{0,2},{1,5},{2,0},{3,7},{4,6},{5,1},{6,4},{7,3},{8,10},{9,13},{10,... | collective-permute-start | bytes 786440 | tf_op jit(solution)/shard_map/ppermute | solution.py:279
  35.9 2.1 %grid_points.1 = (bf16[4,2,64,512]{3,2,1,0:T(8,128)(2,1)S(1)}, bf16[512,3072]{1,0:T(8,128)(2,1)S(1)}) custom-call(bf16[512,256]{1,0:T(8,128)(2,1)S(1)} %get-tuple-element.67.back, bf16[256,3072]{1,0:T(8,128)(2,1)S(1)} %get-tuple-element.50.weights_all.refs_2_, bf16[512,2048]{1,0:T(8,128)(2,1)S(1)} %get-tuple-element.68.slope_own, ...), custom_call_target="tpu_custom_call" | custom-call | flops 1600000000 | bytes 9437184 | tf_op jit(solution)/shard_map/grid_points/pallas_call | solution.py:394
  39.3 1.4 %collective-permute-done.3 = bf16[2,2,64,512]{3,2,1,0:T(8,128)(2,1)S(1)} collective-permute-done((bf16[2,2,64,512]{3,2,1,0:T(8,128)(2,1)S(1)}, bf16[2,2,64,512]{3,2,1,0:T(8,128)(2,1)S(1)}, u32[]{:S(2)}, u32[]{:S(2)}) %collective-permute-start.3) | collective-permute-done | bytes 262176 | tf_op jit(solution)/shard_map/ppermute | solution.py:279
  41.1 1.6 %collective-permute-start.5 = (bf16[2,2,64,512]{3,2,1,0:T(8,128)(2,1)S(1)}, bf16[2,2,64,512]{3,2,1,0:T(8,128)(2,1)S(1)}, u32[]{:S(2)}, u32[]{:S(2)}) collective-permute-start(bf16[2,2,64,512]{3,2,1,0:T(8,128)(2,1)S(1)} %slice.33), channel_id=1, source_target_pairs={{0,2},{1,5},{2,0},{3,7},{4,6},{5,1},{6,4},{7,3},{8,10},{9,13},{10,... | collective-permute-start | bytes 786440 | tf_op jit(solution)/shard_map/ppermute | solution.py:279
  43.4 4.3 %collective-permute-done.5 = bf16[2,2,64,512]{3,2,1,0:T(8,128)(2,1)S(1)} collective-permute-done((bf16[2,2,64,512]{3,2,1,0:T(8,128)(2,1)S(1)}, bf16[2,2,64,512]{3,2,1,0:T(8,128)(2,1)S(1)}, u32[]{:S(2)}, u32[]{:S(2)}) %collective-permute-start.5) | collective-permute-done | bytes 262176 | tf_op jit(solution)/shard_map/ppermute | solution.py:279
  47.8 1.5 %collective-permute-start.6 = (bf16[1,2,64,512]{3,2,1,0:T(8,128)(2,1)S(1)}, bf16[1,2,64,512]{3,2,1,0:T(8,128)(2,1)S(1)}, u32[]{:S(2)}, u32[]{:S(2)}) collective-permute-start(bf16[1,2,64,512]{3,2,1,0:T(8,128)(2,1)S(1)} %slice.35), channel_id=1, source_target_pairs={{0,4},{1,3},{2,6},{3,1},{4,0},{5,7},{6,2},{7,5},{8,12},{9,11},{10,... | collective-permute-start | bytes 393224 | tf_op jit(solution)/shard_map/ppermute | solution.py:279
  49.3 1.8 %collective-permute-start.13 = (bf16[1,2,64,512]{3,2,1,0:T(8,128)(2,1)S(1)}, bf16[1,2,64,512]{3,2,1,0:T(8,128)(2,1)S(1)}, u32[]{:S(2)}, u32[]{:S(2)}) collective-permute-start(bf16[1,2,64,512]{3,2,1,0:T(8,128)(2,1)S(1)} %add_convert_fusion.5), channel_id=1, source_target_pairs={{0,8},{1,9},{2,10},{3,11},{4,12},{5,13},{6,14},{7,15},{8,0},{9,1},... | collective-permute-start | bytes 393224 | tf_op jit(solution)/shard_map/ppermute | solution.py:279
  51.0 1.9 %collective-permute-done.6 = bf16[1,2,64,512]{3,2,1,0:T(8,128)(2,1)S(1)} collective-permute-done((bf16[1,2,64,512]{3,2,1,0:T(8,128)(2,1)S(1)}, bf16[1,2,64,512]{3,2,1,0:T(8,128)(2,1)S(1)}, u32[]{:S(2)}, u32[]{:S(2)}) %collective-permute-start.6) | collective-permute-done | bytes 131104 | tf_op jit(solution)/shard_map/ppermute | solution.py:279
  53.0 3.6 %collective-permute-start.7 = (bf16[1,2,64,512]{3,2,1,0:T(8,128)(2,1)S(1)}, bf16[1,2,64,512]{3,2,1,0:T(8,128)(2,1)S(1)}, u32[]{:S(2)}, u32[]{:S(2)}) collective-permute-start(bf16[1,2,64,512]{3,2,1,0:T(8,128)(2,1)S(1)} %add_convert_fusion.7), channel_id=1, source_target_pairs={{0,8},{1,9},{2,10},{3,11},{4,12},{5,13},{6,14},{7,15},{8,0},{9,1},... | collective-permute-start | bytes 393224 | tf_op jit(solution)/shard_map/ppermute | solution.py:279
  56.6 4.3 %collective-permute-done.13 = bf16[1,2,64,512]{3,2,1,0:T(8,128)(2,1)S(1)} collective-permute-done((bf16[1,2,64,512]{3,2,1,0:T(8,128)(2,1)S(1)}, bf16[1,2,64,512]{3,2,1,0:T(8,128)(2,1)S(1)}, u32[]{:S(2)}, u32[]{:S(2)}) %collective-permute-start.13) | collective-permute-done | bytes 131104 | tf_op jit(solution)/shard_map/ppermute | solution.py:279
  61.0 1.6 %collective-permute-done.7 = bf16[1,2,64,512]{3,2,1,0:T(8,128)(2,1)S(1)} collective-permute-done((bf16[1,2,64,512]{3,2,1,0:T(8,128)(2,1)S(1)}, bf16[1,2,64,512]{3,2,1,0:T(8,128)(2,1)S(1)}, u32[]{:S(2)}, u32[]{:S(2)}) %collective-permute-start.7) | collective-permute-done | bytes 131104 | tf_op jit(solution)/shard_map/ppermute | solution.py:279
  62.6 4.7 %collective-permute-done.14.refs_1_ = bf16[1,2,64,512]{3,2,1,0:T(8,128)(2,1)S(1)} collective-permute-done((bf16[1,2,64,512]{3,2,1,0:T(8,128)(2,1)S(1)}, bf16[1,2,64,512]{3,2,1,0:T(8,128)(2,1)S(1)}, u32[]{:S(2)}, u32[]{:S(2)}) %collective-permute-start.14) | collective-permute-done | bytes 131104 | tf_op jit(solution)/shard_map/ppermute | solution.py:279
  68.7 5.1 %collective-permute-done.15.refs_2_ = bf16[2,2,64,512]{3,2,1,0:T(8,128)(2,1)S(1)} collective-permute-done((bf16[2,2,64,512]{3,2,1,0:T(8,128)(2,1)S(1)}, bf16[2,2,64,512]{3,2,1,0:T(8,128)(2,1)S(1)}, u32[]{:S(2)}, u32[]{:S(2)}) %collective-permute-start.15) | collective-permute-done | bytes 262176 | tf_op jit(solution)/shard_map/ppermute | solution.py:279
  76.7 1.5 %order_a.1 = (f32[512,512]{1,0:T(8,128)}, f32[512,512]{1,0:T(8,128)}) custom-call(bf16[1,2,64,512]{3,2,1,0:T(8,128)(2,1)S(1)} %add_convert_fusion.4.refs_0_, bf16[1,2,64,512]{3,2,1,0:T(8,128)(2,1)S(1)} %collective-permute-done.14.refs_1_, bf16[2,2,64,512]{3,2,1,0:T(8,128)(2,1)S(1)} %collective-permute-done.15.refs_2_, ...), custom_call_target="tpu_custom_call" | custom-call | bytes 3145728 | tf_op jit(solution)/shard_map/order_a/pallas_call | solution.py:416
  78.1 2.2 %collective-permute-done.11.refs_2_ = bf16[2,2,64,512]{3,2,1,0:T(8,128)(2,1)S(1)} collective-permute-done((bf16[2,2,64,512]{3,2,1,0:T(8,128)(2,1)S(1)}, bf16[2,2,64,512]{3,2,1,0:T(8,128)(2,1)S(1)}, u32[]{:S(2)}, u32[]{:S(2)}) %collective-permute-start.11) | collective-permute-done | bytes 262176 | tf_op jit(solution)/shard_map/ppermute | solution.py:279
  (68 shorter events, 13.6 us)
Async XLA Ops:
  2.7 17.2 %collective-permute-start.1 = (bf16[474,512]{1,0:T(8,128)(2,1)S(1)}, bf16[474,512]{1,0:T(8,128)(2,1)S(1)}, u32[]{:S(2)}, u32[]{:S(2)}) collective-permute-start(bf16[474,512]{1,0:T(8,128)(2,1)S(1)} %pack_east.1), channel_id=1, source_target_pairs={{0,4},{4,8},{8,12},{12,0},{1,5},{5,9},{9,13},{13,1},{2,6},{6,10},{... | collective-permute-start | bytes 1456136 | tf_op jit(solution)/shard_map/ppermute | solution.py:346
  6.3 23.3 %collective-permute-start = (bf16[474,512]{1,0:T(8,128)(2,1)S(1)}, bf16[474,512]{1,0:T(8,128)(2,1)S(1)}, u32[]{:S(2)}, u32[]{:S(2)}) collective-permute-start(bf16[474,512]{1,0:T(8,128)(2,1)S(1)} %pack_west.1), channel_id=1, source_target_pairs={{4,0},{8,4},{12,8},{0,12},{5,1},{9,5},{13,9},{1,13},{6,2},{10,6},{... | collective-permute-start | bytes 1456136 | tf_op jit(solution)/shard_map/ppermute | solution.py:349
  17.3 12.3 %copy-start.5 = (bf16[512,512]{1,0:T(8,128)(2,1)S(1)}, bf16[512,512]{1,0:T(8,128)(2,1)}, u32[]{:S(2)}) copy-start(bf16[512,512]{1,0:T(8,128)(2,1)} %message_w.3) | copy-start | bytes 1572868
  17.3 12.3 %copy-start.6 = (bf16[256,512]{1,0:T(8,128)(2,1)S(1)}, bf16[256,512]{1,0:T(8,128)(2,1)}, u32[]{:S(2)}) copy-start(bf16[256,512]{1,0:T(8,128)(2,1)} %mesh_lat.3) | copy-start | bytes 786436
  17.3 12.3 %copy-start.9 = (bf16[512,512]{1,0:T(8,128)(2,1)S(1)}, bf16[512,512]{1,0:T(8,128)(2,1)}, u32[]{:S(2)}) copy-start(bf16[512,512]{1,0:T(8,128)(2,1)} %up_w.1) | copy-start | bytes 1572868
  17.3 12.2 %copy-start.11 = (f32[512]{0:T(512)S(1)}, f32[512]{0:T(512)}, u32[]{:S(2)}) copy-start(f32[512]{0:T(512)} %param.22) | copy-start | bytes 6148
  32.3 1.9 %collective-permute-start.2 = (bf16[4,2,64,512]{3,2,1,0:T(8,128)(2,1)S(1)}, bf16[4,2,64,512]{3,2,1,0:T(8,128)(2,1)S(1)}, u32[]{:S(2)}, u32[]{:S(2)}) collective-permute-start(bf16[4,2,64,512]{3,2,1,0:T(8,128)(2,1)S(1)} %get-tuple-element.64), channel_id=1, source_target_pairs={{0,1},{1,0},{2,3},{3,2},{4,5},{5,4},{6,7},{7,6},{8,9},{9,8},{10,11... | collective-permute-start | bytes 1572872 | tf_op jit(solution)/shard_map/ppermute | solution.py:268
  34.3 6.4 %collective-permute-start.3 = (bf16[2,2,64,512]{3,2,1,0:T(8,128)(2,1)S(1)}, bf16[2,2,64,512]{3,2,1,0:T(8,128)(2,1)S(1)}, u32[]{:S(2)}, u32[]{:S(2)}) collective-permute-start(bf16[2,2,64,512]{3,2,1,0:T(8,128)(2,1)S(1)} %slice.25), channel_id=1, source_target_pairs={{0,2},{1,5},{2,0},{3,7},{4,6},{5,1},{6,4},{7,3},{8,10},{9,13},{10,... | collective-permute-start | bytes 786440 | tf_op jit(solution)/shard_map/ppermute | solution.py:279
  38.0 2.9 %collective-permute-start.4 = (bf16[4,2,64,512]{3,2,1,0:T(8,128)(2,1)S(1)}, bf16[4,2,64,512]{3,2,1,0:T(8,128)(2,1)S(1)}, u32[]{:S(2)}, u32[]{:S(2)}) collective-permute-start(bf16[4,2,64,512]{3,2,1,0:T(8,128)(2,1)S(1)} %get-tuple-element.74), channel_id=1, source_target_pairs={{0,1},{1,0},{2,3},{3,2},{4,5},{5,4},{6,7},{7,6},{8,9},{9,8},{10,11... | collective-permute-start | bytes 1572872 | tf_op jit(solution)/shard_map/ppermute | solution.py:268
  41.1 6.6 %collective-permute-start.5 = (bf16[2,2,64,512]{3,2,1,0:T(8,128)(2,1)S(1)}, bf16[2,2,64,512]{3,2,1,0:T(8,128)(2,1)S(1)}, u32[]{:S(2)}, u32[]{:S(2)}) collective-permute-start(bf16[2,2,64,512]{3,2,1,0:T(8,128)(2,1)S(1)} %slice.33), channel_id=1, source_target_pairs={{0,2},{1,5},{2,0},{3,7},{4,6},{5,1},{6,4},{7,3},{8,10},{9,13},{10,... | collective-permute-start | bytes 786440 | tf_op jit(solution)/shard_map/ppermute | solution.py:279
  42.7 6.6 %collective-permute-start.12 = (bf16[1,2,64,512]{3,2,1,0:T(8,128)(2,1)S(1)}, bf16[1,2,64,512]{3,2,1,0:T(8,128)(2,1)S(1)}, u32[]{:S(2)}, u32[]{:S(2)}) collective-permute-start(bf16[1,2,64,512]{3,2,1,0:T(8,128)(2,1)S(1)} %slice.31), channel_id=1, source_target_pairs={{0,4},{1,3},{2,6},{3,1},{4,0},{5,7},{6,2},{7,5},{8,12},{9,11},{10,... | collective-permute-start | bytes 393224 | tf_op jit(solution)/shard_map/ppermute | solution.py:279
  47.8 5.2 %collective-permute-start.6 = (bf16[1,2,64,512]{3,2,1,0:T(8,128)(2,1)S(1)}, bf16[1,2,64,512]{3,2,1,0:T(8,128)(2,1)S(1)}, u32[]{:S(2)}, u32[]{:S(2)}) collective-permute-start(bf16[1,2,64,512]{3,2,1,0:T(8,128)(2,1)S(1)} %slice.35), channel_id=1, source_target_pairs={{0,4},{1,3},{2,6},{3,1},{4,0},{5,7},{6,2},{7,5},{8,12},{9,11},{10,... | collective-permute-start | bytes 393224 | tf_op jit(solution)/shard_map/ppermute | solution.py:279
  49.3 11.6 %collective-permute-start.13 = (bf16[1,2,64,512]{3,2,1,0:T(8,128)(2,1)S(1)}, bf16[1,2,64,512]{3,2,1,0:T(8,128)(2,1)S(1)}, u32[]{:S(2)}, u32[]{:S(2)}) collective-permute-start(bf16[1,2,64,512]{3,2,1,0:T(8,128)(2,1)S(1)} %add_convert_fusion.5), channel_id=1, source_target_pairs={{0,8},{1,9},{2,10},{3,11},{4,12},{5,13},{6,14},{7,15},{8,0},{9,1},... | collective-permute-start | bytes 393224 | tf_op jit(solution)/shard_map/ppermute | solution.py:279
  53.0 9.6 %collective-permute-start.7 = (bf16[1,2,64,512]{3,2,1,0:T(8,128)(2,1)S(1)}, bf16[1,2,64,512]{3,2,1,0:T(8,128)(2,1)S(1)}, u32[]{:S(2)}, u32[]{:S(2)}) collective-permute-start(bf16[1,2,64,512]{3,2,1,0:T(8,128)(2,1)S(1)} %add_convert_fusion.7), channel_id=1, source_target_pairs={{0,8},{1,9},{2,10},{3,11},{4,12},{5,13},{6,14},{7,15},{8,0},{9,1},... | collective-permute-start | bytes 393224 | tf_op jit(solution)/shard_map/ppermute | solution.py:279
  60.9 6.4 %collective-permute-start.14 = (bf16[1,2,64,512]{3,2,1,0:T(8,128)(2,1)S(1)}, bf16[1,2,64,512]{3,2,1,0:T(8,128)(2,1)S(1)}, u32[]{:S(2)}, u32[]{:S(2)}) collective-permute-start(bf16[1,2,64,512]{3,2,1,0:T(8,128)(2,1)S(1)} %add_convert_fusion.4.refs_0_), channel_id=1, source_target_pairs={{0,4},{1,3},{2,6},{3,1},{4,0},{5,7},{6,2},{7,5},{8,12},{9,11},{10,... | collective-permute-start | bytes 393224 | tf_op jit(solution)/shard_map/ppermute | solution.py:279
  67.4 6.4 %collective-permute-start.15 = (bf16[2,2,64,512]{3,2,1,0:T(8,128)(2,1)S(1)}, bf16[2,2,64,512]{3,2,1,0:T(8,128)(2,1)S(1)}, u32[]{:S(2)}, u32[]{:S(2)}) collective-permute-start(bf16[2,2,64,512]{3,2,1,0:T(8,128)(2,1)S(1)} %pad_maximum_fusion.1), channel_id=1, source_target_pairs={{0,2},{1,5},{2,0},{3,7},{4,6},{5,1},{6,4},{7,3},{8,10},{9,13},{10,... | collective-permute-start | bytes 786440 | tf_op jit(solution)/shard_map/ppermute | solution.py:279
  68.6 5.2 %collective-permute-start.9 = (bf16[1,2,64,512]{3,2,1,0:T(8,128)(2,1)S(1)}, bf16[1,2,64,512]{3,2,1,0:T(8,128)(2,1)S(1)}, u32[]{:S(2)}, u32[]{:S(2)}) collective-permute-start(bf16[1,2,64,512]{3,2,1,0:T(8,128)(2,1)S(1)} %add_convert_fusion.6.refs_0_), channel_id=1, source_target_pairs={{0,4},{1,3},{2,6},{3,1},{4,0},{5,7},{6,2},{7,5},{8,12},{9,11},{10,... | collective-permute-start | bytes 393224 | tf_op jit(solution)/shard_map/ppermute | solution.py:279
  73.8 2.8 %collective-permute-start.18 = (bf16[2,2,64,512]{3,2,1,0:T(8,128)(2,1)S(1)}, bf16[2,2,64,512]{3,2,1,0:T(8,128)(2,1)S(1)}, u32[]{:S(2)}, u32[]{:S(2)}) collective-permute-start(bf16[2,2,64,512]{3,2,1,0:T(8,128)(2,1)S(1)} %collective-permute-done.15.refs_2_), channel_id=1, source_target_pairs={{0,1},{1,0},{2,3},{3,2},{4,5},{5,4},{6,7},{7,6},{8,9},{9,8},{10,11... | collective-permute-start | bytes 786440 | tf_op jit(solution)/shard_map/ppermute | solution.py:268
  73.9 6.4 %collective-permute-start.11 = (bf16[2,2,64,512]{3,2,1,0:T(8,128)(2,1)S(1)}, bf16[2,2,64,512]{3,2,1,0:T(8,128)(2,1)S(1)}, u32[]{:S(2)}, u32[]{:S(2)}) collective-permute-start(bf16[2,2,64,512]{3,2,1,0:T(8,128)(2,1)S(1)} %pad_maximum_fusion), channel_id=1, source_target_pairs={{0,2},{1,5},{2,0},{3,7},{4,6},{5,1},{6,4},{7,3},{8,10},{9,13},{10,... | collective-permute-start | bytes 786440 | tf_op jit(solution)/shard_map/ppermute | solution.py:279
  75.1 1.3 %collective-permute-start.16 = (bf16[1,2,64,512]{3,2,1,0:T(8,128)(2,1)S(1)}, bf16[1,2,64,512]{3,2,1,0:T(8,128)(2,1)S(1)}, u32[]{:S(2)}, u32[]{:S(2)}) collective-permute-start(bf16[1,2,64,512]{3,2,1,0:T(8,128)(2,1)S(1)} %add_convert_fusion.4.refs_0_), channel_id=1, source_target_pairs={{0,1},{1,0},{2,3},{3,2},{4,5},{5,4},{6,7},{7,6},{8,9},{9,8},{10,11... | collective-permute-start | bytes 393224 | tf_op jit(solution)/shard_map/ppermute | solution.py:268
  75.1 1.5 %collective-permute-start.17 = (bf16[1,2,64,512]{3,2,1,0:T(8,128)(2,1)S(1)}, bf16[1,2,64,512]{3,2,1,0:T(8,128)(2,1)S(1)}, u32[]{:S(2)}, u32[]{:S(2)}) collective-permute-start(bf16[1,2,64,512]{3,2,1,0:T(8,128)(2,1)S(1)} %collective-permute-done.14.refs_1_), channel_id=1, source_target_pairs={{0,1},{1,0},{2,3},{3,2},{4,5},{5,4},{6,7},{7,6},{8,9},{9,8},{10,11... | collective-permute-start | bytes 393224 | tf_op jit(solution)/shard_map/ppermute | solution.py:268
  80.3 1.9 %collective-permute-start.19 = (bf16[2,2,64,512]{3,2,1,0:T(8,128)(2,1)S(1)}, bf16[2,2,64,512]{3,2,1,0:T(8,128)(2,1)S(1)}, u32[]{:S(2)}, u32[]{:S(2)}) collective-permute-start(bf16[2,2,64,512]{3,2,1,0:T(8,128)(2,1)S(1)} %collective-permute-done.11.refs_2_), channel_id=1, source_target_pairs={{0,1},{1,0},{2,3},{3,2},{4,5},{5,4},{6,7},{7,6},{8,9},{9,8},{10,11... | collective-permute-start | bytes 786440 | tf_op jit(solution)/shard_map/ppermute | solution.py:268
  80.3 1.7 %collective-permute-start.8 = (bf16[1,2,64,512]{3,2,1,0:T(8,128)(2,1)S(1)}, bf16[1,2,64,512]{3,2,1,0:T(8,128)(2,1)S(1)}, u32[]{:S(2)}, u32[]{:S(2)}) collective-permute-start(bf16[1,2,64,512]{3,2,1,0:T(8,128)(2,1)S(1)} %add_convert_fusion.6.refs_0_), channel_id=1, source_target_pairs={{0,1},{1,0},{2,3},{3,2},{4,5},{5,4},{6,7},{7,6},{8,9},{9,8},{10,11... | collective-permute-start | bytes 393224 | tf_op jit(solution)/shard_map/ppermute | solution.py:268
  80.8 1.4 %collective-permute-start.10 = (bf16[1,2,64,512]{3,2,1,0:T(8,128)(2,1)S(1)}, bf16[1,2,64,512]{3,2,1,0:T(8,128)(2,1)S(1)}, u32[]{:S(2)}, u32[]{:S(2)}) collective-permute-start(bf16[1,2,64,512]{3,2,1,0:T(8,128)(2,1)S(1)} %collective-permute-done.9.refs_1_), channel_id=1, source_target_pairs={{0,1},{1,0},{2,3},{3,2},{4,5},{5,4},{6,7},{7,6},{8,9},{9,8},{10,11... | collective-permute-start | bytes 393224 | tf_op jit(solution)/shard_map/ppermute | solution.py:268
  (8 other events, 55.4 us)

commit v12 on v10

--- a/solution.py
+++ b/solution.py
@@ -122,7 +122,7 @@
 def to_chunks(grads, stack, perm, start):
     count, matrices, size, _ = grads.shape
     for j in range(count):
-        at = pl.ds(pl.multiple_of((perm[start + j] & (count - 1)) * size, size), size)
+        at = pl.ds(pl.multiple_of((perm[start + j] & 3) * size, size), size)
         for k in range(matrices):
             grads[j, k] = stack[k, at, :].astype(BF)
 
@@ -144,7 +144,7 @@
 
 def mesh_kernel(
     x, embed_t, weights_all, h_sum, message_w, up_w, gain, mesh_lat, cot, grad_update,
-    sent, mesh_grad, grad_gain, gathered, grad_aggregate, normed, grad_pre_up, update, slope, stack,
+    sent_high, sent_low, mesh_grad, grad_gain, gathered, grad_aggregate, normed, grad_pre_up, update, slope, stack,
 ):
     perm = chunk_order()
     points = x.shape[1]
@@ -169,21 +169,18 @@
     theirs = rows_of_half(1 - perm[0] // 4, stack.shape[1])
     stack[0] = contract(gathered[:, theirs], grad_aggregate[...], 0, 0).astype(BF)
     stack[1] = contract(normed[:, theirs], grad_pre_up[...], 0, 0).astype(BF)
-    to_chunks(sent, stack, perm, 4)
-
-
-def tail_kernel(
-    gathered, grad_aggregate, normed, grad_pre_up, update, message_w, out_w, mesh_lat, cot,
-    kept, back, mesh_new, grad_out, stack,
-):
+    to_chunks(sent_high, stack, perm, 6)
+    to_chunks(sent_low, stack, perm, 4)
+
+
+def tail_kernel(gathered, grad_aggregate, normed, grad_pre_up, message_w, kept_high, kept_low, back, stack):
     perm = chunk_order()
     mine = rows_of_half(perm[0] // 4, stack.shape[1])
     stack[0] = contract(gathered[:, mine], grad_aggregate[...], 0, 0).astype(BF)
     stack[1] = contract(normed[:, mine], grad_pre_up[...], 0, 0).astype(BF)
-    to_chunks(kept, stack, perm, 0)
+    to_chunks(kept_high, stack, perm, 2)
+    to_chunks(kept_low, stack, perm, 0)
     back[...] = contract(message_w[...], grad_aggregate[...], 1, 1).astype(BF)
-    mesh_new[...] = (mesh_lat[...].astype(F32) + contract(update[...], out_w[...], 1, 0)).astype(BF)
-    grad_out[...] = contract(update[...], cot[...], 0, 0).astype(BF)
 
 
 def points_of(x_own, x_west, x_east):
@@ -212,17 +209,20 @@
 
 
 def grid_kernel(
-    back, weights_all, slope_own, slope_west, slope_east, x_own, x_west, x_east, grad_gain, grad_out,
-    sent, grad_pre, stack,
+    back, weights_all, slope_own, slope_west, slope_east, x_own, x_west, x_east, grad_gain, update, out_w, mesh_lat, cot,
+    sent_high, sent_low, grad_pre, grad_out, mesh_new, stack,
 ):
     perm = chunk_order()
     for slope, at, all_at in points_of(slope_own, slope_west, slope_east):
         hidden = contract(back[...], weights_all[:, all_at], 1, 0)
         grad_pre[:, all_at] = (hidden * slope[:, at].astype(F32)).astype(BF)
+    grad_out[...] = contract(update[...], cot[...], 0, 0).astype(BF)
     half = 1 - perm[0] // 4
     stack[0] = grad_out[rows_of_half(half, stack.shape[1]), :].astype(F32)
     embed_rows(half, (x_own, x_west, x_east), grad_pre, grad_gain, stack.at[1])
-    to_chunks(sent, stack, perm, 4)
+    to_chunks(sent_high, stack, perm, 6)
+    to_chunks(sent_low, stack, perm, 4)
+    mesh_new[...] = (mesh_lat[...].astype(F32) + contract(update[...], out_w[...], 1, 0)).astype(BF)
 
 
 def grid_kept_kernel(grad_pre, x_own, x_west, x_east, grad_gain, sums):
@@ -230,12 +230,14 @@
     embed_rows(perm[0] // 4, (x_own, x_west, x_east), grad_pre, grad_gain, sums)
 
 
-def kept_chunks_kernel(grad_out, sums, kept):
-    perm = chunk_order()
-    count, _, size, _ = kept.shape
-    for j in range(count):
-        kept[j, 0] = grad_out[pl.ds(pl.multiple_of(perm[j] * size, size), size), :]
-        kept[j, 1] = sums[pl.ds(pl.multiple_of((perm[j] & (count - 1)) * size, size), size), :].astype(BF)
+def kept_chunks_kernel(grad_out, sums, kept_high, kept_low):
+    perm = chunk_order()
+    for kept, start in ((kept_high, 2), (kept_low, 0)):
+        count, _, size, _ = kept.shape
+        for j in range(count):
+            chunk = perm[start + j]
+            kept[j, 0] = grad_out[pl.ds(pl.multiple_of(chunk * size, size), size), :]
+            kept[j, 1] = sums[pl.ds(pl.multiple_of((chunk & 3) * size, size), size), :].astype(BF)
 
 
 def order_mesh_kernel(*refs):
@@ -294,8 +296,8 @@
     return (a.astype(F32) + b.astype(F32)).astype(BF)
 
 
-def halved(kept):
-    return added(kept[:2], swapped(kept[2:], 0))
+def halved(high, low):
+    return added(low, swapped(high, 0))
 
 
 def all_summed(kept):
@@ -362,44 +364,46 @@
         600_000_000, 3 * MIB, 16,
     )(x_west, embed_t, weights_all, h_own)
 
-    half_chunks = shape((4, 2, latent // 8, latent), BF)
+    quarter = shape((2, 2, latent // 8, latent), BF)
     node_rows = shape((nodes, latent), BF)
     (
-        sent_a, mesh_grad, gain_term, gathered, grad_aggregate, normed, grad_pre_up, update, slope_east
+        sent_high, sent_low, mesh_grad, gain_term, gathered, grad_aggregate, normed, grad_pre_up, update, slope_east
     ) = call(
         mesh_kernel, "mesh_nodes", [VMEM] * 10,
-        [half_chunks, shape((nodes, latent), F32), shape((1, latent), F32)]
+        [quarter, quarter, shape((nodes, latent), F32), shape((1, latent), F32)]
         + [node_rows] * 5
         + [shape((latent, side), BF)],
         2_000_000_000, 8 * MIB, 16, [pltpu.VMEM((2, latent // 2, latent), BF)],
     )(x_east, embed_t, weights_all, h_sum, message_w, up_w, gain.reshape(1, latent), mesh_lat, cot, grad_update)
-    got_a = core_swapped(sent_a)
-    kept_a, back, mesh_new, grad_out_term = call(
-        tail_kernel, "mesh_tail", [VMEM] * 9,
-        [half_chunks, shape((latent, nodes), BF), node_rows, shape((latent, latent), BF)],
+    got_high, got_low = core_swapped(sent_high), core_swapped(sent_low)
+    kept_high, kept_low, back = call(
+        tail_kernel, "mesh_tail", [VMEM] * 5, [quarter, quarter, shape((latent, nodes), BF)],
         500_000_000, 3 * MIB, 16, [pltpu.VMEM((2, latent // 2, latent), BF)],
-    )(gathered, grad_aggregate, normed, grad_pre_up, update, message_w, out_w, mesh_lat, cot)
-
-    kept_a, back = lax.optimization_barrier((added(kept_a, got_a), back))
+    )(gathered, grad_aggregate, normed, grad_pre_up, message_w)
+
+    high_a, back = lax.optimization_barrier((added(kept_high, got_high), back))
+    low_a = added(kept_low, got_low)
     padded = -(-(features + 1) // 128) * 128
     assert padded == latent
     x_parts = (x_own, x_west, x_east)
-    stack = pltpu.VMEM((2, latent // 2, latent), F32)
-    sent_b, grad_pre = call(
-        grid_kernel, "grid_points", [VMEM] * 10, [half_chunks, shape((latent, points), BF)],
-        1_600_000_000, 9 * MIB, 20, [stack],
-    )(back, weights_all, slope_own, slope_west, slope_east, *x_parts, gain_term, grad_out_term)
-    got_b = core_swapped(sent_b)
+    sent_high, sent_low, grad_pre, grad_out_term, mesh_new = call(
+        grid_kernel, "grid_points", [VMEM] * 13,
+        [quarter, quarter, shape((latent, points), BF), shape((latent, latent), BF), node_rows],
+        1_600_000_000, 9 * MIB, 20, [pltpu.VMEM((2, latent // 2, latent), F32)],
+    )(
+        back, weights_all, slope_own, slope_west, slope_east, *x_parts, gain_term, update, out_w, mesh_lat, cot
+    )
+    got_high, got_low = core_swapped(sent_high), core_swapped(sent_low)
     (sums_b,) = call(
         grid_kept_kernel, "grid_kept", [VMEM] * 5, [shape((latent // 2, latent), F32)], 800_000_000, 6 * MIB, 16
     )(grad_pre, *x_parts, gain_term)
-    kept_a, sums_b = lax.optimization_barrier((halved(kept_a), sums_b))
-    (kept_b,) = call(
-        kept_chunks_kernel, "kept_chunks", [VMEM] * 2, [half_chunks], 8_000_000_000, MIB, 16
+    kept_a, sums_b = lax.optimization_barrier((halved(high_a, low_a), sums_b))
+    kept_high, kept_low = call(
+        kept_chunks_kernel, "kept_chunks", [VMEM] * 2, [quarter, quarter], 8_000_000_000, MIB, 16
     )(grad_out_term, sums_b)
 
     summed_a = all_summed(kept_a)
-    summed_b = all_summed(halved(added(kept_b, got_b)))
+    summed_b = all_summed(halved(added(kept_high, got_high), added(kept_low, got_low)))
     square = shape((latent, latent), F32)
     grad_message, grad_up = call(
         order_mesh_kernel, "order_a", [VMEM] * 6, [square, square], 0, 3 * MIB, 16

time: 80 us -> 79.6 us (level)
  starting transfers between devices: 17.9 us -> 19.9 us
  waiting for transfers between devices: 36.5 us -> 35 us
    ppermute x10, waiting for transfers between devices: 23.9 us -> 21.5 us  [swapped(): return lax.ppermute(value, ('lon', 'lat'), pairs)]
    ppermute x10, starting transfers between devices: 11.6 us -> 12.6 us  [swapped(): return lax.ppermute(value, ('lon', 'lat'), pairs)]
    ppermute x8 -> x10, starting transfers between devices: 1.1 us -> 2.05 us  [core_swapped(): lax.ppermute(value, 'lat', [(i, i ^ 1) for i in range(lax.axis_size('lat'...]
    pallas_call x1, Pallas kernels: 3.93 us -> 3.03 us  [on_device(): call(lambda *refs: weights_kernel(rows, cols // block, *refs), 'slot_weig...]
    ppermute x1, waiting for transfers between devices: 1.97 us -> 2.86 us  [on_device(): lax.ppermute(to_east, 'lon', [(i, (i + 1) % count) for i in range(count)])]
    ppermute x8 -> x10, waiting for transfers between devices: 1.94 us -> 1.91 us  [core_swapped(): lax.ppermute(value, 'lat', [(i, i ^ 1) for i in range(lax.axis_size('lat'...]
  transfers between devices with their start and end apart: 20 -> 22, of which waited for: 14 -> 14; matrix products, arithmetic and copies ran while one was open for 1% -> 1% of each run, Pallas kernels for 22% -> 21%
where the time goes in v12:
time: 79.6 us; the launch traced here: 79.4 us
  waiting for transfers between devices  35 us (44%)
  Pallas kernels  20.9 us (26%)
  starting transfers between devices  19.9 us (25%)
  local copies, waits for them, and re-layouts  1.61 us (2%)
  between operations  1.6 us (2%)
    ppermute x10, waiting for transfers between devices, swapped(): return lax.ppermute(value, ('lon', 'lat'), pairs)  21.5 us
    ppermute x10, starting transfers between devices, swapped(): return lax.ppermute(value, ('lon', 'lat'), pairs)  12.6 us
    ppermute x1, waiting for transfers between devices, on_device(): lax.ppermute(to_west, 'lon', [((i + 1) % count, i) for i in range(count)])  8.72 us
    pallas_call x1, Pallas kernels, on_device(): call(own_kernel, 'own_points', [VMEM] * 3, [shape((nodes, latent), F32),...  3.55 us
    pallas_call x1, Pallas kernels, on_device(): call(grid_kernel, 'grid_points', [VMEM] * 13, [quarter, quarter, shape((l...  3.35 us
    ppermute x1, starting transfers between devices, on_device(): lax.ppermute(to_east, 'lon', [(i, (i + 1) % count) for i in range(count)])  3.08 us
    pallas_call x1, Pallas kernels, on_device(): call(lambda *refs: weights_kernel(rows, cols // block, *refs), 'slot_weig...  3.03 us
    ppermute x1, waiting for transfers between devices, on_device(): lax.ppermute(to_east, 'lon', [(i, (i + 1) % count) for i in range(count)])  2.86 us
  transfers between devices with their start and end apart: 22, of which 14 were waited for; matrix products, arithmetic and copies ran while one was open for 1% of the time, Pallas kernels for 21%

profile of v12, /device:TPU:0, one launch (start us, length us, event | category | flops | bytes accessed | tf_op | source)
XLA Modules:
  0.0 79.4 jit_solution(2115212046305152524)
XLA Ops:
  0.6 1.5 %copy-done = bf16[8,256,474]{1,0,2:T(8,128)(2,1)S(1)} copy-done((bf16[8,256,474]{1,0,2:T(8,128)(2,1)S(1)}, bf16[8,256,474]{1,0,2:T(8,128)(2,1)}, u32[]{:S(2)}) %copy-start) | copy-done | bytes 1941528
  2.7 3.1 %collective-permute-start.1 = (bf16[474,512]{1,0:T(8,128)(2,1)S(1)}, bf16[474,512]{1,0:T(8,128)(2,1)S(1)}, u32[]{:S(2)}, u32[]{:S(2)}) collective-permute-start(bf16[474,512]{1,0:T(8,128)(2,1)S(1)} %pack_east.1), channel_id=1, source_target_pairs={{0,4},{4,8},{8,12},{12,0},{1,5},{5,9},{9,13},{13,1},{2,6},{6,10},{... | collective-permute-start | bytes 1456136 | tf_op jit(solution)/shard_map/ppermute | solution.py:342
  6.3 2.1 %collective-permute-start = (bf16[474,512]{1,0:T(8,128)(2,1)S(1)}, bf16[474,512]{1,0:T(8,128)(2,1)S(1)}, u32[]{:S(2)}, u32[]{:S(2)}) collective-permute-start(bf16[474,512]{1,0:T(8,128)(2,1)S(1)} %pack_west.1), channel_id=1, source_target_pairs={{4,0},{8,4},{12,8},{0,12},{5,1},{9,5},{13,9},{1,13},{6,2},{10,6},{... | collective-permute-start | bytes 1456136 | tf_op jit(solution)/shard_map/ppermute | solution.py:345
  9.1 3.0 %slot_weights.1 = (bf16[256,3072]{1,0:T(8,128)(2,1)S(1)}, f32[256,512]{1,0:T(8,128)S(1)}) custom-call(s32[32]{0:T(128)S(1)} %copy-done.6, s32[32]{0:T(128)S(1)} %copy-done.7, s32[1]{0:T(128)S(6)} %copy.23.refs_2_, bf16[32,128,128]{2,1,0:T(8,128)(2,1)S(1)} %copy-done.3, bf16[256,512]{1,0:T(8,128)(2,1)S(1)} %copy-done.4, bf16[512,512]{1,0:T(8,128)(2,1)S(1)} %copy-done.2), custom_call_target="tpu_custom_call" | custom-call | flops 200000000 | bytes 4194304 | tf_op jit(solution)/shard_map/slot_weights/pallas_call | solution.py:347
  12.2 1.3 %own_rows.1 = (bf16[474,2048]{1,0:T(8,128)(2,1)S(1)}, bf16[512,474]{1,0:T(8,128)(2,1)S(1)}) custom-call(bf16[474,8,256]{2,1,0:T(8,128)(2,1)S(1)} %bitcast.5, bf16[474,512]{1,0:T(8,128)(2,1)S(1)} %copy-done.10), custom_call_target="tpu_custom_call" | custom-call | flops 1000000000 | bytes 5242880 | tf_op jit(solution)/shard_map/own_rows/pallas_call | solution.py:352
  13.5 3.6 %own_points.1 = (f32[256,512]{1,0:T(8,128)S(1)}, bf16[512,2048]{1,0:T(8,128)(2,1)S(1)}) custom-call(bf16[474,2048]{1,0:T(8,128)(2,1)S(1)} %get-tuple-element.54.x_t.x_own, bf16[512,474]{1,0:T(8,128)(2,1)S(1)} %get-tuple-element.52.embed_t.refs_1_, bf16[256,3072]{1,0:T(8,128)(2,1)S(1)} %get-tuple-element.53.weights_all.refs_2_), custom_call_target="tpu_custom_call" | custom-call | flops 2000000000 | bytes 7340032 | tf_op jit(solution)/shard_map/own_points/pallas_call | solution.py:356
  17.1 2.9 %collective-permute-done.1.refs_0_.x_west = bf16[474,512]{1,0:T(8,128)(2,1)S(1)} collective-permute-done((bf16[474,512]{1,0:T(8,128)(2,1)S(1)}, bf16[474,512]{1,0:T(8,128)(2,1)S(1)}, u32[]{:S(2)}, u32[]{:S(2)}) %collective-permute-start.1) | collective-permute-done | bytes 485408 | tf_op jit(solution)/shard_map/ppermute | solution.py:342
  20.9 8.7 %collective-permute-done.x.x_east = bf16[474,512]{1,0:T(8,128)(2,1)S(1)} collective-permute-done((bf16[474,512]{1,0:T(8,128)(2,1)S(1)}, bf16[474,512]{1,0:T(8,128)(2,1)S(1)}, u32[]{:S(2)}, u32[]{:S(2)}) %collective-permute-start) | collective-permute-done | bytes 485408 | tf_op jit(solution)/shard_map/ppermute | solution.py:345
  29.6 2.6 %mesh_nodes.1 = (bf16[2,2,64,512]{3,2,1,0:T(8,128)(2,1)S(1)}, bf16[2,2,64,512]{3,2,1,0:T(8,128)(2,1)S(1)}, f32[256,512]{1,0:T(8,128)}, f32[1,512]{1,0:T(1,128)S(...) custom-call(bf16[474,512]{1,0:T(8,128)(2,1)S(1)} %collective-permute, ...), custom_call_target="tpu_custom_call" | custom-call | flops 2000000000 | bytes 8388608 | tf_op jit(solution)/shard_map/mesh_nodes/pallas_call | solution.py:371
  33.8 1.6 %collective-permute-start.4 = (bf16[2,2,64,512]{3,2,1,0:T(8,128)(2,1)S(1)}, bf16[2,2,64,512]{3,2,1,0:T(8,128)(2,1)S(1)}, u32[]{:S(2)}, u32[]{:S(2)}) collective-permute-start(bf16[2,2,64,512]{3,2,1,0:T(8,128)(2,1)S(1)} %add_convert_fusion.5), channel_id=1, source_target_pairs={{0,2},{1,5},{2,0},{3,7},{4,6},{5,1},{6,4},{7,3},{8,10},{9,13},{10,... | collective-permute-start | bytes 786440 | tf_op jit(solution)/shard_map/ppermute | solution.py:281
  35.4 3.3 %grid_points.1 = (bf16[2,2,64,512]{3,2,1,0:T(8,128)(2,1)S(1)}, bf16[2,2,64,512]{3,2,1,0:T(8,128)(2,1)S(1)}, bf16[512,3072]{1,0:T(8,128)(2,1)S(1)}, bf16[512,512]{1,0:T(8,128)(2,1)S(1)}, bf16[256,512]{1,0:T(8,128)(2,1)}) custom-call(bf16[512,256]{1,0:T(8,128)(2,1)S(1)} %get-tuple-element.65.back, bf16[256,3072]{1,0:T(8,128)(2,1)S(1)} %get-tuple-element.53.weights_all.refs_2_, ...), custom_call_target="tpu_custom_call" | custom-call | flops 1600000000 | bytes 9437184 | tf_op jit(solution)/shard_map/grid_points/pallas_call | solution.py:389
  41.3 1.5 %collective-permute-start.7 = (bf16[2,2,64,512]{3,2,1,0:T(8,128)(2,1)S(1)}, bf16[2,2,64,512]{3,2,1,0:T(8,128)(2,1)S(1)}, u32[]{:S(2)}, u32[]{:S(2)}) collective-permute-start(bf16[2,2,64,512]{3,2,1,0:T(8,128)(2,1)S(1)} %add_convert_fusion.1), channel_id=1, source_target_pairs={{0,2},{1,5},{2,0},{3,7},{4,6},{5,1},{6,4},{7,3},{8,10},{9,13},{10,... | collective-permute-start | bytes 786440 | tf_op jit(solution)/shard_map/ppermute | solution.py:281
  42.8 4.1 %collective-permute-done.14 = bf16[1,2,64,512]{3,2,1,0:T(8,128)(2,1)S(1)} collective-permute-done((bf16[1,2,64,512]{3,2,1,0:T(8,128)(2,1)S(1)}, bf16[1,2,64,512]{3,2,1,0:T(8,128)(2,1)S(1)}, u32[]{:S(2)}, u32[]{:S(2)}) %collective-permute-start.14) | collective-permute-done | bytes 131104 | tf_op jit(solution)/shard_map/ppermute | solution.py:281
  46.9 1.4 %collective-permute-start.15 = (bf16[1,2,64,512]{3,2,1,0:T(8,128)(2,1)S(1)}, bf16[1,2,64,512]{3,2,1,0:T(8,128)(2,1)S(1)}, u32[]{:S(2)}, u32[]{:S(2)}) collective-permute-start(bf16[1,2,64,512]{3,2,1,0:T(8,128)(2,1)S(1)} %add_convert_fusion.7), channel_id=1, source_target_pairs={{0,8},{1,9},{2,10},{3,11},{4,12},{5,13},{6,14},{7,15},{8,0},{9,1},... | collective-permute-start | bytes 393224 | tf_op jit(solution)/shard_map/ppermute | solution.py:281
  48.5 1.9 %collective-permute-start.8 = (bf16[1,2,64,512]{3,2,1,0:T(8,128)(2,1)S(1)}, bf16[1,2,64,512]{3,2,1,0:T(8,128)(2,1)S(1)}, u32[]{:S(2)}, u32[]{:S(2)}) collective-permute-start(bf16[1,2,64,512]{3,2,1,0:T(8,128)(2,1)S(1)} %slice.17), channel_id=1, source_target_pairs={{0,4},{1,3},{2,6},{3,1},{4,0},{5,7},{6,2},{7,5},{8,12},{9,11},{10,... | collective-permute-start | bytes 393224 | tf_op jit(solution)/shard_map/ppermute | solution.py:281
  50.4 3.8 %collective-permute-done.15 = bf16[1,2,64,512]{3,2,1,0:T(8,128)(2,1)S(1)} collective-permute-done((bf16[1,2,64,512]{3,2,1,0:T(8,128)(2,1)S(1)}, bf16[1,2,64,512]{3,2,1,0:T(8,128)(2,1)S(1)}, u32[]{:S(2)}, u32[]{:S(2)}) %collective-permute-start.15) | collective-permute-done | bytes 131104 | tf_op jit(solution)/shard_map/ppermute | solution.py:281
  54.9 2.5 %collective-permute-start.9 = (bf16[1,2,64,512]{3,2,1,0:T(8,128)(2,1)S(1)}, bf16[1,2,64,512]{3,2,1,0:T(8,128)(2,1)S(1)}, u32[]{:S(2)}, u32[]{:S(2)}) collective-permute-start(bf16[1,2,64,512]{3,2,1,0:T(8,128)(2,1)S(1)} %add_convert_fusion.9), channel_id=1, source_target_pairs={{0,8},{1,9},{2,10},{3,11},{4,12},{5,13},{6,14},{7,15},{8,0},{9,1},... | collective-permute-start | bytes 393224 | tf_op jit(solution)/shard_map/ppermute | solution.py:281
  57.4 6.0 %collective-permute-done.16.refs_1_ = bf16[1,2,64,512]{3,2,1,0:T(8,128)(2,1)S(1)} collective-permute-done((bf16[1,2,64,512]{3,2,1,0:T(8,128)(2,1)S(1)}, bf16[1,2,64,512]{3,2,1,0:T(8,128)(2,1)S(1)}, u32[]{:S(2)}, u32[]{:S(2)}) %collective-permute-start.16) | collective-permute-done | bytes 131104 | tf_op jit(solution)/shard_map/ppermute | solution.py:281
  63.4 1.5 %collective-permute-start.17 = (bf16[2,2,64,512]{3,2,1,0:T(8,128)(2,1)S(1)}, bf16[2,2,64,512]{3,2,1,0:T(8,128)(2,1)S(1)}, u32[]{:S(2)}, u32[]{:S(2)}) collective-permute-start(bf16[2,2,64,512]{3,2,1,0:T(8,128)(2,1)S(1)} %pad_maximum_fusion.1), channel_id=1, source_target_pairs={{0,2},{1,5},{2,0},{3,7},{4,6},{5,1},{6,4},{7,3},{8,10},{9,13},{10,... | collective-permute-start | bytes 786440 | tf_op jit(solution)/shard_map/ppermute | solution.py:281
  65.1 4.8 %collective-permute-done.17.refs_2_ = bf16[2,2,64,512]{3,2,1,0:T(8,128)(2,1)S(1)} collective-permute-done((bf16[2,2,64,512]{3,2,1,0:T(8,128)(2,1)S(1)}, bf16[2,2,64,512]{3,2,1,0:T(8,128)(2,1)S(1)}, u32[]{:S(2)}, u32[]{:S(2)}) %collective-permute-start.17) | collective-permute-done | bytes 262176 | tf_op jit(solution)/shard_map/ppermute | solution.py:281
  70.0 1.4 %collective-permute-start.13 = (bf16[2,2,64,512]{3,2,1,0:T(8,128)(2,1)S(1)}, bf16[2,2,64,512]{3,2,1,0:T(8,128)(2,1)S(1)}, u32[]{:S(2)}, u32[]{:S(2)}) collective-permute-start(bf16[2,2,64,512]{3,2,1,0:T(8,128)(2,1)S(1)} %pad_maximum_fusion), channel_id=1, source_target_pairs={{0,2},{1,5},{2,0},{3,7},{4,6},{5,1},{6,4},{7,3},{8,10},{9,13},{10,... | collective-permute-start | bytes 786440 | tf_op jit(solution)/shard_map/ppermute | solution.py:281
  73.0 1.5 %order_a.1 = (f32[512,512]{1,0:T(8,128)}, f32[512,512]{1,0:T(8,128)}) custom-call(bf16[1,2,64,512]{3,2,1,0:T(8,128)(2,1)S(1)} %add_convert_fusion.6.refs_0_, bf16[1,2,64,512]{3,2,1,0:T(8,128)(2,1)S(1)} %collective-permute-done.16.refs_1_, bf16[2,2,64,512]{3,2,1,0:T(8,128)(2,1)S(1)} %collective-permute-done.17.refs_2_, ...), custom_call_target="tpu_custom_call" | custom-call | bytes 3145728 | tf_op jit(solution)/shard_map/order_a/pallas_call | solution.py:408
  74.4 2.1 %collective-permute-done.13.refs_2_ = bf16[2,2,64,512]{3,2,1,0:T(8,128)(2,1)S(1)} collective-permute-done((bf16[2,2,64,512]{3,2,1,0:T(8,128)(2,1)S(1)}, bf16[2,2,64,512]{3,2,1,0:T(8,128)(2,1)S(1)}, u32[]{:S(2)}, u32[]{:S(2)}) %collective-permute-start.13) | collective-permute-done | bytes 262176 | tf_op jit(solution)/shard_map/ppermute | solution.py:281
  77.0 1.0 %order_b.2 = (f32[512,512]{1,0:T(8,128)}, f32[474,512]{1,0:T(8,128)}, f32[1,512]{1,0:T(1,128)S(1)}) custom-call(bf16[1,2,64,512]{3,2,1,0:T(8,128)(2,1)S(1)} %add_convert_fusion.8.refs_0_, bf16[1,2,64,512]{3,2,1,0:T(8,128)(2,1)S(1)} %collective-permute-done.11.refs_1_, bf16[2,2,64,512]{3,2,1,0:T(8,128)(2,1)S(1)} %collective-permute-done.13.refs_2_), custom_call_target="tpu_custom_call" | custom-call | bytes 2097152 | tf_op jit(solution)/shard_map/order_b/pallas_call | solution.py:419
  (70 shorter events, 10.5 us)
Async XLA Ops:
  2.7 17.2 %collective-permute-start.1 = (bf16[474,512]{1,0:T(8,128)(2,1)S(1)}, bf16[474,512]{1,0:T(8,128)(2,1)S(1)}, u32[]{:S(2)}, u32[]{:S(2)}) collective-permute-start(bf16[474,512]{1,0:T(8,128)(2,1)S(1)} %pack_east.1), channel_id=1, source_target_pairs={{0,4},{4,8},{8,12},{12,0},{1,5},{5,9},{9,13},{13,1},{2,6},{6,10},{... | collective-permute-start | bytes 1456136 | tf_op jit(solution)/shard_map/ppermute | solution.py:342
  6.3 23.3 %collective-permute-start = (bf16[474,512]{1,0:T(8,128)(2,1)S(1)}, bf16[474,512]{1,0:T(8,128)(2,1)S(1)}, u32[]{:S(2)}, u32[]{:S(2)}) collective-permute-start(bf16[474,512]{1,0:T(8,128)(2,1)S(1)} %pack_west.1), channel_id=1, source_target_pairs={{4,0},{8,4},{12,8},{0,12},{5,1},{9,5},{13,9},{1,13},{6,2},{10,6},{... | collective-permute-start | bytes 1456136 | tf_op jit(solution)/shard_map/ppermute | solution.py:345
  17.1 12.5 %copy-start.5 = (bf16[256,512]{1,0:T(8,128)(2,1)S(1)}, bf16[256,512]{1,0:T(8,128)(2,1)}, u32[]{:S(2)}) copy-start(bf16[256,512]{1,0:T(8,128)(2,1)} %mesh_lat.3) | copy-start | bytes 786436
  17.1 12.5 %copy-start.8 = (bf16[512,512]{1,0:T(8,128)(2,1)S(1)}, bf16[512,512]{1,0:T(8,128)(2,1)}, u32[]{:S(2)}) copy-start(bf16[512,512]{1,0:T(8,128)(2,1)} %up_w.1) | copy-start | bytes 1572868
  32.2 1.5 %collective-permute-start.2 = (bf16[2,2,64,512]{3,2,1,0:T(8,128)(2,1)S(1)}, bf16[2,2,64,512]{3,2,1,0:T(8,128)(2,1)S(1)}, u32[]{:S(2)}, u32[]{:S(2)}) collective-permute-start(bf16[2,2,64,512]{3,2,1,0:T(8,128)(2,1)S(1)} %get-tuple-element.63), channel_id=1, source_target_pairs={{0,1},{1,0},{2,3},{3,2},{4,5},{5,4},{6,7},{7,6},{8,9},{9,8},{10,11... | collective-permute-start | bytes 786440 | tf_op jit(solution)/shard_map/ppermute | solution.py:270
  32.2 8.1 %collective-permute-start.3 = (bf16[2,2,64,512]{3,2,1,0:T(8,128)(2,1)S(1)}, bf16[2,2,64,512]{3,2,1,0:T(8,128)(2,1)S(1)}, u32[]{:S(2)}, u32[]{:S(2)}) collective-permute-start(bf16[2,2,64,512]{3,2,1,0:T(8,128)(2,1)S(1)} %get-tuple-element.75), channel_id=1, source_target_pairs={{0,1},{1,0},{2,3},{3,2},{4,5},{5,4},{6,7},{7,6},{8,9},{9,8},{10,11... | collective-permute-start | bytes 786440 | tf_op jit(solution)/shard_map/ppermute | solution.py:270
  33.8 6.5 %collective-permute-start.4 = (bf16[2,2,64,512]{3,2,1,0:T(8,128)(2,1)S(1)}, bf16[2,2,64,512]{3,2,1,0:T(8,128)(2,1)S(1)}, u32[]{:S(2)}, u32[]{:S(2)}) collective-permute-start(bf16[2,2,64,512]{3,2,1,0:T(8,128)(2,1)S(1)} %add_convert_fusion.5), channel_id=1, source_target_pairs={{0,2},{1,5},{2,0},{3,7},{4,6},{5,1},{6,4},{7,3},{8,10},{9,13},{10,... | collective-permute-start | bytes 786440 | tf_op jit(solution)/shard_map/ppermute | solution.py:281
  38.8 9.6 %collective-permute-start.5 = (bf16[2,2,64,512]{3,2,1,0:T(8,128)(2,1)S(1)}, bf16[2,2,64,512]{3,2,1,0:T(8,128)(2,1)S(1)}, u32[]{:S(2)}, u32[]{:S(2)}) collective-permute-start(bf16[2,2,64,512]{3,2,1,0:T(8,128)(2,1)S(1)} %get-tuple-element.80), channel_id=1, source_target_pairs={{0,1},{1,0},{2,3},{3,2},{4,5},{5,4},{6,7},{7,6},{8,9},{9,8},{10,11... | collective-permute-start | bytes 786440 | tf_op jit(solution)/shard_map/ppermute | solution.py:270
  38.8 2.4 %collective-permute-start.6 = (bf16[2,2,64,512]{3,2,1,0:T(8,128)(2,1)S(1)}, bf16[2,2,64,512]{3,2,1,0:T(8,128)(2,1)S(1)}, u32[]{:S(2)}, u32[]{:S(2)}) collective-permute-start(bf16[2,2,64,512]{3,2,1,0:T(8,128)(2,1)S(1)} %get-tuple-element.82), channel_id=1, source_target_pairs={{0,1},{1,0},{2,3},{3,2},{4,5},{5,4},{6,7},{7,6},{8,9},{9,8},{10,11... | collective-permute-start | bytes 786440 | tf_op jit(solution)/shard_map/ppermute | solution.py:270
  40.4 6.4 %collective-permute-start.14 = (bf16[1,2,64,512]{3,2,1,0:T(8,128)(2,1)S(1)}, bf16[1,2,64,512]{3,2,1,0:T(8,128)(2,1)S(1)}, u32[]{:S(2)}, u32[]{:S(2)}) collective-permute-start(bf16[1,2,64,512]{3,2,1,0:T(8,128)(2,1)S(1)} %slice.15), channel_id=1, source_target_pairs={{0,4},{1,3},{2,6},{3,1},{4,0},{5,7},{6,2},{7,5},{8,12},{9,11},{10,... | collective-permute-start | bytes 393224 | tf_op jit(solution)/shard_map/ppermute | solution.py:281
  41.3 7.1 %collective-permute-start.7 = (bf16[2,2,64,512]{3,2,1,0:T(8,128)(2,1)S(1)}, bf16[2,2,64,512]{3,2,1,0:T(8,128)(2,1)S(1)}, u32[]{:S(2)}, u32[]{:S(2)}) collective-permute-start(bf16[2,2,64,512]{3,2,1,0:T(8,128)(2,1)S(1)} %add_convert_fusion.1), channel_id=1, source_target_pairs={{0,2},{1,5},{2,0},{3,7},{4,6},{5,1},{6,4},{7,3},{8,10},{9,13},{10,... | collective-permute-start | bytes 786440 | tf_op jit(solution)/shard_map/ppermute | solution.py:281
  46.9 7.3 %collective-permute-start.15 = (bf16[1,2,64,512]{3,2,1,0:T(8,128)(2,1)S(1)}, bf16[1,2,64,512]{3,2,1,0:T(8,128)(2,1)S(1)}, u32[]{:S(2)}, u32[]{:S(2)}) collective-permute-start(bf16[1,2,64,512]{3,2,1,0:T(8,128)(2,1)S(1)} %add_convert_fusion.7), channel_id=1, source_target_pairs={{0,8},{1,9},{2,10},{3,11},{4,12},{5,13},{6,14},{7,15},{8,0},{9,1},... | collective-permute-start | bytes 393224 | tf_op jit(solution)/shard_map/ppermute | solution.py:281
  48.5 6.4 %collective-permute-start.8 = (bf16[1,2,64,512]{3,2,1,0:T(8,128)(2,1)S(1)}, bf16[1,2,64,512]{3,2,1,0:T(8,128)(2,1)S(1)}, u32[]{:S(2)}, u32[]{:S(2)}) collective-permute-start(bf16[1,2,64,512]{3,2,1,0:T(8,128)(2,1)S(1)} %slice.17), channel_id=1, source_target_pairs={{0,4},{1,3},{2,6},{3,1},{4,0},{5,7},{6,2},{7,5},{8,12},{9,11},{10,... | collective-permute-start | bytes 393224 | tf_op jit(solution)/shard_map/ppermute | solution.py:281
  54.3 9.1 %collective-permute-start.16 = (bf16[1,2,64,512]{3,2,1,0:T(8,128)(2,1)S(1)}, bf16[1,2,64,512]{3,2,1,0:T(8,128)(2,1)S(1)}, u32[]{:S(2)}, u32[]{:S(2)}) collective-permute-start(bf16[1,2,64,512]{3,2,1,0:T(8,128)(2,1)S(1)} %add_convert_fusion.6.refs_0_), channel_id=1, source_target_pairs={{0,4},{1,3},{2,6},{3,1},{4,0},{5,7},{6,2},{7,5},{8,12},{9,11},{10,... | collective-permute-start | bytes 393224 | tf_op jit(solution)/shard_map/ppermute | solution.py:281
  54.9 10.1 %collective-permute-start.9 = (bf16[1,2,64,512]{3,2,1,0:T(8,128)(2,1)S(1)}, bf16[1,2,64,512]{3,2,1,0:T(8,128)(2,1)S(1)}, u32[]{:S(2)}, u32[]{:S(2)}) collective-permute-start(bf16[1,2,64,512]{3,2,1,0:T(8,128)(2,1)S(1)} %add_convert_fusion.9), channel_id=1, source_target_pairs={{0,8},{1,9},{2,10},{3,11},{4,12},{5,13},{6,14},{7,15},{8,0},{9,1},... | collective-permute-start | bytes 393224 | tf_op jit(solution)/shard_map/ppermute | solution.py:281
  63.4 6.4 %collective-permute-start.17 = (bf16[2,2,64,512]{3,2,1,0:T(8,128)(2,1)S(1)}, bf16[2,2,64,512]{3,2,1,0:T(8,128)(2,1)S(1)}, u32[]{:S(2)}, u32[]{:S(2)}) collective-permute-start(bf16[2,2,64,512]{3,2,1,0:T(8,128)(2,1)S(1)} %pad_maximum_fusion.1), channel_id=1, source_target_pairs={{0,2},{1,5},{2,0},{3,7},{4,6},{5,1},{6,4},{7,3},{8,10},{9,13},{10,... | collective-permute-start | bytes 786440 | tf_op jit(solution)/shard_map/ppermute | solution.py:281
  65.0 5.0 %collective-permute-start.11 = (bf16[1,2,64,512]{3,2,1,0:T(8,128)(2,1)S(1)}, bf16[1,2,64,512]{3,2,1,0:T(8,128)(2,1)S(1)}, u32[]{:S(2)}, u32[]{:S(2)}) collective-permute-start(bf16[1,2,64,512]{3,2,1,0:T(8,128)(2,1)S(1)} %add_convert_fusion.8.refs_0_), channel_id=1, source_target_pairs={{0,4},{1,3},{2,6},{3,1},{4,0},{5,7},{6,2},{7,5},{8,12},{9,11},{10,... | collective-permute-start | bytes 393224 | tf_op jit(solution)/shard_map/ppermute | solution.py:281
  69.9 3.1 %collective-permute-start.20 = (bf16[2,2,64,512]{3,2,1,0:T(8,128)(2,1)S(1)}, bf16[2,2,64,512]{3,2,1,0:T(8,128)(2,1)S(1)}, u32[]{:S(2)}, u32[]{:S(2)}) collective-permute-start(bf16[2,2,64,512]{3,2,1,0:T(8,128)(2,1)S(1)} %collective-permute-done.17.refs_2_), channel_id=1, source_target_pairs={{0,1},{1,0},{2,3},{3,2},{4,5},{5,4},{6,7},{7,6},{8,9},{9,8},{10,11... | collective-permute-start | bytes 786440 | tf_op jit(solution)/shard_map/ppermute | solution.py:270
  70.0 6.4 %collective-permute-start.13 = (bf16[2,2,64,512]{3,2,1,0:T(8,128)(2,1)S(1)}, bf16[2,2,64,512]{3,2,1,0:T(8,128)(2,1)S(1)}, u32[]{:S(2)}, u32[]{:S(2)}) collective-permute-start(bf16[2,2,64,512]{3,2,1,0:T(8,128)(2,1)S(1)} %pad_maximum_fusion), channel_id=1, source_target_pairs={{0,2},{1,5},{2,0},{3,7},{4,6},{5,1},{6,4},{7,3},{8,10},{9,13},{10,... | collective-permute-start | bytes 786440 | tf_op jit(solution)/shard_map/ppermute | solution.py:281
  71.4 1.3 %collective-permute-start.18 = (bf16[1,2,64,512]{3,2,1,0:T(8,128)(2,1)S(1)}, bf16[1,2,64,512]{3,2,1,0:T(8,128)(2,1)S(1)}, u32[]{:S(2)}, u32[]{:S(2)}) collective-permute-start(bf16[1,2,64,512]{3,2,1,0:T(8,128)(2,1)S(1)} %add_convert_fusion.6.refs_0_), channel_id=1, source_target_pairs={{0,1},{1,0},{2,3},{3,2},{4,5},{5,4},{6,7},{7,6},{8,9},{9,8},{10,11... | collective-permute-start | bytes 393224 | tf_op jit(solution)/shard_map/ppermute | solution.py:270
  71.4 1.5 %collective-permute-start.19 = (bf16[1,2,64,512]{3,2,1,0:T(8,128)(2,1)S(1)}, bf16[1,2,64,512]{3,2,1,0:T(8,128)(2,1)S(1)}, u32[]{:S(2)}, u32[]{:S(2)}) collective-permute-start(bf16[1,2,64,512]{3,2,1,0:T(8,128)(2,1)S(1)} %collective-permute-done.16.refs_1_), channel_id=1, source_target_pairs={{0,1},{1,0},{2,3},{3,2},{4,5},{5,4},{6,7},{7,6},{8,9},{9,8},{10,11... | collective-permute-start | bytes 393224 | tf_op jit(solution)/shard_map/ppermute | solution.py:270
  76.5 1.9 %collective-permute-start.21 = (bf16[2,2,64,512]{3,2,1,0:T(8,128)(2,1)S(1)}, bf16[2,2,64,512]{3,2,1,0:T(8,128)(2,1)S(1)}, u32[]{:S(2)}, u32[]{:S(2)}) collective-permute-start(bf16[2,2,64,512]{3,2,1,0:T(8,128)(2,1)S(1)} %collective-permute-done.13.refs_2_), channel_id=1, source_target_pairs={{0,1},{1,0},{2,3},{3,2},{4,5},{5,4},{6,7},{7,6},{8,9},{9,8},{10,11... | collective-permute-start | bytes 786440 | tf_op jit(solution)/shard_map/ppermute | solution.py:270
  76.5 1.7 %collective-permute-start.10 = (bf16[1,2,64,512]{3,2,1,0:T(8,128)(2,1)S(1)}, bf16[1,2,64,512]{3,2,1,0:T(8,128)(2,1)S(1)}, u32[]{:S(2)}, u32[]{:S(2)}) collective-permute-start(bf16[1,2,64,512]{3,2,1,0:T(8,128)(2,1)S(1)} %add_convert_fusion.8.refs_0_), channel_id=1, source_target_pairs={{0,1},{1,0},{2,3},{3,2},{4,5},{5,4},{6,7},{7,6},{8,9},{9,8},{10,11... | collective-permute-start | bytes 393224 | tf_op jit(solution)/shard_map/ppermute | solution.py:270
  77.0 1.4 %collective-permute-start.12 = (bf16[1,2,64,512]{3,2,1,0:T(8,128)(2,1)S(1)}, bf16[1,2,64,512]{3,2,1,0:T(8,128)(2,1)S(1)}, u32[]{:S(2)}, u32[]{:S(2)}) collective-permute-start(bf16[1,2,64,512]{3,2,1,0:T(8,128)(2,1)S(1)} %collective-permute-done.11.refs_1_), channel_id=1, source_target_pairs={{0,1},{1,0},{2,3},{3,2},{4,5},{5,4},{6,7},{7,6},{8,9},{9,8},{10,11... | collective-permute-start | bytes 393224 | tf_op jit(solution)/shard_map/ppermute | solution.py:270
  (10 other events, 79.9 us)

commit v13 on v12

--- a/solution.py
+++ b/solution.py
@@ -143,8 +143,8 @@
 
 
 def mesh_kernel(
-    x, embed_t, weights_all, h_sum, message_w, up_w, gain, mesh_lat, cot, grad_update,
-    sent_high, sent_low, mesh_grad, grad_gain, gathered, grad_aggregate, normed, grad_pre_up, update, slope, stack,
+    x, embed_t, weights_all, h_sum, message_w, up_w, gain, mesh_lat, grad_update,
+    sent_high, sent_low, grad_mesh, grad_gain, gathered, grad_aggregate, normed, grad_pre_up, update, slope, stack,
 ):
     perm = chunk_order()
     points = x.shape[1]
@@ -165,7 +165,7 @@
     grad_qhat = grad_normed * gains
     grad_q = rinv * (grad_qhat - qhat * jnp.mean(grad_qhat * qhat, axis=1, keepdims=True))
     grad_aggregate[...] = grad_q.astype(BF)
-    mesh_grad[...] = cot[...].astype(F32) + grad_q
+    grad_mesh[...] = grad_q
     theirs = rows_of_half(1 - perm[0] // 4, stack.shape[1])
     stack[0] = contract(gathered[:, theirs], grad_aggregate[...], 0, 0).astype(BF)
     stack[1] = contract(normed[:, theirs], grad_pre_up[...], 0, 0).astype(BF)
@@ -209,8 +209,8 @@
 
 
 def grid_kernel(
-    back, weights_all, slope_own, slope_west, slope_east, x_own, x_west, x_east, grad_gain, update, out_w, mesh_lat, cot,
-    sent_high, sent_low, grad_pre, grad_out, mesh_new, stack,
+    back, weights_all, slope_own, slope_west, slope_east, x_own, x_west, x_east, grad_gain, update, cot,
+    sent_high, sent_low, grad_pre, grad_out, stack,
 ):
     perm = chunk_order()
     for slope, at, all_at in points_of(slope_own, slope_west, slope_east):
@@ -222,7 +222,11 @@
     embed_rows(half, (x_own, x_west, x_east), grad_pre, grad_gain, stack.at[1])
     to_chunks(sent_high, stack, perm, 6)
     to_chunks(sent_low, stack, perm, 4)
+
+
+def nodes_kernel(update, out_w, mesh_lat, cot, grad_mesh, mesh_new, mesh_grad):
     mesh_new[...] = (mesh_lat[...].astype(F32) + contract(update[...], out_w[...], 1, 0)).astype(BF)
+    mesh_grad[...] = cot[...].astype(F32) + grad_mesh[...]
 
 
 def grid_kept_kernel(grad_pre, x_own, x_west, x_east, grad_gain, sums):
@@ -367,14 +371,14 @@
     quarter = shape((2, 2, latent // 8, latent), BF)
     node_rows = shape((nodes, latent), BF)
     (
-        sent_high, sent_low, mesh_grad, gain_term, gathered, grad_aggregate, normed, grad_pre_up, update, slope_east
+        sent_high, sent_low, grad_mesh, gain_term, gathered, grad_aggregate, normed, grad_pre_up, update, slope_east
     ) = call(
-        mesh_kernel, "mesh_nodes", [VMEM] * 10,
+        mesh_kernel, "mesh_nodes", [VMEM] * 9,
         [quarter, quarter, shape((nodes, latent), F32), shape((1, latent), F32)]
         + [node_rows] * 5
         + [shape((latent, side), BF)],
         2_000_000_000, 8 * MIB, 16, [pltpu.VMEM((2, latent // 2, latent), BF)],
-    )(x_east, embed_t, weights_all, h_sum, message_w, up_w, gain.reshape(1, latent), mesh_lat, cot, grad_update)
+    )(x_east, embed_t, weights_all, h_sum, message_w, up_w, gain.reshape(1, latent), mesh_lat, grad_update)
     got_high, got_low = core_swapped(sent_high), core_swapped(sent_low)
     kept_high, kept_low, back = call(
         tail_kernel, "mesh_tail", [VMEM] * 5, [quarter, quarter, shape((latent, nodes), BF)],
@@ -386,12 +390,12 @@
     padded = -(-(features + 1) // 128) * 128
     assert padded == latent
     x_parts = (x_own, x_west, x_east)
-    sent_high, sent_low, grad_pre, grad_out_term, mesh_new = call(
-        grid_kernel, "grid_points", [VMEM] * 13,
-        [quarter, quarter, shape((latent, points), BF), shape((latent, latent), BF), node_rows],
+    sent_high, sent_low, grad_pre, grad_out_term = call(
+        grid_kernel, "grid_points", [VMEM] * 11,
+        [quarter, quarter, shape((latent, points), BF), shape((latent, latent), BF)],
         1_600_000_000, 9 * MIB, 20, [pltpu.VMEM((2, latent // 2, latent), F32)],
     )(
-        back, weights_all, slope_own, slope_west, slope_east, *x_parts, gain_term, update, out_w, mesh_lat, cot
+        back, weights_all, slope_own, slope_west, slope_east, *x_parts, gain_term, update, cot
     )
     got_high, got_low = core_swapped(sent_high), core_swapped(sent_low)
     (sums_b,) = call(
@@ -402,8 +406,14 @@
         kept_chunks_kernel, "kept_chunks", [VMEM] * 2, [quarter, quarter], 8_000_000_000, MIB, 16
     )(grad_out_term, sums_b)
 
+    high_b, low_b = added(kept_high, got_high), added(kept_low, got_low)
+    _, update, grad_mesh = lax.optimization_barrier((high_b, update, grad_mesh))
+    mesh_new, mesh_grad = call(
+        nodes_kernel, "mesh_outputs", [VMEM] * 5, [node_rows, shape((nodes, latent), F32)], 200_000_000, 3 * MIB, 16
+    )(update, out_w, mesh_lat, cot, grad_mesh)
     summed_a = all_summed(kept_a)
-    summed_b = all_summed(halved(added(kept_high, got_high), added(kept_low, got_low)))
+    kept_b, mesh_new, mesh_grad = lax.optimization_barrier((halved(high_b, low_b), mesh_new, mesh_grad))
+    summed_b = all_summed(kept_b)
     square = shape((latent, latent), F32)
     grad_message, grad_up = call(
         order_mesh_kernel, "order_a", [VMEM] * 6, [square, square], 0, 3 * MIB, 16

time: 79.6 us -> 79 us (level)
  starting transfers between devices: 19.9 us -> 19 us
    ppermute x10, starting transfers between devices: 12.6 us -> 11.6 us  [swapped(): return lax.ppermute(value, ('lon', 'lat'), pairs)]
    pallas_call x1, Pallas kernels: 3.03 us -> 3.97 us  [on_device(): call(lambda *refs: weights_kernel(rows, cols // block, *refs), 'slot_weig...]
    ppermute x1, waiting for transfers between devices: 2.86 us -> 1.94 us  [on_device(): lax.ppermute(to_east, 'lon', [(i, (i + 1) % count) for i in range(count)])]
    pallas_call x2 -> x3, Pallas kernels: 5.99 us -> 5.6 us  [the longest x1 2.33 us: on_device(): call(grid_kernel, 'grid_points', [VMEM] * 11, [quarter, quarter, shape((l...]
  transfers between devices with their start and end apart: 22 -> 22, of which waited for: 14 -> 14; matrix products, arithmetic and copies ran while one was open for 1% -> 1% of each run, Pallas kernels for 21% -> 23%
where the time goes in v13:
time: 79 us; the launch traced here: 78.9 us
  waiting for transfers between devices  34.8 us (44%)
  Pallas kernels  21.4 us (27%)
  starting transfers between devices  19 us (24%)
  local copies, waits for them, and re-layouts  1.61 us (2%)
  between operations  1.61 us (2%)
    ppermute x10, waiting for transfers between devices, swapped(): return lax.ppermute(value, ('lon', 'lat'), pairs)  22.2 us
    ppermute x10, starting transfers between devices, swapped(): return lax.ppermute(value, ('lon', 'lat'), pairs)  11.6 us
    ppermute x1, waiting for transfers between devices, on_device(): lax.ppermute(to_west, 'lon', [((i + 1) % count, i) for i in range(count)])  8.71 us
    pallas_call x1, Pallas kernels, on_device(): call(lambda *refs: weights_kernel(rows, cols // block, *refs), 'slot_weig...  3.97 us
    pallas_call x1, Pallas kernels, on_device(): call(own_kernel, 'own_points', [VMEM] * 3, [shape((nodes, latent), F32),...  3.55 us
    ppermute x1, starting transfers between devices, on_device(): lax.ppermute(to_east, 'lon', [(i, (i + 1) % count) for i in range(count)])  3.08 us
    pallas_call x1, Pallas kernels, on_device(): call(grid_kernel, 'grid_points', [VMEM] * 11, [quarter, quarter, shape((l...  2.33 us
    ppermute x10, starting transfers between devices, core_swapped(): lax.ppermute(value, 'lat', [(i, i ^ 1) for i in range(lax.axis_size('lat'...  2.16 us
  transfers between devices with their start and end apart: 22, of which 14 were waited for; matrix products, arithmetic and copies ran while one was open for 1% of the time, Pallas kernels for 23%

profile of v13, /device:TPU:0, one launch (start us, length us, event | category | flops | bytes accessed | tf_op | source)
XLA Modules:
  0.0 78.9 jit_solution(14404449204564607070)
XLA Ops:
  0.6 1.5 %copy-done = bf16[8,256,474]{1,0,2:T(8,128)(2,1)S(1)} copy-done((bf16[8,256,474]{1,0,2:T(8,128)(2,1)S(1)}, bf16[8,256,474]{1,0,2:T(8,128)(2,1)}, u32[]{:S(2)}) %copy-start) | copy-done | bytes 1941528
  2.7 3.1 %collective-permute-start.1 = (bf16[474,512]{1,0:T(8,128)(2,1)S(1)}, bf16[474,512]{1,0:T(8,128)(2,1)S(1)}, u32[]{:S(2)}, u32[]{:S(2)}) collective-permute-start(bf16[474,512]{1,0:T(8,128)(2,1)S(1)} %pack_east.1), channel_id=1, source_target_pairs={{0,4},{4,8},{8,12},{12,0},{1,5},{5,9},{9,13},{13,1},{2,6},{6,10},{... | collective-permute-start | bytes 1456136 | tf_op jit(solution)/shard_map/ppermute | solution.py:346
  6.3 2.1 %collective-permute-start = (bf16[474,512]{1,0:T(8,128)(2,1)S(1)}, bf16[474,512]{1,0:T(8,128)(2,1)S(1)}, u32[]{:S(2)}, u32[]{:S(2)}) collective-permute-start(bf16[474,512]{1,0:T(8,128)(2,1)S(1)} %pack_west.1), channel_id=1, source_target_pairs={{4,0},{8,4},{12,8},{0,12},{5,1},{9,5},{13,9},{1,13},{6,2},{10,6},{... | collective-permute-start | bytes 1456136 | tf_op jit(solution)/shard_map/ppermute | solution.py:349
  9.1 4.0 %slot_weights.1 = (bf16[256,3072]{1,0:T(8,128)(2,1)S(1)}, f32[256,512]{1,0:T(8,128)S(1)}) custom-call(s32[32]{0:T(128)S(1)} %copy-done.6, s32[32]{0:T(128)S(1)} %copy-done.7, s32[1]{0:T(128)S(6)} %copy.23.refs_2_, bf16[32,128,128]{2,1,0:T(8,128)(2,1)S(1)} %copy-done.4, bf16[256,512]{1,0:T(8,128)(2,1)S(1)} %copy-done.2, bf16[512,512]{1,0:T(8,128)(2,1)S(1)} %copy-done.3), custom_call_target="tpu_custom_call" | custom-call | flops 200000000 | bytes 4194304 | tf_op jit(solution)/shard_map/slot_weights/pallas_call | solution.py:351
  13.1 1.3 %own_rows.1 = (bf16[474,2048]{1,0:T(8,128)(2,1)S(1)}, bf16[512,474]{1,0:T(8,128)(2,1)S(1)}) custom-call(bf16[474,8,256]{2,1,0:T(8,128)(2,1)S(1)} %bitcast.5, bf16[474,512]{1,0:T(8,128)(2,1)S(1)} %copy-done.10), custom_call_target="tpu_custom_call" | custom-call | flops 1000000000 | bytes 5242880 | tf_op jit(solution)/shard_map/own_rows/pallas_call | solution.py:356
  14.4 3.6 %own_points.1 = (f32[256,512]{1,0:T(8,128)S(1)}, bf16[512,2048]{1,0:T(8,128)(2,1)S(1)}) custom-call(bf16[474,2048]{1,0:T(8,128)(2,1)S(1)} %get-tuple-element.60.x_t.x_own, bf16[512,474]{1,0:T(8,128)(2,1)S(1)} %get-tuple-element.58.embed_t.refs_1_, bf16[256,3072]{1,0:T(8,128)(2,1)S(1)} %get-tuple-element.59.weights_all.refs_2_), custom_call_target="tpu_custom_call" | custom-call | flops 2000000000 | bytes 7340032 | tf_op jit(solution)/shard_map/own_points/pallas_call | solution.py:360
  18.0 1.9 %collective-permute-done.1.refs_0_.x_west = bf16[474,512]{1,0:T(8,128)(2,1)S(1)} collective-permute-done((bf16[474,512]{1,0:T(8,128)(2,1)S(1)}, bf16[474,512]{1,0:T(8,128)(2,1)S(1)}, u32[]{:S(2)}, u32[]{:S(2)}) %collective-permute-start.1) | collective-permute-done | bytes 485408 | tf_op jit(solution)/shard_map/ppermute | solution.py:346
  20.9 8.7 %collective-permute-done.x.x_east = bf16[474,512]{1,0:T(8,128)(2,1)S(1)} collective-permute-done((bf16[474,512]{1,0:T(8,128)(2,1)S(1)}, bf16[474,512]{1,0:T(8,128)(2,1)S(1)}, u32[]{:S(2)}, u32[]{:S(2)}) %collective-permute-start) | collective-permute-done | bytes 485408 | tf_op jit(solution)/shard_map/ppermute | solution.py:349
  29.6 2.1 %mesh_nodes.1 = (bf16[2,2,64,512]{3,2,1,0:T(8,128)(2,1)S(1)}, bf16[2,2,64,512]{3,2,1,0:T(8,128)(2,1)S(1)}, f32[256,512]{1,0:T(8,128)S(1)}, f32[1,512]{1,0:T(1,12...) custom-call(bf16[474,512]{1,0:T(8,128)(2,1)S(1)} %collective-permute, ...), custom_call_target="tpu_custom_call" | custom-call | flops 2000000000 | bytes 8388608 | tf_op jit(solution)/shard_map/mesh_nodes/pallas_call | solution.py:375
  33.3 1.6 %collective-permute-start.4 = (bf16[2,2,64,512]{3,2,1,0:T(8,128)(2,1)S(1)}, bf16[2,2,64,512]{3,2,1,0:T(8,128)(2,1)S(1)}, u32[]{:S(2)}, u32[]{:S(2)}) collective-permute-start(bf16[2,2,64,512]{3,2,1,0:T(8,128)(2,1)S(1)} %add_convert_fusion.5), channel_id=1, source_target_pairs={{0,2},{1,5},{2,0},{3,7},{4,6},{5,1},{6,4},{7,3},{8,10},{9,13},{10,... | collective-permute-start | bytes 786440 | tf_op jit(solution)/shard_map/ppermute | solution.py:285
  34.9 2.3 %grid_points.1 = (bf16[2,2,64,512]{3,2,1,0:T(8,128)(2,1)S(1)}, bf16[2,2,64,512]{3,2,1,0:T(8,128)(2,1)S(1)}, bf16[512,3072]{1,0:T(8,128)(2,1)S(1)}, bf16[512,512]{1,0:T(8,128)(2,1)S(1)}) custom-call(bf16[512,256]{1,0:T(8,128)(2,1)S(1)} %get-tuple-element.71.back, bf16[256,3072]{1,0:T(8,128)(2,1)S(1)} %get-tuple-element.59.weights_all.refs_2_, ...), custom_call_target="tpu_custom_call" | custom-call | flops 1600000000 | bytes 9437184 | tf_op jit(solution)/shard_map/grid_points/pallas_call | solution.py:393
  40.7 1.6 %collective-permute-start.7 = (bf16[2,2,64,512]{3,2,1,0:T(8,128)(2,1)S(1)}, bf16[2,2,64,512]{3,2,1,0:T(8,128)(2,1)S(1)}, u32[]{:S(2)}, u32[]{:S(2)}) collective-permute-start(bf16[2,2,64,512]{3,2,1,0:T(8,128)(2,1)S(1)} %add_convert_fusion.1), channel_id=1, source_target_pairs={{0,2},{1,5},{2,0},{3,7},{4,6},{5,1},{6,4},{7,3},{8,10},{9,13},{10,... | collective-permute-start | bytes 786440 | tf_op jit(solution)/shard_map/ppermute | solution.py:285
  42.3 1.2 %mesh_outputs.1 = (bf16[256,512]{1,0:T(8,128)(2,1)}, f32[256,512]{1,0:T(8,128)}) custom-call(bf16[256,512]{1,0:T(8,128)(2,1)S(1)} %get-tuple-element.88.update, bf16[512,512]{1,0:T(8,128)(2,1)S(1)} %copy-done.3, bf16[256,512]{1,0:T(8,128)(2,1)S(1)} %copy-done.5, bf16[256,512]{1,0:T(8,128)(2,1)S(1)} %copy-done.2, f32[256,512]{1,0:T(8,128)S(1)} %get-tuple-element.89.grad_mesh), custom_call_target="tpu_custom_call" | custom-call | flops 200000000 | bytes 3145728 | tf_op jit(solution)/shard_map/mesh_outputs/pallas_call | solution.py:411
  43.5 2.8 %collective-permute-done.14 = bf16[1,2,64,512]{3,2,1,0:T(8,128)(2,1)S(1)} collective-permute-done((bf16[1,2,64,512]{3,2,1,0:T(8,128)(2,1)S(1)}, bf16[1,2,64,512]{3,2,1,0:T(8,128)(2,1)S(1)}, u32[]{:S(2)}, u32[]{:S(2)}) %collective-permute-start.14) | collective-permute-done | bytes 131104 | tf_op jit(solution)/shard_map/ppermute | solution.py:285
  46.4 1.7 %collective-permute-start.15 = (bf16[1,2,64,512]{3,2,1,0:T(8,128)(2,1)S(1)}, bf16[1,2,64,512]{3,2,1,0:T(8,128)(2,1)S(1)}, u32[]{:S(2)}, u32[]{:S(2)}) collective-permute-start(bf16[1,2,64,512]{3,2,1,0:T(8,128)(2,1)S(1)} %add_convert_fusion.7), channel_id=1, source_target_pairs={{0,8},{1,9},{2,10},{3,11},{4,12},{5,13},{6,14},{7,15},{8,0},{9,1},... | collective-permute-start | bytes 393224 | tf_op jit(solution)/shard_map/ppermute | solution.py:285
  48.2 1.6 %collective-permute-start.8 = (bf16[1,2,64,512]{3,2,1,0:T(8,128)(2,1)S(1)}, bf16[1,2,64,512]{3,2,1,0:T(8,128)(2,1)S(1)}, u32[]{:S(2)}, u32[]{:S(2)}) collective-permute-start(bf16[1,2,64,512]{3,2,1,0:T(8,128)(2,1)S(1)} %slice.13), channel_id=1, source_target_pairs={{0,4},{1,3},{2,6},{3,1},{4,0},{5,7},{6,2},{7,5},{8,12},{9,11},{10,... | collective-permute-start | bytes 393224 | tf_op jit(solution)/shard_map/ppermute | solution.py:285
  49.9 3.9 %collective-permute-done.15 = bf16[1,2,64,512]{3,2,1,0:T(8,128)(2,1)S(1)} collective-permute-done((bf16[1,2,64,512]{3,2,1,0:T(8,128)(2,1)S(1)}, bf16[1,2,64,512]{3,2,1,0:T(8,128)(2,1)S(1)}, u32[]{:S(2)}, u32[]{:S(2)}) %collective-permute-start.15) | collective-permute-done | bytes 131104 | tf_op jit(solution)/shard_map/ppermute | solution.py:285
  54.6 2.5 %collective-permute-start.9 = (bf16[1,2,64,512]{3,2,1,0:T(8,128)(2,1)S(1)}, bf16[1,2,64,512]{3,2,1,0:T(8,128)(2,1)S(1)}, u32[]{:S(2)}, u32[]{:S(2)}) collective-permute-start(bf16[1,2,64,512]{3,2,1,0:T(8,128)(2,1)S(1)} %add_convert_fusion.9), channel_id=1, source_target_pairs={{0,8},{1,9},{2,10},{3,11},{4,12},{5,13},{6,14},{7,15},{8,0},{9,1},... | collective-permute-start | bytes 393224 | tf_op jit(solution)/shard_map/ppermute | solution.py:285
  57.0 6.0 %collective-permute-done.16.refs_1_ = bf16[1,2,64,512]{3,2,1,0:T(8,128)(2,1)S(1)} collective-permute-done((bf16[1,2,64,512]{3,2,1,0:T(8,128)(2,1)S(1)}, bf16[1,2,64,512]{3,2,1,0:T(8,128)(2,1)S(1)}, u32[]{:S(2)}, u32[]{:S(2)}) %collective-permute-start.16) | collective-permute-done | bytes 131104 | tf_op jit(solution)/shard_map/ppermute | solution.py:285
  64.2 5.3 %collective-permute-done.17.refs_2_ = bf16[2,2,64,512]{3,2,1,0:T(8,128)(2,1)S(1)} collective-permute-done((bf16[2,2,64,512]{3,2,1,0:T(8,128)(2,1)S(1)}, bf16[2,2,64,512]{3,2,1,0:T(8,128)(2,1)S(1)}, u32[]{:S(2)}, u32[]{:S(2)}) %collective-permute-start.17) | collective-permute-done | bytes 262176 | tf_op jit(solution)/shard_map/ppermute | solution.py:285
  71.8 1.5 %order_a.1 = (f32[512,512]{1,0:T(8,128)}, f32[512,512]{1,0:T(8,128)}) custom-call(bf16[1,2,64,512]{3,2,1,0:T(8,128)(2,1)S(1)} %add_convert_fusion.6.refs_0_, bf16[1,2,64,512]{3,2,1,0:T(8,128)(2,1)S(1)} %collective-permute-done.16.refs_1_, bf16[2,2,64,512]{3,2,1,0:T(8,128)(2,1)S(1)} %collective-permute-done.17.refs_2_, ...), custom_call_target="tpu_custom_call" | custom-call | bytes 3145728 | tf_op jit(solution)/shard_map/order_a/pallas_call | solution.py:418
  73.3 2.7 %collective-permute-done.13.refs_2_ = bf16[2,2,64,512]{3,2,1,0:T(8,128)(2,1)S(1)} collective-permute-done((bf16[2,2,64,512]{3,2,1,0:T(8,128)(2,1)S(1)}, bf16[2,2,64,512]{3,2,1,0:T(8,128)(2,1)S(1)}, u32[]{:S(2)}, u32[]{:S(2)}) %collective-permute-start.13) | collective-permute-done | bytes 262176 | tf_op jit(solution)/shard_map/ppermute | solution.py:285
  76.5 1.0 %order_b.2 = (f32[512,512]{1,0:T(8,128)}, f32[474,512]{1,0:T(8,128)}, f32[1,512]{1,0:T(1,128)S(1)}) custom-call(bf16[1,2,64,512]{3,2,1,0:T(8,128)(2,1)S(1)} %add_convert_fusion.8.refs_0_, bf16[1,2,64,512]{3,2,1,0:T(8,128)(2,1)S(1)} %collective-permute-done.11.refs_1_, bf16[2,2,64,512]{3,2,1,0:T(8,128)(2,1)S(1)} %collective-permute-done.13.refs_2_), custom_call_target="tpu_custom_call" | custom-call | bytes 2097152 | tf_op jit(solution)/shard_map/order_b/pallas_call | solution.py:429
  77.9 1.0 %order_b.3 = (f32[512,512]{1,0:T(8,128)}, f32[474,512]{1,0:T(8,128)}, f32[1,512]{1,0:T(1,128)}) custom-call(bf16[1,2,64,512]{3,2,1,0:T(8,128)(2,1)S(1)} %collective-permute-done.10.refs_0_, bf16[1,2,64,512]{3,2,1,0:T(8,128)(2,1)S(1)} %collective-permute-done.12.refs_1_, ...), custom_call_target="tpu_custom_call", output_to_operand_aliasing={{0}: (4, {}), {1}: (5, {})} | custom-call | bytes 2097152 | tf_op jit(solution)/shard_map/order_b/pallas_call | solution.py:429
  (71 shorter events, 12.3 us)
Async XLA Ops:
  2.7 17.2 %collective-permute-start.1 = (bf16[474,512]{1,0:T(8,128)(2,1)S(1)}, bf16[474,512]{1,0:T(8,128)(2,1)S(1)}, u32[]{:S(2)}, u32[]{:S(2)}) collective-permute-start(bf16[474,512]{1,0:T(8,128)(2,1)S(1)} %pack_east.1), channel_id=1, source_target_pairs={{0,4},{4,8},{8,12},{12,0},{1,5},{5,9},{9,13},{13,1},{2,6},{6,10},{... | collective-permute-start | bytes 1456136 | tf_op jit(solution)/shard_map/ppermute | solution.py:346
  6.3 23.3 %collective-permute-start = (bf16[474,512]{1,0:T(8,128)(2,1)S(1)}, bf16[474,512]{1,0:T(8,128)(2,1)S(1)}, u32[]{:S(2)}, u32[]{:S(2)}) collective-permute-start(bf16[474,512]{1,0:T(8,128)(2,1)S(1)} %pack_west.1), channel_id=1, source_target_pairs={{4,0},{8,4},{12,8},{0,12},{5,1},{9,5},{13,9},{1,13},{6,2},{10,6},{... | collective-permute-start | bytes 1456136 | tf_op jit(solution)/shard_map/ppermute | solution.py:349
  18.0 11.6 %copy-start.5 = (bf16[256,512]{1,0:T(8,128)(2,1)S(1)}, bf16[256,512]{1,0:T(8,128)(2,1)}, u32[]{:S(2)}) copy-start(bf16[256,512]{1,0:T(8,128)(2,1)} %mesh_lat.3) | copy-start | bytes 786436
  18.0 11.6 %copy-start.8 = (bf16[512,512]{1,0:T(8,128)(2,1)S(1)}, bf16[512,512]{1,0:T(8,128)(2,1)}, u32[]{:S(2)}) copy-start(bf16[512,512]{1,0:T(8,128)(2,1)} %up_w.1) | copy-start | bytes 1572868
  31.7 1.6 %collective-permute-start.2 = (bf16[2,2,64,512]{3,2,1,0:T(8,128)(2,1)S(1)}, bf16[2,2,64,512]{3,2,1,0:T(8,128)(2,1)S(1)}, u32[]{:S(2)}, u32[]{:S(2)}) collective-permute-start(bf16[2,2,64,512]{3,2,1,0:T(8,128)(2,1)S(1)} %get-tuple-element.69), channel_id=1, source_target_pairs={{0,1},{1,0},{2,3},{3,2},{4,5},{5,4},{6,7},{7,6},{8,9},{9,8},{10,11... | collective-permute-start | bytes 786440 | tf_op jit(solution)/shard_map/ppermute | solution.py:274
  31.8 7.1 %collective-permute-start.3 = (bf16[2,2,64,512]{3,2,1,0:T(8,128)(2,1)S(1)}, bf16[2,2,64,512]{3,2,1,0:T(8,128)(2,1)S(1)}, u32[]{:S(2)}, u32[]{:S(2)}) collective-permute-start(bf16[2,2,64,512]{3,2,1,0:T(8,128)(2,1)S(1)} %get-tuple-element.79), channel_id=1, source_target_pairs={{0,1},{1,0},{2,3},{3,2},{4,5},{5,4},{6,7},{7,6},{8,9},{9,8},{10,11... | collective-permute-start | bytes 786440 | tf_op jit(solution)/shard_map/ppermute | solution.py:274
  33.3 6.4 %collective-permute-start.4 = (bf16[2,2,64,512]{3,2,1,0:T(8,128)(2,1)S(1)}, bf16[2,2,64,512]{3,2,1,0:T(8,128)(2,1)S(1)}, u32[]{:S(2)}, u32[]{:S(2)}) collective-permute-start(bf16[2,2,64,512]{3,2,1,0:T(8,128)(2,1)S(1)} %add_convert_fusion.5), channel_id=1, source_target_pairs={{0,2},{1,5},{2,0},{3,7},{4,6},{5,1},{6,4},{7,3},{8,10},{9,13},{10,... | collective-permute-start | bytes 786440 | tf_op jit(solution)/shard_map/ppermute | solution.py:285
  37.3 10.8 %collective-permute-start.5 = (bf16[2,2,64,512]{3,2,1,0:T(8,128)(2,1)S(1)}, bf16[2,2,64,512]{3,2,1,0:T(8,128)(2,1)S(1)}, u32[]{:S(2)}, u32[]{:S(2)}) collective-permute-start(bf16[2,2,64,512]{3,2,1,0:T(8,128)(2,1)S(1)} %get-tuple-element.84), channel_id=1, source_target_pairs={{0,1},{1,0},{2,3},{3,2},{4,5},{5,4},{6,7},{7,6},{8,9},{9,8},{10,11... | collective-permute-start | bytes 786440 | tf_op jit(solution)/shard_map/ppermute | solution.py:274
  37.3 3.3 %collective-permute-start.6 = (bf16[2,2,64,512]{3,2,1,0:T(8,128)(2,1)S(1)}, bf16[2,2,64,512]{3,2,1,0:T(8,128)(2,1)S(1)}, u32[]{:S(2)}, u32[]{:S(2)}) collective-permute-start(bf16[2,2,64,512]{3,2,1,0:T(8,128)(2,1)S(1)} %get-tuple-element.86), channel_id=1, source_target_pairs={{0,1},{1,0},{2,3},{3,2},{4,5},{5,4},{6,7},{7,6},{8,9},{9,8},{10,11... | collective-permute-start | bytes 786440 | tf_op jit(solution)/shard_map/ppermute | solution.py:274
  39.9 6.4 %collective-permute-start.14 = (bf16[1,2,64,512]{3,2,1,0:T(8,128)(2,1)S(1)}, bf16[1,2,64,512]{3,2,1,0:T(8,128)(2,1)S(1)}, u32[]{:S(2)}, u32[]{:S(2)}) collective-permute-start(bf16[1,2,64,512]{3,2,1,0:T(8,128)(2,1)S(1)} %slice.15), channel_id=1, source_target_pairs={{0,4},{1,3},{2,6},{3,1},{4,0},{5,7},{6,2},{7,5},{8,12},{9,11},{10,... | collective-permute-start | bytes 393224 | tf_op jit(solution)/shard_map/ppermute | solution.py:285
  40.7 7.4 %collective-permute-start.7 = (bf16[2,2,64,512]{3,2,1,0:T(8,128)(2,1)S(1)}, bf16[2,2,64,512]{3,2,1,0:T(8,128)(2,1)S(1)}, u32[]{:S(2)}, u32[]{:S(2)}) collective-permute-start(bf16[2,2,64,512]{3,2,1,0:T(8,128)(2,1)S(1)} %add_convert_fusion.1), channel_id=1, source_target_pairs={{0,2},{1,5},{2,0},{3,7},{4,6},{5,1},{6,4},{7,3},{8,10},{9,13},{10,... | collective-permute-start | bytes 786440 | tf_op jit(solution)/shard_map/ppermute | solution.py:285
  46.4 7.4 %collective-permute-start.15 = (bf16[1,2,64,512]{3,2,1,0:T(8,128)(2,1)S(1)}, bf16[1,2,64,512]{3,2,1,0:T(8,128)(2,1)S(1)}, u32[]{:S(2)}, u32[]{:S(2)}) collective-permute-start(bf16[1,2,64,512]{3,2,1,0:T(8,128)(2,1)S(1)} %add_convert_fusion.7), channel_id=1, source_target_pairs={{0,8},{1,9},{2,10},{3,11},{4,12},{5,13},{6,14},{7,15},{8,0},{9,1},... | collective-permute-start | bytes 393224 | tf_op jit(solution)/shard_map/ppermute | solution.py:285
  48.2 6.3 %collective-permute-start.8 = (bf16[1,2,64,512]{3,2,1,0:T(8,128)(2,1)S(1)}, bf16[1,2,64,512]{3,2,1,0:T(8,128)(2,1)S(1)}, u32[]{:S(2)}, u32[]{:S(2)}) collective-permute-start(bf16[1,2,64,512]{3,2,1,0:T(8,128)(2,1)S(1)} %slice.13), channel_id=1, source_target_pairs={{0,4},{1,3},{2,6},{3,1},{4,0},{5,7},{6,2},{7,5},{8,12},{9,11},{10,... | collective-permute-start | bytes 393224 | tf_op jit(solution)/shard_map/ppermute | solution.py:285
  53.9 9.1 %collective-permute-start.16 = (bf16[1,2,64,512]{3,2,1,0:T(8,128)(2,1)S(1)}, bf16[1,2,64,512]{3,2,1,0:T(8,128)(2,1)S(1)}, u32[]{:S(2)}, u32[]{:S(2)}) collective-permute-start(bf16[1,2,64,512]{3,2,1,0:T(8,128)(2,1)S(1)} %add_convert_fusion.6.refs_0_), channel_id=1, source_target_pairs={{0,4},{1,3},{2,6},{3,1},{4,0},{5,7},{6,2},{7,5},{8,12},{9,11},{10,... | collective-permute-start | bytes 393224 | tf_op jit(solution)/shard_map/ppermute | solution.py:285
  54.6 8.8 %collective-permute-start.9 = (bf16[1,2,64,512]{3,2,1,0:T(8,128)(2,1)S(1)}, bf16[1,2,64,512]{3,2,1,0:T(8,128)(2,1)S(1)}, u32[]{:S(2)}, u32[]{:S(2)}) collective-permute-start(bf16[1,2,64,512]{3,2,1,0:T(8,128)(2,1)S(1)} %add_convert_fusion.9), channel_id=1, source_target_pairs={{0,8},{1,9},{2,10},{3,11},{4,12},{5,13},{6,14},{7,15},{8,0},{9,1},... | collective-permute-start | bytes 393224 | tf_op jit(solution)/shard_map/ppermute | solution.py:285
  63.0 6.4 %collective-permute-start.17 = (bf16[2,2,64,512]{3,2,1,0:T(8,128)(2,1)S(1)}, bf16[2,2,64,512]{3,2,1,0:T(8,128)(2,1)S(1)}, u32[]{:S(2)}, u32[]{:S(2)}) collective-permute-start(bf16[2,2,64,512]{3,2,1,0:T(8,128)(2,1)S(1)} %pad_maximum_fusion.1), channel_id=1, source_target_pairs={{0,2},{1,5},{2,0},{3,7},{4,6},{5,1},{6,4},{7,3},{8,10},{9,13},{10,... | collective-permute-start | bytes 786440 | tf_op jit(solution)/shard_map/ppermute | solution.py:285
  63.4 6.1 %collective-permute-start.11 = (bf16[1,2,64,512]{3,2,1,0:T(8,128)(2,1)S(1)}, bf16[1,2,64,512]{3,2,1,0:T(8,128)(2,1)S(1)}, u32[]{:S(2)}, u32[]{:S(2)}) collective-permute-start(bf16[1,2,64,512]{3,2,1,0:T(8,128)(2,1)S(1)} %add_convert_fusion.8.refs_0_), channel_id=1, source_target_pairs={{0,4},{1,3},{2,6},{3,1},{4,0},{5,7},{6,2},{7,5},{8,12},{9,11},{10,... | collective-permute-start | bytes 393224 | tf_op jit(solution)/shard_map/ppermute | solution.py:285
  69.5 2.4 %collective-permute-start.20 = (bf16[2,2,64,512]{3,2,1,0:T(8,128)(2,1)S(1)}, bf16[2,2,64,512]{3,2,1,0:T(8,128)(2,1)S(1)}, u32[]{:S(2)}, u32[]{:S(2)}) collective-permute-start(bf16[2,2,64,512]{3,2,1,0:T(8,128)(2,1)S(1)} %collective-permute-done.17.refs_2_), channel_id=1, source_target_pairs={{0,1},{1,0},{2,3},{3,2},{4,5},{5,4},{6,7},{7,6},{8,9},{9,8},{10,11... | collective-permute-start | bytes 786440 | tf_op jit(solution)/shard_map/ppermute | solution.py:274
  69.5 6.4 %collective-permute-start.13 = (bf16[2,2,64,512]{3,2,1,0:T(8,128)(2,1)S(1)}, bf16[2,2,64,512]{3,2,1,0:T(8,128)(2,1)S(1)}, u32[]{:S(2)}, u32[]{:S(2)}) collective-permute-start(bf16[2,2,64,512]{3,2,1,0:T(8,128)(2,1)S(1)} %pad_maximum_fusion), channel_id=1, source_target_pairs={{0,2},{1,5},{2,0},{3,7},{4,6},{5,1},{6,4},{7,3},{8,10},{9,13},{10,... | collective-permute-start | bytes 786440 | tf_op jit(solution)/shard_map/ppermute | solution.py:285
  70.3 1.3 %collective-permute-start.18 = (bf16[1,2,64,512]{3,2,1,0:T(8,128)(2,1)S(1)}, bf16[1,2,64,512]{3,2,1,0:T(8,128)(2,1)S(1)}, u32[]{:S(2)}, u32[]{:S(2)}) collective-permute-start(bf16[1,2,64,512]{3,2,1,0:T(8,128)(2,1)S(1)} %add_convert_fusion.6.refs_0_), channel_id=1, source_target_pairs={{0,1},{1,0},{2,3},{3,2},{4,5},{5,4},{6,7},{7,6},{8,9},{9,8},{10,11... | collective-permute-start | bytes 393224 | tf_op jit(solution)/shard_map/ppermute | solution.py:274
  70.3 1.5 %collective-permute-start.19 = (bf16[1,2,64,512]{3,2,1,0:T(8,128)(2,1)S(1)}, bf16[1,2,64,512]{3,2,1,0:T(8,128)(2,1)S(1)}, u32[]{:S(2)}, u32[]{:S(2)}) collective-permute-start(bf16[1,2,64,512]{3,2,1,0:T(8,128)(2,1)S(1)} %collective-permute-done.16.refs_1_), channel_id=1, source_target_pairs={{0,1},{1,0},{2,3},{3,2},{4,5},{5,4},{6,7},{7,6},{8,9},{9,8},{10,11... | collective-permute-start | bytes 393224 | tf_op jit(solution)/shard_map/ppermute | solution.py:274
  76.0 1.9 %collective-permute-start.21 = (bf16[2,2,64,512]{3,2,1,0:T(8,128)(2,1)S(1)}, bf16[2,2,64,512]{3,2,1,0:T(8,128)(2,1)S(1)}, u32[]{:S(2)}, u32[]{:S(2)}) collective-permute-start(bf16[2,2,64,512]{3,2,1,0:T(8,128)(2,1)S(1)} %collective-permute-done.13.refs_2_), channel_id=1, source_target_pairs={{0,1},{1,0},{2,3},{3,2},{4,5},{5,4},{6,7},{7,6},{8,9},{9,8},{10,11... | collective-permute-start | bytes 786440 | tf_op jit(solution)/shard_map/ppermute | solution.py:274
  76.0 1.7 %collective-permute-start.10 = (bf16[1,2,64,512]{3,2,1,0:T(8,128)(2,1)S(1)}, bf16[1,2,64,512]{3,2,1,0:T(8,128)(2,1)S(1)}, u32[]{:S(2)}, u32[]{:S(2)}) collective-permute-start(bf16[1,2,64,512]{3,2,1,0:T(8,128)(2,1)S(1)} %add_convert_fusion.8.refs_0_), channel_id=1, source_target_pairs={{0,1},{1,0},{2,3},{3,2},{4,5},{5,4},{6,7},{7,6},{8,9},{9,8},{10,11... | collective-permute-start | bytes 393224 | tf_op jit(solution)/shard_map/ppermute | solution.py:274
  76.5 1.4 %collective-permute-start.12 = (bf16[1,2,64,512]{3,2,1,0:T(8,128)(2,1)S(1)}, bf16[1,2,64,512]{3,2,1,0:T(8,128)(2,1)S(1)}, u32[]{:S(2)}, u32[]{:S(2)}) collective-permute-start(bf16[1,2,64,512]{3,2,1,0:T(8,128)(2,1)S(1)} %collective-permute-done.11.refs_1_), channel_id=1, source_target_pairs={{0,1},{1,0},{2,3},{3,2},{4,5},{5,4},{6,7},{7,6},{8,9},{9,8},{10,11... | collective-permute-start | bytes 393224 | tf_op jit(solution)/shard_map/ppermute | solution.py:274
  (10 other events, 80.0 us)

commit v14 on v13

--- a/solution.py
+++ b/solution.py
@@ -342,7 +342,9 @@
     strip = shape((features, side), BF)
     wide = pltpu.VMEM((features * rows, block), F32)
     count = lax.axis_size("lon")
-    (to_east,) = call(lambda *refs: pack_kernel(True, *refs), "pack_east", [VMEM], [strip], 0, MIB, 8, [wide])(grid)
+    (to_east,) = call(lambda *refs: pack_kernel(True, *refs), "pack_east", [VMEM], [strip], 0, MIB, 8, [wide])(
+        grid[:, :, cols - block :]
+    )
     x_west = lax.ppermute(to_east, "lon", [(i, (i + 1) % count) for i in range(count)])
     to_east, later = lax.optimization_barrier((to_east, grid))
     (to_west,) = call(lambda *refs: pack_kernel(False, *refs), "pack_west", [VMEM], [strip], 0, MIB, 8, [wide])(later)
@@ -379,14 +381,14 @@
         + [shape((latent, side), BF)],
         2_000_000_000, 8 * MIB, 16, [pltpu.VMEM((2, latent // 2, latent), BF)],
     )(x_east, embed_t, weights_all, h_sum, message_w, up_w, gain.reshape(1, latent), mesh_lat, grad_update)
-    got_high, got_low = core_swapped(sent_high), core_swapped(sent_low)
+    got_high = core_swapped(sent_high)
     kept_high, kept_low, back = call(
         tail_kernel, "mesh_tail", [VMEM] * 5, [quarter, quarter, shape((latent, nodes), BF)],
         500_000_000, 3 * MIB, 16, [pltpu.VMEM((2, latent // 2, latent), BF)],
     )(gathered, grad_aggregate, normed, grad_pre_up, message_w)
 
-    high_a, back = lax.optimization_barrier((added(kept_high, got_high), back))
-    low_a = added(kept_low, got_low)
+    high_a, back, sent_low = lax.optimization_barrier((added(kept_high, got_high), back, sent_low))
+    low_a = added(kept_low, core_swapped(sent_low))
     padded = -(-(features + 1) // 128) * 128
     assert padded == latent
     x_parts = (x_own, x_west, x_east)

time: 79 us -> 79.1 us (level)
  waiting for transfers between devices: 34.8 us -> 36.5 us
  Pallas kernels: 21.4 us -> 20.5 us
    unnamed x24 -> x22, local copies, waits for them, and re-layouts: 1.59 us -> 0.07 us
    slice x0 -> x1, local copies, waits for them, and re-layouts: none -> 1.4 us  [on_device(): grid[:, :, cols - block:]]
    pallas_call x1, Pallas kernels: 3.97 us -> 3.03 us  [on_device(): call(lambda *refs: weights_kernel(rows, cols // block, *refs), 'slot_weig...]
    ppermute x1, waiting for transfers between devices: 1.94 us -> 2.86 us  [on_device(): lax.ppermute(to_east, 'lon', [(i, (i + 1) % count) for i in range(count)])]
  transfers between devices with their start and end apart: 22 -> 22, of which waited for: 14 -> 14; matrix products, arithmetic and copies ran while one was open for 1% -> 1% of each run, Pallas kernels for 23% -> 21%
where the time goes in v14:
time: 79.1 us; the launch traced here: 79 us
  waiting for transfers between devices  36.5 us (46%)
  Pallas kernels  20.5 us (26%)
  starting transfers between devices  18.4 us (23%)
  between operations  1.62 us (2%)
  local copies, waits for them, and re-layouts  1.49 us (2%)
    ppermute x10, waiting for transfers between devices, swapped(): return lax.ppermute(value, ('lon', 'lat'), pairs)  22.5 us
    ppermute x10, starting transfers between devices, swapped(): return lax.ppermute(value, ('lon', 'lat'), pairs)  11.3 us
    ppermute x1, waiting for transfers between devices, on_device(): lax.ppermute(to_west, 'lon', [((i + 1) % count, i) for i in range(count)])  8.72 us
    pallas_call x1, Pallas kernels, on_device(): call(own_kernel, 'own_points', [VMEM] * 3, [shape((nodes, latent), F32),...  3.55 us
    ppermute x1, starting transfers between devices, on_device(): lax.ppermute(to_east, 'lon', [(i, (i + 1) % count) for i in range(count)])  3.08 us
    pallas_call x1, Pallas kernels, on_device(): call(lambda *refs: weights_kernel(rows, cols // block, *refs), 'slot_weig...  3.03 us
    ppermute x1, waiting for transfers between devices, on_device(): lax.ppermute(to_east, 'lon', [(i, (i + 1) % count) for i in range(count)])  2.86 us
    ppermute x10, waiting for transfers between devices, core_swapped(): lax.ppermute(value, 'lat', [(i, i ^ 1) for i in range(lax.axis_size('lat'...  2.41 us
  transfers between devices with their start and end apart: 22, of which 14 were waited for; matrix products, arithmetic and copies ran while one was open for 1% of the time, Pallas kernels for 21%

profile of v14, /device:TPU:0, one launch (start us, length us, event | category | flops | bytes accessed | tf_op | source)
XLA Modules:
  0.0 79.0 jit_solution(1448211511226601534)
XLA Ops:
  0.6 1.4 %slice.20.refs_0_ = bf16[474,8,128]{2,1,0:T(8,128)(2,1)S(1)} slice(bf16[474,8,256]{2,1,0:T(8,128)(2,1)} %bitcast.3), slice={[0:474], [0:8], [128:256]} | slice | bytes 1941504 | tf_op jit(solution)/shard_map/slice | solution.py:346
  2.6 3.1 %collective-permute-start.1 = (bf16[474,512]{1,0:T(8,128)(2,1)S(1)}, bf16[474,512]{1,0:T(8,128)(2,1)S(1)}, u32[]{:S(2)}, u32[]{:S(2)}) collective-permute-start(bf16[474,512]{1,0:T(8,128)(2,1)S(1)} %pack_east.1), channel_id=1, source_target_pairs={{0,4},{4,8},{8,12},{12,0},{1,5},{5,9},{9,13},{13,1},{2,6},{6,10},{... | collective-permute-start | bytes 1456136 | tf_op jit(solution)/shard_map/ppermute | solution.py:348
  6.2 2.1 %collective-permute-start = (bf16[474,512]{1,0:T(8,128)(2,1)S(1)}, bf16[474,512]{1,0:T(8,128)(2,1)S(1)}, u32[]{:S(2)}, u32[]{:S(2)}) collective-permute-start(bf16[474,512]{1,0:T(8,128)(2,1)S(1)} %pack_west.1), channel_id=1, source_target_pairs={{4,0},{8,4},{12,8},{0,12},{5,1},{9,5},{13,9},{1,13},{6,2},{10,6},{... | collective-permute-start | bytes 1456136 | tf_op jit(solution)/shard_map/ppermute | solution.py:351
  9.0 3.0 %slot_weights.1 = (bf16[256,3072]{1,0:T(8,128)(2,1)S(1)}, f32[256,512]{1,0:T(8,128)S(1)}) custom-call(s32[32]{0:T(128)S(1)} %copy-done.5, s32[32]{0:T(128)S(1)} %copy-done.6, s32[1]{0:T(128)S(6)} %copy.23.refs_2_, bf16[32,128,128]{2,1,0:T(8,128)(2,1)S(1)} %copy-done.3, bf16[256,512]{1,0:T(8,128)(2,1)S(1)} %copy-done.1, bf16[512,512]{1,0:T(8,128)(2,1)S(1)} %copy-done.2), custom_call_target="tpu_custom_call" | custom-call | flops 200000000 | bytes 4194304 | tf_op jit(solution)/shard_map/slot_weights/pallas_call | solution.py:353
  12.1 1.3 %own_rows.1 = (bf16[474,2048]{1,0:T(8,128)(2,1)S(1)}, bf16[512,474]{1,0:T(8,128)(2,1)S(1)}) custom-call(bf16[474,8,256]{2,1,0:T(8,128)(2,1)S(1)} %bitcast.5, bf16[474,512]{1,0:T(8,128)(2,1)S(1)} %copy-done.9), custom_call_target="tpu_custom_call" | custom-call | flops 1000000000 | bytes 5242880 | tf_op jit(solution)/shard_map/own_rows/pallas_call | solution.py:358
  13.4 3.5 %own_points.1 = (f32[256,512]{1,0:T(8,128)S(1)}, bf16[512,2048]{1,0:T(8,128)(2,1)S(1)}) custom-call(bf16[474,2048]{1,0:T(8,128)(2,1)S(1)} %get-tuple-element.61.x_t.x_own, bf16[512,474]{1,0:T(8,128)(2,1)S(1)} %get-tuple-element.59.embed_t.refs_1_, bf16[256,3072]{1,0:T(8,128)(2,1)S(1)} %get-tuple-element.60.weights_all.refs_2_), custom_call_target="tpu_custom_call" | custom-call | flops 2000000000 | bytes 7340032 | tf_op jit(solution)/shard_map/own_points/pallas_call | solution.py:362
  17.0 2.9 %collective-permute-done.1.refs_0_.x_west = bf16[474,512]{1,0:T(8,128)(2,1)S(1)} collective-permute-done((bf16[474,512]{1,0:T(8,128)(2,1)S(1)}, bf16[474,512]{1,0:T(8,128)(2,1)S(1)}, u32[]{:S(2)}, u32[]{:S(2)}) %collective-permute-start.1) | collective-permute-done | bytes 485408 | tf_op jit(solution)/shard_map/ppermute | solution.py:348
  20.8 8.7 %collective-permute-done.x.x_east = bf16[474,512]{1,0:T(8,128)(2,1)S(1)} collective-permute-done((bf16[474,512]{1,0:T(8,128)(2,1)S(1)}, bf16[474,512]{1,0:T(8,128)(2,1)S(1)}, u32[]{:S(2)}, u32[]{:S(2)}) %collective-permute-start) | collective-permute-done | bytes 485408 | tf_op jit(solution)/shard_map/ppermute | solution.py:351
  29.5 2.1 %mesh_nodes.1 = (bf16[2,2,64,512]{3,2,1,0:T(8,128)(2,1)S(1)}, bf16[2,2,64,512]{3,2,1,0:T(8,128)(2,1)S(1)}, f32[256,512]{1,0:T(8,128)S(1)}, f32[1,512]{1,0:T(1,12...) custom-call(bf16[474,512]{1,0:T(8,128)(2,1)S(1)} %collective-permute, ...), custom_call_target="tpu_custom_call" | custom-call | flops 2000000000 | bytes 8388608 | tf_op jit(solution)/shard_map/mesh_nodes/pallas_call | solution.py:377
  33.5 1.5 %collective-permute-start.4 = (bf16[2,2,64,512]{3,2,1,0:T(8,128)(2,1)S(1)}, bf16[2,2,64,512]{3,2,1,0:T(8,128)(2,1)S(1)}, u32[]{:S(2)}, u32[]{:S(2)}) collective-permute-start(bf16[2,2,64,512]{3,2,1,0:T(8,128)(2,1)S(1)} %add_convert_fusion.5), channel_id=1, source_target_pairs={{0,2},{1,5},{2,0},{3,7},{4,6},{5,1},{6,4},{7,3},{8,10},{9,13},{10,... | collective-permute-start | bytes 786440 | tf_op jit(solution)/shard_map/ppermute | solution.py:285
  35.0 2.3 %grid_points.1 = (bf16[2,2,64,512]{3,2,1,0:T(8,128)(2,1)S(1)}, bf16[2,2,64,512]{3,2,1,0:T(8,128)(2,1)S(1)}, bf16[512,3072]{1,0:T(8,128)(2,1)S(1)}, bf16[512,512]{1,0:T(8,128)(2,1)S(1)}) custom-call(bf16[512,256]{1,0:T(8,128)(2,1)S(1)} %get-tuple-element.73.back, bf16[256,3072]{1,0:T(8,128)(2,1)S(1)} %get-tuple-element.60.weights_all.refs_2_, ...), custom_call_target="tpu_custom_call" | custom-call | flops 1600000000 | bytes 9437184 | tf_op jit(solution)/shard_map/grid_points/pallas_call | solution.py:395
  40.8 1.6 %collective-permute-start.7 = (bf16[2,2,64,512]{3,2,1,0:T(8,128)(2,1)S(1)}, bf16[2,2,64,512]{3,2,1,0:T(8,128)(2,1)S(1)}, u32[]{:S(2)}, u32[]{:S(2)}) collective-permute-start(bf16[2,2,64,512]{3,2,1,0:T(8,128)(2,1)S(1)} %add_convert_fusion.1), channel_id=1, source_target_pairs={{0,2},{1,5},{2,0},{3,7},{4,6},{5,1},{6,4},{7,3},{8,10},{9,13},{10,... | collective-permute-start | bytes 786440 | tf_op jit(solution)/shard_map/ppermute | solution.py:285
  42.3 1.2 %mesh_outputs.1 = (bf16[256,512]{1,0:T(8,128)(2,1)}, f32[256,512]{1,0:T(8,128)}) custom-call(bf16[256,512]{1,0:T(8,128)(2,1)S(1)} %get-tuple-element.90.update, bf16[512,512]{1,0:T(8,128)(2,1)S(1)} %copy-done.2, bf16[256,512]{1,0:T(8,128)(2,1)S(1)} %copy-done.4, bf16[256,512]{1,0:T(8,128)(2,1)S(1)} %copy-done.1, f32[256,512]{1,0:T(8,128)S(1)} %get-tuple-element.91.grad_mesh), custom_call_target="tpu_custom_call" | custom-call | flops 200000000 | bytes 3145728 | tf_op jit(solution)/shard_map/mesh_outputs/pallas_call | solution.py:413
  43.5 2.9 %collective-permute-done.14 = bf16[1,2,64,512]{3,2,1,0:T(8,128)(2,1)S(1)} collective-permute-done((bf16[1,2,64,512]{3,2,1,0:T(8,128)(2,1)S(1)}, bf16[1,2,64,512]{3,2,1,0:T(8,128)(2,1)S(1)}, u32[]{:S(2)}, u32[]{:S(2)}) %collective-permute-start.14) | collective-permute-done | bytes 131104 | tf_op jit(solution)/shard_map/ppermute | solution.py:285
  46.4 1.7 %collective-permute-start.15 = (bf16[1,2,64,512]{3,2,1,0:T(8,128)(2,1)S(1)}, bf16[1,2,64,512]{3,2,1,0:T(8,128)(2,1)S(1)}, u32[]{:S(2)}, u32[]{:S(2)}) collective-permute-start(bf16[1,2,64,512]{3,2,1,0:T(8,128)(2,1)S(1)} %add_convert_fusion.7), channel_id=1, source_target_pairs={{0,8},{1,9},{2,10},{3,11},{4,12},{5,13},{6,14},{7,15},{8,0},{9,1},... | collective-permute-start | bytes 393224 | tf_op jit(solution)/shard_map/ppermute | solution.py:285
  48.3 1.6 %collective-permute-start.8 = (bf16[1,2,64,512]{3,2,1,0:T(8,128)(2,1)S(1)}, bf16[1,2,64,512]{3,2,1,0:T(8,128)(2,1)S(1)}, u32[]{:S(2)}, u32[]{:S(2)}) collective-permute-start(bf16[1,2,64,512]{3,2,1,0:T(8,128)(2,1)S(1)} %slice.17), channel_id=1, source_target_pairs={{0,4},{1,3},{2,6},{3,1},{4,0},{5,7},{6,2},{7,5},{8,12},{9,11},{10,... | collective-permute-start | bytes 393224 | tf_op jit(solution)/shard_map/ppermute | solution.py:285
  49.9 4.0 %collective-permute-done.15 = bf16[1,2,64,512]{3,2,1,0:T(8,128)(2,1)S(1)} collective-permute-done((bf16[1,2,64,512]{3,2,1,0:T(8,128)(2,1)S(1)}, bf16[1,2,64,512]{3,2,1,0:T(8,128)(2,1)S(1)}, u32[]{:S(2)}, u32[]{:S(2)}) %collective-permute-start.15) | collective-permute-done | bytes 131104 | tf_op jit(solution)/shard_map/ppermute | solution.py:285
  54.6 2.5 %collective-permute-start.9 = (bf16[1,2,64,512]{3,2,1,0:T(8,128)(2,1)S(1)}, bf16[1,2,64,512]{3,2,1,0:T(8,128)(2,1)S(1)}, u32[]{:S(2)}, u32[]{:S(2)}) collective-permute-start(bf16[1,2,64,512]{3,2,1,0:T(8,128)(2,1)S(1)} %add_convert_fusion.9), channel_id=1, source_target_pairs={{0,8},{1,9},{2,10},{3,11},{4,12},{5,13},{6,14},{7,15},{8,0},{9,1},... | collective-permute-start | bytes 393224 | tf_op jit(solution)/shard_map/ppermute | solution.py:285
  57.1 6.0 %collective-permute-done.16.refs_1_ = bf16[1,2,64,512]{3,2,1,0:T(8,128)(2,1)S(1)} collective-permute-done((bf16[1,2,64,512]{3,2,1,0:T(8,128)(2,1)S(1)}, bf16[1,2,64,512]{3,2,1,0:T(8,128)(2,1)S(1)}, u32[]{:S(2)}, u32[]{:S(2)}) %collective-permute-start.16) | collective-permute-done | bytes 131104 | tf_op jit(solution)/shard_map/ppermute | solution.py:285
  64.0 5.5 %collective-permute-done.17.refs_2_ = bf16[2,2,64,512]{3,2,1,0:T(8,128)(2,1)S(1)} collective-permute-done((bf16[2,2,64,512]{3,2,1,0:T(8,128)(2,1)S(1)}, bf16[2,2,64,512]{3,2,1,0:T(8,128)(2,1)S(1)}, u32[]{:S(2)}, u32[]{:S(2)}) %collective-permute-start.17) | collective-permute-done | bytes 262176 | tf_op jit(solution)/shard_map/ppermute | solution.py:285
  71.9 1.5 %order_a.1 = (f32[512,512]{1,0:T(8,128)}, f32[512,512]{1,0:T(8,128)}) custom-call(bf16[1,2,64,512]{3,2,1,0:T(8,128)(2,1)S(1)} %add_convert_fusion.6.refs_0_, bf16[1,2,64,512]{3,2,1,0:T(8,128)(2,1)S(1)} %collective-permute-done.16.refs_1_, bf16[2,2,64,512]{3,2,1,0:T(8,128)(2,1)S(1)} %collective-permute-done.17.refs_2_, ...), custom_call_target="tpu_custom_call" | custom-call | bytes 3145728 | tf_op jit(solution)/shard_map/order_a/pallas_call | solution.py:420
  73.4 2.7 %collective-permute-done.13.refs_2_ = bf16[2,2,64,512]{3,2,1,0:T(8,128)(2,1)S(1)} collective-permute-done((bf16[2,2,64,512]{3,2,1,0:T(8,128)(2,1)S(1)}, bf16[2,2,64,512]{3,2,1,0:T(8,128)(2,1)S(1)}, u32[]{:S(2)}, u32[]{:S(2)}) %collective-permute-start.13) | collective-permute-done | bytes 262176 | tf_op jit(solution)/shard_map/ppermute | solution.py:285
  76.6 1.0 %order_b.2 = (f32[512,512]{1,0:T(8,128)}, f32[474,512]{1,0:T(8,128)}, f32[1,512]{1,0:T(1,128)S(1)}) custom-call(bf16[1,2,64,512]{3,2,1,0:T(8,128)(2,1)S(1)} %add_convert_fusion.8.refs_0_, bf16[1,2,64,512]{3,2,1,0:T(8,128)(2,1)S(1)} %collective-permute-done.11.refs_1_, bf16[2,2,64,512]{3,2,1,0:T(8,128)(2,1)S(1)} %collective-permute-done.13.refs_2_), custom_call_target="tpu_custom_call" | custom-call | bytes 2097152 | tf_op jit(solution)/shard_map/order_b/pallas_call | solution.py:431
  78.0 1.0 %order_b.3 = (f32[512,512]{1,0:T(8,128)}, f32[474,512]{1,0:T(8,128)}, f32[1,512]{1,0:T(1,128)}) custom-call(bf16[1,2,64,512]{3,2,1,0:T(8,128)(2,1)S(1)} %collective-permute-done.10.refs_0_, bf16[1,2,64,512]{3,2,1,0:T(8,128)(2,1)S(1)} %collective-permute-done.12.refs_1_, ...), custom_call_target="tpu_custom_call", output_to_operand_aliasing={{0}: (4, {}), {1}: (5, {})} | custom-call | bytes 2097152 | tf_op jit(solution)/shard_map/order_b/pallas_call | solution.py:431
  (70 shorter events, 12.3 us)
Async XLA Ops:
  2.6 17.2 %collective-permute-start.1 = (bf16[474,512]{1,0:T(8,128)(2,1)S(1)}, bf16[474,512]{1,0:T(8,128)(2,1)S(1)}, u32[]{:S(2)}, u32[]{:S(2)}) collective-permute-start(bf16[474,512]{1,0:T(8,128)(2,1)S(1)} %pack_east.1), channel_id=1, source_target_pairs={{0,4},{4,8},{8,12},{12,0},{1,5},{5,9},{9,13},{13,1},{2,6},{6,10},{... | collective-permute-start | bytes 1456136 | tf_op jit(solution)/shard_map/ppermute | solution.py:348
  6.2 23.3 %collective-permute-start = (bf16[474,512]{1,0:T(8,128)(2,1)S(1)}, bf16[474,512]{1,0:T(8,128)(2,1)S(1)}, u32[]{:S(2)}, u32[]{:S(2)}) collective-permute-start(bf16[474,512]{1,0:T(8,128)(2,1)S(1)} %pack_west.1), channel_id=1, source_target_pairs={{4,0},{8,4},{12,8},{0,12},{5,1},{9,5},{13,9},{1,13},{6,2},{10,6},{... | collective-permute-start | bytes 1456136 | tf_op jit(solution)/shard_map/ppermute | solution.py:351
  17.0 12.5 %copy-start.4 = (bf16[256,512]{1,0:T(8,128)(2,1)S(1)}, bf16[256,512]{1,0:T(8,128)(2,1)}, u32[]{:S(2)}) copy-start(bf16[256,512]{1,0:T(8,128)(2,1)} %mesh_lat.3) | copy-start | bytes 786436
  17.0 12.5 %copy-start.7 = (bf16[512,512]{1,0:T(8,128)(2,1)S(1)}, bf16[512,512]{1,0:T(8,128)(2,1)}, u32[]{:S(2)}) copy-start(bf16[512,512]{1,0:T(8,128)(2,1)} %up_w.1) | copy-start | bytes 1572868
  31.6 1.6 %collective-permute-start.2 = (bf16[2,2,64,512]{3,2,1,0:T(8,128)(2,1)S(1)}, bf16[2,2,64,512]{3,2,1,0:T(8,128)(2,1)S(1)}, u32[]{:S(2)}, u32[]{:S(2)}) collective-permute-start(bf16[2,2,64,512]{3,2,1,0:T(8,128)(2,1)S(1)} %get-tuple-element.70), channel_id=1, source_target_pairs={{0,1},{1,0},{2,3},{3,2},{4,5},{5,4},{6,7},{7,6},{8,9},{9,8},{10,11... | collective-permute-start | bytes 786440 | tf_op jit(solution)/shard_map/ppermute | solution.py:274
  33.3 5.6 %collective-permute-start.3 = (bf16[2,2,64,512]{3,2,1,0:T(8,128)(2,1)S(1)}, bf16[2,2,64,512]{3,2,1,0:T(8,128)(2,1)S(1)}, u32[]{:S(2)}, u32[]{:S(2)}) collective-permute-start(bf16[2,2,64,512]{3,2,1,0:T(8,128)(2,1)S(1)} %get-tuple-element.81), channel_id=1, source_target_pairs={{0,1},{1,0},{2,3},{3,2},{4,5},{5,4},{6,7},{7,6},{8,9},{9,8},{10,11... | collective-permute-start | bytes 786440 | tf_op jit(solution)/shard_map/ppermute | solution.py:274
  33.5 6.4 %collective-permute-start.4 = (bf16[2,2,64,512]{3,2,1,0:T(8,128)(2,1)S(1)}, bf16[2,2,64,512]{3,2,1,0:T(8,128)(2,1)S(1)}, u32[]{:S(2)}, u32[]{:S(2)}) collective-permute-start(bf16[2,2,64,512]{3,2,1,0:T(8,128)(2,1)S(1)} %add_convert_fusion.5), channel_id=1, source_target_pairs={{0,2},{1,5},{2,0},{3,7},{4,6},{5,1},{6,4},{7,3},{8,10},{9,13},{10,... | collective-permute-start | bytes 786440 | tf_op jit(solution)/shard_map/ppermute | solution.py:285
  37.3 10.9 %collective-permute-start.5 = (bf16[2,2,64,512]{3,2,1,0:T(8,128)(2,1)S(1)}, bf16[2,2,64,512]{3,2,1,0:T(8,128)(2,1)S(1)}, u32[]{:S(2)}, u32[]{:S(2)}) collective-permute-start(bf16[2,2,64,512]{3,2,1,0:T(8,128)(2,1)S(1)} %get-tuple-element.86), channel_id=1, source_target_pairs={{0,1},{1,0},{2,3},{3,2},{4,5},{5,4},{6,7},{7,6},{8,9},{9,8},{10,11... | collective-permute-start | bytes 786440 | tf_op jit(solution)/shard_map/ppermute | solution.py:274
  37.4 3.3 %collective-permute-start.6 = (bf16[2,2,64,512]{3,2,1,0:T(8,128)(2,1)S(1)}, bf16[2,2,64,512]{3,2,1,0:T(8,128)(2,1)S(1)}, u32[]{:S(2)}, u32[]{:S(2)}) collective-permute-start(bf16[2,2,64,512]{3,2,1,0:T(8,128)(2,1)S(1)} %get-tuple-element.88), channel_id=1, source_target_pairs={{0,1},{1,0},{2,3},{3,2},{4,5},{5,4},{6,7},{7,6},{8,9},{9,8},{10,11... | collective-permute-start | bytes 786440 | tf_op jit(solution)/shard_map/ppermute | solution.py:274
  40.0 6.4 %collective-permute-start.14 = (bf16[1,2,64,512]{3,2,1,0:T(8,128)(2,1)S(1)}, bf16[1,2,64,512]{3,2,1,0:T(8,128)(2,1)S(1)}, u32[]{:S(2)}, u32[]{:S(2)}) collective-permute-start(bf16[1,2,64,512]{3,2,1,0:T(8,128)(2,1)S(1)} %slice.19), channel_id=1, source_target_pairs={{0,4},{1,3},{2,6},{3,1},{4,0},{5,7},{6,2},{7,5},{8,12},{9,11},{10,... | collective-permute-start | bytes 393224 | tf_op jit(solution)/shard_map/ppermute | solution.py:285
  40.8 7.4 %collective-permute-start.7 = (bf16[2,2,64,512]{3,2,1,0:T(8,128)(2,1)S(1)}, bf16[2,2,64,512]{3,2,1,0:T(8,128)(2,1)S(1)}, u32[]{:S(2)}, u32[]{:S(2)}) collective-permute-start(bf16[2,2,64,512]{3,2,1,0:T(8,128)(2,1)S(1)} %add_convert_fusion.1), channel_id=1, source_target_pairs={{0,2},{1,5},{2,0},{3,7},{4,6},{5,1},{6,4},{7,3},{8,10},{9,13},{10,... | collective-permute-start | bytes 786440 | tf_op jit(solution)/shard_map/ppermute | solution.py:285
  46.4 7.4 %collective-permute-start.15 = (bf16[1,2,64,512]{3,2,1,0:T(8,128)(2,1)S(1)}, bf16[1,2,64,512]{3,2,1,0:T(8,128)(2,1)S(1)}, u32[]{:S(2)}, u32[]{:S(2)}) collective-permute-start(bf16[1,2,64,512]{3,2,1,0:T(8,128)(2,1)S(1)} %add_convert_fusion.7), channel_id=1, source_target_pairs={{0,8},{1,9},{2,10},{3,11},{4,12},{5,13},{6,14},{7,15},{8,0},{9,1},... | collective-permute-start | bytes 393224 | tf_op jit(solution)/shard_map/ppermute | solution.py:285
  48.3 6.3 %collective-permute-start.8 = (bf16[1,2,64,512]{3,2,1,0:T(8,128)(2,1)S(1)}, bf16[1,2,64,512]{3,2,1,0:T(8,128)(2,1)S(1)}, u32[]{:S(2)}, u32[]{:S(2)}) collective-permute-start(bf16[1,2,64,512]{3,2,1,0:T(8,128)(2,1)S(1)} %slice.17), channel_id=1, source_target_pairs={{0,4},{1,3},{2,6},{3,1},{4,0},{5,7},{6,2},{7,5},{8,12},{9,11},{10,... | collective-permute-start | bytes 393224 | tf_op jit(solution)/shard_map/ppermute | solution.py:285
  53.9 9.2 %collective-permute-start.16 = (bf16[1,2,64,512]{3,2,1,0:T(8,128)(2,1)S(1)}, bf16[1,2,64,512]{3,2,1,0:T(8,128)(2,1)S(1)}, u32[]{:S(2)}, u32[]{:S(2)}) collective-permute-start(bf16[1,2,64,512]{3,2,1,0:T(8,128)(2,1)S(1)} %add_convert_fusion.6.refs_0_), channel_id=1, source_target_pairs={{0,4},{1,3},{2,6},{3,1},{4,0},{5,7},{6,2},{7,5},{8,12},{9,11},{10,... | collective-permute-start | bytes 393224 | tf_op jit(solution)/shard_map/ppermute | solution.py:285
  54.6 9.1 %collective-permute-start.9 = (bf16[1,2,64,512]{3,2,1,0:T(8,128)(2,1)S(1)}, bf16[1,2,64,512]{3,2,1,0:T(8,128)(2,1)S(1)}, u32[]{:S(2)}, u32[]{:S(2)}) collective-permute-start(bf16[1,2,64,512]{3,2,1,0:T(8,128)(2,1)S(1)} %add_convert_fusion.9), channel_id=1, source_target_pairs={{0,8},{1,9},{2,10},{3,11},{4,12},{5,13},{6,14},{7,15},{8,0},{9,1},... | collective-permute-start | bytes 393224 | tf_op jit(solution)/shard_map/ppermute | solution.py:285
  63.1 6.4 %collective-permute-start.17 = (bf16[2,2,64,512]{3,2,1,0:T(8,128)(2,1)S(1)}, bf16[2,2,64,512]{3,2,1,0:T(8,128)(2,1)S(1)}, u32[]{:S(2)}, u32[]{:S(2)}) collective-permute-start(bf16[2,2,64,512]{3,2,1,0:T(8,128)(2,1)S(1)} %pad_maximum_fusion.1), channel_id=1, source_target_pairs={{0,2},{1,5},{2,0},{3,7},{4,6},{5,1},{6,4},{7,3},{8,10},{9,13},{10,... | collective-permute-start | bytes 786440 | tf_op jit(solution)/shard_map/ppermute | solution.py:285
  63.7 5.9 %collective-permute-start.11 = (bf16[1,2,64,512]{3,2,1,0:T(8,128)(2,1)S(1)}, bf16[1,2,64,512]{3,2,1,0:T(8,128)(2,1)S(1)}, u32[]{:S(2)}, u32[]{:S(2)}) collective-permute-start(bf16[1,2,64,512]{3,2,1,0:T(8,128)(2,1)S(1)} %add_convert_fusion.8.refs_0_), channel_id=1, source_target_pairs={{0,4},{1,3},{2,6},{3,1},{4,0},{5,7},{6,2},{7,5},{8,12},{9,11},{10,... | collective-permute-start | bytes 393224 | tf_op jit(solution)/shard_map/ppermute | solution.py:285
  69.6 2.4 %collective-permute-start.20 = (bf16[2,2,64,512]{3,2,1,0:T(8,128)(2,1)S(1)}, bf16[2,2,64,512]{3,2,1,0:T(8,128)(2,1)S(1)}, u32[]{:S(2)}, u32[]{:S(2)}) collective-permute-start(bf16[2,2,64,512]{3,2,1,0:T(8,128)(2,1)S(1)} %collective-permute-done.17.refs_2_), channel_id=1, source_target_pairs={{0,1},{1,0},{2,3},{3,2},{4,5},{5,4},{6,7},{7,6},{8,9},{9,8},{10,11... | collective-permute-start | bytes 786440 | tf_op jit(solution)/shard_map/ppermute | solution.py:274
  69.6 6.4 %collective-permute-start.13 = (bf16[2,2,64,512]{3,2,1,0:T(8,128)(2,1)S(1)}, bf16[2,2,64,512]{3,2,1,0:T(8,128)(2,1)S(1)}, u32[]{:S(2)}, u32[]{:S(2)}) collective-permute-start(bf16[2,2,64,512]{3,2,1,0:T(8,128)(2,1)S(1)} %pad_maximum_fusion), channel_id=1, source_target_pairs={{0,2},{1,5},{2,0},{3,7},{4,6},{5,1},{6,4},{7,3},{8,10},{9,13},{10,... | collective-permute-start | bytes 786440 | tf_op jit(solution)/shard_map/ppermute | solution.py:285
  70.4 1.3 %collective-permute-start.18 = (bf16[1,2,64,512]{3,2,1,0:T(8,128)(2,1)S(1)}, bf16[1,2,64,512]{3,2,1,0:T(8,128)(2,1)S(1)}, u32[]{:S(2)}, u32[]{:S(2)}) collective-permute-start(bf16[1,2,64,512]{3,2,1,0:T(8,128)(2,1)S(1)} %add_convert_fusion.6.refs_0_), channel_id=1, source_target_pairs={{0,1},{1,0},{2,3},{3,2},{4,5},{5,4},{6,7},{7,6},{8,9},{9,8},{10,11... | collective-permute-start | bytes 393224 | tf_op jit(solution)/shard_map/ppermute | solution.py:274
  70.4 1.5 %collective-permute-start.19 = (bf16[1,2,64,512]{3,2,1,0:T(8,128)(2,1)S(1)}, bf16[1,2,64,512]{3,2,1,0:T(8,128)(2,1)S(1)}, u32[]{:S(2)}, u32[]{:S(2)}) collective-permute-start(bf16[1,2,64,512]{3,2,1,0:T(8,128)(2,1)S(1)} %collective-permute-done.16.refs_1_), channel_id=1, source_target_pairs={{0,1},{1,0},{2,3},{3,2},{4,5},{5,4},{6,7},{7,6},{8,9},{9,8},{10,11... | collective-permute-start | bytes 393224 | tf_op jit(solution)/shard_map/ppermute | solution.py:274
  76.1 1.9 %collective-permute-start.21 = (bf16[2,2,64,512]{3,2,1,0:T(8,128)(2,1)S(1)}, bf16[2,2,64,512]{3,2,1,0:T(8,128)(2,1)S(1)}, u32[]{:S(2)}, u32[]{:S(2)}) collective-permute-start(bf16[2,2,64,512]{3,2,1,0:T(8,128)(2,1)S(1)} %collective-permute-done.13.refs_2_), channel_id=1, source_target_pairs={{0,1},{1,0},{2,3},{3,2},{4,5},{5,4},{6,7},{7,6},{8,9},{9,8},{10,11... | collective-permute-start | bytes 786440 | tf_op jit(solution)/shard_map/ppermute | solution.py:274
  76.1 1.7 %collective-permute-start.10 = (bf16[1,2,64,512]{3,2,1,0:T(8,128)(2,1)S(1)}, bf16[1,2,64,512]{3,2,1,0:T(8,128)(2,1)S(1)}, u32[]{:S(2)}, u32[]{:S(2)}) collective-permute-start(bf16[1,2,64,512]{3,2,1,0:T(8,128)(2,1)S(1)} %add_convert_fusion.8.refs_0_), channel_id=1, source_target_pairs={{0,1},{1,0},{2,3},{3,2},{4,5},{5,4},{6,7},{7,6},{8,9},{9,8},{10,11... | collective-permute-start | bytes 393224 | tf_op jit(solution)/shard_map/ppermute | solution.py:274
  76.6 1.4 %collective-permute-start.12 = (bf16[1,2,64,512]{3,2,1,0:T(8,128)(2,1)S(1)}, bf16[1,2,64,512]{3,2,1,0:T(8,128)(2,1)S(1)}, u32[]{:S(2)}, u32[]{:S(2)}) collective-permute-start(bf16[1,2,64,512]{3,2,1,0:T(8,128)(2,1)S(1)} %collective-permute-done.11.refs_1_), channel_id=1, source_target_pairs={{0,1},{1,0},{2,3},{3,2},{4,5},{5,4},{6,7},{7,6},{8,9},{9,8},{10,11... | collective-permute-start | bytes 393224 | tf_op jit(solution)/shard_map/ppermute | solution.py:274
  (9 other events, 74.2 us)

commit v15 on v14

--- a/solution.py
+++ b/solution.py
@@ -416,10 +416,13 @@
     summed_a = all_summed(kept_a)
     kept_b, mesh_new, mesh_grad = lax.optimization_barrier((halved(high_b, low_b), mesh_new, mesh_grad))
     summed_b = all_summed(kept_b)
+    chunks_a, early_b = lax.optimization_barrier(
+        (from_both_cores(summed_a), tuple(core_swapped(chunk) for chunk in summed_b[:2]))
+    )
     square = shape((latent, latent), F32)
     grad_message, grad_up = call(
         order_mesh_kernel, "order_a", [VMEM] * 6, [square, square], 0, 3 * MIB, 16
-    )(*from_both_cores(summed_a))
+    )(*chunks_a)
     last, grad_message, grad_up = lax.optimization_barrier((summed_b[2], grad_message, grad_up))
     summed_b = (*summed_b[:2], last)
     rows_half = latent // 2
@@ -440,7 +443,7 @@
             cost_estimate=pl.CostEstimate(flops=0, bytes_accessed=2 * MIB, transcendentals=0),
         )(*chunks, *more)
 
-    from_other = [core_swapped(chunk) for chunk in summed_b]
+    from_other = (*early_b, core_swapped(last))
     held = order_b(0, summed_b, (), [], {})
     grad_out, grad_embed, grad_gain = order_b(
         1, from_other, (held[2], held[0], held[1]), [VMEM] + [pl.BlockSpec(memory_space=pl.ANY)] * 2, {4: 0, 5: 1}

time: 79.1 us -> 78.8 us (level)
  transfers between devices with their start and end apart: 22 -> 22, of which waited for: 14 -> 14; matrix products, arithmetic and copies ran while one was open for 1% -> 1% of each run, Pallas kernels for 21% -> 22%
where the time goes in v15:
time: 78.8 us; the launch traced here: 78.6 us
  waiting for transfers between devices  36.2 us (46%)
  Pallas kernels  20.9 us (27%)
  starting transfers between devices  17.9 us (23%)
  between operations  1.62 us (2%)
  local copies, waits for them, and re-layouts  1.49 us (2%)
    ppermute x10, waiting for transfers between devices, swapped(): return lax.ppermute(value, ('lon', 'lat'), pairs)  22.2 us
    ppermute x10, starting transfers between devices, swapped(): return lax.ppermute(value, ('lon', 'lat'), pairs)  11.3 us
    ppermute x1, waiting for transfers between devices, on_device(): lax.ppermute(to_west, 'lon', [((i + 1) % count, i) for i in range(count)])  8.72 us
    pallas_call x1, Pallas kernels, on_device(): call(own_kernel, 'own_points', [VMEM] * 3, [shape((nodes, latent), F32),...  3.57 us
    pallas_call x1, Pallas kernels, on_device(): call(lambda *refs: weights_kernel(rows, cols // block, *refs), 'slot_weig...  3.42 us
    ppermute x1, starting transfers between devices, on_device(): lax.ppermute(to_east, 'lon', [(i, (i + 1) % count) for i in range(count)])  3.08 us
    ppermute x10, waiting for transfers between devices, core_swapped(): lax.ppermute(value, 'lat', [(i, i ^ 1) for i in range(lax.axis_size('lat'...  2.86 us
    ppermute x1, waiting for transfers between devices, on_device(): lax.ppermute(to_east, 'lon', [(i, (i + 1) % count) for i in range(count)])  2.45 us
  transfers between devices with their start and end apart: 22, of which 14 were waited for; matrix products, arithmetic and copies ran while one was open for 1% of the time, Pallas kernels for 22%

profile of v15, /device:TPU:0, one launch (start us, length us, event | category | flops | bytes accessed | tf_op | source)
XLA Modules:
  0.0 78.6 jit_solution(11346511123466907901)
XLA Ops:
  0.6 1.4 %slice.20.refs_0_ = bf16[474,8,128]{2,1,0:T(8,128)(2,1)S(1)} slice(bf16[474,8,256]{2,1,0:T(8,128)(2,1)} %bitcast.3), slice={[0:474], [0:8], [128:256]} | slice | bytes 1941504 | tf_op jit(solution)/shard_map/slice | solution.py:346
  2.6 3.1 %collective-permute-start.1 = (bf16[474,512]{1,0:T(8,128)(2,1)S(1)}, bf16[474,512]{1,0:T(8,128)(2,1)S(1)}, u32[]{:S(2)}, u32[]{:S(2)}) collective-permute-start(bf16[474,512]{1,0:T(8,128)(2,1)S(1)} %pack_east.1), channel_id=1, source_target_pairs={{0,4},{4,8},{8,12},{12,0},{1,5},{5,9},{9,13},{13,1},{2,6},{6,10},{... | collective-permute-start | bytes 1456136 | tf_op jit(solution)/shard_map/ppermute | solution.py:348
  6.2 2.1 %collective-permute-start = (bf16[474,512]{1,0:T(8,128)(2,1)S(1)}, bf16[474,512]{1,0:T(8,128)(2,1)S(1)}, u32[]{:S(2)}, u32[]{:S(2)}) collective-permute-start(bf16[474,512]{1,0:T(8,128)(2,1)S(1)} %pack_west.1), channel_id=1, source_target_pairs={{4,0},{8,4},{12,8},{0,12},{5,1},{9,5},{13,9},{1,13},{6,2},{10,6},{... | collective-permute-start | bytes 1456136 | tf_op jit(solution)/shard_map/ppermute | solution.py:351
  9.0 3.4 %slot_weights.1 = (bf16[256,3072]{1,0:T(8,128)(2,1)S(1)}, f32[256,512]{1,0:T(8,128)S(1)}) custom-call(s32[32]{0:T(128)S(1)} %copy-done.5, s32[32]{0:T(128)S(1)} %copy-done.6, s32[1]{0:T(128)S(6)} %copy.23.refs_2_, bf16[32,128,128]{2,1,0:T(8,128)(2,1)S(1)} %copy-done.3, bf16[256,512]{1,0:T(8,128)(2,1)S(1)} %copy-done.1, bf16[512,512]{1,0:T(8,128)(2,1)S(1)} %copy-done.2), custom_call_target="tpu_custom_call" | custom-call | flops 200000000 | bytes 4194304 | tf_op jit(solution)/shard_map/slot_weights/pallas_call | solution.py:353
  12.5 1.3 %own_rows.1 = (bf16[474,2048]{1,0:T(8,128)(2,1)S(1)}, bf16[512,474]{1,0:T(8,128)(2,1)S(1)}) custom-call(bf16[474,8,256]{2,1,0:T(8,128)(2,1)S(1)} %bitcast.5, bf16[474,512]{1,0:T(8,128)(2,1)S(1)} %copy-done.9), custom_call_target="tpu_custom_call" | custom-call | flops 1000000000 | bytes 5242880 | tf_op jit(solution)/shard_map/own_rows/pallas_call | solution.py:358
  13.8 3.6 %own_points.1 = (f32[256,512]{1,0:T(8,128)S(1)}, bf16[512,2048]{1,0:T(8,128)(2,1)S(1)}) custom-call(bf16[474,2048]{1,0:T(8,128)(2,1)S(1)} %get-tuple-element.69.x_t.x_own, bf16[512,474]{1,0:T(8,128)(2,1)S(1)} %get-tuple-element.67.embed_t.refs_1_, bf16[256,3072]{1,0:T(8,128)(2,1)S(1)} %get-tuple-element.68.weights_all.refs_2_), custom_call_target="tpu_custom_call" | custom-call | flops 2000000000 | bytes 7340032 | tf_op jit(solution)/shard_map/own_points/pallas_call | solution.py:362
  17.4 2.5 %collective-permute-done.1.refs_0_.x_west = bf16[474,512]{1,0:T(8,128)(2,1)S(1)} collective-permute-done((bf16[474,512]{1,0:T(8,128)(2,1)S(1)}, bf16[474,512]{1,0:T(8,128)(2,1)S(1)}, u32[]{:S(2)}, u32[]{:S(2)}) %collective-permute-start.1) | collective-permute-done | bytes 485408 | tf_op jit(solution)/shard_map/ppermute | solution.py:348
  20.8 8.7 %collective-permute-done.x.x_east = bf16[474,512]{1,0:T(8,128)(2,1)S(1)} collective-permute-done((bf16[474,512]{1,0:T(8,128)(2,1)S(1)}, bf16[474,512]{1,0:T(8,128)(2,1)S(1)}, u32[]{:S(2)}, u32[]{:S(2)}) %collective-permute-start) | collective-permute-done | bytes 485408 | tf_op jit(solution)/shard_map/ppermute | solution.py:351
  29.5 2.1 %mesh_nodes.1 = (bf16[2,2,64,512]{3,2,1,0:T(8,128)(2,1)S(1)}, bf16[2,2,64,512]{3,2,1,0:T(8,128)(2,1)S(1)}, f32[256,512]{1,0:T(8,128)S(1)}, f32[1,512]{1,0:T(1,12...) custom-call(bf16[474,512]{1,0:T(8,128)(2,1)S(1)} %collective-permute, ...), custom_call_target="tpu_custom_call" | custom-call | flops 2000000000 | bytes 8388608 | tf_op jit(solution)/shard_map/mesh_nodes/pallas_call | solution.py:377
  33.5 1.5 %collective-permute-start.4 = (bf16[2,2,64,512]{3,2,1,0:T(8,128)(2,1)S(1)}, bf16[2,2,64,512]{3,2,1,0:T(8,128)(2,1)S(1)}, u32[]{:S(2)}, u32[]{:S(2)}) collective-permute-start(bf16[2,2,64,512]{3,2,1,0:T(8,128)(2,1)S(1)} %add_convert_fusion.5), channel_id=1, source_target_pairs={{0,2},{1,5},{2,0},{3,7},{4,6},{5,1},{6,4},{7,3},{8,10},{9,13},{10,... | collective-permute-start | bytes 786440 | tf_op jit(solution)/shard_map/ppermute | solution.py:285
  35.0 2.3 %grid_points.1 = (bf16[2,2,64,512]{3,2,1,0:T(8,128)(2,1)S(1)}, bf16[2,2,64,512]{3,2,1,0:T(8,128)(2,1)S(1)}, bf16[512,3072]{1,0:T(8,128)(2,1)S(1)}, bf16[512,512]{1,0:T(8,128)(2,1)S(1)}) custom-call(bf16[512,256]{1,0:T(8,128)(2,1)S(1)} %get-tuple-element.81.back, bf16[256,3072]{1,0:T(8,128)(2,1)S(1)} %get-tuple-element.68.weights_all.refs_2_, ...), custom_call_target="tpu_custom_call" | custom-call | flops 1600000000 | bytes 9437184 | tf_op jit(solution)/shard_map/grid_points/pallas_call | solution.py:395
  40.8 1.6 %collective-permute-start.7 = (bf16[2,2,64,512]{3,2,1,0:T(8,128)(2,1)S(1)}, bf16[2,2,64,512]{3,2,1,0:T(8,128)(2,1)S(1)}, u32[]{:S(2)}, u32[]{:S(2)}) collective-permute-start(bf16[2,2,64,512]{3,2,1,0:T(8,128)(2,1)S(1)} %add_convert_fusion.1), channel_id=1, source_target_pairs={{0,2},{1,5},{2,0},{3,7},{4,6},{5,1},{6,4},{7,3},{8,10},{9,13},{10,... | collective-permute-start | bytes 786440 | tf_op jit(solution)/shard_map/ppermute | solution.py:285
  42.3 1.2 %mesh_outputs.1 = (bf16[256,512]{1,0:T(8,128)(2,1)}, f32[256,512]{1,0:T(8,128)}) custom-call(bf16[256,512]{1,0:T(8,128)(2,1)S(1)} %get-tuple-element.98.update, bf16[512,512]{1,0:T(8,128)(2,1)S(1)} %copy-done.2, bf16[256,512]{1,0:T(8,128)(2,1)S(1)} %copy-done.4, bf16[256,512]{1,0:T(8,128)(2,1)S(1)} %copy-done.1, f32[256,512]{1,0:T(8,128)S(1)} %get-tuple-element.99.grad_mesh), custom_call_target="tpu_custom_call" | custom-call | flops 200000000 | bytes 3145728 | tf_op jit(solution)/shard_map/mesh_outputs/pallas_call | solution.py:413
  43.5 2.9 %collective-permute-done.8 = bf16[1,2,64,512]{3,2,1,0:T(8,128)(2,1)S(1)} collective-permute-done((bf16[1,2,64,512]{3,2,1,0:T(8,128)(2,1)S(1)}, bf16[1,2,64,512]{3,2,1,0:T(8,128)(2,1)S(1)}, u32[]{:S(2)}, u32[]{:S(2)}) %collective-permute-start.8) | collective-permute-done | bytes 131104 | tf_op jit(solution)/shard_map/ppermute | solution.py:285
  46.4 1.7 %collective-permute-start.9 = (bf16[1,2,64,512]{3,2,1,0:T(8,128)(2,1)S(1)}, bf16[1,2,64,512]{3,2,1,0:T(8,128)(2,1)S(1)}, u32[]{:S(2)}, u32[]{:S(2)}) collective-permute-start(bf16[1,2,64,512]{3,2,1,0:T(8,128)(2,1)S(1)} %add_convert_fusion.9), channel_id=1, source_target_pairs={{0,8},{1,9},{2,10},{3,11},{4,12},{5,13},{6,14},{7,15},{8,0},{9,1},... | collective-permute-start | bytes 393224 | tf_op jit(solution)/shard_map/ppermute | solution.py:285
  48.3 1.6 %collective-permute-start.15 = (bf16[1,2,64,512]{3,2,1,0:T(8,128)(2,1)S(1)}, bf16[1,2,64,512]{3,2,1,0:T(8,128)(2,1)S(1)}, u32[]{:S(2)}, u32[]{:S(2)}) collective-permute-start(bf16[1,2,64,512]{3,2,1,0:T(8,128)(2,1)S(1)} %slice.19), channel_id=1, source_target_pairs={{0,4},{1,3},{2,6},{3,1},{4,0},{5,7},{6,2},{7,5},{8,12},{9,11},{10,... | collective-permute-start | bytes 393224 | tf_op jit(solution)/shard_map/ppermute | solution.py:285
  49.9 4.0 %collective-permute-done.9 = bf16[1,2,64,512]{3,2,1,0:T(8,128)(2,1)S(1)} collective-permute-done((bf16[1,2,64,512]{3,2,1,0:T(8,128)(2,1)S(1)}, bf16[1,2,64,512]{3,2,1,0:T(8,128)(2,1)S(1)}, u32[]{:S(2)}, u32[]{:S(2)}) %collective-permute-start.9) | collective-permute-done | bytes 131104 | tf_op jit(solution)/shard_map/ppermute | solution.py:285
  54.6 2.5 %collective-permute-start.16 = (bf16[1,2,64,512]{3,2,1,0:T(8,128)(2,1)S(1)}, bf16[1,2,64,512]{3,2,1,0:T(8,128)(2,1)S(1)}, u32[]{:S(2)}, u32[]{:S(2)}) collective-permute-start(bf16[1,2,64,512]{3,2,1,0:T(8,128)(2,1)S(1)} %add_convert_fusion.7), channel_id=1, source_target_pairs={{0,8},{1,9},{2,10},{3,11},{4,12},{5,13},{6,14},{7,15},{8,0},{9,1},... | collective-permute-start | bytes 393224 | tf_op jit(solution)/shard_map/ppermute | solution.py:285
  57.1 6.0 %collective-permute-done.10.refs_1_ = bf16[1,2,64,512]{3,2,1,0:T(8,128)(2,1)S(1)} collective-permute-done((bf16[1,2,64,512]{3,2,1,0:T(8,128)(2,1)S(1)}, bf16[1,2,64,512]{3,2,1,0:T(8,128)(2,1)S(1)}, u32[]{:S(2)}, u32[]{:S(2)}) %collective-permute-start.10) | collective-permute-done | bytes 131104 | tf_op jit(solution)/shard_map/ppermute | solution.py:285
  64.0 5.5 %collective-permute-done.11.refs_2_ = bf16[2,2,64,512]{3,2,1,0:T(8,128)(2,1)S(1)} collective-permute-done((bf16[2,2,64,512]{3,2,1,0:T(8,128)(2,1)S(1)}, bf16[2,2,64,512]{3,2,1,0:T(8,128)(2,1)S(1)}, u32[]{:S(2)}, u32[]{:S(2)}) %collective-permute-start.11) | collective-permute-done | bytes 262176 | tf_op jit(solution)/shard_map/ppermute | solution.py:285
  72.3 1.5 %order_a.1 = (f32[512,512]{1,0:T(8,128)}, f32[512,512]{1,0:T(8,128)}) custom-call(bf16[1,2,64,512]{3,2,1,0:T(8,128)(2,1)S(1)} %add_convert_fusion.8.refs_0_, bf16[1,2,64,512]{3,2,1,0:T(8,128)(2,1)S(1)} %collective-permute-done.10.refs_1_, bf16[2,2,64,512]{3,2,1,0:T(8,128)(2,1)S(1)} %collective-permute-done.11.refs_2_, ...), custom_call_target="tpu_custom_call" | custom-call | bytes 3145728 | tf_op jit(solution)/shard_map/order_a/pallas_call | solution.py:423
  73.7 2.3 %collective-permute-done.20.refs_2_ = bf16[2,2,64,512]{3,2,1,0:T(8,128)(2,1)S(1)} collective-permute-done((bf16[2,2,64,512]{3,2,1,0:T(8,128)(2,1)S(1)}, bf16[2,2,64,512]{3,2,1,0:T(8,128)(2,1)S(1)}, u32[]{:S(2)}, u32[]{:S(2)}) %collective-permute-start.20) | collective-permute-done | bytes 262176 | tf_op jit(solution)/shard_map/ppermute | solution.py:285
  76.1 1.0 %order_b.2 = (f32[512,512]{1,0:T(8,128)}, f32[474,512]{1,0:T(8,128)}, f32[1,512]{1,0:T(1,128)S(1)}) custom-call(bf16[1,2,64,512]{3,2,1,0:T(8,128)(2,1)S(1)} %add_convert_fusion.6.refs_0_, bf16[1,2,64,512]{3,2,1,0:T(8,128)(2,1)S(1)} %collective-permute-done.18.refs_1_, bf16[2,2,64,512]{3,2,1,0:T(8,128)(2,1)S(1)} %collective-permute-done.20.refs_2_), custom_call_target="tpu_custom_call" | custom-call | bytes 2097152 | tf_op jit(solution)/shard_map/order_b/pallas_call | solution.py:434
  77.6 1.0 %order_b.3 = (f32[512,512]{1,0:T(8,128)}, f32[474,512]{1,0:T(8,128)}, f32[1,512]{1,0:T(1,128)}) custom-call(bf16[1,2,64,512]{3,2,1,0:T(8,128)(2,1)S(1)} %collective-permute-done.17.refs_0_, bf16[1,2,64,512]{3,2,1,0:T(8,128)(2,1)S(1)} %collective-permute-done.19.refs_1_, ...), custom_call_target="tpu_custom_call", output_to_operand_aliasing={{0}: (4, {}), {1}: (5, {})} | custom-call | bytes 2097152 | tf_op jit(solution)/shard_map/order_b/pallas_call | solution.py:434
  (70 shorter events, 12.2 us)
Async XLA Ops:
  2.6 17.2 %collective-permute-start.1 = (bf16[474,512]{1,0:T(8,128)(2,1)S(1)}, bf16[474,512]{1,0:T(8,128)(2,1)S(1)}, u32[]{:S(2)}, u32[]{:S(2)}) collective-permute-start(bf16[474,512]{1,0:T(8,128)(2,1)S(1)} %pack_east.1), channel_id=1, source_target_pairs={{0,4},{4,8},{8,12},{12,0},{1,5},{5,9},{9,13},{13,1},{2,6},{6,10},{... | collective-permute-start | bytes 1456136 | tf_op jit(solution)/shard_map/ppermute | solution.py:348
  6.2 23.3 %collective-permute-start = (bf16[474,512]{1,0:T(8,128)(2,1)S(1)}, bf16[474,512]{1,0:T(8,128)(2,1)S(1)}, u32[]{:S(2)}, u32[]{:S(2)}) collective-permute-start(bf16[474,512]{1,0:T(8,128)(2,1)S(1)} %pack_west.1), channel_id=1, source_target_pairs={{4,0},{8,4},{12,8},{0,12},{5,1},{9,5},{13,9},{1,13},{6,2},{10,6},{... | collective-permute-start | bytes 1456136 | tf_op jit(solution)/shard_map/ppermute | solution.py:351
  17.4 12.1 %copy-start.4 = (bf16[256,512]{1,0:T(8,128)(2,1)S(1)}, bf16[256,512]{1,0:T(8,128)(2,1)}, u32[]{:S(2)}) copy-start(bf16[256,512]{1,0:T(8,128)(2,1)} %mesh_lat.3) | copy-start | bytes 786436
  17.4 12.1 %copy-start.7 = (bf16[512,512]{1,0:T(8,128)(2,1)S(1)}, bf16[512,512]{1,0:T(8,128)(2,1)}, u32[]{:S(2)}) copy-start(bf16[512,512]{1,0:T(8,128)(2,1)} %up_w.1) | copy-start | bytes 1572868
  31.6 1.6 %collective-permute-start.2 = (bf16[2,2,64,512]{3,2,1,0:T(8,128)(2,1)S(1)}, bf16[2,2,64,512]{3,2,1,0:T(8,128)(2,1)S(1)}, u32[]{:S(2)}, u32[]{:S(2)}) collective-permute-start(bf16[2,2,64,512]{3,2,1,0:T(8,128)(2,1)S(1)} %get-tuple-element.78), channel_id=1, source_target_pairs={{0,1},{1,0},{2,3},{3,2},{4,5},{5,4},{6,7},{7,6},{8,9},{9,8},{10,11... | collective-permute-start | bytes 786440 | tf_op jit(solution)/shard_map/ppermute | solution.py:274
  33.3 5.6 %collective-permute-start.3 = (bf16[2,2,64,512]{3,2,1,0:T(8,128)(2,1)S(1)}, bf16[2,2,64,512]{3,2,1,0:T(8,128)(2,1)S(1)}, u32[]{:S(2)}, u32[]{:S(2)}) collective-permute-start(bf16[2,2,64,512]{3,2,1,0:T(8,128)(2,1)S(1)} %get-tuple-element.89), channel_id=1, source_target_pairs={{0,1},{1,0},{2,3},{3,2},{4,5},{5,4},{6,7},{7,6},{8,9},{9,8},{10,11... | collective-permute-start | bytes 786440 | tf_op jit(solution)/shard_map/ppermute | solution.py:274
  33.5 6.4 %collective-permute-start.4 = (bf16[2,2,64,512]{3,2,1,0:T(8,128)(2,1)S(1)}, bf16[2,2,64,512]{3,2,1,0:T(8,128)(2,1)S(1)}, u32[]{:S(2)}, u32[]{:S(2)}) collective-permute-start(bf16[2,2,64,512]{3,2,1,0:T(8,128)(2,1)S(1)} %add_convert_fusion.5), channel_id=1, source_target_pairs={{0,2},{1,5},{2,0},{3,7},{4,6},{5,1},{6,4},{7,3},{8,10},{9,13},{10,... | collective-permute-start | bytes 786440 | tf_op jit(solution)/shard_map/ppermute | solution.py:285
  37.3 10.9 %collective-permute-start.5 = (bf16[2,2,64,512]{3,2,1,0:T(8,128)(2,1)S(1)}, bf16[2,2,64,512]{3,2,1,0:T(8,128)(2,1)S(1)}, u32[]{:S(2)}, u32[]{:S(2)}) collective-permute-start(bf16[2,2,64,512]{3,2,1,0:T(8,128)(2,1)S(1)} %get-tuple-element.94), channel_id=1, source_target_pairs={{0,1},{1,0},{2,3},{3,2},{4,5},{5,4},{6,7},{7,6},{8,9},{9,8},{10,11... | collective-permute-start | bytes 786440 | tf_op jit(solution)/shard_map/ppermute | solution.py:274
  37.4 3.3 %collective-permute-start.6 = (bf16[2,2,64,512]{3,2,1,0:T(8,128)(2,1)S(1)}, bf16[2,2,64,512]{3,2,1,0:T(8,128)(2,1)S(1)}, u32[]{:S(2)}, u32[]{:S(2)}) collective-permute-start(bf16[2,2,64,512]{3,2,1,0:T(8,128)(2,1)S(1)} %get-tuple-element.96), channel_id=1, source_target_pairs={{0,1},{1,0},{2,3},{3,2},{4,5},{5,4},{6,7},{7,6},{8,9},{9,8},{10,11... | collective-permute-start | bytes 786440 | tf_op jit(solution)/shard_map/ppermute | solution.py:274
  40.0 6.4 %collective-permute-start.8 = (bf16[1,2,64,512]{3,2,1,0:T(8,128)(2,1)S(1)}, bf16[1,2,64,512]{3,2,1,0:T(8,128)(2,1)S(1)}, u32[]{:S(2)}, u32[]{:S(2)}) collective-permute-start(bf16[1,2,64,512]{3,2,1,0:T(8,128)(2,1)S(1)} %slice.17), channel_id=1, source_target_pairs={{0,4},{1,3},{2,6},{3,1},{4,0},{5,7},{6,2},{7,5},{8,12},{9,11},{10,... | collective-permute-start | bytes 393224 | tf_op jit(solution)/shard_map/ppermute | solution.py:285
  40.8 7.4 %collective-permute-start.7 = (bf16[2,2,64,512]{3,2,1,0:T(8,128)(2,1)S(1)}, bf16[2,2,64,512]{3,2,1,0:T(8,128)(2,1)S(1)}, u32[]{:S(2)}, u32[]{:S(2)}) collective-permute-start(bf16[2,2,64,512]{3,2,1,0:T(8,128)(2,1)S(1)} %add_convert_fusion.1), channel_id=1, source_target_pairs={{0,2},{1,5},{2,0},{3,7},{4,6},{5,1},{6,4},{7,3},{8,10},{9,13},{10,... | collective-permute-start | bytes 786440 | tf_op jit(solution)/shard_map/ppermute | solution.py:285
  46.4 7.4 %collective-permute-start.9 = (bf16[1,2,64,512]{3,2,1,0:T(8,128)(2,1)S(1)}, bf16[1,2,64,512]{3,2,1,0:T(8,128)(2,1)S(1)}, u32[]{:S(2)}, u32[]{:S(2)}) collective-permute-start(bf16[1,2,64,512]{3,2,1,0:T(8,128)(2,1)S(1)} %add_convert_fusion.9), channel_id=1, source_target_pairs={{0,8},{1,9},{2,10},{3,11},{4,12},{5,13},{6,14},{7,15},{8,0},{9,1},... | collective-permute-start | bytes 393224 | tf_op jit(solution)/shard_map/ppermute | solution.py:285
  48.3 6.3 %collective-permute-start.15 = (bf16[1,2,64,512]{3,2,1,0:T(8,128)(2,1)S(1)}, bf16[1,2,64,512]{3,2,1,0:T(8,128)(2,1)S(1)}, u32[]{:S(2)}, u32[]{:S(2)}) collective-permute-start(bf16[1,2,64,512]{3,2,1,0:T(8,128)(2,1)S(1)} %slice.19), channel_id=1, source_target_pairs={{0,4},{1,3},{2,6},{3,1},{4,0},{5,7},{6,2},{7,5},{8,12},{9,11},{10,... | collective-permute-start | bytes 393224 | tf_op jit(solution)/shard_map/ppermute | solution.py:285
  53.9 9.2 %collective-permute-start.10 = (bf16[1,2,64,512]{3,2,1,0:T(8,128)(2,1)S(1)}, bf16[1,2,64,512]{3,2,1,0:T(8,128)(2,1)S(1)}, u32[]{:S(2)}, u32[]{:S(2)}) collective-permute-start(bf16[1,2,64,512]{3,2,1,0:T(8,128)(2,1)S(1)} %add_convert_fusion.8.refs_0_), channel_id=1, source_target_pairs={{0,4},{1,3},{2,6},{3,1},{4,0},{5,7},{6,2},{7,5},{8,12},{9,11},{10,... | collective-permute-start | bytes 393224 | tf_op jit(solution)/shard_map/ppermute | solution.py:285
  54.6 9.1 %collective-permute-start.16 = (bf16[1,2,64,512]{3,2,1,0:T(8,128)(2,1)S(1)}, bf16[1,2,64,512]{3,2,1,0:T(8,128)(2,1)S(1)}, u32[]{:S(2)}, u32[]{:S(2)}) collective-permute-start(bf16[1,2,64,512]{3,2,1,0:T(8,128)(2,1)S(1)} %add_convert_fusion.7), channel_id=1, source_target_pairs={{0,8},{1,9},{2,10},{3,11},{4,12},{5,13},{6,14},{7,15},{8,0},{9,1},... | collective-permute-start | bytes 393224 | tf_op jit(solution)/shard_map/ppermute | solution.py:285
  63.1 6.4 %collective-permute-start.11 = (bf16[2,2,64,512]{3,2,1,0:T(8,128)(2,1)S(1)}, bf16[2,2,64,512]{3,2,1,0:T(8,128)(2,1)S(1)}, u32[]{:S(2)}, u32[]{:S(2)}) collective-permute-start(bf16[2,2,64,512]{3,2,1,0:T(8,128)(2,1)S(1)} %pad_maximum_fusion), channel_id=1, source_target_pairs={{0,2},{1,5},{2,0},{3,7},{4,6},{5,1},{6,4},{7,3},{8,10},{9,13},{10,... | collective-permute-start | bytes 786440 | tf_op jit(solution)/shard_map/ppermute | solution.py:285
  63.7 5.9 %collective-permute-start.18 = (bf16[1,2,64,512]{3,2,1,0:T(8,128)(2,1)S(1)}, bf16[1,2,64,512]{3,2,1,0:T(8,128)(2,1)S(1)}, u32[]{:S(2)}, u32[]{:S(2)}) collective-permute-start(bf16[1,2,64,512]{3,2,1,0:T(8,128)(2,1)S(1)} %add_convert_fusion.6.refs_0_), channel_id=1, source_target_pairs={{0,4},{1,3},{2,6},{3,1},{4,0},{5,7},{6,2},{7,5},{8,12},{9,11},{10,... | collective-permute-start | bytes 393224 | tf_op jit(solution)/shard_map/ppermute | solution.py:285
  64.0 6.9 %collective-permute-start.12 = (bf16[1,2,64,512]{3,2,1,0:T(8,128)(2,1)S(1)}, bf16[1,2,64,512]{3,2,1,0:T(8,128)(2,1)S(1)}, u32[]{:S(2)}, u32[]{:S(2)}) collective-permute-start(bf16[1,2,64,512]{3,2,1,0:T(8,128)(2,1)S(1)} %add_convert_fusion.8.refs_0_), channel_id=1, source_target_pairs={{0,1},{1,0},{2,3},{3,2},{4,5},{5,4},{6,7},{7,6},{8,9},{9,8},{10,11... | collective-permute-start | bytes 393224 | tf_op jit(solution)/shard_map/ppermute | solution.py:274
  69.6 2.7 %collective-permute-start.14 = (bf16[2,2,64,512]{3,2,1,0:T(8,128)(2,1)S(1)}, bf16[2,2,64,512]{3,2,1,0:T(8,128)(2,1)S(1)}, u32[]{:S(2)}, u32[]{:S(2)}) collective-permute-start(bf16[2,2,64,512]{3,2,1,0:T(8,128)(2,1)S(1)} %collective-permute-done.11.refs_2_), channel_id=1, source_target_pairs={{0,1},{1,0},{2,3},{3,2},{4,5},{5,4},{6,7},{7,6},{8,9},{9,8},{10,11... | collective-permute-start | bytes 786440 | tf_op jit(solution)/shard_map/ppermute | solution.py:274
  69.6 6.4 %collective-permute-start.20 = (bf16[2,2,64,512]{3,2,1,0:T(8,128)(2,1)S(1)}, bf16[2,2,64,512]{3,2,1,0:T(8,128)(2,1)S(1)}, u32[]{:S(2)}, u32[]{:S(2)}) collective-permute-start(bf16[2,2,64,512]{3,2,1,0:T(8,128)(2,1)S(1)} %pad_maximum_fusion.1), channel_id=1, source_target_pairs={{0,2},{1,5},{2,0},{3,7},{4,6},{5,1},{6,4},{7,3},{8,10},{9,13},{10,... | collective-permute-start | bytes 786440 | tf_op jit(solution)/shard_map/ppermute | solution.py:285
  70.4 1.3 %collective-permute-start.13 = (bf16[1,2,64,512]{3,2,1,0:T(8,128)(2,1)S(1)}, bf16[1,2,64,512]{3,2,1,0:T(8,128)(2,1)S(1)}, u32[]{:S(2)}, u32[]{:S(2)}) collective-permute-start(bf16[1,2,64,512]{3,2,1,0:T(8,128)(2,1)S(1)} %collective-permute-done.10.refs_1_), channel_id=1, source_target_pairs={{0,1},{1,0},{2,3},{3,2},{4,5},{5,4},{6,7},{7,6},{8,9},{9,8},{10,11... | collective-permute-start | bytes 393224 | tf_op jit(solution)/shard_map/ppermute | solution.py:274
  70.4 1.5 %collective-permute-start.17 = (bf16[1,2,64,512]{3,2,1,0:T(8,128)(2,1)S(1)}, bf16[1,2,64,512]{3,2,1,0:T(8,128)(2,1)S(1)}, u32[]{:S(2)}, u32[]{:S(2)}) collective-permute-start(bf16[1,2,64,512]{3,2,1,0:T(8,128)(2,1)S(1)} %add_convert_fusion.6.refs_0_), channel_id=1, source_target_pairs={{0,1},{1,0},{2,3},{3,2},{4,5},{5,4},{6,7},{7,6},{8,9},{9,8},{10,11... | collective-permute-start | bytes 393224 | tf_op jit(solution)/shard_map/ppermute | solution.py:274
  70.9 1.3 %collective-permute-start.19 = (bf16[1,2,64,512]{3,2,1,0:T(8,128)(2,1)S(1)}, bf16[1,2,64,512]{3,2,1,0:T(8,128)(2,1)S(1)}, u32[]{:S(2)}, u32[]{:S(2)}) collective-permute-start(bf16[1,2,64,512]{3,2,1,0:T(8,128)(2,1)S(1)} %collective-permute-done.18.refs_1_), channel_id=1, source_target_pairs={{0,1},{1,0},{2,3},{3,2},{4,5},{5,4},{6,7},{7,6},{8,9},{9,8},{10,11... | collective-permute-start | bytes 393224 | tf_op jit(solution)/shard_map/ppermute | solution.py:274
  76.1 1.5 %collective-permute-start.21 = (bf16[2,2,64,512]{3,2,1,0:T(8,128)(2,1)S(1)}, bf16[2,2,64,512]{3,2,1,0:T(8,128)(2,1)S(1)}, u32[]{:S(2)}, u32[]{:S(2)}) collective-permute-start(bf16[2,2,64,512]{3,2,1,0:T(8,128)(2,1)S(1)} %collective-permute-done.20.refs_2_), channel_id=1, source_target_pairs={{0,1},{1,0},{2,3},{3,2},{4,5},{5,4},{6,7},{7,6},{8,9},{9,8},{10,11... | collective-permute-start | bytes 786440 | tf_op jit(solution)/shard_map/ppermute | solution.py:274
  (9 other events, 73.8 us)

commit v16 on v15

--- a/solution.py
+++ b/solution.py
@@ -19,8 +19,9 @@
 
 
 def silu_pair(pre):
-    sigma = jax.nn.sigmoid(pre)
-    return pre * sigma, sigma * (1.0 + pre * (1.0 - sigma))
+    sigma = 0.5 * jnp.tanh(0.5 * pre) + 0.5
+    silu = pre * sigma
+    return silu, sigma + silu * (1.0 - sigma)
 
 
 def pack_kernel(from_high, grid, out, wide):

time: 78.8 us -> 78.8 us (level)
  waiting for transfers between devices: 36.2 us -> 35.4 us
  transfers between devices with their start and end apart: 22 -> 22, of which waited for: 14 -> 14; matrix products, arithmetic and copies ran while one was open for 1% -> 1% of each run, Pallas kernels for 22% -> 23%
where the time goes in v16:
time: 78.8 us; the launch traced here: 78.6 us
  waiting for transfers between devices  35.4 us (45%)
  Pallas kernels  21.6 us (27%)
  starting transfers between devices  17.9 us (23%)
  between operations  1.62 us (2%)
  local copies, waits for them, and re-layouts  1.49 us (2%)
    ppermute x10, waiting for transfers between devices, swapped(): return lax.ppermute(value, ('lon', 'lat'), pairs)  22.1 us
    ppermute x10, starting transfers between devices, swapped(): return lax.ppermute(value, ('lon', 'lat'), pairs)  11.4 us
    ppermute x1, waiting for transfers between devices, on_device(): lax.ppermute(to_west, 'lon', [((i + 1) % count, i) for i in range(count)])  8.69 us
    pallas_call x1, Pallas kernels, on_device(): call(lambda *refs: weights_kernel(rows, cols // block, *refs), 'slot_weig...  4.05 us
    pallas_call x1, Pallas kernels, on_device(): call(own_kernel, 'own_points', [VMEM] * 3, [shape((nodes, latent), F32),...  3.64 us
    ppermute x1, starting transfers between devices, on_device(): lax.ppermute(to_east, 'lon', [(i, (i + 1) % count) for i in range(count)])  3.08 us
    ppermute x10, waiting for transfers between devices, core_swapped(): lax.ppermute(value, 'lat', [(i, i ^ 1) for i in range(lax.axis_size('lat'...  2.86 us
    pallas_call x1, Pallas kernels, on_device(): call(grid_kernel, 'grid_points', [VMEM] * 11, [quarter, quarter, shape((l...  2.33 us
  transfers between devices with their start and end apart: 22, of which 14 were waited for; matrix products, arithmetic and copies ran while one was open for 1% of the time, Pallas kernels for 23%

profile of v16, /device:TPU:0, one launch (start us, length us, event | category | flops | bytes accessed | tf_op | source)
XLA Modules:
  0.0 78.6 jit_solution(7544857083416007895)
XLA Ops:
  0.6 1.4 %slice.20.refs_0_ = bf16[474,8,128]{2,1,0:T(8,128)(2,1)S(1)} slice(bf16[474,8,256]{2,1,0:T(8,128)(2,1)} %bitcast.3), slice={[0:474], [0:8], [128:256]} | slice | bytes 1941504 | tf_op jit(solution)/shard_map/slice | solution.py:347
  2.6 3.1 %collective-permute-start.1 = (bf16[474,512]{1,0:T(8,128)(2,1)S(1)}, bf16[474,512]{1,0:T(8,128)(2,1)S(1)}, u32[]{:S(2)}, u32[]{:S(2)}) collective-permute-start(bf16[474,512]{1,0:T(8,128)(2,1)S(1)} %pack_east.1), channel_id=1, source_target_pairs={{0,4},{4,8},{8,12},{12,0},{1,5},{5,9},{9,13},{13,1},{2,6},{6,10},{... | collective-permute-start | bytes 1456136 | tf_op jit(solution)/shard_map/ppermute | solution.py:349
  6.2 2.1 %collective-permute-start = (bf16[474,512]{1,0:T(8,128)(2,1)S(1)}, bf16[474,512]{1,0:T(8,128)(2,1)S(1)}, u32[]{:S(2)}, u32[]{:S(2)}) collective-permute-start(bf16[474,512]{1,0:T(8,128)(2,1)S(1)} %pack_west.1), channel_id=1, source_target_pairs={{4,0},{8,4},{12,8},{0,12},{5,1},{9,5},{13,9},{1,13},{6,2},{10,6},{... | collective-permute-start | bytes 1456136 | tf_op jit(solution)/shard_map/ppermute | solution.py:352
  9.0 4.1 %slot_weights.1 = (bf16[256,3072]{1,0:T(8,128)(2,1)S(1)}, f32[256,512]{1,0:T(8,128)S(1)}) custom-call(s32[32]{0:T(128)S(1)} %copy-done.5, s32[32]{0:T(128)S(1)} %copy-done.6, s32[1]{0:T(128)S(6)} %copy.23.refs_2_, bf16[32,128,128]{2,1,0:T(8,128)(2,1)S(1)} %copy-done.3, bf16[256,512]{1,0:T(8,128)(2,1)S(1)} %copy-done.1, bf16[512,512]{1,0:T(8,128)(2,1)S(1)} %copy-done.2), custom_call_target="tpu_custom_call" | custom-call | flops 200000000 | bytes 4194304 | tf_op jit(solution)/shard_map/slot_weights/pallas_call | solution.py:354
  13.1 1.3 %own_rows.1 = (bf16[474,2048]{1,0:T(8,128)(2,1)S(1)}, bf16[512,474]{1,0:T(8,128)(2,1)S(1)}) custom-call(bf16[474,8,256]{2,1,0:T(8,128)(2,1)S(1)} %bitcast.5, bf16[474,512]{1,0:T(8,128)(2,1)S(1)} %copy-done.9), custom_call_target="tpu_custom_call" | custom-call | flops 1000000000 | bytes 5242880 | tf_op jit(solution)/shard_map/own_rows/pallas_call | solution.py:359
  14.4 3.6 %own_points.1 = (f32[256,512]{1,0:T(8,128)S(1)}, bf16[512,2048]{1,0:T(8,128)(2,1)S(1)}) custom-call(bf16[474,2048]{1,0:T(8,128)(2,1)S(1)} %get-tuple-element.69.x_t.x_own, bf16[512,474]{1,0:T(8,128)(2,1)S(1)} %get-tuple-element.67.embed_t.refs_1_, bf16[256,3072]{1,0:T(8,128)(2,1)S(1)} %get-tuple-element.68.weights_all.refs_2_), custom_call_target="tpu_custom_call" | custom-call | flops 2000000000 | bytes 7340032 | tf_op jit(solution)/shard_map/own_points/pallas_call | solution.py:363
  18.1 1.8 %collective-permute-done.1.refs_0_.x_west = bf16[474,512]{1,0:T(8,128)(2,1)S(1)} collective-permute-done((bf16[474,512]{1,0:T(8,128)(2,1)S(1)}, bf16[474,512]{1,0:T(8,128)(2,1)S(1)}, u32[]{:S(2)}, u32[]{:S(2)}) %collective-permute-start.1) | collective-permute-done | bytes 485408 | tf_op jit(solution)/shard_map/ppermute | solution.py:349
  20.8 8.7 %collective-permute-done.x.x_east = bf16[474,512]{1,0:T(8,128)(2,1)S(1)} collective-permute-done((bf16[474,512]{1,0:T(8,128)(2,1)S(1)}, bf16[474,512]{1,0:T(8,128)(2,1)S(1)}, u32[]{:S(2)}, u32[]{:S(2)}) %collective-permute-start) | collective-permute-done | bytes 485408 | tf_op jit(solution)/shard_map/ppermute | solution.py:352
  29.5 2.1 %mesh_nodes.1 = (bf16[2,2,64,512]{3,2,1,0:T(8,128)(2,1)S(1)}, bf16[2,2,64,512]{3,2,1,0:T(8,128)(2,1)S(1)}, f32[256,512]{1,0:T(8,128)S(1)}, f32[1,512]{1,0:T(1,12...) custom-call(bf16[474,512]{1,0:T(8,128)(2,1)S(1)} %collective-permute, ...), custom_call_target="tpu_custom_call" | custom-call | flops 2000000000 | bytes 8388608 | tf_op jit(solution)/shard_map/mesh_nodes/pallas_call | solution.py:378
  33.5 1.5 %collective-permute-start.4 = (bf16[2,2,64,512]{3,2,1,0:T(8,128)(2,1)S(1)}, bf16[2,2,64,512]{3,2,1,0:T(8,128)(2,1)S(1)}, u32[]{:S(2)}, u32[]{:S(2)}) collective-permute-start(bf16[2,2,64,512]{3,2,1,0:T(8,128)(2,1)S(1)} %add_convert_fusion.5), channel_id=1, source_target_pairs={{0,2},{1,5},{2,0},{3,7},{4,6},{5,1},{6,4},{7,3},{8,10},{9,13},{10,... | collective-permute-start | bytes 786440 | tf_op jit(solution)/shard_map/ppermute | solution.py:286
  35.0 2.3 %grid_points.1 = (bf16[2,2,64,512]{3,2,1,0:T(8,128)(2,1)S(1)}, bf16[2,2,64,512]{3,2,1,0:T(8,128)(2,1)S(1)}, bf16[512,3072]{1,0:T(8,128)(2,1)S(1)}, bf16[512,512]{1,0:T(8,128)(2,1)S(1)}) custom-call(bf16[512,256]{1,0:T(8,128)(2,1)S(1)} %get-tuple-element.81.back, bf16[256,3072]{1,0:T(8,128)(2,1)S(1)} %get-tuple-element.68.weights_all.refs_2_, ...), custom_call_target="tpu_custom_call" | custom-call | flops 1600000000 | bytes 9437184 | tf_op jit(solution)/shard_map/grid_points/pallas_call | solution.py:396
  40.8 1.6 %collective-permute-start.7 = (bf16[2,2,64,512]{3,2,1,0:T(8,128)(2,1)S(1)}, bf16[2,2,64,512]{3,2,1,0:T(8,128)(2,1)S(1)}, u32[]{:S(2)}, u32[]{:S(2)}) collective-permute-start(bf16[2,2,64,512]{3,2,1,0:T(8,128)(2,1)S(1)} %add_convert_fusion.1), channel_id=1, source_target_pairs={{0,2},{1,5},{2,0},{3,7},{4,6},{5,1},{6,4},{7,3},{8,10},{9,13},{10,... | collective-permute-start | bytes 786440 | tf_op jit(solution)/shard_map/ppermute | solution.py:286
  42.3 1.2 %mesh_outputs.1 = (bf16[256,512]{1,0:T(8,128)(2,1)}, f32[256,512]{1,0:T(8,128)}) custom-call(bf16[256,512]{1,0:T(8,128)(2,1)S(1)} %get-tuple-element.98.update, bf16[512,512]{1,0:T(8,128)(2,1)S(1)} %copy-done.2, bf16[256,512]{1,0:T(8,128)(2,1)S(1)} %copy-done.4, bf16[256,512]{1,0:T(8,128)(2,1)S(1)} %copy-done.1, f32[256,512]{1,0:T(8,128)S(1)} %get-tuple-element.99.grad_mesh), custom_call_target="tpu_custom_call" | custom-call | flops 200000000 | bytes 3145728 | tf_op jit(solution)/shard_map/mesh_outputs/pallas_call | solution.py:414
  43.5 2.9 %collective-permute-done.8 = bf16[1,2,64,512]{3,2,1,0:T(8,128)(2,1)S(1)} collective-permute-done((bf16[1,2,64,512]{3,2,1,0:T(8,128)(2,1)S(1)}, bf16[1,2,64,512]{3,2,1,0:T(8,128)(2,1)S(1)}, u32[]{:S(2)}, u32[]{:S(2)}) %collective-permute-start.8) | collective-permute-done | bytes 131104 | tf_op jit(solution)/shard_map/ppermute | solution.py:286
  46.4 1.7 %collective-permute-start.9 = (bf16[1,2,64,512]{3,2,1,0:T(8,128)(2,1)S(1)}, bf16[1,2,64,512]{3,2,1,0:T(8,128)(2,1)S(1)}, u32[]{:S(2)}, u32[]{:S(2)}) collective-permute-start(bf16[1,2,64,512]{3,2,1,0:T(8,128)(2,1)S(1)} %add_convert_fusion.9), channel_id=1, source_target_pairs={{0,8},{1,9},{2,10},{3,11},{4,12},{5,13},{6,14},{7,15},{8,0},{9,1},... | collective-permute-start | bytes 393224 | tf_op jit(solution)/shard_map/ppermute | solution.py:286
  48.3 1.6 %collective-permute-start.15 = (bf16[1,2,64,512]{3,2,1,0:T(8,128)(2,1)S(1)}, bf16[1,2,64,512]{3,2,1,0:T(8,128)(2,1)S(1)}, u32[]{:S(2)}, u32[]{:S(2)}) collective-permute-start(bf16[1,2,64,512]{3,2,1,0:T(8,128)(2,1)S(1)} %slice.19), channel_id=1, source_target_pairs={{0,4},{1,3},{2,6},{3,1},{4,0},{5,7},{6,2},{7,5},{8,12},{9,11},{10,... | collective-permute-start | bytes 393224 | tf_op jit(solution)/shard_map/ppermute | solution.py:286
  50.0 3.9 %collective-permute-done.9 = bf16[1,2,64,512]{3,2,1,0:T(8,128)(2,1)S(1)} collective-permute-done((bf16[1,2,64,512]{3,2,1,0:T(8,128)(2,1)S(1)}, bf16[1,2,64,512]{3,2,1,0:T(8,128)(2,1)S(1)}, u32[]{:S(2)}, u32[]{:S(2)}) %collective-permute-start.9) | collective-permute-done | bytes 131104 | tf_op jit(solution)/shard_map/ppermute | solution.py:286
  54.7 2.5 %collective-permute-start.16 = (bf16[1,2,64,512]{3,2,1,0:T(8,128)(2,1)S(1)}, bf16[1,2,64,512]{3,2,1,0:T(8,128)(2,1)S(1)}, u32[]{:S(2)}, u32[]{:S(2)}) collective-permute-start(bf16[1,2,64,512]{3,2,1,0:T(8,128)(2,1)S(1)} %add_convert_fusion.7), channel_id=1, source_target_pairs={{0,8},{1,9},{2,10},{3,11},{4,12},{5,13},{6,14},{7,15},{8,0},{9,1},... | collective-permute-start | bytes 393224 | tf_op jit(solution)/shard_map/ppermute | solution.py:286
  57.1 6.0 %collective-permute-done.10.refs_1_ = bf16[1,2,64,512]{3,2,1,0:T(8,128)(2,1)S(1)} collective-permute-done((bf16[1,2,64,512]{3,2,1,0:T(8,128)(2,1)S(1)}, bf16[1,2,64,512]{3,2,1,0:T(8,128)(2,1)S(1)}, u32[]{:S(2)}, u32[]{:S(2)}) %collective-permute-start.10) | collective-permute-done | bytes 131104 | tf_op jit(solution)/shard_map/ppermute | solution.py:286
  64.1 5.5 %collective-permute-done.11.refs_2_ = bf16[2,2,64,512]{3,2,1,0:T(8,128)(2,1)S(1)} collective-permute-done((bf16[2,2,64,512]{3,2,1,0:T(8,128)(2,1)S(1)}, bf16[2,2,64,512]{3,2,1,0:T(8,128)(2,1)S(1)}, u32[]{:S(2)}, u32[]{:S(2)}) %collective-permute-start.11) | collective-permute-done | bytes 262176 | tf_op jit(solution)/shard_map/ppermute | solution.py:286
  72.3 1.5 %order_a.1 = (f32[512,512]{1,0:T(8,128)}, f32[512,512]{1,0:T(8,128)}) custom-call(bf16[1,2,64,512]{3,2,1,0:T(8,128)(2,1)S(1)} %add_convert_fusion.8.refs_0_, bf16[1,2,64,512]{3,2,1,0:T(8,128)(2,1)S(1)} %collective-permute-done.10.refs_1_, bf16[2,2,64,512]{3,2,1,0:T(8,128)(2,1)S(1)} %collective-permute-done.11.refs_2_, ...), custom_call_target="tpu_custom_call" | custom-call | bytes 3145728 | tf_op jit(solution)/shard_map/order_a/pallas_call | solution.py:424
  73.7 2.3 %collective-permute-done.20.refs_2_ = bf16[2,2,64,512]{3,2,1,0:T(8,128)(2,1)S(1)} collective-permute-done((bf16[2,2,64,512]{3,2,1,0:T(8,128)(2,1)S(1)}, bf16[2,2,64,512]{3,2,1,0:T(8,128)(2,1)S(1)}, u32[]{:S(2)}, u32[]{:S(2)}) %collective-permute-start.20) | collective-permute-done | bytes 262176 | tf_op jit(solution)/shard_map/ppermute | solution.py:286
  76.1 1.0 %order_b.2 = (f32[512,512]{1,0:T(8,128)}, f32[474,512]{1,0:T(8,128)}, f32[1,512]{1,0:T(1,128)S(1)}) custom-call(bf16[1,2,64,512]{3,2,1,0:T(8,128)(2,1)S(1)} %add_convert_fusion.6.refs_0_, bf16[1,2,64,512]{3,2,1,0:T(8,128)(2,1)S(1)} %collective-permute-done.18.refs_1_, bf16[2,2,64,512]{3,2,1,0:T(8,128)(2,1)S(1)} %collective-permute-done.20.refs_2_), custom_call_target="tpu_custom_call" | custom-call | bytes 2097152 | tf_op jit(solution)/shard_map/order_b/pallas_call | solution.py:435
  77.6 1.0 %order_b.3 = (f32[512,512]{1,0:T(8,128)}, f32[474,512]{1,0:T(8,128)}, f32[1,512]{1,0:T(1,128)}) custom-call(bf16[1,2,64,512]{3,2,1,0:T(8,128)(2,1)S(1)} %collective-permute-done.17.refs_0_, bf16[1,2,64,512]{3,2,1,0:T(8,128)(2,1)S(1)} %collective-permute-done.19.refs_1_, ...), custom_call_target="tpu_custom_call", output_to_operand_aliasing={{0}: (4, {}), {1}: (5, {})} | custom-call | bytes 2097152 | tf_op jit(solution)/shard_map/order_b/pallas_call | solution.py:435
  (70 shorter events, 12.3 us)
Async XLA Ops:
  2.6 17.2 %collective-permute-start.1 = (bf16[474,512]{1,0:T(8,128)(2,1)S(1)}, bf16[474,512]{1,0:T(8,128)(2,1)S(1)}, u32[]{:S(2)}, u32[]{:S(2)}) collective-permute-start(bf16[474,512]{1,0:T(8,128)(2,1)S(1)} %pack_east.1), channel_id=1, source_target_pairs={{0,4},{4,8},{8,12},{12,0},{1,5},{5,9},{9,13},{13,1},{2,6},{6,10},{... | collective-permute-start | bytes 1456136 | tf_op jit(solution)/shard_map/ppermute | solution.py:349
  6.2 23.3 %collective-permute-start = (bf16[474,512]{1,0:T(8,128)(2,1)S(1)}, bf16[474,512]{1,0:T(8,128)(2,1)S(1)}, u32[]{:S(2)}, u32[]{:S(2)}) collective-permute-start(bf16[474,512]{1,0:T(8,128)(2,1)S(1)} %pack_west.1), channel_id=1, source_target_pairs={{4,0},{8,4},{12,8},{0,12},{5,1},{9,5},{13,9},{1,13},{6,2},{10,6},{... | collective-permute-start | bytes 1456136 | tf_op jit(solution)/shard_map/ppermute | solution.py:352
  18.1 11.4 %copy-start.4 = (bf16[256,512]{1,0:T(8,128)(2,1)S(1)}, bf16[256,512]{1,0:T(8,128)(2,1)}, u32[]{:S(2)}) copy-start(bf16[256,512]{1,0:T(8,128)(2,1)} %mesh_lat.3) | copy-start | bytes 786436
  18.1 11.4 %copy-start.7 = (bf16[512,512]{1,0:T(8,128)(2,1)S(1)}, bf16[512,512]{1,0:T(8,128)(2,1)}, u32[]{:S(2)}) copy-start(bf16[512,512]{1,0:T(8,128)(2,1)} %up_w.1) | copy-start | bytes 1572868
  31.6 1.6 %collective-permute-start.2 = (bf16[2,2,64,512]{3,2,1,0:T(8,128)(2,1)S(1)}, bf16[2,2,64,512]{3,2,1,0:T(8,128)(2,1)S(1)}, u32[]{:S(2)}, u32[]{:S(2)}) collective-permute-start(bf16[2,2,64,512]{3,2,1,0:T(8,128)(2,1)S(1)} %get-tuple-element.78), channel_id=1, source_target_pairs={{0,1},{1,0},{2,3},{3,2},{4,5},{5,4},{6,7},{7,6},{8,9},{9,8},{10,11... | collective-permute-start | bytes 786440 | tf_op jit(solution)/shard_map/ppermute | solution.py:275
  33.3 5.6 %collective-permute-start.3 = (bf16[2,2,64,512]{3,2,1,0:T(8,128)(2,1)S(1)}, bf16[2,2,64,512]{3,2,1,0:T(8,128)(2,1)S(1)}, u32[]{:S(2)}, u32[]{:S(2)}) collective-permute-start(bf16[2,2,64,512]{3,2,1,0:T(8,128)(2,1)S(1)} %get-tuple-element.89), channel_id=1, source_target_pairs={{0,1},{1,0},{2,3},{3,2},{4,5},{5,4},{6,7},{7,6},{8,9},{9,8},{10,11... | collective-permute-start | bytes 786440 | tf_op jit(solution)/shard_map/ppermute | solution.py:275
  33.5 6.4 %collective-permute-start.4 = (bf16[2,2,64,512]{3,2,1,0:T(8,128)(2,1)S(1)}, bf16[2,2,64,512]{3,2,1,0:T(8,128)(2,1)S(1)}, u32[]{:S(2)}, u32[]{:S(2)}) collective-permute-start(bf16[2,2,64,512]{3,2,1,0:T(8,128)(2,1)S(1)} %add_convert_fusion.5), channel_id=1, source_target_pairs={{0,2},{1,5},{2,0},{3,7},{4,6},{5,1},{6,4},{7,3},{8,10},{9,13},{10,... | collective-permute-start | bytes 786440 | tf_op jit(solution)/shard_map/ppermute | solution.py:286
  37.3 10.9 %collective-permute-start.5 = (bf16[2,2,64,512]{3,2,1,0:T(8,128)(2,1)S(1)}, bf16[2,2,64,512]{3,2,1,0:T(8,128)(2,1)S(1)}, u32[]{:S(2)}, u32[]{:S(2)}) collective-permute-start(bf16[2,2,64,512]{3,2,1,0:T(8,128)(2,1)S(1)} %get-tuple-element.94), channel_id=1, source_target_pairs={{0,1},{1,0},{2,3},{3,2},{4,5},{5,4},{6,7},{7,6},{8,9},{9,8},{10,11... | collective-permute-start | bytes 786440 | tf_op jit(solution)/shard_map/ppermute | solution.py:275
  37.4 3.3 %collective-permute-start.6 = (bf16[2,2,64,512]{3,2,1,0:T(8,128)(2,1)S(1)}, bf16[2,2,64,512]{3,2,1,0:T(8,128)(2,1)S(1)}, u32[]{:S(2)}, u32[]{:S(2)}) collective-permute-start(bf16[2,2,64,512]{3,2,1,0:T(8,128)(2,1)S(1)} %get-tuple-element.96), channel_id=1, source_target_pairs={{0,1},{1,0},{2,3},{3,2},{4,5},{5,4},{6,7},{7,6},{8,9},{9,8},{10,11... | collective-permute-start | bytes 786440 | tf_op jit(solution)/shard_map/ppermute | solution.py:275
  40.0 6.4 %collective-permute-start.8 = (bf16[1,2,64,512]{3,2,1,0:T(8,128)(2,1)S(1)}, bf16[1,2,64,512]{3,2,1,0:T(8,128)(2,1)S(1)}, u32[]{:S(2)}, u32[]{:S(2)}) collective-permute-start(bf16[1,2,64,512]{3,2,1,0:T(8,128)(2,1)S(1)} %slice.17), channel_id=1, source_target_pairs={{0,4},{1,3},{2,6},{3,1},{4,0},{5,7},{6,2},{7,5},{8,12},{9,11},{10,... | collective-permute-start | bytes 393224 | tf_op jit(solution)/shard_map/ppermute | solution.py:286
  40.8 7.4 %collective-permute-start.7 = (bf16[2,2,64,512]{3,2,1,0:T(8,128)(2,1)S(1)}, bf16[2,2,64,512]{3,2,1,0:T(8,128)(2,1)S(1)}, u32[]{:S(2)}, u32[]{:S(2)}) collective-permute-start(bf16[2,2,64,512]{3,2,1,0:T(8,128)(2,1)S(1)} %add_convert_fusion.1), channel_id=1, source_target_pairs={{0,2},{1,5},{2,0},{3,7},{4,6},{5,1},{6,4},{7,3},{8,10},{9,13},{10,... | collective-permute-start | bytes 786440 | tf_op jit(solution)/shard_map/ppermute | solution.py:286
  46.4 7.4 %collective-permute-start.9 = (bf16[1,2,64,512]{3,2,1,0:T(8,128)(2,1)S(1)}, bf16[1,2,64,512]{3,2,1,0:T(8,128)(2,1)S(1)}, u32[]{:S(2)}, u32[]{:S(2)}) collective-permute-start(bf16[1,2,64,512]{3,2,1,0:T(8,128)(2,1)S(1)} %add_convert_fusion.9), channel_id=1, source_target_pairs={{0,8},{1,9},{2,10},{3,11},{4,12},{5,13},{6,14},{7,15},{8,0},{9,1},... | collective-permute-start | bytes 393224 | tf_op jit(solution)/shard_map/ppermute | solution.py:286
  48.3 6.3 %collective-permute-start.15 = (bf16[1,2,64,512]{3,2,1,0:T(8,128)(2,1)S(1)}, bf16[1,2,64,512]{3,2,1,0:T(8,128)(2,1)S(1)}, u32[]{:S(2)}, u32[]{:S(2)}) collective-permute-start(bf16[1,2,64,512]{3,2,1,0:T(8,128)(2,1)S(1)} %slice.19), channel_id=1, source_target_pairs={{0,4},{1,3},{2,6},{3,1},{4,0},{5,7},{6,2},{7,5},{8,12},{9,11},{10,... | collective-permute-start | bytes 393224 | tf_op jit(solution)/shard_map/ppermute | solution.py:286
  53.9 9.2 %collective-permute-start.10 = (bf16[1,2,64,512]{3,2,1,0:T(8,128)(2,1)S(1)}, bf16[1,2,64,512]{3,2,1,0:T(8,128)(2,1)S(1)}, u32[]{:S(2)}, u32[]{:S(2)}) collective-permute-start(bf16[1,2,64,512]{3,2,1,0:T(8,128)(2,1)S(1)} %add_convert_fusion.8.refs_0_), channel_id=1, source_target_pairs={{0,4},{1,3},{2,6},{3,1},{4,0},{5,7},{6,2},{7,5},{8,12},{9,11},{10,... | collective-permute-start | bytes 393224 | tf_op jit(solution)/shard_map/ppermute | solution.py:286
  54.7 9.0 %collective-permute-start.16 = (bf16[1,2,64,512]{3,2,1,0:T(8,128)(2,1)S(1)}, bf16[1,2,64,512]{3,2,1,0:T(8,128)(2,1)S(1)}, u32[]{:S(2)}, u32[]{:S(2)}) collective-permute-start(bf16[1,2,64,512]{3,2,1,0:T(8,128)(2,1)S(1)} %add_convert_fusion.7), channel_id=1, source_target_pairs={{0,8},{1,9},{2,10},{3,11},{4,12},{5,13},{6,14},{7,15},{8,0},{9,1},... | collective-permute-start | bytes 393224 | tf_op jit(solution)/shard_map/ppermute | solution.py:286
  63.1 6.4 %collective-permute-start.11 = (bf16[2,2,64,512]{3,2,1,0:T(8,128)(2,1)S(1)}, bf16[2,2,64,512]{3,2,1,0:T(8,128)(2,1)S(1)}, u32[]{:S(2)}, u32[]{:S(2)}) collective-permute-start(bf16[2,2,64,512]{3,2,1,0:T(8,128)(2,1)S(1)} %pad_maximum_fusion), channel_id=1, source_target_pairs={{0,2},{1,5},{2,0},{3,7},{4,6},{5,1},{6,4},{7,3},{8,10},{9,13},{10,... | collective-permute-start | bytes 786440 | tf_op jit(solution)/shard_map/ppermute | solution.py:286
  63.7 5.9 %collective-permute-start.18 = (bf16[1,2,64,512]{3,2,1,0:T(8,128)(2,1)S(1)}, bf16[1,2,64,512]{3,2,1,0:T(8,128)(2,1)S(1)}, u32[]{:S(2)}, u32[]{:S(2)}) collective-permute-start(bf16[1,2,64,512]{3,2,1,0:T(8,128)(2,1)S(1)} %add_convert_fusion.6.refs_0_), channel_id=1, source_target_pairs={{0,4},{1,3},{2,6},{3,1},{4,0},{5,7},{6,2},{7,5},{8,12},{9,11},{10,... | collective-permute-start | bytes 393224 | tf_op jit(solution)/shard_map/ppermute | solution.py:286
  64.1 6.8 %collective-permute-start.12 = (bf16[1,2,64,512]{3,2,1,0:T(8,128)(2,1)S(1)}, bf16[1,2,64,512]{3,2,1,0:T(8,128)(2,1)S(1)}, u32[]{:S(2)}, u32[]{:S(2)}) collective-permute-start(bf16[1,2,64,512]{3,2,1,0:T(8,128)(2,1)S(1)} %add_convert_fusion.8.refs_0_), channel_id=1, source_target_pairs={{0,1},{1,0},{2,3},{3,2},{4,5},{5,4},{6,7},{7,6},{8,9},{9,8},{10,11... | collective-permute-start | bytes 393224 | tf_op jit(solution)/shard_map/ppermute | solution.py:275
  69.6 2.7 %collective-permute-start.14 = (bf16[2,2,64,512]{3,2,1,0:T(8,128)(2,1)S(1)}, bf16[2,2,64,512]{3,2,1,0:T(8,128)(2,1)S(1)}, u32[]{:S(2)}, u32[]{:S(2)}) collective-permute-start(bf16[2,2,64,512]{3,2,1,0:T(8,128)(2,1)S(1)} %collective-permute-done.11.refs_2_), channel_id=1, source_target_pairs={{0,1},{1,0},{2,3},{3,2},{4,5},{5,4},{6,7},{7,6},{8,9},{9,8},{10,11... | collective-permute-start | bytes 786440 | tf_op jit(solution)/shard_map/ppermute | solution.py:275
  69.6 6.4 %collective-permute-start.20 = (bf16[2,2,64,512]{3,2,1,0:T(8,128)(2,1)S(1)}, bf16[2,2,64,512]{3,2,1,0:T(8,128)(2,1)S(1)}, u32[]{:S(2)}, u32[]{:S(2)}) collective-permute-start(bf16[2,2,64,512]{3,2,1,0:T(8,128)(2,1)S(1)} %pad_maximum_fusion.1), channel_id=1, source_target_pairs={{0,2},{1,5},{2,0},{3,7},{4,6},{5,1},{6,4},{7,3},{8,10},{9,13},{10,... | collective-permute-start | bytes 786440 | tf_op jit(solution)/shard_map/ppermute | solution.py:286
  70.4 1.3 %collective-permute-start.13 = (bf16[1,2,64,512]{3,2,1,0:T(8,128)(2,1)S(1)}, bf16[1,2,64,512]{3,2,1,0:T(8,128)(2,1)S(1)}, u32[]{:S(2)}, u32[]{:S(2)}) collective-permute-start(bf16[1,2,64,512]{3,2,1,0:T(8,128)(2,1)S(1)} %collective-permute-done.10.refs_1_), channel_id=1, source_target_pairs={{0,1},{1,0},{2,3},{3,2},{4,5},{5,4},{6,7},{7,6},{8,9},{9,8},{10,11... | collective-permute-start | bytes 393224 | tf_op jit(solution)/shard_map/ppermute | solution.py:275
  70.4 1.5 %collective-permute-start.17 = (bf16[1,2,64,512]{3,2,1,0:T(8,128)(2,1)S(1)}, bf16[1,2,64,512]{3,2,1,0:T(8,128)(2,1)S(1)}, u32[]{:S(2)}, u32[]{:S(2)}) collective-permute-start(bf16[1,2,64,512]{3,2,1,0:T(8,128)(2,1)S(1)} %add_convert_fusion.6.refs_0_), channel_id=1, source_target_pairs={{0,1},{1,0},{2,3},{3,2},{4,5},{5,4},{6,7},{7,6},{8,9},{9,8},{10,11... | collective-permute-start | bytes 393224 | tf_op jit(solution)/shard_map/ppermute | solution.py:275
  70.9 1.3 %collective-permute-start.19 = (bf16[1,2,64,512]{3,2,1,0:T(8,128)(2,1)S(1)}, bf16[1,2,64,512]{3,2,1,0:T(8,128)(2,1)S(1)}, u32[]{:S(2)}, u32[]{:S(2)}) collective-permute-start(bf16[1,2,64,512]{3,2,1,0:T(8,128)(2,1)S(1)} %collective-permute-done.18.refs_1_), channel_id=1, source_target_pairs={{0,1},{1,0},{2,3},{3,2},{4,5},{5,4},{6,7},{7,6},{8,9},{9,8},{10,11... | collective-permute-start | bytes 393224 | tf_op jit(solution)/shard_map/ppermute | solution.py:275
  76.1 1.5 %collective-permute-start.21 = (bf16[2,2,64,512]{3,2,1,0:T(8,128)(2,1)S(1)}, bf16[2,2,64,512]{3,2,1,0:T(8,128)(2,1)S(1)}, u32[]{:S(2)}, u32[]{:S(2)}) collective-permute-start(bf16[2,2,64,512]{3,2,1,0:T(8,128)(2,1)S(1)} %collective-permute-done.20.refs_2_), channel_id=1, source_target_pairs={{0,1},{1,0},{2,3},{3,2},{4,5},{5,4},{6,7},{7,6},{8,9},{9,8},{10,11... | collective-permute-start | bytes 786440 | tf_op jit(solution)/shard_map/ppermute | solution.py:275
  (9 other events, 73.0 us)

commit v17 on v15

--- a/solution.py
+++ b/solution.py
@@ -114,11 +114,6 @@
     return contract(weights, hidden.astype(BF), 1, 1)
 
 
-def west_kernel(first, x, embed_t, weights_all, h_own, h_sum, slope):
-    points = x.shape[1]
-    h_sum[...] = h_own[...] + halo_part(x, embed_t, weights_all[:, first : first + points], slope)
-
-
 def to_chunks(grads, stack, perm, start):
     count, matrices, size, _ = grads.shape
     for j in range(count):
@@ -143,13 +138,15 @@
 
 
 def mesh_kernel(
-    x, embed_t, weights_all, h_sum, message_w, up_w, gain, mesh_lat, grad_update,
-    sent_high, sent_low, grad_mesh, grad_gain, gathered, grad_aggregate, normed, grad_pre_up, update, slope, stack,
+    x_west, x_east, embed_t, weights_all, h_own, message_w, up_w, gain, mesh_lat, grad_update,
+    sent_high, sent_low, grad_mesh, grad_gain, gathered, grad_aggregate, normed, grad_pre_up, update, slope_west, slope_east,
+    stack,
 ):
     perm = chunk_order()
-    points = x.shape[1]
-    first = weights_all.shape[1] - points
-    total = h_sum[...] + halo_part(x, embed_t, weights_all[:, first:], slope)
+    side = x_west.shape[1]
+    first = weights_all.shape[1] - 2 * side
+    total = h_own[...] + halo_part(x_west, embed_t, weights_all[:, first : first + side], slope_west)
+    total += halo_part(x_east, embed_t, weights_all[:, first + side :], slope_east)
     gathered[...] = total.astype(BF)
     summed = mesh_lat[...].astype(F32) + contract(gathered[...], message_w[...], 1, 0)
     rinv = lax.rsqrt(jnp.mean(summed * summed, axis=1, keepdims=True) + epsilon)
@@ -364,23 +361,18 @@
         2_000_000_000, 7 * MIB, 16,
     )(x_own, embed_t, weights_all)
 
-    h_sum, slope_west = call(
-        lambda *refs: west_kernel(own, *refs), "west_points", [VMEM] * 4,
-        [shape((nodes, latent), F32), shape((latent, side), BF)],
-        600_000_000, 3 * MIB, 16,
-    )(x_west, embed_t, weights_all, h_own)
-
     quarter = shape((2, 2, latent // 8, latent), BF)
     node_rows = shape((nodes, latent), BF)
     (
-        sent_high, sent_low, grad_mesh, gain_term, gathered, grad_aggregate, normed, grad_pre_up, update, slope_east
+        sent_high, sent_low, grad_mesh, gain_term, gathered, grad_aggregate, normed, grad_pre_up, update, slope_west,
+        slope_east,
     ) = call(
-        mesh_kernel, "mesh_nodes", [VMEM] * 9,
+        mesh_kernel, "mesh_nodes", [VMEM] * 10,
         [quarter, quarter, shape((nodes, latent), F32), shape((1, latent), F32)]
         + [node_rows] * 5
-        + [shape((latent, side), BF)],
+        + [shape((latent, side), BF)] * 2,
         2_000_000_000, 8 * MIB, 16, [pltpu.VMEM((2, latent // 2, latent), BF)],
-    )(x_east, embed_t, weights_all, h_sum, message_w, up_w, gain.reshape(1, latent), mesh_lat, grad_update)
+    )(x_west, x_east, embed_t, weights_all, h_own, message_w, up_w, gain.reshape(1, latent), mesh_lat, grad_update)
     got_high = core_swapped(sent_high)
     kept_high, kept_low, back = call(
         tail_kernel, "mesh_tail", [VMEM] * 5, [quarter, quarter, shape((latent, nodes), BF)],

time: 78.8 us -> 79.7 us (1.011)
  waiting for transfers between devices: 36.2 us -> 37.7 us
    ppermute x1, waiting for transfers between devices: 2.45 us -> 10.3 us  [on_device(): lax.ppermute(to_east, 'lon', [(i, (i + 1) % count) for i in range(count)])]
    ppermute x1, waiting for transfers between devices: 8.72 us -> 2.42 us  [on_device(): lax.ppermute(to_west, 'lon', [((i + 1) % count, i) for i in range(count)])]
    ppermute x1, starting transfers between devices: 3.08 us -> 0.01 us  [on_device(): lax.ppermute(to_east, 'lon', [(i, (i + 1) % count) for i in range(count)])]
    ppermute x1, starting transfers between devices: 2.11 us -> 5.1 us  [on_device(): lax.ppermute(to_west, 'lon', [((i + 1) % count, i) for i in range(count)])]
    pallas_call x2 -> x1, Pallas kernels: 2.95 us -> 2.66 us  [on_device(): call(mesh_kernel, 'mesh_nodes', [VMEM] * 10, [quarter, quarter, shape((no...]
  transfers between devices with their start and end apart: 22 -> 22, of which waited for: 14 -> 14; matrix products, arithmetic and copies ran while one was open for 1% -> 1% of each run, Pallas kernels for 22% -> 20%
where the time goes in v17:
time: 79.7 us; the launch traced here: 79.6 us
  waiting for transfers between devices  37.7 us (47%)
  Pallas kernels  20.9 us (26%)
  starting transfers between devices  17.4 us (22%)
  between operations  1.63 us (2%)
  local copies, waits for them, and re-layouts  1.49 us (2%)
    ppermute x10, waiting for transfers between devices, swapped(): return lax.ppermute(value, ('lon', 'lat'), pairs)  22.1 us
    ppermute x10, starting transfers between devices, swapped(): return lax.ppermute(value, ('lon', 'lat'), pairs)  10.8 us
    ppermute x1, waiting for transfers between devices, on_device(): lax.ppermute(to_east, 'lon', [(i, (i + 1) % count) for i in range(count)])  10.3 us
    ppermute x1, starting transfers between devices, on_device(): lax.ppermute(to_west, 'lon', [((i + 1) % count, i) for i in range(count)])  5.1 us
    pallas_call x1, Pallas kernels, on_device(): call(own_kernel, 'own_points', [VMEM] * 3, [shape((nodes, latent), F32),...  3.56 us
    pallas_call x1, Pallas kernels, on_device(): call(lambda *refs: weights_kernel(rows, cols // block, *refs), 'slot_weig...  3.54 us
    ppermute x10, waiting for transfers between devices, core_swapped(): lax.ppermute(value, 'lat', [(i, i ^ 1) for i in range(lax.axis_size('lat'...  2.86 us
    pallas_call x1, Pallas kernels, on_device(): call(mesh_kernel, 'mesh_nodes', [VMEM] * 10, [quarter, quarter, shape((no...  2.66 us
  transfers between devices with their start and end apart: 22, of which 14 were waited for; matrix products, arithmetic and copies ran while one was open for 1% of the time, Pallas kernels for 20%

profile of v17, /device:TPU:0, one launch (start us, length us, event | category | flops | bytes accessed | tf_op | source)
XLA Modules:
  0.0 79.6 jit_solution(10666135163093846011)
XLA Ops:
  0.6 1.4 %slice.20.refs_0_ = bf16[474,8,128]{2,1,0:T(8,128)(2,1)S(1)} slice(bf16[474,8,256]{2,1,0:T(8,128)(2,1)} %bitcast.3), slice={[0:474], [0:8], [128:256]} | slice | bytes 1941504 | tf_op jit(solution)/shard_map/slice | solution.py:343
  3.2 5.1 %collective-permute-start.1 = (bf16[474,512]{1,0:T(8,128)(2,1)S(1)}, bf16[474,512]{1,0:T(8,128)(2,1)S(1)}, u32[]{:S(2)}, u32[]{:S(2)}) collective-permute-start(bf16[474,512]{1,0:T(8,128)(2,1)S(1)} %pack_west.1), channel_id=1, source_target_pairs={{4,0},{8,4},{12,8},{0,12},{5,1},{9,5},{13,9},{1,13},{6,2},{10,6},{... | collective-permute-start | bytes 1456136 | tf_op jit(solution)/shard_map/ppermute | solution.py:348
  9.0 3.5 %slot_weights.1 = (bf16[256,3072]{1,0:T(8,128)(2,1)S(1)}, f32[256,512]{1,0:T(8,128)S(1)}) custom-call(s32[32]{0:T(128)S(1)} %copy-done.5, s32[32]{0:T(128)S(1)} %copy-done.6, s32[1]{0:T(128)S(6)} %copy.23.refs_2_, bf16[32,128,128]{2,1,0:T(8,128)(2,1)S(1)} %copy-done.3, bf16[256,512]{1,0:T(8,128)(2,1)S(1)} %copy-done.1, bf16[512,512]{1,0:T(8,128)(2,1)S(1)} %copy-done.2), custom_call_target="tpu_custom_call" | custom-call | flops 200000000 | bytes 4194304 | tf_op jit(solution)/shard_map/slot_weights/pallas_call | solution.py:350
  12.5 1.3 %own_rows.1 = (bf16[474,2048]{1,0:T(8,128)(2,1)S(1)}, bf16[512,474]{1,0:T(8,128)(2,1)S(1)}) custom-call(bf16[474,8,256]{2,1,0:T(8,128)(2,1)S(1)} %bitcast.5, bf16[474,512]{1,0:T(8,128)(2,1)S(1)} %copy-done.9), custom_call_target="tpu_custom_call" | custom-call | flops 1000000000 | bytes 5242880 | tf_op jit(solution)/shard_map/own_rows/pallas_call | solution.py:355
  13.9 3.6 %own_points.1 = (f32[256,512]{1,0:T(8,128)S(1)}, bf16[512,2048]{1,0:T(8,128)(2,1)S(1)}) custom-call(bf16[474,2048]{1,0:T(8,128)(2,1)S(1)} %get-tuple-element.68.x_t.x_own, bf16[512,474]{1,0:T(8,128)(2,1)S(1)} %get-tuple-element.66.embed_t, bf16[256,3072]{1,0:T(8,128)(2,1)S(1)} %get-tuple-element.67.weights_all), custom_call_target="tpu_custom_call" | custom-call | flops 2000000000 | bytes 7340032 | tf_op jit(solution)/shard_map/own_points/pallas_call | solution.py:359
  17.5 2.4 %collective-permute-done.1.x_east = bf16[474,512]{1,0:T(8,128)(2,1)S(1)} collective-permute-done((bf16[474,512]{1,0:T(8,128)(2,1)S(1)}, bf16[474,512]{1,0:T(8,128)(2,1)S(1)}, u32[]{:S(2)}, u32[]{:S(2)}) %collective-permute-start.1) | collective-permute-done | bytes 485408 | tf_op jit(solution)/shard_map/ppermute | solution.py:348
  19.9 10.3 %collective-permute-done.x_west = bf16[474,512]{1,0:T(8,128)(2,1)S(1)} collective-permute-done((bf16[474,512]{1,0:T(8,128)(2,1)S(1)}, bf16[474,512]{1,0:T(8,128)(2,1)S(1)}, u32[]{:S(2)}, u32[]{:S(2)}) %collective-permute-start) | collective-permute-done | bytes 485408 | tf_op jit(solution)/shard_map/ppermute | solution.py:345
  30.2 2.7 %mesh_nodes.1 = (bf16[2,2,64,512]{3,2,1,0:T(8,128)(2,1)S(1)}, bf16[2,2,64,512]{3,2,1,0:T(8,128)(2,1)S(1)}, f32[256,512]{1,0:T(8,128)S(1)}, f32[1,512]{1,0:T(1,12...) custom-call(bf16[474,512]{1,0:T(8,128)(2,1)S(1)} %collective-permute, ...), custom_call_target="tpu_custom_call" | custom-call | flops 2000000000 | bytes 8388608 | tf_op jit(solution)/shard_map/mesh_nodes/pallas_call | solution.py:369
  34.7 1.5 %collective-permute-start.4 = (bf16[2,2,64,512]{3,2,1,0:T(8,128)(2,1)S(1)}, bf16[2,2,64,512]{3,2,1,0:T(8,128)(2,1)S(1)}, u32[]{:S(2)}, u32[]{:S(2)}) collective-permute-start(bf16[2,2,64,512]{3,2,1,0:T(8,128)(2,1)S(1)} %add_convert_fusion.5), channel_id=1, source_target_pairs={{0,2},{1,5},{2,0},{3,7},{4,6},{5,1},{6,4},{7,3},{8,10},{9,13},{10,... | collective-permute-start | bytes 786440 | tf_op jit(solution)/shard_map/ppermute | solution.py:282
  36.2 2.3 %grid_points.1 = (bf16[2,2,64,512]{3,2,1,0:T(8,128)(2,1)S(1)}, bf16[2,2,64,512]{3,2,1,0:T(8,128)(2,1)S(1)}, bf16[512,3072]{1,0:T(8,128)(2,1)S(1)}, bf16[512,512]{1,0:T(8,128)(2,1)S(1)}) custom-call(bf16[512,256]{1,0:T(8,128)(2,1)S(1)} %get-tuple-element.79.back, bf16[256,3072]{1,0:T(8,128)(2,1)S(1)} %get-tuple-element.67.weights_all, ...), custom_call_target="tpu_custom_call" | custom-call | flops 1600000000 | bytes 9437184 | tf_op jit(solution)/shard_map/grid_points/pallas_call | solution.py:387
  39.1 1.2 %grid_kept.1.sums = f32[256,512]{1,0:T(8,128)S(1)} custom-call(bf16[512,3072]{1,0:T(8,128)(2,1)S(1)} %get-tuple-element.89.grad_pre, bf16[474,2048]{1,0:T(8,128)(2,1)S(1)} %get-tuple-element.68.x_t.x_own, bf16[474,512]{1,0:T(8,128)(2,1)S(1)} %collective-permute-done.x_west, bf16[474,512]{1,0:T(8,128)(2,1)S(1)} %collective-permute-done.1.x_east, ...), custom_call_target="tpu_custom_call" | custom-call | flops 800000000 | bytes 6291456 | tf_op jit(solution)/shard_map/grid_kept/pallas_call | solution.py:395
  41.2 1.7 %collective-permute-start.8 = (bf16[1,2,64,512]{3,2,1,0:T(8,128)(2,1)S(1)}, bf16[1,2,64,512]{3,2,1,0:T(8,128)(2,1)S(1)}, u32[]{:S(2)}, u32[]{:S(2)}) collective-permute-start(bf16[1,2,64,512]{3,2,1,0:T(8,128)(2,1)S(1)} %slice.17), channel_id=1, source_target_pairs={{0,4},{1,3},{2,6},{3,1},{4,0},{5,7},{6,2},{7,5},{8,12},{9,11},{10,... | collective-permute-start | bytes 393224 | tf_op jit(solution)/shard_map/ppermute | solution.py:282
  43.1 1.6 %collective-permute-start.7 = (bf16[2,2,64,512]{3,2,1,0:T(8,128)(2,1)S(1)}, bf16[2,2,64,512]{3,2,1,0:T(8,128)(2,1)S(1)}, u32[]{:S(2)}, u32[]{:S(2)}) collective-permute-start(bf16[2,2,64,512]{3,2,1,0:T(8,128)(2,1)S(1)} %add_convert_fusion.1), channel_id=1, source_target_pairs={{0,2},{1,5},{2,0},{3,7},{4,6},{5,1},{6,4},{7,3},{8,10},{9,13},{10,... | collective-permute-start | bytes 786440 | tf_op jit(solution)/shard_map/ppermute | solution.py:282
  44.6 1.2 %mesh_outputs.1 = (bf16[256,512]{1,0:T(8,128)(2,1)}, f32[256,512]{1,0:T(8,128)}) custom-call(bf16[256,512]{1,0:T(8,128)(2,1)S(1)} %get-tuple-element.96.update, bf16[512,512]{1,0:T(8,128)(2,1)S(1)} %copy-done.2, bf16[256,512]{1,0:T(8,128)(2,1)S(1)} %copy-done.4, bf16[256,512]{1,0:T(8,128)(2,1)S(1)} %copy-done.1, f32[256,512]{1,0:T(8,128)S(1)} %get-tuple-element.97.grad_mesh), custom_call_target="tpu_custom_call" | custom-call | flops 200000000 | bytes 3145728 | tf_op jit(solution)/shard_map/mesh_outputs/pallas_call | solution.py:405
  45.8 1.8 %collective-permute-done.8 = bf16[1,2,64,512]{3,2,1,0:T(8,128)(2,1)S(1)} collective-permute-done((bf16[1,2,64,512]{3,2,1,0:T(8,128)(2,1)S(1)}, bf16[1,2,64,512]{3,2,1,0:T(8,128)(2,1)S(1)}, u32[]{:S(2)}, u32[]{:S(2)}) %collective-permute-start.8) | collective-permute-done | bytes 131104 | tf_op jit(solution)/shard_map/ppermute | solution.py:282
  50.3 4.8 %collective-permute-done.9 = bf16[1,2,64,512]{3,2,1,0:T(8,128)(2,1)S(1)} collective-permute-done((bf16[1,2,64,512]{3,2,1,0:T(8,128)(2,1)S(1)}, bf16[1,2,64,512]{3,2,1,0:T(8,128)(2,1)S(1)}, u32[]{:S(2)}, u32[]{:S(2)}) %collective-permute-start.9) | collective-permute-done | bytes 131104 | tf_op jit(solution)/shard_map/ppermute | solution.py:282
  55.5 2.1 %collective-permute-start.16 = (bf16[1,2,64,512]{3,2,1,0:T(8,128)(2,1)S(1)}, bf16[1,2,64,512]{3,2,1,0:T(8,128)(2,1)S(1)}, u32[]{:S(2)}, u32[]{:S(2)}) collective-permute-start(bf16[1,2,64,512]{3,2,1,0:T(8,128)(2,1)S(1)} %add_convert_fusion.7), channel_id=1, source_target_pairs={{0,8},{1,9},{2,10},{3,11},{4,12},{5,13},{6,14},{7,15},{8,0},{9,1},... | collective-permute-start | bytes 393224 | tf_op jit(solution)/shard_map/ppermute | solution.py:282
  57.6 6.5 %collective-permute-done.10.refs_1_ = bf16[1,2,64,512]{3,2,1,0:T(8,128)(2,1)S(1)} collective-permute-done((bf16[1,2,64,512]{3,2,1,0:T(8,128)(2,1)S(1)}, bf16[1,2,64,512]{3,2,1,0:T(8,128)(2,1)S(1)}, u32[]{:S(2)}, u32[]{:S(2)}) %collective-permute-start.10) | collective-permute-done | bytes 131104 | tf_op jit(solution)/shard_map/ppermute | solution.py:282
  64.1 1.0 %collective-permute-start.11 = (bf16[2,2,64,512]{3,2,1,0:T(8,128)(2,1)S(1)}, bf16[2,2,64,512]{3,2,1,0:T(8,128)(2,1)S(1)}, u32[]{:S(2)}, u32[]{:S(2)}) collective-permute-start(bf16[2,2,64,512]{3,2,1,0:T(8,128)(2,1)S(1)} %pad_maximum_fusion), channel_id=1, source_target_pairs={{0,2},{1,5},{2,0},{3,7},{4,6},{5,1},{6,4},{7,3},{8,10},{9,13},{10,... | collective-permute-start | bytes 786440 | tf_op jit(solution)/shard_map/ppermute | solution.py:282
  65.4 5.2 %collective-permute-done.11.refs_2_ = bf16[2,2,64,512]{3,2,1,0:T(8,128)(2,1)S(1)} collective-permute-done((bf16[2,2,64,512]{3,2,1,0:T(8,128)(2,1)S(1)}, bf16[2,2,64,512]{3,2,1,0:T(8,128)(2,1)S(1)}, u32[]{:S(2)}, u32[]{:S(2)}) %collective-permute-start.11) | collective-permute-done | bytes 262176 | tf_op jit(solution)/shard_map/ppermute | solution.py:282
  70.6 1.0 %collective-permute-start.20 = (bf16[2,2,64,512]{3,2,1,0:T(8,128)(2,1)S(1)}, bf16[2,2,64,512]{3,2,1,0:T(8,128)(2,1)S(1)}, u32[]{:S(2)}, u32[]{:S(2)}) collective-permute-start(bf16[2,2,64,512]{3,2,1,0:T(8,128)(2,1)S(1)} %pad_maximum_fusion.1), channel_id=1, source_target_pairs={{0,2},{1,5},{2,0},{3,7},{4,6},{5,1},{6,4},{7,3},{8,10},{9,13},{10,... | collective-permute-start | bytes 786440 | tf_op jit(solution)/shard_map/ppermute | solution.py:282
  73.5 1.5 %order_a.1 = (f32[512,512]{1,0:T(8,128)}, f32[512,512]{1,0:T(8,128)}) custom-call(bf16[1,2,64,512]{3,2,1,0:T(8,128)(2,1)S(1)} %add_convert_fusion.8.refs_0_, bf16[1,2,64,512]{3,2,1,0:T(8,128)(2,1)S(1)} %collective-permute-done.10.refs_1_, bf16[2,2,64,512]{3,2,1,0:T(8,128)(2,1)S(1)} %collective-permute-done.11.refs_2_, ...), custom_call_target="tpu_custom_call" | custom-call | bytes 3145728 | tf_op jit(solution)/shard_map/order_a/pallas_call | solution.py:415
  75.0 2.1 %collective-permute-done.20.refs_2_ = bf16[2,2,64,512]{3,2,1,0:T(8,128)(2,1)S(1)} collective-permute-done((bf16[2,2,64,512]{3,2,1,0:T(8,128)(2,1)S(1)}, bf16[2,2,64,512]{3,2,1,0:T(8,128)(2,1)S(1)}, u32[]{:S(2)}, u32[]{:S(2)}) %collective-permute-start.20) | collective-permute-done | bytes 262176 | tf_op jit(solution)/shard_map/ppermute | solution.py:282
  77.0 1.0 %order_b.2 = (f32[512,512]{1,0:T(8,128)}, f32[474,512]{1,0:T(8,128)}, f32[1,512]{1,0:T(1,128)S(1)}) custom-call(bf16[1,2,64,512]{3,2,1,0:T(8,128)(2,1)S(1)} %add_convert_fusion.6.refs_0_, bf16[1,2,64,512]{3,2,1,0:T(8,128)(2,1)S(1)} %collective-permute-done.18.refs_1_, bf16[2,2,64,512]{3,2,1,0:T(8,128)(2,1)S(1)} %collective-permute-done.20.refs_2_), custom_call_target="tpu_custom_call" | custom-call | bytes 2097152 | tf_op jit(solution)/shard_map/order_b/pallas_call | solution.py:426
  (69 shorter events, 11.2 us)
Async XLA Ops:
  3.2 16.7 %collective-permute-start.1 = (bf16[474,512]{1,0:T(8,128)(2,1)S(1)}, bf16[474,512]{1,0:T(8,128)(2,1)S(1)}, u32[]{:S(2)}, u32[]{:S(2)}) collective-permute-start(bf16[474,512]{1,0:T(8,128)(2,1)S(1)} %pack_west.1), channel_id=1, source_target_pairs={{4,0},{8,4},{12,8},{0,12},{5,1},{9,5},{13,9},{1,13},{6,2},{10,6},{... | collective-permute-start | bytes 1456136 | tf_op jit(solution)/shard_map/ppermute | solution.py:348
  8.3 21.9 %collective-permute-start = (bf16[474,512]{1,0:T(8,128)(2,1)S(1)}, bf16[474,512]{1,0:T(8,128)(2,1)S(1)}, u32[]{:S(2)}, u32[]{:S(2)}) collective-permute-start(bf16[474,512]{1,0:T(8,128)(2,1)S(1)} %pack_east.1), channel_id=1, source_target_pairs={{0,4},{4,8},{8,12},{12,0},{1,5},{5,9},{9,13},{13,1},{2,6},{6,10},{... | collective-permute-start | bytes 1456136 | tf_op jit(solution)/shard_map/ppermute | solution.py:345
  13.9 16.3 %copy-start.4 = (bf16[256,512]{1,0:T(8,128)(2,1)S(1)}, bf16[256,512]{1,0:T(8,128)(2,1)}, u32[]{:S(2)}) copy-start(bf16[256,512]{1,0:T(8,128)(2,1)} %mesh_lat.3) | copy-start | bytes 786436
  13.9 16.3 %copy-start.7 = (bf16[512,512]{1,0:T(8,128)(2,1)S(1)}, bf16[512,512]{1,0:T(8,128)(2,1)}, u32[]{:S(2)}) copy-start(bf16[512,512]{1,0:T(8,128)(2,1)} %up_w.1) | copy-start | bytes 1572868
  32.9 1.6 %collective-permute-start.2 = (bf16[2,2,64,512]{3,2,1,0:T(8,128)(2,1)S(1)}, bf16[2,2,64,512]{3,2,1,0:T(8,128)(2,1)S(1)}, u32[]{:S(2)}, u32[]{:S(2)}) collective-permute-start(bf16[2,2,64,512]{3,2,1,0:T(8,128)(2,1)S(1)} %get-tuple-element.76), channel_id=1, source_target_pairs={{0,1},{1,0},{2,3},{3,2},{4,5},{5,4},{6,7},{7,6},{8,9},{9,8},{10,11... | collective-permute-start | bytes 786440 | tf_op jit(solution)/shard_map/ppermute | solution.py:271
  34.5 5.8 %collective-permute-start.3 = (bf16[2,2,64,512]{3,2,1,0:T(8,128)(2,1)S(1)}, bf16[2,2,64,512]{3,2,1,0:T(8,128)(2,1)S(1)}, u32[]{:S(2)}, u32[]{:S(2)}) collective-permute-start(bf16[2,2,64,512]{3,2,1,0:T(8,128)(2,1)S(1)} %get-tuple-element.87), channel_id=1, source_target_pairs={{0,1},{1,0},{2,3},{3,2},{4,5},{5,4},{6,7},{7,6},{8,9},{9,8},{10,11... | collective-permute-start | bytes 786440 | tf_op jit(solution)/shard_map/ppermute | solution.py:271
  34.7 6.4 %collective-permute-start.4 = (bf16[2,2,64,512]{3,2,1,0:T(8,128)(2,1)S(1)}, bf16[2,2,64,512]{3,2,1,0:T(8,128)(2,1)S(1)}, u32[]{:S(2)}, u32[]{:S(2)}) collective-permute-start(bf16[2,2,64,512]{3,2,1,0:T(8,128)(2,1)S(1)} %add_convert_fusion.5), channel_id=1, source_target_pairs={{0,2},{1,5},{2,0},{3,7},{4,6},{5,1},{6,4},{7,3},{8,10},{9,13},{10,... | collective-permute-start | bytes 786440 | tf_op jit(solution)/shard_map/ppermute | solution.py:282
  38.5 10.0 %collective-permute-start.5 = (bf16[2,2,64,512]{3,2,1,0:T(8,128)(2,1)S(1)}, bf16[2,2,64,512]{3,2,1,0:T(8,128)(2,1)S(1)}, u32[]{:S(2)}, u32[]{:S(2)}) collective-permute-start(bf16[2,2,64,512]{3,2,1,0:T(8,128)(2,1)S(1)} %get-tuple-element.92), channel_id=1, source_target_pairs={{0,1},{1,0},{2,3},{3,2},{4,5},{5,4},{6,7},{7,6},{8,9},{9,8},{10,11... | collective-permute-start | bytes 786440 | tf_op jit(solution)/shard_map/ppermute | solution.py:271
  38.7 4.2 %collective-permute-start.6 = (bf16[2,2,64,512]{3,2,1,0:T(8,128)(2,1)S(1)}, bf16[2,2,64,512]{3,2,1,0:T(8,128)(2,1)S(1)}, u32[]{:S(2)}, u32[]{:S(2)}) collective-permute-start(bf16[2,2,64,512]{3,2,1,0:T(8,128)(2,1)S(1)} %get-tuple-element.94), channel_id=1, source_target_pairs={{0,1},{1,0},{2,3},{3,2},{4,5},{5,4},{6,7},{7,6},{8,9},{9,8},{10,11... | collective-permute-start | bytes 786440 | tf_op jit(solution)/shard_map/ppermute | solution.py:271
  41.2 6.4 %collective-permute-start.8 = (bf16[1,2,64,512]{3,2,1,0:T(8,128)(2,1)S(1)}, bf16[1,2,64,512]{3,2,1,0:T(8,128)(2,1)S(1)}, u32[]{:S(2)}, u32[]{:S(2)}) collective-permute-start(bf16[1,2,64,512]{3,2,1,0:T(8,128)(2,1)S(1)} %slice.17), channel_id=1, source_target_pairs={{0,4},{1,3},{2,6},{3,1},{4,0},{5,7},{6,2},{7,5},{8,12},{9,11},{10,... | collective-permute-start | bytes 393224 | tf_op jit(solution)/shard_map/ppermute | solution.py:282
  43.1 6.4 %collective-permute-start.7 = (bf16[2,2,64,512]{3,2,1,0:T(8,128)(2,1)S(1)}, bf16[2,2,64,512]{3,2,1,0:T(8,128)(2,1)S(1)}, u32[]{:S(2)}, u32[]{:S(2)}) collective-permute-start(bf16[2,2,64,512]{3,2,1,0:T(8,128)(2,1)S(1)} %add_convert_fusion.1), channel_id=1, source_target_pairs={{0,2},{1,5},{2,0},{3,7},{4,6},{5,1},{6,4},{7,3},{8,10},{9,13},{10,... | collective-permute-start | bytes 786440 | tf_op jit(solution)/shard_map/ppermute | solution.py:282
  47.7 7.3 %collective-permute-start.9 = (bf16[1,2,64,512]{3,2,1,0:T(8,128)(2,1)S(1)}, bf16[1,2,64,512]{3,2,1,0:T(8,128)(2,1)S(1)}, u32[]{:S(2)}, u32[]{:S(2)}) collective-permute-start(bf16[1,2,64,512]{3,2,1,0:T(8,128)(2,1)S(1)} %add_convert_fusion.9), channel_id=1, source_target_pairs={{0,8},{1,9},{2,10},{3,11},{4,12},{5,13},{6,14},{7,15},{8,0},{9,1},... | collective-permute-start | bytes 393224 | tf_op jit(solution)/shard_map/ppermute | solution.py:282
  49.6 5.9 %collective-permute-start.15 = (bf16[1,2,64,512]{3,2,1,0:T(8,128)(2,1)S(1)}, bf16[1,2,64,512]{3,2,1,0:T(8,128)(2,1)S(1)}, u32[]{:S(2)}, u32[]{:S(2)}) collective-permute-start(bf16[1,2,64,512]{3,2,1,0:T(8,128)(2,1)S(1)} %slice.19), channel_id=1, source_target_pairs={{0,4},{1,3},{2,6},{3,1},{4,0},{5,7},{6,2},{7,5},{8,12},{9,11},{10,... | collective-permute-start | bytes 393224 | tf_op jit(solution)/shard_map/ppermute | solution.py:282
  55.1 9.0 %collective-permute-start.10 = (bf16[1,2,64,512]{3,2,1,0:T(8,128)(2,1)S(1)}, bf16[1,2,64,512]{3,2,1,0:T(8,128)(2,1)S(1)}, u32[]{:S(2)}, u32[]{:S(2)}) collective-permute-start(bf16[1,2,64,512]{3,2,1,0:T(8,128)(2,1)S(1)} %add_convert_fusion.8.refs_0_), channel_id=1, source_target_pairs={{0,4},{1,3},{2,6},{3,1},{4,0},{5,7},{6,2},{7,5},{8,12},{9,11},{10,... | collective-permute-start | bytes 393224 | tf_op jit(solution)/shard_map/ppermute | solution.py:282
  55.5 9.6 %collective-permute-start.16 = (bf16[1,2,64,512]{3,2,1,0:T(8,128)(2,1)S(1)}, bf16[1,2,64,512]{3,2,1,0:T(8,128)(2,1)S(1)}, u32[]{:S(2)}, u32[]{:S(2)}) collective-permute-start(bf16[1,2,64,512]{3,2,1,0:T(8,128)(2,1)S(1)} %add_convert_fusion.7), channel_id=1, source_target_pairs={{0,8},{1,9},{2,10},{3,11},{4,12},{5,13},{6,14},{7,15},{8,0},{9,1},... | collective-permute-start | bytes 393224 | tf_op jit(solution)/shard_map/ppermute | solution.py:282
  64.1 6.4 %collective-permute-start.11 = (bf16[2,2,64,512]{3,2,1,0:T(8,128)(2,1)S(1)}, bf16[2,2,64,512]{3,2,1,0:T(8,128)(2,1)S(1)}, u32[]{:S(2)}, u32[]{:S(2)}) collective-permute-start(bf16[2,2,64,512]{3,2,1,0:T(8,128)(2,1)S(1)} %pad_maximum_fusion), channel_id=1, source_target_pairs={{0,2},{1,5},{2,0},{3,7},{4,6},{5,1},{6,4},{7,3},{8,10},{9,13},{10,... | collective-permute-start | bytes 786440 | tf_op jit(solution)/shard_map/ppermute | solution.py:282
  65.2 5.4 %collective-permute-start.18 = (bf16[1,2,64,512]{3,2,1,0:T(8,128)(2,1)S(1)}, bf16[1,2,64,512]{3,2,1,0:T(8,128)(2,1)S(1)}, u32[]{:S(2)}, u32[]{:S(2)}) collective-permute-start(bf16[1,2,64,512]{3,2,1,0:T(8,128)(2,1)S(1)} %add_convert_fusion.6.refs_0_), channel_id=1, source_target_pairs={{0,4},{1,3},{2,6},{3,1},{4,0},{5,7},{6,2},{7,5},{8,12},{9,11},{10,... | collective-permute-start | bytes 393224 | tf_op jit(solution)/shard_map/ppermute | solution.py:282
  65.3 6.9 %collective-permute-start.12 = (bf16[1,2,64,512]{3,2,1,0:T(8,128)(2,1)S(1)}, bf16[1,2,64,512]{3,2,1,0:T(8,128)(2,1)S(1)}, u32[]{:S(2)}, u32[]{:S(2)}) collective-permute-start(bf16[1,2,64,512]{3,2,1,0:T(8,128)(2,1)S(1)} %add_convert_fusion.8.refs_0_), channel_id=1, source_target_pairs={{0,1},{1,0},{2,3},{3,2},{4,5},{5,4},{6,7},{7,6},{8,9},{9,8},{10,11... | collective-permute-start | bytes 393224 | tf_op jit(solution)/shard_map/ppermute | solution.py:271
  70.5 3.0 %collective-permute-start.14 = (bf16[2,2,64,512]{3,2,1,0:T(8,128)(2,1)S(1)}, bf16[2,2,64,512]{3,2,1,0:T(8,128)(2,1)S(1)}, u32[]{:S(2)}, u32[]{:S(2)}) collective-permute-start(bf16[2,2,64,512]{3,2,1,0:T(8,128)(2,1)S(1)} %collective-permute-done.11.refs_2_), channel_id=1, source_target_pairs={{0,1},{1,0},{2,3},{3,2},{4,5},{5,4},{6,7},{7,6},{8,9},{9,8},{10,11... | collective-permute-start | bytes 786440 | tf_op jit(solution)/shard_map/ppermute | solution.py:271
  70.6 6.4 %collective-permute-start.20 = (bf16[2,2,64,512]{3,2,1,0:T(8,128)(2,1)S(1)}, bf16[2,2,64,512]{3,2,1,0:T(8,128)(2,1)S(1)}, u32[]{:S(2)}, u32[]{:S(2)}) collective-permute-start(bf16[2,2,64,512]{3,2,1,0:T(8,128)(2,1)S(1)} %pad_maximum_fusion.1), channel_id=1, source_target_pairs={{0,2},{1,5},{2,0},{3,7},{4,6},{5,1},{6,4},{7,3},{8,10},{9,13},{10,... | collective-permute-start | bytes 786440 | tf_op jit(solution)/shard_map/ppermute | solution.py:282
  71.6 1.3 %collective-permute-start.13 = (bf16[1,2,64,512]{3,2,1,0:T(8,128)(2,1)S(1)}, bf16[1,2,64,512]{3,2,1,0:T(8,128)(2,1)S(1)}, u32[]{:S(2)}, u32[]{:S(2)}) collective-permute-start(bf16[1,2,64,512]{3,2,1,0:T(8,128)(2,1)S(1)} %collective-permute-done.10.refs_1_), channel_id=1, source_target_pairs={{0,1},{1,0},{2,3},{3,2},{4,5},{5,4},{6,7},{7,6},{8,9},{9,8},{10,11... | collective-permute-start | bytes 393224 | tf_op jit(solution)/shard_map/ppermute | solution.py:271
  71.6 1.5 %collective-permute-start.17 = (bf16[1,2,64,512]{3,2,1,0:T(8,128)(2,1)S(1)}, bf16[1,2,64,512]{3,2,1,0:T(8,128)(2,1)S(1)}, u32[]{:S(2)}, u32[]{:S(2)}) collective-permute-start(bf16[1,2,64,512]{3,2,1,0:T(8,128)(2,1)S(1)} %add_convert_fusion.6.refs_0_), channel_id=1, source_target_pairs={{0,1},{1,0},{2,3},{3,2},{4,5},{5,4},{6,7},{7,6},{8,9},{9,8},{10,11... | collective-permute-start | bytes 393224 | tf_op jit(solution)/shard_map/ppermute | solution.py:271
  72.2 1.3 %collective-permute-start.19 = (bf16[1,2,64,512]{3,2,1,0:T(8,128)(2,1)S(1)}, bf16[1,2,64,512]{3,2,1,0:T(8,128)(2,1)S(1)}, u32[]{:S(2)}, u32[]{:S(2)}) collective-permute-start(bf16[1,2,64,512]{3,2,1,0:T(8,128)(2,1)S(1)} %collective-permute-done.18.refs_1_), channel_id=1, source_target_pairs={{0,1},{1,0},{2,3},{3,2},{4,5},{5,4},{6,7},{7,6},{8,9},{9,8},{10,11... | collective-permute-start | bytes 393224 | tf_op jit(solution)/shard_map/ppermute | solution.py:271
  77.0 1.5 %collective-permute-start.21 = (bf16[2,2,64,512]{3,2,1,0:T(8,128)(2,1)S(1)}, bf16[2,2,64,512]{3,2,1,0:T(8,128)(2,1)S(1)}, u32[]{:S(2)}, u32[]{:S(2)}) collective-permute-start(bf16[2,2,64,512]{3,2,1,0:T(8,128)(2,1)S(1)} %collective-permute-done.20.refs_2_), channel_id=1, source_target_pairs={{0,1},{1,0},{2,3},{3,2},{4,5},{5,4},{6,7},{7,6},{8,9},{9,8},{10,11... | collective-permute-start | bytes 786440 | tf_op jit(solution)/shard_map/ppermute | solution.py:271
  (9 other events, 78.8 us)

commit v18 on v15

--- a/solution.py
+++ b/solution.py
@@ -23,7 +23,7 @@
     return pre * sigma, sigma * (1.0 + pre * (1.0 - sigma))
 
 
-def pack_kernel(from_high, grid, out, wide):
+def pack_side(from_high, grid, out, wide):
     features, rows, cols = grid.shape
     block = wide.shape[1]
     half = block // 2
@@ -40,12 +40,23 @@
         out[:, pair * block : (pair + 1) * block] = jnp.where(lane < half, even, odd).astype(BF)
 
 
+def pack_kernel(second, grid, out, wide):
+    odd_tile = lax.axis_index("lon") & 1
+    high = odd_tile if second else 1 - odd_tile
+    for side in range(2):
+
+        @pl.when(high == side)
+        def _():
+            pack_side(side == 1, grid, out, wide)
+
+
 def weights_kernel(rows, own_blocks, src, dst, count, edge_w, cot, out_w, weights_all, grad_update, acc):
     block = edge_w.shape[1]
     half = block // 2
     windows = 2 * own_blocks + 1
-    west_base = rows * own_blocks
-    east_base = west_base + rows // 2
+    odd_tile = lax.axis_index("lon") & 1
+    west_base = rows * own_blocks + (1 - odd_tile) * (rows // 2)
+    east_base = rows * own_blocks + odd_tile * (rows // 2)
     acc[...] = jnp.zeros(acc.shape, F32)
     lane = lax.broadcasted_iota(jnp.int32, (block, block), 1)
 
@@ -114,7 +125,7 @@
     return contract(weights, hidden.astype(BF), 1, 1)
 
 
-def west_kernel(first, x, embed_t, weights_all, h_own, h_sum, slope):
+def first_kernel(first, x, embed_t, weights_all, h_own, h_sum, slope):
     points = x.shape[1]
     h_sum[...] = h_own[...] + halo_part(x, embed_t, weights_all[:, first : first + points], slope)
 
@@ -183,10 +194,10 @@
     back[...] = contract(message_w[...], grad_aggregate[...], 1, 1).astype(BF)
 
 
-def points_of(x_own, x_west, x_east):
-    tile = x_west.shape[1]
+def points_of(x_own, x_first, x_second):
+    tile = x_first.shape[1]
     pieces = []
-    for x in (x_own, x_west, x_east):
+    for x in (x_own, x_first, x_second):
         pieces += [(x, slice(k * tile, (k + 1) * tile)) for k in range(x.shape[1] // tile)]
     return [(x, at, slice(n * tile, (n + 1) * tile)) for n, (x, at) in enumerate(pieces)]
 
@@ -209,17 +220,17 @@
 
 
 def grid_kernel(
-    back, weights_all, slope_own, slope_west, slope_east, x_own, x_west, x_east, grad_gain, update, cot,
+    back, weights_all, slope_own, slope_first, slope_second, x_own, x_first, x_second, grad_gain, update, cot,
     sent_high, sent_low, grad_pre, grad_out, stack,
 ):
     perm = chunk_order()
-    for slope, at, all_at in points_of(slope_own, slope_west, slope_east):
+    for slope, at, all_at in points_of(slope_own, slope_first, slope_second):
         hidden = contract(back[...], weights_all[:, all_at], 1, 0)
         grad_pre[:, all_at] = (hidden * slope[:, at].astype(F32)).astype(BF)
     grad_out[...] = contract(update[...], cot[...], 0, 0).astype(BF)
     half = 1 - perm[0] // 4
     stack[0] = grad_out[rows_of_half(half, stack.shape[1]), :].astype(F32)
-    embed_rows(half, (x_own, x_west, x_east), grad_pre, grad_gain, stack.at[1])
+    embed_rows(half, (x_own, x_first, x_second), grad_pre, grad_gain, stack.at[1])
     to_chunks(sent_high, stack, perm, 6)
     to_chunks(sent_low, stack, perm, 4)
 
@@ -229,9 +240,9 @@
     mesh_grad[...] = cot[...].astype(F32) + grad_mesh[...]
 
 
-def grid_kept_kernel(grad_pre, x_own, x_west, x_east, grad_gain, sums):
-    perm = chunk_order()
-    embed_rows(perm[0] // 4, (x_own, x_west, x_east), grad_pre, grad_gain, sums)
+def grid_kept_kernel(grad_pre, x_own, x_first, x_second, grad_gain, sums):
+    perm = chunk_order()
+    embed_rows(perm[0] // 4, (x_own, x_first, x_second), grad_pre, grad_gain, sums)
 
 
 def kept_chunks_kernel(grad_out, sums, kept_high, kept_low):
@@ -339,16 +350,18 @@
             cost_estimate=pl.CostEstimate(flops=flops, bytes_accessed=bytes_accessed, transcendentals=0),
         )
 
-    strip = shape((features, side), BF)
+    strip_shape = shape((features, side), BF)
     wide = pltpu.VMEM((features * rows, block), F32)
     count = lax.axis_size("lon")
-    (to_east,) = call(lambda *refs: pack_kernel(True, *refs), "pack_east", [VMEM], [strip], 0, MIB, 8, [wide])(
-        grid[:, :, cols - block :]
-    )
-    x_west = lax.ppermute(to_east, "lon", [(i, (i + 1) % count) for i in range(count)])
-    to_east, later = lax.optimization_barrier((to_east, grid))
-    (to_west,) = call(lambda *refs: pack_kernel(False, *refs), "pack_west", [VMEM], [strip], 0, MIB, 8, [wide])(later)
-    x_east = lax.ppermute(to_west, "lon", [((i + 1) % count, i) for i in range(count)])
+    (strip,) = call(
+        lambda *refs: pack_kernel(False, *refs), "pack_first", [VMEM], [strip_shape], 0, MIB, 8, [wide]
+    )(grid)
+    x_first = lax.ppermute(strip, "lon", [(i, i ^ 1) for i in range(count)])
+    strip, later = lax.optimization_barrier((strip, grid))
+    (strip,) = call(
+        lambda *refs: pack_kernel(True, *refs), "pack_second", [VMEM], [strip_shape], 0, MIB, 8, [wide]
+    )(later)
+    x_second = lax.ppermute(strip, "lon", [(i, (i + 1 if i % 2 else i - 1) % count) for i in range(count)])
 
     weights_all, grad_update = call(
         lambda *refs: weights_kernel(rows, cols // block, *refs), "slot_weights", [SMEM] * 3 + [VMEM] * 3,
@@ -364,23 +377,23 @@
         2_000_000_000, 7 * MIB, 16,
     )(x_own, embed_t, weights_all)
 
-    h_sum, slope_west = call(
-        lambda *refs: west_kernel(own, *refs), "west_points", [VMEM] * 4,
+    h_sum, slope_first = call(
+        lambda *refs: first_kernel(own, *refs), "first_points", [VMEM] * 4,
         [shape((nodes, latent), F32), shape((latent, side), BF)],
         600_000_000, 3 * MIB, 16,
-    )(x_west, embed_t, weights_all, h_own)
+    )(x_first, embed_t, weights_all, h_own)
 
     quarter = shape((2, 2, latent // 8, latent), BF)
     node_rows = shape((nodes, latent), BF)
     (
-        sent_high, sent_low, grad_mesh, gain_term, gathered, grad_aggregate, normed, grad_pre_up, update, slope_east
+        sent_high, sent_low, grad_mesh, gain_term, gathered, grad_aggregate, normed, grad_pre_up, update, slope_second
     ) = call(
         mesh_kernel, "mesh_nodes", [VMEM] * 9,
         [quarter, quarter, shape((nodes, latent), F32), shape((1, latent), F32)]
         + [node_rows] * 5
         + [shape((latent, side), BF)],
         2_000_000_000, 8 * MIB, 16, [pltpu.VMEM((2, latent // 2, latent), BF)],
-    )(x_east, embed_t, weights_all, h_sum, message_w, up_w, gain.reshape(1, latent), mesh_lat, grad_update)
+    )(x_second, embed_t, weights_all, h_sum, message_w, up_w, gain.reshape(1, latent), mesh_lat, grad_update)
     got_high = core_swapped(sent_high)
     kept_high, kept_low, back = call(
         tail_kernel, "mesh_tail", [VMEM] * 5, [quarter, quarter, shape((latent, nodes), BF)],
@@ -391,13 +404,13 @@
     low_a = added(kept_low, core_swapped(sent_low))
     padded = -(-(features + 1) // 128) * 128
     assert padded == latent
-    x_parts = (x_own, x_west, x_east)
+    x_parts = (x_own, x_first, x_second)
     sent_high, sent_low, grad_pre, grad_out_term = call(
         grid_kernel, "grid_points", [VMEM] * 11,
         [quarter, quarter, shape((latent, points), BF), shape((latent, latent), BF)],
         1_600_000_000, 9 * MIB, 20, [pltpu.VMEM((2, latent // 2, latent), F32)],
     )(
-        back, weights_all, slope_own, slope_west, slope_east, *x_parts, gain_term, update, cot
+        back, weights_all, slope_own, slope_first, slope_second, *x_parts, gain_term, update, cot
     )
     got_high, got_low = core_swapped(sent_high), core_swapped(sent_low)
     (sums_b,) = call(

time: 78.8 us -> 79.2 us (level)
  starting transfers between devices: 17.9 us -> 18.7 us
    unnamed x22 -> x24, local copies, waits for them, and re-layouts: 0.07 us -> 1.59 us
    slice x1 -> x0, local copies, waits for them, and re-layouts: 1.4 us -> none  [on_device(): grid[:, :, cols - block:]]
  transfers between devices with their start and end apart: 22 -> 22, of which waited for: 14 -> 13; matrix products, arithmetic and copies ran while one was open for 1% -> 1% of each run, Pallas kernels for 22% -> 22%
where the time goes in v18:
time: 79.2 us; the launch traced here: 79 us
  waiting for transfers between devices  35.6 us (45%)
  Pallas kernels  21 us (27%)
  starting transfers between devices  18.7 us (24%)
  between operations  1.64 us (2%)
  local copies, waits for them, and re-layouts  1.61 us (2%)
    ppermute x10, waiting for transfers between devices, swapped(): return lax.ppermute(value, ('lon', 'lat'), pairs)  21.6 us
    ppermute x10, starting transfers between devices, swapped(): return lax.ppermute(value, ('lon', 'lat'), pairs)  11.6 us
    ppermute x1, waiting for transfers between devices, on_device(): lax.ppermute(strip, 'lon', [(i, (i + 1 if i % 2 else i - 1) % count) for...  11.1 us
    pallas_call x1, Pallas kernels, on_device(): call(own_kernel, 'own_points', [VMEM] * 3, [shape((nodes, latent), F32),...  3.55 us
    pallas_call x1, Pallas kernels, on_device(): call(lambda *refs: weights_kernel(rows, cols // block, *refs), 'slot_weig...  3.3 us
    ppermute x1, starting transfers between devices, on_device(): x_first = lax.ppermute(strip, 'lon', [(i, i ^ 1) for i in range(count)])  3.09 us
    ppermute x10, waiting for transfers between devices, core_swapped(): lax.ppermute(value, 'lat', [(i, i ^ 1) for i in range(lax.axis_size('lat'...  2.86 us
    ppermute x1, starting transfers between devices, on_device(): lax.ppermute(strip, 'lon', [(i, (i + 1 if i % 2 else i - 1) % count) for...  2.54 us
  transfers between devices with their start and end apart: 22, of which 13 were waited for; matrix products, arithmetic and copies ran while one was open for 1% of the time, Pallas kernels for 22%

profile of v18, /device:TPU:0, one launch (start us, length us, event | category | flops | bytes accessed | tf_op | source)
XLA Modules:
  0.0 79.0 jit_solution(8116190916567794185)
XLA Ops:
  0.6 1.5 %copy-done = bf16[8,256,474]{1,0,2:T(8,128)(2,1)S(1)} copy-done((bf16[8,256,474]{1,0,2:T(8,128)(2,1)S(1)}, bf16[8,256,474]{1,0,2:T(8,128)(2,1)}, u32[]{:S(2)}) %copy-start) | copy-done | bytes 1941528
  2.7 3.1 %collective-permute-start.1 = (bf16[474,512]{1,0:T(8,128)(2,1)S(1)}, bf16[474,512]{1,0:T(8,128)(2,1)S(1)}, u32[]{:S(2)}, u32[]{:S(2)}) collective-permute-start(bf16[474,512]{1,0:T(8,128)(2,1)S(1)} %pack_first.1), channel_id=1, source_target_pairs={{0,4},{4,0},{8,12},{12,8},{1,5},{5,1},{9,13},{13,9},{2,6},{6,2},{1... | collective-permute-start | bytes 1456136 | tf_op jit(solution)/shard_map/ppermute | solution.py:359
  6.3 2.5 %collective-permute-start = (bf16[474,512]{1,0:T(8,128)(2,1)S(1)}, bf16[474,512]{1,0:T(8,128)(2,1)S(1)}, u32[]{:S(2)}, u32[]{:S(2)}) collective-permute-start(bf16[474,512]{1,0:T(8,128)(2,1)S(1)} %pack_second.1), channel_id=1, source_target_pairs={{0,12},{4,8},{8,4},{12,0},{1,13},{5,9},{9,5},{13,1},{2,14},{6,10},... | collective-permute-start | bytes 1456136 | tf_op jit(solution)/shard_map/ppermute | solution.py:364
  9.6 3.3 %slot_weights.1 = (bf16[256,3072]{1,0:T(8,128)(2,1)S(1)}, f32[256,512]{1,0:T(8,128)S(1)}) custom-call(s32[32]{0:T(128)S(1)} %copy-done.6, s32[32]{0:T(128)S(1)} %copy-done.7, s32[1]{0:T(128)S(6)} %copy.23.refs_2_, bf16[32,128,128]{2,1,0:T(8,128)(2,1)S(1)} %copy-done.4, bf16[256,512]{1,0:T(8,128)(2,1)S(1)} %copy-done.2, bf16[512,512]{1,0:T(8,128)(2,1)S(1)} %copy-done.3), custom_call_target="tpu_custom_call" | custom-call | flops 200000000 | bytes 4194304 | tf_op jit(solution)/shard_map/slot_weights/pallas_call | solution.py:366
  12.9 1.3 %own_rows.1 = (bf16[474,2048]{1,0:T(8,128)(2,1)S(1)}, bf16[512,474]{1,0:T(8,128)(2,1)S(1)}) custom-call(bf16[474,8,256]{2,1,0:T(8,128)(2,1)S(1)} %bitcast.5, bf16[474,512]{1,0:T(8,128)(2,1)S(1)} %copy-done.10), custom_call_target="tpu_custom_call" | custom-call | flops 1000000000 | bytes 5242880 | tf_op jit(solution)/shard_map/own_rows/pallas_call | solution.py:371
  14.3 3.6 %own_points.1 = (f32[256,512]{1,0:T(8,128)S(1)}, bf16[512,2048]{1,0:T(8,128)(2,1)S(1)}) custom-call(bf16[474,2048]{1,0:T(8,128)(2,1)S(1)} %get-tuple-element.69.x_t.x_own, bf16[512,474]{1,0:T(8,128)(2,1)S(1)} %get-tuple-element.67.embed_t.refs_1_, bf16[256,3072]{1,0:T(8,128)(2,1)S(1)} %get-tuple-element.68.weights_all.refs_2_), custom_call_target="tpu_custom_call" | custom-call | flops 2000000000 | bytes 7340032 | tf_op jit(solution)/shard_map/own_points/pallas_call | solution.py:375
  18.8 11.1 %collective-permute-done.x.x_second = bf16[474,512]{1,0:T(8,128)(2,1)S(1)} collective-permute-done((bf16[474,512]{1,0:T(8,128)(2,1)S(1)}, bf16[474,512]{1,0:T(8,128)(2,1)S(1)}, u32[]{:S(2)}, u32[]{:S(2)}) %collective-permute-start) | collective-permute-done | bytes 485408 | tf_op jit(solution)/shard_map/ppermute | solution.py:364
  29.9 2.1 %mesh_nodes.1 = (bf16[2,2,64,512]{3,2,1,0:T(8,128)(2,1)S(1)}, bf16[2,2,64,512]{3,2,1,0:T(8,128)(2,1)S(1)}, f32[256,512]{1,0:T(8,128)S(1)}, f32[1,512]{1,0:T(1,12...) custom-call(bf16[474,512]{1,0:T(8,128)(2,1)S(1)} %collective-permute, ...), custom_call_target="tpu_custom_call" | custom-call | flops 2000000000 | bytes 8388608 | tf_op jit(solution)/shard_map/mesh_nodes/pallas_call | solution.py:390
  33.9 1.5 %collective-permute-start.4 = (bf16[2,2,64,512]{3,2,1,0:T(8,128)(2,1)S(1)}, bf16[2,2,64,512]{3,2,1,0:T(8,128)(2,1)S(1)}, u32[]{:S(2)}, u32[]{:S(2)}) collective-permute-start(bf16[2,2,64,512]{3,2,1,0:T(8,128)(2,1)S(1)} %add_convert_fusion.5), channel_id=1, source_target_pairs={{0,2},{1,5},{2,0},{3,7},{4,6},{5,1},{6,4},{7,3},{8,10},{9,13},{10,... | collective-permute-start | bytes 786440 | tf_op jit(solution)/shard_map/ppermute | solution.py:296
  35.4 2.5 %grid_points.1 = (bf16[2,2,64,512]{3,2,1,0:T(8,128)(2,1)S(1)}, bf16[2,2,64,512]{3,2,1,0:T(8,128)(2,1)S(1)}, bf16[512,3072]{1,0:T(8,128)(2,1)S(1)}, bf16[512,512]{1,0:T(8,128)(2,1)S(1)}) custom-call(bf16[512,256]{1,0:T(8,128)(2,1)S(1)} %get-tuple-element.81.back, bf16[256,3072]{1,0:T(8,128)(2,1)S(1)} %get-tuple-element.68.weights_all.refs_2_, ...), custom_call_target="tpu_custom_call" | custom-call | flops 1600000000 | bytes 9437184 | tf_op jit(solution)/shard_map/grid_points/pallas_call | solution.py:408
  40.4 1.2 %collective-permute-start.8 = (bf16[1,2,64,512]{3,2,1,0:T(8,128)(2,1)S(1)}, bf16[1,2,64,512]{3,2,1,0:T(8,128)(2,1)S(1)}, u32[]{:S(2)}, u32[]{:S(2)}) collective-permute-start(bf16[1,2,64,512]{3,2,1,0:T(8,128)(2,1)S(1)} %slice.13), channel_id=1, source_target_pairs={{0,4},{1,3},{2,6},{3,1},{4,0},{5,7},{6,2},{7,5},{8,12},{9,11},{10,... | collective-permute-start | bytes 393224 | tf_op jit(solution)/shard_map/ppermute | solution.py:296
  41.7 1.5 %collective-permute-start.7 = (bf16[2,2,64,512]{3,2,1,0:T(8,128)(2,1)S(1)}, bf16[2,2,64,512]{3,2,1,0:T(8,128)(2,1)S(1)}, u32[]{:S(2)}, u32[]{:S(2)}) collective-permute-start(bf16[2,2,64,512]{3,2,1,0:T(8,128)(2,1)S(1)} %add_convert_fusion.1), channel_id=1, source_target_pairs={{0,2},{1,5},{2,0},{3,7},{4,6},{5,1},{6,4},{7,3},{8,10},{9,13},{10,... | collective-permute-start | bytes 786440 | tf_op jit(solution)/shard_map/ppermute | solution.py:296
  43.3 1.2 %mesh_outputs.1 = (bf16[256,512]{1,0:T(8,128)(2,1)}, f32[256,512]{1,0:T(8,128)}) custom-call(bf16[256,512]{1,0:T(8,128)(2,1)S(1)} %get-tuple-element.98.update, bf16[512,512]{1,0:T(8,128)(2,1)S(1)} %copy-done.3, bf16[256,512]{1,0:T(8,128)(2,1)S(1)} %copy-done.5, bf16[256,512]{1,0:T(8,128)(2,1)S(1)} %copy-done.2, f32[256,512]{1,0:T(8,128)S(1)} %get-tuple-element.99.grad_mesh), custom_call_target="tpu_custom_call" | custom-call | flops 200000000 | bytes 3145728 | tf_op jit(solution)/shard_map/mesh_outputs/pallas_call | solution.py:426
  44.5 2.3 %collective-permute-done.8 = bf16[1,2,64,512]{3,2,1,0:T(8,128)(2,1)S(1)} collective-permute-done((bf16[1,2,64,512]{3,2,1,0:T(8,128)(2,1)S(1)}, bf16[1,2,64,512]{3,2,1,0:T(8,128)(2,1)S(1)}, u32[]{:S(2)}, u32[]{:S(2)}) %collective-permute-start.8) | collective-permute-done | bytes 131104 | tf_op jit(solution)/shard_map/ppermute | solution.py:296
  46.9 2.4 %collective-permute-start.9 = (bf16[1,2,64,512]{3,2,1,0:T(8,128)(2,1)S(1)}, bf16[1,2,64,512]{3,2,1,0:T(8,128)(2,1)S(1)}, u32[]{:S(2)}, u32[]{:S(2)}) collective-permute-start(bf16[1,2,64,512]{3,2,1,0:T(8,128)(2,1)S(1)} %add_convert_fusion.9), channel_id=1, source_target_pairs={{0,8},{1,9},{2,10},{3,11},{4,12},{5,13},{6,14},{7,15},{8,0},{9,1},... | collective-permute-start | bytes 393224 | tf_op jit(solution)/shard_map/ppermute | solution.py:296
  50.1 4.2 %collective-permute-done.9 = bf16[1,2,64,512]{3,2,1,0:T(8,128)(2,1)S(1)} collective-permute-done((bf16[1,2,64,512]{3,2,1,0:T(8,128)(2,1)S(1)}, bf16[1,2,64,512]{3,2,1,0:T(8,128)(2,1)S(1)}, u32[]{:S(2)}, u32[]{:S(2)}) %collective-permute-start.9) | collective-permute-done | bytes 131104 | tf_op jit(solution)/shard_map/ppermute | solution.py:296
  55.2 2.2 %collective-permute-start.16 = (bf16[1,2,64,512]{3,2,1,0:T(8,128)(2,1)S(1)}, bf16[1,2,64,512]{3,2,1,0:T(8,128)(2,1)S(1)}, u32[]{:S(2)}, u32[]{:S(2)}) collective-permute-start(bf16[1,2,64,512]{3,2,1,0:T(8,128)(2,1)S(1)} %add_convert_fusion.7), channel_id=1, source_target_pairs={{0,8},{1,9},{2,10},{3,11},{4,12},{5,13},{6,14},{7,15},{8,0},{9,1},... | collective-permute-start | bytes 393224 | tf_op jit(solution)/shard_map/ppermute | solution.py:296
  57.3 6.2 %collective-permute-done.10.refs_1_ = bf16[1,2,64,512]{3,2,1,0:T(8,128)(2,1)S(1)} collective-permute-done((bf16[1,2,64,512]{3,2,1,0:T(8,128)(2,1)S(1)}, bf16[1,2,64,512]{3,2,1,0:T(8,128)(2,1)S(1)}, u32[]{:S(2)}, u32[]{:S(2)}) %collective-permute-start.10) | collective-permute-done | bytes 131104 | tf_op jit(solution)/shard_map/ppermute | solution.py:296
  63.5 1.0 %collective-permute-start.11 = (bf16[2,2,64,512]{3,2,1,0:T(8,128)(2,1)S(1)}, bf16[2,2,64,512]{3,2,1,0:T(8,128)(2,1)S(1)}, u32[]{:S(2)}, u32[]{:S(2)}) collective-permute-start(bf16[2,2,64,512]{3,2,1,0:T(8,128)(2,1)S(1)} %pad_maximum_fusion), channel_id=1, source_target_pairs={{0,2},{1,5},{2,0},{3,7},{4,6},{5,1},{6,4},{7,3},{8,10},{9,13},{10,... | collective-permute-start | bytes 786440 | tf_op jit(solution)/shard_map/ppermute | solution.py:296
  64.8 5.2 %collective-permute-done.11.refs_2_ = bf16[2,2,64,512]{3,2,1,0:T(8,128)(2,1)S(1)} collective-permute-done((bf16[2,2,64,512]{3,2,1,0:T(8,128)(2,1)S(1)}, bf16[2,2,64,512]{3,2,1,0:T(8,128)(2,1)S(1)}, u32[]{:S(2)}, u32[]{:S(2)}) %collective-permute-start.11) | collective-permute-done | bytes 262176 | tf_op jit(solution)/shard_map/ppermute | solution.py:296
  70.0 1.0 %collective-permute-start.20 = (bf16[2,2,64,512]{3,2,1,0:T(8,128)(2,1)S(1)}, bf16[2,2,64,512]{3,2,1,0:T(8,128)(2,1)S(1)}, u32[]{:S(2)}, u32[]{:S(2)}) collective-permute-start(bf16[2,2,64,512]{3,2,1,0:T(8,128)(2,1)S(1)} %pad_maximum_fusion.1), channel_id=1, source_target_pairs={{0,2},{1,5},{2,0},{3,7},{4,6},{5,1},{6,4},{7,3},{8,10},{9,13},{10,... | collective-permute-start | bytes 786440 | tf_op jit(solution)/shard_map/ppermute | solution.py:296
  72.9 1.5 %order_a.1 = (f32[512,512]{1,0:T(8,128)}, f32[512,512]{1,0:T(8,128)}) custom-call(bf16[1,2,64,512]{3,2,1,0:T(8,128)(2,1)S(1)} %add_convert_fusion.8.refs_0_, bf16[1,2,64,512]{3,2,1,0:T(8,128)(2,1)S(1)} %collective-permute-done.10.refs_1_, bf16[2,2,64,512]{3,2,1,0:T(8,128)(2,1)S(1)} %collective-permute-done.11.refs_2_, ...), custom_call_target="tpu_custom_call" | custom-call | bytes 3145728 | tf_op jit(solution)/shard_map/order_a/pallas_call | solution.py:436
  74.4 2.1 %collective-permute-done.20.refs_2_ = bf16[2,2,64,512]{3,2,1,0:T(8,128)(2,1)S(1)} collective-permute-done((bf16[2,2,64,512]{3,2,1,0:T(8,128)(2,1)S(1)}, bf16[2,2,64,512]{3,2,1,0:T(8,128)(2,1)S(1)}, u32[]{:S(2)}, u32[]{:S(2)}) %collective-permute-start.20) | collective-permute-done | bytes 262176 | tf_op jit(solution)/shard_map/ppermute | solution.py:296
  76.5 1.0 %order_b.2 = (f32[512,512]{1,0:T(8,128)}, f32[474,512]{1,0:T(8,128)}, f32[1,512]{1,0:T(1,128)S(1)}) custom-call(bf16[1,2,64,512]{3,2,1,0:T(8,128)(2,1)S(1)} %add_convert_fusion.6.refs_0_, bf16[1,2,64,512]{3,2,1,0:T(8,128)(2,1)S(1)} %collective-permute-done.18.refs_1_, bf16[2,2,64,512]{3,2,1,0:T(8,128)(2,1)S(1)} %collective-permute-done.20.refs_2_), custom_call_target="tpu_custom_call" | custom-call | bytes 2097152 | tf_op jit(solution)/shard_map/order_b/pallas_call | solution.py:447
  (71 shorter events, 11.7 us)
Async XLA Ops:
  2.7 15.1 %collective-permute-start.1 = (bf16[474,512]{1,0:T(8,128)(2,1)S(1)}, bf16[474,512]{1,0:T(8,128)(2,1)S(1)}, u32[]{:S(2)}, u32[]{:S(2)}) collective-permute-start(bf16[474,512]{1,0:T(8,128)(2,1)S(1)} %pack_first.1), channel_id=1, source_target_pairs={{0,4},{4,0},{8,12},{12,8},{1,5},{5,1},{9,13},{13,9},{2,6},{6,2},{1... | collective-permute-start | bytes 1456136 | tf_op jit(solution)/shard_map/ppermute | solution.py:359
  6.3 23.5 %collective-permute-start = (bf16[474,512]{1,0:T(8,128)(2,1)S(1)}, bf16[474,512]{1,0:T(8,128)(2,1)S(1)}, u32[]{:S(2)}, u32[]{:S(2)}) collective-permute-start(bf16[474,512]{1,0:T(8,128)(2,1)S(1)} %pack_second.1), channel_id=1, source_target_pairs={{0,12},{4,8},{8,4},{12,0},{1,13},{5,9},{9,5},{13,1},{2,14},{6,10},... | collective-permute-start | bytes 1456136 | tf_op jit(solution)/shard_map/ppermute | solution.py:364
  17.8 12.1 %copy-start.5 = (bf16[256,512]{1,0:T(8,128)(2,1)S(1)}, bf16[256,512]{1,0:T(8,128)(2,1)}, u32[]{:S(2)}) copy-start(bf16[256,512]{1,0:T(8,128)(2,1)} %mesh_lat.3) | copy-start | bytes 786436
  17.8 12.1 %copy-start.8 = (bf16[512,512]{1,0:T(8,128)(2,1)S(1)}, bf16[512,512]{1,0:T(8,128)(2,1)}, u32[]{:S(2)}) copy-start(bf16[512,512]{1,0:T(8,128)(2,1)} %up_w.1) | copy-start | bytes 1572868
  32.0 1.6 %collective-permute-start.2 = (bf16[2,2,64,512]{3,2,1,0:T(8,128)(2,1)S(1)}, bf16[2,2,64,512]{3,2,1,0:T(8,128)(2,1)S(1)}, u32[]{:S(2)}, u32[]{:S(2)}) collective-permute-start(bf16[2,2,64,512]{3,2,1,0:T(8,128)(2,1)S(1)} %get-tuple-element.78), channel_id=1, source_target_pairs={{0,1},{1,0},{2,3},{3,2},{4,5},{5,4},{6,7},{7,6},{8,9},{9,8},{10,11... | collective-permute-start | bytes 786440 | tf_op jit(solution)/shard_map/ppermute | solution.py:285
  33.7 5.8 %collective-permute-start.3 = (bf16[2,2,64,512]{3,2,1,0:T(8,128)(2,1)S(1)}, bf16[2,2,64,512]{3,2,1,0:T(8,128)(2,1)S(1)}, u32[]{:S(2)}, u32[]{:S(2)}) collective-permute-start(bf16[2,2,64,512]{3,2,1,0:T(8,128)(2,1)S(1)} %get-tuple-element.89), channel_id=1, source_target_pairs={{0,1},{1,0},{2,3},{3,2},{4,5},{5,4},{6,7},{7,6},{8,9},{9,8},{10,11... | collective-permute-start | bytes 786440 | tf_op jit(solution)/shard_map/ppermute | solution.py:285
  33.9 6.4 %collective-permute-start.4 = (bf16[2,2,64,512]{3,2,1,0:T(8,128)(2,1)S(1)}, bf16[2,2,64,512]{3,2,1,0:T(8,128)(2,1)S(1)}, u32[]{:S(2)}, u32[]{:S(2)}) collective-permute-start(bf16[2,2,64,512]{3,2,1,0:T(8,128)(2,1)S(1)} %add_convert_fusion.5), channel_id=1, source_target_pairs={{0,2},{1,5},{2,0},{3,7},{4,6},{5,1},{6,4},{7,3},{8,10},{9,13},{10,... | collective-permute-start | bytes 786440 | tf_op jit(solution)/shard_map/ppermute | solution.py:296
  37.9 11.4 %collective-permute-start.5 = (bf16[2,2,64,512]{3,2,1,0:T(8,128)(2,1)S(1)}, bf16[2,2,64,512]{3,2,1,0:T(8,128)(2,1)S(1)}, u32[]{:S(2)}, u32[]{:S(2)}) collective-permute-start(bf16[2,2,64,512]{3,2,1,0:T(8,128)(2,1)S(1)} %get-tuple-element.94), channel_id=1, source_target_pairs={{0,1},{1,0},{2,3},{3,2},{4,5},{5,4},{6,7},{7,6},{8,9},{9,8},{10,11... | collective-permute-start | bytes 786440 | tf_op jit(solution)/shard_map/ppermute | solution.py:285
  37.9 3.7 %collective-permute-start.6 = (bf16[2,2,64,512]{3,2,1,0:T(8,128)(2,1)S(1)}, bf16[2,2,64,512]{3,2,1,0:T(8,128)(2,1)S(1)}, u32[]{:S(2)}, u32[]{:S(2)}) collective-permute-start(bf16[2,2,64,512]{3,2,1,0:T(8,128)(2,1)S(1)} %get-tuple-element.96), channel_id=1, source_target_pairs={{0,1},{1,0},{2,3},{3,2},{4,5},{5,4},{6,7},{7,6},{8,9},{9,8},{10,11... | collective-permute-start | bytes 786440 | tf_op jit(solution)/shard_map/ppermute | solution.py:285
  40.4 6.4 %collective-permute-start.8 = (bf16[1,2,64,512]{3,2,1,0:T(8,128)(2,1)S(1)}, bf16[1,2,64,512]{3,2,1,0:T(8,128)(2,1)S(1)}, u32[]{:S(2)}, u32[]{:S(2)}) collective-permute-start(bf16[1,2,64,512]{3,2,1,0:T(8,128)(2,1)S(1)} %slice.13), channel_id=1, source_target_pairs={{0,4},{1,3},{2,6},{3,1},{4,0},{5,7},{6,2},{7,5},{8,12},{9,11},{10,... | collective-permute-start | bytes 393224 | tf_op jit(solution)/shard_map/ppermute | solution.py:296
  41.7 7.5 %collective-permute-start.7 = (bf16[2,2,64,512]{3,2,1,0:T(8,128)(2,1)S(1)}, bf16[2,2,64,512]{3,2,1,0:T(8,128)(2,1)S(1)}, u32[]{:S(2)}, u32[]{:S(2)}) collective-permute-start(bf16[2,2,64,512]{3,2,1,0:T(8,128)(2,1)S(1)} %add_convert_fusion.1), channel_id=1, source_target_pairs={{0,2},{1,5},{2,0},{3,7},{4,6},{5,1},{6,4},{7,3},{8,10},{9,13},{10,... | collective-permute-start | bytes 786440 | tf_op jit(solution)/shard_map/ppermute | solution.py:296
  46.9 7.4 %collective-permute-start.9 = (bf16[1,2,64,512]{3,2,1,0:T(8,128)(2,1)S(1)}, bf16[1,2,64,512]{3,2,1,0:T(8,128)(2,1)S(1)}, u32[]{:S(2)}, u32[]{:S(2)}) collective-permute-start(bf16[1,2,64,512]{3,2,1,0:T(8,128)(2,1)S(1)} %add_convert_fusion.9), channel_id=1, source_target_pairs={{0,8},{1,9},{2,10},{3,11},{4,12},{5,13},{6,14},{7,15},{8,0},{9,1},... | collective-permute-start | bytes 393224 | tf_op jit(solution)/shard_map/ppermute | solution.py:296
  49.4 5.7 %collective-permute-start.15 = (bf16[1,2,64,512]{3,2,1,0:T(8,128)(2,1)S(1)}, bf16[1,2,64,512]{3,2,1,0:T(8,128)(2,1)S(1)}, u32[]{:S(2)}, u32[]{:S(2)}) collective-permute-start(bf16[1,2,64,512]{3,2,1,0:T(8,128)(2,1)S(1)} %slice.15), channel_id=1, source_target_pairs={{0,4},{1,3},{2,6},{3,1},{4,0},{5,7},{6,2},{7,5},{8,12},{9,11},{10,... | collective-permute-start | bytes 393224 | tf_op jit(solution)/shard_map/ppermute | solution.py:296
  54.3 9.2 %collective-permute-start.10 = (bf16[1,2,64,512]{3,2,1,0:T(8,128)(2,1)S(1)}, bf16[1,2,64,512]{3,2,1,0:T(8,128)(2,1)S(1)}, u32[]{:S(2)}, u32[]{:S(2)}) collective-permute-start(bf16[1,2,64,512]{3,2,1,0:T(8,128)(2,1)S(1)} %add_convert_fusion.8.refs_0_), channel_id=1, source_target_pairs={{0,4},{1,3},{2,6},{3,1},{4,0},{5,7},{6,2},{7,5},{8,12},{9,11},{10,... | collective-permute-start | bytes 393224 | tf_op jit(solution)/shard_map/ppermute | solution.py:296
  55.2 9.4 %collective-permute-start.16 = (bf16[1,2,64,512]{3,2,1,0:T(8,128)(2,1)S(1)}, bf16[1,2,64,512]{3,2,1,0:T(8,128)(2,1)S(1)}, u32[]{:S(2)}, u32[]{:S(2)}) collective-permute-start(bf16[1,2,64,512]{3,2,1,0:T(8,128)(2,1)S(1)} %add_convert_fusion.7), channel_id=1, source_target_pairs={{0,8},{1,9},{2,10},{3,11},{4,12},{5,13},{6,14},{7,15},{8,0},{9,1},... | collective-permute-start | bytes 393224 | tf_op jit(solution)/shard_map/ppermute | solution.py:296
  63.5 6.4 %collective-permute-start.11 = (bf16[2,2,64,512]{3,2,1,0:T(8,128)(2,1)S(1)}, bf16[2,2,64,512]{3,2,1,0:T(8,128)(2,1)S(1)}, u32[]{:S(2)}, u32[]{:S(2)}) collective-permute-start(bf16[2,2,64,512]{3,2,1,0:T(8,128)(2,1)S(1)} %pad_maximum_fusion), channel_id=1, source_target_pairs={{0,2},{1,5},{2,0},{3,7},{4,6},{5,1},{6,4},{7,3},{8,10},{9,13},{10,... | collective-permute-start | bytes 786440 | tf_op jit(solution)/shard_map/ppermute | solution.py:296
  64.6 5.4 %collective-permute-start.18 = (bf16[1,2,64,512]{3,2,1,0:T(8,128)(2,1)S(1)}, bf16[1,2,64,512]{3,2,1,0:T(8,128)(2,1)S(1)}, u32[]{:S(2)}, u32[]{:S(2)}) collective-permute-start(bf16[1,2,64,512]{3,2,1,0:T(8,128)(2,1)S(1)} %add_convert_fusion.6.refs_0_), channel_id=1, source_target_pairs={{0,4},{1,3},{2,6},{3,1},{4,0},{5,7},{6,2},{7,5},{8,12},{9,11},{10,... | collective-permute-start | bytes 393224 | tf_op jit(solution)/shard_map/ppermute | solution.py:296
  64.7 6.9 %collective-permute-start.12 = (bf16[1,2,64,512]{3,2,1,0:T(8,128)(2,1)S(1)}, bf16[1,2,64,512]{3,2,1,0:T(8,128)(2,1)S(1)}, u32[]{:S(2)}, u32[]{:S(2)}) collective-permute-start(bf16[1,2,64,512]{3,2,1,0:T(8,128)(2,1)S(1)} %add_convert_fusion.8.refs_0_), channel_id=1, source_target_pairs={{0,1},{1,0},{2,3},{3,2},{4,5},{5,4},{6,7},{7,6},{8,9},{9,8},{10,11... | collective-permute-start | bytes 393224 | tf_op jit(solution)/shard_map/ppermute | solution.py:285
  70.0 2.9 %collective-permute-start.14 = (bf16[2,2,64,512]{3,2,1,0:T(8,128)(2,1)S(1)}, bf16[2,2,64,512]{3,2,1,0:T(8,128)(2,1)S(1)}, u32[]{:S(2)}, u32[]{:S(2)}) collective-permute-start(bf16[2,2,64,512]{3,2,1,0:T(8,128)(2,1)S(1)} %collective-permute-done.11.refs_2_), channel_id=1, source_target_pairs={{0,1},{1,0},{2,3},{3,2},{4,5},{5,4},{6,7},{7,6},{8,9},{9,8},{10,11... | collective-permute-start | bytes 786440 | tf_op jit(solution)/shard_map/ppermute | solution.py:285
  70.0 6.4 %collective-permute-start.20 = (bf16[2,2,64,512]{3,2,1,0:T(8,128)(2,1)S(1)}, bf16[2,2,64,512]{3,2,1,0:T(8,128)(2,1)S(1)}, u32[]{:S(2)}, u32[]{:S(2)}) collective-permute-start(bf16[2,2,64,512]{3,2,1,0:T(8,128)(2,1)S(1)} %pad_maximum_fusion.1), channel_id=1, source_target_pairs={{0,2},{1,5},{2,0},{3,7},{4,6},{5,1},{6,4},{7,3},{8,10},{9,13},{10,... | collective-permute-start | bytes 786440 | tf_op jit(solution)/shard_map/ppermute | solution.py:296
  71.0 1.3 %collective-permute-start.13 = (bf16[1,2,64,512]{3,2,1,0:T(8,128)(2,1)S(1)}, bf16[1,2,64,512]{3,2,1,0:T(8,128)(2,1)S(1)}, u32[]{:S(2)}, u32[]{:S(2)}) collective-permute-start(bf16[1,2,64,512]{3,2,1,0:T(8,128)(2,1)S(1)} %collective-permute-done.10.refs_1_), channel_id=1, source_target_pairs={{0,1},{1,0},{2,3},{3,2},{4,5},{5,4},{6,7},{7,6},{8,9},{9,8},{10,11... | collective-permute-start | bytes 393224 | tf_op jit(solution)/shard_map/ppermute | solution.py:285
  71.0 1.5 %collective-permute-start.17 = (bf16[1,2,64,512]{3,2,1,0:T(8,128)(2,1)S(1)}, bf16[1,2,64,512]{3,2,1,0:T(8,128)(2,1)S(1)}, u32[]{:S(2)}, u32[]{:S(2)}) collective-permute-start(bf16[1,2,64,512]{3,2,1,0:T(8,128)(2,1)S(1)} %add_convert_fusion.6.refs_0_), channel_id=1, source_target_pairs={{0,1},{1,0},{2,3},{3,2},{4,5},{5,4},{6,7},{7,6},{8,9},{9,8},{10,11... | collective-permute-start | bytes 393224 | tf_op jit(solution)/shard_map/ppermute | solution.py:285
  71.6 1.3 %collective-permute-start.19 = (bf16[1,2,64,512]{3,2,1,0:T(8,128)(2,1)S(1)}, bf16[1,2,64,512]{3,2,1,0:T(8,128)(2,1)S(1)}, u32[]{:S(2)}, u32[]{:S(2)}) collective-permute-start(bf16[1,2,64,512]{3,2,1,0:T(8,128)(2,1)S(1)} %collective-permute-done.18.refs_1_), channel_id=1, source_target_pairs={{0,1},{1,0},{2,3},{3,2},{4,5},{5,4},{6,7},{7,6},{8,9},{9,8},{10,11... | collective-permute-start | bytes 393224 | tf_op jit(solution)/shard_map/ppermute | solution.py:285
  76.5 1.5 %collective-permute-start.21 = (bf16[2,2,64,512]{3,2,1,0:T(8,128)(2,1)S(1)}, bf16[2,2,64,512]{3,2,1,0:T(8,128)(2,1)S(1)}, u32[]{:S(2)}, u32[]{:S(2)}) collective-permute-start(bf16[2,2,64,512]{3,2,1,0:T(8,128)(2,1)S(1)} %collective-permute-done.20.refs_2_), channel_id=1, source_target_pairs={{0,1},{1,0},{2,3},{3,2},{4,5},{5,4},{6,7},{7,6},{8,9},{9,8},{10,11... | collective-permute-start | bytes 786440 | tf_op jit(solution)/shard_map/ppermute | solution.py:285
  (10 other events, 82.9 us)

commit v19 on v18

--- a/solution.py
+++ b/solution.py
@@ -42,7 +42,7 @@
 
 def pack_kernel(second, grid, out, wide):
     odd_tile = lax.axis_index("lon") & 1
-    high = odd_tile if second else 1 - odd_tile
+    high = 1 - odd_tile if second else odd_tile
     for side in range(2):
 
         @pl.when(high == side)
@@ -55,8 +55,8 @@
     half = block // 2
     windows = 2 * own_blocks + 1
     odd_tile = lax.axis_index("lon") & 1
-    west_base = rows * own_blocks + (1 - odd_tile) * (rows // 2)
-    east_base = rows * own_blocks + odd_tile * (rows // 2)
+    west_base = rows * own_blocks + odd_tile * (rows // 2)
+    east_base = rows * own_blocks + (1 - odd_tile) * (rows // 2)
     acc[...] = jnp.zeros(acc.shape, F32)
     lane = lax.broadcasted_iota(jnp.int32, (block, block), 1)
 
@@ -356,12 +356,12 @@
     (strip,) = call(
         lambda *refs: pack_kernel(False, *refs), "pack_first", [VMEM], [strip_shape], 0, MIB, 8, [wide]
     )(grid)
-    x_first = lax.ppermute(strip, "lon", [(i, i ^ 1) for i in range(count)])
+    x_first = lax.ppermute(strip, "lon", [(i, (i + 1 if i % 2 else i - 1) % count) for i in range(count)])
     strip, later = lax.optimization_barrier((strip, grid))
     (strip,) = call(
         lambda *refs: pack_kernel(True, *refs), "pack_second", [VMEM], [strip_shape], 0, MIB, 8, [wide]
     )(later)
-    x_second = lax.ppermute(strip, "lon", [(i, (i + 1 if i % 2 else i - 1) % count) for i in range(count)])
+    x_second = lax.ppermute(strip, "lon", [(i, i ^ 1) for i in range(count)])
 
     weights_all, grad_update = call(
         lambda *refs: weights_kernel(rows, cols // block, *refs), "slot_weights", [SMEM] * 3 + [VMEM] * 3,

time: 79.2 us -> 78.9 us (level)
  starting transfers between devices: 18.7 us -> 19.8 us
  waiting for transfers between devices: 35.6 us -> 34.7 us
    ppermute x1, waiting for transfers between devices: 0.01 us -> 8.83 us  [on_device(): x_second = lax.ppermute(strip, 'lon', [(i, i ^ 1) for i in range(count)])]
    ppermute x1, waiting for transfers between devices: 11.1 us -> 3.01 us  [on_device(): lax.ppermute(strip, 'lon', [(i, (i + 1 if i % 2 else i - 1) % count) for...]
    ppermute x1, starting transfers between devices: 3.09 us -> 0.07 us  [on_device(): x_second = lax.ppermute(strip, 'lon', [(i, i ^ 1) for i in range(count)])]
    ppermute x1, starting transfers between devices: 2.54 us -> 5.11 us  [on_device(): lax.ppermute(strip, 'lon', [(i, (i + 1 if i % 2 else i - 1) % count) for...]
    ppermute x10, waiting for transfers between devices: 21.6 us -> 20 us  [swapped(): return lax.ppermute(value, ('lon', 'lat'), pairs)]
    ppermute x10, starting transfers between devices: 11.6 us -> 13.2 us  [swapped(): return lax.ppermute(value, ('lon', 'lat'), pairs)]
  transfers between devices with their start and end apart: 22 -> 22, of which waited for: 13 -> 14; matrix products, arithmetic and copies ran while one was open for 1% -> 1% of each run, Pallas kernels for 22% -> 21%
where the time goes in v19:
time: 78.9 us; the launch traced here: 78.7 us
  waiting for transfers between devices  34.7 us (44%)
  Pallas kernels  20.5 us (26%)
  starting transfers between devices  19.8 us (25%)
  local copies, waits for them, and re-layouts  1.61 us (2%)
  between operations  1.61 us (2%)
    ppermute x10, waiting for transfers between devices, swapped(): return lax.ppermute(value, ('lon', 'lat'), pairs)  20 us
    ppermute x10, starting transfers between devices, swapped(): return lax.ppermute(value, ('lon', 'lat'), pairs)  13.2 us
    ppermute x1, waiting for transfers between devices, on_device(): x_second = lax.ppermute(strip, 'lon', [(i, i ^ 1) for i in range(count)])  8.83 us
    ppermute x1, starting transfers between devices, on_device(): lax.ppermute(strip, 'lon', [(i, (i + 1 if i % 2 else i - 1) % count) for...  5.11 us
    pallas_call x1, Pallas kernels, on_device(): call(own_kernel, 'own_points', [VMEM] * 3, [shape((nodes, latent), F32),...  3.55 us
    ppermute x1, waiting for transfers between devices, on_device(): lax.ppermute(strip, 'lon', [(i, (i + 1 if i % 2 else i - 1) % count) for...  3.01 us
    pallas_call x1, Pallas kernels, on_device(): call(lambda *refs: weights_kernel(rows, cols // block, *refs), 'slot_weig...  2.87 us
    ppermute x10, waiting for transfers between devices, core_swapped(): lax.ppermute(value, 'lat', [(i, i ^ 1) for i in range(lax.axis_size('lat'...  2.86 us
  transfers between devices with their start and end apart: 22, of which 14 were waited for; matrix products, arithmetic and copies ran while one was open for 1% of the time, Pallas kernels for 21%

profile of v19, /device:TPU:0, one launch (start us, length us, event | category | flops | bytes accessed | tf_op | source)
XLA Modules:
  0.0 78.7 jit_solution(17890924543312579227)
XLA Ops:
  0.6 1.5 %copy-done = bf16[8,256,474]{1,0,2:T(8,128)(2,1)S(1)} copy-done((bf16[8,256,474]{1,0,2:T(8,128)(2,1)S(1)}, bf16[8,256,474]{1,0,2:T(8,128)(2,1)}, u32[]{:S(2)}) %copy-start) | copy-done | bytes 1941528
  2.7 5.1 %collective-permute-start.1 = (bf16[474,512]{1,0:T(8,128)(2,1)S(1)}, bf16[474,512]{1,0:T(8,128)(2,1)S(1)}, u32[]{:S(2)}, u32[]{:S(2)}) collective-permute-start(bf16[474,512]{1,0:T(8,128)(2,1)S(1)} %pack_first.1), channel_id=1, source_target_pairs={{0,12},{4,8},{8,4},{12,0},{1,13},{5,9},{9,5},{13,1},{2,14},{6,10},... | collective-permute-start | bytes 1456136 | tf_op jit(solution)/shard_map/ppermute | solution.py:359
  9.1 2.9 %slot_weights.1 = (bf16[256,3072]{1,0:T(8,128)(2,1)S(1)}, f32[256,512]{1,0:T(8,128)S(1)}) custom-call(s32[32]{0:T(128)S(1)} %copy-done.6, s32[32]{0:T(128)S(1)} %copy-done.7, s32[1]{0:T(128)S(6)} %copy.23.refs_2_, bf16[32,128,128]{2,1,0:T(8,128)(2,1)S(1)} %copy-done.4, bf16[256,512]{1,0:T(8,128)(2,1)S(1)} %copy-done.2, bf16[512,512]{1,0:T(8,128)(2,1)S(1)} %copy-done.3), custom_call_target="tpu_custom_call" | custom-call | flops 200000000 | bytes 4194304 | tf_op jit(solution)/shard_map/slot_weights/pallas_call | solution.py:366
  12.0 1.3 %own_rows.1 = (bf16[474,2048]{1,0:T(8,128)(2,1)S(1)}, bf16[512,474]{1,0:T(8,128)(2,1)S(1)}) custom-call(bf16[474,8,256]{2,1,0:T(8,128)(2,1)S(1)} %bitcast.5, bf16[474,512]{1,0:T(8,128)(2,1)S(1)} %copy-done.10), custom_call_target="tpu_custom_call" | custom-call | flops 1000000000 | bytes 5242880 | tf_op jit(solution)/shard_map/own_rows/pallas_call | solution.py:371
  13.4 3.6 %own_points.1 = (f32[256,512]{1,0:T(8,128)S(1)}, bf16[512,2048]{1,0:T(8,128)(2,1)S(1)}) custom-call(bf16[474,2048]{1,0:T(8,128)(2,1)S(1)} %get-tuple-element.69.x_t.x_own, bf16[512,474]{1,0:T(8,128)(2,1)S(1)} %get-tuple-element.67.embed_t.refs_1_, bf16[256,3072]{1,0:T(8,128)(2,1)S(1)} %get-tuple-element.68.weights_all.refs_2_), custom_call_target="tpu_custom_call" | custom-call | flops 2000000000 | bytes 7340032 | tf_op jit(solution)/shard_map/own_points/pallas_call | solution.py:375
  17.0 3.0 %collective-permute-done.1.refs_0_.x_first = bf16[474,512]{1,0:T(8,128)(2,1)S(1)} collective-permute-done((bf16[474,512]{1,0:T(8,128)(2,1)S(1)}, bf16[474,512]{1,0:T(8,128)(2,1)S(1)}, u32[]{:S(2)}, u32[]{:S(2)}) %collective-permute-start.1) | collective-permute-done | bytes 485408 | tf_op jit(solution)/shard_map/ppermute | solution.py:359
  20.9 8.8 %collective-permute-done.x.x_second = bf16[474,512]{1,0:T(8,128)(2,1)S(1)} collective-permute-done((bf16[474,512]{1,0:T(8,128)(2,1)S(1)}, bf16[474,512]{1,0:T(8,128)(2,1)S(1)}, u32[]{:S(2)}, u32[]{:S(2)}) %collective-permute-start) | collective-permute-done | bytes 485408 | tf_op jit(solution)/shard_map/ppermute | solution.py:364
  29.7 2.1 %mesh_nodes.1 = (bf16[2,2,64,512]{3,2,1,0:T(8,128)(2,1)S(1)}, bf16[2,2,64,512]{3,2,1,0:T(8,128)(2,1)S(1)}, f32[256,512]{1,0:T(8,128)S(1)}, f32[1,512]{1,0:T(1,12...) custom-call(bf16[474,512]{1,0:T(8,128)(2,1)S(1)} %collective-permute, ...), custom_call_target="tpu_custom_call" | custom-call | flops 2000000000 | bytes 8388608 | tf_op jit(solution)/shard_map/mesh_nodes/pallas_call | solution.py:390
  33.7 1.5 %collective-permute-start.4 = (bf16[2,2,64,512]{3,2,1,0:T(8,128)(2,1)S(1)}, bf16[2,2,64,512]{3,2,1,0:T(8,128)(2,1)S(1)}, u32[]{:S(2)}, u32[]{:S(2)}) collective-permute-start(bf16[2,2,64,512]{3,2,1,0:T(8,128)(2,1)S(1)} %add_convert_fusion.5), channel_id=1, source_target_pairs={{0,2},{1,5},{2,0},{3,7},{4,6},{5,1},{6,4},{7,3},{8,10},{9,13},{10,... | collective-permute-start | bytes 786440 | tf_op jit(solution)/shard_map/ppermute | solution.py:296
  35.2 2.5 %grid_points.1 = (bf16[2,2,64,512]{3,2,1,0:T(8,128)(2,1)S(1)}, bf16[2,2,64,512]{3,2,1,0:T(8,128)(2,1)S(1)}, bf16[512,3072]{1,0:T(8,128)(2,1)S(1)}, bf16[512,512]{1,0:T(8,128)(2,1)S(1)}) custom-call(bf16[512,256]{1,0:T(8,128)(2,1)S(1)} %get-tuple-element.81.back, bf16[256,3072]{1,0:T(8,128)(2,1)S(1)} %get-tuple-element.68.weights_all.refs_2_, ...), custom_call_target="tpu_custom_call" | custom-call | flops 1600000000 | bytes 9437184 | tf_op jit(solution)/shard_map/grid_points/pallas_call | solution.py:408
  40.2 1.8 %collective-permute-start.8 = (bf16[1,2,64,512]{3,2,1,0:T(8,128)(2,1)S(1)}, bf16[1,2,64,512]{3,2,1,0:T(8,128)(2,1)S(1)}, u32[]{:S(2)}, u32[]{:S(2)}) collective-permute-start(bf16[1,2,64,512]{3,2,1,0:T(8,128)(2,1)S(1)} %slice.13), channel_id=1, source_target_pairs={{0,4},{1,3},{2,6},{3,1},{4,0},{5,7},{6,2},{7,5},{8,12},{9,11},{10,... | collective-permute-start | bytes 393224 | tf_op jit(solution)/shard_map/ppermute | solution.py:296
  42.1 1.6 %collective-permute-start.7 = (bf16[2,2,64,512]{3,2,1,0:T(8,128)(2,1)S(1)}, bf16[2,2,64,512]{3,2,1,0:T(8,128)(2,1)S(1)}, u32[]{:S(2)}, u32[]{:S(2)}) collective-permute-start(bf16[2,2,64,512]{3,2,1,0:T(8,128)(2,1)S(1)} %add_convert_fusion.1), channel_id=1, source_target_pairs={{0,2},{1,5},{2,0},{3,7},{4,6},{5,1},{6,4},{7,3},{8,10},{9,13},{10,... | collective-permute-start | bytes 786440 | tf_op jit(solution)/shard_map/ppermute | solution.py:296
  43.6 1.2 %mesh_outputs.1 = (bf16[256,512]{1,0:T(8,128)(2,1)}, f32[256,512]{1,0:T(8,128)}) custom-call(bf16[256,512]{1,0:T(8,128)(2,1)S(1)} %get-tuple-element.98.update, bf16[512,512]{1,0:T(8,128)(2,1)S(1)} %copy-done.3, bf16[256,512]{1,0:T(8,128)(2,1)S(1)} %copy-done.5, bf16[256,512]{1,0:T(8,128)(2,1)S(1)} %copy-done.2, f32[256,512]{1,0:T(8,128)S(1)} %get-tuple-element.99.grad_mesh), custom_call_target="tpu_custom_call" | custom-call | flops 200000000 | bytes 3145728 | tf_op jit(solution)/shard_map/mesh_outputs/pallas_call | solution.py:426
  44.8 1.8 %collective-permute-done.8 = bf16[1,2,64,512]{3,2,1,0:T(8,128)(2,1)S(1)} collective-permute-done((bf16[1,2,64,512]{3,2,1,0:T(8,128)(2,1)S(1)}, bf16[1,2,64,512]{3,2,1,0:T(8,128)(2,1)S(1)}, u32[]{:S(2)}, u32[]{:S(2)}) %collective-permute-start.8) | collective-permute-done | bytes 131104 | tf_op jit(solution)/shard_map/ppermute | solution.py:296
  46.7 1.6 %collective-permute-start.9 = (bf16[1,2,64,512]{3,2,1,0:T(8,128)(2,1)S(1)}, bf16[1,2,64,512]{3,2,1,0:T(8,128)(2,1)S(1)}, u32[]{:S(2)}, u32[]{:S(2)}) collective-permute-start(bf16[1,2,64,512]{3,2,1,0:T(8,128)(2,1)S(1)} %add_convert_fusion.9), channel_id=1, source_target_pairs={{0,8},{1,9},{2,10},{3,11},{4,12},{5,13},{6,14},{7,15},{8,0},{9,1},... | collective-permute-start | bytes 393224 | tf_op jit(solution)/shard_map/ppermute | solution.py:296
  48.6 1.1 %collective-permute-start.15 = (bf16[1,2,64,512]{3,2,1,0:T(8,128)(2,1)S(1)}, bf16[1,2,64,512]{3,2,1,0:T(8,128)(2,1)S(1)}, u32[]{:S(2)}, u32[]{:S(2)}) collective-permute-start(bf16[1,2,64,512]{3,2,1,0:T(8,128)(2,1)S(1)} %slice.15), channel_id=1, source_target_pairs={{0,4},{1,3},{2,6},{3,1},{4,0},{5,7},{6,2},{7,5},{8,12},{9,11},{10,... | collective-permute-start | bytes 393224 | tf_op jit(solution)/shard_map/ppermute | solution.py:296
  49.8 4.3 %collective-permute-done.9 = bf16[1,2,64,512]{3,2,1,0:T(8,128)(2,1)S(1)} collective-permute-done((bf16[1,2,64,512]{3,2,1,0:T(8,128)(2,1)S(1)}, bf16[1,2,64,512]{3,2,1,0:T(8,128)(2,1)S(1)}, u32[]{:S(2)}, u32[]{:S(2)}) %collective-permute-start.9) | collective-permute-done | bytes 131104 | tf_op jit(solution)/shard_map/ppermute | solution.py:296
  54.5 2.6 %collective-permute-start.16 = (bf16[1,2,64,512]{3,2,1,0:T(8,128)(2,1)S(1)}, bf16[1,2,64,512]{3,2,1,0:T(8,128)(2,1)S(1)}, u32[]{:S(2)}, u32[]{:S(2)}) collective-permute-start(bf16[1,2,64,512]{3,2,1,0:T(8,128)(2,1)S(1)} %add_convert_fusion.7), channel_id=1, source_target_pairs={{0,8},{1,9},{2,10},{3,11},{4,12},{5,13},{6,14},{7,15},{8,0},{9,1},... | collective-permute-start | bytes 393224 | tf_op jit(solution)/shard_map/ppermute | solution.py:296
  57.1 6.1 %collective-permute-done.10.refs_1_ = bf16[1,2,64,512]{3,2,1,0:T(8,128)(2,1)S(1)} collective-permute-done((bf16[1,2,64,512]{3,2,1,0:T(8,128)(2,1)S(1)}, bf16[1,2,64,512]{3,2,1,0:T(8,128)(2,1)S(1)}, u32[]{:S(2)}, u32[]{:S(2)}) %collective-permute-start.10) | collective-permute-done | bytes 131104 | tf_op jit(solution)/shard_map/ppermute | solution.py:296
  63.3 1.3 %collective-permute-start.11 = (bf16[2,2,64,512]{3,2,1,0:T(8,128)(2,1)S(1)}, bf16[2,2,64,512]{3,2,1,0:T(8,128)(2,1)S(1)}, u32[]{:S(2)}, u32[]{:S(2)}) collective-permute-start(bf16[2,2,64,512]{3,2,1,0:T(8,128)(2,1)S(1)} %pad_maximum_fusion), channel_id=1, source_target_pairs={{0,2},{1,5},{2,0},{3,7},{4,6},{5,1},{6,4},{7,3},{8,10},{9,13},{10,... | collective-permute-start | bytes 786440 | tf_op jit(solution)/shard_map/ppermute | solution.py:296
  64.7 5.0 %collective-permute-done.11.refs_2_ = bf16[2,2,64,512]{3,2,1,0:T(8,128)(2,1)S(1)} collective-permute-done((bf16[2,2,64,512]{3,2,1,0:T(8,128)(2,1)S(1)}, bf16[2,2,64,512]{3,2,1,0:T(8,128)(2,1)S(1)}, u32[]{:S(2)}, u32[]{:S(2)}) %collective-permute-start.11) | collective-permute-done | bytes 262176 | tf_op jit(solution)/shard_map/ppermute | solution.py:296
  69.7 1.3 %collective-permute-start.20 = (bf16[2,2,64,512]{3,2,1,0:T(8,128)(2,1)S(1)}, bf16[2,2,64,512]{3,2,1,0:T(8,128)(2,1)S(1)}, u32[]{:S(2)}, u32[]{:S(2)}) collective-permute-start(bf16[2,2,64,512]{3,2,1,0:T(8,128)(2,1)S(1)} %pad_maximum_fusion.1), channel_id=1, source_target_pairs={{0,2},{1,5},{2,0},{3,7},{4,6},{5,1},{6,4},{7,3},{8,10},{9,13},{10,... | collective-permute-start | bytes 786440 | tf_op jit(solution)/shard_map/ppermute | solution.py:296
  72.9 1.5 %order_a.1 = (f32[512,512]{1,0:T(8,128)}, f32[512,512]{1,0:T(8,128)}) custom-call(bf16[1,2,64,512]{3,2,1,0:T(8,128)(2,1)S(1)} %add_convert_fusion.8.refs_0_, bf16[1,2,64,512]{3,2,1,0:T(8,128)(2,1)S(1)} %collective-permute-done.10.refs_1_, bf16[2,2,64,512]{3,2,1,0:T(8,128)(2,1)S(1)} %collective-permute-done.11.refs_2_, ...), custom_call_target="tpu_custom_call" | custom-call | bytes 3145728 | tf_op jit(solution)/shard_map/order_a/pallas_call | solution.py:436
  74.3 1.9 %collective-permute-done.20.refs_2_ = bf16[2,2,64,512]{3,2,1,0:T(8,128)(2,1)S(1)} collective-permute-done((bf16[2,2,64,512]{3,2,1,0:T(8,128)(2,1)S(1)}, bf16[2,2,64,512]{3,2,1,0:T(8,128)(2,1)S(1)}, u32[]{:S(2)}, u32[]{:S(2)}) %collective-permute-start.20) | collective-permute-done | bytes 262176 | tf_op jit(solution)/shard_map/ppermute | solution.py:296
  (71 shorter events, 12.0 us)
Async XLA Ops:
  2.7 17.3 %collective-permute-start.1 = (bf16[474,512]{1,0:T(8,128)(2,1)S(1)}, bf16[474,512]{1,0:T(8,128)(2,1)S(1)}, u32[]{:S(2)}, u32[]{:S(2)}) collective-permute-start(bf16[474,512]{1,0:T(8,128)(2,1)S(1)} %pack_first.1), channel_id=1, source_target_pairs={{0,12},{4,8},{8,4},{12,0},{1,13},{5,9},{9,5},{13,1},{2,14},{6,10},... | collective-permute-start | bytes 1456136 | tf_op jit(solution)/shard_map/ppermute | solution.py:359
  8.4 21.3 %collective-permute-start = (bf16[474,512]{1,0:T(8,128)(2,1)S(1)}, bf16[474,512]{1,0:T(8,128)(2,1)S(1)}, u32[]{:S(2)}, u32[]{:S(2)}) collective-permute-start(bf16[474,512]{1,0:T(8,128)(2,1)S(1)} %pack_second.1), channel_id=1, source_target_pairs={{0,4},{4,0},{8,12},{12,8},{1,5},{5,1},{9,13},{13,9},{2,6},{6,2},{1... | collective-permute-start | bytes 1456136 | tf_op jit(solution)/shard_map/ppermute | solution.py:364
  16.9 12.8 %copy-start.5 = (bf16[256,512]{1,0:T(8,128)(2,1)S(1)}, bf16[256,512]{1,0:T(8,128)(2,1)}, u32[]{:S(2)}) copy-start(bf16[256,512]{1,0:T(8,128)(2,1)} %mesh_lat.3) | copy-start | bytes 786436
  17.0 12.8 %copy-start.8 = (bf16[512,512]{1,0:T(8,128)(2,1)S(1)}, bf16[512,512]{1,0:T(8,128)(2,1)}, u32[]{:S(2)}) copy-start(bf16[512,512]{1,0:T(8,128)(2,1)} %up_w.1) | copy-start | bytes 1572868
  31.8 1.6 %collective-permute-start.2 = (bf16[2,2,64,512]{3,2,1,0:T(8,128)(2,1)S(1)}, bf16[2,2,64,512]{3,2,1,0:T(8,128)(2,1)S(1)}, u32[]{:S(2)}, u32[]{:S(2)}) collective-permute-start(bf16[2,2,64,512]{3,2,1,0:T(8,128)(2,1)S(1)} %get-tuple-element.78), channel_id=1, source_target_pairs={{0,1},{1,0},{2,3},{3,2},{4,5},{5,4},{6,7},{7,6},{8,9},{9,8},{10,11... | collective-permute-start | bytes 786440 | tf_op jit(solution)/shard_map/ppermute | solution.py:285
  33.5 5.8 %collective-permute-start.3 = (bf16[2,2,64,512]{3,2,1,0:T(8,128)(2,1)S(1)}, bf16[2,2,64,512]{3,2,1,0:T(8,128)(2,1)S(1)}, u32[]{:S(2)}, u32[]{:S(2)}) collective-permute-start(bf16[2,2,64,512]{3,2,1,0:T(8,128)(2,1)S(1)} %get-tuple-element.89), channel_id=1, source_target_pairs={{0,1},{1,0},{2,3},{3,2},{4,5},{5,4},{6,7},{7,6},{8,9},{9,8},{10,11... | collective-permute-start | bytes 786440 | tf_op jit(solution)/shard_map/ppermute | solution.py:285
  33.7 6.4 %collective-permute-start.4 = (bf16[2,2,64,512]{3,2,1,0:T(8,128)(2,1)S(1)}, bf16[2,2,64,512]{3,2,1,0:T(8,128)(2,1)S(1)}, u32[]{:S(2)}, u32[]{:S(2)}) collective-permute-start(bf16[2,2,64,512]{3,2,1,0:T(8,128)(2,1)S(1)} %add_convert_fusion.5), channel_id=1, source_target_pairs={{0,2},{1,5},{2,0},{3,7},{4,6},{5,1},{6,4},{7,3},{8,10},{9,13},{10,... | collective-permute-start | bytes 786440 | tf_op jit(solution)/shard_map/ppermute | solution.py:296
  37.7 10.6 %collective-permute-start.5 = (bf16[2,2,64,512]{3,2,1,0:T(8,128)(2,1)S(1)}, bf16[2,2,64,512]{3,2,1,0:T(8,128)(2,1)S(1)}, u32[]{:S(2)}, u32[]{:S(2)}) collective-permute-start(bf16[2,2,64,512]{3,2,1,0:T(8,128)(2,1)S(1)} %get-tuple-element.94), channel_id=1, source_target_pairs={{0,1},{1,0},{2,3},{3,2},{4,5},{5,4},{6,7},{7,6},{8,9},{9,8},{10,11... | collective-permute-start | bytes 786440 | tf_op jit(solution)/shard_map/ppermute | solution.py:285
  38.0 4.0 %collective-permute-start.6 = (bf16[2,2,64,512]{3,2,1,0:T(8,128)(2,1)S(1)}, bf16[2,2,64,512]{3,2,1,0:T(8,128)(2,1)S(1)}, u32[]{:S(2)}, u32[]{:S(2)}) collective-permute-start(bf16[2,2,64,512]{3,2,1,0:T(8,128)(2,1)S(1)} %get-tuple-element.96), channel_id=1, source_target_pairs={{0,1},{1,0},{2,3},{3,2},{4,5},{5,4},{6,7},{7,6},{8,9},{9,8},{10,11... | collective-permute-start | bytes 786440 | tf_op jit(solution)/shard_map/ppermute | solution.py:285
  40.2 6.4 %collective-permute-start.8 = (bf16[1,2,64,512]{3,2,1,0:T(8,128)(2,1)S(1)}, bf16[1,2,64,512]{3,2,1,0:T(8,128)(2,1)S(1)}, u32[]{:S(2)}, u32[]{:S(2)}) collective-permute-start(bf16[1,2,64,512]{3,2,1,0:T(8,128)(2,1)S(1)} %slice.13), channel_id=1, source_target_pairs={{0,4},{1,3},{2,6},{3,1},{4,0},{5,7},{6,2},{7,5},{8,12},{9,11},{10,... | collective-permute-start | bytes 393224 | tf_op jit(solution)/shard_map/ppermute | solution.py:296
  42.1 6.4 %collective-permute-start.7 = (bf16[2,2,64,512]{3,2,1,0:T(8,128)(2,1)S(1)}, bf16[2,2,64,512]{3,2,1,0:T(8,128)(2,1)S(1)}, u32[]{:S(2)}, u32[]{:S(2)}) collective-permute-start(bf16[2,2,64,512]{3,2,1,0:T(8,128)(2,1)S(1)} %add_convert_fusion.1), channel_id=1, source_target_pairs={{0,2},{1,5},{2,0},{3,7},{4,6},{5,1},{6,4},{7,3},{8,10},{9,13},{10,... | collective-permute-start | bytes 786440 | tf_op jit(solution)/shard_map/ppermute | solution.py:296
  46.7 7.3 %collective-permute-start.9 = (bf16[1,2,64,512]{3,2,1,0:T(8,128)(2,1)S(1)}, bf16[1,2,64,512]{3,2,1,0:T(8,128)(2,1)S(1)}, u32[]{:S(2)}, u32[]{:S(2)}) collective-permute-start(bf16[1,2,64,512]{3,2,1,0:T(8,128)(2,1)S(1)} %add_convert_fusion.9), channel_id=1, source_target_pairs={{0,8},{1,9},{2,10},{3,11},{4,12},{5,13},{6,14},{7,15},{8,0},{9,1},... | collective-permute-start | bytes 393224 | tf_op jit(solution)/shard_map/ppermute | solution.py:296
  48.6 5.9 %collective-permute-start.15 = (bf16[1,2,64,512]{3,2,1,0:T(8,128)(2,1)S(1)}, bf16[1,2,64,512]{3,2,1,0:T(8,128)(2,1)S(1)}, u32[]{:S(2)}, u32[]{:S(2)}) collective-permute-start(bf16[1,2,64,512]{3,2,1,0:T(8,128)(2,1)S(1)} %slice.15), channel_id=1, source_target_pairs={{0,4},{1,3},{2,6},{3,1},{4,0},{5,7},{6,2},{7,5},{8,12},{9,11},{10,... | collective-permute-start | bytes 393224 | tf_op jit(solution)/shard_map/ppermute | solution.py:296
  54.1 9.2 %collective-permute-start.10 = (bf16[1,2,64,512]{3,2,1,0:T(8,128)(2,1)S(1)}, bf16[1,2,64,512]{3,2,1,0:T(8,128)(2,1)S(1)}, u32[]{:S(2)}, u32[]{:S(2)}) collective-permute-start(bf16[1,2,64,512]{3,2,1,0:T(8,128)(2,1)S(1)} %add_convert_fusion.8.refs_0_), channel_id=1, source_target_pairs={{0,4},{1,3},{2,6},{3,1},{4,0},{5,7},{6,2},{7,5},{8,12},{9,11},{10,... | collective-permute-start | bytes 393224 | tf_op jit(solution)/shard_map/ppermute | solution.py:296
  54.5 10.0 %collective-permute-start.16 = (bf16[1,2,64,512]{3,2,1,0:T(8,128)(2,1)S(1)}, bf16[1,2,64,512]{3,2,1,0:T(8,128)(2,1)S(1)}, u32[]{:S(2)}, u32[]{:S(2)}) collective-permute-start(bf16[1,2,64,512]{3,2,1,0:T(8,128)(2,1)S(1)} %add_convert_fusion.7), channel_id=1, source_target_pairs={{0,8},{1,9},{2,10},{3,11},{4,12},{5,13},{6,14},{7,15},{8,0},{9,1},... | collective-permute-start | bytes 393224 | tf_op jit(solution)/shard_map/ppermute | solution.py:296
  63.3 6.4 %collective-permute-start.11 = (bf16[2,2,64,512]{3,2,1,0:T(8,128)(2,1)S(1)}, bf16[2,2,64,512]{3,2,1,0:T(8,128)(2,1)S(1)}, u32[]{:S(2)}, u32[]{:S(2)}) collective-permute-start(bf16[2,2,64,512]{3,2,1,0:T(8,128)(2,1)S(1)} %pad_maximum_fusion), channel_id=1, source_target_pairs={{0,2},{1,5},{2,0},{3,7},{4,6},{5,1},{6,4},{7,3},{8,10},{9,13},{10,... | collective-permute-start | bytes 786440 | tf_op jit(solution)/shard_map/ppermute | solution.py:296
  64.6 5.1 %collective-permute-start.18 = (bf16[1,2,64,512]{3,2,1,0:T(8,128)(2,1)S(1)}, bf16[1,2,64,512]{3,2,1,0:T(8,128)(2,1)S(1)}, u32[]{:S(2)}, u32[]{:S(2)}) collective-permute-start(bf16[1,2,64,512]{3,2,1,0:T(8,128)(2,1)S(1)} %add_convert_fusion.6.refs_0_), channel_id=1, source_target_pairs={{0,4},{1,3},{2,6},{3,1},{4,0},{5,7},{6,2},{7,5},{8,12},{9,11},{10,... | collective-permute-start | bytes 393224 | tf_op jit(solution)/shard_map/ppermute | solution.py:296
  64.6 6.9 %collective-permute-start.12 = (bf16[1,2,64,512]{3,2,1,0:T(8,128)(2,1)S(1)}, bf16[1,2,64,512]{3,2,1,0:T(8,128)(2,1)S(1)}, u32[]{:S(2)}, u32[]{:S(2)}) collective-permute-start(bf16[1,2,64,512]{3,2,1,0:T(8,128)(2,1)S(1)} %add_convert_fusion.8.refs_0_), channel_id=1, source_target_pairs={{0,1},{1,0},{2,3},{3,2},{4,5},{5,4},{6,7},{7,6},{8,9},{9,8},{10,11... | collective-permute-start | bytes 393224 | tf_op jit(solution)/shard_map/ppermute | solution.py:285
  69.7 3.2 %collective-permute-start.14 = (bf16[2,2,64,512]{3,2,1,0:T(8,128)(2,1)S(1)}, bf16[2,2,64,512]{3,2,1,0:T(8,128)(2,1)S(1)}, u32[]{:S(2)}, u32[]{:S(2)}) collective-permute-start(bf16[2,2,64,512]{3,2,1,0:T(8,128)(2,1)S(1)} %collective-permute-done.11.refs_2_), channel_id=1, source_target_pairs={{0,1},{1,0},{2,3},{3,2},{4,5},{5,4},{6,7},{7,6},{8,9},{9,8},{10,11... | collective-permute-start | bytes 786440 | tf_op jit(solution)/shard_map/ppermute | solution.py:285
  69.7 6.4 %collective-permute-start.20 = (bf16[2,2,64,512]{3,2,1,0:T(8,128)(2,1)S(1)}, bf16[2,2,64,512]{3,2,1,0:T(8,128)(2,1)S(1)}, u32[]{:S(2)}, u32[]{:S(2)}) collective-permute-start(bf16[2,2,64,512]{3,2,1,0:T(8,128)(2,1)S(1)} %pad_maximum_fusion.1), channel_id=1, source_target_pairs={{0,2},{1,5},{2,0},{3,7},{4,6},{5,1},{6,4},{7,3},{8,10},{9,13},{10,... | collective-permute-start | bytes 786440 | tf_op jit(solution)/shard_map/ppermute | solution.py:296
  71.0 1.3 %collective-permute-start.13 = (bf16[1,2,64,512]{3,2,1,0:T(8,128)(2,1)S(1)}, bf16[1,2,64,512]{3,2,1,0:T(8,128)(2,1)S(1)}, u32[]{:S(2)}, u32[]{:S(2)}) collective-permute-start(bf16[1,2,64,512]{3,2,1,0:T(8,128)(2,1)S(1)} %collective-permute-done.10.refs_1_), channel_id=1, source_target_pairs={{0,1},{1,0},{2,3},{3,2},{4,5},{5,4},{6,7},{7,6},{8,9},{9,8},{10,11... | collective-permute-start | bytes 393224 | tf_op jit(solution)/shard_map/ppermute | solution.py:285
  71.0 1.5 %collective-permute-start.17 = (bf16[1,2,64,512]{3,2,1,0:T(8,128)(2,1)S(1)}, bf16[1,2,64,512]{3,2,1,0:T(8,128)(2,1)S(1)}, u32[]{:S(2)}, u32[]{:S(2)}) collective-permute-start(bf16[1,2,64,512]{3,2,1,0:T(8,128)(2,1)S(1)} %add_convert_fusion.6.refs_0_), channel_id=1, source_target_pairs={{0,1},{1,0},{2,3},{3,2},{4,5},{5,4},{6,7},{7,6},{8,9},{9,8},{10,11... | collective-permute-start | bytes 393224 | tf_op jit(solution)/shard_map/ppermute | solution.py:285
  71.5 1.3 %collective-permute-start.19 = (bf16[1,2,64,512]{3,2,1,0:T(8,128)(2,1)S(1)}, bf16[1,2,64,512]{3,2,1,0:T(8,128)(2,1)S(1)}, u32[]{:S(2)}, u32[]{:S(2)}) collective-permute-start(bf16[1,2,64,512]{3,2,1,0:T(8,128)(2,1)S(1)} %collective-permute-done.18.refs_1_), channel_id=1, source_target_pairs={{0,1},{1,0},{2,3},{3,2},{4,5},{5,4},{6,7},{7,6},{8,9},{9,8},{10,11... | collective-permute-start | bytes 393224 | tf_op jit(solution)/shard_map/ppermute | solution.py:285
  76.2 1.5 %collective-permute-start.21 = (bf16[2,2,64,512]{3,2,1,0:T(8,128)(2,1)S(1)}, bf16[2,2,64,512]{3,2,1,0:T(8,128)(2,1)S(1)}, u32[]{:S(2)}, u32[]{:S(2)}) collective-permute-start(bf16[2,2,64,512]{3,2,1,0:T(8,128)(2,1)S(1)} %collective-permute-done.20.refs_2_), channel_id=1, source_target_pairs={{0,1},{1,0},{2,3},{3,2},{4,5},{5,4},{6,7},{7,6},{8,9},{9,8},{10,11... | collective-permute-start | bytes 786440 | tf_op jit(solution)/shard_map/ppermute | solution.py:285
  (10 other events, 80.3 us)

commit v20 on v15

--- a/solution.py
+++ b/solution.py
@@ -266,8 +266,8 @@
 def role_steps():
     lat = [("lat", 2 << k) for k in range(lax.axis_size("lat").bit_length() - 2)]
     lon = [("lon", 1 << k) for k in range(lax.axis_size("lon").bit_length() - 1)]
-    rest = lat[1:] + lon[1:]
-    return ([lat[0], lon[0]] + rest, [lon[0], lat[0]] + rest)
+    rest = lat[1:] + lon[2:]
+    return (lat[:1] + lon[:2] + rest, lon[:2] + lat[:1] + rest)
 
 
 def core_swapped(value):

time: 78.8 us -> 82.4 us (1.046)
  starting transfers between devices: 17.9 us -> 20 us
  waiting for transfers between devices: 36.2 us -> 37.4 us
    ppermute x10, starting transfers between devices: 11.3 us -> 13.4 us  [swapped(): return lax.ppermute(value, ('lon', 'lat'), pairs)]
    ppermute x10, waiting for transfers between devices: 22.2 us -> 23.7 us  [swapped(): return lax.ppermute(value, ('lon', 'lat'), pairs)]
  transfers between devices with their start and end apart: 22 -> 22, of which waited for: 14 -> 14; matrix products, arithmetic and copies ran while one was open for 1% -> 1% of each run, Pallas kernels for 22% -> 21%
where the time goes in v20:
time: 82.4 us; the launch traced here: 82.3 us
  waiting for transfers between devices  37.4 us (45%)
  Pallas kernels  21.2 us (26%)
  starting transfers between devices  20 us (24%)
  between operations  1.63 us (2%)
  local copies, waits for them, and re-layouts  1.49 us (2%)
    ppermute x10, waiting for transfers between devices, swapped(): return lax.ppermute(value, ('lon', 'lat'), pairs)  23.7 us
    ppermute x10, starting transfers between devices, swapped(): return lax.ppermute(value, ('lon', 'lat'), pairs)  13.4 us
    ppermute x1, waiting for transfers between devices, on_device(): lax.ppermute(to_west, 'lon', [((i + 1) % count, i) for i in range(count)])  8.72 us
    pallas_call x1, Pallas kernels, on_device(): call(lambda *refs: weights_kernel(rows, cols // block, *refs), 'slot_weig...  3.77 us
    pallas_call x1, Pallas kernels, on_device(): call(own_kernel, 'own_points', [VMEM] * 3, [shape((nodes, latent), F32),...  3.55 us
    ppermute x1, starting transfers between devices, on_device(): lax.ppermute(to_east, 'lon', [(i, (i + 1) % count) for i in range(count)])  3.08 us
    ppermute x10, waiting for transfers between devices, core_swapped(): lax.ppermute(value, 'lat', [(i, i ^ 1) for i in range(lax.axis_size('lat'...  2.86 us
    pallas_call x1, Pallas kernels, on_device(): call(grid_kernel, 'grid_points', [VMEM] * 11, [quarter, quarter, shape((l...  2.33 us
  transfers between devices with their start and end apart: 22, of which 14 were waited for; matrix products, arithmetic and copies ran while one was open for 1% of the time, Pallas kernels for 21%

profile of v20, /device:TPU:0, one launch (start us, length us, event | category | flops | bytes accessed | tf_op | source)
XLA Modules:
  0.0 82.3 jit_solution(495984551902197439)
XLA Ops:
  0.6 1.4 %slice.20.refs_0_ = bf16[474,8,128]{2,1,0:T(8,128)(2,1)S(1)} slice(bf16[474,8,256]{2,1,0:T(8,128)(2,1)} %bitcast.3), slice={[0:474], [0:8], [128:256]} | slice | bytes 1941504 | tf_op jit(solution)/shard_map/slice | solution.py:346
  2.6 3.1 %collective-permute-start.1 = (bf16[474,512]{1,0:T(8,128)(2,1)S(1)}, bf16[474,512]{1,0:T(8,128)(2,1)S(1)}, u32[]{:S(2)}, u32[]{:S(2)}) collective-permute-start(bf16[474,512]{1,0:T(8,128)(2,1)S(1)} %pack_east.1), channel_id=1, source_target_pairs={{0,4},{4,8},{8,12},{12,0},{1,5},{5,9},{9,13},{13,1},{2,6},{6,10},{... | collective-permute-start | bytes 1456136 | tf_op jit(solution)/shard_map/ppermute | solution.py:348
  6.2 2.1 %collective-permute-start = (bf16[474,512]{1,0:T(8,128)(2,1)S(1)}, bf16[474,512]{1,0:T(8,128)(2,1)S(1)}, u32[]{:S(2)}, u32[]{:S(2)}) collective-permute-start(bf16[474,512]{1,0:T(8,128)(2,1)S(1)} %pack_west.1), channel_id=1, source_target_pairs={{4,0},{8,4},{12,8},{0,12},{5,1},{9,5},{13,9},{1,13},{6,2},{10,6},{... | collective-permute-start | bytes 1456136 | tf_op jit(solution)/shard_map/ppermute | solution.py:351
  9.0 3.8 %slot_weights.1 = (bf16[256,3072]{1,0:T(8,128)(2,1)S(1)}, f32[256,512]{1,0:T(8,128)S(1)}) custom-call(s32[32]{0:T(128)S(1)} %copy-done.5, s32[32]{0:T(128)S(1)} %copy-done.6, s32[1]{0:T(128)S(6)} %copy.23.refs_2_, bf16[32,128,128]{2,1,0:T(8,128)(2,1)S(1)} %copy-done.3, bf16[256,512]{1,0:T(8,128)(2,1)S(1)} %copy-done.1, bf16[512,512]{1,0:T(8,128)(2,1)S(1)} %copy-done.2), custom_call_target="tpu_custom_call" | custom-call | flops 200000000 | bytes 4194304 | tf_op jit(solution)/shard_map/slot_weights/pallas_call | solution.py:353
  12.8 1.3 %own_rows.1 = (bf16[474,2048]{1,0:T(8,128)(2,1)S(1)}, bf16[512,474]{1,0:T(8,128)(2,1)S(1)}) custom-call(bf16[474,8,256]{2,1,0:T(8,128)(2,1)S(1)} %bitcast.5, bf16[474,512]{1,0:T(8,128)(2,1)S(1)} %copy-done.9), custom_call_target="tpu_custom_call" | custom-call | flops 1000000000 | bytes 5242880 | tf_op jit(solution)/shard_map/own_rows/pallas_call | solution.py:358
  14.2 3.6 %own_points.1 = (f32[256,512]{1,0:T(8,128)S(1)}, bf16[512,2048]{1,0:T(8,128)(2,1)S(1)}) custom-call(bf16[474,2048]{1,0:T(8,128)(2,1)S(1)} %get-tuple-element.69.x_t.x_own, bf16[512,474]{1,0:T(8,128)(2,1)S(1)} %get-tuple-element.67.embed_t.refs_1_, bf16[256,3072]{1,0:T(8,128)(2,1)S(1)} %get-tuple-element.68.weights_all.refs_2_), custom_call_target="tpu_custom_call" | custom-call | flops 2000000000 | bytes 7340032 | tf_op jit(solution)/shard_map/own_points/pallas_call | solution.py:362
  17.8 2.1 %collective-permute-done.1.refs_0_.x_west = bf16[474,512]{1,0:T(8,128)(2,1)S(1)} collective-permute-done((bf16[474,512]{1,0:T(8,128)(2,1)S(1)}, bf16[474,512]{1,0:T(8,128)(2,1)S(1)}, u32[]{:S(2)}, u32[]{:S(2)}) %collective-permute-start.1) | collective-permute-done | bytes 485408 | tf_op jit(solution)/shard_map/ppermute | solution.py:348
  20.8 8.7 %collective-permute-done.x.x_east = bf16[474,512]{1,0:T(8,128)(2,1)S(1)} collective-permute-done((bf16[474,512]{1,0:T(8,128)(2,1)S(1)}, bf16[474,512]{1,0:T(8,128)(2,1)S(1)}, u32[]{:S(2)}, u32[]{:S(2)}) %collective-permute-start) | collective-permute-done | bytes 485408 | tf_op jit(solution)/shard_map/ppermute | solution.py:351
  29.5 2.1 %mesh_nodes.1 = (bf16[2,2,64,512]{3,2,1,0:T(8,128)(2,1)S(1)}, bf16[2,2,64,512]{3,2,1,0:T(8,128)(2,1)S(1)}, f32[256,512]{1,0:T(8,128)S(1)}, f32[1,512]{1,0:T(1,12...) custom-call(bf16[474,512]{1,0:T(8,128)(2,1)S(1)} %collective-permute, ...), custom_call_target="tpu_custom_call" | custom-call | flops 2000000000 | bytes 8388608 | tf_op jit(solution)/shard_map/mesh_nodes/pallas_call | solution.py:377
  33.5 1.5 %collective-permute-start.4 = (bf16[2,2,64,512]{3,2,1,0:T(8,128)(2,1)S(1)}, bf16[2,2,64,512]{3,2,1,0:T(8,128)(2,1)S(1)}, u32[]{:S(2)}, u32[]{:S(2)}) collective-permute-start(bf16[2,2,64,512]{3,2,1,0:T(8,128)(2,1)S(1)} %add_convert_fusion.5), channel_id=1, source_target_pairs={{0,2},{1,5},{2,0},{3,7},{4,6},{5,1},{6,4},{7,3},{8,10},{9,13},{10,... | collective-permute-start | bytes 786440 | tf_op jit(solution)/shard_map/ppermute | solution.py:285
  35.0 2.3 %grid_points.1 = (bf16[2,2,64,512]{3,2,1,0:T(8,128)(2,1)S(1)}, bf16[2,2,64,512]{3,2,1,0:T(8,128)(2,1)S(1)}, bf16[512,3072]{1,0:T(8,128)(2,1)S(1)}, bf16[512,512]{1,0:T(8,128)(2,1)S(1)}) custom-call(bf16[512,256]{1,0:T(8,128)(2,1)S(1)} %get-tuple-element.81.back, bf16[256,3072]{1,0:T(8,128)(2,1)S(1)} %get-tuple-element.68.weights_all.refs_2_, ...), custom_call_target="tpu_custom_call" | custom-call | flops 1600000000 | bytes 9437184 | tf_op jit(solution)/shard_map/grid_points/pallas_call | solution.py:395
  40.8 1.6 %collective-permute-start.7 = (bf16[2,2,64,512]{3,2,1,0:T(8,128)(2,1)S(1)}, bf16[2,2,64,512]{3,2,1,0:T(8,128)(2,1)S(1)}, u32[]{:S(2)}, u32[]{:S(2)}) collective-permute-start(bf16[2,2,64,512]{3,2,1,0:T(8,128)(2,1)S(1)} %add_convert_fusion.1), channel_id=1, source_target_pairs={{0,2},{1,5},{2,0},{3,7},{4,6},{5,1},{6,4},{7,3},{8,10},{9,13},{10,... | collective-permute-start | bytes 786440 | tf_op jit(solution)/shard_map/ppermute | solution.py:285
  42.3 1.2 %mesh_outputs.1 = (bf16[256,512]{1,0:T(8,128)(2,1)}, f32[256,512]{1,0:T(8,128)}) custom-call(bf16[256,512]{1,0:T(8,128)(2,1)S(1)} %get-tuple-element.98.update, bf16[512,512]{1,0:T(8,128)(2,1)S(1)} %copy-done.2, bf16[256,512]{1,0:T(8,128)(2,1)S(1)} %copy-done.4, bf16[256,512]{1,0:T(8,128)(2,1)S(1)} %copy-done.1, f32[256,512]{1,0:T(8,128)S(1)} %get-tuple-element.99.grad_mesh), custom_call_target="tpu_custom_call" | custom-call | flops 200000000 | bytes 3145728 | tf_op jit(solution)/shard_map/mesh_outputs/pallas_call | solution.py:413
  43.5 4.0 %collective-permute-done.8 = bf16[1,2,64,512]{3,2,1,0:T(8,128)(2,1)S(1)} collective-permute-done((bf16[1,2,64,512]{3,2,1,0:T(8,128)(2,1)S(1)}, bf16[1,2,64,512]{3,2,1,0:T(8,128)(2,1)S(1)}, u32[]{:S(2)}, u32[]{:S(2)}) %collective-permute-start.8) | collective-permute-done | bytes 131104 | tf_op jit(solution)/shard_map/ppermute | solution.py:285
  48.7 2.5 %collective-permute-start.15 = (bf16[1,2,64,512]{3,2,1,0:T(8,128)(2,1)S(1)}, bf16[1,2,64,512]{3,2,1,0:T(8,128)(2,1)S(1)}, u32[]{:S(2)}, u32[]{:S(2)}) collective-permute-start(bf16[1,2,64,512]{3,2,1,0:T(8,128)(2,1)S(1)} %slice.19), channel_id=1, source_target_pairs={{0,4},{1,9},{2,6},{3,11},{4,0},{5,13},{6,2},{7,15},{8,12},{9,1},{1... | collective-permute-start | bytes 393224 | tf_op jit(solution)/shard_map/ppermute | solution.py:285
  51.2 7.8 %collective-permute-done.9 = bf16[1,2,64,512]{3,2,1,0:T(8,128)(2,1)S(1)} collective-permute-done((bf16[1,2,64,512]{3,2,1,0:T(8,128)(2,1)S(1)}, bf16[1,2,64,512]{3,2,1,0:T(8,128)(2,1)S(1)}, u32[]{:S(2)}, u32[]{:S(2)}) %collective-permute-start.9) | collective-permute-done | bytes 131104 | tf_op jit(solution)/shard_map/ppermute | solution.py:285
  59.2 2.6 %collective-permute-start.16 = (bf16[1,2,64,512]{3,2,1,0:T(8,128)(2,1)S(1)}, bf16[1,2,64,512]{3,2,1,0:T(8,128)(2,1)S(1)}, u32[]{:S(2)}, u32[]{:S(2)}) collective-permute-start(bf16[1,2,64,512]{3,2,1,0:T(8,128)(2,1)S(1)} %add_convert_fusion.7), channel_id=1, source_target_pairs={{0,8},{1,3},{2,10},{3,1},{4,12},{5,7},{6,14},{7,5},{8,0},{9,11},{1... | collective-permute-start | bytes 393224 | tf_op jit(solution)/shard_map/ppermute | solution.py:285
  61.8 4.7 %collective-permute-done.10.refs_1_ = bf16[1,2,64,512]{3,2,1,0:T(8,128)(2,1)S(1)} collective-permute-done((bf16[1,2,64,512]{3,2,1,0:T(8,128)(2,1)S(1)}, bf16[1,2,64,512]{3,2,1,0:T(8,128)(2,1)S(1)}, u32[]{:S(2)}, u32[]{:S(2)}) %collective-permute-start.10) | collective-permute-done | bytes 131104 | tf_op jit(solution)/shard_map/ppermute | solution.py:285
  66.5 1.6 %collective-permute-start.11 = (bf16[2,2,64,512]{3,2,1,0:T(8,128)(2,1)S(1)}, bf16[2,2,64,512]{3,2,1,0:T(8,128)(2,1)S(1)}, u32[]{:S(2)}, u32[]{:S(2)}) collective-permute-start(bf16[2,2,64,512]{3,2,1,0:T(8,128)(2,1)S(1)} %pad_maximum_fusion), channel_id=1, source_target_pairs={{0,2},{1,5},{2,0},{3,7},{4,6},{5,1},{6,4},{7,3},{8,10},{9,13},{10,... | collective-permute-start | bytes 786440 | tf_op jit(solution)/shard_map/ppermute | solution.py:285
  68.7 4.3 %collective-permute-done.11.refs_2_ = bf16[2,2,64,512]{3,2,1,0:T(8,128)(2,1)S(1)} collective-permute-done((bf16[2,2,64,512]{3,2,1,0:T(8,128)(2,1)S(1)}, bf16[2,2,64,512]{3,2,1,0:T(8,128)(2,1)S(1)}, u32[]{:S(2)}, u32[]{:S(2)}) %collective-permute-start.11) | collective-permute-done | bytes 262176 | tf_op jit(solution)/shard_map/ppermute | solution.py:285
  73.3 1.4 %collective-permute-start.20 = (bf16[2,2,64,512]{3,2,1,0:T(8,128)(2,1)S(1)}, bf16[2,2,64,512]{3,2,1,0:T(8,128)(2,1)S(1)}, u32[]{:S(2)}, u32[]{:S(2)}) collective-permute-start(bf16[2,2,64,512]{3,2,1,0:T(8,128)(2,1)S(1)} %pad_maximum_fusion.1), channel_id=1, source_target_pairs={{0,2},{1,5},{2,0},{3,7},{4,6},{5,1},{6,4},{7,3},{8,10},{9,13},{10,... | collective-permute-start | bytes 786440 | tf_op jit(solution)/shard_map/ppermute | solution.py:285
  76.5 1.5 %order_a.1 = (f32[512,512]{1,0:T(8,128)}, f32[512,512]{1,0:T(8,128)}) custom-call(bf16[1,2,64,512]{3,2,1,0:T(8,128)(2,1)S(1)} %add_convert_fusion.8.refs_0_, bf16[1,2,64,512]{3,2,1,0:T(8,128)(2,1)S(1)} %collective-permute-done.10.refs_1_, bf16[2,2,64,512]{3,2,1,0:T(8,128)(2,1)S(1)} %collective-permute-done.11.refs_2_, ...), custom_call_target="tpu_custom_call" | custom-call | bytes 3145728 | tf_op jit(solution)/shard_map/order_a/pallas_call | solution.py:423
  78.0 1.7 %collective-permute-done.20.refs_2_ = bf16[2,2,64,512]{3,2,1,0:T(8,128)(2,1)S(1)} collective-permute-done((bf16[2,2,64,512]{3,2,1,0:T(8,128)(2,1)S(1)}, bf16[2,2,64,512]{3,2,1,0:T(8,128)(2,1)S(1)}, u32[]{:S(2)}, u32[]{:S(2)}) %collective-permute-start.20) | collective-permute-done | bytes 262176 | tf_op jit(solution)/shard_map/ppermute | solution.py:285
  79.7 1.0 %order_b.2 = (f32[512,512]{1,0:T(8,128)}, f32[474,512]{1,0:T(8,128)}, f32[1,512]{1,0:T(1,128)S(1)}) custom-call(bf16[1,2,64,512]{3,2,1,0:T(8,128)(2,1)S(1)} %add_convert_fusion.6.refs_0_, bf16[1,2,64,512]{3,2,1,0:T(8,128)(2,1)S(1)} %collective-permute-done.18.refs_1_, bf16[2,2,64,512]{3,2,1,0:T(8,128)(2,1)S(1)} %collective-permute-done.20.refs_2_), custom_call_target="tpu_custom_call" | custom-call | bytes 2097152 | tf_op jit(solution)/shard_map/order_b/pallas_call | solution.py:434
  (70 shorter events, 12.7 us)
Async XLA Ops:
  2.6 17.2 %collective-permute-start.1 = (bf16[474,512]{1,0:T(8,128)(2,1)S(1)}, bf16[474,512]{1,0:T(8,128)(2,1)S(1)}, u32[]{:S(2)}, u32[]{:S(2)}) collective-permute-start(bf16[474,512]{1,0:T(8,128)(2,1)S(1)} %pack_east.1), channel_id=1, source_target_pairs={{0,4},{4,8},{8,12},{12,0},{1,5},{5,9},{9,13},{13,1},{2,6},{6,10},{... | collective-permute-start | bytes 1456136 | tf_op jit(solution)/shard_map/ppermute | solution.py:348
  6.2 23.3 %collective-permute-start = (bf16[474,512]{1,0:T(8,128)(2,1)S(1)}, bf16[474,512]{1,0:T(8,128)(2,1)S(1)}, u32[]{:S(2)}, u32[]{:S(2)}) collective-permute-start(bf16[474,512]{1,0:T(8,128)(2,1)S(1)} %pack_west.1), channel_id=1, source_target_pairs={{4,0},{8,4},{12,8},{0,12},{5,1},{9,5},{13,9},{1,13},{6,2},{10,6},{... | collective-permute-start | bytes 1456136 | tf_op jit(solution)/shard_map/ppermute | solution.py:351
  17.7 11.8 %copy-start.4 = (bf16[256,512]{1,0:T(8,128)(2,1)S(1)}, bf16[256,512]{1,0:T(8,128)(2,1)}, u32[]{:S(2)}) copy-start(bf16[256,512]{1,0:T(8,128)(2,1)} %mesh_lat.3) | copy-start | bytes 786436
  17.7 11.8 %copy-start.7 = (bf16[512,512]{1,0:T(8,128)(2,1)S(1)}, bf16[512,512]{1,0:T(8,128)(2,1)}, u32[]{:S(2)}) copy-start(bf16[512,512]{1,0:T(8,128)(2,1)} %up_w.1) | copy-start | bytes 1572868
  31.6 1.6 %collective-permute-start.2 = (bf16[2,2,64,512]{3,2,1,0:T(8,128)(2,1)S(1)}, bf16[2,2,64,512]{3,2,1,0:T(8,128)(2,1)S(1)}, u32[]{:S(2)}, u32[]{:S(2)}) collective-permute-start(bf16[2,2,64,512]{3,2,1,0:T(8,128)(2,1)S(1)} %get-tuple-element.78), channel_id=1, source_target_pairs={{0,1},{1,0},{2,3},{3,2},{4,5},{5,4},{6,7},{7,6},{8,9},{9,8},{10,11... | collective-permute-start | bytes 786440 | tf_op jit(solution)/shard_map/ppermute | solution.py:274
  33.3 5.6 %collective-permute-start.3 = (bf16[2,2,64,512]{3,2,1,0:T(8,128)(2,1)S(1)}, bf16[2,2,64,512]{3,2,1,0:T(8,128)(2,1)S(1)}, u32[]{:S(2)}, u32[]{:S(2)}) collective-permute-start(bf16[2,2,64,512]{3,2,1,0:T(8,128)(2,1)S(1)} %get-tuple-element.89), channel_id=1, source_target_pairs={{0,1},{1,0},{2,3},{3,2},{4,5},{5,4},{6,7},{7,6},{8,9},{9,8},{10,11... | collective-permute-start | bytes 786440 | tf_op jit(solution)/shard_map/ppermute | solution.py:274
  33.5 6.4 %collective-permute-start.4 = (bf16[2,2,64,512]{3,2,1,0:T(8,128)(2,1)S(1)}, bf16[2,2,64,512]{3,2,1,0:T(8,128)(2,1)S(1)}, u32[]{:S(2)}, u32[]{:S(2)}) collective-permute-start(bf16[2,2,64,512]{3,2,1,0:T(8,128)(2,1)S(1)} %add_convert_fusion.5), channel_id=1, source_target_pairs={{0,2},{1,5},{2,0},{3,7},{4,6},{5,1},{6,4},{7,3},{8,10},{9,13},{10,... | collective-permute-start | bytes 786440 | tf_op jit(solution)/shard_map/ppermute | solution.py:285
  37.3 11.2 %collective-permute-start.5 = (bf16[2,2,64,512]{3,2,1,0:T(8,128)(2,1)S(1)}, bf16[2,2,64,512]{3,2,1,0:T(8,128)(2,1)S(1)}, u32[]{:S(2)}, u32[]{:S(2)}) collective-permute-start(bf16[2,2,64,512]{3,2,1,0:T(8,128)(2,1)S(1)} %get-tuple-element.94), channel_id=1, source_target_pairs={{0,1},{1,0},{2,3},{3,2},{4,5},{5,4},{6,7},{7,6},{8,9},{9,8},{10,11... | collective-permute-start | bytes 786440 | tf_op jit(solution)/shard_map/ppermute | solution.py:274
  37.4 3.3 %collective-permute-start.6 = (bf16[2,2,64,512]{3,2,1,0:T(8,128)(2,1)S(1)}, bf16[2,2,64,512]{3,2,1,0:T(8,128)(2,1)S(1)}, u32[]{:S(2)}, u32[]{:S(2)}) collective-permute-start(bf16[2,2,64,512]{3,2,1,0:T(8,128)(2,1)S(1)} %get-tuple-element.96), channel_id=1, source_target_pairs={{0,1},{1,0},{2,3},{3,2},{4,5},{5,4},{6,7},{7,6},{8,9},{9,8},{10,11... | collective-permute-start | bytes 786440 | tf_op jit(solution)/shard_map/ppermute | solution.py:274
  40.0 7.6 %collective-permute-start.8 = (bf16[1,2,64,512]{3,2,1,0:T(8,128)(2,1)S(1)}, bf16[1,2,64,512]{3,2,1,0:T(8,128)(2,1)S(1)}, u32[]{:S(2)}, u32[]{:S(2)}) collective-permute-start(bf16[1,2,64,512]{3,2,1,0:T(8,128)(2,1)S(1)} %slice.17), channel_id=1, source_target_pairs={{0,4},{1,9},{2,6},{3,11},{4,0},{5,13},{6,2},{7,15},{8,12},{9,1},{1... | collective-permute-start | bytes 393224 | tf_op jit(solution)/shard_map/ppermute | solution.py:285
  40.8 7.8 %collective-permute-start.7 = (bf16[2,2,64,512]{3,2,1,0:T(8,128)(2,1)S(1)}, bf16[2,2,64,512]{3,2,1,0:T(8,128)(2,1)S(1)}, u32[]{:S(2)}, u32[]{:S(2)}) collective-permute-start(bf16[2,2,64,512]{3,2,1,0:T(8,128)(2,1)S(1)} %add_convert_fusion.1), channel_id=1, source_target_pairs={{0,2},{1,5},{2,0},{3,7},{4,6},{5,1},{6,4},{7,3},{8,10},{9,13},{10,... | collective-permute-start | bytes 786440 | tf_op jit(solution)/shard_map/ppermute | solution.py:285
  47.6 11.4 %collective-permute-start.9 = (bf16[1,2,64,512]{3,2,1,0:T(8,128)(2,1)S(1)}, bf16[1,2,64,512]{3,2,1,0:T(8,128)(2,1)S(1)}, u32[]{:S(2)}, u32[]{:S(2)}) collective-permute-start(bf16[1,2,64,512]{3,2,1,0:T(8,128)(2,1)S(1)} %add_convert_fusion.9), channel_id=1, source_target_pairs={{0,8},{1,3},{2,10},{3,1},{4,12},{5,7},{6,14},{7,5},{8,0},{9,11},{1... | collective-permute-start | bytes 393224 | tf_op jit(solution)/shard_map/ppermute | solution.py:285
  48.7 10.4 %collective-permute-start.15 = (bf16[1,2,64,512]{3,2,1,0:T(8,128)(2,1)S(1)}, bf16[1,2,64,512]{3,2,1,0:T(8,128)(2,1)S(1)}, u32[]{:S(2)}, u32[]{:S(2)}) collective-permute-start(bf16[1,2,64,512]{3,2,1,0:T(8,128)(2,1)S(1)} %slice.19), channel_id=1, source_target_pairs={{0,4},{1,9},{2,6},{3,11},{4,0},{5,13},{6,2},{7,15},{8,12},{9,1},{1... | collective-permute-start | bytes 393224 | tf_op jit(solution)/shard_map/ppermute | solution.py:285
  59.0 7.5 %collective-permute-start.10 = (bf16[1,2,64,512]{3,2,1,0:T(8,128)(2,1)S(1)}, bf16[1,2,64,512]{3,2,1,0:T(8,128)(2,1)S(1)}, u32[]{:S(2)}, u32[]{:S(2)}) collective-permute-start(bf16[1,2,64,512]{3,2,1,0:T(8,128)(2,1)S(1)} %add_convert_fusion.8.refs_0_), channel_id=1, source_target_pairs={{0,4},{1,9},{2,6},{3,11},{4,0},{5,13},{6,2},{7,15},{8,12},{9,1},{1... | collective-permute-start | bytes 393224 | tf_op jit(solution)/shard_map/ppermute | solution.py:285
  59.2 9.0 %collective-permute-start.16 = (bf16[1,2,64,512]{3,2,1,0:T(8,128)(2,1)S(1)}, bf16[1,2,64,512]{3,2,1,0:T(8,128)(2,1)S(1)}, u32[]{:S(2)}, u32[]{:S(2)}) collective-permute-start(bf16[1,2,64,512]{3,2,1,0:T(8,128)(2,1)S(1)} %add_convert_fusion.7), channel_id=1, source_target_pairs={{0,8},{1,3},{2,10},{3,1},{4,12},{5,7},{6,14},{7,5},{8,0},{9,11},{1... | collective-permute-start | bytes 393224 | tf_op jit(solution)/shard_map/ppermute | solution.py:285
  66.5 6.4 %collective-permute-start.11 = (bf16[2,2,64,512]{3,2,1,0:T(8,128)(2,1)S(1)}, bf16[2,2,64,512]{3,2,1,0:T(8,128)(2,1)S(1)}, u32[]{:S(2)}, u32[]{:S(2)}) collective-permute-start(bf16[2,2,64,512]{3,2,1,0:T(8,128)(2,1)S(1)} %pad_maximum_fusion), channel_id=1, source_target_pairs={{0,2},{1,5},{2,0},{3,7},{4,6},{5,1},{6,4},{7,3},{8,10},{9,13},{10,... | collective-permute-start | bytes 786440 | tf_op jit(solution)/shard_map/ppermute | solution.py:285
  68.2 5.0 %collective-permute-start.18 = (bf16[1,2,64,512]{3,2,1,0:T(8,128)(2,1)S(1)}, bf16[1,2,64,512]{3,2,1,0:T(8,128)(2,1)S(1)}, u32[]{:S(2)}, u32[]{:S(2)}) collective-permute-start(bf16[1,2,64,512]{3,2,1,0:T(8,128)(2,1)S(1)} %add_convert_fusion.6.refs_0_), channel_id=1, source_target_pairs={{0,4},{1,9},{2,6},{3,11},{4,0},{5,13},{6,2},{7,15},{8,12},{9,1},{1... | collective-permute-start | bytes 393224 | tf_op jit(solution)/shard_map/ppermute | solution.py:285
  68.7 6.5 %collective-permute-start.12 = (bf16[1,2,64,512]{3,2,1,0:T(8,128)(2,1)S(1)}, bf16[1,2,64,512]{3,2,1,0:T(8,128)(2,1)S(1)}, u32[]{:S(2)}, u32[]{:S(2)}) collective-permute-start(bf16[1,2,64,512]{3,2,1,0:T(8,128)(2,1)S(1)} %add_convert_fusion.8.refs_0_), channel_id=1, source_target_pairs={{0,1},{1,0},{2,3},{3,2},{4,5},{5,4},{6,7},{7,6},{8,9},{9,8},{10,11... | collective-permute-start | bytes 393224 | tf_op jit(solution)/shard_map/ppermute | solution.py:274
  73.0 3.6 %collective-permute-start.14 = (bf16[2,2,64,512]{3,2,1,0:T(8,128)(2,1)S(1)}, bf16[2,2,64,512]{3,2,1,0:T(8,128)(2,1)S(1)}, u32[]{:S(2)}, u32[]{:S(2)}) collective-permute-start(bf16[2,2,64,512]{3,2,1,0:T(8,128)(2,1)S(1)} %collective-permute-done.11.refs_2_), channel_id=1, source_target_pairs={{0,1},{1,0},{2,3},{3,2},{4,5},{5,4},{6,7},{7,6},{8,9},{9,8},{10,11... | collective-permute-start | bytes 786440 | tf_op jit(solution)/shard_map/ppermute | solution.py:274
  73.3 6.4 %collective-permute-start.20 = (bf16[2,2,64,512]{3,2,1,0:T(8,128)(2,1)S(1)}, bf16[2,2,64,512]{3,2,1,0:T(8,128)(2,1)S(1)}, u32[]{:S(2)}, u32[]{:S(2)}) collective-permute-start(bf16[2,2,64,512]{3,2,1,0:T(8,128)(2,1)S(1)} %pad_maximum_fusion.1), channel_id=1, source_target_pairs={{0,2},{1,5},{2,0},{3,7},{4,6},{5,1},{6,4},{7,3},{8,10},{9,13},{10,... | collective-permute-start | bytes 786440 | tf_op jit(solution)/shard_map/ppermute | solution.py:285
  74.6 1.3 %collective-permute-start.13 = (bf16[1,2,64,512]{3,2,1,0:T(8,128)(2,1)S(1)}, bf16[1,2,64,512]{3,2,1,0:T(8,128)(2,1)S(1)}, u32[]{:S(2)}, u32[]{:S(2)}) collective-permute-start(bf16[1,2,64,512]{3,2,1,0:T(8,128)(2,1)S(1)} %collective-permute-done.10.refs_1_), channel_id=1, source_target_pairs={{0,1},{1,0},{2,3},{3,2},{4,5},{5,4},{6,7},{7,6},{8,9},{9,8},{10,11... | collective-permute-start | bytes 393224 | tf_op jit(solution)/shard_map/ppermute | solution.py:274
  74.6 1.5 %collective-permute-start.17 = (bf16[1,2,64,512]{3,2,1,0:T(8,128)(2,1)S(1)}, bf16[1,2,64,512]{3,2,1,0:T(8,128)(2,1)S(1)}, u32[]{:S(2)}, u32[]{:S(2)}) collective-permute-start(bf16[1,2,64,512]{3,2,1,0:T(8,128)(2,1)S(1)} %add_convert_fusion.6.refs_0_), channel_id=1, source_target_pairs={{0,1},{1,0},{2,3},{3,2},{4,5},{5,4},{6,7},{7,6},{8,9},{9,8},{10,11... | collective-permute-start | bytes 393224 | tf_op jit(solution)/shard_map/ppermute | solution.py:274
  75.2 1.3 %collective-permute-start.19 = (bf16[1,2,64,512]{3,2,1,0:T(8,128)(2,1)S(1)}, bf16[1,2,64,512]{3,2,1,0:T(8,128)(2,1)S(1)}, u32[]{:S(2)}, u32[]{:S(2)}) collective-permute-start(bf16[1,2,64,512]{3,2,1,0:T(8,128)(2,1)S(1)} %collective-permute-done.18.refs_1_), channel_id=1, source_target_pairs={{0,1},{1,0},{2,3},{3,2},{4,5},{5,4},{6,7},{7,6},{8,9},{9,8},{10,11... | collective-permute-start | bytes 393224 | tf_op jit(solution)/shard_map/ppermute | solution.py:274
  79.7 1.5 %collective-permute-start.21 = (bf16[2,2,64,512]{3,2,1,0:T(8,128)(2,1)S(1)}, bf16[2,2,64,512]{3,2,1,0:T(8,128)(2,1)S(1)}, u32[]{:S(2)}, u32[]{:S(2)}) collective-permute-start(bf16[2,2,64,512]{3,2,1,0:T(8,128)(2,1)S(1)} %collective-permute-done.20.refs_2_), channel_id=1, source_target_pairs={{0,1},{1,0},{2,3},{3,2},{4,5},{5,4},{6,7},{7,6},{8,9},{9,8},{10,11... | collective-permute-start | bytes 786440 | tf_op jit(solution)/shard_map/ppermute | solution.py:274
  (9 other events, 73.5 us)
